TPU v7x, 32 devices: a whole 2x2x4 slice. The times are simulated.
32 devices in a mesh: ctx: 8 (over y, x, core), tp: 4 (over z).
Axes of the slice: x: 2, y: 2, z: 4, core: 2. Of those that a mesh axis runs over, the one named last changes fastest.
Arguments:
- streams: bfloat16 [3, 4096, 1024], P(None, 'tp', 'ctx'), may hold values from -6 to 6
- conv_weight: float32 [3, 7, 4096], P(None, None, 'tp'), may hold values from -2 to 2
- rates: float32 [512, 16], P('tp'), may hold values from 0.0001953125 to 0.05
- residues: float32 [512, 16], P('tp'), may hold values from -4 to 4
- skip: float32 [4096], P('tp'), may hold values from -4 to 4
- out_weight: bfloat16 [4096, 4096], P('ctx', 'tp'), may hold values from -0.09375 to 0.09375
Outputs:
- result: bfloat16 [1024, 4096], P('ctx', 'tp')
All inputs are finite; a program needn't handle non-finite values.
Results may differ from a plain program's by a relative error of at most 0.014.
Values may be sent and summed in bfloat16 or wider, within the bound.
No kernel may reach another device: no remote copies, remote signals or barrier semaphores. Data moves between devices by JAX's collectives and lax.ppermute only.
A program may use at most 128 MiB of HBM per device.

v0:
```python
import math

import jax
import jax.numpy as jnp
from jax import lax
from jax.sharding import PartitionSpec as P


def from_behind(value, axis, steps):
    count = lax.axis_size(axis)
    leading, last = (max(0, -steps), min(count, count - steps))
    return lax.ppermute(value, axis, [(source, source + steps) for source in range(leading, last)])


def block_parts(signal, coefficient, rates):
    groups = coefficient.shape[0]
    channels, length = signal.shape
    group_width = channels // groups
    block_len = 128
    block_count = length // block_len
    blocks = signal.reshape(groups, group_width, block_count, block_len)
    position = jnp.arange(block_len, dtype=jnp.float32)
    centre = (block_len - 1.0) * 0.5
    left_factor = coefficient[:, :, None] * jnp.exp(-rates[:, :, None] * (position - centre))
    right_factor = jnp.exp(rates[:, :, None] * (position - centre))
    causal = (position[:, None] >= position[None, :]).astype(jnp.float32)
    toeplitz = (
        jnp.einsum("gni,gnj->gij", left_factor, right_factor, precision=lax.Precision.HIGHEST)
        * causal
    )
    inside = jnp.einsum("gij,gcbj->gcbi", toeplitz, blocks, precision=lax.Precision.HIGHEST)
    tail_decay = jnp.exp(-rates[:, :, None] * (block_len - 1.0 - position))
    block_ends = jnp.einsum("gnj,gcbj->gcbn", tail_decay, blocks, precision=lax.Precision.HIGHEST)
    block_index = jnp.arange(block_count, dtype=jnp.float32)
    lag = block_index[:, None] - block_index[None, :]
    earlier_mask = (lag >= 1.0).astype(jnp.float32)
    steps_back = jnp.maximum(lag - 1.0, 0.0)
    carry_matrix = jnp.exp(-rates[:, :, None, None] * block_len * steps_back) * earlier_mask
    entering = jnp.einsum(
        "gnab,gcbn->gcan", carry_matrix, block_ends, precision=lax.Precision.HIGHEST
    )
    last_decay = jnp.exp(-rates[:, :, None] * block_len * (block_count - 1.0 - block_index))
    segment_end = jnp.einsum(
        "gnb,gcbn->gcn", last_decay, block_ends, precision=lax.Precision.HIGHEST
    )
    return (inside, entering, segment_end)


def finish_conv(inside, entering, coefficient, rates):
    groups, group_width, block_count, block_len = inside.shape
    position = jnp.arange(block_len, dtype=jnp.float32)
    lift_out = coefficient[:, :, None] * jnp.exp(-rates[:, :, None] * (position + 1.0))
    total = inside + jnp.einsum(
        "gni,gcbn->gcbi", lift_out, entering, precision=lax.Precision.HIGHEST
    )
    return total.reshape(groups * group_width, block_count * block_len)


def local(streams, conv_weight, rates, residues, skip, out_weight):
    tap_count = conv_weight.shape[1]
    rim_width = tap_count - 1
    length = streams.shape[2]
    tail_rows = jnp.swapaxes(streams[:, :, length - rim_width :], 1, 2)
    before = from_behind(tail_rows, "ctx", 1)
    extended = jnp.concatenate([jnp.swapaxes(before, 1, 2), streams], axis=2)
    filtered = conv_weight[:, 0, :, None] * extended[:, :, rim_width:].astype(jnp.float32)
    for shift_by in range(1, tap_count):
        filtered = filtered + conv_weight[:, shift_by, :, None] * extended[
            :, :, rim_width - shift_by : rim_width - shift_by + length
        ].astype(jnp.float32)
    queries = filtered[0]
    gated_in = (filtered[1] * filtered[2]).astype(jnp.bfloat16)
    gated_wide = gated_in.astype(jnp.float32)
    coefficient = residues * jnp.sqrt(2.0 * rates) / math.sqrt(rates.shape[1])
    by_channel = lax.all_to_all(gated_in, "ctx", split_axis=0, concat_axis=1, tiled=True)
    per_device = rates.shape[0] // lax.axis_size("ctx")
    first_group = lax.axis_index("ctx") * per_device
    coef_mine = lax.dynamic_slice_in_dim(coefficient, first_group, per_device, 0)
    rates_mine = lax.dynamic_slice_in_dim(rates, first_group, per_device, 0)
    inside, entering, segment_end = block_parts(
        by_channel.astype(jnp.float32), coef_mine, rates_mine
    )
    filtered_all = finish_conv(inside, entering, coef_mine, rates_mine)
    conv_out = lax.all_to_all(filtered_all, "ctx", split_axis=1, concat_axis=0, tiled=True)
    mixed_out = (queries * (conv_out + skip[:, None] * gated_wide)).astype(jnp.bfloat16)
    features = lax.all_gather(mixed_out, "tp", axis=0, tiled=True)
    summed = lax.dot_general(
        features,
        lax.all_gather(out_weight, "ctx", axis=0, tiled=True),
        (((0,), (0,)), ((), ())),
        preferred_element_type=jnp.float32,
    )
    return summed.astype(jnp.bfloat16)


def solution(mesh):
    return jax.shard_map(
        local,
        mesh=mesh,
        in_specs=(
            P(None, "tp", "ctx"),
            P(None, None, "tp"),
            P("tp", None),
            P("tp", None),
            P("tp"),
            P("ctx", "tp"),
        ),
        out_specs=P("ctx", "tp"),
        check_vma=False,
    )
```

profile of v0, /device:TPU:0, one launch (start us, length us, event | category | flops | bytes accessed | tf_op | source)
XLA Modules:
  0.0 148.7 jit_solution(17110852851964881601)
XLA Ops:
  6.5 1.5 %slice.53 = bf16[3,1024,6]{2,1,0:T(8,128)(2,1)S(1)} slice(bf16[3,1024,128]{2,1,0:T(8,128)(2,1)} %param.6), slice={[0:3], [0:1024], [122:128]} | slice | bytes 73728 | tf_op jit(solution)/shard_map/slice | solution.py:63
  8.0 0.3 copy.39
  8.3 2.4 %collective-permute-start = (bf16[3,6,1024]{2,1,0:T(8,128)(2,1)S(1)}, bf16[3,6,1024]{2,1,0:T(8,128)(2,1)S(1)}, u32[]{:S(2)}, u32[]{:S(2)}) collective-permute-start(bf16[3,6,1024]{2,1,0:T(8,128)(2,1)S(1)} %bitcast.61), channel_id=1, source_target_pairs={{0,4},{4,8},{8,12},{12,16},{16,20},{20,24},{24,28},{1,5},{5,9},{9,... | collective-permute-start | bytes 110600 | tf_op jit(solution)/shard_map/ppermute | solution.py:12
  10.8 0.1 fusion.43
  10.9 0.1 broadcast_multiply_fusion
  11.0 0.1 fusion.40
  11.1 0.1 copy.24
  11.2 0.1 copy.23
  11.2 0.1 copy.25
  11.3 0.1 copy.22
  11.4 0.2 collective-permute-done
  11.6 0.4 copy.20
  12.0 5.6 %multiply_add_fusion = f32[3,1024,128]{2,1,0:T(8,128)S(1)} fusion(bf16[3,1024,128]{2,1,0:T(8,128)(2,1)S(1)} %copy-done.1, bf16[3,1024,6]{2,1,0:T(8,128)(2,1)S(1)} %copy.20, f32[3,1024]{1,0:T(4,128)S(1)} %get-tuple-element.16, f32[3,1024]{1,0:T(4,128)S(1)} %get-tuple-element.17, f32[3,1024]{1,0:T(4,128)S(1)} %get-tuple-element.18, ...), kind=kLoop, calls=%fused_computation.10 | loop fusion | flops 14942208 | bytes 2482176 | tf_op jit(solution)/shard_map/add | solution.py:68
  17.6 0.8 fusion.10
  18.3 7.4 %all-to-all-start = ((bf16[8,128,128]{2,1,0:T(8,128)(2,1)}), bf16[8,128,128]{2,1,0:T(8,128)(2,1)S(1)}, u32[]{:S(2)}, u32[]{:S(2)}) async-start(bf16[8,128,128]{2,1,0:T(8,128)(2,1)} %bitcast.3), calls=%async_computation | async-start | bytes 524288 | tf_op jit(solution)/shard_map/all_to_all | solution.py:75
  25.7 1.9 %fusion = f32[16,128,128,1]{2,1,3,0:T(8,128)S(1)} fusion(f32[128,128]{1,0:T(8,128)S(1)} %fusion.39, f32[16,16]{1,0:T(8,128)S(1)} %copy.24, f32[128]{0:T(128)S(1)} %iota_add_fusion.1, f32[16,16]{1,0:T(8,128)S(1)} %copy.23, f32[16,16]{1,0:T(8,128)S(1)} %copy.22), kind=kOutput, calls=%fused_computation.13 | convolution fusion | flops 50692096 | bytes 1117696 | tf_op jit(solution)/shard_map/gni,gnj->gij/dot_general | solution.py:28
  27.7 4.9 %all-to-all-done = bf16[8,128,128]{2,1,0:T(8,128)(2,1)S(1)} async-done(((bf16[8,128,128]{2,1,0:T(8,128)(2,1)}), bf16[8,128,128]{2,1,0:T(8,128)(2,1)S(1)}, u32[]{:S(2)}, u32[]{:S(2)}) %all-to-all-start) | async-done | bytes 262176 | tf_op jit(solution)/shard_map/all_to_all | solution.py:75
  32.6 0.2 copy.21
  32.8 0.4 fusion.18
  33.2 1.4 copy.26
  34.6 1.1 fusion.44
  35.7 0.1 copy-done
  35.8 1.9 %convolution_bitcast_fusion = f32[16,8,8,16]{2,1,3,0:T(8,128)S(1)} fusion(f32[16,8,8,16]{2,1,3,0:T(8,128)S(1)} %copy-done, f32[8,8]{1,0:T(8,128)S(1)} %fusion.42, f32[8,8]{1,0:T(8,128)S(1)} %add_maximum_fusion, f32[16,16]{1,0:T(8,128)S(1)} %copy.25), kind=kOutput, calls=%fused_computation.11 | convolution fusion | flops 1605632 | bytes 132608 | tf_op jit(solution)/shard_map/gnab,gcbn->gcan/dot_general | solution.py:39
  37.8 1.9 %convolution_add_fusion = f32[16,8,8,128]{3,2,1,0:T(8,128)S(1)} fusion(f32[16,8,8,128]{3,2,1,0:T(8,128)S(1)} %fusion.44, f32[16,8,8,16]{2,1,3,0:T(8,128)S(1)} %convolution_bitcast_fusion, f32[128]{0:T(128)S(1)} %iota_add_fusion, f32[16,16]{1,0:T(8,128)S(1)} %copy.23, f32[16,16]{1,0:T(8,128)S(1)} %copy.22), kind=kOutput, calls=%fused_computation.14 | convolution fusion | flops 25362432 | bytes 1116672 | tf_op jit(solution)/shard_map/gni,gcbn->gcbi/dot_general | solution.py:53
  39.7 0.1 copy.28
  39.8 12.2 %all_to_all.32 = f32[128,8,128]{2,0,1:T(8,128)S(1)} all-to-all(f32[128,8,128]{2,0,1:T(8,128)S(1)} %copy.28), channel_id=1, replica_groups=mesh['ctx'=8,'tp'=4] {'ctx'}, dimensions={1} | all-to-all | bytes 1048576 | tf_op jit(solution)/shard_map/all_to_all | solution.py:84
  51.9 0.9 fusion.12
  52.9 0.0 all-gather.5.cloned.1.call-start
  52.9 0.7 all-gather.5.cloned.1.call-update
  53.6 26.7 %all-gather.3.cloned.1.call-done = bf16[4096,128]{1,0:T(8,128)(2,1)} async-done(((bf16[1024,128]{1,0:T(8,128)(2,1)}), bf16[4096,128]{1,0:T(8,128)(2,1)}) %all-gather.3.cloned.1.call-update) | async-done | bytes 1048592 | tf_op jit(solution)/shard_map/all_gather | solution.py:86
  80.3 55.8 %all-gather.5.cloned.1.call-done = bf16[4096,1024]{1,0:T(8,128)(2,1)} async-done(((bf16[512,1024]{1,0:T(8,128)(2,1)}), bf16[4096,1024]{1,0:T(8,128)(2,1)}) %all-gather.5.cloned.1.call-update) | async-done | bytes 8388624 | tf_op jit(solution)/shard_map/all_gather | solution.py:89
  136.1 5.7 %convolution_convert_fusion = bf16[128,1024]{1,0:T(8,128)(2,1)} fusion(bf16[4096,128]{1,0:T(8,128)(2,1)} %all-gather.3.cloned.1.call-done, bf16[4096,1024]{1,0:T(8,128)(2,1)} %all-gather.5.cloned.1.call-done), kind=kOutput, calls=%fused_computation.15 | convolution fusion | flops 1073872896 | bytes 9699328 | tf_op jit(solution)/shard_map/dot_general | solution.py:87
  (23 shorter events, 0.2 us)
Async XLA Ops:
  6.5 4.3 %copy-start.2 = (f32[3,7,1024]{2,1,0:T(8,128)S(1)}, f32[3,7,1024]{2,1,0:T(8,128)}, u32[]{:S(2)}) copy-start(f32[3,7,1024]{2,1,0:T(8,128)} %param.7) | copy-start | bytes 258052
  6.5 4.4 %copy-start.3 = (f32[128,16]{0,1:T(8,128)S(1)}, f32[128,16]{0,1:T(8,128)}, u32[]{:S(2)}) copy-start(f32[128,16]{0,1:T(8,128)} %param.8) | copy-start | bytes 24580
  6.5 4.5 %copy-start.4 = (f32[128,16]{0,1:T(8,128)S(1)}, f32[128,16]{0,1:T(8,128)}, u32[]{:S(2)}) copy-start(f32[128,16]{0,1:T(8,128)} %param.9) | copy-start | bytes 24580
  6.5 5.5 %copy-start.1 = (bf16[3,1024,128]{2,1,0:T(8,128)(2,1)S(1)}, bf16[3,1024,128]{2,1,0:T(8,128)(2,1)}, u32[]{:S(2)}) copy-start(bf16[3,1024,128]{2,1,0:T(8,128)(2,1)} %param.6) | copy-start | bytes 2359300
  8.3 3.2 %collective-permute-start = (bf16[3,6,1024]{2,1,0:T(8,128)(2,1)S(1)}, bf16[3,6,1024]{2,1,0:T(8,128)(2,1)S(1)}, u32[]{:S(2)}, u32[]{:S(2)}) collective-permute-start(bf16[3,6,1024]{2,1,0:T(8,128)(2,1)S(1)} %bitcast.61), channel_id=1, source_target_pairs={{0,4},{4,8},{8,12},{12,16},{16,20},{20,24},{24,28},{1,5},{5,9},{9,... | collective-permute-start | bytes 110600 | tf_op jit(solution)/shard_map/ppermute | solution.py:12
  18.3 14.3 %all-to-all-start = ((bf16[8,128,128]{2,1,0:T(8,128)(2,1)}), bf16[8,128,128]{2,1,0:T(8,128)(2,1)S(1)}, u32[]{:S(2)}, u32[]{:S(2)}) async-start(bf16[8,128,128]{2,1,0:T(8,128)(2,1)} %bitcast.3), calls=%async_computation | async-start | bytes 524288 | tf_op jit(solution)/shard_map/all_to_all | solution.py:75
  25.7 54.6 %all-gather.3.cloned.1.call-start = ((), (), s32[]{:S(2)}) async-start(), calls=%async_computation.2 | async-start | bytes 1310720 | tf_op jit(solution)/shard_map/all_gather | solution.py:86
  34.6 1.2 copy-start
  39.7 12.3 %copy-start.5 = (f32[1024]{0:T(1024)S(1)}, f32[1024]{0:T(1024)}, u32[]{:S(2)}) copy-start(f32[1024]{0:T(1024)} %param.10) | copy-start | bytes 12292
  52.9 83.3 %all-gather.5.cloned.1.call-start = ((), (), s32[]{:S(2)}) async-start(), calls=%async_computation.3 | async-start | bytes 9437184 | tf_op jit(solution)/shard_map/all_gather | solution.py:89
Sparse Core Ops, SparseCore 0:
  53.0 27.2 all-gather.2
  82.2 53.8 all-gather.4
where the time goes:
time: 149 us
  waiting for transfers between devices  88.3 us (59%)
  between operations  13.6 us (9%)
  matrix products  13 us (9%)
  blocking collectives  12.2 us (8%)
  starting transfers between devices  9.79 us (7%)
  other arithmetic  7.46 us (5%)
  local copies, waits for them, and re-layouts  4.34 us (3%)
    all_gather x1, waiting for transfers between devices, local(): lax.all_gather(out_weight, 'ctx', axis=0, tiled=True)  55.8 us
    all_gather x1, waiting for transfers between devices, local(): features = lax.all_gather(mixed_out, 'tp', axis=0, tiled=True)  26.7 us
    all_to_all x1, blocking collectives, local(): lax.all_to_all(filtered_all, 'ctx', split_axis=1, concat_axis=0, tiled=True)  12.2 us
    all_to_all x1, starting transfers between devices, local(): lax.all_to_all(gated_in, 'ctx', split_axis=0, concat_axis=1, tiled=True)  7.35 us
    dot_general x1, matrix products, local(): lax.dot_general(features, lax.all_gather(out_weight, 'ctx', axis=0, tiled...  5.7 us
    add x1, other arithmetic, local(): filtered + conv_weight[:, shift_by, :, None] * extended[:, :, rim_width -...  5.58 us
    all_to_all x1, waiting for transfers between devices, local(): lax.all_to_all(gated_in, 'ctx', split_axis=0, concat_axis=1, tiled=True)  4.94 us
  transfers between devices with their start and end apart: 4, of which 4 were waited for; matrix products, arithmetic and copies ran while one was open for 2% of the time, Pallas kernels for 0%

commit v1 on v0

--- a/solution.py
+++ b/solution.py
@@ -83,7 +83,10 @@
     filtered_all = finish_conv(inside, entering, coef_mine, rates_mine)
     conv_out = lax.all_to_all(filtered_all, "ctx", split_axis=1, concat_axis=0, tiled=True)
     mixed_out = (queries * (conv_out + skip[:, None] * gated_wide)).astype(jnp.bfloat16)
-    features = lax.all_gather(mixed_out, "tp", axis=0, tiled=True)
+    layers = lax.axis_size("tp")
+    copies = jnp.broadcast_to(mixed_out[None], (layers,) + mixed_out.shape)
+    features = lax.all_to_all(copies, "tp", split_axis=0, concat_axis=0, tiled=True)
+    features = features.reshape(layers * mixed_out.shape[0], length)
     summed = lax.dot_general(
         features,
         lax.all_gather(out_weight, "ctx", axis=0, tiled=True),

time: 149 us -> 102 us (0.68)
  waiting for transfers between devices: 88.3 us -> 8.99 us
  blocking collectives: 12.2 us -> 45.9 us
    all_gather x1, waiting for transfers between devices: 55.8 us -> 0.01 us  [local(): lax.all_gather(out_weight, 'ctx', axis=0, tiled=True)]
    all_to_all x0 -> x1, blocking collectives: none -> 27.8 us  [local(): lax.all_to_all(copies, 'tp', split_axis=0, concat_axis=0, tiled=True)]
    all_gather x1 -> x0, waiting for transfers between devices: 26.7 us -> none  [local(): features = lax.all_gather(mixed_out, 'tp', axis=0, tiled=True)]
    all_to_all x1, blocking collectives: 12.2 us -> 18.1 us  [local(): lax.all_to_all(filtered_all, 'ctx', split_axis=1, concat_axis=0, tiled=True)]
    all_to_all x1, waiting for transfers between devices: 4.94 us -> 8.12 us  [local(): lax.all_to_all(gated_in, 'ctx', split_axis=0, concat_axis=1, tiled=True)]
  transfers between devices with their start and end apart: 4 -> 3, of which waited for: 4 -> 2; matrix products, arithmetic and copies ran while one was open for 2% -> 17% of each run, Pallas kernels for 0% -> 0%
where the time goes in v1:
time: 102 us; the launch traced here: 101 us
  blocking collectives  45.9 us (45%)
  between operations  13.6 us (13%)
  matrix products  12.7 us (12%)
  starting transfers between devices  9.74 us (10%)
  waiting for transfers between devices  8.99 us (9%)
  other arithmetic  6.76 us (7%)
  local copies, waits for them, and re-layouts  3.71 us (4%)
    all_to_all x1, blocking collectives, local(): lax.all_to_all(copies, 'tp', split_axis=0, concat_axis=0, tiled=True)  27.8 us
    all_to_all x1, blocking collectives, local(): lax.all_to_all(filtered_all, 'ctx', split_axis=1, concat_axis=0, tiled=True)  18.1 us
    all_to_all x1, waiting for transfers between devices, local(): lax.all_to_all(gated_in, 'ctx', split_axis=0, concat_axis=1, tiled=True)  8.12 us
    all_to_all x1, starting transfers between devices, local(): lax.all_to_all(gated_in, 'ctx', split_axis=0, concat_axis=1, tiled=True)  7.35 us
    add x1, other arithmetic, local(): filtered + conv_weight[:, shift_by, :, None] * extended[:, :, rim_width -...  5.57 us
    dot_general x1, matrix products, local(): lax.dot_general(features, lax.all_gather(out_weight, 'ctx', axis=0, tiled...  5.37 us
    ppermute x1, starting transfers between devices, from_behind(): lax.ppermute(value, axis, [(source, source + steps) for source in range(l...  2.36 us
  transfers between devices with their start and end apart: 3, of which 2 were waited for; matrix products, arithmetic and copies ran while one was open for 17% of the time, Pallas kernels for 0%

profile of v1, /device:TPU:0, one launch (start us, length us, event | category | flops | bytes accessed | tf_op | source)
XLA Modules:
  0.0 101.3 jit_solution(8147741235769882368)
XLA Ops:
  6.6 0.7 all-gather.2.cloned.1.call-update
  7.3 0.4 copy-done.1
  7.7 0.3 slice.53
  7.9 0.3 copy.39
  8.3 2.4 %collective-permute-start = (bf16[3,6,1024]{2,1,0:T(8,128)(2,1)S(1)}, bf16[3,6,1024]{2,1,0:T(8,128)(2,1)S(1)}, u32[]{:S(2)}, u32[]{:S(2)}) collective-permute-start(bf16[3,6,1024]{2,1,0:T(8,128)(2,1)S(1)} %bitcast.58), channel_id=1, source_target_pairs={{0,4},{4,8},{8,12},{12,16},{16,20},{20,24},{24,28},{1,5},{5,9},{9,... | collective-permute-start | bytes 110600 | tf_op jit(solution)/shard_map/ppermute | solution.py:12
  10.7 0.1 broadcast_multiply_fusion
  10.8 0.1 fusion.38
  10.9 0.1 fusion.41
  11.0 0.1 copy.24
  11.1 0.1 copy.23
  11.2 0.1 copy.25
  11.2 0.1 copy.22
  11.3 0.2 collective-permute-done
  11.5 0.4 copy.20
  11.9 5.6 %multiply_add_fusion = f32[3,1024,128]{2,1,0:T(8,128)S(1)} fusion(bf16[3,1024,128]{2,1,0:T(8,128)(2,1)S(1)} %copy-done.1, bf16[3,1024,6]{2,1,0:T(8,128)(2,1)S(1)} %copy.20, f32[3,1024]{1,0:T(4,128)S(1)} %get-tuple-element.16, f32[3,1024]{1,0:T(4,128)S(1)} %get-tuple-element.17, f32[3,1024]{1,0:T(4,128)S(1)} %get-tuple-element.18, ...), kind=kLoop, calls=%fused_computation.10 | loop fusion | flops 14942208 | bytes 2482176 | tf_op jit(solution)/shard_map/add | solution.py:68
  17.5 0.8 fusion.10
  18.2 7.4 %all-to-all-start = ((bf16[8,128,128]{2,1,0:T(8,128)(2,1)}), bf16[8,128,128]{2,1,0:T(8,128)(2,1)S(1)}, u32[]{:S(2)}, u32[]{:S(2)}) async-start(bf16[8,128,128]{2,1,0:T(8,128)(2,1)} %bitcast.2), calls=%async_computation | async-start | bytes 524288 | tf_op jit(solution)/shard_map/all_to_all | solution.py:75
  25.6 1.9 %fusion = f32[16,128,128,1]{2,1,3,0:T(8,128)S(1)} fusion(f32[128,128]{1,0:T(8,128)S(1)} %fusion.37, f32[16,16]{1,0:T(8,128)S(1)} %copy.24, f32[128]{0:T(128)S(1)} %iota_add_fusion.1, f32[16,16]{1,0:T(8,128)S(1)} %copy.23, f32[16,16]{1,0:T(8,128)S(1)} %copy.22), kind=kOutput, calls=%fused_computation.13 | convolution fusion | flops 50692096 | bytes 1117696 | tf_op jit(solution)/shard_map/gni,gnj->gij/dot_general | solution.py:28
  27.5 8.1 %all-to-all-done = bf16[8,128,128]{2,1,0:T(8,128)(2,1)S(1)} async-done(((bf16[8,128,128]{2,1,0:T(8,128)(2,1)}), bf16[8,128,128]{2,1,0:T(8,128)(2,1)S(1)}, u32[]{:S(2)}, u32[]{:S(2)}) %all-to-all-start) | async-done | bytes 262176 | tf_op jit(solution)/shard_map/all_to_all | solution.py:75
  35.7 0.2 copy.21
  35.8 0.4 fusion.16
  36.3 1.4 %copy.26 = f32[16,8,8,16]{2,1,3,0:T(8,128)} copy(f32[16,8,8,16]{3,2,1,0:T(8,128)S(1)} %fusion.16) | data formatting | bytes 131072 | tf_op jit(solution)/shard_map/gnj,gcbj->gcbn/dot_general | solution.py:33
  37.7 1.1 %fusion.42 = f32[16,8,8,128]{3,2,1,0:T(8,128)S(1)} fusion(bf16[16,8,8,128]{3,2,1,0:T(8,128)(2,1)S(1)} %bitcast.53, f32[16,128,128,1]{2,1,3,0:T(8,128)S(1)} %fusion), kind=kOutput, calls=%fused_computation.77 | convolution fusion | flops 201326592 | bytes 1835008 | tf_op jit(solution)/shard_map/gij,gcbj->gcbi/dot_general | solution.py:31
  38.8 0.1 copy-done
  38.9 1.9 %convolution_bitcast_fusion = f32[16,8,8,16]{2,1,3,0:T(8,128)S(1)} fusion(f32[16,8,8,16]{2,1,3,0:T(8,128)S(1)} %copy-done, f32[8,8]{1,0:T(8,128)S(1)} %fusion.40, f32[8,8]{1,0:T(8,128)S(1)} %add_maximum_fusion, f32[16,16]{1,0:T(8,128)S(1)} %copy.25), kind=kOutput, calls=%fused_computation.11 | convolution fusion | flops 1605632 | bytes 132608 | tf_op jit(solution)/shard_map/gnab,gcbn->gcan/dot_general | solution.py:39
  40.9 1.9 %convolution_add_fusion = f32[16,8,8,128]{3,2,1,0:T(8,128)S(1)} fusion(f32[16,8,8,128]{3,2,1,0:T(8,128)S(1)} %fusion.42, f32[16,8,8,16]{2,1,3,0:T(8,128)S(1)} %convolution_bitcast_fusion, f32[128]{0:T(128)S(1)} %iota_add_fusion, f32[16,16]{1,0:T(8,128)S(1)} %copy.23, f32[16,16]{1,0:T(8,128)S(1)} %copy.22), kind=kOutput, calls=%fused_computation.14 | convolution fusion | flops 25362432 | bytes 1116672 | tf_op jit(solution)/shard_map/gni,gcbn->gcbi/dot_general | solution.py:53
  42.8 0.1 copy.28
  42.9 18.1 %all_to_all.37 = f32[128,8,128]{2,0,1:T(8,128)S(1)} all-to-all(f32[128,8,128]{2,0,1:T(8,128)S(1)} %copy.28), channel_id=1, replica_groups=mesh['ctx'=8,'tp'=4] {'ctx'}, dimensions={1} | all-to-all | bytes 1048576 | tf_op jit(solution)/shard_map/all_to_all | solution.py:84
  61.0 0.2 fusion.11
  61.2 0.1 broadcast_in_dim.5
  61.3 27.8 %all_to_all.38 = bf16[4,1024,128]{2,1,0:T(8,128)(2,1)S(1)} all-to-all(bf16[4,1024,128]{2,1,0:T(8,128)(2,1)S(1)} %broadcast_in_dim.5), channel_id=1, replica_groups=mesh['ctx'=8,'tp'=4] {'tp'}, dimensions={0} | all-to-all | bytes 2097152 | tf_op jit(solution)/shard_map/all_to_all | solution.py:88
  89.1 5.4 %convolution_convert_fusion = bf16[128,1024]{1,0:T(8,128)(2,1)} fusion(bf16[4096,128]{1,0:T(8,128)(2,1)S(1)} %bitcast.51, bf16[4096,1024]{1,0:T(8,128)(2,1)} %all-gather.2.cloned.1.call-done), kind=kOutput, calls=%fused_computation.15 | convolution fusion | flops 1073872896 | bytes 9699328 | tf_op jit(solution)/shard_map/dot_general | solution.py:90
  (22 shorter events, 0.2 us)
Async XLA Ops:
  6.5 1.1 %copy-start.1 = (bf16[3,1024,128]{2,1,0:T(8,128)(2,1)S(1)}, bf16[3,1024,128]{2,1,0:T(8,128)(2,1)}, u32[]{:S(2)}) copy-start(bf16[3,1024,128]{2,1,0:T(8,128)(2,1)} %param.6) | copy-start | bytes 2359300
  6.5 4.1 %copy-start.3 = (f32[128,16]{0,1:T(8,128)S(1)}, f32[128,16]{0,1:T(8,128)}, u32[]{:S(2)}) copy-start(f32[128,16]{0,1:T(8,128)} %param.8) | copy-start | bytes 24580
  6.5 4.2 %copy-start.4 = (f32[128,16]{0,1:T(8,128)S(1)}, f32[128,16]{0,1:T(8,128)}, u32[]{:S(2)}) copy-start(f32[128,16]{0,1:T(8,128)} %param.9) | copy-start | bytes 24580
  6.5 4.3 %copy-start.2 = (f32[3,7,1024]{2,1,0:T(8,128)S(1)}, f32[3,7,1024]{2,1,0:T(8,128)}, u32[]{:S(2)}) copy-start(f32[3,7,1024]{2,1,0:T(8,128)} %param.7) | copy-start | bytes 258052
  6.5 82.6 %all-gather.2.cloned.1.call-start = ((), (), s32[]{:S(2)}) async-start(), calls=%async_computation.3 | async-start | bytes 9437184 | tf_op jit(solution)/shard_map/all_gather | solution.py:92
  8.3 3.2 %collective-permute-start = (bf16[3,6,1024]{2,1,0:T(8,128)(2,1)S(1)}, bf16[3,6,1024]{2,1,0:T(8,128)(2,1)S(1)}, u32[]{:S(2)}, u32[]{:S(2)}) collective-permute-start(bf16[3,6,1024]{2,1,0:T(8,128)(2,1)S(1)} %bitcast.58), channel_id=1, source_target_pairs={{0,4},{4,8},{8,12},{12,16},{16,20},{20,24},{24,28},{1,5},{5,9},{9,... | collective-permute-start | bytes 110600 | tf_op jit(solution)/shard_map/ppermute | solution.py:12
  18.2 17.4 %all-to-all-start = ((bf16[8,128,128]{2,1,0:T(8,128)(2,1)}), bf16[8,128,128]{2,1,0:T(8,128)(2,1)S(1)}, u32[]{:S(2)}, u32[]{:S(2)}) async-start(bf16[8,128,128]{2,1,0:T(8,128)(2,1)} %bitcast.2), calls=%async_computation | async-start | bytes 524288 | tf_op jit(solution)/shard_map/all_to_all | solution.py:75
  37.7 1.2 %copy-start = (f32[16,8,8,16]{2,1,3,0:T(8,128)S(1)}, f32[16,8,8,16]{2,1,3,0:T(8,128)}, u32[]{:S(2)}) copy-start(f32[16,8,8,16]{2,1,3,0:T(8,128)} %copy.26) | copy-start | bytes 196612
  42.8 18.2 %copy-start.5 = (f32[1024]{0:T(1024)S(1)}, f32[1024]{0:T(1024)}, u32[]{:S(2)}) copy-start(f32[1024]{0:T(1024)} %param.10) | copy-start | bytes 12292
Sparse Core Ops, SparseCore 0:
  9.3 65.5 all-gather.1

commit v2 on v0

v2 whole, which is shorter than its diff:
```python
import math

import jax
import jax.numpy as jnp
from jax import lax
from jax.experimental import pallas as pl
from jax.experimental.pallas import tpu as pltpu
from jax.sharding import PartitionSpec as P

F32 = jnp.float32
BF16 = jnp.bfloat16
ROWS = 8
TILE = 128
VMEM_LIMIT = 40 * 1024 * 1024
CONTRACT_LANES = (((1,), (1,)), ((), ()))
CONTRACT_ROWS = (((0,), (0,)), ((), ()))


def from_behind(value, axis, steps):
    count = lax.axis_size(axis)
    leading, last = (max(0, -steps), min(count, count - steps))
    return lax.ppermute(value, axis, [(source, source + steps) for source in range(leading, last)])


def dot(left, right, dims=(((1,), (0,)), ((), ()))):
    return lax.dot_general(left, right, dims, preferred_element_type=F32)


def halves(value):
    high = value.astype(BF16)
    return high, (value - high.astype(F32)).astype(BF16)


def whole(count):
    return [pl.BlockSpec(memory_space=pltpu.VMEM)] * count


def call(kernel, outs, name, *operands, specs=None, scratch=()):
    return pl.pallas_call(
        kernel,
        out_shape=outs,
        in_specs=whole(len(operands)) if specs is None else specs,
        out_specs=tuple(whole(len(outs))),
        scratch_shapes=scratch,
        compiler_params=pltpu.CompilerParams(vmem_limit_bytes=VMEM_LIMIT),
        name=name,
    )(*operands)


def tails_kernel(streams_ref, tails_ref):
    length = streams_ref.shape[2]
    row = lax.broadcasted_iota(jnp.int32, (2 * ROWS, length), 0)
    lane = lax.broadcasted_iota(jnp.int32, (2 * ROWS, length), 1)
    pick = (lane == row + (length - ROWS)).astype(BF16)
    for stream in range(streams_ref.shape[0]):
        rows = dot(pick, streams_ref[stream], CONTRACT_LANES)
        tails_ref[stream] = rows[:ROWS].astype(BF16)


def filtered_tile(stream, chans, lane, columns, streams_ref, taps_ref, mine_ref, before_ref):
    taps = taps_ref.shape[1]
    signal = streams_ref[stream, chans, :].astype(F32)
    first = stream * taps
    total = columns[:, first : first + 1] * signal
    for shift in range(1, taps):
        total = total + columns[:, first + shift : first + shift + 1] * pltpu.roll(signal, shift, 1)
    change = before_ref[stream, :, chans].astype(F32) - mine_ref[stream, :, chans].astype(F32)
    row = lax.broadcasted_iota(jnp.int32, change.shape, 0)
    head = jnp.zeros_like(change)
    for shift in range(1, taps):
        moved = pltpu.roll(change, shift, 0)
        head = head + jnp.where(row < shift, taps_ref[stream, shift : shift + 1, chans] * moved, 0.0)
    wide = jnp.concatenate([head, jnp.zeros((TILE - ROWS, TILE), F32)], axis=0)
    return total + wide.T


def tap_columns(chans, taps_ref):
    streams, taps = taps_ref.shape[:2]
    rows = [taps_ref[stream, :, chans] for stream in range(streams)]
    rows.append(jnp.zeros((TILE - streams * taps, TILE), F32))
    return jnp.concatenate(rows, axis=0).T


def gate_kernel(streams_ref, taps_ref, mine_ref, before_ref, rates_ref, gated_ref, ends_ref):
    channels, length = gated_ref.shape
    poles, groups = rates_ref.shape
    width = channels // groups
    in_tile = TILE // width
    lane = lax.broadcasted_iota(jnp.int32, (TILE, length), 1)
    lag = (length - 1) - lax.broadcasted_iota(jnp.int32, (poles, length), 1).astype(F32)
    owner = lax.broadcasted_iota(jnp.int32, (poles, TILE), 1) // width

    def tile(index, carry):
        chans = pl.ds(pl.multiple_of(index * TILE, TILE), TILE)
        columns = tap_columns(chans, taps_ref)
        left = filtered_tile(1, chans, lane, columns, streams_ref, taps_ref, mine_ref, before_ref)
        right = filtered_tile(2, chans, lane, columns, streams_ref, taps_ref, mine_ref, before_ref)
        gated = (left * right).astype(BF16)
        gated_ref[chans, :] = gated
        here = pltpu.roll(rates_ref[...], groups - index * in_tile, 1)
        decay = jnp.concatenate(
            [jnp.exp(-here[:, g : g + 1] * lag) for g in range(in_tile)], axis=0
        )
        high, low = halves(decay)
        every = dot(high, gated, CONTRACT_LANES) + dot(low, gated, CONTRACT_LANES)
        ends = jnp.zeros((poles, TILE), F32)
        for g in range(in_tile):
            ends = jnp.where(owner == g, every[g * poles : (g + 1) * poles], ends)
        ends_ref[:, chans] = ends.astype(ends_ref.dtype)
        return carry

    lax.fori_loop(0, channels // TILE, tile, 0)


def inside_kernel(streams_ref, taps_ref, mine_ref, before_ref, rates_ref, coef_ref, skip_ref, gated_ref, query_ref, base_ref):
    channels, length = gated_ref.shape
    poles, groups = rates_ref.shape
    width = channels // groups
    in_tile = TILE // width
    lane = lax.broadcasted_iota(jnp.int32, (TILE, length), 1)
    time = lax.broadcasted_iota(jnp.int32, (poles, length), 1).astype(F32)
    causal = lax.broadcasted_iota(jnp.int32, (length, length), 1) >= lax.broadcasted_iota(
        jnp.int32, (length, length), 0
    )

    def tile(index, carry):
        chans = pl.ds(pl.multiple_of(index * TILE, TILE), TILE)
        columns = tap_columns(chans, taps_ref)
        query_ref[chans, :] = filtered_tile(
            0, chans, lane, columns, streams_ref, taps_ref, mine_ref, before_ref
        )
        skip = jnp.concatenate(
            [skip_ref[:, chans], jnp.zeros((TILE - 1, TILE), F32)], axis=0
        ).T[:, 0:1]
        gated = gated_ref[chans, :]
        here = pltpu.roll(rates_ref[...], groups - index * in_tile, 1)
        coef = pltpu.roll(coef_ref[...], groups - index * in_tile, 1)
        parts = []
        for g in range(in_tile):
            terms = coef[:, g : g + 1] * jnp.exp(-here[:, g : g + 1] * time)
            impulse = jnp.sum(terms, axis=0, keepdims=True)
            spread = jnp.broadcast_to(impulse, (length, length))
            shifted = pltpu.roll(spread, 0, 1, stride=1, stride_axis=0)
            toeplitz = jnp.where(causal, shifted, 0.0).astype(BF16)
            parts.append(dot(gated[g * width : (g + 1) * width], toeplitz))
        base_ref[chans, :] = jnp.concatenate(parts, axis=0) + skip * gated.astype(F32)
        return carry

    lax.fori_loop(0, channels // TILE, tile, 0)


def finish_kernel(me_ref, ends_ref, wide_ref, rates_ref, coef_ref, query_ref, base_ref, mixed_ref):
    channels, length = mixed_ref.shape
    poles, groups = rates_ref.shape
    width = channels // groups
    in_tile = TILE // width
    blocks = ends_ref.shape[0]
    me = me_ref[0]
    step_decay = jnp.exp(-wide_ref[...] * length)

    def earlier(block, state):
        return jnp.where(block < me, step_decay * state + ends_ref[block].astype(F32), state)

    state = lax.fori_loop(0, blocks - 1, earlier, jnp.zeros((poles, channels), F32))
    wide_ref[...] = state
    time = 1.0 + lax.broadcasted_iota(jnp.int32, (poles, length), 1).astype(F32)
    owner = lax.broadcasted_iota(jnp.int32, (poles, TILE), 1) // width

    def tile(index, carry):
        chans = pl.ds(pl.multiple_of(index * TILE, TILE), TILE)
        here = pltpu.roll(rates_ref[...], groups - index * in_tile, 1)
        coef = pltpu.roll(coef_ref[...], groups - index * in_tile, 1)
        entering = wide_ref[:, chans]
        lift = jnp.concatenate(
            [coef[:, g : g + 1] * jnp.exp(-here[:, g : g + 1] * time) for g in range(in_tile)], axis=0
        )
        apart = jnp.concatenate(
            [jnp.where(owner == g, entering, 0.0) for g in range(in_tile)], axis=0
        )
        lift_high, lift_low = halves(lift)
        high, low = halves(apart)
        carried = (
            dot(high, lift_high, CONTRACT_ROWS)
            + dot(low, lift_high, CONTRACT_ROWS)
            + dot(high, lift_low, CONTRACT_ROWS)
        )
        mixed_ref[chans, :] = (query_ref[chans, :] * (base_ref[chans, :] + carried)).astype(BF16)
        return carry

    lax.fori_loop(0, channels // TILE, tile, 0)


def broadcast_exchange(value, axis):
    count = lax.axis_size(axis)
    copies = jnp.broadcast_to(value[None], (count,) + value.shape)
    return lax.all_to_all(copies, axis, split_axis=0, concat_axis=0, tiled=True)


def local(streams, conv_weight, rates, residues, skip, out_weight):
    channels, length = streams.shape[1:]
    groups, poles = rates.shape
    layers = lax.axis_size("tp")
    weight = lax.all_gather(out_weight, "ctx", axis=0, tiled=True)

    rates_t = rates.T
    coef_t = residues.T * jnp.sqrt(2.0 * rates_t) / math.sqrt(poles)
    rates_wide = jnp.repeat(rates_t, channels // groups, axis=1)
    skip_row = skip[None, :]

    shape = jax.ShapeDtypeStruct
    (mine,) = call(tails_kernel, (shape((3, ROWS, channels), BF16),), "tails", streams)
    before = from_behind(mine, "ctx", 1)
    gated, ends = call(
        gate_kernel,
        (shape((channels, length), BF16), shape((poles, channels), BF16)),
        "gate",
        streams, conv_weight, mine, before, rates_t,
    )
    all_ends = broadcast_exchange(ends, "ctx")
    query, base = call(
        inside_kernel,
        (shape((channels, length), F32), shape((channels, length), F32)),
        "inside",
        streams, conv_weight, mine, before, rates_t, coef_t, skip_row, gated,
    )
    me = lax.axis_index("ctx").astype(jnp.int32)[None]
    (mixed,) = call(
        finish_kernel_with_scratch,
        (shape((channels, length), BF16),),
        "finish",
        me, all_ends, rates_wide, rates_t, coef_t, query, base,
        specs=[pl.BlockSpec(memory_space=pltpu.SMEM)] + whole(6),
        scratch=[pltpu.VMEM((poles, channels), F32)],
    )
    features = broadcast_exchange(mixed, "tp").reshape(layers * channels, length)
    summed = lax.dot_general(features, weight, CONTRACT_ROWS, preferred_element_type=F32)
    return summed.astype(BF16)


def finish_kernel_with_scratch(me_ref, ends_ref, wide_ref, rates_ref, coef_ref, query_ref, base_ref, mixed_ref, state_ref):
    state_ref[...] = wide_ref[...]
    finish_kernel(me_ref, ends_ref, state_ref, rates_ref, coef_ref, query_ref, base_ref, mixed_ref)


def solution(mesh):
    return jax.shard_map(
        local,
        mesh=mesh,
        in_specs=(
            P(None, "tp", "ctx"),
            P(None, None, "tp"),
            P("tp", None),
            P("tp", None),
            P("tp"),
            P("ctx", "tp"),
        ),
        out_specs=P("ctx", "tp"),
        check_vma=False,
    )
```

time: 149 us -> 94.5 us (0.63)
  waiting for transfers between devices: 88.3 us -> 0.78 us
  Pallas kernels: 0 us -> 22.8 us
  blocking collectives: 12.2 us -> 31.1 us
  matrix products: 13 us -> 5.36 us
  other arithmetic: 7.46 us -> 0.73 us
  local copies, waits for them, and re-layouts: 4.34 us -> 9.82 us
    all_gather x2 -> x1, waiting for transfers between devices: 82.5 us -> 0.01 us  [local(): weight = lax.all_gather(out_weight, 'ctx', axis=0, tiled=True)]
    pallas_call x0 -> x4, Pallas kernels: none -> 22.8 us  [call(): pl.pallas_call(kernel, out_shape=outs, in_specs=whole(len(operands)) if s...]
    all_to_all x1, blocking collectives: 12.2 us -> 31.1 us  [broadcast_exchange(): return lax.all_to_all(copies, axis, split_axis=0, concat_axis=0, tiled=True)]
    dot_general x6 -> x1, matrix products: 13 us -> 5.36 us  [local(): lax.dot_general(features, weight, CONTRACT_ROWS, preferred_element_type=F32)]
    unnamed x17 -> x18, local copies, waits for them, and re-layouts: 0.45 us -> 7.96 us
    add x2 -> x0, other arithmetic: 5.58 us -> none  [the longest x1 5.58 us: local(): filtered + conv_weight[:, shift_by, :, None] * extended[:, :, rim_width -...]
    all_to_all x1, waiting for transfers between devices: 4.94 us -> 0.01 us  [broadcast_exchange(): return lax.all_to_all(copies, axis, split_axis=0, concat_axis=0, tiled=True)]
    convert_element_type x4 -> x0, other arithmetic: 1.7 us -> none  [the longest x1 0.91 us: local(): (queries * (conv_out + skip[:, None] * gated_wide)).astype(jnp.bfloat16)]
  transfers between devices with their start and end apart: 4 -> 3, of which waited for: 4 -> 1; matrix products, arithmetic and copies ran while one was open for 2% -> 3% of each run, Pallas kernels for 0% -> 24%
where the time goes in v2:
time: 94.5 us; the launch traced here: 93.8 us
  blocking collectives  31.1 us (33%)
  Pallas kernels  22.8 us (24%)
  between operations  13.5 us (14%)
  local copies, waits for them, and re-layouts  9.82 us (10%)
  starting transfers between devices  9.72 us (10%)
  matrix products  5.36 us (6%)
    all_to_all x1, blocking collectives, broadcast_exchange(): return lax.all_to_all(copies, axis, split_axis=0, concat_axis=0, tiled=True)  31.1 us
    pallas_call x4, Pallas kernels, call(): pl.pallas_call(kernel, out_shape=outs, in_specs=whole(len(operands)) if s...  22.8 us
    unnamed x18, local copies, waits for them, and re-layouts  7.96 us
    all_to_all x1, starting transfers between devices, broadcast_exchange(): return lax.all_to_all(copies, axis, split_axis=0, concat_axis=0, tiled=True)  7.35 us
    dot_general x1, matrix products, local(): lax.dot_general(features, weight, CONTRACT_ROWS, preferred_element_type=F32)  5.36 us
    ppermute x1, starting transfers between devices, from_behind(): lax.ppermute(value, axis, [(source, source + steps) for source in range(l...  2.37 us
  transfers between devices with their start and end apart: 3, of which 1 were waited for; matrix products, arithmetic and copies ran while one was open for 3% of the time, Pallas kernels for 24%

profile of v2, /device:TPU:0, one launch (start us, length us, event | category | flops | bytes accessed | tf_op | source)
XLA Modules:
  0.0 93.8 jit_solution(2785858730521643632)
XLA Ops:
  6.5 0.0 all-gather.2.cloned.1.call-start
  6.5 0.7 all-gather.2.cloned.1.call-update
  7.3 0.0 copy-start
  7.3 1.1 %copy-done = bf16[3,1024,128]{2,1,0:T(8,128)(2,1)S(1)} copy-done((bf16[3,1024,128]{2,1,0:T(8,128)(2,1)S(1)}, bf16[3,1024,128]{2,1,0:T(8,128)(2,1)}, u32[]{:S(2)}) %copy-start) | copy-done | bytes 786456
  8.4 0.3 tails.1.mine_ref
  8.7 2.4 %collective-permute-start = (bf16[3,8,1024]{2,1,0:T(8,128)(2,1)S(1)}, bf16[3,8,1024]{2,1,0:T(8,128)(2,1)S(1)}, u32[]{:S(2)}, u32[]{:S(2)}) collective-permute-start(bf16[3,8,1024]{2,1,0:T(8,128)(2,1)S(1)} %tails.1.mine_ref), channel_id=1, source_target_pairs={{0,4},{4,8},{8,12},{12,16},{16,20},{20,24},{24,28},{1,5},{5,9},{9,... | collective-permute-start | bytes 147464 | tf_op jit(solution)/shard_map/ppermute | solution.py:22
  11.1 0.8 copy.7
  11.9 0.1 collective-permute-done.before_ref
  11.9 0.0 copy-start.1
  11.9 1.1 %copy-done.1 = bf16[3,1024,128]{2,1,0:T(8,128)(2,1)S(1)} copy-done((bf16[3,1024,128]{2,1,0:T(8,128)(2,1)S(1)}, bf16[3,1024,128]{2,1,0:T(8,128)(2,1)}, u32[]{:S(2)}) %copy-start.1) | copy-done | bytes 786456
  13.1 0.0 copy-start.3
  13.1 0.9 copy-done.3
  14.0 0.7 copy-done.5
  14.7 7.1 %gate.1 = (bf16[1024,128]{1,0:T(8,128)(2,1)S(1)}, bf16[16,1024]{1,0:T(8,128)(2,1)S(1)}) custom-call(bf16[3,1024,128]{2,1,0:T(8,128)(2,1)S(1)} %copy-done.1, f32[3,7,1024]{2,1,0:T(8,128)S(1)} %copy-done.3, bf16[3,8,1024]{2,1,0:T(8,128)(2,1)S(1)} %tails.1.mine_ref, bf16[3,8,1024]{2,1,0:T(8,128)(2,1)S(1)} %collective-permute-done.before_ref, f32[16,128]{1,0:T(8,128)S(1)} %bitcast.14), custom_call_target="tpu_custom_call" | custom-call | tf_op jit(solution)/shard_map/gate/pallas_call | solution.py:39
  21.8 0.7 broadcast_in_dim.22
  22.5 7.4 %all-to-all-start = ((bf16[8,16,1024]{2,1,0:T(8,128)(2,1)}), bf16[8,16,1024]{2,1,0:T(8,128)(2,1)S(1)}, u32[]{:S(2)}, u32[]{:S(2)}) async-start(bf16[8,16,1024]{2,1,0:T(8,128)(2,1)} %broadcast_in_dim.22), calls=%async_computation | async-start | bytes 524288 | tf_op jit(solution)/shard_map/all_to_all | solution.py:196
  29.9 0.2 copy.8.wide_ref
  30.0 0.7 fusion.coef_ref
  30.8 0.0 copy-start.2
  30.8 1.1 %copy-done.2 = bf16[3,1024,128]{2,1,0:T(8,128)(2,1)S(1)} copy-done((bf16[3,1024,128]{2,1,0:T(8,128)(2,1)S(1)}, bf16[3,1024,128]{2,1,0:T(8,128)(2,1)}, u32[]{:S(2)}) %copy-start.2) | copy-done | bytes 786456
  31.9 0.0 copy-start.4
  31.9 0.9 copy-done.4
  32.8 0.0 copy-start.6
  32.8 0.7 copy-done.6
  33.5 0.7 copy-done.8
  34.2 11.8 %inside.1 = (f32[1024,128]{1,0:T(8,128)S(1)}, f32[1024,128]{1,0:T(8,128)S(1)}) custom-call(bf16[3,1024,128]{2,1,0:T(8,128)(2,1)S(1)} %copy-done.2, f32[3,7,1024]{2,1,0:T(8,128)S(1)} %copy-done.4, bf16[3,8,1024]{2,1,0:T(8,128)(2,1)S(1)} %tails.1.mine_ref, bf16[3,8,1024]{2,1,0:T(8,128)(2,1)S(1)} %collective-permute-done.before_ref, f32[16,128]{1,0:T(8,128)S(1)} %bitcast.15, ...), custom_call_target="tpu_custom_call" | custom-call | tf_op jit(solution)/shard_map/inside/pallas_call | solution.py:39
  46.0 0.0 all-to-all-done.ends_ref
  46.0 0.7 copy-done.7
  46.7 3.6 %finish.1 = bf16[1024,128]{1,0:T(8,128)(2,1)S(1)} custom-call(s32[1]{0:T(128)} %bitcast.me_ref, bf16[8,16,1024]{2,1,0:T(8,128)(2,1)S(1)} %all-to-all-done.ends_ref, f32[16,1024]{1,0:T(8,128)S(1)} %copy.8.wide_ref, f32[16,128]{1,0:T(8,128)S(1)} %bitcast.16, f32[16,128]{1,0:T(8,128)S(1)} %fusion.coef_ref, f32[1024,128]{1,0:T(8,128)S(1)} %get-tuple-element.11.query_ref, ...), custom_call_target="tpu_custom_call" | custom-call | tf_op jit(solution)/shard_map/finish/pallas_call | solution.py:39
  50.3 0.1 broadcast_in_dim.25
  50.5 31.1 %all_to_all.10 = bf16[4,1024,128]{2,1,0:T(8,128)(2,1)S(1)} all-to-all(bf16[4,1024,128]{2,1,0:T(8,128)(2,1)S(1)} %broadcast_in_dim.25), channel_id=1, replica_groups=mesh['ctx'=8,'tp'=4] {'tp'}, dimensions={0} | all-to-all | bytes 2097152 | tf_op jit(solution)/shard_map/all_to_all | solution.py:196
  81.5 5.4 %convolution_convert_fusion = bf16[128,1024]{1,0:T(8,128)(2,1)} fusion(bf16[4096,128]{1,0:T(8,128)(2,1)S(1)} %bitcast.18, bf16[4096,1024]{1,0:T(8,128)(2,1)} %all-gather.2.cloned.1.call-done), kind=kOutput, calls=%fused_computation | convolution fusion | flops 1073872896 | bytes 9699328 | tf_op jit(solution)/shard_map/dot_general | solution.py:236
  (5 shorter events, 0.0 us)
Async XLA Ops:
  6.5 75.0 %all-gather.2.cloned.1.call-start = ((), (), s32[]{:S(2)}) async-start(), calls=%async_computation.2 | async-start | bytes 9437184 | tf_op jit(solution)/shard_map/all_gather | solution.py:203
  7.3 1.1 %copy-start = (bf16[3,1024,128]{2,1,0:T(8,128)(2,1)S(1)}, bf16[3,1024,128]{2,1,0:T(8,128)(2,1)}, u32[]{:S(2)}) copy-start(bf16[3,1024,128]{2,1,0:T(8,128)(2,1)} %streams_ref.5) | copy-start | bytes 2359300
  8.7 3.2 %collective-permute-start = (bf16[3,8,1024]{2,1,0:T(8,128)(2,1)S(1)}, bf16[3,8,1024]{2,1,0:T(8,128)(2,1)S(1)}, u32[]{:S(2)}, u32[]{:S(2)}) collective-permute-start(bf16[3,8,1024]{2,1,0:T(8,128)(2,1)S(1)} %tails.1.mine_ref), channel_id=1, source_target_pairs={{0,4},{4,8},{8,12},{12,16},{16,20},{20,24},{24,28},{1,5},{5,9},{9,... | collective-permute-start | bytes 147464 | tf_op jit(solution)/shard_map/ppermute | solution.py:22
  11.9 1.1 %copy-start.1 = (bf16[3,1024,128]{2,1,0:T(8,128)(2,1)S(1)}, bf16[3,1024,128]{2,1,0:T(8,128)(2,1)}, u32[]{:S(2)}) copy-start(bf16[3,1024,128]{2,1,0:T(8,128)(2,1)} %streams_ref.5) | copy-start | bytes 2359300
  13.1 0.9 copy-start.3
  14.0 0.7 copy-start.5
  22.5 23.5 %all-to-all-start = ((bf16[8,16,1024]{2,1,0:T(8,128)(2,1)}), bf16[8,16,1024]{2,1,0:T(8,128)(2,1)S(1)}, u32[]{:S(2)}, u32[]{:S(2)}) async-start(bf16[8,16,1024]{2,1,0:T(8,128)(2,1)} %broadcast_in_dim.22), calls=%async_computation | async-start | bytes 524288 | tf_op jit(solution)/shard_map/all_to_all | solution.py:196
  30.8 1.1 %copy-start.2 = (bf16[3,1024,128]{2,1,0:T(8,128)(2,1)S(1)}, bf16[3,1024,128]{2,1,0:T(8,128)(2,1)}, u32[]{:S(2)}) copy-start(bf16[3,1024,128]{2,1,0:T(8,128)(2,1)} %streams_ref.5) | copy-start | bytes 2359300
  31.9 0.9 copy-start.4
  32.8 0.7 copy-start.6
  33.5 0.7 copy-start.8
  46.0 0.7 copy-start.7
Sparse Core Ops, SparseCore 0:
  9.2 59.9 all-gather.1

commit v3 on v0

v3 whole, which is shorter than its diff:
```python
import math

import jax
import jax.numpy as jnp
from jax import lax
from jax.experimental import pallas as pl
from jax.experimental.pallas import tpu as pltpu
from jax.sharding import PartitionSpec as P

F32 = jnp.float32
BF16 = jnp.bfloat16
ROWS = 8
TILE = 128
CORES = 2
VMEM_LIMIT = 24 * 1024 * 1024
PLAIN = (((1,), (0,)), ((), ()))
CONTRACT_LANES = (((1,), (1,)), ((), ()))


def from_behind(value, axis, steps):
    count = lax.axis_size(axis)
    leading, last = (max(0, -steps), min(count, count - steps))
    return lax.ppermute(value, axis, [(source, source + steps) for source in range(leading, last)])


def dot(left, right, dims=PLAIN):
    return lax.dot_general(left, right, dims, preferred_element_type=F32)


def halves(value):
    high = value.astype(BF16)
    return high, (value - high.astype(F32)).astype(BF16)


def iota(shape, axis):
    return lax.broadcasted_iota(jnp.int32, shape, axis)


def identity(size):
    return (iota((size, size), 0) == iota((size, size), 1)).astype(BF16)


def turned(value, unit):
    return dot(unit, value, CONTRACT_LANES)


def whole(count):
    return [pl.BlockSpec(memory_space=pltpu.VMEM)] * count


def call(kernel, outs, name, *operands, specs=None, scratch=(), flops=10**8):
    return pl.pallas_call(
        kernel,
        out_shape=tuple(jax.ShapeDtypeStruct(*out) for out in outs),
        in_specs=whole(len(operands)) if specs is None else specs,
        out_specs=tuple(whole(len(outs))),
        scratch_shapes=scratch,
        compiler_params=pltpu.CompilerParams(vmem_limit_bytes=VMEM_LIMIT),
        cost_estimate=pl.CostEstimate(flops=flops, bytes_accessed=10**6, transcendentals=0),
        name=name,
    )(*operands)


def tile_of(index, size=TILE):
    return pl.ds(pl.multiple_of(index * size, size), size)


def tails_kernel(streams_ref, tails_ref):
    length = streams_ref.shape[2]
    pick = (iota((2 * ROWS, length), 1) == iota((2 * ROWS, length), 0) + (length - ROWS)).astype(BF16)
    for stream in range(streams_ref.shape[0]):
        rows = dot(pick, streams_ref[stream], CONTRACT_LANES)
        tails_ref[stream] = rows[:ROWS].astype(BF16)


def short_conv(stream, chans, rows, padded_ref, taps_ref):
    total = None
    for shift in range(taps_ref.shape[1]):
        term = taps_ref[stream, shift : shift + 1, chans] * padded_ref[stream, pl.ds(ROWS - shift, rows), :]
        total = term if total is None else total + term
    return total


def prepare_kernel(
    streams_ref, taps_ref, rates_ref, residues_ref,
    heads_ref, query_ref, gated_ref, decay_ref, lift_ref, toeplitz_ref, step_ref, padded_ref,
):
    channels, length = streams_ref.shape[1:]
    poles, groups = rates_ref.shape
    width = channels // groups
    in_tile = TILE // width
    unit = identity(length)
    time = iota((poles, length), 1).astype(F32)
    owner = iota((poles, TILE), 1) // width
    member = (iota((in_tile, in_tile * poles), 1) // poles == iota((in_tile, in_tile * poles), 0)).astype(BF16)
    causal = iota((length, length), 1) >= iota((length, length), 0)
    for stream in range(3):
        padded_ref[stream, :ROWS, :] = jnp.zeros((ROWS, TILE), F32)

    def tile(index, carry):
        chans = tile_of(index)
        for stream in range(3):
            padded_ref[stream, ROWS:, :] = turned(streams_ref[stream, chans, :], unit)
            heads_ref[stream, :, chans] = padded_ref[stream, ROWS : 2 * ROWS, :]
        query_ref[:, chans] = short_conv(0, chans, length, padded_ref, taps_ref)
        left = short_conv(1, chans, length, padded_ref, taps_ref)
        gated_ref[:, chans] = left * short_conv(2, chans, length, padded_ref, taps_ref)

        shift = groups - index * in_tile
        rates = pltpu.roll(rates_ref[...], shift, 1)
        coef = pltpu.roll(residues_ref[...], shift, 1) * jnp.sqrt(2.0 * rates) / math.sqrt(poles)
        decay, impulse, lift = [], [], []
        wide = jnp.zeros((poles, TILE), F32)
        for g in range(in_tile):
            rate = jnp.broadcast_to(rates[:, g : g + 1], (poles, length))
            scale = jnp.broadcast_to(coef[:, g : g + 1], (poles, length))
            decay.append(jnp.exp(-rate * ((length - 1) - time)))
            impulse.append(scale * jnp.exp(-rate * time))
            lift.append(scale * jnp.exp(-rate * (time + 1.0)))
            wide = jnp.where(owner == g, rate[:, :TILE], wide)
        step_ref[:, chans] = jnp.exp(-wide * length)
        states = tile_of(index, in_tile * poles)
        for part, value in enumerate(halves(jnp.concatenate(decay, axis=0))):
            decay_ref[part, states, :] = value
        for part, value in enumerate(halves(jnp.concatenate(lift, axis=0))):
            lift_ref[part, :, states] = turned(value, unit).astype(BF16)
        high, low = halves(jnp.concatenate(impulse, axis=0))
        response = dot(member, high) + dot(member, low)
        for g in range(in_tile):
            spread = jnp.broadcast_to(response[g : g + 1], (length, length))
            shifted = pltpu.roll(spread, 0, 1, stride=1, stride_axis=0)
            block = jnp.where(causal, shifted, 0.0).astype(BF16)
            toeplitz_ref[index * (in_tile // 2) + g // 2, :, (g % 2) * length : (g % 2 + 1) * length] = block
        return carry

    lax.fori_loop(0, channels // TILE, tile, 0)


def states_kernel(before_ref, heads_ref, taps_ref, gated_ref, decay_ref, ends_ref, final_ref, first_ref, padded_ref):
    length, channels = gated_ref.shape
    poles = ends_ref.shape[1]
    in_tile = decay_ref.shape[1] // poles * TILE // channels
    owner = iota((poles, TILE), 1) // (TILE // in_tile)

    def tile(index, carry):
        chans = tile_of(index)
        for stream in range(3):
            padded_ref[stream, :ROWS, :] = before_ref[stream, :, chans].astype(F32)
            padded_ref[stream, ROWS:, :] = heads_ref[stream, :, chans]
        first_ref[:, chans] = short_conv(0, chans, ROWS, padded_ref, taps_ref)
        head = short_conv(1, chans, ROWS, padded_ref, taps_ref) * short_conv(2, chans, ROWS, padded_ref, taps_ref)
        gated = jnp.concatenate([head, gated_ref[ROWS:, chans]], axis=0).astype(BF16)
        final_ref[:, chans] = gated
        states = tile_of(index, in_tile * poles)
        every = dot(decay_ref[0, states, :], gated) + dot(decay_ref[1, states, :], gated)
        ends = jnp.zeros((poles, TILE), F32)
        for g in range(in_tile):
            ends = jnp.where(owner == g, every[g * poles : (g + 1) * poles], ends)
        ends = ends.astype(BF16)
        for block in range(ends_ref.shape[0]):
            ends_ref[block, :, chans] = ends
        return carry

    lax.fori_loop(0, channels // TILE, tile, 0)


def inside_kernel(gated_ref, toeplitz_ref, skip_ref, base_ref):
    length, channels = gated_ref.shape
    pairs = toeplitz_ref.shape[0] * TILE // channels
    width = TILE // (2 * pairs)
    unit = identity(length)

    def tile(index, carry):
        chans = tile_of(index)
        gated = gated_ref[:, chans]
        signal = turned(gated, unit).astype(BF16)
        parts = []
        for pair in range(pairs):
            both = dot(signal[pair * 2 * width : (pair + 1) * 2 * width], toeplitz_ref[index * pairs + pair])
            parts += [both[:width, :length], both[width:, length:]]
        high, low = halves(jnp.concatenate(parts, axis=0))
        base_ref[:, chans] = turned(high, unit) + turned(low, unit) + skip_ref[:, chans] * gated.astype(F32)
        return carry

    lax.fori_loop(0, channels // TILE, tile, 0)


def finish_kernel(me_ref, ends_ref, step_ref, lift_ref, query_ref, first_ref, base_ref, mixed_ref, state_ref):
    length, channels = mixed_ref.shape
    poles = step_ref.shape[0]
    in_tile = lift_ref.shape[2] // poles * TILE // channels
    me = me_ref[0]

    def earlier(block, state):
        return jnp.where(block < me, step_ref[...] * state + ends_ref[block].astype(F32), state)

    state_ref[...] = lax.fori_loop(0, ends_ref.shape[0] - 1, earlier, jnp.zeros((poles, channels), F32))
    owner = iota((poles, TILE), 1) // (TILE // in_tile)

    def tile(index, carry):
        chans = tile_of(index)
        entering = state_ref[:, chans]
        apart = jnp.concatenate([jnp.where(owner == g, entering, 0.0) for g in range(in_tile)], axis=0)
        high, low = halves(apart)
        states = tile_of(index, in_tile * poles)
        lift = lift_ref[0, :, states]
        carried = dot(lift, high) + dot(lift, low) + dot(lift_ref[1, :, states], high)
        query = jnp.concatenate([first_ref[:, chans], query_ref[ROWS:, chans]], axis=0)
        mixed_ref[:, chans] = (query * (base_ref[:, chans] + carried)).astype(BF16)
        return carry

    lax.fori_loop(0, channels // TILE, tile, 0)


def local(streams, conv_weight, rates, residues, skip, out_weight):
    channels, length = streams.shape[1:]
    groups, poles = rates.shape
    blocks, layers = lax.axis_size("ctx"), lax.axis_size("tp")
    rows, features = out_weight.shape
    core_groups = [list(range(core, blocks, CORES)) for core in range(CORES)]
    weight = lax.all_gather(out_weight, "ctx", axis=0, axis_index_groups=core_groups)

    (mine,) = call(tails_kernel, [((3, ROWS, channels), BF16)], "tails", streams)
    before = from_behind(mine, "ctx", 1)
    heads, query, gated, decay, lift, toeplitz, step = call(
        prepare_kernel,
        [
            ((3, ROWS, channels), F32),
            ((length, channels), F32),
            ((length, channels), F32),
            ((2, groups * poles, length), BF16),
            ((2, length, groups * poles), BF16),
            ((groups // 2, length, 2 * length), BF16),
            ((poles, channels), F32),
        ],
        "prepare",
        streams, conv_weight, rates.T, residues.T,
        scratch=[pltpu.VMEM((3, ROWS + length, TILE), F32)],
        flops=10**9,
    )
    ends, gated, first = call(
        states_kernel,
        [((blocks, poles, channels), BF16), ((length, channels), BF16), ((ROWS, channels), F32)],
        "states",
        before, heads, conv_weight, gated, decay,
        scratch=[pltpu.VMEM((3, 2 * ROWS, TILE), F32)],
    )
    all_ends = lax.all_to_all(ends, "ctx", split_axis=0, concat_axis=0, tiled=True)
    (base,) = call(
        inside_kernel, [((length, channels), F32)], "inside", gated, toeplitz, skip[None, :], flops=10**9
    )
    me = lax.axis_index("ctx").astype(jnp.int32)[None]
    (mixed,) = call(
        finish_kernel,
        [((length, channels), BF16)],
        "finish",
        me, all_ends, step, lift, query, first, base,
        specs=[pl.BlockSpec(memory_space=pltpu.SMEM)] + whole(6),
        scratch=[pltpu.VMEM((poles, channels), F32)],
    )
    share = channels // CORES
    by_core = mixed.reshape(length, share // rows, CORES, rows).transpose(2, 0, 1, 3)
    copies = jnp.broadcast_to(
        by_core.reshape(CORES, 1, length, share), (CORES, layers, length, share)
    ).reshape(CORES * layers, length, share)
    columns = [
        [(chip * CORES + core) * layers + layer for core in range(CORES) for layer in range(layers)]
        for chip in range(blocks // CORES)
    ]
    arrived = lax.all_to_all(
        copies, ("ctx", "tp"), split_axis=0, concat_axis=0, axis_index_groups=columns, tiled=True
    ).reshape(CORES, layers, length, share)
    summed = jnp.einsum(
        "cltk,lke->cte", arrived, weight.reshape(layers, share, features), preferred_element_type=F32
    )
    core = lax.axis_index("ctx") % CORES
    other = lax.dynamic_index_in_dim(summed, 1 - core, 0, keepdims=False).astype(BF16)
    mine = lax.dynamic_index_in_dim(summed, core, 0, keepdims=False)
    other = lax.ppermute(other, "ctx", [(source, source ^ 1) for source in range(blocks)])
    return (mine + other.astype(F32)).astype(BF16)


def solution(mesh):
    return jax.shard_map(
        local,
        mesh=mesh,
        in_specs=(
            P(None, "tp", "ctx"),
            P(None, None, "tp"),
            P("tp", None),
            P("tp", None),
            P("tp"),
            P("ctx", "tp"),
        ),
        out_specs=P("ctx", "tp"),
        check_vma=False,
    )
```

time: 149 us -> 84.4 us (0.57)
  waiting for transfers between devices: 88.3 us -> 31.1 us
  Pallas kernels: 0 us -> 13.9 us
  blocking collectives: 12.2 us -> 0 us
  matrix products: 13 us -> 3.43 us
  other arithmetic: 7.46 us -> 0.76 us
  local copies, waits for them, and re-layouts: 4.34 us -> 8.88 us
  starting transfers between devices: 9.79 us -> 12.4 us
    all_gather x2 -> x1, waiting for transfers between devices: 82.5 us -> 0.01 us  [local(): lax.all_gather(out_weight, 'ctx', axis=0, axis_index_groups=core_groups)]
    all_to_all x1 -> x2, waiting for transfers between devices: 4.94 us -> 29.1 us  [the longest x1 26.1 us: local(): lax.all_to_all(copies, ('ctx', 'tp'), split_axis=0, concat_axis=0, axis_i...]
    pallas_call x0 -> x5, Pallas kernels: none -> 13.9 us  [call(): pl.pallas_call(kernel, out_shape=tuple((jax.ShapeDtypeStruct(*out) for ou...]
    all_to_all x1 -> x0, blocking collectives: 12.2 us -> none  [local(): lax.all_to_all(filtered_all, 'ctx', split_axis=1, concat_axis=0, tiled=True)]
    dot_general x6 -> x1, matrix products: 13 us -> 3.43 us  [local(): jnp.einsum('cltk,lke->cte', arrived, weight.reshape(layers, share, featur...]
    unnamed x17 -> x14, local copies, waits for them, and re-layouts: 0.45 us -> 7.56 us
    add x2 -> x0, other arithmetic: 5.58 us -> none  [the longest x1 5.58 us: local(): filtered + conv_weight[:, shift_by, :, None] * extended[:, :, rim_width -...]
    all_to_all x1 -> x2, starting transfers between devices: 7.35 us -> 9.62 us  [the longest x1 5 us: local(): lax.all_to_all(ends, 'ctx', split_axis=0, concat_axis=0, tiled=True)]
  transfers between devices with their start and end apart: 4 -> 5, of which waited for: 4 -> 3; matrix products, arithmetic and copies ran while one was open for 2% -> 2% of each run, Pallas kernels for 0% -> 17%
where the time goes in v3:
time: 84.4 us; the launch traced here: 83.9 us
  waiting for transfers between devices  31.1 us (37%)
  Pallas kernels  13.9 us (16%)
  between operations  13.5 us (16%)
  starting transfers between devices  12.4 us (15%)
  local copies, waits for them, and re-layouts  8.88 us (11%)
  matrix products  3.43 us (4%)
    all_to_all x1, waiting for transfers between devices, local(): lax.all_to_all(copies, ('ctx', 'tp'), split_axis=0, concat_axis=0, axis_i...  26.1 us
    pallas_call x5, Pallas kernels, call(): pl.pallas_call(kernel, out_shape=tuple((jax.ShapeDtypeStruct(*out) for ou...  13.9 us
    unnamed x14, local copies, waits for them, and re-layouts  7.56 us
    all_to_all x1, starting transfers between devices, local(): lax.all_to_all(ends, 'ctx', split_axis=0, concat_axis=0, tiled=True)  5 us
    all_to_all x1, starting transfers between devices, local(): lax.all_to_all(copies, ('ctx', 'tp'), split_axis=0, concat_axis=0, axis_i...  4.62 us
    dot_general x1, matrix products, local(): jnp.einsum('cltk,lke->cte', arrived, weight.reshape(layers, share, featur...  3.43 us
    all_to_all x1, waiting for transfers between devices, local(): lax.all_to_all(ends, 'ctx', split_axis=0, concat_axis=0, tiled=True)  3 us
    ppermute x1, starting transfers between devices, from_behind(): lax.ppermute(value, axis, [(source, source + steps) for source in range(l...  2.37 us
  transfers between devices with their start and end apart: 5, of which 3 were waited for; matrix products, arithmetic and copies ran while one was open for 2% of the time, Pallas kernels for 17%

profile of v3, /device:TPU:0, one launch (start us, length us, event | category | flops | bytes accessed | tf_op | source)
XLA Modules:
  0.0 83.9 jit_solution(6512098064800311182)
XLA Ops:
  6.5 0.0 copy-start.4
  6.5 0.0 all-gather.3.cloned.1.call-start
  6.5 0.7 all-gather.3.cloned.1.call-update
  7.3 0.0 copy-start.2
  7.3 1.1 %copy-done.2 = bf16[3,1024,128]{2,1,0:T(8,128)(2,1)S(1)} copy-done((bf16[3,1024,128]{2,1,0:T(8,128)(2,1)S(1)}, bf16[3,1024,128]{2,1,0:T(8,128)(2,1)}, u32[]{:S(2)}) %copy-start.2) | copy-done | bytes 786456
  8.4 0.3 tails.1
  8.7 2.4 %collective-permute-start = (bf16[3,8,1024]{2,1,0:T(8,128)(2,1)S(1)}, bf16[3,8,1024]{2,1,0:T(8,128)(2,1)S(1)}, u32[]{:S(2)}, u32[]{:S(2)}) collective-permute-start(bf16[3,8,1024]{2,1,0:T(8,128)(2,1)S(1)} %tails.1), channel_id=1, source_target_pairs={{0,4},{4,8},{8,12},{12,16},{16,20},{20,24},{24,28},{1,5},{5,9},{9,... | collective-permute-start | bytes 147464 | tf_op jit(solution)/shard_map/ppermute | solution.py:23
  11.1 0.0 copy-start.3
  11.1 0.9 %copy-done.3 = f32[3,7,1024]{2,1,0:T(8,128)S(1)} copy-done((f32[3,7,1024]{2,1,0:T(8,128)S(1)}, f32[3,7,1024]{2,1,0:T(8,128)}, u32[]{:S(2)}) %copy-start.3) | copy-done | bytes 86040
  12.0 0.0 copy-start.5
  12.0 0.7 copy-done.5
  12.7 0.7 copy-done.6
  13.4 5.4 %prepare.1 = (f32[3,8,1024]{2,1,0:T(8,128)S(1)}, f32[128,1024]{1,0:T(8,128)S(1)}, f32[128,1024]{1,0:T(8,128)S(1)}, bf16[2,2048,128]{2,1,0:T(8,128)(2,1)S(1)}, bf...) custom-call(bf16[3,1024,128]{2,1,0:T(8,128)(2,1)S(1)} %copy-done.2, ...), custom_call_target="tpu_custom_call" | custom-call | flops 1000000000 | bytes 1000000 | tf_op jit(solution)/shard_map/prepare/pallas_call | solution.py:52
  18.7 0.0 copy-start
  18.8 2.0 %copy-done = bf16[64,128,256]{2,1,0:T(8,128)(2,1)} copy-done((bf16[64,128,256]{2,1,0:T(8,128)(2,1)}, bf16[64,128,256]{2,1,0:T(8,128)(2,1)S(1)}, u32[]{:S(2)}) %copy-start) | copy-done | bytes 4194328
  20.7 0.0 collective-permute-done.before_ref
  20.7 2.4 %states.1 = (bf16[8,16,1024]{2,1,0:T(8,128)(2,1)}, bf16[128,1024]{1,0:T(8,128)(2,1)S(1)}, f32[8,1024]{1,0:T(8,128)S(1)}) custom-call(bf16[3,8,1024]{2,1,0:T(8,128)(2,1)S(1)} %collective-permute-done.before_ref, f32[3,8,1024]{2,1,0:T(8,128)S(1)} %get-tuple-element.15.heads_ref, f32[3,7,1024]{2,1,0:T(8,128)S(1)} %copy-done.3, ...), custom_call_target="tpu_custom_call" | custom-call | flops 100000000 | bytes 1000000 | tf_op jit(solution)/shard_map/states/pallas_call | solution.py:52
  23.1 5.0 %all-to-all-start = ((bf16[8,16,1024]{2,1,0:T(8,128)(2,1)}), bf16[8,16,1024]{2,1,0:T(8,128)(2,1)S(1)}, u32[]{:S(2)}, u32[]{:S(2)}) async-start(bf16[8,16,1024]{2,1,0:T(8,128)(2,1)} %get-tuple-element.18), calls=%async_computation | async-start | bytes 524288 | tf_op jit(solution)/shard_map/all_to_all | solution.py:248
  28.1 0.0 copy-done.4
  28.1 0.0 copy-start.1
  28.1 2.2 %copy-done.1 = bf16[64,128,256]{2,1,0:T(8,128)(2,1)S(1)} copy-done((bf16[64,128,256]{2,1,0:T(8,128)(2,1)S(1)}, bf16[64,128,256]{2,1,0:T(8,128)(2,1)}, u32[]{:S(2)}) %copy-start.1) | copy-done | bytes 4194328
  30.3 4.1 %inside.1.base_ref = f32[128,1024]{1,0:T(8,128)S(1)} custom-call(bf16[128,1024]{1,0:T(8,128)(2,1)S(1)} %get-tuple-element.23.gated_ref, bf16[64,128,256]{2,1,0:T(8,128)(2,1)S(1)} %copy-done.1, f32[1,1024]{1,0:T(1,128)S(1)} %bitcast.23), custom_call_target="tpu_custom_call" | custom-call | flops 1000000000 | bytes 1000000 | tf_op jit(solution)/shard_map/inside/pallas_call | solution.py:52
  34.4 3.0 %all-to-all-done.ends_ref = bf16[8,16,1024]{2,1,0:T(8,128)(2,1)S(1)} async-done(((bf16[8,16,1024]{2,1,0:T(8,128)(2,1)}), bf16[8,16,1024]{2,1,0:T(8,128)(2,1)S(1)}, u32[]{:S(2)}, u32[]{:S(2)}) %all-to-all-start) | async-done | bytes 262176 | tf_op jit(solution)/shard_map/all_to_all | solution.py:248
  37.4 1.8 %finish.1 = bf16[128,1024]{1,0:T(8,128)(2,1)S(1)} custom-call(s32[1]{0:T(128)} %bitcast.me_ref, bf16[8,16,1024]{2,1,0:T(8,128)(2,1)S(1)} %all-to-all-done.ends_ref, f32[16,1024]{1,0:T(8,128)S(1)} %get-tuple-element.19.step_ref, bf16[2,128,2048]{2,1,0:T(8,128)(2,1)S(1)} %get-tuple-element.20.lift_ref, f32[128,1024]{1,0:T(8,128)S(1)} %get-tuple-element.21.query_ref, ...), custom_call_target="tpu_custom_call" | custom-call | flops 100000000 | bytes 1000000 | tf_op jit(solution)/shard_map/finish/pallas_call | solution.py:52
  39.2 0.2 reshape.12
  39.4 1.1 %broadcast_in_dim.16 = bf16[2,4,128,512]{3,2,1,0:T(8,128)(2,1)} broadcast(bf16[2,128,512]{2,1,0:T(8,128)(2,1)S(1)} %copy.7), dimensions={0,2,3} | broadcast | bytes 1310720 | tf_op jit(solution)/shard_map/broadcast_in_dim | solution.py:263
  40.5 4.6 %all-to-all-start.1 = ((bf16[8,128,512]{2,1,0:T(8,128)(2,1)}), bf16[8,128,512]{2,1,0:T(8,128)(2,1)S(1)}, u32[]{:S(2)}, u32[]{:S(2)}) async-start(bf16[8,128,512]{2,1,0:T(8,128)(2,1)} %bitcast.6), calls=%async_computation.1 | async-start | bytes 2097152 | tf_op jit(solution)/shard_map/all_to_all | solution.py:270
  45.1 26.1 %all-to-all-done.1 = bf16[8,128,512]{2,1,0:T(8,128)(2,1)S(1)} async-done(((bf16[8,128,512]{2,1,0:T(8,128)(2,1)}), bf16[8,128,512]{2,1,0:T(8,128)(2,1)S(1)}, u32[]{:S(2)}, u32[]{:S(2)}) %all-to-all-start.1) | async-done | bytes 1048608 | tf_op jit(solution)/shard_map/all_to_all | solution.py:270
  71.2 3.4 %convolution_bitcast_fusion = f32[2,128,1024]{2,1,0:T(8,128)S(1)} fusion(bf16[2,4,128,512]{3,2,1,0:T(8,128)(2,1)S(1)} %bitcast.26, bf16[4,512,1024,1]{2,1,0,3:T(8,128)(2,1)} %bitcast.28), kind=kOutput, calls=%fused_computation | convolution fusion | flops 1073741824 | bytes 6291456 | tf_op jit(solution)/shard_map/cltk,lke->cte/dot_general | solution.py:273
  74.7 0.4 collective-permute-start.1
  75.1 1.2 %collective-permute-done.1 = bf16[128,1024]{1,0:T(8,128)(2,1)S(1)} collective-permute-done((bf16[128,1024]{1,0:T(8,128)(2,1)S(1)}, bf16[128,1024]{1,0:T(8,128)(2,1)S(1)}, u32[]{:S(2)}, u32[]{:S(2)}) %collective-permute-start.1) | collective-permute-done | bytes 262176 | tf_op jit(solution)/shard_map/ppermute | solution.py:279
  76.3 0.8 fusion
  (4 shorter events, 0.1 us)
Async XLA Ops:
  6.5 21.6 %copy-start.4 = (f32[1024]{0:T(1024)S(1)}, f32[1024]{0:T(1024)}, u32[]{:S(2)}) copy-start(f32[1024]{0:T(1024)} %param.10) | copy-start | bytes 12292
  6.5 64.7 %all-gather.3.cloned.1.call-start = ((), (), s32[]{:S(2)}) async-start(), calls=%async_computation.2 | async-start | bytes 5242880 | tf_op jit(solution)/shard_map/all_gather | solution.py:221
  7.3 1.1 %copy-start.2 = (bf16[3,1024,128]{2,1,0:T(8,128)(2,1)S(1)}, bf16[3,1024,128]{2,1,0:T(8,128)(2,1)}, u32[]{:S(2)}) copy-start(bf16[3,1024,128]{2,1,0:T(8,128)(2,1)} %streams_ref.3) | copy-start | bytes 2359300
  8.7 12.0 %collective-permute-start = (bf16[3,8,1024]{2,1,0:T(8,128)(2,1)S(1)}, bf16[3,8,1024]{2,1,0:T(8,128)(2,1)S(1)}, u32[]{:S(2)}, u32[]{:S(2)}) collective-permute-start(bf16[3,8,1024]{2,1,0:T(8,128)(2,1)S(1)} %tails.1), channel_id=1, source_target_pairs={{0,4},{4,8},{8,12},{12,16},{16,20},{20,24},{24,28},{1,5},{5,9},{9,... | collective-permute-start | bytes 147464 | tf_op jit(solution)/shard_map/ppermute | solution.py:23
  11.1 0.9 %copy-start.3 = (f32[3,7,1024]{2,1,0:T(8,128)S(1)}, f32[3,7,1024]{2,1,0:T(8,128)}, u32[]{:S(2)}) copy-start(f32[3,7,1024]{2,1,0:T(8,128)} %taps_ref.3) | copy-start | bytes 258052
  12.0 0.7 copy-start.5
  12.7 0.7 copy-start.6
  18.7 2.0 %copy-start = (bf16[64,128,256]{2,1,0:T(8,128)(2,1)}, bf16[64,128,256]{2,1,0:T(8,128)(2,1)S(1)}, u32[]{:S(2)}) copy-start(bf16[64,128,256]{2,1,0:T(8,128)(2,1)S(1)} %get-tuple-element.24.toeplitz_ref) | copy-start | bytes 12582916
  23.1 14.3 %all-to-all-start = ((bf16[8,16,1024]{2,1,0:T(8,128)(2,1)}), bf16[8,16,1024]{2,1,0:T(8,128)(2,1)S(1)}, u32[]{:S(2)}, u32[]{:S(2)}) async-start(bf16[8,16,1024]{2,1,0:T(8,128)(2,1)} %get-tuple-element.18), calls=%async_computation | async-start | bytes 524288 | tf_op jit(solution)/shard_map/all_to_all | solution.py:248
  28.1 2.2 %copy-start.1 = (bf16[64,128,256]{2,1,0:T(8,128)(2,1)S(1)}, bf16[64,128,256]{2,1,0:T(8,128)(2,1)}, u32[]{:S(2)}) copy-start(bf16[64,128,256]{2,1,0:T(8,128)(2,1)} %copy-done) | copy-start | bytes 12582916
  40.5 30.7 %all-to-all-start.1 = ((bf16[8,128,512]{2,1,0:T(8,128)(2,1)}), bf16[8,128,512]{2,1,0:T(8,128)(2,1)S(1)}, u32[]{:S(2)}, u32[]{:S(2)}) async-start(bf16[8,128,512]{2,1,0:T(8,128)(2,1)} %bitcast.6), calls=%async_computation.1 | async-start | bytes 2097152 | tf_op jit(solution)/shard_map/all_to_all | solution.py:270
  74.7 1.6 %collective-permute-start.1 = (bf16[128,1024]{1,0:T(8,128)(2,1)S(1)}, bf16[128,1024]{1,0:T(8,128)(2,1)S(1)}, u32[]{:S(2)}, u32[]{:S(2)}) collective-permute-start(bf16[128,1024]{1,0:T(8,128)(2,1)S(1)} %fusion.1), channel_id=1, source_target_pairs={{0,4},{4,0},{8,12},{12,8},{16,20},{20,16},{24,28},{28,24},{1,5},{5... | collective-permute-start | bytes 786440 | tf_op jit(solution)/shard_map/ppermute | solution.py:279
Sparse Core Ops, SparseCore 0:
  9.2 58.2 all-gather.2

commit v4 on v3

v4 whole, which is shorter than its diff:
```python
import functools
import math

import jax
import jax.numpy as jnp
from jax import lax
from jax.experimental import pallas as pl
from jax.experimental.pallas import tpu as pltpu
from jax.sharding import PartitionSpec as P

F32 = jnp.float32
BF16 = jnp.bfloat16
ROWS = 8
TILE = 128
CORES = 2
VMEM_LIMIT = 24 * 1024 * 1024
FETCH_LIMIT = 58 * 1024 * 1024
PLAIN = (((1,), (0,)), ((), ()))
CONTRACT_LANES = (((1,), (1,)), ((), ()))


def from_behind(value, axis, steps):
    count = lax.axis_size(axis)
    leading, last = (max(0, -steps), min(count, count - steps))
    return lax.ppermute(value, axis, [(source, source + steps) for source in range(leading, last)])


def dot(left, right, dims=PLAIN):
    return lax.dot_general(left, right, dims, preferred_element_type=F32)


def halves(value):
    high = value.astype(BF16)
    return high, (value - high.astype(F32)).astype(BF16)


def iota(shape, axis):
    return lax.broadcasted_iota(jnp.int32, shape, axis)


def identity(size):
    return (iota((size, size), 0) == iota((size, size), 1)).astype(BF16)


def turned(value, unit):
    return dot(unit, value, CONTRACT_LANES)


def whole(count):
    return [pl.BlockSpec(memory_space=pltpu.VMEM)] * count


def call(kernel, outs, name, *operands, specs=None, scratch=(), flops=10**8, limit=VMEM_LIMIT):
    return pl.pallas_call(
        kernel,
        out_shape=tuple(jax.ShapeDtypeStruct(*out) for out in outs),
        in_specs=whole(len(operands)) if specs is None else specs,
        out_specs=tuple(whole(len(outs))),
        scratch_shapes=scratch,
        compiler_params=pltpu.CompilerParams(vmem_limit_bytes=limit),
        cost_estimate=pl.CostEstimate(flops=flops, bytes_accessed=10**6, transcendentals=0),
        name=name,
    )(*operands)


def tile_of(index, size=TILE):
    return pl.ds(pl.multiple_of(index * size, size), size)


def unrolled(count, body):
    def step(index, carry):
        body(index)
        return carry

    lax.fori_loop(0, count, step, 0, unroll=math.gcd(count, 4))


def tails_kernel(
    streams_hbm, taps_hbm, rates_hbm, residues_hbm, skip_hbm,
    tails_ref, streams_ref, taps_ref, rates_ref, residues_ref, skip_ref, sems,
):
    pairs = [
        (streams_hbm, streams_ref),
        (taps_hbm, taps_ref),
        (rates_hbm, rates_ref),
        (residues_hbm, residues_ref),
        (skip_hbm, skip_ref),
    ]
    copies = [pltpu.make_async_copy(src, dst, sems.at[at]) for at, (src, dst) in enumerate(pairs)]
    for copy in copies:
        copy.start()
    for copy in copies:
        copy.wait()
    length = streams_ref.shape[2]
    pick = (iota((2 * ROWS, length), 1) == iota((2 * ROWS, length), 0) + (length - ROWS)).astype(BF16)
    for stream in range(streams_ref.shape[0]):
        rows = dot(pick, streams_ref[stream], CONTRACT_LANES)
        tails_ref[stream] = rows[:ROWS].astype(BF16)


def short_conv(stream, chans, rows, padded, taps_ref):
    total = None
    for shift in range(taps_ref.shape[1]):
        term = taps_ref[stream, shift : shift + 1, chans] * padded[pl.ds(ROWS - shift, rows), :]
        total = term if total is None else total + term
    return total


def prepare_kernel(streams_ref, taps_ref, rates_ref, heads_ref, query_ref, gated_ref, decay_ref, step_ref, padded_ref):
    channels, length = streams_ref.shape[1:]
    poles, groups = rates_ref.shape
    width = channels // groups
    in_tile = TILE // width
    unit = identity(length)
    lag = (length - 1) - iota((poles, length), 1).astype(F32)
    owner = iota((poles, TILE), 1) // width

    def turn(index):
        chans = tile_of(index)
        for stream in range(3):
            tokens = turned(streams_ref[stream, chans, :], unit)
            padded_ref[index * 3 + stream, :ROWS, :] = jnp.zeros((ROWS, TILE), F32)
            padded_ref[index * 3 + stream, ROWS:, :] = tokens
            heads_ref[stream, :, chans] = tokens[:ROWS]

    def decays(index):
        rates = pltpu.roll(rates_ref[...], groups - index * in_tile, 1)
        decay = []
        wide = jnp.zeros((poles, TILE), F32)
        for g in range(in_tile):
            rate = jnp.broadcast_to(rates[:, g : g + 1], (poles, length))
            decay.append(jnp.exp(-rate * lag))
            wide = jnp.where(owner == g, rate[:, :TILE], wide)
        step_ref[:, tile_of(index)] = jnp.exp(-wide * length)
        for part, value in enumerate(halves(jnp.concatenate(decay, axis=0))):
            decay_ref[part, tile_of(index, in_tile * poles), :] = value

    def filters(index):
        chans = tile_of(index)
        query, left, right = (
            short_conv(stream, chans, length, padded_ref.at[index * 3 + stream], taps_ref) for stream in range(3)
        )
        query_ref[:, chans] = query
        gated_ref[:, chans] = left * right

    unrolled(channels // TILE, turn)
    unrolled(channels // TILE, decays)
    unrolled(channels // TILE, filters)


def states_kernel(before_ref, heads_ref, taps_ref, gated_ref, decay_ref, ends_ref, final_ref, first_ref, padded_ref):
    length, channels = gated_ref.shape
    poles = ends_ref.shape[1]
    in_tile = decay_ref.shape[1] // poles * TILE // channels
    owner = iota((poles, TILE), 1) // (TILE // in_tile)

    def begin(index):
        chans = tile_of(index)
        for stream in range(3):
            padded_ref[index * 3 + stream, :ROWS, :] = before_ref[stream, :, chans].astype(F32)
            padded_ref[index * 3 + stream, ROWS:, :] = heads_ref[stream, :, chans]
        query, left, right = (
            short_conv(stream, chans, ROWS, padded_ref.at[index * 3 + stream], taps_ref) for stream in range(3)
        )
        first_ref[:, chans] = query
        final_ref[:, chans] = jnp.concatenate([left * right, gated_ref[ROWS:, chans]], axis=0).astype(BF16)

    def leave(index):
        chans = tile_of(index)
        gated = final_ref[:, chans]
        states = tile_of(index, in_tile * poles)
        every = dot(decay_ref[0, states, :], gated) + dot(decay_ref[1, states, :], gated)
        ends = jnp.zeros((poles, TILE), F32)
        for g in range(in_tile):
            ends = jnp.where(owner == g, every[g * poles : (g + 1) * poles], ends)
        ends = ends.astype(BF16)
        for block in range(ends_ref.shape[0]):
            ends_ref[block, :, chans] = ends

    unrolled(channels // TILE, begin)
    unrolled(channels // TILE, leave)


def inside_kernel(gated_ref, skip_ref, rates_ref, residues_ref, lift_ref, base_ref):
    length, channels = gated_ref.shape
    poles, groups = rates_ref.shape
    width = channels // groups
    in_tile = TILE // width
    unit = identity(length)
    time = iota((poles, length), 1).astype(F32)
    member = (iota((in_tile, in_tile * poles), 1) // poles == iota((in_tile, in_tile * poles), 0)).astype(BF16)
    causal = iota((length, length), 1) >= iota((length, length), 0)

    def tile(index):
        chans = tile_of(index)
        shift = groups - index * in_tile
        rates = pltpu.roll(rates_ref[...], shift, 1)
        coef = pltpu.roll(residues_ref[...], shift, 1) * jnp.sqrt(2.0 * rates) / math.sqrt(poles)
        impulse, lift = [], []
        for g in range(in_tile):
            rate = jnp.broadcast_to(rates[:, g : g + 1], (poles, length))
            scale = jnp.broadcast_to(coef[:, g : g + 1], (poles, length))
            impulse.append(scale * jnp.exp(-rate * time))
            lift.append(scale * jnp.exp(-rate * (time + 1.0)))
        states = tile_of(index, in_tile * poles)
        for part, value in enumerate(halves(jnp.concatenate(lift, axis=0))):
            lift_ref[part, :, states] = turned(value, unit).astype(BF16)
        high, low = halves(jnp.concatenate(impulse, axis=0))
        response = dot(member, high) + dot(member, low)
        gated = gated_ref[:, chans]
        signal = turned(gated, unit).astype(BF16)
        parts = []
        for pair in range(in_tile // 2):
            blocks = []
            for g in (2 * pair, 2 * pair + 1):
                spread = jnp.broadcast_to(response[g : g + 1], (length, length))
                shifted = pltpu.roll(spread, 0, 1, stride=1, stride_axis=0)
                blocks.append(jnp.where(causal, shifted, 0.0).astype(BF16))
            both = dot(signal[pair * 2 * width : (pair + 1) * 2 * width], jnp.concatenate(blocks, axis=1))
            parts += [both[:width, :length], both[width:, length:]]
        high, low = halves(jnp.concatenate(parts, axis=0))
        base_ref[:, chans] = turned(high, unit) + turned(low, unit) + skip_ref[:, chans] * gated.astype(F32)

    unrolled(channels // TILE, tile)


def finish_kernel(at_ref, ends_ref, step_ref, lift_ref, query_ref, first_ref, base_ref, mine_ref, other_ref, mixed_ref, state_ref):
    length, channels = mixed_ref.shape
    poles = step_ref.shape[0]
    in_tile = lift_ref.shape[2] // poles * TILE // channels
    me, core = at_ref[0], at_ref[1]

    def earlier(block, state):
        return jnp.where(block < me, step_ref[...] * state + ends_ref[block].astype(F32), state)

    state_ref[...] = lax.fori_loop(0, ends_ref.shape[0] - 1, earlier, jnp.zeros((poles, channels), F32))
    owner = iota((poles, TILE), 1) // (TILE // in_tile)

    def tile(index):
        chans = tile_of(index)
        entering = state_ref[:, chans]
        apart = jnp.concatenate([jnp.where(owner == g, entering, 0.0) for g in range(in_tile)], axis=0)
        high, low = halves(apart)
        states = tile_of(index, in_tile * poles)
        lift = lift_ref[0, :, states]
        carried = dot(lift, high) + dot(lift, low) + dot(lift_ref[1, :, states], high)
        query = jnp.concatenate([first_ref[:, chans], query_ref[ROWS:, chans]], axis=0)
        mixed_ref[:, chans] = (query * (base_ref[:, chans] + carried)).astype(BF16)

    unrolled(channels // TILE, tile)
    share = channels // CORES
    mine_ref[...] = mixed_ref[:, tile_of(core, share)]
    other_ref[...] = mixed_ref[:, tile_of(1 - core, share)]


def project_kernel(place, at_ref, own_ref, below_ref, above_ref, middle_ref, far_ref, weight_hbm, mine_ref, other_ref, weight_ref, sems):
    layer = at_ref[0]
    edge = (layer == 0) | (layer == 3)
    sources = [layer, jnp.where(layer == 0, 1, layer - 1), (layer + 2) % 4, jnp.where(edge, 3 - layer, layer + 1)]
    copies = []
    for at, source in enumerate(sources):
        row = sum(jnp.where(source == index, place[index], 0) for index in range(4))
        copies.append(pltpu.make_async_copy(weight_hbm.at[row], weight_ref.at[at], sems.at[at]))
        copies[-1].start()
    blocks = [
        lambda: own_ref[...],
        lambda: jnp.where(layer == 0, above_ref[...], below_ref[...]),
        lambda: middle_ref[...],
        lambda: jnp.where(edge, far_ref[...], above_ref[...]),
    ]
    total = None
    for copy, block, rows in zip(copies, blocks, range(4)):
        copy.wait()
        term = dot(block(), weight_ref[rows])
        total = term if total is None else total + term
    length = mine_ref.shape[0]
    mine_ref[...] = total[:length]
    other_ref[...] = total[length:].astype(BF16)


def over_layers(block):
    layer = lax.axis_index("tp")
    below = lax.ppermute(block, "tp", [(0, 1), (1, 2), (2, 3)])
    above = lax.ppermute(block, "tp", [(1, 0), (2, 1), (3, 2)])
    far = lax.ppermute(block, "tp", [(0, 3), (3, 0)])
    onward = jnp.where(layer == 1, above, jnp.where(layer == 2, below, block))
    middle = lax.ppermute(onward, "tp", [(0, 2), (3, 1), (2, 3), (1, 0)])
    return below, above, middle, far


def local(streams, conv_weight, rates, residues, skip, out_weight):
    channels, length = streams.shape[1:]
    groups, poles = rates.shape
    blocks, layers = lax.axis_size("ctx"), lax.axis_size("tp")
    rows, features = out_weight.shape
    share = channels // CORES
    chips = blocks // CORES
    ring = [0, 1, 3, 2] if chips == 4 and rows == share else list(range(chips))
    core_groups = [[chip * CORES + core for chip in ring] for core in range(CORES)]
    weight = lax.all_gather(out_weight, "ctx", axis=0, axis_index_groups=core_groups)
    weight = weight.reshape(layers, share, features)
    place = ring if rows == share else list(range(layers))

    tails, streams, conv_weight, rates, residues, skip = call(
        tails_kernel,
        [
            ((3, ROWS, channels), BF16),
            (streams.shape, BF16),
            (conv_weight.shape, F32),
            ((poles, groups), F32),
            ((poles, groups), F32),
            ((1, channels), F32),
        ],
        "tails",
        streams, conv_weight, rates.T, residues.T, skip[None, :],
        specs=[pl.BlockSpec(memory_space=pltpu.HBM)] * 5,
        scratch=[pltpu.SemaphoreType.DMA((5,))],
        limit=FETCH_LIMIT,
    )
    before = from_behind(tails, "ctx", 1)
    tiles = channels // TILE
    heads, query, gated, decay, step = call(
        prepare_kernel,
        [
            ((3, ROWS, channels), F32),
            ((length, channels), F32),
            ((length, channels), F32),
            ((2, groups * poles, length), BF16),
            ((poles, channels), F32),
        ],
        "prepare",
        streams, conv_weight, rates,
        scratch=[pltpu.VMEM((3 * tiles, ROWS + length, TILE), F32)],
        flops=10**9,
    )
    ends, gated, first = call(
        states_kernel,
        [((blocks, poles, channels), BF16), ((length, channels), BF16), ((ROWS, channels), F32)],
        "states",
        before, heads, conv_weight, gated, decay,
        scratch=[pltpu.VMEM((3 * tiles, 2 * ROWS, TILE), F32)],
    )
    all_ends = lax.all_to_all(ends, "ctx", split_axis=0, concat_axis=0, tiled=True)
    lift, base = call(
        inside_kernel,
        [((2, length, groups * poles), BF16), ((length, channels), F32)],
        "inside",
        gated, skip, rates, residues,
        flops=10**9,
    )
    me = lax.axis_index("ctx").astype(jnp.int32)
    core = me % CORES
    smem = [pl.BlockSpec(memory_space=pltpu.SMEM)]
    outs = [((length, share), BF16), ((length, share), BF16), ((length, channels), BF16)]
    mine, other, mixed = call(
        finish_kernel,
        outs,
        "finish",
        jnp.stack([me, core]), all_ends, step, lift, query, first, base,
        specs=smem + whole(6),
        scratch=[pltpu.VMEM((poles, channels), F32)],
    )
    if rows != share:
        by_core = mixed.reshape(length, share // rows, CORES, rows).transpose(2, 0, 1, 3)
        by_core = by_core.reshape(CORES, length, share)
        mine = lax.dynamic_index_in_dim(by_core, core, 0, keepdims=False)
        other = lax.dynamic_index_in_dim(by_core, 1 - core, 0, keepdims=False)
    siblings = [(source, source ^ 1) for source in range(blocks)]
    block = jnp.concatenate([mine, lax.ppermute(other, "ctx", siblings)], axis=0)
    layer = lax.axis_index("tp").astype(jnp.int32)
    mine, other = call(
        functools.partial(project_kernel, place),
        [((length, features), F32), ((length, features), BF16)],
        "project",
        layer[None], block, *over_layers(block), weight,
        specs=smem + whole(5) + [pl.BlockSpec(memory_space=pltpu.HBM)],
        scratch=[pltpu.VMEM((layers, share, features), BF16), pltpu.SemaphoreType.DMA((layers,))],
        limit=FETCH_LIMIT,
    )
    other = lax.ppermute(other, "ctx", siblings)
    return (mine + other.astype(F32)).astype(BF16)


def solution(mesh):
    return jax.shard_map(
        local,
        mesh=mesh,
        in_specs=(
            P(None, "tp", "ctx"),
            P(None, None, "tp"),
            P("tp", None),
            P("tp", None),
            P("tp"),
            P("ctx", "tp"),
        ),
        out_specs=P("ctx", "tp"),
        check_vma=False,
    )
```

time: 84.4 us -> 80 us (0.948)
  waiting for transfers between devices: 31.1 us -> 19.6 us
  starting transfers between devices: 12.4 us -> 22.5 us
  local copies, waits for them, and re-layouts: 8.88 us -> 3.46 us
  Pallas kernels: 13.9 us -> 18.4 us
  matrix products: 3.43 us -> 0 us
  other arithmetic: 0.76 us -> 1.92 us
    all_to_all x1 -> x0, waiting for transfers between devices: 26.1 us -> none  [local(): lax.all_to_all(copies, ('ctx', 'tp'), split_axis=0, concat_axis=0, axis_i...]
    ppermute x1 -> x6, starting transfers between devices: 0.36 us -> 15.2 us  [the longest x1 6.57 us: over_layers(): far = lax.ppermute(block, 'tp', [(0, 3), (3, 0)])]
    ppermute x1 -> x6, waiting for transfers between devices: 1.24 us -> 13.9 us  [the longest x1 5 us: over_layers(): far = lax.ppermute(block, 'tp', [(0, 3), (3, 0)])]
    all_to_all x1 -> x0, starting transfers between devices: 4.62 us -> none  [local(): lax.all_to_all(copies, ('ctx', 'tp'), split_axis=0, concat_axis=0, axis_i...]
    pallas_call x5 -> x6, Pallas kernels: 13.9 us -> 18.4 us  [call(): pl.pallas_call(kernel, out_shape=tuple((jax.ShapeDtypeStruct(*out) for ou...]
    unnamed x14 -> x23, local copies, waits for them, and re-layouts: 7.56 us -> 3.45 us
    dot_general x1 -> x0, matrix products: 3.43 us -> none  [local(): jnp.einsum('cltk,lke->cte', arrived, weight.reshape(layers, share, featur...]
    all_to_all x1, waiting for transfers between devices: 3 us -> 4.93 us  [local(): lax.all_to_all(ends, 'ctx', split_axis=0, concat_axis=0, tiled=True)]
  transfers between devices with their start and end apart: 5 -> 9, of which waited for: 3 -> 6; matrix products, arithmetic and copies ran while one was open for 2% -> 0% of each run, Pallas kernels for 17% -> 17%
where the time goes in v4:
time: 80 us; the launch traced here: 79.5 us
  starting transfers between devices  22.5 us (28%)
  waiting for transfers between devices  19.6 us (25%)
  Pallas kernels  18.4 us (23%)
  between operations  13.6 us (17%)
  local copies, waits for them, and re-layouts  3.46 us (4%)
  other arithmetic  1.92 us (2%)
    pallas_call x6, Pallas kernels, call(): pl.pallas_call(kernel, out_shape=tuple((jax.ShapeDtypeStruct(*out) for ou...  18.4 us
    ppermute x1, starting transfers between devices, over_layers(): far = lax.ppermute(block, 'tp', [(0, 3), (3, 0)])  6.57 us
    ppermute x1, waiting for transfers between devices, over_layers(): far = lax.ppermute(block, 'tp', [(0, 3), (3, 0)])  5 us
    all_to_all x1, starting transfers between devices, local(): lax.all_to_all(ends, 'ctx', split_axis=0, concat_axis=0, tiled=True)  4.99 us
    all_to_all x1, waiting for transfers between devices, local(): lax.all_to_all(ends, 'ctx', split_axis=0, concat_axis=0, tiled=True)  4.93 us
    ppermute x1, waiting for transfers between devices, over_layers(): middle = lax.ppermute(onward, 'tp', [(0, 2), (3, 1), (2, 3), (1, 0)])  3.8 us
    ppermute x1, starting transfers between devices, over_layers(): middle = lax.ppermute(onward, 'tp', [(0, 2), (3, 1), (2, 3), (1, 0)])  3.74 us
    ppermute x1, starting transfers between devices, over_layers(): below = lax.ppermute(block, 'tp', [(0, 1), (1, 2), (2, 3)])  3.5 us
  transfers between devices with their start and end apart: 9, of which 6 were waited for; matrix products, arithmetic and copies ran while one was open for 0% of the time, Pallas kernels for 17%

profile of v4, /device:TPU:0, one launch (start us, length us, event | category | flops | bytes accessed | tf_op | source)
XLA Modules:
  0.0 79.5 jit_solution(12901078888821841240)
XLA Ops:
  6.5 0.7 all-gather.3.cloned.1.call-update
  7.3 2.1 %tails.1 = (bf16[3,8,1024]{2,1,0:T(8,128)(2,1)}, bf16[3,1024,128]{2,1,0:T(8,128)(2,1)}, f32[3,7,1024]{2,1,0:T(8,128)}, f32[16,128]{1,0:T(8,128)}, f32[16,128]{1,0:T(8,128)}, /*index=5*/f32[1,1024]{1,0:T(1,128)}) custom-call(bf16[3,1024,128]{2,1,0:T(8,128)(2,1)} %streams_hbm.1, f32[3,7,1024]{2,1,0:T(8,128)} %taps_hbm.1, f32[16,128]{1,0:T(8,128)} %bitcast.8, ...), custom_call_target="tpu_custom_call" | custom-call | flops 100000000 | bytes 1000000 | tf_op jit(solution)/shard_map/tails/pallas_call | solution.py:54
  9.4 2.4 %collective-permute-start = (bf16[3,8,1024]{2,1,0:T(8,128)(2,1)}, bf16[3,8,1024]{2,1,0:T(8,128)(2,1)S(1)}, u32[]{:S(2)}, u32[]{:S(2)}) collective-permute-start(bf16[3,8,1024]{2,1,0:T(8,128)(2,1)} %get-tuple-element.25), channel_id=1, source_target_pairs={{0,4},{4,8},{8,12},{12,16},{16,20},{20,24},{24,28},{1,5},{5,9},{9,... | collective-permute-start | bytes 147464 | tf_op jit(solution)/shard_map/ppermute | solution.py:25
  11.8 0.0 copy-start
  11.8 0.9 %copy-done = f32[3,7,1024]{2,1,0:T(8,128)S(1)} copy-done((f32[3,7,1024]{2,1,0:T(8,128)S(1)}, f32[3,7,1024]{2,1,0:T(8,128)}, u32[]{:S(2)}) %copy-start) | copy-done | bytes 86040
  12.7 1.1 %copy-done.1 = bf16[3,1024,128]{2,1,0:T(8,128)(2,1)S(1)} copy-done((bf16[3,1024,128]{2,1,0:T(8,128)(2,1)S(1)}, bf16[3,1024,128]{2,1,0:T(8,128)(2,1)}, u32[]{:S(2)}) %copy-start.1) | copy-done | bytes 786456
  13.8 0.7 copy-done.2
  14.5 2.6 %prepare.1 = (f32[3,8,1024]{2,1,0:T(8,128)S(1)}, f32[128,1024]{1,0:T(8,128)S(1)}, f32[128,1024]{1,0:T(8,128)S(1)}, bf16[2,2048,128]{2,1,0:T(8,128)(2,1)S(1)}, f32[16,1024]{1,0:T(8,128)S(1)}) custom-call(bf16[3,1024,128]{2,1,0:T(8,128)(2,1)S(1)} %copy-done.1, f32[3,7,1024]{2,1,0:T(8,128)S(1)} %copy-done, f32[16,128]{1,0:T(8,128)S(1)} %copy-done.2), custom_call_target="tpu_custom_call" | custom-call | flops 1000000000 | bytes 1000000 | tf_op jit(solution)/shard_map/prepare/pallas_call | solution.py:54
  17.1 0.0 collective-permute-done.before_ref
  17.1 1.5 %states.1 = (bf16[8,16,1024]{2,1,0:T(8,128)(2,1)}, bf16[128,1024]{1,0:T(8,128)(2,1)S(1)}, f32[8,1024]{1,0:T(8,128)S(1)}) custom-call(bf16[3,8,1024]{2,1,0:T(8,128)(2,1)S(1)} %collective-permute-done.before_ref, f32[3,8,1024]{2,1,0:T(8,128)S(1)} %get-tuple-element.29.heads_ref, f32[3,7,1024]{2,1,0:T(8,128)S(1)} %copy-done, ...), custom_call_target="tpu_custom_call" | custom-call | flops 100000000 | bytes 1000000 | tf_op jit(solution)/shard_map/states/pallas_call | solution.py:54
  18.6 5.0 %all-to-all-start = ((bf16[8,16,1024]{2,1,0:T(8,128)(2,1)}), bf16[8,16,1024]{2,1,0:T(8,128)(2,1)S(1)}, u32[]{:S(2)}, u32[]{:S(2)}) async-start(bf16[8,16,1024]{2,1,0:T(8,128)(2,1)} %get-tuple-element.32), calls=%async_computation | async-start | bytes 524288 | tf_op jit(solution)/shard_map/all_to_all | solution.py:343
  23.6 0.1 pad_add_fusion.at_ref
  23.7 0.0 copy-done.3
  23.7 5.0 %inside.1 = (bf16[2,128,2048]{2,1,0:T(8,128)(2,1)S(1)}, f32[128,1024]{1,0:T(8,128)S(1)}) custom-call(bf16[128,1024]{1,0:T(8,128)(2,1)S(1)} %get-tuple-element.34.gated_ref, f32[1,1024]{1,0:T(1,128)S(1)} %copy-done.5, f32[16,128]{1,0:T(8,128)S(1)} %copy-done.3, f32[16,128]{1,0:T(8,128)S(1)} %copy-done.4), custom_call_target="tpu_custom_call" | custom-call | flops 1000000000 | bytes 1000000 | tf_op jit(solution)/shard_map/inside/pallas_call | solution.py:54
  28.8 4.9 %all-to-all-done.ends_ref = bf16[8,16,1024]{2,1,0:T(8,128)(2,1)S(1)} async-done(((bf16[8,16,1024]{2,1,0:T(8,128)(2,1)}), bf16[8,16,1024]{2,1,0:T(8,128)(2,1)S(1)}, u32[]{:S(2)}, u32[]{:S(2)}) %all-to-all-start) | async-done | bytes 262176 | tf_op jit(solution)/shard_map/all_to_all | solution.py:343
  33.7 2.1 %finish.1 = (bf16[128,512]{1,0:T(8,128)(2,1)S(1)}, bf16[128,512]{1,0:T(8,128)(2,1)S(1)}, bf16[128,1024]{1,0:T(8,128)(2,1)}) custom-call(s32[2]{0:T(128)S(1)} %pad_add_fusion.at_ref, bf16[8,16,1024]{2,1,0:T(8,128)(2,1)S(1)} %all-to-all-done.ends_ref, f32[16,1024]{1,0:T(8,128)S(1)} %get-tuple-element.33.step_ref, ...), custom_call_target="tpu_custom_call" | custom-call | flops 100000000 | bytes 1000000 | tf_op jit(solution)/shard_map/finish/pallas_call | solution.py:54
  35.8 0.0 collective-permute-start.1
  35.8 1.3 %collective-permute-done.1 = bf16[128,512]{1,0:T(8,128)(2,1)S(1)} collective-permute-done((bf16[128,512]{1,0:T(8,128)(2,1)S(1)}, bf16[128,512]{1,0:T(8,128)(2,1)S(1)}, u32[]{:S(2)}, u32[]{:S(2)}) %collective-permute-start.1) | collective-permute-done | bytes 131104 | tf_op jit(solution)/shard_map/ppermute | solution.py:369
  37.1 0.0 copy-start.6
  37.1 3.5 %collective-permute-start.2 = (bf16[256,512]{1,0:T(8,128)(2,1)S(1)}, bf16[256,512]{1,0:T(8,128)(2,1)S(1)}, u32[]{:S(2)}, u32[]{:S(2)}) collective-permute-start(bf16[256,512]{1,0:T(8,128)(2,1)S(1)} %constant_dynamic-update-slice_fusion.own_ref), channel_id=1, source_target_pairs={{0,1},{1,2},{2,3},{4,5},{5,6},{6,7},{8,9},{9,10},{10,11},{12,13},{... | collective-permute-start | bytes 786440 | tf_op jit(solution)/shard_map/ppermute | solution.py:283
  40.7 1.3 %collective-permute-start.3 = (bf16[256,512]{1,0:T(8,128)(2,1)S(1)}, bf16[256,512]{1,0:T(8,128)(2,1)S(1)}, u32[]{:S(2)}, u32[]{:S(2)}) collective-permute-start(bf16[256,512]{1,0:T(8,128)(2,1)S(1)} %constant_dynamic-update-slice_fusion.own_ref), channel_id=1, source_target_pairs={{1,0},{2,1},{3,2},{5,4},{6,5},{7,6},{9,8},{10,9},{11,10},{13,12},{... | collective-permute-start | bytes 786440 | tf_op jit(solution)/shard_map/ppermute | solution.py:284
  42.0 6.6 %collective-permute-start.5 = (bf16[256,512]{1,0:T(8,128)(2,1)S(1)}, bf16[256,512]{1,0:T(8,128)(2,1)S(1)}, u32[]{:S(2)}, u32[]{:S(2)}) collective-permute-start(bf16[256,512]{1,0:T(8,128)(2,1)S(1)} %constant_dynamic-update-slice_fusion.own_ref), channel_id=1, source_target_pairs={{0,3},{3,0},{4,7},{7,4},{8,11},{11,8},{12,15},{15,12},{16,19},{19,... | collective-permute-start | bytes 786440 | tf_op jit(solution)/shard_map/ppermute | solution.py:285
  48.5 0.0 collective-permute-done.2.below_ref
  48.6 2.1 %collective-permute-done.3.above_ref = bf16[256,512]{1,0:T(8,128)(2,1)S(1)} collective-permute-done((bf16[256,512]{1,0:T(8,128)(2,1)S(1)}, bf16[256,512]{1,0:T(8,128)(2,1)S(1)}, u32[]{:S(2)}, u32[]{:S(2)}) %collective-permute-start.3) | collective-permute-done | bytes 262176 | tf_op jit(solution)/shard_map/ppermute | solution.py:284
  50.7 3.7 %collective-permute-start.4 = (bf16[256,512]{1,0:T(8,128)(2,1)S(1)}, bf16[256,512]{1,0:T(8,128)(2,1)S(1)}, u32[]{:S(2)}, u32[]{:S(2)}) collective-permute-start(bf16[256,512]{1,0:T(8,128)(2,1)S(1)} %select_select_fusion), channel_id=1, source_target_pairs={{0,2},{3,1},{2,3},{1,0},{4,6},{7,5},{6,7},{5,4},{8,10},{11,9},{10,... | collective-permute-start | bytes 786440 | tf_op jit(solution)/shard_map/ppermute | solution.py:287
  54.4 5.0 %collective-permute-done.5.far_ref = bf16[256,512]{1,0:T(8,128)(2,1)S(1)} collective-permute-done((bf16[256,512]{1,0:T(8,128)(2,1)S(1)}, bf16[256,512]{1,0:T(8,128)(2,1)S(1)}, u32[]{:S(2)}, u32[]{:S(2)}) %collective-permute-start.5) | collective-permute-done | bytes 262176 | tf_op jit(solution)/shard_map/ppermute | solution.py:285
  59.4 3.8 %collective-permute-done.4.middle_ref = bf16[256,512]{1,0:T(8,128)(2,1)S(1)} collective-permute-done((bf16[256,512]{1,0:T(8,128)(2,1)S(1)}, bf16[256,512]{1,0:T(8,128)(2,1)S(1)}, u32[]{:S(2)}, u32[]{:S(2)}) %collective-permute-start.4) | collective-permute-done | bytes 262176 | tf_op jit(solution)/shard_map/ppermute | solution.py:287
  63.2 0.7 copy-done.10
  63.9 5.1 %project.1 = (f32[128,1024]{1,0:T(8,128)}, bf16[128,1024]{1,0:T(8,128)(2,1)}) custom-call(s32[1]{0:T(128)} %bitcast.at_ref, bf16[256,512]{1,0:T(8,128)(2,1)} %copy-done.6, bf16[256,512]{1,0:T(8,128)(2,1)} %copy-done.7, bf16[256,512]{1,0:T(8,128)(2,1)} %copy-done.8, bf16[256,512]{1,0:T(8,128)(2,1)} %copy-done.10, bf16[256,512]{1,0:T(8,128)(2,1)} %copy-done.9, ...), custom_call_target="tpu_custom_call" | custom-call | flops 100000000 | bytes 1000000 | tf_op jit(solution)/shard_map/project/pallas_call | solution.py:54
  69.0 0.1 collective-permute-start.6
  69.1 1.7 %collective-permute-done.6 = bf16[128,1024]{1,0:T(8,128)(2,1)S(1)} collective-permute-done((bf16[128,1024]{1,0:T(8,128)(2,1)}, bf16[128,1024]{1,0:T(8,128)(2,1)S(1)}, u32[]{:S(2)}, u32[]{:S(2)}) %collective-permute-start.6) | collective-permute-done | bytes 262176 | tf_op jit(solution)/shard_map/ppermute | solution.py:380
  70.8 1.8 %add_convert_fusion = bf16[128,1024]{1,0:T(8,128)(2,1)} fusion(f32[128,1024]{1,0:T(8,128)} %get-tuple-element.43, bf16[128,1024]{1,0:T(8,128)(2,1)S(1)} %collective-permute-done.6), kind=kLoop, calls=%fused_computation | loop fusion | flops 393216 | bytes 1048576 | tf_op jit(solution)/shard_map/convert_element_type | solution.py:381
  (20 shorter events, 0.1 us)
Async XLA Ops:
  6.5 56.7 %all-gather.3.cloned.1.call-start = ((), (), s32[]{:S(2)}) async-start(), calls=%async_computation.1 | async-start | bytes 5242880 | tf_op jit(solution)/shard_map/all_gather | solution.py:300
  9.4 14.3 %copy-start.5 = (f32[1,1024]{1,0:T(1,128)S(1)}, f32[1,1024]{1,0:T(1,128)}, u32[]{:S(2)}) copy-start(f32[1,1024]{1,0:T(1,128)} %get-tuple-element.35.skip_ref) | copy-start | bytes 12292
  9.4 7.7 %collective-permute-start = (bf16[3,8,1024]{2,1,0:T(8,128)(2,1)}, bf16[3,8,1024]{2,1,0:T(8,128)(2,1)S(1)}, u32[]{:S(2)}, u32[]{:S(2)}) collective-permute-start(bf16[3,8,1024]{2,1,0:T(8,128)(2,1)} %get-tuple-element.25), channel_id=1, source_target_pairs={{0,4},{4,8},{8,12},{12,16},{16,20},{20,24},{24,28},{1,5},{5,9},{9,... | collective-permute-start | bytes 147464 | tf_op jit(solution)/shard_map/ppermute | solution.py:25
  11.8 0.9 %copy-start = (f32[3,7,1024]{2,1,0:T(8,128)S(1)}, f32[3,7,1024]{2,1,0:T(8,128)}, u32[]{:S(2)}) copy-start(f32[3,7,1024]{2,1,0:T(8,128)} %get-tuple-element.27.taps_ref) | copy-start | bytes 258052
  12.7 1.1 %copy-start.1 = (bf16[3,1024,128]{2,1,0:T(8,128)(2,1)S(1)}, bf16[3,1024,128]{2,1,0:T(8,128)(2,1)}, u32[]{:S(2)}) copy-start(bf16[3,1024,128]{2,1,0:T(8,128)(2,1)} %get-tuple-element.26.streams_ref) | copy-start | bytes 2359300
  13.8 0.7 copy-start.2
  14.5 9.2 %copy-start.3 = (f32[16,128]{1,0:T(8,128)S(1)}, f32[16,128]{1,0:T(8,128)}, u32[]{:S(2)}) copy-start(f32[16,128]{1,0:T(8,128)} %get-tuple-element.28.rates_ref) | copy-start | bytes 24580
  14.5 9.2 %copy-start.4 = (f32[16,128]{1,0:T(8,128)S(1)}, f32[16,128]{1,0:T(8,128)}, u32[]{:S(2)}) copy-start(f32[16,128]{1,0:T(8,128)} %get-tuple-element.36.residues_ref) | copy-start | bytes 24580
  18.6 15.1 %all-to-all-start = ((bf16[8,16,1024]{2,1,0:T(8,128)(2,1)}), bf16[8,16,1024]{2,1,0:T(8,128)(2,1)S(1)}, u32[]{:S(2)}, u32[]{:S(2)}) async-start(bf16[8,16,1024]{2,1,0:T(8,128)(2,1)} %get-tuple-element.32), calls=%async_computation | async-start | bytes 524288 | tf_op jit(solution)/shard_map/all_to_all | solution.py:343
  35.8 1.3 %collective-permute-start.1 = (bf16[128,512]{1,0:T(8,128)(2,1)S(1)}, bf16[128,512]{1,0:T(8,128)(2,1)S(1)}, u32[]{:S(2)}, u32[]{:S(2)}) collective-permute-start(bf16[128,512]{1,0:T(8,128)(2,1)S(1)} %get-tuple-element.42), channel_id=1, source_target_pairs={{0,4},{4,0},{8,12},{12,8},{16,20},{20,16},{24,28},{28,24},{1,5},{5... | collective-permute-start | bytes 393224 | tf_op jit(solution)/shard_map/ppermute | solution.py:369
  37.1 26.1 %copy-start.6 = (bf16[256,512]{1,0:T(8,128)(2,1)}, bf16[256,512]{1,0:T(8,128)(2,1)S(1)}, u32[]{:S(2)}) copy-start(bf16[256,512]{1,0:T(8,128)(2,1)S(1)} %constant_dynamic-update-slice_fusion.own_ref) | copy-start | bytes 786436
  37.1 11.4 %collective-permute-start.2 = (bf16[256,512]{1,0:T(8,128)(2,1)S(1)}, bf16[256,512]{1,0:T(8,128)(2,1)S(1)}, u32[]{:S(2)}, u32[]{:S(2)}) collective-permute-start(bf16[256,512]{1,0:T(8,128)(2,1)S(1)} %constant_dynamic-update-slice_fusion.own_ref), channel_id=1, source_target_pairs={{0,1},{1,2},{2,3},{4,5},{5,6},{6,7},{8,9},{9,10},{10,11},{12,13},{... | collective-permute-start | bytes 786440 | tf_op jit(solution)/shard_map/ppermute | solution.py:283
  40.7 10.0 %collective-permute-start.3 = (bf16[256,512]{1,0:T(8,128)(2,1)S(1)}, bf16[256,512]{1,0:T(8,128)(2,1)S(1)}, u32[]{:S(2)}, u32[]{:S(2)}) collective-permute-start(bf16[256,512]{1,0:T(8,128)(2,1)S(1)} %constant_dynamic-update-slice_fusion.own_ref), channel_id=1, source_target_pairs={{1,0},{2,1},{3,2},{5,4},{6,5},{7,6},{9,8},{10,9},{11,10},{13,12},{... | collective-permute-start | bytes 786440 | tf_op jit(solution)/shard_map/ppermute | solution.py:284
  42.0 17.4 %collective-permute-start.5 = (bf16[256,512]{1,0:T(8,128)(2,1)S(1)}, bf16[256,512]{1,0:T(8,128)(2,1)S(1)}, u32[]{:S(2)}, u32[]{:S(2)}) collective-permute-start(bf16[256,512]{1,0:T(8,128)(2,1)S(1)} %constant_dynamic-update-slice_fusion.own_ref), channel_id=1, source_target_pairs={{0,3},{3,0},{4,7},{7,4},{8,11},{11,8},{12,15},{15,12},{16,19},{19,... | collective-permute-start | bytes 786440 | tf_op jit(solution)/shard_map/ppermute | solution.py:285
  48.6 14.7 %copy-start.7 = (bf16[256,512]{1,0:T(8,128)(2,1)}, bf16[256,512]{1,0:T(8,128)(2,1)S(1)}, u32[]{:S(2)}) copy-start(bf16[256,512]{1,0:T(8,128)(2,1)S(1)} %collective-permute-done.2.below_ref) | copy-start | bytes 786436
  50.6 12.6 %copy-start.8 = (bf16[256,512]{1,0:T(8,128)(2,1)}, bf16[256,512]{1,0:T(8,128)(2,1)S(1)}, u32[]{:S(2)}) copy-start(bf16[256,512]{1,0:T(8,128)(2,1)S(1)} %collective-permute-done.3.above_ref) | copy-start | bytes 786436
  50.7 12.5 %collective-permute-start.4 = (bf16[256,512]{1,0:T(8,128)(2,1)S(1)}, bf16[256,512]{1,0:T(8,128)(2,1)S(1)}, u32[]{:S(2)}, u32[]{:S(2)}) collective-permute-start(bf16[256,512]{1,0:T(8,128)(2,1)S(1)} %select_select_fusion), channel_id=1, source_target_pairs={{0,2},{3,1},{2,3},{1,0},{4,6},{7,5},{6,7},{5,4},{8,10},{11,9},{10,... | collective-permute-start | bytes 786440 | tf_op jit(solution)/shard_map/ppermute | solution.py:287
  59.4 3.8 %copy-start.9 = (bf16[256,512]{1,0:T(8,128)(2,1)}, bf16[256,512]{1,0:T(8,128)(2,1)S(1)}, u32[]{:S(2)}) copy-start(bf16[256,512]{1,0:T(8,128)(2,1)S(1)} %collective-permute-done.5.far_ref) | copy-start | bytes 786436
  63.2 0.7 copy-start.10
  69.0 1.8 %collective-permute-start.6 = (bf16[128,1024]{1,0:T(8,128)(2,1)}, bf16[128,1024]{1,0:T(8,128)(2,1)S(1)}, u32[]{:S(2)}, u32[]{:S(2)}) collective-permute-start(bf16[128,1024]{1,0:T(8,128)(2,1)} %get-tuple-element.44), channel_id=1, source_target_pairs={{0,4},{4,0},{8,12},{12,8},{16,20},{20,16},{24,28},{28,24},{1,5},{5... | collective-permute-start | bytes 786440 | tf_op jit(solution)/shard_map/ppermute | solution.py:380
Sparse Core Ops, SparseCore 0:
  8.9 50.5 all-gather.2

commit v5 on v4

--- a/solution.py
+++ b/solution.py
@@ -1,4 +1,3 @@
-import functools
 import math
 
 import jax
@@ -14,7 +13,7 @@
 TILE = 128
 CORES = 2
 VMEM_LIMIT = 24 * 1024 * 1024
-FETCH_LIMIT = 58 * 1024 * 1024
+FETCH_LIMIT = 52 * 1024 * 1024
 PLAIN = (((1,), (0,)), ((), ()))
 CONTRACT_LANES = (((1,), (1,)), ((), ()))
 
@@ -253,29 +252,36 @@
     other_ref[...] = mixed_ref[:, tile_of(1 - core, share)]
 
 
-def project_kernel(place, at_ref, own_ref, below_ref, above_ref, middle_ref, far_ref, weight_hbm, mine_ref, other_ref, weight_ref, sems):
-    layer = at_ref[0]
+def project_kernel(at_ref, own_ref, below_ref, above_ref, middle_ref, far_ref, *rest):
+    *weight_refs, mine_ref, other_ref, layers_ref = rest
+    layer, chip = at_ref[0], at_ref[1]
     edge = (layer == 0) | (layer == 3)
-    sources = [layer, jnp.where(layer == 0, 1, layer - 1), (layer + 2) % 4, jnp.where(edge, 3 - layer, layer + 1)]
-    copies = []
-    for at, source in enumerate(sources):
-        row = sum(jnp.where(source == index, place[index], 0) for index in range(4))
-        copies.append(pltpu.make_async_copy(weight_hbm.at[row], weight_ref.at[at], sems.at[at]))
-        copies[-1].start()
-    blocks = [
-        lambda: own_ref[...],
-        lambda: jnp.where(layer == 0, above_ref[...], below_ref[...]),
-        lambda: middle_ref[...],
-        lambda: jnp.where(edge, far_ref[...], above_ref[...]),
-    ]
-    total = None
-    for copy, block, rows in zip(copies, blocks, range(4)):
-        copy.wait()
-        term = dot(block(), weight_ref[rows])
+    layers_ref[layer] = own_ref[...]
+    layers_ref[jnp.where(layer == 0, 1, layer - 1)] = jnp.where(layer == 0, above_ref[...], below_ref[...])
+    layers_ref[lax.rem(layer + 2, 4)] = middle_ref[...]
+    layers_ref[jnp.where(edge, 3 - layer, layer + 1)] = jnp.where(edge, far_ref[...], above_ref[...])
+    total, row = None, 0
+    share = own_ref.shape[1]
+    for weight_ref in weight_refs:
+        start = row % share
+        rows = weight_ref.shape[0]
+        block = layers_ref[chip ^ (row // share), :, start : start + rows]
+        term = dot(block, weight_ref[...])
         total = term if total is None else total + term
+        row += rows
     length = mine_ref.shape[0]
     mine_ref[...] = total[:length]
     other_ref[...] = total[length:].astype(BF16)
+
+
+def over_square(own):
+    half = own.shape[0] // 2
+
+    def swap(value, bit):
+        return lax.ppermute(value, "ctx", [(source, source ^ bit) for source in range(8)])
+
+    across, along = swap(own, 2), swap(own, 4)
+    return own, across, along, swap(across[:half], 4), swap(along[half:], 2)
 
 
 def over_layers(block):
@@ -294,12 +300,13 @@
     blocks, layers = lax.axis_size("ctx"), lax.axis_size("tp")
     rows, features = out_weight.shape
     share = channels // CORES
-    chips = blocks // CORES
-    ring = [0, 1, 3, 2] if chips == 4 and rows == share else list(range(chips))
-    core_groups = [[chip * CORES + core for chip in ring] for core in range(CORES)]
-    weight = lax.all_gather(out_weight, "ctx", axis=0, axis_index_groups=core_groups)
-    weight = weight.reshape(layers, share, features)
-    place = ring if rows == share else list(range(layers))
+    square = blocks == 8 and rows == share
+    if square:
+        weight = over_square(out_weight)
+    else:
+        core_groups = [list(range(core, blocks, CORES)) for core in range(CORES)]
+        weight = lax.all_gather(out_weight, "ctx", axis=0, axis_index_groups=core_groups)
+        weight = weight.reshape(layers, share, features)
 
     tails, streams, conv_weight, rates, residues, skip = call(
         tails_kernel,
@@ -368,14 +375,16 @@
     siblings = [(source, source ^ 1) for source in range(blocks)]
     block = jnp.concatenate([mine, lax.ppermute(other, "ctx", siblings)], axis=0)
     layer = lax.axis_index("tp").astype(jnp.int32)
+    if not square:
+        weight = tuple(weight)
+    chip = me // CORES if square else jnp.zeros_like(me)
     mine, other = call(
-        functools.partial(project_kernel, place),
+        project_kernel,
         [((length, features), F32), ((length, features), BF16)],
         "project",
-        layer[None], block, *over_layers(block), weight,
-        specs=smem + whole(5) + [pl.BlockSpec(memory_space=pltpu.HBM)],
-        scratch=[pltpu.VMEM((layers, share, features), BF16), pltpu.SemaphoreType.DMA((layers,))],
-        limit=FETCH_LIMIT,
+        jnp.stack([layer, chip]), block, *over_layers(block), *weight,
+        specs=smem + whole(5 + len(weight)),
+        scratch=[pltpu.VMEM((layers,) + block.shape, BF16)],
     )
     other = lax.ppermute(other, "ctx", siblings)
     return (mine + other.astype(F32)).astype(BF16)

time: 80 us -> 79.4 us (level)
  starting transfers between devices: 22.5 us -> 38.8 us
  between operations: 13.6 us -> 0.15 us
  local copies, waits for them, and re-layouts: 3.46 us -> 10.9 us
  waiting for transfers between devices: 19.6 us -> 12.9 us
  Pallas kernels: 18.4 us -> 14.3 us
    all_to_all x1, starting transfers between devices: 4.99 us -> 17.8 us  [local(): lax.all_to_all(ends, 'ctx', split_axis=0, concat_axis=0, tiled=True)]
    ppermute x0 -> x4, starting transfers between devices: none -> 7.79 us  [swap(): lax.ppermute(value, 'ctx', [(source, source ^ bit) for source in range(8)])]
    unnamed x23 -> x25, local copies, waits for them, and re-layouts: 3.45 us -> 9.21 us
    all_to_all x1, waiting for transfers between devices: 4.93 us -> 0.06 us  [local(): lax.all_to_all(ends, 'ctx', split_axis=0, concat_axis=0, tiled=True)]
    pallas_call x6, Pallas kernels: 18.4 us -> 14.3 us  [call(): pl.pallas_call(kernel, out_shape=tuple((jax.ShapeDtypeStruct(*out) for ou...]
    ppermute x1, starting transfers between devices: 3.74 us -> 0.01 us  [over_layers(): middle = lax.ppermute(onward, 'tp', [(0, 2), (3, 1), (2, 3), (1, 0)])]
    ppermute x1, waiting for transfers between devices: 2.06 us -> 0.01 us  [over_layers(): above = lax.ppermute(block, 'tp', [(1, 0), (2, 1), (3, 2)])]
    slice x0 -> x2, local copies, waits for them, and re-layouts: none -> 1.7 us  [over_square(): return (own, across, along, swap(across[:half], 4), swap(along[half:], 2))]
  transfers between devices with their start and end apart: 9 -> 12, of which waited for: 6 -> 5; matrix products, arithmetic and copies ran while one was open for 0% -> 3% of each run, Pallas kernels for 17% -> 15%
where the time goes in v5:
time: 79.4 us; the launch traced here: 78.7 us
  starting transfers between devices  38.8 us (49%)
  Pallas kernels  14.3 us (18%)
  waiting for transfers between devices  12.9 us (16%)
  local copies, waits for them, and re-layouts  10.9 us (14%)
  other arithmetic  1.65 us (2%)
    all_to_all x1, starting transfers between devices, local(): lax.all_to_all(ends, 'ctx', split_axis=0, concat_axis=0, tiled=True)  17.8 us
    pallas_call x6, Pallas kernels, call(): pl.pallas_call(kernel, out_shape=tuple((jax.ShapeDtypeStruct(*out) for ou...  14.3 us
    unnamed x25, local copies, waits for them, and re-layouts  9.21 us
    ppermute x4, starting transfers between devices, swap(): lax.ppermute(value, 'ctx', [(source, source ^ bit) for source in range(8)])  7.79 us
    ppermute x1, starting transfers between devices, over_layers(): far = lax.ppermute(block, 'tp', [(0, 3), (3, 0)])  6.56 us
    ppermute x1, waiting for transfers between devices, over_layers(): far = lax.ppermute(block, 'tp', [(0, 3), (3, 0)])  6.47 us
    ppermute x1, waiting for transfers between devices, over_layers(): middle = lax.ppermute(onward, 'tp', [(0, 2), (3, 1), (2, 3), (1, 0)])  3.89 us
    ppermute x1, starting transfers between devices, over_layers(): below = lax.ppermute(block, 'tp', [(0, 1), (1, 2), (2, 3)])  3.51 us
  transfers between devices with their start and end apart: 12, of which 5 were waited for; matrix products, arithmetic and copies ran while one was open for 3% of the time, Pallas kernels for 15%

profile of v5, /device:TPU:0, one launch (start us, length us, event | category | flops | bytes accessed | tf_op | source)
XLA Modules:
  0.0 78.7 jit_solution(13994480532371941795)
XLA Ops:
  0.0 2.9 %collective-permute-start.6 = (bf16[512,1024]{1,0:T(8,128)(2,1)}, bf16[512,1024]{1,0:T(8,128)(2,1)S(1)}, u32[]{:S(2)}, u32[]{:S(2)}) collective-permute-start(bf16[512,1024]{1,0:T(8,128)(2,1)} %rest_0_.1), channel_id=1, source_target_pairs={{0,8},{4,12},{8,0},{12,4},{16,24},{20,28},{24,16},{28,20},{1,9},{5... | collective-permute-start | bytes 3145736 | tf_op jit(solution)/shard_map/ppermute | solution.py:281
  2.9 1.5 %collective-permute-start.7 = (bf16[512,1024]{1,0:T(8,128)(2,1)}, bf16[512,1024]{1,0:T(8,128)(2,1)S(1)}, u32[]{:S(2)}, u32[]{:S(2)}) collective-permute-start(bf16[512,1024]{1,0:T(8,128)(2,1)} %rest_0_.1), channel_id=1, source_target_pairs={{0,16},{4,20},{8,24},{12,28},{16,0},{20,4},{24,8},{28,12},{1,17},{... | collective-permute-start | bytes 3145736 | tf_op jit(solution)/shard_map/ppermute | solution.py:281
  4.5 1.1 %copy-done.1 = bf16[3,1024,128]{2,1,0:T(8,128)(2,1)S(1)} copy-done((bf16[3,1024,128]{2,1,0:T(8,128)(2,1)S(1)}, bf16[3,1024,128]{2,1,0:T(8,128)(2,1)}, u32[]{:S(2)}) %copy-start.1) | copy-done | bytes 786456
  5.6 0.9 %copy-done.6 = f32[3,7,1024]{2,1,0:T(8,128)S(1)} copy-done((f32[3,7,1024]{2,1,0:T(8,128)S(1)}, f32[3,7,1024]{2,1,0:T(8,128)}, u32[]{:S(2)}) %copy-start.6) | copy-done | bytes 86040
  6.5 0.7 copy-done.7
  7.2 0.7 copy-done.8
  8.5 1.3 %collective-permute-start = (bf16[3,8,1024]{2,1,0:T(8,128)(2,1)S(1)}, bf16[3,8,1024]{2,1,0:T(8,128)(2,1)S(1)}, u32[]{:S(2)}, u32[]{:S(2)}) collective-permute-start(bf16[3,8,1024]{2,1,0:T(8,128)(2,1)S(1)} %get-tuple-element.25), channel_id=1, source_target_pairs={{0,4},{4,8},{8,12},{12,16},{16,20},{20,24},{24,28},{1,5},{5,9},{9,... | collective-permute-start | bytes 147464 | tf_op jit(solution)/shard_map/ppermute | solution.py:24
  9.8 2.6 %prepare.1 = (f32[3,8,1024]{2,1,0:T(8,128)S(1)}, f32[128,1024]{1,0:T(8,128)S(1)}, f32[128,1024]{1,0:T(8,128)S(1)}, bf16[2,2048,128]{2,1,0:T(8,128)(2,1)S(1)}, f32[16,1024]{1,0:T(8,128)S(1)}) custom-call(bf16[3,1024,128]{2,1,0:T(8,128)(2,1)S(1)} %get-tuple-element.26.streams_ref, f32[3,7,1024]{2,1,0:T(8,128)S(1)} %get-tuple-element.27.taps_ref, ...), custom_call_target="tpu_custom_call" | custom-call | flops 1000000000 | bytes 1000000 | tf_op jit(solution)/shard_map/prepare/pallas_call | solution.py:53
  12.4 1.5 %states.1 = (bf16[8,16,1024]{2,1,0:T(8,128)(2,1)}, bf16[128,1024]{1,0:T(8,128)(2,1)S(1)}, f32[8,1024]{1,0:T(8,128)S(1)}) custom-call(bf16[3,8,1024]{2,1,0:T(8,128)(2,1)S(1)} %collective-permute-done.before_ref, f32[3,8,1024]{2,1,0:T(8,128)S(1)} %get-tuple-element.29.heads_ref, f32[3,7,1024]{2,1,0:T(8,128)S(1)} %get-tuple-element.27.taps_ref, ...), custom_call_target="tpu_custom_call" | custom-call | flops 100000000 | bytes 1000000 | tf_op jit(solution)/shard_map/states/pallas_call | solution.py:53
  13.9 0.7 copy-done.10
  14.6 17.8 %all-to-all-start = ((bf16[8,16,1024]{2,1,0:T(8,128)(2,1)}), bf16[8,16,1024]{2,1,0:T(8,128)(2,1)S(1)}, u32[]{:S(2)}, u32[]{:S(2)}) async-start(bf16[8,16,1024]{2,1,0:T(8,128)(2,1)} %get-tuple-element.32), calls=%async_computation | async-start | bytes 524288 | tf_op jit(solution)/shard_map/all_to_all | solution.py:350
  32.5 0.9 %copy-done.11 = bf16[128,1024]{1,0:T(8,128)(2,1)S(1)} copy-done((bf16[128,1024]{1,0:T(8,128)(2,1)S(1)}, bf16[128,1024]{1,0:T(8,128)(2,1)}, u32[]{:S(2)}) %copy-start.11) | copy-done | bytes 262168
  33.4 5.0 %inside.1 = (bf16[2,128,2048]{2,1,0:T(8,128)(2,1)S(1)}, f32[128,1024]{1,0:T(8,128)S(1)}) custom-call(bf16[128,1024]{1,0:T(8,128)(2,1)S(1)} %copy-done.11, f32[1,1024]{1,0:T(1,128)S(1)} %get-tuple-element.35.skip_ref, f32[16,128]{1,0:T(8,128)S(1)} %get-tuple-element.28.rates_ref, f32[16,128]{1,0:T(8,128)S(1)} %get-tuple-element.36.residues_ref), custom_call_target="tpu_custom_call" | custom-call | flops 1000000000 | bytes 1000000 | tf_op jit(solution)/shard_map/inside/pallas_call | solution.py:53
  38.5 0.8 %copy-done.4 = f32[128,1024]{1,0:T(8,128)} copy-done((f32[128,1024]{1,0:T(8,128)}, f32[128,1024]{1,0:T(8,128)S(1)}, u32[]{:S(2)}) %copy-start.4) | copy-done | bytes 524312
  39.3 1.0 %copy-done.3 = f32[128,1024]{1,0:T(8,128)S(1)} copy-done((f32[128,1024]{1,0:T(8,128)S(1)}, f32[128,1024]{1,0:T(8,128)}, u32[]{:S(2)}) %copy-start.3) | copy-done | bytes 524312
  40.4 1.0 %copy-done.5 = f32[128,1024]{1,0:T(8,128)S(1)} copy-done((f32[128,1024]{1,0:T(8,128)S(1)}, f32[128,1024]{1,0:T(8,128)}, u32[]{:S(2)}) %copy-start.5) | copy-done | bytes 524312
  41.4 2.1 %finish.1 = (bf16[128,512]{1,0:T(8,128)(2,1)S(1)}, bf16[128,512]{1,0:T(8,128)(2,1)S(1)}, bf16[128,1024]{1,0:T(8,128)(2,1)}) custom-call(s32[2]{0:T(128)S(1)} %pad_add_fusion.1.at_ref, bf16[8,16,1024]{2,1,0:T(8,128)(2,1)S(1)} %all-to-all-done.ends_ref, f32[16,1024]{1,0:T(8,128)S(1)} %get-tuple-element.33.step_ref, ...), custom_call_target="tpu_custom_call" | custom-call | flops 100000000 | bytes 1000000 | tf_op jit(solution)/shard_map/finish/pallas_call | solution.py:53
  44.0 1.0 %collective-permute-done.1 = bf16[128,512]{1,0:T(8,128)(2,1)S(1)} collective-permute-done((bf16[128,512]{1,0:T(8,128)(2,1)S(1)}, bf16[128,512]{1,0:T(8,128)(2,1)S(1)}, u32[]{:S(2)}, u32[]{:S(2)}) %collective-permute-start.1) | collective-permute-done | bytes 131104 | tf_op jit(solution)/shard_map/ppermute | solution.py:376
  45.0 3.5 %collective-permute-start.2 = (bf16[256,512]{1,0:T(8,128)(2,1)S(1)}, bf16[256,512]{1,0:T(8,128)(2,1)S(1)}, u32[]{:S(2)}, u32[]{:S(2)}) collective-permute-start(bf16[256,512]{1,0:T(8,128)(2,1)S(1)} %constant_dynamic-update-slice_fusion.own_ref), channel_id=1, source_target_pairs={{0,1},{1,2},{2,3},{4,5},{5,6},{6,7},{8,9},{9,10},{10,11},{12,13},{... | collective-permute-start | bytes 786440 | tf_op jit(solution)/shard_map/ppermute | solution.py:289
  48.5 1.3 %collective-permute-start.3 = (bf16[256,512]{1,0:T(8,128)(2,1)S(1)}, bf16[256,512]{1,0:T(8,128)(2,1)S(1)}, u32[]{:S(2)}, u32[]{:S(2)}) collective-permute-start(bf16[256,512]{1,0:T(8,128)(2,1)S(1)} %constant_dynamic-update-slice_fusion.own_ref), channel_id=1, source_target_pairs={{1,0},{2,1},{3,2},{5,4},{6,5},{7,6},{9,8},{10,9},{11,10},{13,12},{... | collective-permute-start | bytes 786440 | tf_op jit(solution)/shard_map/ppermute | solution.py:290
  49.8 0.9 %slice.8 = bf16[256,1024]{1,0:T(8,128)(2,1)} slice(bf16[512,1024]{1,0:T(8,128)(2,1)S(1)} %collective-permute-done.6.rest_1_), slice={[0:256], [0:1024]} | slice | bytes 1048576 | tf_op jit(solution)/shard_map/slice | solution.py:284
  50.7 1.9 %collective-permute-start.8 = (bf16[256,1024]{1,0:T(8,128)(2,1)}, bf16[256,1024]{1,0:T(8,128)(2,1)S(1)}, u32[]{:S(2)}, u32[]{:S(2)}) collective-permute-start(bf16[256,1024]{1,0:T(8,128)(2,1)} %slice.8), channel_id=1, source_target_pairs={{0,16},{4,20},{8,24},{12,28},{16,0},{20,4},{24,8},{28,12},{1,17},{... | collective-permute-start | bytes 1572872 | tf_op jit(solution)/shard_map/ppermute | solution.py:281
  52.5 0.8 %slice.9 = bf16[256,1024]{1,0:T(8,128)(2,1)} slice(bf16[512,1024]{1,0:T(8,128)(2,1)S(1)} %collective-permute-done.7.rest_2_), slice={[256:512], [0:1024]} | slice | bytes 1048576 | tf_op jit(solution)/shard_map/slice | solution.py:284
  53.4 1.5 %collective-permute-start.9 = (bf16[256,1024]{1,0:T(8,128)(2,1)}, bf16[256,1024]{1,0:T(8,128)(2,1)}, u32[]{:S(2)}, u32[]{:S(2)}) collective-permute-start(bf16[256,1024]{1,0:T(8,128)(2,1)} %slice.9), channel_id=1, source_target_pairs={{0,8},{4,12},{8,0},{12,4},{16,24},{20,28},{24,16},{28,20},{1,9},{5... | collective-permute-start | bytes 1572872 | tf_op jit(solution)/shard_map/ppermute | solution.py:281
  54.8 6.6 %collective-permute-start.5 = (bf16[256,512]{1,0:T(8,128)(2,1)S(1)}, bf16[256,512]{1,0:T(8,128)(2,1)}, u32[]{:S(2)}, u32[]{:S(2)}) collective-permute-start(bf16[256,512]{1,0:T(8,128)(2,1)S(1)} %constant_dynamic-update-slice_fusion.own_ref), channel_id=1, source_target_pairs={{0,3},{3,0},{4,7},{7,4},{8,11},{11,8},{12,15},{15,12},{16,19},{19,... | collective-permute-start | bytes 786440 | tf_op jit(solution)/shard_map/ppermute | solution.py:291
  61.4 0.7 select_select_fusion
  62.2 6.5 %collective-permute-done.5.far_ref = bf16[256,512]{1,0:T(8,128)(2,1)} collective-permute-done((bf16[256,512]{1,0:T(8,128)(2,1)S(1)}, bf16[256,512]{1,0:T(8,128)(2,1)}, u32[]{:S(2)}, u32[]{:S(2)}) %collective-permute-start.5) | collective-permute-done | bytes 262176 | tf_op jit(solution)/shard_map/ppermute | solution.py:291
  68.7 3.9 %collective-permute-done.4.middle_ref = bf16[256,512]{1,0:T(8,128)(2,1)} collective-permute-done((bf16[256,512]{1,0:T(8,128)(2,1)}, bf16[256,512]{1,0:T(8,128)(2,1)}, u32[]{:S(2)}, u32[]{:S(2)}) %collective-permute-start.4) | collective-permute-done | bytes 262176 | tf_op jit(solution)/shard_map/ppermute | solution.py:293
  72.6 1.2 %copy-done = bf16[512,1024]{1,0:T(8,128)(2,1)S(1)} copy-done((bf16[512,1024]{1,0:T(8,128)(2,1)S(1)}, bf16[512,1024]{1,0:T(8,128)(2,1)}, u32[]{:S(2)}) %copy-start) | copy-done | bytes 1048600
  73.8 2.5 %project.1 = (f32[128,1024]{1,0:T(8,128)S(1)}, bf16[128,1024]{1,0:T(8,128)(2,1)S(1)}) custom-call(s32[2]{0:T(128)S(1)} %pad_add_fusion.at_ref, bf16[256,512]{1,0:T(8,128)(2,1)S(1)} %constant_dynamic-update-slice_fusion.own_ref, bf16[256,512]{1,0:T(8,128)(2,1)S(1)} %collective-permute-done.2.below_ref, bf16[256,512]{1,0:T(8,128)(2,1)S(1)} %collective-permute-done.3.above_ref, ...), custom_call_target="tpu_custom_call" | custom-call | flops 100000000 | bytes 1000000 | tf_op jit(solution)/shard_map/project/pallas_call | solution.py:53
  76.5 1.5 %collective-permute-done.10 = bf16[128,1024]{1,0:T(8,128)(2,1)S(1)} collective-permute-done((bf16[128,1024]{1,0:T(8,128)(2,1)S(1)}, bf16[128,1024]{1,0:T(8,128)(2,1)S(1)}, u32[]{:S(2)}, u32[]{:S(2)}) %collective-permute-start.10) | collective-permute-done | bytes 262176 | tf_op jit(solution)/shard_map/ppermute | solution.py:389
  78.0 0.8 add_convert_fusion
  (30 shorter events, 1.4 us)
Async XLA Ops:
  0.0 4.5 %copy-start.9 = (f32[1024]{0:T(1024)S(1)}, f32[1024]{0:T(1024)}, u32[]{:S(2)}) copy-start(f32[1024]{0:T(1024)} %param.10) | copy-start | bytes 12292
  0.0 49.8 %collective-permute-start.6 = (bf16[512,1024]{1,0:T(8,128)(2,1)}, bf16[512,1024]{1,0:T(8,128)(2,1)S(1)}, u32[]{:S(2)}, u32[]{:S(2)}) collective-permute-start(bf16[512,1024]{1,0:T(8,128)(2,1)} %rest_0_.1), channel_id=1, source_target_pairs={{0,8},{4,12},{8,0},{12,4},{16,24},{20,28},{24,16},{28,20},{1,9},{5... | collective-permute-start | bytes 3145736 | tf_op jit(solution)/shard_map/ppermute | solution.py:281
  2.9 49.6 %collective-permute-start.7 = (bf16[512,1024]{1,0:T(8,128)(2,1)}, bf16[512,1024]{1,0:T(8,128)(2,1)S(1)}, u32[]{:S(2)}, u32[]{:S(2)}) collective-permute-start(bf16[512,1024]{1,0:T(8,128)(2,1)} %rest_0_.1), channel_id=1, source_target_pairs={{0,16},{4,20},{8,24},{12,28},{16,0},{20,4},{24,8},{28,12},{1,17},{... | collective-permute-start | bytes 3145736 | tf_op jit(solution)/shard_map/ppermute | solution.py:281
  4.5 1.1 %copy-start.1 = (bf16[3,1024,128]{2,1,0:T(8,128)(2,1)S(1)}, bf16[3,1024,128]{2,1,0:T(8,128)(2,1)}, u32[]{:S(2)}) copy-start(bf16[3,1024,128]{2,1,0:T(8,128)(2,1)} %streams_hbm.1) | copy-start | bytes 2359300
  5.6 0.9 %copy-start.6 = (f32[3,7,1024]{2,1,0:T(8,128)S(1)}, f32[3,7,1024]{2,1,0:T(8,128)}, u32[]{:S(2)}) copy-start(f32[3,7,1024]{2,1,0:T(8,128)} %taps_hbm.1) | copy-start | bytes 258052
  6.5 0.7 copy-start.7
  7.2 0.7 copy-start.8
  8.5 3.9 %collective-permute-start = (bf16[3,8,1024]{2,1,0:T(8,128)(2,1)S(1)}, bf16[3,8,1024]{2,1,0:T(8,128)(2,1)S(1)}, u32[]{:S(2)}, u32[]{:S(2)}) collective-permute-start(bf16[3,8,1024]{2,1,0:T(8,128)(2,1)S(1)} %get-tuple-element.25), channel_id=1, source_target_pairs={{0,4},{4,8},{8,12},{12,16},{16,20},{20,24},{24,28},{1,5},{5,9},{9,... | collective-permute-start | bytes 147464 | tf_op jit(solution)/shard_map/ppermute | solution.py:24
  12.4 1.5 %copy-start.2 = (f32[128,1024]{1,0:T(8,128)}, f32[128,1024]{1,0:T(8,128)S(1)}, u32[]{:S(2)}) copy-start(f32[128,1024]{1,0:T(8,128)S(1)} %get-tuple-element.38.query_ref) | copy-start | bytes 1572868
  13.9 0.7 copy-start.10
  14.6 24.7 %all-to-all-start = ((bf16[8,16,1024]{2,1,0:T(8,128)(2,1)}), bf16[8,16,1024]{2,1,0:T(8,128)(2,1)S(1)}, u32[]{:S(2)}, u32[]{:S(2)}) async-start(bf16[8,16,1024]{2,1,0:T(8,128)(2,1)} %get-tuple-element.32), calls=%async_computation | async-start | bytes 524288 | tf_op jit(solution)/shard_map/all_to_all | solution.py:350
  32.5 0.9 %copy-start.11 = (bf16[128,1024]{1,0:T(8,128)(2,1)S(1)}, bf16[128,1024]{1,0:T(8,128)(2,1)}, u32[]{:S(2)}) copy-start(bf16[128,1024]{1,0:T(8,128)(2,1)} %copy-done.10) | copy-start | bytes 786436
  38.5 0.8 %copy-start.4 = (f32[128,1024]{1,0:T(8,128)}, f32[128,1024]{1,0:T(8,128)S(1)}, u32[]{:S(2)}) copy-start(f32[128,1024]{1,0:T(8,128)S(1)} %get-tuple-element.40.base_ref) | copy-start | bytes 1572868
  39.3 1.0 %copy-start.3 = (f32[128,1024]{1,0:T(8,128)S(1)}, f32[128,1024]{1,0:T(8,128)}, u32[]{:S(2)}) copy-start(f32[128,1024]{1,0:T(8,128)} %copy-done.2) | copy-start | bytes 1572868
  40.4 1.0 %copy-start.5 = (f32[128,1024]{1,0:T(8,128)S(1)}, f32[128,1024]{1,0:T(8,128)}, u32[]{:S(2)}) copy-start(f32[128,1024]{1,0:T(8,128)} %copy-done.4) | copy-start | bytes 1572868
  43.5 1.4 %collective-permute-start.1 = (bf16[128,512]{1,0:T(8,128)(2,1)S(1)}, bf16[128,512]{1,0:T(8,128)(2,1)S(1)}, u32[]{:S(2)}, u32[]{:S(2)}) collective-permute-start(bf16[128,512]{1,0:T(8,128)(2,1)S(1)} %get-tuple-element.42), channel_id=1, source_target_pairs={{0,4},{4,0},{8,12},{12,8},{16,20},{20,16},{24,28},{28,24},{1,5},{5... | collective-permute-start | bytes 393224 | tf_op jit(solution)/shard_map/ppermute | solution.py:376
  45.0 16.4 %collective-permute-start.2 = (bf16[256,512]{1,0:T(8,128)(2,1)S(1)}, bf16[256,512]{1,0:T(8,128)(2,1)S(1)}, u32[]{:S(2)}, u32[]{:S(2)}) collective-permute-start(bf16[256,512]{1,0:T(8,128)(2,1)S(1)} %constant_dynamic-update-slice_fusion.own_ref), channel_id=1, source_target_pairs={{0,1},{1,2},{2,3},{4,5},{5,6},{6,7},{8,9},{9,10},{10,11},{12,13},{... | collective-permute-start | bytes 786440 | tf_op jit(solution)/shard_map/ppermute | solution.py:289
  48.5 12.9 %collective-permute-start.3 = (bf16[256,512]{1,0:T(8,128)(2,1)S(1)}, bf16[256,512]{1,0:T(8,128)(2,1)S(1)}, u32[]{:S(2)}, u32[]{:S(2)}) collective-permute-start(bf16[256,512]{1,0:T(8,128)(2,1)S(1)} %constant_dynamic-update-slice_fusion.own_ref), channel_id=1, source_target_pairs={{1,0},{2,1},{3,2},{5,4},{6,5},{7,6},{9,8},{10,9},{11,10},{13,12},{... | collective-permute-start | bytes 786440 | tf_op jit(solution)/shard_map/ppermute | solution.py:290
  50.7 22.0 %collective-permute-start.8 = (bf16[256,1024]{1,0:T(8,128)(2,1)}, bf16[256,1024]{1,0:T(8,128)(2,1)S(1)}, u32[]{:S(2)}, u32[]{:S(2)}) collective-permute-start(bf16[256,1024]{1,0:T(8,128)(2,1)} %slice.8), channel_id=1, source_target_pairs={{0,16},{4,20},{8,24},{12,28},{16,0},{20,4},{24,8},{28,12},{1,17},{... | collective-permute-start | bytes 1572872 | tf_op jit(solution)/shard_map/ppermute | solution.py:281
  53.4 19.2 %collective-permute-start.9 = (bf16[256,1024]{1,0:T(8,128)(2,1)}, bf16[256,1024]{1,0:T(8,128)(2,1)}, u32[]{:S(2)}, u32[]{:S(2)}) collective-permute-start(bf16[256,1024]{1,0:T(8,128)(2,1)} %slice.9), channel_id=1, source_target_pairs={{0,8},{4,12},{8,0},{12,4},{16,24},{20,28},{24,16},{28,20},{1,9},{5... | collective-permute-start | bytes 1572872 | tf_op jit(solution)/shard_map/ppermute | solution.py:281
  54.8 13.9 %collective-permute-start.5 = (bf16[256,512]{1,0:T(8,128)(2,1)S(1)}, bf16[256,512]{1,0:T(8,128)(2,1)}, u32[]{:S(2)}, u32[]{:S(2)}) collective-permute-start(bf16[256,512]{1,0:T(8,128)(2,1)S(1)} %constant_dynamic-update-slice_fusion.own_ref), channel_id=1, source_target_pairs={{0,3},{3,0},{4,7},{7,4},{8,11},{11,8},{12,15},{15,12},{16,19},{19,... | collective-permute-start | bytes 786440 | tf_op jit(solution)/shard_map/ppermute | solution.py:291
  62.2 10.4 %collective-permute-start.4 = (bf16[256,512]{1,0:T(8,128)(2,1)}, bf16[256,512]{1,0:T(8,128)(2,1)}, u32[]{:S(2)}, u32[]{:S(2)}) collective-permute-start(bf16[256,512]{1,0:T(8,128)(2,1)} %select_select_fusion), channel_id=1, source_target_pairs={{0,2},{3,1},{2,3},{1,0},{4,6},{7,5},{6,7},{5,4},{8,10},{11,9},{10,... | collective-permute-start | bytes 786440 | tf_op jit(solution)/shard_map/ppermute | solution.py:293
  72.6 1.2 %copy-start = (bf16[512,1024]{1,0:T(8,128)(2,1)S(1)}, bf16[512,1024]{1,0:T(8,128)(2,1)}, u32[]{:S(2)}) copy-start(bf16[512,1024]{1,0:T(8,128)(2,1)} %rest_0_.1) | copy-start | bytes 3145732
  76.4 1.6 %collective-permute-start.10 = (bf16[128,1024]{1,0:T(8,128)(2,1)S(1)}, bf16[128,1024]{1,0:T(8,128)(2,1)S(1)}, u32[]{:S(2)}, u32[]{:S(2)}) collective-permute-start(bf16[128,1024]{1,0:T(8,128)(2,1)S(1)} %get-tuple-element.44), channel_id=1, source_target_pairs={{0,4},{4,0},{8,12},{12,8},{16,20},{20,16},{24,28},{28,24},{1,5},{5... | collective-permute-start | bytes 786440 | tf_op jit(solution)/shard_map/ppermute | solution.py:389

commit v6 on v5

--- a/solution.py
+++ b/solution.py
@@ -12,8 +12,8 @@
 ROWS = 8
 TILE = 128
 CORES = 2
+FIRST_ROWS = 128
 VMEM_LIMIT = 24 * 1024 * 1024
-FETCH_LIMIT = 52 * 1024 * 1024
 PLAIN = (((1,), (0,)), ((), ()))
 CONTRACT_LANES = (((1,), (1,)), ((), ()))
 
@@ -49,14 +49,14 @@
     return [pl.BlockSpec(memory_space=pltpu.VMEM)] * count
 
 
-def call(kernel, outs, name, *operands, specs=None, scratch=(), flops=10**8, limit=VMEM_LIMIT):
+def call(kernel, outs, name, *operands, specs=None, scratch=(), flops=10**8):
     return pl.pallas_call(
         kernel,
         out_shape=tuple(jax.ShapeDtypeStruct(*out) for out in outs),
         in_specs=whole(len(operands)) if specs is None else specs,
         out_specs=tuple(whole(len(outs))),
         scratch_shapes=scratch,
-        compiler_params=pltpu.CompilerParams(vmem_limit_bytes=limit),
+        compiler_params=pltpu.CompilerParams(vmem_limit_bytes=VMEM_LIMIT),
         cost_estimate=pl.CostEstimate(flops=flops, bytes_accessed=10**6, transcendentals=0),
         name=name,
     )(*operands)
@@ -74,22 +74,7 @@
     lax.fori_loop(0, count, step, 0, unroll=math.gcd(count, 4))
 
 
-def tails_kernel(
-    streams_hbm, taps_hbm, rates_hbm, residues_hbm, skip_hbm,
-    tails_ref, streams_ref, taps_ref, rates_ref, residues_ref, skip_ref, sems,
-):
-    pairs = [
-        (streams_hbm, streams_ref),
-        (taps_hbm, taps_ref),
-        (rates_hbm, rates_ref),
-        (residues_hbm, residues_ref),
-        (skip_hbm, skip_ref),
-    ]
-    copies = [pltpu.make_async_copy(src, dst, sems.at[at]) for at, (src, dst) in enumerate(pairs)]
-    for copy in copies:
-        copy.start()
-    for copy in copies:
-        copy.wait()
+def tails_kernel(streams_ref, tails_ref):
     length = streams_ref.shape[2]
     pick = (iota((2 * ROWS, length), 1) == iota((2 * ROWS, length), 0) + (length - ROWS)).astype(BF16)
     for stream in range(streams_ref.shape[0]):
@@ -274,14 +259,13 @@
     other_ref[...] = total[length:].astype(BF16)
 
 
-def over_square(own):
-    half = own.shape[0] // 2
-
-    def swap(value, bit):
-        return lax.ppermute(value, "ctx", [(source, source ^ bit) for source in range(8)])
-
-    across, along = swap(own, 2), swap(own, 4)
-    return own, across, along, swap(across[:half], 4), swap(along[half:], 2)
+def swap(value, bit):
+    count = lax.axis_size("ctx")
+    return lax.ppermute(value, "ctx", [(source, source ^ bit) for source in range(count)])
+
+
+def after(value, earlier):
+    return lax.optimization_barrier((value, earlier))[0]
 
 
 def over_layers(block):
@@ -301,30 +285,14 @@
     rows, features = out_weight.shape
     share = channels // CORES
     square = blocks == 8 and rows == share
+
+    rates, residues, skip = rates.T, residues.T, skip[None, :]
+    (tails,) = call(tails_kernel, [((3, ROWS, channels), BF16)], "tails", streams)
+    before = from_behind(tails, "ctx", 1)
+    piece, half = FIRST_ROWS, rows // 2
     if square:
-        weight = over_square(out_weight)
-    else:
-        core_groups = [list(range(core, blocks, CORES)) for core in range(CORES)]
-        weight = lax.all_gather(out_weight, "ctx", axis=0, axis_index_groups=core_groups)
-        weight = weight.reshape(layers, share, features)
-
-    tails, streams, conv_weight, rates, residues, skip = call(
-        tails_kernel,
-        [
-            ((3, ROWS, channels), BF16),
-            (streams.shape, BF16),
-            (conv_weight.shape, F32),
-            ((poles, groups), F32),
-            ((poles, groups), F32),
-            ((1, channels), F32),
-        ],
-        "tails",
-        streams, conv_weight, rates.T, residues.T, skip[None, :],
-        specs=[pl.BlockSpec(memory_space=pltpu.HBM)] * 5,
-        scratch=[pltpu.SemaphoreType.DMA((5,))],
-        limit=FETCH_LIMIT,
-    )
-    before = from_behind(tails, "ctx", 1)
+        across_first = swap(after(out_weight, tails)[:piece], 2)
+        along_first = swap(after(out_weight, tails)[rows - piece :], 4)
     tiles = channels // TILE
     heads, query, gated, decay, step = call(
         prepare_kernel,
@@ -348,6 +316,10 @@
         scratch=[pltpu.VMEM((3 * tiles, 2 * ROWS, TILE), F32)],
     )
     all_ends = lax.all_to_all(ends, "ctx", split_axis=0, concat_axis=0, tiled=True)
+    if square:
+        gated, across_first, along_first = lax.optimization_barrier((gated, across_first, along_first))
+        across_rest = swap(after(out_weight, all_ends)[piece:], 2)
+        along_rest = swap(after(out_weight, all_ends)[: rows - piece], 4)
     lift, base = call(
         inside_kernel,
         [((2, length, groups * poles), BF16), ((length, channels), F32)],
@@ -372,11 +344,24 @@
         by_core = by_core.reshape(CORES, length, share)
         mine = lax.dynamic_index_in_dim(by_core, core, 0, keepdims=False)
         other = lax.dynamic_index_in_dim(by_core, 1 - core, 0, keepdims=False)
-    siblings = [(source, source ^ 1) for source in range(blocks)]
-    block = jnp.concatenate([mine, lax.ppermute(other, "ctx", siblings)], axis=0)
+    block = jnp.concatenate([mine, swap(other, 1)], axis=0)
     layer = lax.axis_index("tp").astype(jnp.int32)
-    if not square:
-        weight = tuple(weight)
+    if square:
+        weight = (
+            out_weight,
+            across_first,
+            across_rest,
+            along_rest,
+            along_first,
+            swap(after(across_first, block), 4),
+            swap(across_rest[: half - piece], 4),
+            swap(along_rest[half:], 2),
+            swap(after(along_first, block), 2),
+        )
+    else:
+        core_groups = [list(range(core, blocks, CORES)) for core in range(CORES)]
+        weight = lax.all_gather(out_weight, "ctx", axis=0, axis_index_groups=core_groups)
+        weight = tuple(weight.reshape(layers, share, features))
     chip = me // CORES if square else jnp.zeros_like(me)
     mine, other = call(
         project_kernel,
@@ -386,7 +371,7 @@
         specs=smem + whole(5 + len(weight)),
         scratch=[pltpu.VMEM((layers,) + block.shape, BF16)],
     )
-    other = lax.ppermute(other, "ctx", siblings)
+    other = swap(other, 1)
     return (mine + other.astype(F32)).astype(BF16)
 
 

time: 79.4 us -> 69.4 us (0.87)
  starting transfers between devices: 38.8 us -> 26.7 us
  waiting for transfers between devices: 12.9 us -> 19 us
  local copies, waits for them, and re-layouts: 10.9 us -> 6.68 us
    all_to_all x1, starting transfers between devices: 17.8 us -> 3.41 us  [local(): lax.all_to_all(ends, 'ctx', split_axis=0, concat_axis=0, tiled=True)]
    all_to_all x1, waiting for transfers between devices: 0.06 us -> 6.75 us  [local(): lax.all_to_all(ends, 'ctx', split_axis=0, concat_axis=0, tiled=True)]
    ppermute x1, waiting for transfers between devices: 6.47 us -> 0.01 us  [over_layers(): far = lax.ppermute(block, 'tp', [(0, 3), (3, 0)])]
    unnamed x25 -> x21, local copies, waits for them, and re-layouts: 9.21 us -> 2.83 us
    ppermute x1, starting transfers between devices: 6.56 us -> 3.48 us  [over_layers(): far = lax.ppermute(block, 'tp', [(0, 3), (3, 0)])]
    ppermute x6 -> x10, waiting for transfers between devices: 2.51 us -> 5.57 us  [swap(): lax.ppermute(value, 'ctx', [(source, source ^ bit) for source in range(co...]
    ppermute x1, waiting for transfers between devices: 0.01 us -> 2.85 us  [over_layers(): above = lax.ppermute(block, 'tp', [(1, 0), (2, 1), (3, 2)])]
    slice x2 -> x4, local copies, waits for them, and re-layouts: 1.7 us -> 3.84 us  [the longest x1 1.34 us: local(): along_rest = swap(after(out_weight, all_ends)[:rows - piece], 4)]
  transfers between devices with their start and end apart: 12 -> 16, of which waited for: 5 -> 6; matrix products, arithmetic and copies ran while one was open for 3% -> 5% of each run, Pallas kernels for 15% -> 16%
where the time goes in v6:
time: 69.4 us; the launch traced here: 69 us
  starting transfers between devices  26.7 us (38%)
  waiting for transfers between devices  19 us (27%)
  Pallas kernels  14.8 us (21%)
  local copies, waits for them, and re-layouts  6.68 us (10%)
  other arithmetic  1.65 us (2%)
    pallas_call x6, Pallas kernels, call(): pl.pallas_call(kernel, out_shape=tuple((jax.ShapeDtypeStruct(*out) for ou...  14.8 us
    ppermute x10, starting transfers between devices, swap(): lax.ppermute(value, 'ctx', [(source, source ^ bit) for source in range(co...  10.4 us
    all_to_all x1, waiting for transfers between devices, local(): lax.all_to_all(ends, 'ctx', split_axis=0, concat_axis=0, tiled=True)  6.75 us
    ppermute x10, waiting for transfers between devices, swap(): lax.ppermute(value, 'ctx', [(source, source ^ bit) for source in range(co...  5.57 us
    ppermute x1, starting transfers between devices, over_layers(): below = lax.ppermute(block, 'tp', [(0, 1), (1, 2), (2, 3)])  4.56 us
    ppermute x1, waiting for transfers between devices, over_layers(): middle = lax.ppermute(onward, 'tp', [(0, 2), (3, 1), (2, 3), (1, 0)])  3.81 us
    ppermute x1, starting transfers between devices, over_layers(): far = lax.ppermute(block, 'tp', [(0, 3), (3, 0)])  3.48 us
    all_to_all x1, starting transfers between devices, local(): lax.all_to_all(ends, 'ctx', split_axis=0, concat_axis=0, tiled=True)  3.41 us
  transfers between devices with their start and end apart: 16, of which 6 were waited for; matrix products, arithmetic and copies ran while one was open for 5% of the time, Pallas kernels for 16%

profile of v6, /device:TPU:0, one launch (start us, length us, event | category | flops | bytes accessed | tf_op | source)
XLA Modules:
  0.0 69.0 jit_solution(6779886581997882852)
XLA Ops:
  0.0 1.1 %copy-done.1 = bf16[3,1024,128]{2,1,0:T(8,128)(2,1)S(1)} copy-done((bf16[3,1024,128]{2,1,0:T(8,128)(2,1)S(1)}, bf16[3,1024,128]{2,1,0:T(8,128)(2,1)}, u32[]{:S(2)}) %copy-start.1) | copy-done | bytes 786456
  1.4 2.5 %collective-permute-start = (bf16[3,8,1024]{2,1,0:T(8,128)(2,1)S(1)}, bf16[3,8,1024]{2,1,0:T(8,128)(2,1)S(1)}, u32[]{:S(2)}, u32[]{:S(2)}) collective-permute-start(bf16[3,8,1024]{2,1,0:T(8,128)(2,1)S(1)} %tails.1), channel_id=1, source_target_pairs={{0,4},{4,8},{8,12},{12,16},{16,20},{20,24},{24,28},{1,5},{5,9},{9,... | collective-permute-start | bytes 147464 | tf_op jit(solution)/shard_map/ppermute | solution.py:24
  3.9 1.1 %fusion.1 = (bf16[128,1024]{1,0:T(8,128)(2,1)S(1)}, bf16[128,1024]{1,0:T(8,128)(2,1)S(1)}) fusion(bf16[512,1024]{1,0:T(8,128)(2,1)} %rest_0_.1), kind=kLoop, calls=%fused_computation.7 | loop fusion | bytes 1048576 | tf_op jit(solution)/shard_map/slice | solution.py:295
  5.0 2.6 %collective-permute-start.2 = (bf16[128,1024]{1,0:T(8,128)(2,1)S(1)}, bf16[128,1024]{1,0:T(8,128)(2,1)S(1)}, u32[]{:S(2)}, u32[]{:S(2)}) collective-permute-start(bf16[128,1024]{1,0:T(8,128)(2,1)S(1)} %get-tuple-element.49), channel_id=1, source_target_pairs={{0,16},{4,20},{8,24},{12,28},{16,0},{20,4},{24,8},{28,12},{1,17},{... | collective-permute-start | bytes 786440 | tf_op jit(solution)/shard_map/ppermute | solution.py:264
  7.6 1.5 %collective-permute-start.1 = (bf16[128,1024]{1,0:T(8,128)(2,1)S(1)}, bf16[128,1024]{1,0:T(8,128)(2,1)}, u32[]{:S(2)}, u32[]{:S(2)}) collective-permute-start(bf16[128,1024]{1,0:T(8,128)(2,1)S(1)} %get-tuple-element.50), channel_id=1, source_target_pairs={{0,8},{4,12},{8,0},{12,4},{16,24},{20,28},{24,16},{28,20},{1,9},{5... | collective-permute-start | bytes 786440 | tf_op jit(solution)/shard_map/ppermute | solution.py:264
  9.1 2.6 %prepare.1 = (f32[3,8,1024]{2,1,0:T(8,128)S(1)}, f32[128,1024]{1,0:T(8,128)S(1)}, f32[128,1024]{1,0:T(8,128)S(1)}, bf16[2,2048,128]{2,1,0:T(8,128)(2,1)S(1)}, f32[16,1024]{1,0:T(8,128)S(1)}) custom-call(bf16[3,1024,128]{2,1,0:T(8,128)(2,1)S(1)} %copy-done.1, f32[3,7,1024]{2,1,0:T(8,128)S(1)} %copy-done.4, f32[16,128]{1,0:T(8,128)S(1)} %bitcast.7), custom_call_target="tpu_custom_call" | custom-call | flops 1000000000 | bytes 1000000 | tf_op jit(solution)/shard_map/prepare/pallas_call | solution.py:53
  11.7 1.5 %states.1 = (bf16[8,16,1024]{2,1,0:T(8,128)(2,1)}, bf16[128,1024]{1,0:T(8,128)(2,1)S(1)}, f32[8,1024]{1,0:T(8,128)S(1)}) custom-call(bf16[3,8,1024]{2,1,0:T(8,128)(2,1)S(1)} %collective-permute-done.before_ref, f32[3,8,1024]{2,1,0:T(8,128)S(1)} %get-tuple-element.26.heads_ref, f32[3,7,1024]{2,1,0:T(8,128)S(1)} %copy-done.4, ...), custom_call_target="tpu_custom_call" | custom-call | flops 100000000 | bytes 1000000 | tf_op jit(solution)/shard_map/states/pallas_call | solution.py:53
  13.2 0.7 %copy-done.5 = bf16[128,1024]{1,0:T(8,128)(2,1)} copy-done((bf16[128,1024]{1,0:T(8,128)(2,1)}, bf16[128,1024]{1,0:T(8,128)(2,1)S(1)}, u32[]{:S(2)}) %copy-start.5) | copy-done | bytes 262168
  14.0 3.4 %all-to-all-start = ((bf16[8,16,1024]{2,1,0:T(8,128)(2,1)}), bf16[8,16,1024]{2,1,0:T(8,128)(2,1)S(1)}, u32[]{:S(2)}, u32[]{:S(2)}) async-start(bf16[8,16,1024]{2,1,0:T(8,128)(2,1)} %get-tuple-element.29), calls=%async_computation | async-start | bytes 524288 | tf_op jit(solution)/shard_map/all_to_all | solution.py:318
  17.5 6.8 %all-to-all-done.ends_ref = bf16[8,16,1024]{2,1,0:T(8,128)(2,1)S(1)} async-done(((bf16[8,16,1024]{2,1,0:T(8,128)(2,1)}), bf16[8,16,1024]{2,1,0:T(8,128)(2,1)S(1)}, u32[]{:S(2)}, u32[]{:S(2)}) %all-to-all-start) | async-done | bytes 262176 | tf_op jit(solution)/shard_map/all_to_all | solution.py:318
  24.2 1.3 %fusion = (bf16[384,1024]{1,0:T(8,128)(2,1)}, bf16[384,1024]{1,0:T(8,128)(2,1)}) fusion(bf16[512,1024]{1,0:T(8,128)(2,1)S(1)} %copy-done), kind=kLoop, calls=%fused_computation.6 | loop fusion | bytes 3145728 | tf_op jit(solution)/shard_map/slice | solution.py:322
  26.1 0.6 collective-permute-start.8
  26.7 5.0 %inside.1 = (bf16[2,128,2048]{2,1,0:T(8,128)(2,1)S(1)}, f32[128,1024]{1,0:T(8,128)S(1)}) custom-call(bf16[128,1024]{1,0:T(8,128)(2,1)S(1)} %copy-done.6, f32[1,1024]{1,0:T(1,128)S(1)} %bitcast.10, f32[16,128]{1,0:T(8,128)S(1)} %bitcast.8, f32[16,128]{1,0:T(8,128)S(1)} %bitcast.9), custom_call_target="tpu_custom_call" | custom-call | flops 1000000000 | bytes 1000000 | tf_op jit(solution)/shard_map/inside/pallas_call | solution.py:53
  31.8 2.1 %finish.1 = (bf16[128,512]{1,0:T(8,128)(2,1)S(1)}, bf16[128,512]{1,0:T(8,128)(2,1)S(1)}, bf16[128,1024]{1,0:T(8,128)(2,1)}) custom-call(s32[2]{0:T(128)S(1)} %pad_add_fusion.1.at_ref, bf16[8,16,1024]{2,1,0:T(8,128)(2,1)S(1)} %all-to-all-done.ends_ref, f32[16,1024]{1,0:T(8,128)S(1)} %get-tuple-element.30.step_ref, ...), custom_call_target="tpu_custom_call" | custom-call | flops 100000000 | bytes 1000000 | tf_op jit(solution)/shard_map/finish/pallas_call | solution.py:53
  33.9 1.3 %collective-permute-done.3 = bf16[128,512]{1,0:T(8,128)(2,1)S(1)} collective-permute-done((bf16[128,512]{1,0:T(8,128)(2,1)S(1)}, bf16[128,512]{1,0:T(8,128)(2,1)S(1)}, u32[]{:S(2)}, u32[]{:S(2)}) %collective-permute-start.3) | collective-permute-done | bytes 131104 | tf_op jit(solution)/shard_map/ppermute | solution.py:264
  35.2 1.3 %collective-permute-start.5 = (bf16[256,512]{1,0:T(8,128)(2,1)S(1)}, bf16[256,512]{1,0:T(8,128)(2,1)S(1)}, u32[]{:S(2)}, u32[]{:S(2)}) collective-permute-start(bf16[256,512]{1,0:T(8,128)(2,1)S(1)} %constant_dynamic-update-slice_fusion.own_ref), channel_id=1, source_target_pairs={{1,0},{2,1},{3,2},{5,4},{6,5},{7,6},{9,8},{10,9},{11,10},{13,12},{... | collective-permute-start | bytes 786440 | tf_op jit(solution)/shard_map/ppermute | solution.py:274
  36.5 4.6 %collective-permute-start.4 = (bf16[256,512]{1,0:T(8,128)(2,1)S(1)}, bf16[256,512]{1,0:T(8,128)(2,1)S(1)}, u32[]{:S(2)}, u32[]{:S(2)}) collective-permute-start(bf16[256,512]{1,0:T(8,128)(2,1)S(1)} %constant_dynamic-update-slice_fusion.own_ref), channel_id=1, source_target_pairs={{0,1},{1,2},{2,3},{4,5},{5,6},{6,7},{8,9},{9,10},{10,11},{12,13},{... | collective-permute-start | bytes 786440 | tf_op jit(solution)/shard_map/ppermute | solution.py:273
  41.1 1.5 %collective-permute-start.10 = (bf16[128,1024]{1,0:T(8,128)(2,1)}, bf16[128,1024]{1,0:T(8,128)(2,1)}, u32[]{:S(2)}, u32[]{:S(2)}) collective-permute-start(bf16[128,1024]{1,0:T(8,128)(2,1)} %collective-permute-done.1.rest_1_), channel_id=1, source_target_pairs={{0,16},{4,20},{8,24},{12,28},{16,0},{20,4},{24,8},{28,12},{1,17},{... | collective-permute-start | bytes 786440 | tf_op jit(solution)/shard_map/ppermute | solution.py:264
  42.6 2.9 %collective-permute-done.5.above_ref = bf16[256,512]{1,0:T(8,128)(2,1)S(1)} collective-permute-done((bf16[256,512]{1,0:T(8,128)(2,1)S(1)}, bf16[256,512]{1,0:T(8,128)(2,1)S(1)}, u32[]{:S(2)}, u32[]{:S(2)}) %collective-permute-start.5) | collective-permute-done | bytes 262176 | tf_op jit(solution)/shard_map/ppermute | solution.py:274
  45.5 3.5 %collective-permute-start.7 = (bf16[256,512]{1,0:T(8,128)(2,1)S(1)}, bf16[256,512]{1,0:T(8,128)(2,1)}, u32[]{:S(2)}, u32[]{:S(2)}) collective-permute-start(bf16[256,512]{1,0:T(8,128)(2,1)S(1)} %constant_dynamic-update-slice_fusion.own_ref), channel_id=1, source_target_pairs={{0,3},{3,0},{4,7},{7,4},{8,11},{11,8},{12,15},{15,12},{16,19},{19,... | collective-permute-start | bytes 786440 | tf_op jit(solution)/shard_map/ppermute | solution.py:275
  49.0 1.5 %collective-permute-start.13 = (bf16[128,1024]{1,0:T(8,128)(2,1)}, bf16[128,1024]{1,0:T(8,128)(2,1)}, u32[]{:S(2)}, u32[]{:S(2)}) collective-permute-start(bf16[128,1024]{1,0:T(8,128)(2,1)} %copy-done.2), channel_id=1, source_target_pairs={{0,8},{4,12},{8,0},{12,4},{16,24},{20,28},{24,16},{28,20},{1,9},{5... | collective-permute-start | bytes 786440 | tf_op jit(solution)/shard_map/ppermute | solution.py:264
  50.5 0.7 %select_select_fusion = bf16[256,512]{1,0:T(8,128)(2,1)} fusion(bf16[256,512]{1,0:T(8,128)(2,1)S(1)} %collective-permute-done.5.above_ref, bf16[256,512]{1,0:T(8,128)(2,1)S(1)} %collective-permute-done.4.below_ref, bf16[256,512]{1,0:T(8,128)(2,1)S(1)} %constant_dynamic-update-slice_fusion.own_ref, pred[]{:T(512)S(6)} %eq.9, pred[]{:T(512)S(6)} %eq.8), kind=kLoop, calls=%fused_computation.1 | loop fusion | flops 262144 | bytes 1048578 | tf_op jit(solution)/shard_map/jit(_where)/select_n | solution.py:276
  51.2 1.1 %collective-permute-start.6 = (bf16[256,512]{1,0:T(8,128)(2,1)}, bf16[256,512]{1,0:T(8,128)(2,1)}, u32[]{:S(2)}, u32[]{:S(2)}) collective-permute-start(bf16[256,512]{1,0:T(8,128)(2,1)} %select_select_fusion), channel_id=1, source_target_pairs={{0,2},{3,1},{2,3},{1,0},{4,6},{7,5},{6,7},{5,4},{8,10},{11,9},{10,... | collective-permute-start | bytes 786440 | tf_op jit(solution)/shard_map/ppermute | solution.py:277
  52.3 0.7 %slice.25 = bf16[128,1024]{1,0:T(8,128)(2,1)} slice(bf16[384,1024]{1,0:T(8,128)(2,1)S(1)} %collective-permute-done.9.rest_3_), slice={[256:384], [0:1024]} | slice | bytes 524288 | tf_op jit(solution)/shard_map/slice | solution.py:358
  53.6 0.7 %slice.24 = bf16[128,1024]{1,0:T(8,128)(2,1)} slice(bf16[384,1024]{1,0:T(8,128)(2,1)S(1)} %collective-permute-done.8.rest_2_), slice={[0:128], [0:1024]} | slice | bytes 524288 | tf_op jit(solution)/shard_map/slice | solution.py:357
  54.3 1.5 %collective-permute-start.11 = (bf16[128,1024]{1,0:T(8,128)(2,1)}, bf16[128,1024]{1,0:T(8,128)(2,1)}, u32[]{:S(2)}, u32[]{:S(2)}) collective-permute-start(bf16[128,1024]{1,0:T(8,128)(2,1)} %slice.24), channel_id=1, source_target_pairs={{0,16},{4,20},{8,24},{12,28},{16,0},{20,4},{24,8},{28,12},{1,17},{... | collective-permute-start | bytes 786440 | tf_op jit(solution)/shard_map/ppermute | solution.py:264
  55.9 2.7 %collective-permute-done.13.rest_8_ = bf16[128,1024]{1,0:T(8,128)(2,1)} collective-permute-done((bf16[128,1024]{1,0:T(8,128)(2,1)}, bf16[128,1024]{1,0:T(8,128)(2,1)}, u32[]{:S(2)}, u32[]{:S(2)}) %collective-permute-start.13) | collective-permute-done | bytes 262176 | tf_op jit(solution)/shard_map/ppermute | solution.py:264
  58.6 3.8 %collective-permute-done.6.middle_ref = bf16[256,512]{1,0:T(8,128)(2,1)} collective-permute-done((bf16[256,512]{1,0:T(8,128)(2,1)}, bf16[256,512]{1,0:T(8,128)(2,1)}, u32[]{:S(2)}, u32[]{:S(2)}) %collective-permute-start.6) | collective-permute-done | bytes 262176 | tf_op jit(solution)/shard_map/ppermute | solution.py:277
  62.4 0.9 %copy-done.3 = bf16[128,1024]{1,0:T(8,128)(2,1)S(1)} copy-done((bf16[128,1024]{1,0:T(8,128)(2,1)S(1)}, bf16[128,1024]{1,0:T(8,128)(2,1)}, u32[]{:S(2)}) %copy-start.3) | copy-done | bytes 262168
  63.4 3.3 %project.1 = (f32[128,1024]{1,0:T(8,128)S(1)}, bf16[128,1024]{1,0:T(8,128)(2,1)S(1)}) custom-call(s32[2]{0:T(128)S(1)} %pad_add_fusion.at_ref, bf16[256,512]{1,0:T(8,128)(2,1)S(1)} %constant_dynamic-update-slice_fusion.own_ref, bf16[256,512]{1,0:T(8,128)(2,1)S(1)} %collective-permute-done.4.below_ref, bf16[256,512]{1,0:T(8,128)(2,1)S(1)} %collective-permute-done.5.above_ref, ...), custom_call_target="tpu_custom_call" | custom-call | flops 100000000 | bytes 1000000 | tf_op jit(solution)/shard_map/project/pallas_call | solution.py:53
  66.7 1.5 %collective-permute-done.14 = bf16[128,1024]{1,0:T(8,128)(2,1)S(1)} collective-permute-done((bf16[128,1024]{1,0:T(8,128)(2,1)S(1)}, bf16[128,1024]{1,0:T(8,128)(2,1)S(1)}, u32[]{:S(2)}, u32[]{:S(2)}) %collective-permute-start.14) | collective-permute-done | bytes 262176 | tf_op jit(solution)/shard_map/ppermute | solution.py:264
  68.2 0.8 %add_convert_fusion = bf16[128,1024]{1,0:T(8,128)(2,1)} fusion(f32[128,1024]{1,0:T(8,128)S(1)} %get-tuple-element.45, bf16[128,1024]{1,0:T(8,128)(2,1)S(1)} %collective-permute-done.14), kind=kLoop, calls=%fused_computation | loop fusion | flops 393216 | bytes 1048576 | tf_op jit(solution)/shard_map/convert_element_type | solution.py:375
  (36 shorter events, 1.7 us)
Async XLA Ops:
  0.0 1.1 %copy-start.1 = (bf16[3,1024,128]{2,1,0:T(8,128)(2,1)S(1)}, bf16[3,1024,128]{2,1,0:T(8,128)(2,1)}, u32[]{:S(2)}) copy-start(bf16[3,1024,128]{2,1,0:T(8,128)(2,1)} %streams_ref.3) | copy-start | bytes 2359300
  1.4 7.7 %copy-start.4 = (f32[3,7,1024]{2,1,0:T(8,128)S(1)}, f32[3,7,1024]{2,1,0:T(8,128)}, u32[]{:S(2)}) copy-start(f32[3,7,1024]{2,1,0:T(8,128)} %taps_ref.3) | copy-start | bytes 258052
  1.4 7.7 %copy-start.7 = (f32[128,16]{0,1:T(8,128)S(1)}, f32[128,16]{0,1:T(8,128)}, u32[]{:S(2)}) copy-start(f32[128,16]{0,1:T(8,128)} %param.8) | copy-start | bytes 24580
  1.4 10.3 %collective-permute-start = (bf16[3,8,1024]{2,1,0:T(8,128)(2,1)S(1)}, bf16[3,8,1024]{2,1,0:T(8,128)(2,1)S(1)}, u32[]{:S(2)}, u32[]{:S(2)}) collective-permute-start(bf16[3,8,1024]{2,1,0:T(8,128)(2,1)S(1)} %tails.1), channel_id=1, source_target_pairs={{0,4},{4,8},{8,12},{12,16},{16,20},{20,24},{24,28},{1,5},{5,9},{9,... | collective-permute-start | bytes 147464 | tf_op jit(solution)/shard_map/ppermute | solution.py:24
  5.0 12.4 %collective-permute-start.2 = (bf16[128,1024]{1,0:T(8,128)(2,1)S(1)}, bf16[128,1024]{1,0:T(8,128)(2,1)S(1)}, u32[]{:S(2)}, u32[]{:S(2)}) collective-permute-start(bf16[128,1024]{1,0:T(8,128)(2,1)S(1)} %get-tuple-element.49), channel_id=1, source_target_pairs={{0,16},{4,20},{8,24},{12,28},{16,0},{20,4},{24,8},{28,12},{1,17},{... | collective-permute-start | bytes 786440 | tf_op jit(solution)/shard_map/ppermute | solution.py:264
  7.6 9.9 %collective-permute-start.1 = (bf16[128,1024]{1,0:T(8,128)(2,1)S(1)}, bf16[128,1024]{1,0:T(8,128)(2,1)}, u32[]{:S(2)}, u32[]{:S(2)}) collective-permute-start(bf16[128,1024]{1,0:T(8,128)(2,1)S(1)} %get-tuple-element.50), channel_id=1, source_target_pairs={{0,8},{4,12},{8,0},{12,4},{16,24},{20,28},{24,16},{28,20},{1,9},{5... | collective-permute-start | bytes 786440 | tf_op jit(solution)/shard_map/ppermute | solution.py:264
  11.7 12.5 %copy-start = (bf16[512,1024]{1,0:T(8,128)(2,1)S(1)}, bf16[512,1024]{1,0:T(8,128)(2,1)}, u32[]{:S(2)}) copy-start(bf16[512,1024]{1,0:T(8,128)(2,1)} %rest_0_.1) | copy-start | bytes 3145732
  13.2 0.7 %copy-start.5 = (bf16[128,1024]{1,0:T(8,128)(2,1)}, bf16[128,1024]{1,0:T(8,128)(2,1)S(1)}, u32[]{:S(2)}) copy-start(bf16[128,1024]{1,0:T(8,128)(2,1)S(1)} %get-tuple-element.33.gated_ref) | copy-start | bytes 786436
  14.0 10.3 %all-to-all-start = ((bf16[8,16,1024]{2,1,0:T(8,128)(2,1)}), bf16[8,16,1024]{2,1,0:T(8,128)(2,1)S(1)}, u32[]{:S(2)}, u32[]{:S(2)}) async-start(bf16[8,16,1024]{2,1,0:T(8,128)(2,1)} %get-tuple-element.29), calls=%async_computation | async-start | bytes 524288 | tf_op jit(solution)/shard_map/all_to_all | solution.py:318
  17.5 8.1 %copy-start.2 = (bf16[128,1024]{1,0:T(8,128)(2,1)}, bf16[128,1024]{1,0:T(8,128)(2,1)S(1)}, u32[]{:S(2)}) copy-start(bf16[128,1024]{1,0:T(8,128)(2,1)S(1)} %collective-permute-done.2.rest_4_) | copy-start | bytes 786436
  17.5 9.2 %copy-start.8 = (f32[128,16]{0,1:T(8,128)S(1)}, f32[128,16]{0,1:T(8,128)}, u32[]{:S(2)}) copy-start(f32[128,16]{0,1:T(8,128)} %param.9) | copy-start | bytes 24580
  24.2 2.5 %copy-start.6 = (bf16[128,1024]{1,0:T(8,128)(2,1)S(1)}, bf16[128,1024]{1,0:T(8,128)(2,1)}, u32[]{:S(2)}) copy-start(bf16[128,1024]{1,0:T(8,128)(2,1)} %copy-done.5) | copy-start | bytes 786436
  25.6 1.1 %copy-start.9 = (f32[1024]{0:T(1024)S(1)}, f32[1024]{0:T(1024)}, u32[]{:S(2)}) copy-start(f32[1024]{0:T(1024)} %param.10) | copy-start | bytes 12292
  25.6 25.6 %collective-permute-start.9 = (bf16[384,1024]{1,0:T(8,128)(2,1)}, bf16[384,1024]{1,0:T(8,128)(2,1)S(1)}, u32[]{:S(2)}, u32[]{:S(2)}) collective-permute-start(bf16[384,1024]{1,0:T(8,128)(2,1)} %get-tuple-element.47), channel_id=1, source_target_pairs={{0,16},{4,20},{8,24},{12,28},{16,0},{20,4},{24,8},{28,12},{1,17},{... | collective-permute-start | bytes 2359304 | tf_op jit(solution)/shard_map/ppermute | solution.py:264
  26.1 26.9 %collective-permute-start.8 = (bf16[384,1024]{1,0:T(8,128)(2,1)}, bf16[384,1024]{1,0:T(8,128)(2,1)S(1)}, u32[]{:S(2)}, u32[]{:S(2)}) collective-permute-start(bf16[384,1024]{1,0:T(8,128)(2,1)} %get-tuple-element.48), channel_id=1, source_target_pairs={{0,8},{4,12},{8,0},{12,4},{16,24},{20,28},{24,16},{28,20},{1,9},{5... | collective-permute-start | bytes 2359304 | tf_op jit(solution)/shard_map/ppermute | solution.py:264
  33.9 1.3 %collective-permute-start.3 = (bf16[128,512]{1,0:T(8,128)(2,1)S(1)}, bf16[128,512]{1,0:T(8,128)(2,1)S(1)}, u32[]{:S(2)}, u32[]{:S(2)}) collective-permute-start(bf16[128,512]{1,0:T(8,128)(2,1)S(1)} %get-tuple-element.39), channel_id=1, source_target_pairs={{0,4},{4,0},{8,12},{12,8},{16,20},{20,16},{24,28},{28,24},{1,5},{5... | collective-permute-start | bytes 393224 | tf_op jit(solution)/shard_map/ppermute | solution.py:264
  35.2 10.3 %collective-permute-start.5 = (bf16[256,512]{1,0:T(8,128)(2,1)S(1)}, bf16[256,512]{1,0:T(8,128)(2,1)S(1)}, u32[]{:S(2)}, u32[]{:S(2)}) collective-permute-start(bf16[256,512]{1,0:T(8,128)(2,1)S(1)} %constant_dynamic-update-slice_fusion.own_ref), channel_id=1, source_target_pairs={{1,0},{2,1},{3,2},{5,4},{6,5},{7,6},{9,8},{10,9},{11,10},{13,12},{... | collective-permute-start | bytes 786440 | tf_op jit(solution)/shard_map/ppermute | solution.py:274
  36.5 12.4 %collective-permute-start.4 = (bf16[256,512]{1,0:T(8,128)(2,1)S(1)}, bf16[256,512]{1,0:T(8,128)(2,1)S(1)}, u32[]{:S(2)}, u32[]{:S(2)}) collective-permute-start(bf16[256,512]{1,0:T(8,128)(2,1)S(1)} %constant_dynamic-update-slice_fusion.own_ref), channel_id=1, source_target_pairs={{0,1},{1,2},{2,3},{4,5},{5,6},{6,7},{8,9},{9,10},{10,11},{12,13},{... | collective-permute-start | bytes 786440 | tf_op jit(solution)/shard_map/ppermute | solution.py:273
  41.1 13.3 %collective-permute-start.10 = (bf16[128,1024]{1,0:T(8,128)(2,1)}, bf16[128,1024]{1,0:T(8,128)(2,1)}, u32[]{:S(2)}, u32[]{:S(2)}) collective-permute-start(bf16[128,1024]{1,0:T(8,128)(2,1)} %collective-permute-done.1.rest_1_), channel_id=1, source_target_pairs={{0,16},{4,20},{8,24},{12,28},{16,0},{20,4},{24,8},{28,12},{1,17},{... | collective-permute-start | bytes 786440 | tf_op jit(solution)/shard_map/ppermute | solution.py:264
  45.5 13.1 %collective-permute-start.7 = (bf16[256,512]{1,0:T(8,128)(2,1)S(1)}, bf16[256,512]{1,0:T(8,128)(2,1)}, u32[]{:S(2)}, u32[]{:S(2)}) collective-permute-start(bf16[256,512]{1,0:T(8,128)(2,1)S(1)} %constant_dynamic-update-slice_fusion.own_ref), channel_id=1, source_target_pairs={{0,3},{3,0},{4,7},{7,4},{8,11},{11,8},{12,15},{15,12},{16,19},{19,... | collective-permute-start | bytes 786440 | tf_op jit(solution)/shard_map/ppermute | solution.py:275
  49.0 9.6 %collective-permute-start.13 = (bf16[128,1024]{1,0:T(8,128)(2,1)}, bf16[128,1024]{1,0:T(8,128)(2,1)}, u32[]{:S(2)}, u32[]{:S(2)}) collective-permute-start(bf16[128,1024]{1,0:T(8,128)(2,1)} %copy-done.2), channel_id=1, source_target_pairs={{0,8},{4,12},{8,0},{12,4},{16,24},{20,28},{24,16},{28,20},{1,9},{5... | collective-permute-start | bytes 786440 | tf_op jit(solution)/shard_map/ppermute | solution.py:264
  51.2 11.2 %collective-permute-start.6 = (bf16[256,512]{1,0:T(8,128)(2,1)}, bf16[256,512]{1,0:T(8,128)(2,1)}, u32[]{:S(2)}, u32[]{:S(2)}) collective-permute-start(bf16[256,512]{1,0:T(8,128)(2,1)} %select_select_fusion), channel_id=1, source_target_pairs={{0,2},{3,1},{2,3},{1,0},{4,6},{7,5},{6,7},{5,4},{8,10},{11,9},{10,... | collective-permute-start | bytes 786440 | tf_op jit(solution)/shard_map/ppermute | solution.py:277
  53.1 9.3 %collective-permute-start.12 = (bf16[128,1024]{1,0:T(8,128)(2,1)}, bf16[128,1024]{1,0:T(8,128)(2,1)}, u32[]{:S(2)}, u32[]{:S(2)}) collective-permute-start(bf16[128,1024]{1,0:T(8,128)(2,1)} %slice.25), channel_id=1, source_target_pairs={{0,8},{4,12},{8,0},{12,4},{16,24},{20,28},{24,16},{28,20},{1,9},{5... | collective-permute-start | bytes 786440 | tf_op jit(solution)/shard_map/ppermute | solution.py:264
  54.3 8.1 %collective-permute-start.11 = (bf16[128,1024]{1,0:T(8,128)(2,1)}, bf16[128,1024]{1,0:T(8,128)(2,1)}, u32[]{:S(2)}, u32[]{:S(2)}) collective-permute-start(bf16[128,1024]{1,0:T(8,128)(2,1)} %slice.24), channel_id=1, source_target_pairs={{0,16},{4,20},{8,24},{12,28},{16,0},{20,4},{24,8},{28,12},{1,17},{... | collective-permute-start | bytes 786440 | tf_op jit(solution)/shard_map/ppermute | solution.py:264
  62.4 1.0 %copy-start.3 = (bf16[128,1024]{1,0:T(8,128)(2,1)S(1)}, bf16[128,1024]{1,0:T(8,128)(2,1)}, u32[]{:S(2)}) copy-start(bf16[128,1024]{1,0:T(8,128)(2,1)} %copy-done.2) | copy-start | bytes 786436
  66.6 1.6 %collective-permute-start.14 = (bf16[128,1024]{1,0:T(8,128)(2,1)S(1)}, bf16[128,1024]{1,0:T(8,128)(2,1)S(1)}, u32[]{:S(2)}, u32[]{:S(2)}) collective-permute-start(bf16[128,1024]{1,0:T(8,128)(2,1)S(1)} %get-tuple-element.46), channel_id=1, source_target_pairs={{0,4},{4,0},{8,12},{12,8},{16,20},{20,16},{24,28},{28,24},{1,5},{5... | collective-permute-start | bytes 786440 | tf_op jit(solution)/shard_map/ppermute | solution.py:264

commit v7 on v6

--- a/solution.py
+++ b/solution.py
@@ -1,3 +1,4 @@
+import functools
 import math
 
 import jax
@@ -12,7 +13,7 @@
 ROWS = 8
 TILE = 128
 CORES = 2
-FIRST_ROWS = 128
+FIRST_ROWS = 192
 VMEM_LIMIT = 24 * 1024 * 1024
 PLAIN = (((1,), (0,)), ((), ()))
 CONTRACT_LANES = (((1,), (1,)), ((), ()))
@@ -57,7 +58,7 @@
         out_specs=tuple(whole(len(outs))),
         scratch_shapes=scratch,
         compiler_params=pltpu.CompilerParams(vmem_limit_bytes=VMEM_LIMIT),
-        cost_estimate=pl.CostEstimate(flops=flops, bytes_accessed=10**6, transcendentals=0),
+        cost_estimate=pl.CostEstimate(flops=flops, bytes_accessed=flops // 100, transcendentals=0),
         name=name,
     )(*operands)
 
@@ -187,8 +188,7 @@
             impulse.append(scale * jnp.exp(-rate * time))
             lift.append(scale * jnp.exp(-rate * (time + 1.0)))
         states = tile_of(index, in_tile * poles)
-        for part, value in enumerate(halves(jnp.concatenate(lift, axis=0))):
-            lift_ref[part, :, states] = turned(value, unit).astype(BF16)
+        lift_ref[:, states] = turned(jnp.concatenate(lift, axis=0).astype(BF16), unit).astype(BF16)
         high, low = halves(jnp.concatenate(impulse, axis=0))
         response = dot(member, high) + dot(member, low)
         gated = gated_ref[:, chans]
@@ -211,7 +211,7 @@
 def finish_kernel(at_ref, ends_ref, step_ref, lift_ref, query_ref, first_ref, base_ref, mine_ref, other_ref, mixed_ref, state_ref):
     length, channels = mixed_ref.shape
     poles = step_ref.shape[0]
-    in_tile = lift_ref.shape[2] // poles * TILE // channels
+    in_tile = lift_ref.shape[1] // poles * TILE // channels
     me, core = at_ref[0], at_ref[1]
 
     def earlier(block, state):
@@ -226,8 +226,8 @@
         apart = jnp.concatenate([jnp.where(owner == g, entering, 0.0) for g in range(in_tile)], axis=0)
         high, low = halves(apart)
         states = tile_of(index, in_tile * poles)
-        lift = lift_ref[0, :, states]
-        carried = dot(lift, high) + dot(lift, low) + dot(lift_ref[1, :, states], high)
+        lift = lift_ref[:, states]
+        carried = dot(lift, high) + dot(lift, low)
         query = jnp.concatenate([first_ref[:, chans], query_ref[ROWS:, chans]], axis=0)
         mixed_ref[:, chans] = (query * (base_ref[:, chans] + carried)).astype(BF16)
 
@@ -237,26 +237,28 @@
     other_ref[...] = mixed_ref[:, tile_of(1 - core, share)]
 
 
-def project_kernel(at_ref, own_ref, below_ref, above_ref, middle_ref, far_ref, *rest):
-    *weight_refs, mine_ref, other_ref, layers_ref = rest
+def early_kernel(pieces, at_ref, own_ref, up_ref, second_ref, down_ref, *rest):
+    *weight_refs, total_ref, diagonal_ref, layers_ref = rest
     layer, chip = at_ref[0], at_ref[1]
-    edge = (layer == 0) | (layer == 3)
     layers_ref[layer] = own_ref[...]
-    layers_ref[jnp.where(layer == 0, 1, layer - 1)] = jnp.where(layer == 0, above_ref[...], below_ref[...])
-    layers_ref[lax.rem(layer + 2, 4)] = middle_ref[...]
-    layers_ref[jnp.where(edge, 3 - layer, layer + 1)] = jnp.where(edge, far_ref[...], above_ref[...])
-    total, row = None, 0
-    share = own_ref.shape[1]
-    for weight_ref in weight_refs:
-        start = row % share
-        rows = weight_ref.shape[0]
-        block = layers_ref[chip ^ (row // share), :, start : start + rows]
-        term = dot(block, weight_ref[...])
+    layers_ref[lax.rem(layer + 3, 4)] = up_ref[...]
+    layers_ref[lax.rem(layer + 2, 4)] = second_ref[...]
+    layers_ref[lax.rem(layer + 1, 4)] = down_ref[...]
+    total = None
+    for ref, (relation, start) in zip(weight_refs, pieces):
+        term = dot(layers_ref[chip ^ relation, :, start : start + ref.shape[0]], ref[...])
         total = term if total is None else total + term
-        row += rows
-    length = mine_ref.shape[0]
-    mine_ref[...] = total[:length]
-    other_ref[...] = total[length:].astype(BF16)
+    total_ref[...] = total
+    diagonal_ref[...] = layers_ref[chip ^ 3]
+
+
+def late_kernel(first, pieces, total_ref, diagonal_ref, *rest):
+    *weight_refs, out_ref = rest
+    tokens = pl.ds(first, out_ref.shape[0])
+    total = total_ref[tokens, :]
+    for ref, start in zip(weight_refs, pieces):
+        total = total + dot(diagonal_ref[tokens, start : start + ref.shape[0]], ref[...])
+    out_ref[...] = total.astype(out_ref.dtype)
 
 
 def swap(value, bit):
@@ -268,14 +270,9 @@
     return lax.optimization_barrier((value, earlier))[0]
 
 
-def over_layers(block):
-    layer = lax.axis_index("tp")
-    below = lax.ppermute(block, "tp", [(0, 1), (1, 2), (2, 3)])
-    above = lax.ppermute(block, "tp", [(1, 0), (2, 1), (3, 2)])
-    far = lax.ppermute(block, "tp", [(0, 3), (3, 0)])
-    onward = jnp.where(layer == 1, above, jnp.where(layer == 2, below, block))
-    middle = lax.ppermute(onward, "tp", [(0, 2), (3, 1), (2, 3), (1, 0)])
-    return below, above, middle, far
+def around(value, steps):
+    count = lax.axis_size("tp")
+    return lax.ppermute(value, "tp", [(source, (source + steps) % count) for source in range(count)])
 
 
 def local(streams, conv_weight, rates, residues, skip, out_weight):
@@ -287,12 +284,14 @@
     square = blocks == 8 and rows == share
 
     rates, residues, skip = rates.T, residues.T, skip[None, :]
+    piece, half = FIRST_ROWS, rows // 2
+    if square:
+        upper, lower = out_weight[:piece], out_weight[rows - piece :]
+        streams, upper, lower = lax.optimization_barrier((streams, upper, lower))
     (tails,) = call(tails_kernel, [((3, ROWS, channels), BF16)], "tails", streams)
     before = from_behind(tails, "ctx", 1)
-    piece, half = FIRST_ROWS, rows // 2
     if square:
-        across_first = swap(after(out_weight, tails)[:piece], 2)
-        along_first = swap(after(out_weight, tails)[rows - piece :], 4)
+        across_first, along_first = swap(upper, 2), swap(lower, 4)
     tiles = channels // TILE
     heads, query, gated, decay, step = call(
         prepare_kernel,
@@ -318,15 +317,16 @@
     all_ends = lax.all_to_all(ends, "ctx", split_axis=0, concat_axis=0, tiled=True)
     if square:
         gated, across_first, along_first = lax.optimization_barrier((gated, across_first, along_first))
-        across_rest = swap(after(out_weight, all_ends)[piece:], 2)
-        along_rest = swap(after(out_weight, all_ends)[: rows - piece], 4)
     lift, base = call(
         inside_kernel,
-        [((2, length, groups * poles), BF16), ((length, channels), F32)],
+        [((length, groups * poles), BF16), ((length, channels), F32)],
         "inside",
         gated, skip, rates, residues,
         flops=10**9,
     )
+    if square:
+        across_rest = swap(after(after(out_weight, base)[piece:], all_ends), 2)
+        along_rest = swap(after(after(out_weight, base)[: rows - piece], all_ends), 4)
     me = lax.axis_index("ctx").astype(jnp.int32)
     core = me % CORES
     smem = [pl.BlockSpec(memory_space=pltpu.SMEM)]
@@ -346,31 +346,46 @@
         other = lax.dynamic_index_in_dim(by_core, 1 - core, 0, keepdims=False)
     block = jnp.concatenate([mine, swap(other, 1)], axis=0)
     layer = lax.axis_index("tp").astype(jnp.int32)
+    up, down = around(block, 1), around(block, -1)
+    second = around(after(up, down), 1)
     if square:
         weight = (
-            out_weight,
-            across_first,
-            across_rest,
-            along_rest,
-            along_first,
-            swap(after(across_first, block), 4),
-            swap(across_rest[: half - piece], 4),
-            swap(along_rest[half:], 2),
-            swap(after(along_first, block), 2),
+            (0, 0, out_weight),
+            (1, 0, across_first),
+            (1, piece, across_rest),
+            (2, 0, along_rest),
+            (2, rows - piece, along_first),
+            (3, 0, swap(after(across_first, (block, across_rest)), 4)),
+            (3, rows - piece, swap(after(along_first, (block, along_rest)), 2)),
+        )
+        last = (
+            (piece, swap(after(across_rest, block)[: half - piece], 4)),
+            (half, swap(after(along_rest, block)[half:], 2)),
         )
     else:
         core_groups = [list(range(core, blocks, CORES)) for core in range(CORES)]
         weight = lax.all_gather(out_weight, "ctx", axis=0, axis_index_groups=core_groups)
-        weight = tuple(weight.reshape(layers, share, features))
+        weight = tuple((index, 0, part) for index, part in enumerate(weight.reshape(layers, share, features)))
+        last = ()
     chip = me // CORES if square else jnp.zeros_like(me)
-    mine, other = call(
-        project_kernel,
-        [((length, features), F32), ((length, features), BF16)],
-        "project",
-        jnp.stack([layer, chip]), block, *over_layers(block), *weight,
-        specs=smem + whole(5 + len(weight)),
+    total, diagonal = call(
+        functools.partial(early_kernel, [part[:2] for part in weight]),
+        [((CORES * length, features), F32), (block.shape, BF16)],
+        "early",
+        jnp.stack([layer, chip]), block, up, second, down, *(part[2] for part in weight),
+        specs=smem + whole(4 + len(weight)),
         scratch=[pltpu.VMEM((layers,) + block.shape, BF16)],
-    )
+        flops=10**9,
+    )
+    sides = []
+    for side, kind in ((1, BF16), (0, F32)):
+        sides += call(
+            functools.partial(late_kernel, side * length, [part[0] for part in last]),
+            [((length, features), kind)],
+            "late",
+            total, diagonal, *(part[1] for part in last),
+        )
+    other, mine = sides
     other = swap(other, 1)
     return (mine + other.astype(F32)).astype(BF16)
 

time: 69.4 us -> 71 us (1.023)
  local copies, waits for them, and re-layouts: 6.68 us -> 10 us
  starting transfers between devices: 26.7 us -> 25.8 us
  other arithmetic: 1.65 us -> 0.91 us
    all_to_all x1, waiting for transfers between devices: 6.75 us -> 0.01 us  [local(): lax.all_to_all(ends, 'ctx', split_axis=0, concat_axis=0, tiled=True)]
    ppermute x4 -> x3, waiting for transfers between devices: 6.67 us -> 13.2 us  [around(): lax.ppermute(value, 'tp', [(source, (source + steps) % count) for source...]
    ppermute x4 -> x3, starting transfers between devices: 10.4 us -> 5.01 us  [around(): lax.ppermute(value, 'tp', [(source, (source + steps) % count) for source...]
    all_to_all x1, starting transfers between devices: 3.41 us -> 7.53 us  [local(): lax.all_to_all(ends, 'ctx', split_axis=0, concat_axis=0, tiled=True)]
    unnamed x21 -> x37, local copies, waits for them, and re-layouts: 2.83 us -> 6.6 us
    ppermute x10, starting transfers between devices: 10.4 us -> 11.9 us  [swap(): lax.ppermute(value, 'ctx', [(source, source ^ bit) for source in range(co...]
    ppermute x1, starting transfers between devices: 2.5 us -> 1.3 us  [from_behind(): lax.ppermute(value, axis, [(source, source + steps) for source in range(l...]
    select_n x1 -> x0, other arithmetic: 0.74 us -> none  [over_layers(): onward = jnp.where(layer == 1, above, jnp.where(layer == 2, below, block))]
  transfers between devices with their start and end apart: 16 -> 15, of which waited for: 6 -> 6; matrix products, arithmetic and copies ran while one was open for 5% -> 2% of each run, Pallas kernels for 16% -> 21%
where the time goes in v7:
time: 71 us; the launch traced here: 70.4 us
  starting transfers between devices  25.8 us (36%)
  waiting for transfers between devices  18.7 us (26%)
  Pallas kernels  14.9 us (21%)
  local copies, waits for them, and re-layouts  10 us (14%)
  other arithmetic  0.91 us (1%)
    pallas_call x8, Pallas kernels, call(): pl.pallas_call(kernel, out_shape=tuple((jax.ShapeDtypeStruct(*out) for ou...  14.9 us
    ppermute x3, waiting for transfers between devices, around(): lax.ppermute(value, 'tp', [(source, (source + steps) % count) for source...  13.2 us
    ppermute x10, starting transfers between devices, swap(): lax.ppermute(value, 'ctx', [(source, source ^ bit) for source in range(co...  11.9 us
    all_to_all x1, starting transfers between devices, local(): lax.all_to_all(ends, 'ctx', split_axis=0, concat_axis=0, tiled=True)  7.53 us
    unnamed x37, local copies, waits for them, and re-layouts  6.6 us
    ppermute x10, waiting for transfers between devices, swap(): lax.ppermute(value, 'ctx', [(source, source ^ bit) for source in range(co...  5.45 us
    ppermute x3, starting transfers between devices, around(): lax.ppermute(value, 'tp', [(source, (source + steps) % count) for source...  5.01 us
    slice x1, local copies, waits for them, and re-layouts, local(): upper, lower = (out_weight[:piece], out_weight[rows - piece:])  2.13 us
  transfers between devices with their start and end apart: 15, of which 6 were waited for; matrix products, arithmetic and copies ran while one was open for 2% of the time, Pallas kernels for 21%

profile of v7, /device:TPU:0, one launch (start us, length us, event | category | flops | bytes accessed | tf_op | source)
XLA Modules:
  0.0 70.4 jit_solution(10940268675894320262)
XLA Ops:
  0.0 2.1 %fusion.1 = (bf16[192,1024]{1,0:T(8,128)(2,1)}, bf16[192,1024]{1,0:T(8,128)(2,1)}) fusion(bf16[512,1024]{1,0:T(8,128)(2,1)} %rest_0_.1), kind=kLoop, calls=%fused_computation.6 | loop fusion | bytes 1572864 | tf_op jit(solution)/shard_map/slice | solution.py:289
  2.1 2.9 %collective-permute-start.1 = (bf16[192,1024]{1,0:T(8,128)(2,1)}, bf16[192,1024]{1,0:T(8,128)(2,1)S(1)}, u32[]{:S(2)}, u32[]{:S(2)}) collective-permute-start(bf16[192,1024]{1,0:T(8,128)(2,1)} %get-tuple-element.40), channel_id=1, source_target_pairs={{0,8},{4,12},{8,0},{12,4},{16,24},{20,28},{24,16},{28,20},{1,9},{5... | collective-permute-start | bytes 1179656 | tf_op jit(solution)/shard_map/ppermute | solution.py:266
  5.1 1.5 %collective-permute-start.2 = (bf16[192,1024]{1,0:T(8,128)(2,1)}, bf16[192,1024]{1,0:T(8,128)(2,1)S(1)}, u32[]{:S(2)}, u32[]{:S(2)}) collective-permute-start(bf16[192,1024]{1,0:T(8,128)(2,1)} %get-tuple-element.41), channel_id=1, source_target_pairs={{0,16},{4,20},{8,24},{12,28},{16,0},{20,4},{24,8},{28,12},{1,17},{... | collective-permute-start | bytes 1179656 | tf_op jit(solution)/shard_map/ppermute | solution.py:266
  6.9 1.3 %collective-permute-start = (bf16[3,8,1024]{2,1,0:T(8,128)(2,1)S(1)}, bf16[3,8,1024]{2,1,0:T(8,128)(2,1)S(1)}, u32[]{:S(2)}, u32[]{:S(2)}) collective-permute-start(bf16[3,8,1024]{2,1,0:T(8,128)(2,1)S(1)} %tails.1), channel_id=1, source_target_pairs={{0,4},{4,8},{8,12},{12,16},{16,20},{20,24},{24,28},{1,5},{5,9},{9,... | collective-permute-start | bytes 147464 | tf_op jit(solution)/shard_map/ppermute | solution.py:25
  8.2 2.6 %prepare.1 = (f32[3,8,1024]{2,1,0:T(8,128)S(1)}, f32[128,1024]{1,0:T(8,128)S(1)}, f32[128,1024]{1,0:T(8,128)S(1)}, bf16[2,2048,128]{2,1,0:T(8,128)(2,1)S(1)}, f32[16,1024]{1,0:T(8,128)S(1)}) custom-call(bf16[3,1024,128]{2,1,0:T(8,128)(2,1)S(1)} %copy-done.1, f32[3,7,1024]{2,1,0:T(8,128)S(1)} %copy-done.10, f32[16,128]{1,0:T(8,128)S(1)} %bitcast.7), custom_call_target="tpu_custom_call" | custom-call | flops 1000000000 | bytes 10000000 | tf_op jit(solution)/shard_map/prepare/pallas_call | solution.py:54
  10.9 1.5 %states.1 = (bf16[8,16,1024]{2,1,0:T(8,128)(2,1)}, bf16[128,1024]{1,0:T(8,128)(2,1)S(1)}, f32[8,1024]{1,0:T(8,128)S(1)}) custom-call(bf16[3,8,1024]{2,1,0:T(8,128)(2,1)S(1)} %collective-permute-done.before_ref, f32[3,8,1024]{2,1,0:T(8,128)S(1)} %get-tuple-element.34.heads_ref, f32[3,7,1024]{2,1,0:T(8,128)S(1)} %copy-done.10, ...), custom_call_target="tpu_custom_call" | custom-call | flops 100000000 | bytes 1000000 | tf_op jit(solution)/shard_map/states/pallas_call | solution.py:54
  13.0 7.5 %all-to-all-start = ((bf16[8,16,1024]{2,1,0:T(8,128)(2,1)}), bf16[8,16,1024]{2,1,0:T(8,128)(2,1)S(1)}, u32[]{:S(2)}, u32[]{:S(2)}) async-start(bf16[8,16,1024]{2,1,0:T(8,128)(2,1)} %get-tuple-element.37), calls=%async_computation | async-start | bytes 524288 | tf_op jit(solution)/shard_map/all_to_all | solution.py:317
  20.6 0.8 %copy-done.6 = bf16[192,1024]{1,0:T(8,128)(2,1)} copy-done((bf16[192,1024]{1,0:T(8,128)(2,1)}, bf16[192,1024]{1,0:T(8,128)(2,1)S(1)}, u32[]{:S(2)}) %copy-start.6) | copy-done | bytes 393240
  21.3 5.0 %inside.1 = (bf16[128,2048]{1,0:T(8,128)(2,1)S(1)}, f32[128,1024]{1,0:T(8,128)S(1)}) custom-call(bf16[128,1024]{1,0:T(8,128)(2,1)S(1)} %get-tuple-element.42.gated_ref, f32[1,1024]{1,0:T(1,128)S(1)} %bitcast.10, f32[16,128]{1,0:T(8,128)S(1)} %bitcast.8, f32[16,128]{1,0:T(8,128)S(1)} %bitcast.9), custom_call_target="tpu_custom_call" | custom-call | flops 1000000000 | bytes 10000000 | tf_op jit(solution)/shard_map/inside/pallas_call | solution.py:54
  26.4 0.8 %copy-done.2 = bf16[128,2048]{1,0:T(8,128)(2,1)} copy-done((bf16[128,2048]{1,0:T(8,128)(2,1)}, bf16[128,2048]{1,0:T(8,128)(2,1)S(1)}, u32[]{:S(2)}) %copy-start.2) | copy-done | bytes 524312
  27.2 1.3 %fusion = (bf16[320,1024]{1,0:T(8,128)(2,1)}, bf16[320,1024]{1,0:T(8,128)(2,1)}) fusion(bf16[512,1024]{1,0:T(8,128)(2,1)S(1)} %copy-done), kind=kLoop, calls=%fused_computation.5 | loop fusion | bytes 2621440 | tf_op jit(solution)/shard_map/slice | solution.py:329
  28.4 2.0 %collective-permute-start.7 = (bf16[320,1024]{1,0:T(8,128)(2,1)}, bf16[320,1024]{1,0:T(8,128)(2,1)S(1)}, u32[]{:S(2)}, u32[]{:S(2)}) collective-permute-start(bf16[320,1024]{1,0:T(8,128)(2,1)} %get-tuple-element.52), channel_id=1, source_target_pairs={{0,8},{4,12},{8,0},{12,4},{16,24},{20,28},{24,16},{28,20},{1,9},{5... | collective-permute-start | bytes 1966088 | tf_op jit(solution)/shard_map/ppermute | solution.py:266
  30.5 1.5 %collective-permute-start.8 = (bf16[320,1024]{1,0:T(8,128)(2,1)}, bf16[320,1024]{1,0:T(8,128)(2,1)S(1)}, u32[]{:S(2)}, u32[]{:S(2)}) collective-permute-start(bf16[320,1024]{1,0:T(8,128)(2,1)} %get-tuple-element.53), channel_id=1, source_target_pairs={{0,16},{4,20},{8,24},{12,28},{16,0},{20,4},{24,8},{28,12},{1,17},{... | collective-permute-start | bytes 1966088 | tf_op jit(solution)/shard_map/ppermute | solution.py:266
  32.0 1.0 %copy-done.3 = bf16[128,2048]{1,0:T(8,128)(2,1)S(1)} copy-done((bf16[128,2048]{1,0:T(8,128)(2,1)S(1)}, bf16[128,2048]{1,0:T(8,128)(2,1)}, u32[]{:S(2)}) %copy-start.3) | copy-done | bytes 524312
  33.0 1.0 %copy-done.5 = f32[128,1024]{1,0:T(8,128)S(1)} copy-done((f32[128,1024]{1,0:T(8,128)S(1)}, f32[128,1024]{1,0:T(8,128)}, u32[]{:S(2)}) %copy-start.5) | copy-done | bytes 524312
  34.1 0.8 %copy-done.12 = f32[16,1024]{1,0:T(8,128)S(1)} copy-done((f32[16,1024]{1,0:T(8,128)S(1)}, f32[16,1024]{1,0:T(8,128)}, u32[]{:S(2)}) %copy-start.12) | copy-done | bytes 65560
  34.9 0.8 %copy-done.14 = f32[8,1024]{1,0:T(8,128)S(1)} copy-done((f32[8,1024]{1,0:T(8,128)S(1)}, f32[8,1024]{1,0:T(8,128)}, u32[]{:S(2)}) %copy-start.14) | copy-done | bytes 32792
  35.7 1.9 %finish.1 = (bf16[128,512]{1,0:T(8,128)(2,1)S(1)}, bf16[128,512]{1,0:T(8,128)(2,1)S(1)}, bf16[128,1024]{1,0:T(8,128)(2,1)}) custom-call(s32[2]{0:T(128)S(1)} %pad_add_fusion.1.at_ref, bf16[8,16,1024]{2,1,0:T(8,128)(2,1)S(1)} %all-to-all-done.ends_ref, f32[16,1024]{1,0:T(8,128)S(1)} %copy-done.12, bf16[128,2048]{1,0:T(8,128)(2,1)S(1)} %copy-done.3, ...), custom_call_target="tpu_custom_call" | custom-call | flops 100000000 | bytes 1000000 | tf_op jit(solution)/shard_map/finish/pallas_call | solution.py:54
  37.6 1.3 %collective-permute-done.3 = bf16[128,512]{1,0:T(8,128)(2,1)S(1)} collective-permute-done((bf16[128,512]{1,0:T(8,128)(2,1)S(1)}, bf16[128,512]{1,0:T(8,128)(2,1)S(1)}, u32[]{:S(2)}, u32[]{:S(2)}) %collective-permute-start.3) | collective-permute-done | bytes 131104 | tf_op jit(solution)/shard_map/ppermute | solution.py:266
  39.0 1.6 %collective-permute-start.4 = (bf16[256,512]{1,0:T(8,128)(2,1)S(1)}, bf16[256,512]{1,0:T(8,128)(2,1)}, u32[]{:S(2)}, u32[]{:S(2)}) collective-permute-start(bf16[256,512]{1,0:T(8,128)(2,1)S(1)} %constant_dynamic-update-slice_fusion.own_ref), channel_id=1, source_target_pairs={{0,1},{1,2},{2,3},{3,0},{4,5},{5,6},{6,7},{7,4},{8,9},{9,10},{10,1... | collective-permute-start | bytes 786440 | tf_op jit(solution)/shard_map/ppermute | solution.py:275
  40.6 2.3 %collective-permute-start.5 = (bf16[256,512]{1,0:T(8,128)(2,1)S(1)}, bf16[256,512]{1,0:T(8,128)(2,1)S(1)}, u32[]{:S(2)}, u32[]{:S(2)}) collective-permute-start(bf16[256,512]{1,0:T(8,128)(2,1)S(1)} %constant_dynamic-update-slice_fusion.own_ref), channel_id=1, source_target_pairs={{0,3},{1,0},{2,1},{3,2},{4,7},{5,4},{6,5},{7,6},{8,11},{9,8},{10,9... | collective-permute-start | bytes 786440 | tf_op jit(solution)/shard_map/ppermute | solution.py:275
  42.9 2.9 %collective-permute-done.7.rest_2_ = bf16[320,1024]{1,0:T(8,128)(2,1)S(1)} collective-permute-done((bf16[320,1024]{1,0:T(8,128)(2,1)}, bf16[320,1024]{1,0:T(8,128)(2,1)S(1)}, u32[]{:S(2)}, u32[]{:S(2)}) %collective-permute-start.7) | collective-permute-done | bytes 655392 | tf_op jit(solution)/shard_map/ppermute | solution.py:266
  45.8 1.7 %collective-permute-start.9 = (bf16[192,1024]{1,0:T(8,128)(2,1)S(1)}, bf16[192,1024]{1,0:T(8,128)(2,1)}, u32[]{:S(2)}, u32[]{:S(2)}) collective-permute-start(bf16[192,1024]{1,0:T(8,128)(2,1)S(1)} %collective-permute-done.1.rest_1_), channel_id=1, source_target_pairs={{0,16},{4,20},{8,24},{12,28},{16,0},{20,4},{24,8},{28,12},{1,17},{... | collective-permute-start | bytes 1179656 | tf_op jit(solution)/shard_map/ppermute | solution.py:266
  47.5 1.5 %collective-permute-start.10 = (bf16[192,1024]{1,0:T(8,128)(2,1)S(1)}, bf16[192,1024]{1,0:T(8,128)(2,1)}, u32[]{:S(2)}, u32[]{:S(2)}) collective-permute-start(bf16[192,1024]{1,0:T(8,128)(2,1)S(1)} %copy-done.7), channel_id=1, source_target_pairs={{0,8},{4,12},{8,0},{12,4},{16,24},{20,28},{24,16},{28,20},{1,9},{5... | collective-permute-start | bytes 1179656 | tf_op jit(solution)/shard_map/ppermute | solution.py:266
  48.9 1.2 %collective-permute-done.4.up_ref = bf16[256,512]{1,0:T(8,128)(2,1)} collective-permute-done((bf16[256,512]{1,0:T(8,128)(2,1)S(1)}, bf16[256,512]{1,0:T(8,128)(2,1)}, u32[]{:S(2)}, u32[]{:S(2)}) %collective-permute-start.4) | collective-permute-done | bytes 262176 | tf_op jit(solution)/shard_map/ppermute | solution.py:275
  50.1 4.2 %collective-permute-done.5.down_ref = bf16[256,512]{1,0:T(8,128)(2,1)S(1)} collective-permute-done((bf16[256,512]{1,0:T(8,128)(2,1)S(1)}, bf16[256,512]{1,0:T(8,128)(2,1)S(1)}, u32[]{:S(2)}, u32[]{:S(2)}) %collective-permute-start.5) | collective-permute-done | bytes 262176 | tf_op jit(solution)/shard_map/ppermute | solution.py:275
  54.3 0.7 copy-done.8
  55.0 1.1 %collective-permute-start.6 = (bf16[256,512]{1,0:T(8,128)(2,1)}, bf16[256,512]{1,0:T(8,128)(2,1)}, u32[]{:S(2)}, u32[]{:S(2)}) collective-permute-start(bf16[256,512]{1,0:T(8,128)(2,1)} %collective-permute-done.4.up_ref), channel_id=1, source_target_pairs={{0,1},{1,2},{2,3},{3,0},{4,5},{5,6},{6,7},{7,4},{8,9},{9,10},{10,1... | collective-permute-start | bytes 786440 | tf_op jit(solution)/shard_map/ppermute | solution.py:275
  57.0 7.9 %collective-permute-done.6.second_ref = bf16[256,512]{1,0:T(8,128)(2,1)} collective-permute-done((bf16[256,512]{1,0:T(8,128)(2,1)}, bf16[256,512]{1,0:T(8,128)(2,1)}, u32[]{:S(2)}, u32[]{:S(2)}) %collective-permute-start.6) | collective-permute-done | bytes 262176 | tf_op jit(solution)/shard_map/ppermute | solution.py:275
  64.9 2.8 %early.1 = (f32[256,1024]{1,0:T(8,128)S(1)}, bf16[256,512]{1,0:T(8,128)(2,1)S(1)}) custom-call(s32[2]{0:T(128)S(1)} %pad_add_fusion.at_ref, bf16[256,512]{1,0:T(8,128)(2,1)S(1)} %constant_dynamic-update-slice_fusion.own_ref, bf16[256,512]{1,0:T(8,128)(2,1)} %collective-permute-done.4.up_ref, bf16[256,512]{1,0:T(8,128)(2,1)} %collective-permute-done.6.second_ref, ...), custom_call_target="tpu_custom_call" | custom-call | flops 1000000000 | bytes 10000000 | tf_op jit(solution)/shard_map/early/pallas_call | solution.py:54
  68.5 1.2 %collective-permute-done.13 = bf16[128,1024]{1,0:T(8,128)(2,1)S(1)} collective-permute-done((bf16[128,1024]{1,0:T(8,128)(2,1)S(1)}, bf16[128,1024]{1,0:T(8,128)(2,1)S(1)}, u32[]{:S(2)}, u32[]{:S(2)}) %collective-permute-start.13) | collective-permute-done | bytes 262176 | tf_op jit(solution)/shard_map/ppermute | solution.py:266
  69.7 0.8 %add_convert_fusion = bf16[128,1024]{1,0:T(8,128)(2,1)} fusion(f32[128,1024]{1,0:T(8,128)S(1)} %late.2, bf16[128,1024]{1,0:T(8,128)(2,1)S(1)} %collective-permute-done.13), kind=kLoop, calls=%fused_computation | loop fusion | flops 393216 | bytes 1048576 | tf_op jit(solution)/shard_map/convert_element_type | solution.py:390
  (51 shorter events, 2.7 us)
Async XLA Ops:
  0.0 6.6 %copy-start.1 = (bf16[3,1024,128]{2,1,0:T(8,128)(2,1)S(1)}, bf16[3,1024,128]{2,1,0:T(8,128)(2,1)}, u32[]{:S(2)}) copy-start(bf16[3,1024,128]{2,1,0:T(8,128)(2,1)} %streams_ref.1) | copy-start | bytes 2359300
  2.1 6.1 %copy-start.10 = (f32[3,7,1024]{2,1,0:T(8,128)S(1)}, f32[3,7,1024]{2,1,0:T(8,128)}, u32[]{:S(2)}) copy-start(f32[3,7,1024]{2,1,0:T(8,128)} %taps_ref.3) | copy-start | bytes 258052
  2.1 6.1 %copy-start.15 = (f32[128,16]{0,1:T(8,128)S(1)}, f32[128,16]{0,1:T(8,128)}, u32[]{:S(2)}) copy-start(f32[128,16]{0,1:T(8,128)} %param.8) | copy-start | bytes 24580
  2.1 18.4 %collective-permute-start.1 = (bf16[192,1024]{1,0:T(8,128)(2,1)}, bf16[192,1024]{1,0:T(8,128)(2,1)S(1)}, u32[]{:S(2)}, u32[]{:S(2)}) collective-permute-start(bf16[192,1024]{1,0:T(8,128)(2,1)} %get-tuple-element.40), channel_id=1, source_target_pairs={{0,8},{4,12},{8,0},{12,4},{16,24},{20,28},{24,16},{28,20},{1,9},{5... | collective-permute-start | bytes 1179656 | tf_op jit(solution)/shard_map/ppermute | solution.py:266
  5.1 15.5 %collective-permute-start.2 = (bf16[192,1024]{1,0:T(8,128)(2,1)}, bf16[192,1024]{1,0:T(8,128)(2,1)S(1)}, u32[]{:S(2)}, u32[]{:S(2)}) collective-permute-start(bf16[192,1024]{1,0:T(8,128)(2,1)} %get-tuple-element.41), channel_id=1, source_target_pairs={{0,16},{4,20},{8,24},{12,28},{16,0},{20,4},{24,8},{28,12},{1,17},{... | collective-permute-start | bytes 1179656 | tf_op jit(solution)/shard_map/ppermute | solution.py:266
  6.9 4.0 %collective-permute-start = (bf16[3,8,1024]{2,1,0:T(8,128)(2,1)S(1)}, bf16[3,8,1024]{2,1,0:T(8,128)(2,1)S(1)}, u32[]{:S(2)}, u32[]{:S(2)}) collective-permute-start(bf16[3,8,1024]{2,1,0:T(8,128)(2,1)S(1)} %tails.1), channel_id=1, source_target_pairs={{0,4},{4,8},{8,12},{12,16},{16,20},{20,24},{24,28},{1,5},{5,9},{9,... | collective-permute-start | bytes 147464 | tf_op jit(solution)/shard_map/ppermute | solution.py:25
  10.8 1.5 %copy-start.11 = (f32[16,1024]{1,0:T(8,128)}, f32[16,1024]{1,0:T(8,128)S(1)}, u32[]{:S(2)}) copy-start(f32[16,1024]{1,0:T(8,128)S(1)} %get-tuple-element.38.step_ref) | copy-start | bytes 196612
  13.0 8.3 %copy-start.16 = (f32[128,16]{0,1:T(8,128)S(1)}, f32[128,16]{0,1:T(8,128)}, u32[]{:S(2)}) copy-start(f32[128,16]{0,1:T(8,128)} %param.9) | copy-start | bytes 24580
  13.0 15.4 %all-to-all-start = ((bf16[8,16,1024]{2,1,0:T(8,128)(2,1)}), bf16[8,16,1024]{2,1,0:T(8,128)(2,1)S(1)}, u32[]{:S(2)}, u32[]{:S(2)}) async-start(bf16[8,16,1024]{2,1,0:T(8,128)(2,1)} %get-tuple-element.37), calls=%async_computation | async-start | bytes 524288 | tf_op jit(solution)/shard_map/all_to_all | solution.py:317
  20.5 0.8 %copy-start.17 = (f32[1024]{0:T(1024)S(1)}, f32[1024]{0:T(1024)}, u32[]{:S(2)}) copy-start(f32[1024]{0:T(1024)} %param.10) | copy-start | bytes 12292
  20.6 0.8 %copy-start.6 = (bf16[192,1024]{1,0:T(8,128)(2,1)}, bf16[192,1024]{1,0:T(8,128)(2,1)S(1)}, u32[]{:S(2)}) copy-start(bf16[192,1024]{1,0:T(8,128)(2,1)S(1)} %collective-permute-done.2.rest_4_) | copy-start | bytes 1179652
  21.3 5.8 %copy-start = (bf16[512,1024]{1,0:T(8,128)(2,1)S(1)}, bf16[512,1024]{1,0:T(8,128)(2,1)}, u32[]{:S(2)}) copy-start(bf16[512,1024]{1,0:T(8,128)(2,1)} %rest_0_.1) | copy-start | bytes 3145732
  26.4 0.8 %copy-start.2 = (bf16[128,2048]{1,0:T(8,128)(2,1)}, bf16[128,2048]{1,0:T(8,128)(2,1)S(1)}, u32[]{:S(2)}) copy-start(bf16[128,2048]{1,0:T(8,128)(2,1)S(1)} %get-tuple-element.43.lift_ref) | copy-start | bytes 1572868
  27.2 1.3 %copy-start.4 = (f32[128,1024]{1,0:T(8,128)}, f32[128,1024]{1,0:T(8,128)S(1)}, u32[]{:S(2)}) copy-start(f32[128,1024]{1,0:T(8,128)S(1)} %get-tuple-element.46.base_ref) | copy-start | bytes 1572868
  28.4 17.3 %collective-permute-start.7 = (bf16[320,1024]{1,0:T(8,128)(2,1)}, bf16[320,1024]{1,0:T(8,128)(2,1)S(1)}, u32[]{:S(2)}, u32[]{:S(2)}) collective-permute-start(bf16[320,1024]{1,0:T(8,128)(2,1)} %get-tuple-element.52), channel_id=1, source_target_pairs={{0,8},{4,12},{8,0},{12,4},{16,24},{20,28},{24,16},{28,20},{1,9},{5... | collective-permute-start | bytes 1966088 | tf_op jit(solution)/shard_map/ppermute | solution.py:266
  30.5 17.0 %collective-permute-start.8 = (bf16[320,1024]{1,0:T(8,128)(2,1)}, bf16[320,1024]{1,0:T(8,128)(2,1)S(1)}, u32[]{:S(2)}, u32[]{:S(2)}) collective-permute-start(bf16[320,1024]{1,0:T(8,128)(2,1)} %get-tuple-element.53), channel_id=1, source_target_pairs={{0,16},{4,20},{8,24},{12,28},{16,0},{20,4},{24,8},{28,12},{1,17},{... | collective-permute-start | bytes 1966088 | tf_op jit(solution)/shard_map/ppermute | solution.py:266
  32.0 1.0 %copy-start.3 = (bf16[128,2048]{1,0:T(8,128)(2,1)S(1)}, bf16[128,2048]{1,0:T(8,128)(2,1)}, u32[]{:S(2)}) copy-start(bf16[128,2048]{1,0:T(8,128)(2,1)} %copy-done.2) | copy-start | bytes 1572868
  33.0 1.0 %copy-start.5 = (f32[128,1024]{1,0:T(8,128)S(1)}, f32[128,1024]{1,0:T(8,128)}, u32[]{:S(2)}) copy-start(f32[128,1024]{1,0:T(8,128)} %copy-done.4) | copy-start | bytes 1572868
  34.1 0.8 %copy-start.12 = (f32[16,1024]{1,0:T(8,128)S(1)}, f32[16,1024]{1,0:T(8,128)}, u32[]{:S(2)}) copy-start(f32[16,1024]{1,0:T(8,128)} %copy-done.11) | copy-start | bytes 196612
  34.9 0.8 %copy-start.14 = (f32[8,1024]{1,0:T(8,128)S(1)}, f32[8,1024]{1,0:T(8,128)}, u32[]{:S(2)}) copy-start(f32[8,1024]{1,0:T(8,128)} %copy-done.13) | copy-start | bytes 98308
  37.6 9.8 %copy-start.7 = (bf16[192,1024]{1,0:T(8,128)(2,1)S(1)}, bf16[192,1024]{1,0:T(8,128)(2,1)}, u32[]{:S(2)}) copy-start(bf16[192,1024]{1,0:T(8,128)(2,1)} %copy-done.6) | copy-start | bytes 1179652
  37.6 1.3 %collective-permute-start.3 = (bf16[128,512]{1,0:T(8,128)(2,1)S(1)}, bf16[128,512]{1,0:T(8,128)(2,1)S(1)}, u32[]{:S(2)}, u32[]{:S(2)}) collective-permute-start(bf16[128,512]{1,0:T(8,128)(2,1)S(1)} %get-tuple-element.48), channel_id=1, source_target_pairs={{0,4},{4,0},{8,12},{12,8},{16,20},{20,16},{24,28},{28,24},{1,5},{5... | collective-permute-start | bytes 393224 | tf_op jit(solution)/shard_map/ppermute | solution.py:266
  39.0 11.1 %collective-permute-start.4 = (bf16[256,512]{1,0:T(8,128)(2,1)S(1)}, bf16[256,512]{1,0:T(8,128)(2,1)}, u32[]{:S(2)}, u32[]{:S(2)}) collective-permute-start(bf16[256,512]{1,0:T(8,128)(2,1)S(1)} %constant_dynamic-update-slice_fusion.own_ref), channel_id=1, source_target_pairs={{0,1},{1,2},{2,3},{3,0},{4,5},{5,6},{6,7},{7,4},{8,9},{9,10},{10,1... | collective-permute-start | bytes 786440 | tf_op jit(solution)/shard_map/ppermute | solution.py:275
  40.6 13.7 %collective-permute-start.5 = (bf16[256,512]{1,0:T(8,128)(2,1)S(1)}, bf16[256,512]{1,0:T(8,128)(2,1)S(1)}, u32[]{:S(2)}, u32[]{:S(2)}) collective-permute-start(bf16[256,512]{1,0:T(8,128)(2,1)S(1)} %constant_dynamic-update-slice_fusion.own_ref), channel_id=1, source_target_pairs={{0,3},{1,0},{2,1},{3,2},{4,7},{5,4},{6,5},{7,6},{8,11},{9,8},{10,9... | collective-permute-start | bytes 786440 | tf_op jit(solution)/shard_map/ppermute | solution.py:275
  45.8 19.1 %collective-permute-start.9 = (bf16[192,1024]{1,0:T(8,128)(2,1)S(1)}, bf16[192,1024]{1,0:T(8,128)(2,1)}, u32[]{:S(2)}, u32[]{:S(2)}) collective-permute-start(bf16[192,1024]{1,0:T(8,128)(2,1)S(1)} %collective-permute-done.1.rest_1_), channel_id=1, source_target_pairs={{0,16},{4,20},{8,24},{12,28},{16,0},{20,4},{24,8},{28,12},{1,17},{... | collective-permute-start | bytes 1179656 | tf_op jit(solution)/shard_map/ppermute | solution.py:266
  47.5 17.4 %collective-permute-start.10 = (bf16[192,1024]{1,0:T(8,128)(2,1)S(1)}, bf16[192,1024]{1,0:T(8,128)(2,1)}, u32[]{:S(2)}, u32[]{:S(2)}) collective-permute-start(bf16[192,1024]{1,0:T(8,128)(2,1)S(1)} %copy-done.7), channel_id=1, source_target_pairs={{0,8},{4,12},{8,0},{12,4},{16,24},{20,28},{24,16},{28,20},{1,9},{5... | collective-permute-start | bytes 1179656 | tf_op jit(solution)/shard_map/ppermute | solution.py:266
  54.3 0.7 copy-start.8
  55.0 9.9 %collective-permute-start.6 = (bf16[256,512]{1,0:T(8,128)(2,1)}, bf16[256,512]{1,0:T(8,128)(2,1)}, u32[]{:S(2)}, u32[]{:S(2)}) collective-permute-start(bf16[256,512]{1,0:T(8,128)(2,1)} %collective-permute-done.4.up_ref), channel_id=1, source_target_pairs={{0,1},{1,2},{2,3},{3,0},{4,5},{5,6},{6,7},{7,4},{8,9},{9,10},{10,1... | collective-permute-start | bytes 786440 | tf_op jit(solution)/shard_map/ppermute | solution.py:275
  56.1 8.7 %copy-start.9 = (bf16[256,512]{1,0:T(8,128)(2,1)S(1)}, bf16[256,512]{1,0:T(8,128)(2,1)}, u32[]{:S(2)}) copy-start(bf16[256,512]{1,0:T(8,128)(2,1)} %copy-done.8) | copy-start | bytes 786436
  56.2 11.6 %collective-permute-start.11 = (bf16[64,1024]{1,0:T(8,128)(2,1)S(1)}, bf16[64,1024]{1,0:T(8,128)(2,1)S(1)}, u32[]{:S(2)}, u32[]{:S(2)}) collective-permute-start(bf16[64,1024]{1,0:T(8,128)(2,1)S(1)} %slice.22), channel_id=1, source_target_pairs={{0,16},{4,20},{8,24},{12,28},{16,0},{20,4},{24,8},{28,12},{1,17},{... | collective-permute-start | bytes 393224 | tf_op jit(solution)/shard_map/ppermute | solution.py:266
  56.8 10.9 %collective-permute-start.12 = (bf16[64,1024]{1,0:T(8,128)(2,1)S(1)}, bf16[64,1024]{1,0:T(8,128)(2,1)S(1)}, u32[]{:S(2)}, u32[]{:S(2)}) collective-permute-start(bf16[64,1024]{1,0:T(8,128)(2,1)S(1)} %slice.23), channel_id=1, source_target_pairs={{0,8},{4,12},{8,0},{12,4},{16,24},{20,28},{24,16},{28,20},{1,9},{5... | collective-permute-start | bytes 393224 | tf_op jit(solution)/shard_map/ppermute | solution.py:266
  68.1 1.6 %collective-permute-start.13 = (bf16[128,1024]{1,0:T(8,128)(2,1)S(1)}, bf16[128,1024]{1,0:T(8,128)(2,1)S(1)}, u32[]{:S(2)}, u32[]{:S(2)}) collective-permute-start(bf16[128,1024]{1,0:T(8,128)(2,1)S(1)} %late.3), channel_id=1, source_target_pairs={{0,4},{4,0},{8,12},{12,8},{16,20},{20,16},{24,28},{28,24},{1,5},{5... | collective-permute-start | bytes 786440 | tf_op jit(solution)/shard_map/ppermute | solution.py:266
  (1 other events, 0.6 us)

commit v8 on v7

--- a/solution.py
+++ b/solution.py
@@ -13,7 +13,7 @@
 ROWS = 8
 TILE = 128
 CORES = 2
-FIRST_ROWS = 192
+COLUMNS = 256
 VMEM_LIMIT = 24 * 1024 * 1024
 PLAIN = (((1,), (0,)), ((), ()))
 CONTRACT_LANES = (((1,), (1,)), ((), ()))
@@ -237,33 +237,28 @@
     other_ref[...] = mixed_ref[:, tile_of(1 - core, share)]
 
 
-def early_kernel(pieces, at_ref, own_ref, up_ref, second_ref, down_ref, *rest):
-    *weight_refs, total_ref, diagonal_ref, layers_ref = rest
-    layer, chip = at_ref[0], at_ref[1]
+def project_kernel(at_ref, own_ref, up_ref, second_ref, down_ref, *rest):
+    *weight_refs, mine_ref, other_ref, layers_ref = rest
+    layer = at_ref[0]
     layers_ref[layer] = own_ref[...]
     layers_ref[lax.rem(layer + 3, 4)] = up_ref[...]
     layers_ref[lax.rem(layer + 2, 4)] = second_ref[...]
     layers_ref[lax.rem(layer + 1, 4)] = down_ref[...]
-    total = None
-    for ref, (relation, start) in zip(weight_refs, pieces):
-        term = dot(layers_ref[chip ^ relation, :, start : start + ref.shape[0]], ref[...])
-        total = term if total is None else total + term
-    total_ref[...] = total
-    diagonal_ref[...] = layers_ref[chip ^ 3]
-
-
-def late_kernel(first, pieces, total_ref, diagonal_ref, *rest):
-    *weight_refs, out_ref = rest
-    tokens = pl.ds(first, out_ref.shape[0])
-    total = total_ref[tokens, :]
-    for ref, start in zip(weight_refs, pieces):
-        total = total + dot(diagonal_ref[tokens, start : start + ref.shape[0]], ref[...])
-    out_ref[...] = total.astype(out_ref.dtype)
-
-
-def swap(value, bit):
+    length, features = mine_ref.shape
+    for column in range(0, features, COLUMNS):
+        columns = slice(column, column + COLUMNS)
+        total = None
+        for at, ref in enumerate(weight_refs):
+            term = dot(layers_ref[at_ref[1 + at]], ref[:, columns])
+            total = term if total is None else total + term
+        mine_ref[:, columns] = total[:length]
+        other_ref[:, columns] = total[length:].astype(BF16)
+
+
+def swap(value, *bits):
     count = lax.axis_size("ctx")
-    return lax.ppermute(value, "ctx", [(source, source ^ bit) for source in range(count)])
+    pairs = [(source, source ^ bits[source % len(bits)]) for source in range(count)]
+    return lax.ppermute(value, "ctx", pairs)
 
 
 def after(value, earlier):
@@ -284,14 +279,10 @@
     square = blocks == 8 and rows == share
 
     rates, residues, skip = rates.T, residues.T, skip[None, :]
-    piece, half = FIRST_ROWS, rows // 2
-    if square:
-        upper, lower = out_weight[:piece], out_weight[rows - piece :]
-        streams, upper, lower = lax.optimization_barrier((streams, upper, lower))
     (tails,) = call(tails_kernel, [((3, ROWS, channels), BF16)], "tails", streams)
     before = from_behind(tails, "ctx", 1)
     if square:
-        across_first, along_first = swap(upper, 2), swap(lower, 4)
+        near = swap(after(out_weight, tails), 2, 4)
     tiles = channels // TILE
     heads, query, gated, decay, step = call(
         prepare_kernel,
@@ -315,8 +306,6 @@
         scratch=[pltpu.VMEM((3 * tiles, 2 * ROWS, TILE), F32)],
     )
     all_ends = lax.all_to_all(ends, "ctx", split_axis=0, concat_axis=0, tiled=True)
-    if square:
-        gated, across_first, along_first = lax.optimization_barrier((gated, across_first, along_first))
     lift, base = call(
         inside_kernel,
         [((length, groups * poles), BF16), ((length, channels), F32)],
@@ -325,8 +314,8 @@
         flops=10**9,
     )
     if square:
-        across_rest = swap(after(after(out_weight, base)[piece:], all_ends), 2)
-        along_rest = swap(after(after(out_weight, base)[: rows - piece], all_ends), 4)
+        base, near = lax.optimization_barrier((base, near))
+        other_near = swap(after(out_weight, base), 4, 2)
     me = lax.axis_index("ctx").astype(jnp.int32)
     core = me % CORES
     smem = [pl.BlockSpec(memory_space=pltpu.SMEM)]
@@ -349,43 +338,24 @@
     up, down = around(block, 1), around(block, -1)
     second = around(after(up, down), 1)
     if square:
-        weight = (
-            (0, 0, out_weight),
-            (1, 0, across_first),
-            (1, piece, across_rest),
-            (2, 0, along_rest),
-            (2, rows - piece, along_first),
-            (3, 0, swap(after(across_first, (block, across_rest)), 4)),
-            (3, rows - piece, swap(after(along_first, (block, along_rest)), 2)),
-        )
-        last = (
-            (piece, swap(after(across_rest, block)[: half - piece], 4)),
-            (half, swap(after(along_rest, block)[half:], 2)),
-        )
+        diagonal = swap(after(near, block), 4, 2)
+        weight = (out_weight, near, other_near, diagonal)
     else:
         core_groups = [list(range(core, blocks, CORES)) for core in range(CORES)]
         weight = lax.all_gather(out_weight, "ctx", axis=0, axis_index_groups=core_groups)
-        weight = tuple((index, 0, part) for index, part in enumerate(weight.reshape(layers, share, features)))
-        last = ()
-    chip = me // CORES if square else jnp.zeros_like(me)
-    total, diagonal = call(
-        functools.partial(early_kernel, [part[:2] for part in weight]),
-        [((CORES * length, features), F32), (block.shape, BF16)],
-        "early",
-        jnp.stack([layer, chip]), block, up, second, down, *(part[2] for part in weight),
+        weight = tuple(weight.reshape(layers, share, features))
+    first_row = jnp.where(core == 0, 1, 2)
+    chip = me // CORES
+    place = [chip, chip ^ first_row, chip ^ (3 - first_row), chip ^ 3] if square else [jnp.full_like(me, at) for at in range(4)]
+    mine, other = call(
+        project_kernel,
+        [((length, features), F32), ((length, features), BF16)],
+        "project",
+        jnp.stack([layer] + place), block, up, second, down, *weight,
         specs=smem + whole(4 + len(weight)),
         scratch=[pltpu.VMEM((layers,) + block.shape, BF16)],
         flops=10**9,
     )
-    sides = []
-    for side, kind in ((1, BF16), (0, F32)):
-        sides += call(
-            functools.partial(late_kernel, side * length, [part[0] for part in last]),
-            [((length, features), kind)],
-            "late",
-            total, diagonal, *(part[1] for part in last),
-        )
-    other, mine = sides
     other = swap(other, 1)
     return (mine + other.astype(F32)).astype(BF16)
 

time: 71 us -> 60.1 us (0.85)
  starting transfers between devices: 25.8 us -> 18.5 us
  local copies, waits for them, and re-layouts: 10 us -> 5.35 us
  waiting for transfers between devices: 18.7 us -> 20.9 us
  Pallas kernels: 14.9 us -> 14.1 us
    ppermute x3, waiting for transfers between devices: 13.2 us -> 19 us  [around(): lax.ppermute(value, 'tp', [(source, (source + steps) % count) for source...]
    ppermute x10 -> x5, starting transfers between devices: 11.9 us -> 6.22 us  [swap(): return lax.ppermute(value, 'ctx', pairs)]
    ppermute x10 -> x5, waiting for transfers between devices: 5.45 us -> 1.53 us  [swap(): return lax.ppermute(value, 'ctx', pairs)]
    slice x4 -> x0, local copies, waits for them, and re-layouts: 3.41 us -> none  [the longest x1 2.13 us: local(): upper, lower = (out_weight[:piece], out_weight[rows - piece:])]
    all_to_all x1, starting transfers between devices: 7.53 us -> 5.55 us  [local(): lax.all_to_all(ends, 'ctx', split_axis=0, concat_axis=0, tiled=True)]
    unnamed x37 -> x21, local copies, waits for them, and re-layouts: 6.6 us -> 5.25 us
    pallas_call x8 -> x6, Pallas kernels: 14.9 us -> 14.1 us  [call(): pl.pallas_call(kernel, out_shape=tuple((jax.ShapeDtypeStruct(*out) for ou...]
  transfers between devices with their start and end apart: 15 -> 10, of which waited for: 6 -> 5; matrix products, arithmetic and copies ran while one was open for 2% -> 0% of each run, Pallas kernels for 21% -> 15%
where the time goes in v8:
time: 60.1 us; the launch traced here: 59.7 us
  waiting for transfers between devices  20.9 us (35%)
  starting transfers between devices  18.5 us (31%)
  Pallas kernels  14.1 us (23%)
  local copies, waits for them, and re-layouts  5.35 us (9%)
  other arithmetic  0.83 us (1%)
    ppermute x3, waiting for transfers between devices, around(): lax.ppermute(value, 'tp', [(source, (source + steps) % count) for source...  19 us
    pallas_call x6, Pallas kernels, call(): pl.pallas_call(kernel, out_shape=tuple((jax.ShapeDtypeStruct(*out) for ou...  14.1 us
    ppermute x5, starting transfers between devices, swap(): return lax.ppermute(value, 'ctx', pairs)  6.22 us
    all_to_all x1, starting transfers between devices, local(): lax.all_to_all(ends, 'ctx', split_axis=0, concat_axis=0, tiled=True)  5.55 us
    unnamed x21, local copies, waits for them, and re-layouts  5.25 us
    ppermute x3, starting transfers between devices, around(): lax.ppermute(value, 'tp', [(source, (source + steps) % count) for source...  5.23 us
    ppermute x5, waiting for transfers between devices, swap(): return lax.ppermute(value, 'ctx', pairs)  1.53 us
    ppermute x1, starting transfers between devices, from_behind(): lax.ppermute(value, axis, [(source, source + steps) for source in range(l...  1.48 us
  transfers between devices with their start and end apart: 10, of which 5 were waited for; matrix products, arithmetic and copies ran while one was open for 0% of the time, Pallas kernels for 15%

profile of v8, /device:TPU:0, one launch (start us, length us, event | category | flops | bytes accessed | tf_op | source)
XLA Modules:
  0.0 59.7 jit_solution(5768062855061986553)
XLA Ops:
  0.0 1.1 %copy-done.1 = bf16[3,1024,128]{2,1,0:T(8,128)(2,1)S(1)} copy-done((bf16[3,1024,128]{2,1,0:T(8,128)(2,1)S(1)}, bf16[3,1024,128]{2,1,0:T(8,128)(2,1)}, u32[]{:S(2)}) %copy-start.1) | copy-done | bytes 786456
  1.1 0.3 tails.1
  1.4 3.0 %collective-permute-start.1 = (bf16[512,1024]{1,0:T(8,128)(2,1)}, bf16[512,1024]{1,0:T(8,128)(2,1)S(1)}, u32[]{:S(2)}, u32[]{:S(2)}) collective-permute-start(bf16[512,1024]{1,0:T(8,128)(2,1)} %rest_0_.1), channel_id=1, source_target_pairs={{0,8},{4,20},{8,0},{12,28},{16,24},{20,4},{24,16},{28,12},{1,9},{5... | collective-permute-start | bytes 3145736 | tf_op jit(solution)/shard_map/ppermute | solution.py:261
  4.4 1.5 %collective-permute-start = (bf16[3,8,1024]{2,1,0:T(8,128)(2,1)S(1)}, bf16[3,8,1024]{2,1,0:T(8,128)(2,1)S(1)}, u32[]{:S(2)}, u32[]{:S(2)}) collective-permute-start(bf16[3,8,1024]{2,1,0:T(8,128)(2,1)S(1)} %tails.1), channel_id=1, source_target_pairs={{0,4},{4,8},{8,12},{12,16},{16,20},{20,24},{24,28},{1,5},{5,9},{9,... | collective-permute-start | bytes 147464 | tf_op jit(solution)/shard_map/ppermute | solution.py:25
  5.9 2.6 %prepare.1 = (f32[3,8,1024]{2,1,0:T(8,128)S(1)}, f32[128,1024]{1,0:T(8,128)S(1)}, f32[128,1024]{1,0:T(8,128)S(1)}, bf16[2,2048,128]{2,1,0:T(8,128)(2,1)S(1)}, f32[16,1024]{1,0:T(8,128)S(1)}) custom-call(bf16[3,1024,128]{2,1,0:T(8,128)(2,1)S(1)} %copy-done.1, f32[3,7,1024]{2,1,0:T(8,128)S(1)} %copy-done.6, f32[16,128]{1,0:T(8,128)S(1)} %bitcast.10), custom_call_target="tpu_custom_call" | custom-call | flops 1000000000 | bytes 10000000 | tf_op jit(solution)/shard_map/prepare/pallas_call | solution.py:54
  8.5 1.5 %states.1 = (bf16[8,16,1024]{2,1,0:T(8,128)(2,1)}, bf16[128,1024]{1,0:T(8,128)(2,1)S(1)}, f32[8,1024]{1,0:T(8,128)S(1)}) custom-call(bf16[3,8,1024]{2,1,0:T(8,128)(2,1)S(1)} %collective-permute-done.before_ref, f32[3,8,1024]{2,1,0:T(8,128)S(1)} %get-tuple-element.25.heads_ref, f32[3,7,1024]{2,1,0:T(8,128)S(1)} %copy-done.6, ...), custom_call_target="tpu_custom_call" | custom-call | flops 100000000 | bytes 1000000 | tf_op jit(solution)/shard_map/states/pallas_call | solution.py:54
  10.0 5.5 %all-to-all-start = ((bf16[8,16,1024]{2,1,0:T(8,128)(2,1)}), bf16[8,16,1024]{2,1,0:T(8,128)(2,1)S(1)}, u32[]{:S(2)}, u32[]{:S(2)}) async-start(bf16[8,16,1024]{2,1,0:T(8,128)(2,1)} %get-tuple-element.28), calls=%async_computation | async-start | bytes 524288 | tf_op jit(solution)/shard_map/all_to_all | solution.py:308
  15.6 0.0 copy-start.9
  15.6 0.1 pad_add_fusion.at_ref
  15.7 0.6 %copy-done.8 = f32[128,16]{0,1:T(8,128)S(1)} copy-done((f32[128,16]{0,1:T(8,128)S(1)}, f32[128,16]{0,1:T(8,128)}, u32[]{:S(2)}) %copy-start.8) | copy-done | bytes 8216
  16.3 0.0 copy-done.9
  16.3 5.0 %inside.1 = (bf16[128,2048]{1,0:T(8,128)(2,1)S(1)}, f32[128,1024]{1,0:T(8,128)S(1)}) custom-call(bf16[128,1024]{1,0:T(8,128)(2,1)S(1)} %get-tuple-element.30.gated_ref, f32[1,1024]{1,0:T(1,128)S(1)} %bitcast.13, f32[16,128]{1,0:T(8,128)S(1)} %bitcast.11, f32[16,128]{1,0:T(8,128)S(1)} %bitcast.12), custom_call_target="tpu_custom_call" | custom-call | flops 1000000000 | bytes 10000000 | tf_op jit(solution)/shard_map/inside/pallas_call | solution.py:54
  21.3 0.8 %copy-done.2 = f32[128,1024]{1,0:T(8,128)} copy-done((f32[128,1024]{1,0:T(8,128)}, f32[128,1024]{1,0:T(8,128)S(1)}, u32[]{:S(2)}) %copy-start.2) | copy-done | bytes 524312
  22.1 0.4 all-to-all-done.ends_ref
  22.5 1.0 %copy-done.3 = f32[128,1024]{1,0:T(8,128)S(1)} copy-done((f32[128,1024]{1,0:T(8,128)S(1)}, f32[128,1024]{1,0:T(8,128)}, u32[]{:S(2)}) %copy-start.3) | copy-done | bytes 524312
  23.6 1.9 %finish.1 = (bf16[128,512]{1,0:T(8,128)(2,1)S(1)}, bf16[128,512]{1,0:T(8,128)(2,1)S(1)}, bf16[128,1024]{1,0:T(8,128)(2,1)}) custom-call(s32[2]{0:T(128)S(1)} %pad_add_fusion.at_ref, bf16[8,16,1024]{2,1,0:T(8,128)(2,1)S(1)} %all-to-all-done.ends_ref, f32[16,1024]{1,0:T(8,128)S(1)} %get-tuple-element.29.step_ref, ...), custom_call_target="tpu_custom_call" | custom-call | flops 100000000 | bytes 1000000 | tf_op jit(solution)/shard_map/finish/pallas_call | solution.py:54
  25.5 0.2 collective-permute-start.2
  25.7 1.7 %collective-permute-start.6 = (bf16[512,1024]{1,0:T(8,128)(2,1)S(1)}, bf16[512,1024]{1,0:T(8,128)(2,1)S(1)}, u32[]{:S(2)}, u32[]{:S(2)}) collective-permute-start(bf16[512,1024]{1,0:T(8,128)(2,1)S(1)} %copy-done), channel_id=1, source_target_pairs={{0,16},{4,12},{8,24},{12,4},{16,0},{20,28},{24,8},{28,20},{1,17},{... | collective-permute-start | bytes 3145736 | tf_op jit(solution)/shard_map/ppermute | solution.py:261
  27.4 0.0 collective-permute-done.2
  27.4 1.3 %collective-permute-start.7 = (bf16[512,1024]{1,0:T(8,128)(2,1)S(1)}, bf16[512,1024]{1,0:T(8,128)(2,1)}, u32[]{:S(2)}, u32[]{:S(2)}) collective-permute-start(bf16[512,1024]{1,0:T(8,128)(2,1)S(1)} %collective-permute-done.1.rest_1_), channel_id=1, source_target_pairs={{0,16},{4,12},{8,24},{12,4},{16,0},{20,28},{24,8},{28,20},{1,17},{... | collective-permute-start | bytes 3145736 | tf_op jit(solution)/shard_map/ppermute | solution.py:261
  28.7 3.6 %collective-permute-start.4 = (bf16[256,512]{1,0:T(8,128)(2,1)S(1)}, bf16[256,512]{1,0:T(8,128)(2,1)S(1)}, u32[]{:S(2)}, u32[]{:S(2)}) collective-permute-start(bf16[256,512]{1,0:T(8,128)(2,1)S(1)} %constant_dynamic-update-slice_fusion.own_ref), channel_id=1, source_target_pairs={{0,3},{1,0},{2,1},{3,2},{4,7},{5,4},{6,5},{7,6},{8,11},{9,8},{10,9... | collective-permute-start | bytes 786440 | tf_op jit(solution)/shard_map/ppermute | solution.py:270
  32.3 6.7 %collective-permute-done.4.down_ref = bf16[256,512]{1,0:T(8,128)(2,1)S(1)} collective-permute-done((bf16[256,512]{1,0:T(8,128)(2,1)S(1)}, bf16[256,512]{1,0:T(8,128)(2,1)S(1)}, u32[]{:S(2)}, u32[]{:S(2)}) %collective-permute-start.4) | collective-permute-done | bytes 262176 | tf_op jit(solution)/shard_map/ppermute | solution.py:270
  39.1 0.7 %copy-done.4 = bf16[256,512]{1,0:T(8,128)(2,1)} copy-done((bf16[256,512]{1,0:T(8,128)(2,1)}, bf16[256,512]{1,0:T(8,128)(2,1)S(1)}, u32[]{:S(2)}) %copy-start.4) | copy-done | bytes 262168
  39.8 4.7 %collective-permute-done.3.up_ref = bf16[256,512]{1,0:T(8,128)(2,1)} collective-permute-done((bf16[256,512]{1,0:T(8,128)(2,1)S(1)}, bf16[256,512]{1,0:T(8,128)(2,1)}, u32[]{:S(2)}, u32[]{:S(2)}) %collective-permute-start.3) | collective-permute-done | bytes 262176 | tf_op jit(solution)/shard_map/ppermute | solution.py:270
  44.5 1.6 %collective-permute-start.5 = (bf16[256,512]{1,0:T(8,128)(2,1)}, bf16[256,512]{1,0:T(8,128)(2,1)}, u32[]{:S(2)}, u32[]{:S(2)}) collective-permute-start(bf16[256,512]{1,0:T(8,128)(2,1)} %collective-permute-done.3.up_ref), channel_id=1, source_target_pairs={{0,1},{1,2},{2,3},{3,0},{4,5},{5,6},{6,7},{7,4},{8,9},{9,10},{10,1... | collective-permute-start | bytes 786440 | tf_op jit(solution)/shard_map/ppermute | solution.py:270
  46.1 0.1 stack.32.at_ref
  46.2 7.5 %collective-permute-done.5.second_ref = bf16[256,512]{1,0:T(8,128)(2,1)} collective-permute-done((bf16[256,512]{1,0:T(8,128)(2,1)}, bf16[256,512]{1,0:T(8,128)(2,1)}, u32[]{:S(2)}, u32[]{:S(2)}) %collective-permute-start.5) | collective-permute-done | bytes 262176 | tf_op jit(solution)/shard_map/ppermute | solution.py:270
  53.7 0.9 %copy-done.5 = bf16[256,512]{1,0:T(8,128)(2,1)S(1)} copy-done((bf16[256,512]{1,0:T(8,128)(2,1)S(1)}, bf16[256,512]{1,0:T(8,128)(2,1)}, u32[]{:S(2)}) %copy-start.5) | copy-done | bytes 262168
  54.7 2.7 %project.1 = (f32[128,1024]{1,0:T(8,128)S(1)}, bf16[128,1024]{1,0:T(8,128)(2,1)S(1)}) custom-call(s32[5]{0:T(128)S(1)} %stack.32.at_ref, bf16[256,512]{1,0:T(8,128)(2,1)S(1)} %constant_dynamic-update-slice_fusion.own_ref, bf16[256,512]{1,0:T(8,128)(2,1)} %collective-permute-done.3.up_ref, bf16[256,512]{1,0:T(8,128)(2,1)} %collective-permute-done.5.second_ref, ...), custom_call_target="tpu_custom_call" | custom-call | flops 1000000000 | bytes 10000000 | tf_op jit(solution)/shard_map/project/pallas_call | solution.py:54
  57.4 0.1 collective-permute-start.8
  57.5 1.5 %collective-permute-done.8 = bf16[128,1024]{1,0:T(8,128)(2,1)S(1)} collective-permute-done((bf16[128,1024]{1,0:T(8,128)(2,1)S(1)}, bf16[128,1024]{1,0:T(8,128)(2,1)S(1)}, u32[]{:S(2)}, u32[]{:S(2)}) %collective-permute-start.8) | collective-permute-done | bytes 262176 | tf_op jit(solution)/shard_map/ppermute | solution.py:261
  59.0 0.8 %add_convert_fusion = bf16[128,1024]{1,0:T(8,128)(2,1)} fusion(f32[128,1024]{1,0:T(8,128)S(1)} %get-tuple-element.43, bf16[128,1024]{1,0:T(8,128)(2,1)S(1)} %collective-permute-done.8), kind=kLoop, calls=%fused_computation | loop fusion | flops 393216 | bytes 1048576 | tf_op jit(solution)/shard_map/convert_element_type | solution.py:360
  (19 shorter events, 0.1 us)
Async XLA Ops:
  0.0 1.1 %copy-start.1 = (bf16[3,1024,128]{2,1,0:T(8,128)(2,1)S(1)}, bf16[3,1024,128]{2,1,0:T(8,128)(2,1)}, u32[]{:S(2)}) copy-start(bf16[3,1024,128]{2,1,0:T(8,128)(2,1)} %streams_ref.3) | copy-start | bytes 2359300
  1.1 4.8 %copy-start.6 = (f32[3,7,1024]{2,1,0:T(8,128)S(1)}, f32[3,7,1024]{2,1,0:T(8,128)}, u32[]{:S(2)}) copy-start(f32[3,7,1024]{2,1,0:T(8,128)} %taps_ref.3) | copy-start | bytes 258052
  1.1 4.8 %copy-start.7 = (f32[128,16]{0,1:T(8,128)S(1)}, f32[128,16]{0,1:T(8,128)}, u32[]{:S(2)}) copy-start(f32[128,16]{0,1:T(8,128)} %param.8) | copy-start | bytes 24580
  1.4 20.7 %collective-permute-start.1 = (bf16[512,1024]{1,0:T(8,128)(2,1)}, bf16[512,1024]{1,0:T(8,128)(2,1)S(1)}, u32[]{:S(2)}, u32[]{:S(2)}) collective-permute-start(bf16[512,1024]{1,0:T(8,128)(2,1)} %rest_0_.1), channel_id=1, source_target_pairs={{0,8},{4,20},{8,0},{12,28},{16,24},{20,4},{24,16},{28,12},{1,9},{5... | collective-permute-start | bytes 3145736 | tf_op jit(solution)/shard_map/ppermute | solution.py:261
  4.4 4.1 %collective-permute-start = (bf16[3,8,1024]{2,1,0:T(8,128)(2,1)S(1)}, bf16[3,8,1024]{2,1,0:T(8,128)(2,1)S(1)}, u32[]{:S(2)}, u32[]{:S(2)}) collective-permute-start(bf16[3,8,1024]{2,1,0:T(8,128)(2,1)S(1)} %tails.1), channel_id=1, source_target_pairs={{0,4},{4,8},{8,12},{12,16},{16,20},{20,24},{24,28},{1,5},{5,9},{9,... | collective-permute-start | bytes 147464 | tf_op jit(solution)/shard_map/ppermute | solution.py:25
  10.0 12.5 %all-to-all-start = ((bf16[8,16,1024]{2,1,0:T(8,128)(2,1)}), bf16[8,16,1024]{2,1,0:T(8,128)(2,1)S(1)}, u32[]{:S(2)}, u32[]{:S(2)}) async-start(bf16[8,16,1024]{2,1,0:T(8,128)(2,1)} %get-tuple-element.28), calls=%async_computation | async-start | bytes 524288 | tf_op jit(solution)/shard_map/all_to_all | solution.py:308
  15.6 0.7 %copy-start.8 = (f32[128,16]{0,1:T(8,128)S(1)}, f32[128,16]{0,1:T(8,128)}, u32[]{:S(2)}) copy-start(f32[128,16]{0,1:T(8,128)} %param.9) | copy-start | bytes 24580
  15.6 0.7 %copy-start.9 = (f32[1024]{0:T(1024)S(1)}, f32[1024]{0:T(1024)}, u32[]{:S(2)}) copy-start(f32[1024]{0:T(1024)} %param.10) | copy-start | bytes 12292
  21.3 0.8 %copy-start.2 = (f32[128,1024]{1,0:T(8,128)}, f32[128,1024]{1,0:T(8,128)S(1)}, u32[]{:S(2)}) copy-start(f32[128,1024]{1,0:T(8,128)S(1)} %get-tuple-element.36.base_ref) | copy-start | bytes 1572868
  22.1 3.6 %copy-start = (bf16[512,1024]{1,0:T(8,128)(2,1)S(1)}, bf16[512,1024]{1,0:T(8,128)(2,1)}, u32[]{:S(2)}) copy-start(bf16[512,1024]{1,0:T(8,128)(2,1)} %rest_0_.1) | copy-start | bytes 3145732
  22.5 1.0 %copy-start.3 = (f32[128,1024]{1,0:T(8,128)S(1)}, f32[128,1024]{1,0:T(8,128)}, u32[]{:S(2)}) copy-start(f32[128,1024]{1,0:T(8,128)} %copy-done.2) | copy-start | bytes 1572868
  25.5 1.9 %collective-permute-start.2 = (bf16[128,512]{1,0:T(8,128)(2,1)S(1)}, bf16[128,512]{1,0:T(8,128)(2,1)S(1)}, u32[]{:S(2)}, u32[]{:S(2)}) collective-permute-start(bf16[128,512]{1,0:T(8,128)(2,1)S(1)} %get-tuple-element.38), channel_id=1, source_target_pairs={{0,4},{4,0},{8,12},{12,8},{16,20},{20,16},{24,28},{28,24},{1,5},{5... | collective-permute-start | bytes 393224 | tf_op jit(solution)/shard_map/ppermute | solution.py:261
  25.7 28.0 %collective-permute-start.6 = (bf16[512,1024]{1,0:T(8,128)(2,1)S(1)}, bf16[512,1024]{1,0:T(8,128)(2,1)S(1)}, u32[]{:S(2)}, u32[]{:S(2)}) collective-permute-start(bf16[512,1024]{1,0:T(8,128)(2,1)S(1)} %copy-done), channel_id=1, source_target_pairs={{0,16},{4,12},{8,24},{12,4},{16,0},{20,28},{24,8},{28,20},{1,17},{... | collective-permute-start | bytes 3145736 | tf_op jit(solution)/shard_map/ppermute | solution.py:261
  27.4 26.3 %collective-permute-start.7 = (bf16[512,1024]{1,0:T(8,128)(2,1)S(1)}, bf16[512,1024]{1,0:T(8,128)(2,1)}, u32[]{:S(2)}, u32[]{:S(2)}) collective-permute-start(bf16[512,1024]{1,0:T(8,128)(2,1)S(1)} %collective-permute-done.1.rest_1_), channel_id=1, source_target_pairs={{0,16},{4,12},{8,24},{12,4},{16,0},{20,28},{24,8},{28,20},{1,17},{... | collective-permute-start | bytes 3145736 | tf_op jit(solution)/shard_map/ppermute | solution.py:261
  28.7 10.3 %collective-permute-start.4 = (bf16[256,512]{1,0:T(8,128)(2,1)S(1)}, bf16[256,512]{1,0:T(8,128)(2,1)S(1)}, u32[]{:S(2)}, u32[]{:S(2)}) collective-permute-start(bf16[256,512]{1,0:T(8,128)(2,1)S(1)} %constant_dynamic-update-slice_fusion.own_ref), channel_id=1, source_target_pairs={{0,3},{1,0},{2,1},{3,2},{4,7},{5,4},{6,5},{7,6},{8,11},{9,8},{10,9... | collective-permute-start | bytes 786440 | tf_op jit(solution)/shard_map/ppermute | solution.py:270
  32.3 12.1 %collective-permute-start.3 = (bf16[256,512]{1,0:T(8,128)(2,1)S(1)}, bf16[256,512]{1,0:T(8,128)(2,1)}, u32[]{:S(2)}, u32[]{:S(2)}) collective-permute-start(bf16[256,512]{1,0:T(8,128)(2,1)S(1)} %constant_dynamic-update-slice_fusion.own_ref), channel_id=1, source_target_pairs={{0,1},{1,2},{2,3},{3,0},{4,5},{5,6},{6,7},{7,4},{8,9},{9,10},{10,1... | collective-permute-start | bytes 786440 | tf_op jit(solution)/shard_map/ppermute | solution.py:270
  39.1 0.7 %copy-start.4 = (bf16[256,512]{1,0:T(8,128)(2,1)}, bf16[256,512]{1,0:T(8,128)(2,1)S(1)}, u32[]{:S(2)}) copy-start(bf16[256,512]{1,0:T(8,128)(2,1)S(1)} %collective-permute-done.4.down_ref) | copy-start | bytes 786436
  44.5 9.2 %collective-permute-start.5 = (bf16[256,512]{1,0:T(8,128)(2,1)}, bf16[256,512]{1,0:T(8,128)(2,1)}, u32[]{:S(2)}, u32[]{:S(2)}) collective-permute-start(bf16[256,512]{1,0:T(8,128)(2,1)} %collective-permute-done.3.up_ref), channel_id=1, source_target_pairs={{0,1},{1,2},{2,3},{3,0},{4,5},{5,6},{6,7},{7,4},{8,9},{9,10},{10,1... | collective-permute-start | bytes 786440 | tf_op jit(solution)/shard_map/ppermute | solution.py:270
  53.7 1.0 %copy-start.5 = (bf16[256,512]{1,0:T(8,128)(2,1)S(1)}, bf16[256,512]{1,0:T(8,128)(2,1)}, u32[]{:S(2)}) copy-start(bf16[256,512]{1,0:T(8,128)(2,1)} %copy-done.4) | copy-start | bytes 786436
  57.4 1.6 %collective-permute-start.8 = (bf16[128,1024]{1,0:T(8,128)(2,1)S(1)}, bf16[128,1024]{1,0:T(8,128)(2,1)S(1)}, u32[]{:S(2)}, u32[]{:S(2)}) collective-permute-start(bf16[128,1024]{1,0:T(8,128)(2,1)S(1)} %get-tuple-element.44), channel_id=1, source_target_pairs={{0,4},{4,0},{8,12},{12,8},{16,20},{20,16},{24,28},{28,24},{1,5},{5... | collective-permute-start | bytes 786440 | tf_op jit(solution)/shard_map/ppermute | solution.py:261

commit v9 on v8

--- a/solution.py
+++ b/solution.py
@@ -58,7 +58,7 @@
         out_specs=tuple(whole(len(outs))),
         scratch_shapes=scratch,
         compiler_params=pltpu.CompilerParams(vmem_limit_bytes=VMEM_LIMIT),
-        cost_estimate=pl.CostEstimate(flops=flops, bytes_accessed=flops // 100, transcendentals=0),
+        cost_estimate=pl.CostEstimate(flops=flops, bytes_accessed=flops // 1000, transcendentals=0),
         name=name,
     )(*operands)
 
@@ -125,7 +125,7 @@
         query, left, right = (
             short_conv(stream, chans, length, padded_ref.at[index * 3 + stream], taps_ref) for stream in range(3)
         )
-        query_ref[:, chans] = query
+        query_ref[:, chans] = query.astype(BF16)
         gated_ref[:, chans] = left * right
 
     unrolled(channels // TILE, turn)
@@ -228,7 +228,7 @@
         states = tile_of(index, in_tile * poles)
         lift = lift_ref[:, states]
         carried = dot(lift, high) + dot(lift, low)
-        query = jnp.concatenate([first_ref[:, chans], query_ref[ROWS:, chans]], axis=0)
+        query = jnp.concatenate([first_ref[:, chans], query_ref[:, chans].astype(F32)[ROWS:]], axis=0)
         mixed_ref[:, chans] = (query * (base_ref[:, chans] + carried)).astype(BF16)
 
     unrolled(channels // TILE, tile)
@@ -237,22 +237,31 @@
     other_ref[...] = mixed_ref[:, tile_of(1 - core, share)]
 
 
-def project_kernel(at_ref, own_ref, up_ref, second_ref, down_ref, *rest):
-    *weight_refs, mine_ref, other_ref, layers_ref = rest
+def early_kernel(at_ref, own_ref, up_ref, down_ref, *rest):
+    *weight_refs, total_ref, layers_ref = rest
     layer = at_ref[0]
     layers_ref[layer] = own_ref[...]
     layers_ref[lax.rem(layer + 3, 4)] = up_ref[...]
-    layers_ref[lax.rem(layer + 2, 4)] = second_ref[...]
+    layers_ref[lax.rem(layer + 2, 4)] = jnp.zeros_like(own_ref)
     layers_ref[lax.rem(layer + 1, 4)] = down_ref[...]
-    length, features = mine_ref.shape
-    for column in range(0, features, COLUMNS):
+    for column in range(0, total_ref.shape[1], COLUMNS):
         columns = slice(column, column + COLUMNS)
         total = None
         for at, ref in enumerate(weight_refs):
             term = dot(layers_ref[at_ref[1 + at]], ref[:, columns])
             total = term if total is None else total + term
-        mine_ref[:, columns] = total[:length]
-        other_ref[:, columns] = total[length:].astype(BF16)
+        total_ref[:, columns] = total
+
+
+def late_kernel(first, at_ref, second_ref, total_ref, *rest):
+    *weight_refs, out_ref = rest
+    tokens = pl.ds(first, out_ref.shape[0])
+    last = lax.rem(at_ref[0] + 2, 4)
+    for at, ref in enumerate(weight_refs):
+
+        @pl.when(at_ref[1 + at] == last)
+        def _():
+            out_ref[...] = (total_ref[tokens, :] + dot(second_ref[tokens, :], ref[...])).astype(out_ref.dtype)
 
 
 def swap(value, *bits):
@@ -288,7 +297,7 @@
         prepare_kernel,
         [
             ((3, ROWS, channels), F32),
-            ((length, channels), F32),
+            ((length, channels), BF16),
             ((length, channels), F32),
             ((2, groups * poles, length), BF16),
             ((poles, channels), F32),
@@ -338,7 +347,7 @@
     up, down = around(block, 1), around(block, -1)
     second = around(after(up, down), 1)
     if square:
-        diagonal = swap(after(near, block), 4, 2)
+        diagonal = swap(after(near, (down, other_near)), 4, 2)
         weight = (out_weight, near, other_near, diagonal)
     else:
         core_groups = [list(range(core, blocks, CORES)) for core in range(CORES)]
@@ -347,15 +356,26 @@
     first_row = jnp.where(core == 0, 1, 2)
     chip = me // CORES
     place = [chip, chip ^ first_row, chip ^ (3 - first_row), chip ^ 3] if square else [jnp.full_like(me, at) for at in range(4)]
-    mine, other = call(
-        project_kernel,
-        [((length, features), F32), ((length, features), BF16)],
-        "project",
-        jnp.stack([layer] + place), block, up, second, down, *weight,
-        specs=smem + whole(4 + len(weight)),
+    at = jnp.stack([layer] + place)
+    (total,) = call(
+        early_kernel,
+        [((CORES * length, features), F32)],
+        "early",
+        at, block, up, down, *weight,
+        specs=smem + whole(3 + len(weight)),
         scratch=[pltpu.VMEM((layers,) + block.shape, BF16)],
-        flops=10**9,
-    )
+        flops=1,
+    )
+    sides = []
+    for side, kind in ((1, BF16), (0, F32)):
+        sides += call(
+            functools.partial(late_kernel, side * length),
+            [((length, features), kind)],
+            "late",
+            at, second, total, *weight,
+            specs=smem + whole(2 + len(weight)),
+        )
+    other, mine = sides
     other = swap(other, 1)
     return (mine + other.astype(F32)).astype(BF16)
 

time: 60.1 us -> 78.4 us (1.30)
  waiting for transfers between devices: 20.9 us -> 30.9 us
  local copies, waits for them, and re-layouts: 5.35 us -> 11.3 us
  Pallas kernels: 14.1 us -> 16.5 us
  starting transfers between devices: 18.5 us -> 17.6 us
    all_to_all x1, waiting for transfers between devices: 0.4 us -> 12.1 us  [local(): lax.all_to_all(ends, 'ctx', split_axis=0, concat_axis=0, tiled=True)]
    unnamed x21 -> x35, local copies, waits for them, and re-layouts: 5.25 us -> 11.2 us
    ppermute x3, waiting for transfers between devices: 19 us -> 13.6 us  [around(): lax.ppermute(value, 'tp', [(source, (source + steps) % count) for source...]
    ppermute x5, waiting for transfers between devices: 1.53 us -> 5.27 us  [swap(): return lax.ppermute(value, 'ctx', pairs)]
    ppermute x5, starting transfers between devices: 6.22 us -> 8.62 us  [swap(): return lax.ppermute(value, 'ctx', pairs)]
    pallas_call x6 -> x8, Pallas kernels: 14.1 us -> 16.5 us  [call(): pl.pallas_call(kernel, out_shape=tuple((jax.ShapeDtypeStruct(*out) for ou...]
    all_to_all x1, starting transfers between devices: 5.55 us -> 3.41 us  [local(): lax.all_to_all(ends, 'ctx', split_axis=0, concat_axis=0, tiled=True)]
    ppermute x3, starting transfers between devices: 5.23 us -> 4.13 us  [around(): lax.ppermute(value, 'tp', [(source, (source + steps) % count) for source...]
  transfers between devices with their start and end apart: 10 -> 10, of which waited for: 5 -> 5; matrix products, arithmetic and copies ran while one was open for 0% -> 0% of each run, Pallas kernels for 15% -> 19%
where the time goes in v9:
time: 78.4 us; the launch traced here: 77.3 us
  waiting for transfers between devices  30.9 us (39%)
  starting transfers between devices  17.6 us (22%)
  Pallas kernels  16.5 us (21%)
  local copies, waits for them, and re-layouts  11.3 us (14%)
  other arithmetic  0.84 us (1%)
    pallas_call x8, Pallas kernels, call(): pl.pallas_call(kernel, out_shape=tuple((jax.ShapeDtypeStruct(*out) for ou...  16.5 us
    ppermute x3, waiting for transfers between devices, around(): lax.ppermute(value, 'tp', [(source, (source + steps) % count) for source...  13.6 us
    all_to_all x1, waiting for transfers between devices, local(): lax.all_to_all(ends, 'ctx', split_axis=0, concat_axis=0, tiled=True)  12.1 us
    unnamed x35, local copies, waits for them, and re-layouts  11.2 us
    ppermute x5, starting transfers between devices, swap(): return lax.ppermute(value, 'ctx', pairs)  8.62 us
    ppermute x5, waiting for transfers between devices, swap(): return lax.ppermute(value, 'ctx', pairs)  5.27 us
    ppermute x3, starting transfers between devices, around(): lax.ppermute(value, 'tp', [(source, (source + steps) % count) for source...  4.13 us
    all_to_all x1, starting transfers between devices, local(): lax.all_to_all(ends, 'ctx', split_axis=0, concat_axis=0, tiled=True)  3.41 us
  transfers between devices with their start and end apart: 10, of which 5 were waited for; matrix products, arithmetic and copies ran while one was open for 0% of the time, Pallas kernels for 19%

profile of v9, /device:TPU:0, one launch (start us, length us, event | category | flops | bytes accessed | tf_op | source)
XLA Modules:
  0.0 77.3 jit_solution(11913086170091120874)
XLA Ops:
  0.0 1.1 %copy-done.1 = bf16[3,1024,128]{2,1,0:T(8,128)(2,1)S(1)} copy-done((bf16[3,1024,128]{2,1,0:T(8,128)(2,1)S(1)}, bf16[3,1024,128]{2,1,0:T(8,128)(2,1)}, u32[]{:S(2)}) %copy-start.1) | copy-done | bytes 786456
  1.4 3.0 %collective-permute-start.1 = (bf16[512,1024]{1,0:T(8,128)(2,1)}, bf16[512,1024]{1,0:T(8,128)(2,1)S(1)}, u32[]{:S(2)}, u32[]{:S(2)}) collective-permute-start(bf16[512,1024]{1,0:T(8,128)(2,1)} %rest_0_.5), channel_id=1, source_target_pairs={{0,8},{4,20},{8,0},{12,28},{16,24},{20,4},{24,16},{28,12},{1,9},{5... | collective-permute-start | bytes 3145736 | tf_op jit(solution)/shard_map/ppermute | solution.py:270
  4.4 1.5 %collective-permute-start = (bf16[3,8,1024]{2,1,0:T(8,128)(2,1)S(1)}, bf16[3,8,1024]{2,1,0:T(8,128)(2,1)S(1)}, u32[]{:S(2)}, u32[]{:S(2)}) collective-permute-start(bf16[3,8,1024]{2,1,0:T(8,128)(2,1)S(1)} %tails.1), channel_id=1, source_target_pairs={{0,4},{4,8},{8,12},{12,16},{16,20},{20,24},{24,28},{1,5},{5,9},{9,... | collective-permute-start | bytes 147464 | tf_op jit(solution)/shard_map/ppermute | solution.py:25
  5.9 2.6 %prepare.1 = (f32[3,8,1024]{2,1,0:T(8,128)S(1)}, bf16[128,1024]{1,0:T(8,128)(2,1)S(1)}, f32[128,1024]{1,0:T(8,128)S(1)}, bf16[2,2048,128]{2,1,0:T(8,128)(2,1)S(1)}, f32[16,1024]{1,0:T(8,128)S(1)}) custom-call(bf16[3,1024,128]{2,1,0:T(8,128)(2,1)S(1)} %copy-done.1, f32[3,7,1024]{2,1,0:T(8,128)S(1)} %copy-done.13, f32[16,128]{1,0:T(8,128)S(1)} %bitcast.10), custom_call_target="tpu_custom_call" | custom-call | flops 1000000000 | bytes 1000000 | tf_op jit(solution)/shard_map/prepare/pallas_call | solution.py:54
  8.5 0.7 copy-done.11
  9.2 0.8 %states.1 = (bf16[8,16,1024]{2,1,0:T(8,128)(2,1)S(1)}, bf16[128,1024]{1,0:T(8,128)(2,1)S(1)}, f32[8,1024]{1,0:T(8,128)S(1)}) custom-call(bf16[3,8,1024]{2,1,0:T(8,128)(2,1)S(1)} %collective-permute-done.before_ref, f32[3,8,1024]{2,1,0:T(8,128)S(1)} %get-tuple-element.23.heads_ref, f32[3,7,1024]{2,1,0:T(8,128)S(1)} %copy-done.13, ...), custom_call_target="tpu_custom_call" | custom-call | flops 100000000 | bytes 100000 | tf_op jit(solution)/shard_map/states/pallas_call | solution.py:54
  10.1 0.7 copy-done.10
  10.8 0.7 copy-done.16
  11.4 5.0 %inside.1 = (bf16[128,2048]{1,0:T(8,128)(2,1)S(1)}, f32[128,1024]{1,0:T(8,128)S(1)}) custom-call(bf16[128,1024]{1,0:T(8,128)(2,1)S(1)} %get-tuple-element.28.gated_ref, f32[1,1024]{1,0:T(1,128)S(1)} %bitcast.13, f32[16,128]{1,0:T(8,128)S(1)} %bitcast.11, f32[16,128]{1,0:T(8,128)S(1)} %bitcast.12), custom_call_target="tpu_custom_call" | custom-call | flops 1000000000 | bytes 1000000 | tf_op jit(solution)/shard_map/inside/pallas_call | solution.py:54
  16.5 0.8 %copy-done.4 = bf16[128,2048]{1,0:T(8,128)(2,1)} copy-done((bf16[128,2048]{1,0:T(8,128)(2,1)}, bf16[128,2048]{1,0:T(8,128)(2,1)S(1)}, u32[]{:S(2)}) %copy-start.4) | copy-done | bytes 524312
  17.3 0.8 %copy-done.6 = f32[128,1024]{1,0:T(8,128)} copy-done((f32[128,1024]{1,0:T(8,128)}, f32[128,1024]{1,0:T(8,128)S(1)}, u32[]{:S(2)}) %copy-start.6) | copy-done | bytes 524312
  18.1 3.6 %collective-permute-start.6 = (bf16[512,1024]{1,0:T(8,128)(2,1)S(1)}, bf16[512,1024]{1,0:T(8,128)(2,1)S(1)}, u32[]{:S(2)}, u32[]{:S(2)}) collective-permute-start(bf16[512,1024]{1,0:T(8,128)(2,1)S(1)} %copy-done), channel_id=1, source_target_pairs={{0,16},{4,12},{8,24},{12,4},{16,0},{20,28},{24,8},{28,20},{1,17},{... | collective-permute-start | bytes 3145736 | tf_op jit(solution)/shard_map/ppermute | solution.py:270
  21.7 3.4 %all-to-all-start = ((bf16[8,16,1024]{2,1,0:T(8,128)(2,1)}), bf16[8,16,1024]{2,1,0:T(8,128)(2,1)S(1)}, u32[]{:S(2)}, u32[]{:S(2)}) async-start(bf16[8,16,1024]{2,1,0:T(8,128)(2,1)} %copy-done.10), calls=%async_computation | async-start | bytes 524288 | tf_op jit(solution)/shard_map/all_to_all | solution.py:317
  25.2 12.1 %all-to-all-done.ends_ref = bf16[8,16,1024]{2,1,0:T(8,128)(2,1)S(1)} async-done(((bf16[8,16,1024]{2,1,0:T(8,128)(2,1)}), bf16[8,16,1024]{2,1,0:T(8,128)(2,1)S(1)}, u32[]{:S(2)}, u32[]{:S(2)}) %all-to-all-start) | async-done | bytes 262176 | tf_op jit(solution)/shard_map/all_to_all | solution.py:317
  37.3 1.0 %copy-done.5 = bf16[128,2048]{1,0:T(8,128)(2,1)S(1)} copy-done((bf16[128,2048]{1,0:T(8,128)(2,1)S(1)}, bf16[128,2048]{1,0:T(8,128)(2,1)}, u32[]{:S(2)}) %copy-start.5) | copy-done | bytes 524312
  38.3 1.0 %copy-done.7 = f32[128,1024]{1,0:T(8,128)S(1)} copy-done((f32[128,1024]{1,0:T(8,128)S(1)}, f32[128,1024]{1,0:T(8,128)}, u32[]{:S(2)}) %copy-start.7) | copy-done | bytes 524312
  39.3 0.9 %copy-done.12 = bf16[128,1024]{1,0:T(8,128)(2,1)S(1)} copy-done((bf16[128,1024]{1,0:T(8,128)(2,1)S(1)}, bf16[128,1024]{1,0:T(8,128)(2,1)}, u32[]{:S(2)}) %copy-start.12) | copy-done | bytes 262168
  40.3 1.9 %finish.1 = (bf16[128,512]{1,0:T(8,128)(2,1)S(1)}, bf16[128,512]{1,0:T(8,128)(2,1)S(1)}, bf16[128,1024]{1,0:T(8,128)(2,1)}) custom-call(s32[2]{0:T(128)S(1)} %pad_add_fusion.at_ref, bf16[8,16,1024]{2,1,0:T(8,128)(2,1)S(1)} %all-to-all-done.ends_ref, f32[16,1024]{1,0:T(8,128)S(1)} %get-tuple-element.27.step_ref, bf16[128,2048]{1,0:T(8,128)(2,1)S(1)} %copy-done.5, ...), custom_call_target="tpu_custom_call" | custom-call | flops 100000000 | bytes 100000 | tf_op jit(solution)/shard_map/finish/pallas_call | solution.py:54
  42.2 1.3 %collective-permute-done.2 = bf16[128,512]{1,0:T(8,128)(2,1)S(1)} collective-permute-done((bf16[128,512]{1,0:T(8,128)(2,1)S(1)}, bf16[128,512]{1,0:T(8,128)(2,1)S(1)}, u32[]{:S(2)}, u32[]{:S(2)}) %collective-permute-start.2) | collective-permute-done | bytes 131104 | tf_op jit(solution)/shard_map/ppermute | solution.py:270
  43.6 3.7 %collective-permute-start.4 = (bf16[256,512]{1,0:T(8,128)(2,1)S(1)}, bf16[256,512]{1,0:T(8,128)(2,1)S(1)}, u32[]{:S(2)}, u32[]{:S(2)}) collective-permute-start(bf16[256,512]{1,0:T(8,128)(2,1)S(1)} %constant_dynamic-update-slice_fusion.own_ref), channel_id=1, source_target_pairs={{0,3},{1,0},{2,1},{3,2},{4,7},{5,4},{6,5},{7,6},{8,11},{9,8},{10,9... | collective-permute-start | bytes 786440 | tf_op jit(solution)/shard_map/ppermute | solution.py:279
  47.3 5.9 %collective-permute-done.4.down_ref = bf16[256,512]{1,0:T(8,128)(2,1)S(1)} collective-permute-done((bf16[256,512]{1,0:T(8,128)(2,1)S(1)}, bf16[256,512]{1,0:T(8,128)(2,1)S(1)}, u32[]{:S(2)}, u32[]{:S(2)}) %collective-permute-start.4) | collective-permute-done | bytes 262176 | tf_op jit(solution)/shard_map/ppermute | solution.py:279
  53.1 0.7 copy-done.8
  53.8 2.0 %collective-permute-start.7 = (bf16[512,1024]{1,0:T(8,128)(2,1)S(1)}, bf16[512,1024]{1,0:T(8,128)(2,1)}, u32[]{:S(2)}, u32[]{:S(2)}) collective-permute-start(bf16[512,1024]{1,0:T(8,128)(2,1)S(1)} %collective-permute-done.1.rest_1_), channel_id=1, source_target_pairs={{0,16},{4,12},{8,24},{12,4},{16,0},{20,28},{24,8},{28,20},{1,17},{... | collective-permute-start | bytes 3145736 | tf_op jit(solution)/shard_map/ppermute | solution.py:270
  56.3 0.7 copy-done.2
  57.0 7.7 %collective-permute-done.3.up_ref = bf16[256,512]{1,0:T(8,128)(2,1)} collective-permute-done((bf16[256,512]{1,0:T(8,128)(2,1)S(1)}, bf16[256,512]{1,0:T(8,128)(2,1)}, u32[]{:S(2)}, u32[]{:S(2)}) %collective-permute-start.3) | collective-permute-done | bytes 262176 | tf_op jit(solution)/shard_map/ppermute | solution.py:279
  64.8 3.9 %collective-permute-done.7.rest_3_ = bf16[512,1024]{1,0:T(8,128)(2,1)} collective-permute-done((bf16[512,1024]{1,0:T(8,128)(2,1)S(1)}, bf16[512,1024]{1,0:T(8,128)(2,1)}, u32[]{:S(2)}, u32[]{:S(2)}) %collective-permute-start.7) | collective-permute-done | bytes 1048608 | tf_op jit(solution)/shard_map/ppermute | solution.py:270
  68.7 0.9 %copy-done.3 = bf16[256,512]{1,0:T(8,128)(2,1)S(1)} copy-done((bf16[256,512]{1,0:T(8,128)(2,1)S(1)}, bf16[256,512]{1,0:T(8,128)(2,1)}, u32[]{:S(2)}) %copy-start.3) | copy-done | bytes 262168
  69.7 0.9 %copy-done.9 = bf16[256,512]{1,0:T(8,128)(2,1)S(1)} copy-done((bf16[256,512]{1,0:T(8,128)(2,1)S(1)}, bf16[256,512]{1,0:T(8,128)(2,1)}, u32[]{:S(2)}) %copy-start.9) | copy-done | bytes 262168
  70.6 2.6 %early.1.total_ref = f32[256,1024]{1,0:T(8,128)S(1)} custom-call(s32[5]{0:T(128)S(1)} %stack.32.at_ref, bf16[256,512]{1,0:T(8,128)(2,1)S(1)} %copy-done.3, bf16[256,512]{1,0:T(8,128)(2,1)} %collective-permute-done.3.up_ref, bf16[256,512]{1,0:T(8,128)(2,1)S(1)} %copy-done.9, bf16[512,1024]{1,0:T(8,128)(2,1)S(1)} %copy-done, ...), custom_call_target="tpu_custom_call" | custom-call | flops 1 | tf_op jit(solution)/shard_map/early/pallas_call | solution.py:54
  73.3 1.6 %late.3 = bf16[128,1024]{1,0:T(8,128)(2,1)S(1)} custom-call(s32[5]{0:T(128)S(1)} %stack.32.at_ref, bf16[256,512]{1,0:T(8,128)(2,1)S(1)} %collective-permute-done.5.second_ref, f32[256,1024]{1,0:T(8,128)S(1)} %early.1.total_ref, bf16[512,1024]{1,0:T(8,128)(2,1)S(1)} %copy-done, bf16[512,1024]{1,0:T(8,128)(2,1)S(1)} %collective-permute-done.1.rest_1_, ...), custom_call_target="tpu_custom_call" | custom-call | flops 100000000 | bytes 100000 | tf_op jit(solution)/shard_map/late/pallas_call | solution.py:54
  75.0 1.6 %late.2 = f32[128,1024]{1,0:T(8,128)S(1)} custom-call(s32[5]{0:T(128)S(1)} %stack.32.at_ref, bf16[256,512]{1,0:T(8,128)(2,1)S(1)} %collective-permute-done.5.second_ref, f32[256,1024]{1,0:T(8,128)S(1)} %early.1.total_ref, bf16[512,1024]{1,0:T(8,128)(2,1)S(1)} %copy-done, bf16[512,1024]{1,0:T(8,128)(2,1)S(1)} %collective-permute-done.1.rest_1_, ...), custom_call_target="tpu_custom_call" | custom-call | flops 100000000 | bytes 100000 | tf_op jit(solution)/shard_map/late/pallas_call | solution.py:54
  76.5 0.8 add_convert_fusion
  (35 shorter events, 1.1 us)
Async XLA Ops:
  0.0 1.1 %copy-start.1 = (bf16[3,1024,128]{2,1,0:T(8,128)(2,1)S(1)}, bf16[3,1024,128]{2,1,0:T(8,128)(2,1)}, u32[]{:S(2)}) copy-start(bf16[3,1024,128]{2,1,0:T(8,128)(2,1)} %streams_ref.3) | copy-start | bytes 2359300
  1.1 4.8 %copy-start.13 = (f32[3,7,1024]{2,1,0:T(8,128)S(1)}, f32[3,7,1024]{2,1,0:T(8,128)}, u32[]{:S(2)}) copy-start(f32[3,7,1024]{2,1,0:T(8,128)} %taps_ref.3) | copy-start | bytes 258052
  1.1 4.8 %copy-start.14 = (f32[128,16]{0,1:T(8,128)S(1)}, f32[128,16]{0,1:T(8,128)}, u32[]{:S(2)}) copy-start(f32[128,16]{0,1:T(8,128)} %param.8) | copy-start | bytes 24580
  1.4 16.7 %collective-permute-start.1 = (bf16[512,1024]{1,0:T(8,128)(2,1)}, bf16[512,1024]{1,0:T(8,128)(2,1)S(1)}, u32[]{:S(2)}, u32[]{:S(2)}) collective-permute-start(bf16[512,1024]{1,0:T(8,128)(2,1)} %rest_0_.5), channel_id=1, source_target_pairs={{0,8},{4,20},{8,0},{12,28},{16,24},{20,4},{24,16},{28,12},{1,9},{5... | collective-permute-start | bytes 3145736 | tf_op jit(solution)/shard_map/ppermute | solution.py:270
  4.4 4.8 %collective-permute-start = (bf16[3,8,1024]{2,1,0:T(8,128)(2,1)S(1)}, bf16[3,8,1024]{2,1,0:T(8,128)(2,1)S(1)}, u32[]{:S(2)}, u32[]{:S(2)}) collective-permute-start(bf16[3,8,1024]{2,1,0:T(8,128)(2,1)S(1)} %tails.1), channel_id=1, source_target_pairs={{0,4},{4,8},{8,12},{12,16},{16,20},{20,24},{24,28},{1,5},{5,9},{9,... | collective-permute-start | bytes 147464 | tf_op jit(solution)/shard_map/ppermute | solution.py:25
  8.5 0.7 copy-start.11
  9.2 1.5 %copy-start.15 = (f32[128,16]{0,1:T(8,128)S(1)}, f32[128,16]{0,1:T(8,128)}, u32[]{:S(2)}) copy-start(f32[128,16]{0,1:T(8,128)} %param.9) | copy-start | bytes 24580
  10.0 0.7 copy-start.10
  10.8 0.7 copy-start.16
  11.4 6.7 %copy-start = (bf16[512,1024]{1,0:T(8,128)(2,1)S(1)}, bf16[512,1024]{1,0:T(8,128)(2,1)}, u32[]{:S(2)}) copy-start(bf16[512,1024]{1,0:T(8,128)(2,1)} %rest_0_.5) | copy-start | bytes 3145732
  16.5 0.8 %copy-start.4 = (bf16[128,2048]{1,0:T(8,128)(2,1)}, bf16[128,2048]{1,0:T(8,128)(2,1)S(1)}, u32[]{:S(2)}) copy-start(bf16[128,2048]{1,0:T(8,128)(2,1)S(1)} %get-tuple-element.29.lift_ref) | copy-start | bytes 1572868
  17.3 0.8 %copy-start.6 = (f32[128,1024]{1,0:T(8,128)}, f32[128,1024]{1,0:T(8,128)S(1)}, u32[]{:S(2)}) copy-start(f32[128,1024]{1,0:T(8,128)S(1)} %get-tuple-element.34.base_ref) | copy-start | bytes 1572868
  18.1 35.7 %collective-permute-start.6 = (bf16[512,1024]{1,0:T(8,128)(2,1)S(1)}, bf16[512,1024]{1,0:T(8,128)(2,1)S(1)}, u32[]{:S(2)}, u32[]{:S(2)}) collective-permute-start(bf16[512,1024]{1,0:T(8,128)(2,1)S(1)} %copy-done), channel_id=1, source_target_pairs={{0,16},{4,12},{8,24},{12,4},{16,0},{20,28},{24,8},{28,20},{1,17},{... | collective-permute-start | bytes 3145736 | tf_op jit(solution)/shard_map/ppermute | solution.py:270
  21.7 15.6 %all-to-all-start = ((bf16[8,16,1024]{2,1,0:T(8,128)(2,1)}), bf16[8,16,1024]{2,1,0:T(8,128)(2,1)S(1)}, u32[]{:S(2)}, u32[]{:S(2)}) async-start(bf16[8,16,1024]{2,1,0:T(8,128)(2,1)} %copy-done.10), calls=%async_computation | async-start | bytes 524288 | tf_op jit(solution)/shard_map/all_to_all | solution.py:317
  37.3 1.0 %copy-start.5 = (bf16[128,2048]{1,0:T(8,128)(2,1)S(1)}, bf16[128,2048]{1,0:T(8,128)(2,1)}, u32[]{:S(2)}) copy-start(bf16[128,2048]{1,0:T(8,128)(2,1)} %copy-done.4) | copy-start | bytes 1572868
  38.3 1.0 %copy-start.7 = (f32[128,1024]{1,0:T(8,128)S(1)}, f32[128,1024]{1,0:T(8,128)}, u32[]{:S(2)}) copy-start(f32[128,1024]{1,0:T(8,128)} %copy-done.6) | copy-start | bytes 1572868
  39.3 0.9 %copy-start.12 = (bf16[128,1024]{1,0:T(8,128)(2,1)S(1)}, bf16[128,1024]{1,0:T(8,128)(2,1)}, u32[]{:S(2)}) copy-start(bf16[128,1024]{1,0:T(8,128)(2,1)} %copy-done.11) | copy-start | bytes 786436
  42.2 1.3 %collective-permute-start.2 = (bf16[128,512]{1,0:T(8,128)(2,1)S(1)}, bf16[128,512]{1,0:T(8,128)(2,1)S(1)}, u32[]{:S(2)}, u32[]{:S(2)}) collective-permute-start(bf16[128,512]{1,0:T(8,128)(2,1)S(1)} %get-tuple-element.36), channel_id=1, source_target_pairs={{0,4},{4,0},{8,12},{12,8},{16,20},{20,16},{24,28},{28,24},{1,5},{5... | collective-permute-start | bytes 393224 | tf_op jit(solution)/shard_map/ppermute | solution.py:270
  43.6 9.5 %collective-permute-start.4 = (bf16[256,512]{1,0:T(8,128)(2,1)S(1)}, bf16[256,512]{1,0:T(8,128)(2,1)S(1)}, u32[]{:S(2)}, u32[]{:S(2)}) collective-permute-start(bf16[256,512]{1,0:T(8,128)(2,1)S(1)} %constant_dynamic-update-slice_fusion.own_ref), channel_id=1, source_target_pairs={{0,3},{1,0},{2,1},{3,2},{4,7},{5,4},{6,5},{7,6},{8,11},{9,8},{10,9... | collective-permute-start | bytes 786440 | tf_op jit(solution)/shard_map/ppermute | solution.py:279
  53.1 0.7 copy-start.8
  53.8 14.9 %collective-permute-start.7 = (bf16[512,1024]{1,0:T(8,128)(2,1)S(1)}, bf16[512,1024]{1,0:T(8,128)(2,1)}, u32[]{:S(2)}, u32[]{:S(2)}) collective-permute-start(bf16[512,1024]{1,0:T(8,128)(2,1)S(1)} %collective-permute-done.1.rest_1_), channel_id=1, source_target_pairs={{0,16},{4,12},{8,24},{12,4},{16,0},{20,28},{24,8},{28,20},{1,17},{... | collective-permute-start | bytes 3145736 | tf_op jit(solution)/shard_map/ppermute | solution.py:270
  55.9 8.9 %collective-permute-start.3 = (bf16[256,512]{1,0:T(8,128)(2,1)S(1)}, bf16[256,512]{1,0:T(8,128)(2,1)}, u32[]{:S(2)}, u32[]{:S(2)}) collective-permute-start(bf16[256,512]{1,0:T(8,128)(2,1)S(1)} %constant_dynamic-update-slice_fusion.own_ref), channel_id=1, source_target_pairs={{0,1},{1,2},{2,3},{3,0},{4,5},{5,6},{6,7},{7,4},{8,9},{9,10},{10,1... | collective-permute-start | bytes 786440 | tf_op jit(solution)/shard_map/ppermute | solution.py:279
  56.3 0.7 copy-start.2
  64.7 8.5 %collective-permute-start.5 = (bf16[256,512]{1,0:T(8,128)(2,1)}, bf16[256,512]{1,0:T(8,128)(2,1)S(1)}, u32[]{:S(2)}, u32[]{:S(2)}) collective-permute-start(bf16[256,512]{1,0:T(8,128)(2,1)} %collective-permute-done.3.up_ref), channel_id=1, source_target_pairs={{0,1},{1,2},{2,3},{3,0},{4,5},{5,6},{6,7},{7,4},{8,9},{9,10},{10,1... | collective-permute-start | bytes 786440 | tf_op jit(solution)/shard_map/ppermute | solution.py:279
  68.7 1.0 %copy-start.3 = (bf16[256,512]{1,0:T(8,128)(2,1)S(1)}, bf16[256,512]{1,0:T(8,128)(2,1)}, u32[]{:S(2)}) copy-start(bf16[256,512]{1,0:T(8,128)(2,1)} %copy-done.2) | copy-start | bytes 786436
  69.7 0.9 %copy-start.9 = (bf16[256,512]{1,0:T(8,128)(2,1)S(1)}, bf16[256,512]{1,0:T(8,128)(2,1)}, u32[]{:S(2)}) copy-start(bf16[256,512]{1,0:T(8,128)(2,1)} %copy-done.8) | copy-start | bytes 786436
  74.9 1.7 %collective-permute-start.8 = (bf16[128,1024]{1,0:T(8,128)(2,1)S(1)}, bf16[128,1024]{1,0:T(8,128)(2,1)S(1)}, u32[]{:S(2)}, u32[]{:S(2)}) collective-permute-start(bf16[128,1024]{1,0:T(8,128)(2,1)S(1)} %late.3), channel_id=1, source_target_pairs={{0,4},{4,0},{8,12},{12,8},{16,20},{20,16},{24,28},{28,24},{1,5},{5... | collective-permute-start | bytes 786440 | tf_op jit(solution)/shard_map/ppermute | solution.py:270

commit v10 on v8

--- a/solution.py
+++ b/solution.py
@@ -125,7 +125,7 @@
         query, left, right = (
             short_conv(stream, chans, length, padded_ref.at[index * 3 + stream], taps_ref) for stream in range(3)
         )
-        query_ref[:, chans] = query
+        query_ref[:, chans] = query.astype(BF16)
         gated_ref[:, chans] = left * right
 
     unrolled(channels // TILE, turn)
@@ -228,7 +228,7 @@
         states = tile_of(index, in_tile * poles)
         lift = lift_ref[:, states]
         carried = dot(lift, high) + dot(lift, low)
-        query = jnp.concatenate([first_ref[:, chans], query_ref[ROWS:, chans]], axis=0)
+        query = jnp.concatenate([first_ref[:, chans], query_ref[:, chans].astype(F32)[ROWS:]], axis=0)
         mixed_ref[:, chans] = (query * (base_ref[:, chans] + carried)).astype(BF16)
 
     unrolled(channels // TILE, tile)
@@ -237,13 +237,14 @@
     other_ref[...] = mixed_ref[:, tile_of(1 - core, share)]
 
 
-def project_kernel(at_ref, own_ref, up_ref, second_ref, down_ref, *rest):
+def project_kernel(at_ref, own_ref, below_ref, above_ref, second_ref, far_ref, *rest):
     *weight_refs, mine_ref, other_ref, layers_ref = rest
     layer = at_ref[0]
+    edge = (layer == 0) | (layer == 3)
     layers_ref[layer] = own_ref[...]
-    layers_ref[lax.rem(layer + 3, 4)] = up_ref[...]
+    layers_ref[jnp.where(layer == 0, 1, layer - 1)] = jnp.where(layer == 0, above_ref[...], below_ref[...])
     layers_ref[lax.rem(layer + 2, 4)] = second_ref[...]
-    layers_ref[lax.rem(layer + 1, 4)] = down_ref[...]
+    layers_ref[jnp.where(edge, 3 - layer, layer + 1)] = jnp.where(edge, far_ref[...], above_ref[...])
     length, features = mine_ref.shape
     for column in range(0, features, COLUMNS):
         columns = slice(column, column + COLUMNS)
@@ -265,9 +266,14 @@
     return lax.optimization_barrier((value, earlier))[0]
 
 
-def around(value, steps):
-    count = lax.axis_size("tp")
-    return lax.ppermute(value, "tp", [(source, (source + steps) % count) for source in range(count)])
+def over_layers(block):
+    layer = lax.axis_index("tp")
+    below = lax.ppermute(block, "tp", [(0, 1), (1, 2), (2, 3)])
+    above = lax.ppermute(block, "tp", [(1, 0), (2, 1), (3, 2)])
+    onward = jnp.where(layer == 1, above, jnp.where(layer == 2, below, block))
+    second = lax.ppermute(onward, "tp", [(0, 2), (3, 1), (2, 3), (1, 0)])
+    far = lax.ppermute(block, "tp", [(0, 3), (3, 0)])
+    return below, above, second, far
 
 
 def local(streams, conv_weight, rates, residues, skip, out_weight):
@@ -282,13 +288,13 @@
     (tails,) = call(tails_kernel, [((3, ROWS, channels), BF16)], "tails", streams)
     before = from_behind(tails, "ctx", 1)
     if square:
-        near = swap(after(out_weight, tails), 2, 4)
+        near = swap(out_weight, 2, 4)
     tiles = channels // TILE
     heads, query, gated, decay, step = call(
         prepare_kernel,
         [
             ((3, ROWS, channels), F32),
-            ((length, channels), F32),
+            ((length, channels), BF16),
             ((length, channels), F32),
             ((2, groups * poles, length), BF16),
             ((poles, channels), F32),
@@ -335,8 +341,7 @@
         other = lax.dynamic_index_in_dim(by_core, 1 - core, 0, keepdims=False)
     block = jnp.concatenate([mine, swap(other, 1)], axis=0)
     layer = lax.axis_index("tp").astype(jnp.int32)
-    up, down = around(block, 1), around(block, -1)
-    second = around(after(up, down), 1)
+    blocks_of_layers = over_layers(block)
     if square:
         diagonal = swap(after(near, block), 4, 2)
         weight = (out_weight, near, other_near, diagonal)
@@ -351,8 +356,8 @@
         project_kernel,
         [((length, features), F32), ((length, features), BF16)],
         "project",
-        jnp.stack([layer] + place), block, up, second, down, *weight,
-        specs=smem + whole(4 + len(weight)),
+        jnp.stack([layer] + place), block, *blocks_of_layers, *weight,
+        specs=smem + whole(5 + len(weight)),
         scratch=[pltpu.VMEM((layers,) + block.shape, BF16)],
         flops=10**9,
     )

time: 60.1 us -> 61.5 us (1.023)
  starting transfers between devices: 18.5 us -> 31.8 us
  waiting for transfers between devices: 20.9 us -> 10.5 us
  local copies, waits for them, and re-layouts: 5.35 us -> 2.81 us
  other arithmetic: 0.83 us -> 1.58 us
    ppermute x3 -> x4, starting transfers between devices: 5.23 us -> 19.6 us  [the longest x1 10.4 us: over_layers(): second = lax.ppermute(onward, 'tp', [(0, 2), (3, 1), (2, 3), (1, 0)])]
    ppermute x3 -> x4, waiting for transfers between devices: 19 us -> 7.51 us  [the longest x1 4.12 us: over_layers(): second = lax.ppermute(onward, 'tp', [(0, 2), (3, 1), (2, 3), (1, 0)])]
    unnamed x21 -> x17, local copies, waits for them, and re-layouts: 5.25 us -> 2.72 us
    ppermute x5, starting transfers between devices: 6.22 us -> 5.18 us  [swap(): return lax.ppermute(value, 'ctx', pairs)]
    all_to_all x1, waiting for transfers between devices: 0.4 us -> 1.18 us  [local(): lax.all_to_all(ends, 'ctx', split_axis=0, concat_axis=0, tiled=True)]
    select_n x0 -> x1, other arithmetic: none -> 0.74 us  [over_layers(): onward = jnp.where(layer == 1, above, jnp.where(layer == 2, below, block))]
  transfers between devices with their start and end apart: 10 -> 11, of which waited for: 5 -> 6; matrix products, arithmetic and copies ran while one was open for 0% -> 2% of each run, Pallas kernels for 15% -> 15%
where the time goes in v10:
time: 61.5 us; the launch traced here: 61 us
  starting transfers between devices  31.8 us (52%)
  Pallas kernels  14.2 us (23%)
  waiting for transfers between devices  10.5 us (17%)
  local copies, waits for them, and re-layouts  2.81 us (5%)
  other arithmetic  1.58 us (3%)
    pallas_call x6, Pallas kernels, call(): pl.pallas_call(kernel, out_shape=tuple((jax.ShapeDtypeStruct(*out) for ou...  14.2 us
    ppermute x1, starting transfers between devices, over_layers(): second = lax.ppermute(onward, 'tp', [(0, 2), (3, 1), (2, 3), (1, 0)])  10.4 us
    all_to_all x1, starting transfers between devices, local(): lax.all_to_all(ends, 'ctx', split_axis=0, concat_axis=0, tiled=True)  5.53 us
    ppermute x5, starting transfers between devices, swap(): return lax.ppermute(value, 'ctx', pairs)  5.18 us
    ppermute x1, starting transfers between devices, over_layers(): below = lax.ppermute(block, 'tp', [(0, 1), (1, 2), (2, 3)])  4.56 us
    ppermute x1, waiting for transfers between devices, over_layers(): second = lax.ppermute(onward, 'tp', [(0, 2), (3, 1), (2, 3), (1, 0)])  4.12 us
    ppermute x1, starting transfers between devices, over_layers(): far = lax.ppermute(block, 'tp', [(0, 3), (3, 0)])  3.32 us
    unnamed x17, local copies, waits for them, and re-layouts  2.72 us
  transfers between devices with their start and end apart: 11, of which 6 were waited for; matrix products, arithmetic and copies ran while one was open for 2% of the time, Pallas kernels for 15%

profile of v10, /device:TPU:0, one launch (start us, length us, event | category | flops | bytes accessed | tf_op | source)
XLA Modules:
  0.0 61.0 jit_solution(2061484895294296378)
XLA Ops:
  0.0 2.9 %collective-permute-start.1 = (bf16[512,1024]{1,0:T(8,128)(2,1)}, bf16[512,1024]{1,0:T(8,128)(2,1)S(1)}, u32[]{:S(2)}, u32[]{:S(2)}) collective-permute-start(bf16[512,1024]{1,0:T(8,128)(2,1)} %rest_0_.1), channel_id=1, source_target_pairs={{0,8},{4,20},{8,0},{12,28},{16,24},{20,4},{24,16},{28,12},{1,9},{5... | collective-permute-start | bytes 3145736 | tf_op jit(solution)/shard_map/ppermute | solution.py:262
  2.9 1.1 %copy-done.1 = bf16[3,1024,128]{2,1,0:T(8,128)(2,1)S(1)} copy-done((bf16[3,1024,128]{2,1,0:T(8,128)(2,1)S(1)}, bf16[3,1024,128]{2,1,0:T(8,128)(2,1)}, u32[]{:S(2)}) %copy-start.1) | copy-done | bytes 786456
  4.1 0.3 tails.1
  4.4 1.5 %collective-permute-start = (bf16[3,8,1024]{2,1,0:T(8,128)(2,1)S(1)}, bf16[3,8,1024]{2,1,0:T(8,128)(2,1)S(1)}, u32[]{:S(2)}, u32[]{:S(2)}) collective-permute-start(bf16[3,8,1024]{2,1,0:T(8,128)(2,1)S(1)} %tails.1), channel_id=1, source_target_pairs={{0,4},{4,8},{8,12},{12,16},{16,20},{20,24},{24,28},{1,5},{5,9},{9,... | collective-permute-start | bytes 147464 | tf_op jit(solution)/shard_map/ppermute | solution.py:25
  5.9 2.6 %prepare.1 = (f32[3,8,1024]{2,1,0:T(8,128)S(1)}, bf16[128,1024]{1,0:T(8,128)(2,1)S(1)}, f32[128,1024]{1,0:T(8,128)S(1)}, bf16[2,2048,128]{2,1,0:T(8,128)(2,1)S(1)}, f32[16,1024]{1,0:T(8,128)S(1)}) custom-call(bf16[3,1024,128]{2,1,0:T(8,128)(2,1)S(1)} %copy-done.1, f32[3,7,1024]{2,1,0:T(8,128)S(1)} %copy-done.4, f32[16,128]{1,0:T(8,128)S(1)} %bitcast.10), custom_call_target="tpu_custom_call" | custom-call | flops 1000000000 | bytes 10000000 | tf_op jit(solution)/shard_map/prepare/pallas_call | solution.py:54
  8.6 1.5 %states.1 = (bf16[8,16,1024]{2,1,0:T(8,128)(2,1)}, bf16[128,1024]{1,0:T(8,128)(2,1)S(1)}, f32[8,1024]{1,0:T(8,128)S(1)}) custom-call(bf16[3,8,1024]{2,1,0:T(8,128)(2,1)S(1)} %collective-permute-done.before_ref, f32[3,8,1024]{2,1,0:T(8,128)S(1)} %get-tuple-element.23.heads_ref, f32[3,7,1024]{2,1,0:T(8,128)S(1)} %copy-done.4, ...), custom_call_target="tpu_custom_call" | custom-call | flops 100000000 | bytes 1000000 | tf_op jit(solution)/shard_map/states/pallas_call | solution.py:54
  10.1 5.5 %all-to-all-start = ((bf16[8,16,1024]{2,1,0:T(8,128)(2,1)}), bf16[8,16,1024]{2,1,0:T(8,128)(2,1)S(1)}, u32[]{:S(2)}, u32[]{:S(2)}) async-start(bf16[8,16,1024]{2,1,0:T(8,128)(2,1)} %get-tuple-element.26), calls=%async_computation | async-start | bytes 524288 | tf_op jit(solution)/shard_map/all_to_all | solution.py:314
  15.6 0.0 copy-start.7
  15.6 0.1 pad_add_fusion.at_ref
  15.7 0.6 copy-done.6
  16.3 0.0 copy-done.7
  16.3 5.0 %inside.1 = (bf16[128,2048]{1,0:T(8,128)(2,1)S(1)}, f32[128,1024]{1,0:T(8,128)S(1)}) custom-call(bf16[128,1024]{1,0:T(8,128)(2,1)S(1)} %get-tuple-element.28.gated_ref, f32[1,1024]{1,0:T(1,128)S(1)} %bitcast.13, f32[16,128]{1,0:T(8,128)S(1)} %bitcast.11, f32[16,128]{1,0:T(8,128)S(1)} %bitcast.12), custom_call_target="tpu_custom_call" | custom-call | flops 1000000000 | bytes 10000000 | tf_op jit(solution)/shard_map/inside/pallas_call | solution.py:54
  21.3 0.0 copy-start
  21.4 1.2 %all-to-all-done.ends_ref = bf16[8,16,1024]{2,1,0:T(8,128)(2,1)S(1)} async-done(((bf16[8,16,1024]{2,1,0:T(8,128)(2,1)}), bf16[8,16,1024]{2,1,0:T(8,128)(2,1)S(1)}, u32[]{:S(2)}, u32[]{:S(2)}) %all-to-all-start) | async-done | bytes 262176 | tf_op jit(solution)/shard_map/all_to_all | solution.py:314
  22.5 0.9 %copy-done.3 = bf16[128,1024]{1,0:T(8,128)(2,1)S(1)} copy-done((bf16[128,1024]{1,0:T(8,128)(2,1)S(1)}, bf16[128,1024]{1,0:T(8,128)(2,1)}, u32[]{:S(2)}) %copy-start.3) | copy-done | bytes 262168
  23.5 1.9 %finish.1 = (bf16[128,512]{1,0:T(8,128)(2,1)S(1)}, bf16[128,512]{1,0:T(8,128)(2,1)S(1)}, bf16[128,1024]{1,0:T(8,128)(2,1)}) custom-call(s32[2]{0:T(128)S(1)} %pad_add_fusion.at_ref, bf16[8,16,1024]{2,1,0:T(8,128)(2,1)S(1)} %all-to-all-done.ends_ref, f32[16,1024]{1,0:T(8,128)S(1)} %get-tuple-element.27.step_ref, ...), custom_call_target="tpu_custom_call" | custom-call | flops 100000000 | bytes 1000000 | tf_op jit(solution)/shard_map/finish/pallas_call | solution.py:54
  25.4 1.1 %collective-permute-start.7 = (bf16[512,1024]{1,0:T(8,128)(2,1)S(1)}, bf16[512,1024]{1,0:T(8,128)(2,1)}, u32[]{:S(2)}, u32[]{:S(2)}) collective-permute-start(bf16[512,1024]{1,0:T(8,128)(2,1)S(1)} %copy-done), channel_id=1, source_target_pairs={{0,16},{4,12},{8,24},{12,4},{16,0},{20,28},{24,8},{28,20},{1,17},{... | collective-permute-start | bytes 3145736 | tf_op jit(solution)/shard_map/ppermute | solution.py:262
  26.5 0.2 collective-permute-done.2
  26.8 1.1 %collective-permute-start.8 = (bf16[512,1024]{1,0:T(8,128)(2,1)S(1)}, bf16[512,1024]{1,0:T(8,128)(2,1)}, u32[]{:S(2)}, u32[]{:S(2)}) collective-permute-start(bf16[512,1024]{1,0:T(8,128)(2,1)S(1)} %collective-permute-done.1.rest_1_), channel_id=1, source_target_pairs={{0,16},{4,12},{8,24},{12,4},{16,0},{20,28},{24,8},{28,20},{1,17},{... | collective-permute-start | bytes 3145736 | tf_op jit(solution)/shard_map/ppermute | solution.py:262
  27.9 1.3 %collective-permute-start.4 = (bf16[256,512]{1,0:T(8,128)(2,1)S(1)}, bf16[256,512]{1,0:T(8,128)(2,1)S(1)}, u32[]{:S(2)}, u32[]{:S(2)}) collective-permute-start(bf16[256,512]{1,0:T(8,128)(2,1)S(1)} %constant_dynamic-update-slice_fusion.own_ref), channel_id=1, source_target_pairs={{1,0},{2,1},{3,2},{5,4},{6,5},{7,6},{9,8},{10,9},{11,10},{13,12},{... | collective-permute-start | bytes 786440 | tf_op jit(solution)/shard_map/ppermute | solution.py:272
  29.2 4.6 %collective-permute-start.3 = (bf16[256,512]{1,0:T(8,128)(2,1)S(1)}, bf16[256,512]{1,0:T(8,128)(2,1)S(1)}, u32[]{:S(2)}, u32[]{:S(2)}) collective-permute-start(bf16[256,512]{1,0:T(8,128)(2,1)S(1)} %constant_dynamic-update-slice_fusion.own_ref), channel_id=1, source_target_pairs={{0,1},{1,2},{2,3},{4,5},{5,6},{6,7},{8,9},{9,10},{10,11},{12,13},{... | collective-permute-start | bytes 786440 | tf_op jit(solution)/shard_map/ppermute | solution.py:271
  33.7 3.3 %collective-permute-start.6 = (bf16[256,512]{1,0:T(8,128)(2,1)S(1)}, bf16[256,512]{1,0:T(8,128)(2,1)S(1)}, u32[]{:S(2)}, u32[]{:S(2)}) collective-permute-start(bf16[256,512]{1,0:T(8,128)(2,1)S(1)} %constant_dynamic-update-slice_fusion.own_ref), channel_id=1, source_target_pairs={{0,3},{3,0},{4,7},{7,4},{8,11},{11,8},{12,15},{15,12},{16,19},{19,... | collective-permute-start | bytes 786440 | tf_op jit(solution)/shard_map/ppermute | solution.py:275
  37.1 0.7 %collective-permute-done.4.above_ref = bf16[256,512]{1,0:T(8,128)(2,1)S(1)} collective-permute-done((bf16[256,512]{1,0:T(8,128)(2,1)S(1)}, bf16[256,512]{1,0:T(8,128)(2,1)S(1)}, u32[]{:S(2)}, u32[]{:S(2)}) %collective-permute-start.4) | collective-permute-done | bytes 262176 | tf_op jit(solution)/shard_map/ppermute | solution.py:272
  37.7 2.7 %collective-permute-done.3.below_ref = bf16[256,512]{1,0:T(8,128)(2,1)S(1)} collective-permute-done((bf16[256,512]{1,0:T(8,128)(2,1)S(1)}, bf16[256,512]{1,0:T(8,128)(2,1)S(1)}, u32[]{:S(2)}, u32[]{:S(2)}) %collective-permute-start.3) | collective-permute-done | bytes 262176 | tf_op jit(solution)/shard_map/ppermute | solution.py:271
  40.5 0.7 %select_select_fusion = bf16[256,512]{1,0:T(8,128)(2,1)} fusion(bf16[256,512]{1,0:T(8,128)(2,1)S(1)} %collective-permute-done.4.above_ref, bf16[256,512]{1,0:T(8,128)(2,1)S(1)} %collective-permute-done.3.below_ref, bf16[256,512]{1,0:T(8,128)(2,1)S(1)} %constant_dynamic-update-slice_fusion.own_ref, pred[]{:T(512)S(6)} %eq.13, pred[]{:T(512)S(6)} %eq.12), kind=kLoop, calls=%fused_computation.1 | loop fusion | flops 262144 | bytes 1048578 | tf_op jit(solution)/shard_map/jit(_where)/select_n | solution.py:273
  41.2 10.4 %collective-permute-start.5 = (bf16[256,512]{1,0:T(8,128)(2,1)}, bf16[256,512]{1,0:T(8,128)(2,1)S(1)}, u32[]{:S(2)}, u32[]{:S(2)}) collective-permute-start(bf16[256,512]{1,0:T(8,128)(2,1)} %select_select_fusion), channel_id=1, source_target_pairs={{0,2},{3,1},{2,3},{1,0},{4,6},{7,5},{6,7},{5,4},{8,10},{11,9},{10,... | collective-permute-start | bytes 786440 | tf_op jit(solution)/shard_map/ppermute | solution.py:274
  51.6 0.1 stack.32.at_ref
  51.7 4.1 %collective-permute-done.5.second_ref = bf16[256,512]{1,0:T(8,128)(2,1)S(1)} collective-permute-done((bf16[256,512]{1,0:T(8,128)(2,1)}, bf16[256,512]{1,0:T(8,128)(2,1)S(1)}, u32[]{:S(2)}, u32[]{:S(2)}) %collective-permute-start.5) | collective-permute-done | bytes 262176 | tf_op jit(solution)/shard_map/ppermute | solution.py:274
  55.8 2.9 %project.1 = (f32[128,1024]{1,0:T(8,128)S(1)}, bf16[128,1024]{1,0:T(8,128)(2,1)S(1)}) custom-call(s32[5]{0:T(128)S(1)} %stack.32.at_ref, bf16[256,512]{1,0:T(8,128)(2,1)S(1)} %constant_dynamic-update-slice_fusion.own_ref, bf16[256,512]{1,0:T(8,128)(2,1)S(1)} %collective-permute-done.3.below_ref, bf16[256,512]{1,0:T(8,128)(2,1)S(1)} %collective-permute-done.4.above_ref, ...), custom_call_target="tpu_custom_call" | custom-call | flops 1000000000 | bytes 10000000 | tf_op jit(solution)/shard_map/project/pallas_call | solution.py:54
  58.7 0.1 collective-permute-start.9
  58.7 1.5 %collective-permute-done.9 = bf16[128,1024]{1,0:T(8,128)(2,1)S(1)} collective-permute-done((bf16[128,1024]{1,0:T(8,128)(2,1)S(1)}, bf16[128,1024]{1,0:T(8,128)(2,1)S(1)}, u32[]{:S(2)}, u32[]{:S(2)}) %collective-permute-start.9) | collective-permute-done | bytes 262176 | tf_op jit(solution)/shard_map/ppermute | solution.py:262
  60.3 0.8 %add_convert_fusion = bf16[128,1024]{1,0:T(8,128)(2,1)} fusion(f32[128,1024]{1,0:T(8,128)S(1)} %get-tuple-element.39, bf16[128,1024]{1,0:T(8,128)(2,1)S(1)} %collective-permute-done.9), kind=kLoop, calls=%fused_computation | loop fusion | flops 393216 | bytes 1048576 | tf_op jit(solution)/shard_map/convert_element_type | solution.py:365
  (18 shorter events, 0.1 us)
Async XLA Ops:
  0.0 21.3 %collective-permute-start.1 = (bf16[512,1024]{1,0:T(8,128)(2,1)}, bf16[512,1024]{1,0:T(8,128)(2,1)S(1)}, u32[]{:S(2)}, u32[]{:S(2)}) collective-permute-start(bf16[512,1024]{1,0:T(8,128)(2,1)} %rest_0_.1), channel_id=1, source_target_pairs={{0,8},{4,20},{8,0},{12,28},{16,24},{20,4},{24,16},{28,12},{1,9},{5... | collective-permute-start | bytes 3145736 | tf_op jit(solution)/shard_map/ppermute | solution.py:262
  2.9 1.1 %copy-start.1 = (bf16[3,1024,128]{2,1,0:T(8,128)(2,1)S(1)}, bf16[3,1024,128]{2,1,0:T(8,128)(2,1)}, u32[]{:S(2)}) copy-start(bf16[3,1024,128]{2,1,0:T(8,128)(2,1)} %streams_ref.3) | copy-start | bytes 2359300
  4.1 1.8 %copy-start.4 = (f32[3,7,1024]{2,1,0:T(8,128)S(1)}, f32[3,7,1024]{2,1,0:T(8,128)}, u32[]{:S(2)}) copy-start(f32[3,7,1024]{2,1,0:T(8,128)} %taps_ref.3) | copy-start | bytes 258052
  4.1 1.8 %copy-start.5 = (f32[128,16]{0,1:T(8,128)S(1)}, f32[128,16]{0,1:T(8,128)}, u32[]{:S(2)}) copy-start(f32[128,16]{0,1:T(8,128)} %param.8) | copy-start | bytes 24580
  4.4 4.2 %collective-permute-start = (bf16[3,8,1024]{2,1,0:T(8,128)(2,1)S(1)}, bf16[3,8,1024]{2,1,0:T(8,128)(2,1)S(1)}, u32[]{:S(2)}, u32[]{:S(2)}) collective-permute-start(bf16[3,8,1024]{2,1,0:T(8,128)(2,1)S(1)} %tails.1), channel_id=1, source_target_pairs={{0,4},{4,8},{8,12},{12,16},{16,20},{20,24},{24,28},{1,5},{5,9},{9,... | collective-permute-start | bytes 147464 | tf_op jit(solution)/shard_map/ppermute | solution.py:25
  8.5 1.5 %copy-start.2 = (bf16[128,1024]{1,0:T(8,128)(2,1)}, bf16[128,1024]{1,0:T(8,128)(2,1)S(1)}, u32[]{:S(2)}) copy-start(bf16[128,1024]{1,0:T(8,128)(2,1)S(1)} %get-tuple-element.30.query_ref) | copy-start | bytes 786436
  10.1 12.5 %all-to-all-start = ((bf16[8,16,1024]{2,1,0:T(8,128)(2,1)}), bf16[8,16,1024]{2,1,0:T(8,128)(2,1)S(1)}, u32[]{:S(2)}, u32[]{:S(2)}) async-start(bf16[8,16,1024]{2,1,0:T(8,128)(2,1)} %get-tuple-element.26), calls=%async_computation | async-start | bytes 524288 | tf_op jit(solution)/shard_map/all_to_all | solution.py:314
  15.6 0.7 %copy-start.6 = (f32[128,16]{0,1:T(8,128)S(1)}, f32[128,16]{0,1:T(8,128)}, u32[]{:S(2)}) copy-start(f32[128,16]{0,1:T(8,128)} %param.9) | copy-start | bytes 24580
  15.6 0.7 %copy-start.7 = (f32[1024]{0:T(1024)S(1)}, f32[1024]{0:T(1024)}, u32[]{:S(2)}) copy-start(f32[1024]{0:T(1024)} %param.10) | copy-start | bytes 12292
  21.3 4.1 %copy-start = (bf16[512,1024]{1,0:T(8,128)(2,1)S(1)}, bf16[512,1024]{1,0:T(8,128)(2,1)}, u32[]{:S(2)}) copy-start(bf16[512,1024]{1,0:T(8,128)(2,1)} %rest_0_.1) | copy-start | bytes 3145732
  22.5 1.0 %copy-start.3 = (bf16[128,1024]{1,0:T(8,128)(2,1)S(1)}, bf16[128,1024]{1,0:T(8,128)(2,1)}, u32[]{:S(2)}) copy-start(bf16[128,1024]{1,0:T(8,128)(2,1)} %copy-done.2) | copy-start | bytes 786436
  25.4 1.3 %collective-permute-start.2 = (bf16[128,512]{1,0:T(8,128)(2,1)S(1)}, bf16[128,512]{1,0:T(8,128)(2,1)S(1)}, u32[]{:S(2)}, u32[]{:S(2)}) collective-permute-start(bf16[128,512]{1,0:T(8,128)(2,1)S(1)} %get-tuple-element.35), channel_id=1, source_target_pairs={{0,4},{4,0},{8,12},{12,8},{16,20},{20,16},{24,28},{28,24},{1,5},{5... | collective-permute-start | bytes 393224 | tf_op jit(solution)/shard_map/ppermute | solution.py:262
  25.4 30.4 %collective-permute-start.7 = (bf16[512,1024]{1,0:T(8,128)(2,1)S(1)}, bf16[512,1024]{1,0:T(8,128)(2,1)}, u32[]{:S(2)}, u32[]{:S(2)}) collective-permute-start(bf16[512,1024]{1,0:T(8,128)(2,1)S(1)} %copy-done), channel_id=1, source_target_pairs={{0,16},{4,12},{8,24},{12,4},{16,0},{20,28},{24,8},{28,20},{1,17},{... | collective-permute-start | bytes 3145736 | tf_op jit(solution)/shard_map/ppermute | solution.py:262
  26.8 29.0 %collective-permute-start.8 = (bf16[512,1024]{1,0:T(8,128)(2,1)S(1)}, bf16[512,1024]{1,0:T(8,128)(2,1)}, u32[]{:S(2)}, u32[]{:S(2)}) collective-permute-start(bf16[512,1024]{1,0:T(8,128)(2,1)S(1)} %collective-permute-done.1.rest_1_), channel_id=1, source_target_pairs={{0,16},{4,12},{8,24},{12,4},{16,0},{20,28},{24,8},{28,20},{1,17},{... | collective-permute-start | bytes 3145736 | tf_op jit(solution)/shard_map/ppermute | solution.py:262
  27.9 9.9 %collective-permute-start.4 = (bf16[256,512]{1,0:T(8,128)(2,1)S(1)}, bf16[256,512]{1,0:T(8,128)(2,1)S(1)}, u32[]{:S(2)}, u32[]{:S(2)}) collective-permute-start(bf16[256,512]{1,0:T(8,128)(2,1)S(1)} %constant_dynamic-update-slice_fusion.own_ref), channel_id=1, source_target_pairs={{1,0},{2,1},{3,2},{5,4},{6,5},{7,6},{9,8},{10,9},{11,10},{13,12},{... | collective-permute-start | bytes 786440 | tf_op jit(solution)/shard_map/ppermute | solution.py:272
  29.2 11.3 %collective-permute-start.3 = (bf16[256,512]{1,0:T(8,128)(2,1)S(1)}, bf16[256,512]{1,0:T(8,128)(2,1)S(1)}, u32[]{:S(2)}, u32[]{:S(2)}) collective-permute-start(bf16[256,512]{1,0:T(8,128)(2,1)S(1)} %constant_dynamic-update-slice_fusion.own_ref), channel_id=1, source_target_pairs={{0,1},{1,2},{2,3},{4,5},{5,6},{6,7},{8,9},{9,10},{10,11},{12,13},{... | collective-permute-start | bytes 786440 | tf_op jit(solution)/shard_map/ppermute | solution.py:271
  33.7 17.9 %collective-permute-start.6 = (bf16[256,512]{1,0:T(8,128)(2,1)S(1)}, bf16[256,512]{1,0:T(8,128)(2,1)S(1)}, u32[]{:S(2)}, u32[]{:S(2)}) collective-permute-start(bf16[256,512]{1,0:T(8,128)(2,1)S(1)} %constant_dynamic-update-slice_fusion.own_ref), channel_id=1, source_target_pairs={{0,3},{3,0},{4,7},{7,4},{8,11},{11,8},{12,15},{15,12},{16,19},{19,... | collective-permute-start | bytes 786440 | tf_op jit(solution)/shard_map/ppermute | solution.py:275
  41.2 14.6 %collective-permute-start.5 = (bf16[256,512]{1,0:T(8,128)(2,1)}, bf16[256,512]{1,0:T(8,128)(2,1)S(1)}, u32[]{:S(2)}, u32[]{:S(2)}) collective-permute-start(bf16[256,512]{1,0:T(8,128)(2,1)} %select_select_fusion), channel_id=1, source_target_pairs={{0,2},{3,1},{2,3},{1,0},{4,6},{7,5},{6,7},{5,4},{8,10},{11,9},{10,... | collective-permute-start | bytes 786440 | tf_op jit(solution)/shard_map/ppermute | solution.py:274
  58.7 1.6 %collective-permute-start.9 = (bf16[128,1024]{1,0:T(8,128)(2,1)S(1)}, bf16[128,1024]{1,0:T(8,128)(2,1)S(1)}, u32[]{:S(2)}, u32[]{:S(2)}) collective-permute-start(bf16[128,1024]{1,0:T(8,128)(2,1)S(1)} %get-tuple-element.40), channel_id=1, source_target_pairs={{0,4},{4,0},{8,12},{12,8},{16,20},{20,16},{24,28},{28,24},{1,5},{5... | collective-permute-start | bytes 786440 | tf_op jit(solution)/shard_map/ppermute | solution.py:262

commit v11 on v8

--- a/solution.py
+++ b/solution.py
@@ -91,7 +91,10 @@
     return total
 
 
-def prepare_kernel(streams_ref, taps_ref, rates_ref, heads_ref, query_ref, gated_ref, decay_ref, step_ref, padded_ref):
+def prepare_kernel(
+    streams_ref, taps_ref, rates_ref, residues_ref,
+    heads_ref, query_ref, gated_ref, decay_ref, step_ref, coef_ref, padded_ref,
+):
     channels, length = streams_ref.shape[1:]
     poles, groups = rates_ref.shape
     width = channels // groups
@@ -99,6 +102,7 @@
     unit = identity(length)
     lag = (length - 1) - iota((poles, length), 1).astype(F32)
     owner = iota((poles, TILE), 1) // width
+    coef_ref[...] = residues_ref[...] * jnp.sqrt(2.0 * rates_ref[...]) / math.sqrt(poles)
 
     def turn(index):
         chans = tile_of(index)
@@ -125,7 +129,7 @@
         query, left, right = (
             short_conv(stream, chans, length, padded_ref.at[index * 3 + stream], taps_ref) for stream in range(3)
         )
-        query_ref[:, chans] = query
+        query_ref[:, chans] = query.astype(BF16)
         gated_ref[:, chans] = left * right
 
     unrolled(channels // TILE, turn)
@@ -166,7 +170,7 @@
     unrolled(channels // TILE, leave)
 
 
-def inside_kernel(gated_ref, skip_ref, rates_ref, residues_ref, lift_ref, base_ref):
+def inside_kernel(gated_ref, skip_ref, rates_ref, coef_ref, lift_ref, base_ref):
     length, channels = gated_ref.shape
     poles, groups = rates_ref.shape
     width = channels // groups
@@ -180,7 +184,7 @@
         chans = tile_of(index)
         shift = groups - index * in_tile
         rates = pltpu.roll(rates_ref[...], shift, 1)
-        coef = pltpu.roll(residues_ref[...], shift, 1) * jnp.sqrt(2.0 * rates) / math.sqrt(poles)
+        coef = pltpu.roll(coef_ref[...], shift, 1)
         impulse, lift = [], []
         for g in range(in_tile):
             rate = jnp.broadcast_to(rates[:, g : g + 1], (poles, length))
@@ -228,7 +232,7 @@
         states = tile_of(index, in_tile * poles)
         lift = lift_ref[:, states]
         carried = dot(lift, high) + dot(lift, low)
-        query = jnp.concatenate([first_ref[:, chans], query_ref[ROWS:, chans]], axis=0)
+        query = jnp.concatenate([first_ref[:, chans], query_ref[:, chans].astype(F32)[ROWS:]], axis=0)
         mixed_ref[:, chans] = (query * (base_ref[:, chans] + carried)).astype(BF16)
 
     unrolled(channels // TILE, tile)
@@ -237,13 +241,11 @@
     other_ref[...] = mixed_ref[:, tile_of(1 - core, share)]
 
 
-def project_kernel(at_ref, own_ref, up_ref, second_ref, down_ref, *rest):
+def project_kernel(at_ref, own_ref, beside_ref, beyond_ref, across_ref, *rest):
     *weight_refs, mine_ref, other_ref, layers_ref = rest
     layer = at_ref[0]
-    layers_ref[layer] = own_ref[...]
-    layers_ref[lax.rem(layer + 3, 4)] = up_ref[...]
-    layers_ref[lax.rem(layer + 2, 4)] = second_ref[...]
-    layers_ref[lax.rem(layer + 1, 4)] = down_ref[...]
+    for bits, ref in enumerate((own_ref, beside_ref, beyond_ref, across_ref)):
+        layers_ref[layer ^ bits] = ref[...]
     length, features = mine_ref.shape
     for column in range(0, features, COLUMNS):
         columns = slice(column, column + COLUMNS)
@@ -265,9 +267,9 @@
     return lax.optimization_barrier((value, earlier))[0]
 
 
-def around(value, steps):
+def trade(value, bits):
     count = lax.axis_size("tp")
-    return lax.ppermute(value, "tp", [(source, (source + steps) % count) for source in range(count)])
+    return lax.ppermute(value, "tp", [(source, source ^ bits) for source in range(count)])
 
 
 def local(streams, conv_weight, rates, residues, skip, out_weight):
@@ -282,19 +284,20 @@
     (tails,) = call(tails_kernel, [((3, ROWS, channels), BF16)], "tails", streams)
     before = from_behind(tails, "ctx", 1)
     if square:
-        near = swap(after(out_weight, tails), 2, 4)
+        near = swap(out_weight, 2, 4)
     tiles = channels // TILE
-    heads, query, gated, decay, step = call(
+    heads, query, gated, decay, step, coef = call(
         prepare_kernel,
         [
             ((3, ROWS, channels), F32),
-            ((length, channels), F32),
+            ((length, channels), BF16),
             ((length, channels), F32),
             ((2, groups * poles, length), BF16),
             ((poles, channels), F32),
+            ((poles, groups), F32),
         ],
         "prepare",
-        streams, conv_weight, rates,
+        streams, conv_weight, rates, residues,
         scratch=[pltpu.VMEM((3 * tiles, ROWS + length, TILE), F32)],
         flops=10**9,
     )
@@ -310,7 +313,7 @@
         inside_kernel,
         [((length, groups * poles), BF16), ((length, channels), F32)],
         "inside",
-        gated, skip, rates, residues,
+        gated, skip, rates, coef,
         flops=10**9,
     )
     if square:
@@ -335,8 +338,8 @@
         other = lax.dynamic_index_in_dim(by_core, 1 - core, 0, keepdims=False)
     block = jnp.concatenate([mine, swap(other, 1)], axis=0)
     layer = lax.axis_index("tp").astype(jnp.int32)
-    up, down = around(block, 1), around(block, -1)
-    second = around(after(up, down), 1)
+    beside, across = trade(block, 1), trade(block, 3)
+    beyond = trade(across, 1)
     if square:
         diagonal = swap(after(near, block), 4, 2)
         weight = (out_weight, near, other_near, diagonal)
@@ -351,7 +354,7 @@
         project_kernel,
         [((length, features), F32), ((length, features), BF16)],
         "project",
-        jnp.stack([layer] + place), block, up, second, down, *weight,
+        jnp.stack([layer] + place), block, beside, beyond, across, *weight,
         specs=smem + whole(4 + len(weight)),
         scratch=[pltpu.VMEM((layers,) + block.shape, BF16)],
         flops=10**9,

time: 60.1 us -> 57.1 us (0.950)
  local copies, waits for them, and re-layouts: 5.35 us -> 2.81 us
  waiting for transfers between devices: 20.9 us -> 18.9 us
  starting transfers between devices: 18.5 us -> 19.9 us
    ppermute x3, waiting for transfers between devices: 19 us -> 13.5 us  [trade(): lax.ppermute(value, 'tp', [(source, source ^ bits) for source in range(co...]
    ppermute x5, waiting for transfers between devices: 1.53 us -> 4.22 us  [swap(): return lax.ppermute(value, 'ctx', pairs)]
    unnamed x21 -> x17, local copies, waits for them, and re-layouts: 5.25 us -> 2.72 us
    ppermute x3, starting transfers between devices: 5.23 us -> 7.75 us  [trade(): lax.ppermute(value, 'tp', [(source, source ^ bits) for source in range(co...]
    ppermute x5, starting transfers between devices: 6.22 us -> 5.14 us  [swap(): return lax.ppermute(value, 'ctx', pairs)]
    all_to_all x1, waiting for transfers between devices: 0.4 us -> 1.2 us  [local(): lax.all_to_all(ends, 'ctx', split_axis=0, concat_axis=0, tiled=True)]
  transfers between devices with their start and end apart: 10 -> 10, of which waited for: 5 -> 7; matrix products, arithmetic and copies ran while one was open for 0% -> 0% of each run, Pallas kernels for 15% -> 17%
where the time goes in v11:
time: 57.1 us; the launch traced here: 56.7 us
  starting transfers between devices  19.9 us (35%)
  waiting for transfers between devices  18.9 us (33%)
  Pallas kernels  14.1 us (25%)
  local copies, waits for them, and re-layouts  2.81 us (5%)
  other arithmetic  0.84 us (1%)
    pallas_call x6, Pallas kernels, call(): pl.pallas_call(kernel, out_shape=tuple((jax.ShapeDtypeStruct(*out) for ou...  14.1 us
    ppermute x3, waiting for transfers between devices, trade(): lax.ppermute(value, 'tp', [(source, source ^ bits) for source in range(co...  13.5 us
    ppermute x3, starting transfers between devices, trade(): lax.ppermute(value, 'tp', [(source, source ^ bits) for source in range(co...  7.75 us
    all_to_all x1, starting transfers between devices, local(): lax.all_to_all(ends, 'ctx', split_axis=0, concat_axis=0, tiled=True)  5.52 us
    ppermute x5, starting transfers between devices, swap(): return lax.ppermute(value, 'ctx', pairs)  5.14 us
    ppermute x5, waiting for transfers between devices, swap(): return lax.ppermute(value, 'ctx', pairs)  4.22 us
    unnamed x17, local copies, waits for them, and re-layouts  2.72 us
    ppermute x1, starting transfers between devices, from_behind(): lax.ppermute(value, axis, [(source, source + steps) for source in range(l...  1.5 us
  transfers between devices with their start and end apart: 10, of which 7 were waited for; matrix products, arithmetic and copies ran while one was open for 0% of the time, Pallas kernels for 17%

profile of v11, /device:TPU:0, one launch (start us, length us, event | category | flops | bytes accessed | tf_op | source)
XLA Modules:
  0.0 56.7 jit_solution(6702201335400534096)
XLA Ops:
  0.0 2.9 %collective-permute-start.1 = (bf16[512,1024]{1,0:T(8,128)(2,1)}, bf16[512,1024]{1,0:T(8,128)(2,1)S(1)}, u32[]{:S(2)}, u32[]{:S(2)}) collective-permute-start(bf16[512,1024]{1,0:T(8,128)(2,1)} %rest_0_.1), channel_id=1, source_target_pairs={{0,8},{4,20},{8,0},{12,28},{16,24},{20,4},{24,16},{28,12},{1,9},{5... | collective-permute-start | bytes 3145736 | tf_op jit(solution)/shard_map/ppermute | solution.py:263
  2.9 1.1 %copy-done.1 = bf16[3,1024,128]{2,1,0:T(8,128)(2,1)S(1)} copy-done((bf16[3,1024,128]{2,1,0:T(8,128)(2,1)S(1)}, bf16[3,1024,128]{2,1,0:T(8,128)(2,1)}, u32[]{:S(2)}) %copy-start.1) | copy-done | bytes 786456
  4.1 0.3 tails.1
  4.4 1.5 %collective-permute-start = (bf16[3,8,1024]{2,1,0:T(8,128)(2,1)S(1)}, bf16[3,8,1024]{2,1,0:T(8,128)(2,1)S(1)}, u32[]{:S(2)}, u32[]{:S(2)}) collective-permute-start(bf16[3,8,1024]{2,1,0:T(8,128)(2,1)S(1)} %tails.1), channel_id=1, source_target_pairs={{0,4},{4,8},{8,12},{12,16},{16,20},{20,24},{24,28},{1,5},{5,9},{9,... | collective-permute-start | bytes 147464 | tf_op jit(solution)/shard_map/ppermute | solution.py:25
  5.9 2.6 %prepare.1 = (f32[3,8,1024]{2,1,0:T(8,128)S(1)}, bf16[128,1024]{1,0:T(8,128)(2,1)S(1)}, f32[128,1024]{1,0:T(8,128)S(1)}, bf16[2,2048,128]{2,1,0:T(8,128)(2,1)S(1...) custom-call(bf16[3,1024,128]{2,1,0:T(8,128)(2,1)S(1)} %copy-done.1, f32[3,7,1024]{2,1,0:T(8,128)S(1)} %copy-done.4, ...), custom_call_target="tpu_custom_call" | custom-call | flops 1000000000 | bytes 10000000 | tf_op jit(solution)/shard_map/prepare/pallas_call | solution.py:54
  8.6 1.5 %states.1 = (bf16[8,16,1024]{2,1,0:T(8,128)(2,1)}, bf16[128,1024]{1,0:T(8,128)(2,1)S(1)}, f32[8,1024]{1,0:T(8,128)S(1)}) custom-call(bf16[3,8,1024]{2,1,0:T(8,128)(2,1)S(1)} %collective-permute-done.before_ref, f32[3,8,1024]{2,1,0:T(8,128)S(1)} %get-tuple-element.24.heads_ref, f32[3,7,1024]{2,1,0:T(8,128)S(1)} %copy-done.4, ...), custom_call_target="tpu_custom_call" | custom-call | flops 100000000 | bytes 1000000 | tf_op jit(solution)/shard_map/states/pallas_call | solution.py:54
  10.1 5.5 %all-to-all-start = ((bf16[8,16,1024]{2,1,0:T(8,128)(2,1)}), bf16[8,16,1024]{2,1,0:T(8,128)(2,1)S(1)}, u32[]{:S(2)}, u32[]{:S(2)}) async-start(bf16[8,16,1024]{2,1,0:T(8,128)(2,1)} %get-tuple-element.27), calls=%async_computation | async-start | bytes 524288 | tf_op jit(solution)/shard_map/all_to_all | solution.py:311
  15.6 0.1 pad_add_fusion.at_ref
  15.7 0.6 %copy-done.7 = f32[1024]{0:T(1024)S(1)} copy-done((f32[1024]{0:T(1024)S(1)}, f32[1024]{0:T(1024)}, u32[]{:S(2)}) %copy-start.7) | copy-done | bytes 4120
  16.3 5.0 %inside.1 = (bf16[128,2048]{1,0:T(8,128)(2,1)S(1)}, f32[128,1024]{1,0:T(8,128)S(1)}) custom-call(bf16[128,1024]{1,0:T(8,128)(2,1)S(1)} %get-tuple-element.29.gated_ref, f32[1,1024]{1,0:T(1,128)S(1)} %bitcast.13, f32[16,128]{1,0:T(8,128)S(1)} %bitcast.12, f32[16,128]{1,0:T(8,128)S(1)} %get-tuple-element.30.coef_ref), custom_call_target="tpu_custom_call" | custom-call | flops 1000000000 | bytes 10000000 | tf_op jit(solution)/shard_map/inside/pallas_call | solution.py:54
  21.3 0.0 copy-start
  21.3 0.0 collective-permute-done.1.rest_1_
  21.3 1.2 %all-to-all-done.ends_ref = bf16[8,16,1024]{2,1,0:T(8,128)(2,1)S(1)} async-done(((bf16[8,16,1024]{2,1,0:T(8,128)(2,1)}), bf16[8,16,1024]{2,1,0:T(8,128)(2,1)S(1)}, u32[]{:S(2)}, u32[]{:S(2)}) %all-to-all-start) | async-done | bytes 262176 | tf_op jit(solution)/shard_map/all_to_all | solution.py:311
  22.5 0.9 %copy-done.3 = bf16[128,1024]{1,0:T(8,128)(2,1)S(1)} copy-done((bf16[128,1024]{1,0:T(8,128)(2,1)S(1)}, bf16[128,1024]{1,0:T(8,128)(2,1)}, u32[]{:S(2)}) %copy-start.3) | copy-done | bytes 262168
  23.5 1.9 %finish.1 = (bf16[128,512]{1,0:T(8,128)(2,1)S(1)}, bf16[128,512]{1,0:T(8,128)(2,1)S(1)}, bf16[128,1024]{1,0:T(8,128)(2,1)}) custom-call(s32[2]{0:T(128)S(1)} %pad_add_fusion.at_ref, bf16[8,16,1024]{2,1,0:T(8,128)(2,1)S(1)} %all-to-all-done.ends_ref, f32[16,1024]{1,0:T(8,128)S(1)} %get-tuple-element.28.step_ref, ...), custom_call_target="tpu_custom_call" | custom-call | flops 100000000 | bytes 1000000 | tf_op jit(solution)/shard_map/finish/pallas_call | solution.py:54
  25.4 0.0 collective-permute-start.2
  25.4 1.1 %collective-permute-start.6 = (bf16[512,1024]{1,0:T(8,128)(2,1)S(1)}, bf16[512,1024]{1,0:T(8,128)(2,1)S(1)}, u32[]{:S(2)}, u32[]{:S(2)}) collective-permute-start(bf16[512,1024]{1,0:T(8,128)(2,1)S(1)} %copy-done), channel_id=1, source_target_pairs={{0,16},{4,12},{8,24},{12,4},{16,0},{20,28},{24,8},{28,20},{1,17},{... | collective-permute-start | bytes 3145736 | tf_op jit(solution)/shard_map/ppermute | solution.py:263
  26.5 0.3 collective-permute-done.2
  26.8 1.1 %collective-permute-start.7 = (bf16[512,1024]{1,0:T(8,128)(2,1)S(1)}, bf16[512,1024]{1,0:T(8,128)(2,1)}, u32[]{:S(2)}, u32[]{:S(2)}) collective-permute-start(bf16[512,1024]{1,0:T(8,128)(2,1)S(1)} %collective-permute-done.1.rest_1_), channel_id=1, source_target_pairs={{0,16},{4,12},{8,24},{12,4},{16,0},{20,28},{24,8},{28,20},{1,17},{... | collective-permute-start | bytes 3145736 | tf_op jit(solution)/shard_map/ppermute | solution.py:263
  27.9 3.6 %collective-permute-start.4 = (bf16[256,512]{1,0:T(8,128)(2,1)S(1)}, bf16[256,512]{1,0:T(8,128)(2,1)}, u32[]{:S(2)}, u32[]{:S(2)}) collective-permute-start(bf16[256,512]{1,0:T(8,128)(2,1)S(1)} %constant_dynamic-update-slice_fusion.own_ref), channel_id=1, source_target_pairs={{0,3},{1,2},{2,1},{3,0},{4,7},{5,6},{6,5},{7,4},{8,11},{9,10},{10,... | collective-permute-start | bytes 786440 | tf_op jit(solution)/shard_map/ppermute | solution.py:272
  31.5 0.0 collective-permute-start.3
  31.5 7.5 %collective-permute-done.4.across_ref = bf16[256,512]{1,0:T(8,128)(2,1)} collective-permute-done((bf16[256,512]{1,0:T(8,128)(2,1)S(1)}, bf16[256,512]{1,0:T(8,128)(2,1)}, u32[]{:S(2)}, u32[]{:S(2)}) %collective-permute-start.4) | collective-permute-done | bytes 262176 | tf_op jit(solution)/shard_map/ppermute | solution.py:272
  39.0 4.1 %collective-permute-start.5 = (bf16[256,512]{1,0:T(8,128)(2,1)}, bf16[256,512]{1,0:T(8,128)(2,1)}, u32[]{:S(2)}, u32[]{:S(2)}) collective-permute-start(bf16[256,512]{1,0:T(8,128)(2,1)} %collective-permute-done.4.across_ref), channel_id=1, source_target_pairs={{0,1},{1,0},{2,3},{3,2},{4,5},{5,4},{6,7},{7,6},{8,9},{9,8},{10,11... | collective-permute-start | bytes 786440 | tf_op jit(solution)/shard_map/ppermute | solution.py:272
  43.1 0.1 stack.32.at_ref
  43.2 0.3 collective-permute-done.3.beside_ref
  43.5 5.6 %collective-permute-done.5.beyond_ref = bf16[256,512]{1,0:T(8,128)(2,1)} collective-permute-done((bf16[256,512]{1,0:T(8,128)(2,1)}, bf16[256,512]{1,0:T(8,128)(2,1)}, u32[]{:S(2)}, u32[]{:S(2)}) %collective-permute-start.5) | collective-permute-done | bytes 262176 | tf_op jit(solution)/shard_map/ppermute | solution.py:272
  49.1 0.0 collective-permute-done.6.rest_2_
  49.1 2.4 %collective-permute-done.7.rest_3_ = bf16[512,1024]{1,0:T(8,128)(2,1)} collective-permute-done((bf16[512,1024]{1,0:T(8,128)(2,1)S(1)}, bf16[512,1024]{1,0:T(8,128)(2,1)}, u32[]{:S(2)}, u32[]{:S(2)}) %collective-permute-start.7) | collective-permute-done | bytes 1048608 | tf_op jit(solution)/shard_map/ppermute | solution.py:263
  51.6 2.8 %project.1 = (f32[128,1024]{1,0:T(8,128)S(1)}, bf16[128,1024]{1,0:T(8,128)(2,1)S(1)}) custom-call(s32[5]{0:T(128)S(1)} %stack.32.at_ref, bf16[256,512]{1,0:T(8,128)(2,1)S(1)} %constant_dynamic-update-slice_fusion.own_ref, bf16[256,512]{1,0:T(8,128)(2,1)} %collective-permute-done.3.beside_ref, bf16[256,512]{1,0:T(8,128)(2,1)} %collective-permute-done.5.beyond_ref, ...), custom_call_target="tpu_custom_call" | custom-call | flops 1000000000 | bytes 10000000 | tf_op jit(solution)/shard_map/project/pallas_call | solution.py:54
  54.4 0.1 collective-permute-start.8
  54.4 1.5 %collective-permute-done.8 = bf16[128,1024]{1,0:T(8,128)(2,1)S(1)} collective-permute-done((bf16[128,1024]{1,0:T(8,128)(2,1)S(1)}, bf16[128,1024]{1,0:T(8,128)(2,1)S(1)}, u32[]{:S(2)}, u32[]{:S(2)}) %collective-permute-start.8) | collective-permute-done | bytes 262176 | tf_op jit(solution)/shard_map/ppermute | solution.py:263
  56.0 0.8 %add_convert_fusion = bf16[128,1024]{1,0:T(8,128)(2,1)} fusion(f32[128,1024]{1,0:T(8,128)S(1)} %get-tuple-element.41, bf16[128,1024]{1,0:T(8,128)(2,1)S(1)} %collective-permute-done.8), kind=kLoop, calls=%fused_computation | loop fusion | flops 393216 | bytes 1048576 | tf_op jit(solution)/shard_map/convert_element_type | solution.py:363
  (15 shorter events, 0.0 us)
Async XLA Ops:
  0.0 21.3 %collective-permute-start.1 = (bf16[512,1024]{1,0:T(8,128)(2,1)}, bf16[512,1024]{1,0:T(8,128)(2,1)S(1)}, u32[]{:S(2)}, u32[]{:S(2)}) collective-permute-start(bf16[512,1024]{1,0:T(8,128)(2,1)} %rest_0_.1), channel_id=1, source_target_pairs={{0,8},{4,20},{8,0},{12,28},{16,24},{20,4},{24,16},{28,12},{1,9},{5... | collective-permute-start | bytes 3145736 | tf_op jit(solution)/shard_map/ppermute | solution.py:263
  2.9 1.1 %copy-start.1 = (bf16[3,1024,128]{2,1,0:T(8,128)(2,1)S(1)}, bf16[3,1024,128]{2,1,0:T(8,128)(2,1)}, u32[]{:S(2)}) copy-start(bf16[3,1024,128]{2,1,0:T(8,128)(2,1)} %streams_ref.3) | copy-start | bytes 2359300
  4.1 1.8 %copy-start.4 = (f32[3,7,1024]{2,1,0:T(8,128)S(1)}, f32[3,7,1024]{2,1,0:T(8,128)}, u32[]{:S(2)}) copy-start(f32[3,7,1024]{2,1,0:T(8,128)} %taps_ref.3) | copy-start | bytes 258052
  4.1 1.8 %copy-start.5 = (f32[128,16]{0,1:T(8,128)S(1)}, f32[128,16]{0,1:T(8,128)}, u32[]{:S(2)}) copy-start(f32[128,16]{0,1:T(8,128)} %param.9) | copy-start | bytes 24580
  4.1 1.8 %copy-start.6 = (f32[128,16]{0,1:T(8,128)S(1)}, f32[128,16]{0,1:T(8,128)}, u32[]{:S(2)}) copy-start(f32[128,16]{0,1:T(8,128)} %param.8) | copy-start | bytes 24580
  4.4 4.2 %collective-permute-start = (bf16[3,8,1024]{2,1,0:T(8,128)(2,1)S(1)}, bf16[3,8,1024]{2,1,0:T(8,128)(2,1)S(1)}, u32[]{:S(2)}, u32[]{:S(2)}) collective-permute-start(bf16[3,8,1024]{2,1,0:T(8,128)(2,1)S(1)} %tails.1), channel_id=1, source_target_pairs={{0,4},{4,8},{8,12},{12,16},{16,20},{20,24},{24,28},{1,5},{5,9},{9,... | collective-permute-start | bytes 147464 | tf_op jit(solution)/shard_map/ppermute | solution.py:25
  8.5 1.5 %copy-start.2 = (bf16[128,1024]{1,0:T(8,128)(2,1)}, bf16[128,1024]{1,0:T(8,128)(2,1)S(1)}, u32[]{:S(2)}) copy-start(bf16[128,1024]{1,0:T(8,128)(2,1)S(1)} %get-tuple-element.32.query_ref) | copy-start | bytes 786436
  10.1 12.5 %all-to-all-start = ((bf16[8,16,1024]{2,1,0:T(8,128)(2,1)}), bf16[8,16,1024]{2,1,0:T(8,128)(2,1)S(1)}, u32[]{:S(2)}, u32[]{:S(2)}) async-start(bf16[8,16,1024]{2,1,0:T(8,128)(2,1)} %get-tuple-element.27), calls=%async_computation | async-start | bytes 524288 | tf_op jit(solution)/shard_map/all_to_all | solution.py:311
  15.6 0.7 %copy-start.7 = (f32[1024]{0:T(1024)S(1)}, f32[1024]{0:T(1024)}, u32[]{:S(2)}) copy-start(f32[1024]{0:T(1024)} %param.10) | copy-start | bytes 12292
  21.3 4.1 %copy-start = (bf16[512,1024]{1,0:T(8,128)(2,1)S(1)}, bf16[512,1024]{1,0:T(8,128)(2,1)}, u32[]{:S(2)}) copy-start(bf16[512,1024]{1,0:T(8,128)(2,1)} %rest_0_.1) | copy-start | bytes 3145732
  22.5 1.0 %copy-start.3 = (bf16[128,1024]{1,0:T(8,128)(2,1)S(1)}, bf16[128,1024]{1,0:T(8,128)(2,1)}, u32[]{:S(2)}) copy-start(bf16[128,1024]{1,0:T(8,128)(2,1)} %copy-done.2) | copy-start | bytes 786436
  25.4 1.3 %collective-permute-start.2 = (bf16[128,512]{1,0:T(8,128)(2,1)S(1)}, bf16[128,512]{1,0:T(8,128)(2,1)S(1)}, u32[]{:S(2)}, u32[]{:S(2)}) collective-permute-start(bf16[128,512]{1,0:T(8,128)(2,1)S(1)} %get-tuple-element.37), channel_id=1, source_target_pairs={{0,4},{4,0},{8,12},{12,8},{16,20},{20,16},{24,28},{28,24},{1,5},{5... | collective-permute-start | bytes 393224 | tf_op jit(solution)/shard_map/ppermute | solution.py:263
  25.4 23.7 %collective-permute-start.6 = (bf16[512,1024]{1,0:T(8,128)(2,1)S(1)}, bf16[512,1024]{1,0:T(8,128)(2,1)S(1)}, u32[]{:S(2)}, u32[]{:S(2)}) collective-permute-start(bf16[512,1024]{1,0:T(8,128)(2,1)S(1)} %copy-done), channel_id=1, source_target_pairs={{0,16},{4,12},{8,24},{12,4},{16,0},{20,28},{24,8},{28,20},{1,17},{... | collective-permute-start | bytes 3145736 | tf_op jit(solution)/shard_map/ppermute | solution.py:263
  26.8 24.8 %collective-permute-start.7 = (bf16[512,1024]{1,0:T(8,128)(2,1)S(1)}, bf16[512,1024]{1,0:T(8,128)(2,1)}, u32[]{:S(2)}, u32[]{:S(2)}) collective-permute-start(bf16[512,1024]{1,0:T(8,128)(2,1)S(1)} %collective-permute-done.1.rest_1_), channel_id=1, source_target_pairs={{0,16},{4,12},{8,24},{12,4},{16,0},{20,28},{24,8},{28,20},{1,17},{... | collective-permute-start | bytes 3145736 | tf_op jit(solution)/shard_map/ppermute | solution.py:263
  27.9 11.1 %collective-permute-start.4 = (bf16[256,512]{1,0:T(8,128)(2,1)S(1)}, bf16[256,512]{1,0:T(8,128)(2,1)}, u32[]{:S(2)}, u32[]{:S(2)}) collective-permute-start(bf16[256,512]{1,0:T(8,128)(2,1)S(1)} %constant_dynamic-update-slice_fusion.own_ref), channel_id=1, source_target_pairs={{0,3},{1,2},{2,1},{3,0},{4,7},{5,6},{6,5},{7,4},{8,11},{9,10},{10,... | collective-permute-start | bytes 786440 | tf_op jit(solution)/shard_map/ppermute | solution.py:272
  31.5 12.1 %collective-permute-start.3 = (bf16[256,512]{1,0:T(8,128)(2,1)S(1)}, bf16[256,512]{1,0:T(8,128)(2,1)}, u32[]{:S(2)}, u32[]{:S(2)}) collective-permute-start(bf16[256,512]{1,0:T(8,128)(2,1)S(1)} %constant_dynamic-update-slice_fusion.own_ref), channel_id=1, source_target_pairs={{0,1},{1,0},{2,3},{3,2},{4,5},{5,4},{6,7},{7,6},{8,9},{9,8},{10,11... | collective-permute-start | bytes 786440 | tf_op jit(solution)/shard_map/ppermute | solution.py:272
  39.0 10.1 %collective-permute-start.5 = (bf16[256,512]{1,0:T(8,128)(2,1)}, bf16[256,512]{1,0:T(8,128)(2,1)}, u32[]{:S(2)}, u32[]{:S(2)}) collective-permute-start(bf16[256,512]{1,0:T(8,128)(2,1)} %collective-permute-done.4.across_ref), channel_id=1, source_target_pairs={{0,1},{1,0},{2,3},{3,2},{4,5},{5,4},{6,7},{7,6},{8,9},{9,8},{10,11... | collective-permute-start | bytes 786440 | tf_op jit(solution)/shard_map/ppermute | solution.py:272
  54.4 1.6 %collective-permute-start.8 = (bf16[128,1024]{1,0:T(8,128)(2,1)S(1)}, bf16[128,1024]{1,0:T(8,128)(2,1)S(1)}, u32[]{:S(2)}, u32[]{:S(2)}) collective-permute-start(bf16[128,1024]{1,0:T(8,128)(2,1)S(1)} %get-tuple-element.42), channel_id=1, source_target_pairs={{0,4},{4,0},{8,12},{12,8},{16,20},{20,16},{24,28},{28,24},{1,5},{5... | collective-permute-start | bytes 786440 | tf_op jit(solution)/shard_map/ppermute | solution.py:263

commit v12 on v11

--- a/solution.py
+++ b/solution.py
@@ -92,8 +92,8 @@
 
 
 def prepare_kernel(
-    streams_ref, taps_ref, rates_ref, residues_ref,
-    heads_ref, query_ref, gated_ref, decay_ref, step_ref, coef_ref, padded_ref,
+    streams_ref, taps_ref, rates_ref, residues_ref, skip_ref,
+    heads_ref, query_ref, gated_ref, decay_ref, step_ref, coef_ref, direct_ref, padded_ref,
 ):
     channels, length = streams_ref.shape[1:]
     poles, groups = rates_ref.shape
@@ -103,6 +103,7 @@
     lag = (length - 1) - iota((poles, length), 1).astype(F32)
     owner = iota((poles, TILE), 1) // width
     coef_ref[...] = residues_ref[...] * jnp.sqrt(2.0 * rates_ref[...]) / math.sqrt(poles)
+    direct_ref[...] = skip_ref[...]
 
     def turn(index):
         chans = tile_of(index)
@@ -242,16 +243,23 @@
 
 
 def project_kernel(at_ref, own_ref, beside_ref, beyond_ref, across_ref, *rest):
-    *weight_refs, mine_ref, other_ref, layers_ref = rest
+    *weight_hbms, mine_ref, other_ref, layers_ref, weight_ref, sems = rest
+    copies = [
+        pltpu.make_async_copy(hbm, weight_ref.at[at], sems.at[at]) for at, hbm in enumerate(weight_hbms)
+    ]
+    for copy in copies:
+        copy.start()
     layer = at_ref[0]
     for bits, ref in enumerate((own_ref, beside_ref, beyond_ref, across_ref)):
         layers_ref[layer ^ bits] = ref[...]
+    for copy in copies:
+        copy.wait()
     length, features = mine_ref.shape
     for column in range(0, features, COLUMNS):
         columns = slice(column, column + COLUMNS)
         total = None
-        for at, ref in enumerate(weight_refs):
-            term = dot(layers_ref[at_ref[1 + at]], ref[:, columns])
+        for at in range(len(copies)):
+            term = dot(layers_ref[at_ref[1 + at]], weight_ref[at, :, columns])
             total = term if total is None else total + term
         mine_ref[:, columns] = total[:length]
         other_ref[:, columns] = total[length:].astype(BF16)
@@ -286,7 +294,7 @@
     if square:
         near = swap(out_weight, 2, 4)
     tiles = channels // TILE
-    heads, query, gated, decay, step, coef = call(
+    heads, query, gated, decay, step, coef, skip = call(
         prepare_kernel,
         [
             ((3, ROWS, channels), F32),
@@ -295,9 +303,10 @@
             ((2, groups * poles, length), BF16),
             ((poles, channels), F32),
             ((poles, groups), F32),
+            ((1, channels), F32),
         ],
         "prepare",
-        streams, conv_weight, rates, residues,
+        streams, conv_weight, rates, residues, skip,
         scratch=[pltpu.VMEM((3 * tiles, ROWS + length, TILE), F32)],
         flops=10**9,
     )
@@ -317,8 +326,7 @@
         flops=10**9,
     )
     if square:
-        base, near = lax.optimization_barrier((base, near))
-        other_near = swap(after(out_weight, base), 4, 2)
+        other_near = swap(after(out_weight, gated), 4, 2)
     me = lax.axis_index("ctx").astype(jnp.int32)
     core = me % CORES
     smem = [pl.BlockSpec(memory_space=pltpu.SMEM)]
@@ -339,7 +347,7 @@
     block = jnp.concatenate([mine, swap(other, 1)], axis=0)
     layer = lax.axis_index("tp").astype(jnp.int32)
     beside, across = trade(block, 1), trade(block, 3)
-    beyond = trade(across, 1)
+    beyond = trade(after(across, other_near) if square else across, 1)
     if square:
         diagonal = swap(after(near, block), 4, 2)
         weight = (out_weight, near, other_near, diagonal)
@@ -354,9 +362,13 @@
         project_kernel,
         [((length, features), F32), ((length, features), BF16)],
         "project",
-        jnp.stack([layer] + place), block, beside, beyond, across, *weight,
-        specs=smem + whole(4 + len(weight)),
-        scratch=[pltpu.VMEM((layers,) + block.shape, BF16)],
+        jnp.stack([layer] + place), block, beside, beyond, across, *(pltpu.with_memory_space_constraint(part, pltpu.HBM) for part in weight),
+        specs=smem + whole(4) + [pl.BlockSpec(memory_space=pltpu.HBM)] * len(weight),
+        scratch=[
+            pltpu.VMEM((layers,) + block.shape, BF16),
+            pltpu.VMEM((layers, share, features), BF16),
+            pltpu.SemaphoreType.DMA((layers,)),
+        ],
         flops=10**9,
     )
     other = swap(other, 1)

time: 57.1 us -> 55.8 us (0.977)
  waiting for transfers between devices: 18.9 us -> 16.5 us
  local copies, waits for them, and re-layouts: 2.81 us -> 1.26 us
  starting transfers between devices: 19.9 us -> 21.4 us
  Pallas kernels: 14.1 us -> 15.4 us
    unnamed x17 -> x13, local copies, waits for them, and re-layouts: 2.72 us -> 1.16 us
    ppermute x5, waiting for transfers between devices: 4.22 us -> 2.86 us  [swap(): return lax.ppermute(value, 'ctx', pairs)]
    pallas_call x6, Pallas kernels: 14.1 us -> 15.4 us  [call(): pl.pallas_call(kernel, out_shape=tuple((jax.ShapeDtypeStruct(*out) for ou...]
    all_to_all x1, waiting for transfers between devices: 1.2 us -> 0.19 us  [local(): lax.all_to_all(ends, 'ctx', split_axis=0, concat_axis=0, tiled=True)]
    ppermute x5, starting transfers between devices: 5.14 us -> 5.9 us  [swap(): return lax.ppermute(value, 'ctx', pairs)]
    ppermute x3, starting transfers between devices: 7.75 us -> 8.37 us  [trade(): lax.ppermute(value, 'tp', [(source, source ^ bits) for source in range(co...]
  transfers between devices with their start and end apart: 10 -> 10, of which waited for: 7 -> 6; matrix products, arithmetic and copies ran while one was open for 0% -> 0% of each run, Pallas kernels for 17% -> 21%
where the time goes in v12:
time: 55.8 us; the launch traced here: 55.5 us
  starting transfers between devices  21.4 us (38%)
  waiting for transfers between devices  16.5 us (30%)
  Pallas kernels  15.4 us (28%)
  local copies, waits for them, and re-layouts  1.26 us (2%)
  other arithmetic  0.84 us (2%)
    pallas_call x6, Pallas kernels, call(): pl.pallas_call(kernel, out_shape=tuple((jax.ShapeDtypeStruct(*out) for ou...  15.4 us
    ppermute x3, waiting for transfers between devices, trade(): lax.ppermute(value, 'tp', [(source, source ^ bits) for source in range(co...  13.4 us
    ppermute x3, starting transfers between devices, trade(): lax.ppermute(value, 'tp', [(source, source ^ bits) for source in range(co...  8.37 us
    ppermute x5, starting transfers between devices, swap(): return lax.ppermute(value, 'ctx', pairs)  5.9 us
    all_to_all x1, starting transfers between devices, local(): lax.all_to_all(ends, 'ctx', split_axis=0, concat_axis=0, tiled=True)  5.51 us
    ppermute x5, waiting for transfers between devices, swap(): return lax.ppermute(value, 'ctx', pairs)  2.86 us
    ppermute x1, starting transfers between devices, from_behind(): lax.ppermute(value, axis, [(source, source + steps) for source in range(l...  1.63 us
    unnamed x13, local copies, waits for them, and re-layouts  1.16 us
  transfers between devices with their start and end apart: 10, of which 6 were waited for; matrix products, arithmetic and copies ran while one was open for 0% of the time, Pallas kernels for 21%

profile of v12, /device:TPU:0, one launch (start us, length us, event | category | flops | bytes accessed | tf_op | source)
XLA Modules:
  0.0 55.5 jit_solution(7200362306744140742)
XLA Ops:
  0.0 2.9 %collective-permute-start.6 = (bf16[512,1024]{1,0:T(8,128)(2,1)}, bf16[512,1024]{1,0:T(8,128)(2,1)}, u32[]{:S(2)}, u32[]{:S(2)}) collective-permute-start(bf16[512,1024]{1,0:T(8,128)(2,1)} %rest_0_.1), channel_id=1, source_target_pairs={{0,8},{4,20},{8,0},{12,28},{16,24},{20,4},{24,16},{28,12},{1,9},{5... | collective-permute-start | bytes 3145736 | tf_op jit(solution)/shard_map/ppermute | solution.py:271
  2.9 1.1 %copy-done = bf16[3,1024,128]{2,1,0:T(8,128)(2,1)S(1)} copy-done((bf16[3,1024,128]{2,1,0:T(8,128)(2,1)S(1)}, bf16[3,1024,128]{2,1,0:T(8,128)(2,1)}, u32[]{:S(2)}) %copy-start) | copy-done | bytes 786456
  4.1 0.3 tails.1
  4.4 1.6 %collective-permute-start = (bf16[3,8,1024]{2,1,0:T(8,128)(2,1)S(1)}, bf16[3,8,1024]{2,1,0:T(8,128)(2,1)S(1)}, u32[]{:S(2)}, u32[]{:S(2)}) collective-permute-start(bf16[3,8,1024]{2,1,0:T(8,128)(2,1)S(1)} %tails.1), channel_id=1, source_target_pairs={{0,4},{4,8},{8,12},{12,16},{16,20},{20,24},{24,28},{1,5},{5,9},{9,... | collective-permute-start | bytes 147464 | tf_op jit(solution)/shard_map/ppermute | solution.py:25
  6.1 2.6 %prepare.1 = (f32[3,8,1024]{2,1,0:T(8,128)S(1)}, bf16[128,1024]{1,0:T(8,128)(2,1)S(1)}, f32[128,1024]{1,0:T(8,128)S(1)}, bf16[2,2048,128]{2,1,0:T(8,128)(2,1)S(1...) custom-call(bf16[3,1024,128]{2,1,0:T(8,128)(2,1)S(1)} %copy-done, ...), custom_call_target="tpu_custom_call" | custom-call | flops 1000000000 | bytes 10000000 | tf_op jit(solution)/shard_map/prepare/pallas_call | solution.py:54
  8.7 0.0 collective-permute-done.before_ref
  8.7 0.0 copy-start.5
  8.7 1.5 %states.1 = (bf16[8,16,1024]{2,1,0:T(8,128)(2,1)}, bf16[128,1024]{1,0:T(8,128)(2,1)S(1)}, f32[8,1024]{1,0:T(8,128)S(1)}) custom-call(bf16[3,8,1024]{2,1,0:T(8,128)(2,1)S(1)} %collective-permute-done.before_ref, f32[3,8,1024]{2,1,0:T(8,128)S(1)} %get-tuple-element.24.heads_ref, f32[3,7,1024]{2,1,0:T(8,128)S(1)} %copy-done.1, ...), custom_call_target="tpu_custom_call" | custom-call | flops 100000000 | bytes 1000000 | tf_op jit(solution)/shard_map/states/pallas_call | solution.py:54
  10.2 5.5 %all-to-all-start = ((bf16[8,16,1024]{2,1,0:T(8,128)(2,1)}), bf16[8,16,1024]{2,1,0:T(8,128)(2,1)S(1)}, u32[]{:S(2)}, u32[]{:S(2)}) async-start(bf16[8,16,1024]{2,1,0:T(8,128)(2,1)} %get-tuple-element.27), calls=%async_computation | async-start | bytes 524288 | tf_op jit(solution)/shard_map/all_to_all | solution.py:320
  15.7 0.1 pad_add_fusion.at_ref
  15.8 0.0 copy-done.5
  15.8 2.1 %collective-permute-start.4 = (bf16[512,1024]{1,0:T(8,128)(2,1)S(1)}, bf16[512,1024]{1,0:T(8,128)(2,1)}, u32[]{:S(2)}, u32[]{:S(2)}) collective-permute-start(bf16[512,1024]{1,0:T(8,128)(2,1)S(1)} %copy-done.5), channel_id=1, source_target_pairs={{0,16},{4,12},{8,24},{12,4},{16,0},{20,28},{24,8},{28,20},{1,17},{... | collective-permute-start | bytes 3145736 | tf_op jit(solution)/shard_map/ppermute | solution.py:271
  17.9 5.0 %inside.1 = (bf16[128,2048]{1,0:T(8,128)(2,1)S(1)}, f32[128,1024]{1,0:T(8,128)S(1)}) custom-call(bf16[128,1024]{1,0:T(8,128)(2,1)S(1)} %get-tuple-element.29.gated_ref, f32[1,1024]{1,0:T(1,128)S(1)} %get-tuple-element.30.skip_ref, f32[16,128]{1,0:T(8,128)S(1)} %bitcast.12, f32[16,128]{1,0:T(8,128)S(1)} %get-tuple-element.31.coef_ref), custom_call_target="tpu_custom_call" | custom-call | flops 1000000000 | bytes 10000000 | tf_op jit(solution)/shard_map/inside/pallas_call | solution.py:54
  22.9 0.2 all-to-all-done.ends_ref
  23.1 1.9 %finish.1 = (bf16[128,512]{1,0:T(8,128)(2,1)S(1)}, bf16[128,512]{1,0:T(8,128)(2,1)S(1)}, bf16[128,1024]{1,0:T(8,128)(2,1)}) custom-call(s32[2]{0:T(128)S(1)} %pad_add_fusion.at_ref, bf16[8,16,1024]{2,1,0:T(8,128)(2,1)S(1)} %all-to-all-done.ends_ref, f32[16,1024]{1,0:T(8,128)S(1)} %get-tuple-element.28.step_ref, ...), custom_call_target="tpu_custom_call" | custom-call | flops 100000000 | bytes 1000000 | tf_op jit(solution)/shard_map/finish/pallas_call | solution.py:54
  25.1 0.0 collective-permute-start.1
  25.1 1.3 %collective-permute-done.1 = bf16[128,512]{1,0:T(8,128)(2,1)S(1)} collective-permute-done((bf16[128,512]{1,0:T(8,128)(2,1)S(1)}, bf16[128,512]{1,0:T(8,128)(2,1)S(1)}, u32[]{:S(2)}, u32[]{:S(2)}) %collective-permute-start.1) | collective-permute-done | bytes 131104 | tf_op jit(solution)/shard_map/ppermute | solution.py:271
  26.4 0.0 collective-permute-done.6.rest_1_
  26.5 0.8 %collective-permute-start.7 = (bf16[512,1024]{1,0:T(8,128)(2,1)}, bf16[512,1024]{1,0:T(8,128)(2,1)}, u32[]{:S(2)}, u32[]{:S(2)}) collective-permute-start(bf16[512,1024]{1,0:T(8,128)(2,1)} %collective-permute-done.6.rest_1_), channel_id=1, source_target_pairs={{0,16},{4,12},{8,24},{12,4},{16,0},{20,28},{24,8},{28,20},{1,17},{... | collective-permute-start | bytes 3145736 | tf_op jit(solution)/shard_map/ppermute | solution.py:271
  27.2 3.6 %collective-permute-start.3 = (bf16[256,512]{1,0:T(8,128)(2,1)S(1)}, bf16[256,512]{1,0:T(8,128)(2,1)S(1)}, u32[]{:S(2)}, u32[]{:S(2)}) collective-permute-start(bf16[256,512]{1,0:T(8,128)(2,1)S(1)} %constant_dynamic-update-slice_fusion.own_ref), channel_id=1, source_target_pairs={{0,3},{1,2},{2,1},{3,0},{4,7},{5,6},{6,5},{7,4},{8,11},{9,10},{10,... | collective-permute-start | bytes 786440 | tf_op jit(solution)/shard_map/ppermute | solution.py:280
  30.8 0.0 collective-permute-start.2
  30.8 7.4 %collective-permute-done.3.across_ref = bf16[256,512]{1,0:T(8,128)(2,1)S(1)} collective-permute-done((bf16[256,512]{1,0:T(8,128)(2,1)S(1)}, bf16[256,512]{1,0:T(8,128)(2,1)S(1)}, u32[]{:S(2)}, u32[]{:S(2)}) %collective-permute-start.3) | collective-permute-done | bytes 262176 | tf_op jit(solution)/shard_map/ppermute | solution.py:280
  38.2 0.0 collective-permute-done.4.rest_2_
  38.2 4.8 %collective-permute-start.5 = (bf16[256,512]{1,0:T(8,128)(2,1)S(1)}, bf16[256,512]{1,0:T(8,128)(2,1)S(1)}, u32[]{:S(2)}, u32[]{:S(2)}) collective-permute-start(bf16[256,512]{1,0:T(8,128)(2,1)S(1)} %collective-permute-done.3.across_ref), channel_id=1, source_target_pairs={{0,1},{1,0},{2,3},{3,2},{4,5},{5,4},{6,7},{7,6},{8,9},{9,8},{10,11... | collective-permute-start | bytes 786440 | tf_op jit(solution)/shard_map/ppermute | solution.py:280
  43.0 0.1 stack.32.at_ref
  43.1 0.3 collective-permute-done.2.beside_ref
  43.4 5.7 %collective-permute-done.5.beyond_ref = bf16[256,512]{1,0:T(8,128)(2,1)S(1)} collective-permute-done((bf16[256,512]{1,0:T(8,128)(2,1)S(1)}, bf16[256,512]{1,0:T(8,128)(2,1)S(1)}, u32[]{:S(2)}, u32[]{:S(2)}) %collective-permute-start.5) | collective-permute-done | bytes 262176 | tf_op jit(solution)/shard_map/ppermute | solution.py:280
  49.1 0.0 collective-permute-done.7.rest_3_
  49.1 4.0 %project.1 = (f32[128,1024]{1,0:T(8,128)S(1)}, bf16[128,1024]{1,0:T(8,128)(2,1)S(1)}) custom-call(s32[5]{0:T(128)S(1)} %stack.32.at_ref, bf16[256,512]{1,0:T(8,128)(2,1)S(1)} %constant_dynamic-update-slice_fusion.own_ref, bf16[256,512]{1,0:T(8,128)(2,1)S(1)} %collective-permute-done.2.beside_ref, bf16[256,512]{1,0:T(8,128)(2,1)S(1)} %collective-permute-done.5.beyond_ref, ...), custom_call_target="tpu_custom_call" | custom-call | flops 1000000000 | bytes 10000000 | tf_op jit(solution)/shard_map/project/pallas_call | solution.py:54
  53.1 0.1 collective-permute-start.8
  53.2 1.5 %collective-permute-done.8 = bf16[128,1024]{1,0:T(8,128)(2,1)S(1)} collective-permute-done((bf16[128,1024]{1,0:T(8,128)(2,1)S(1)}, bf16[128,1024]{1,0:T(8,128)(2,1)S(1)}, u32[]{:S(2)}, u32[]{:S(2)}) %collective-permute-start.8) | collective-permute-done | bytes 262176 | tf_op jit(solution)/shard_map/ppermute | solution.py:271
  54.7 0.8 %add_convert_fusion = bf16[128,1024]{1,0:T(8,128)(2,1)} fusion(f32[128,1024]{1,0:T(8,128)S(1)} %get-tuple-element.41, bf16[128,1024]{1,0:T(8,128)(2,1)S(1)} %collective-permute-done.8), kind=kLoop, calls=%fused_computation | loop fusion | flops 393216 | bytes 1048576 | tf_op jit(solution)/shard_map/convert_element_type | solution.py:375
  (11 shorter events, 0.0 us)
Async XLA Ops:
  0.0 26.4 %collective-permute-start.6 = (bf16[512,1024]{1,0:T(8,128)(2,1)}, bf16[512,1024]{1,0:T(8,128)(2,1)}, u32[]{:S(2)}, u32[]{:S(2)}) collective-permute-start(bf16[512,1024]{1,0:T(8,128)(2,1)} %rest_0_.1), channel_id=1, source_target_pairs={{0,8},{4,20},{8,0},{12,28},{16,24},{20,4},{24,16},{28,12},{1,9},{5... | collective-permute-start | bytes 3145736 | tf_op jit(solution)/shard_map/ppermute | solution.py:271
  2.9 1.1 %copy-start = (bf16[3,1024,128]{2,1,0:T(8,128)(2,1)S(1)}, bf16[3,1024,128]{2,1,0:T(8,128)(2,1)}, u32[]{:S(2)}) copy-start(bf16[3,1024,128]{2,1,0:T(8,128)(2,1)} %streams_ref.3) | copy-start | bytes 2359300
  4.1 1.9 %copy-start.1 = (f32[3,7,1024]{2,1,0:T(8,128)S(1)}, f32[3,7,1024]{2,1,0:T(8,128)}, u32[]{:S(2)}) copy-start(f32[3,7,1024]{2,1,0:T(8,128)} %taps_ref.3) | copy-start | bytes 258052
  4.1 2.0 %copy-start.2 = (f32[128,16]{0,1:T(8,128)S(1)}, f32[128,16]{0,1:T(8,128)}, u32[]{:S(2)}) copy-start(f32[128,16]{0,1:T(8,128)} %param.9) | copy-start | bytes 24580
  4.1 2.0 %copy-start.3 = (f32[128,16]{0,1:T(8,128)S(1)}, f32[128,16]{0,1:T(8,128)}, u32[]{:S(2)}) copy-start(f32[128,16]{0,1:T(8,128)} %param.8) | copy-start | bytes 24580
  4.4 1.7 %copy-start.4 = (f32[1024]{0:T(1024)S(1)}, f32[1024]{0:T(1024)}, u32[]{:S(2)}) copy-start(f32[1024]{0:T(1024)} %param.10) | copy-start | bytes 12292
  4.4 4.3 %collective-permute-start = (bf16[3,8,1024]{2,1,0:T(8,128)(2,1)S(1)}, bf16[3,8,1024]{2,1,0:T(8,128)(2,1)S(1)}, u32[]{:S(2)}, u32[]{:S(2)}) collective-permute-start(bf16[3,8,1024]{2,1,0:T(8,128)(2,1)S(1)} %tails.1), channel_id=1, source_target_pairs={{0,4},{4,8},{8,12},{12,16},{16,20},{20,24},{24,28},{1,5},{5,9},{9,... | collective-permute-start | bytes 147464 | tf_op jit(solution)/shard_map/ppermute | solution.py:25
  8.7 7.1 %copy-start.5 = (bf16[512,1024]{1,0:T(8,128)(2,1)S(1)}, bf16[512,1024]{1,0:T(8,128)(2,1)}, u32[]{:S(2)}) copy-start(bf16[512,1024]{1,0:T(8,128)(2,1)} %rest_0_.1) | copy-start | bytes 3145732
  10.2 12.9 %all-to-all-start = ((bf16[8,16,1024]{2,1,0:T(8,128)(2,1)}), bf16[8,16,1024]{2,1,0:T(8,128)(2,1)S(1)}, u32[]{:S(2)}, u32[]{:S(2)}) async-start(bf16[8,16,1024]{2,1,0:T(8,128)(2,1)} %get-tuple-element.27), calls=%async_computation | async-start | bytes 524288 | tf_op jit(solution)/shard_map/all_to_all | solution.py:320
  15.8 22.4 %collective-permute-start.4 = (bf16[512,1024]{1,0:T(8,128)(2,1)S(1)}, bf16[512,1024]{1,0:T(8,128)(2,1)}, u32[]{:S(2)}, u32[]{:S(2)}) collective-permute-start(bf16[512,1024]{1,0:T(8,128)(2,1)S(1)} %copy-done.5), channel_id=1, source_target_pairs={{0,16},{4,12},{8,24},{12,4},{16,0},{20,28},{24,8},{28,20},{1,17},{... | collective-permute-start | bytes 3145736 | tf_op jit(solution)/shard_map/ppermute | solution.py:271
  25.1 1.3 %collective-permute-start.1 = (bf16[128,512]{1,0:T(8,128)(2,1)S(1)}, bf16[128,512]{1,0:T(8,128)(2,1)S(1)}, u32[]{:S(2)}, u32[]{:S(2)}) collective-permute-start(bf16[128,512]{1,0:T(8,128)(2,1)S(1)} %get-tuple-element.37), channel_id=1, source_target_pairs={{0,4},{4,0},{8,12},{12,8},{16,20},{20,16},{24,28},{28,24},{1,5},{5... | collective-permute-start | bytes 393224 | tf_op jit(solution)/shard_map/ppermute | solution.py:271
  26.5 22.7 %collective-permute-start.7 = (bf16[512,1024]{1,0:T(8,128)(2,1)}, bf16[512,1024]{1,0:T(8,128)(2,1)}, u32[]{:S(2)}, u32[]{:S(2)}) collective-permute-start(bf16[512,1024]{1,0:T(8,128)(2,1)} %collective-permute-done.6.rest_1_), channel_id=1, source_target_pairs={{0,16},{4,12},{8,24},{12,4},{16,0},{20,28},{24,8},{28,20},{1,17},{... | collective-permute-start | bytes 3145736 | tf_op jit(solution)/shard_map/ppermute | solution.py:271
  27.2 11.0 %collective-permute-start.3 = (bf16[256,512]{1,0:T(8,128)(2,1)S(1)}, bf16[256,512]{1,0:T(8,128)(2,1)S(1)}, u32[]{:S(2)}, u32[]{:S(2)}) collective-permute-start(bf16[256,512]{1,0:T(8,128)(2,1)S(1)} %constant_dynamic-update-slice_fusion.own_ref), channel_id=1, source_target_pairs={{0,3},{1,2},{2,1},{3,0},{4,7},{5,6},{6,5},{7,4},{8,11},{9,10},{10,... | collective-permute-start | bytes 786440 | tf_op jit(solution)/shard_map/ppermute | solution.py:280
  30.8 12.5 %collective-permute-start.2 = (bf16[256,512]{1,0:T(8,128)(2,1)S(1)}, bf16[256,512]{1,0:T(8,128)(2,1)S(1)}, u32[]{:S(2)}, u32[]{:S(2)}) collective-permute-start(bf16[256,512]{1,0:T(8,128)(2,1)S(1)} %constant_dynamic-update-slice_fusion.own_ref), channel_id=1, source_target_pairs={{0,1},{1,0},{2,3},{3,2},{4,5},{5,4},{6,7},{7,6},{8,9},{9,8},{10,11... | collective-permute-start | bytes 786440 | tf_op jit(solution)/shard_map/ppermute | solution.py:280
  38.2 10.9 %collective-permute-start.5 = (bf16[256,512]{1,0:T(8,128)(2,1)S(1)}, bf16[256,512]{1,0:T(8,128)(2,1)S(1)}, u32[]{:S(2)}, u32[]{:S(2)}) collective-permute-start(bf16[256,512]{1,0:T(8,128)(2,1)S(1)} %collective-permute-done.3.across_ref), channel_id=1, source_target_pairs={{0,1},{1,0},{2,3},{3,2},{4,5},{5,4},{6,7},{7,6},{8,9},{9,8},{10,11... | collective-permute-start | bytes 786440 | tf_op jit(solution)/shard_map/ppermute | solution.py:280
  53.1 1.6 %collective-permute-start.8 = (bf16[128,1024]{1,0:T(8,128)(2,1)S(1)}, bf16[128,1024]{1,0:T(8,128)(2,1)S(1)}, u32[]{:S(2)}, u32[]{:S(2)}) collective-permute-start(bf16[128,1024]{1,0:T(8,128)(2,1)S(1)} %get-tuple-element.42), channel_id=1, source_target_pairs={{0,4},{4,0},{8,12},{12,8},{16,20},{20,16},{24,28},{28,24},{1,5},{5... | collective-permute-start | bytes 786440 | tf_op jit(solution)/shard_map/ppermute | solution.py:271

commit v13 on v12

--- a/solution.py
+++ b/solution.py
@@ -14,6 +14,7 @@
 TILE = 128
 CORES = 2
 COLUMNS = 256
+STRIP = 32
 VMEM_LIMIT = 24 * 1024 * 1024
 PLAIN = (((1,), (0,)), ((), ()))
 CONTRACT_LANES = (((1,), (1,)), ((), ()))
@@ -179,7 +180,9 @@
     unit = identity(length)
     time = iota((poles, length), 1).astype(F32)
     member = (iota((in_tile, in_tile * poles), 1) // poles == iota((in_tile, in_tile * poles), 0)).astype(BF16)
-    causal = iota((length, length), 1) >= iota((length, length), 0)
+    strip = STRIP
+    lane = iota((width, length), 1)
+    causal = iota((strip, length), 1) >= iota((strip, length), 0)
 
     def tile(index):
         chans = tile_of(index)
@@ -197,72 +200,90 @@
         high, low = halves(jnp.concatenate(impulse, axis=0))
         response = dot(member, high) + dot(member, low)
         gated = gated_ref[:, chans]
-        signal = turned(gated, unit).astype(BF16)
+        pieces = [turned(gated[at : at + strip], unit).astype(BF16) for at in range(0, length, strip)]
         parts = []
         for pair in range(in_tile // 2):
             blocks = []
             for g in (2 * pair, 2 * pair + 1):
-                spread = jnp.broadcast_to(response[g : g + 1], (length, length))
+                spread = jnp.broadcast_to(response[g : g + 1], (strip, length))
                 shifted = pltpu.roll(spread, 0, 1, stride=1, stride_axis=0)
                 blocks.append(jnp.where(causal, shifted, 0.0).astype(BF16))
-            both = dot(signal[pair * 2 * width : (pair + 1) * 2 * width], jnp.concatenate(blocks, axis=1))
-            parts += [both[:width, :length], both[width:, length:]]
+            rows = slice(pair * 2 * width, (pair + 1) * 2 * width)
+            signal = jnp.concatenate([piece[rows] for piece in pieces], axis=0)
+            both = dot(signal, jnp.concatenate(blocks, axis=1))
+            for g in range(2):
+                total = None
+                for at in range(length // strip):
+                    first = at * 2 * width + g * width
+                    term = both[first : first + width, g * length : (g + 1) * length]
+                    if at:
+                        term = jnp.where(lane >= at * strip, pltpu.roll(term, at * strip, 1), 0.0)
+                    total = term if total is None else total + term
+                parts.append(total)
         high, low = halves(jnp.concatenate(parts, axis=0))
         base_ref[:, chans] = turned(high, unit) + turned(low, unit) + skip_ref[:, chans] * gated.astype(F32)
 
     unrolled(channels // TILE, tile)
 
 
-def finish_kernel(at_ref, ends_ref, step_ref, lift_ref, query_ref, first_ref, base_ref, mine_ref, other_ref, mixed_ref, state_ref):
-    length, channels = mixed_ref.shape
-    poles = step_ref.shape[0]
+def finish_kernel(at_ref, ends_ref, step_ref, lift_ref, query_ref, first_ref, base_ref, mixed_ref, state_ref):
+    length, share = mixed_ref.shape
+    poles, channels = step_ref.shape
     in_tile = lift_ref.shape[1] // poles * TILE // channels
-    me, core = at_ref[0], at_ref[1]
+    me, half = at_ref[0], at_ref[1]
+    here = tile_of(half, share)
+    step = step_ref[:, here]
 
     def earlier(block, state):
-        return jnp.where(block < me, step_ref[...] * state + ends_ref[block].astype(F32), state)
-
-    state_ref[...] = lax.fori_loop(0, ends_ref.shape[0] - 1, earlier, jnp.zeros((poles, channels), F32))
+        return jnp.where(block < me, step * state + ends_ref[block, :, here].astype(F32), state)
+
+    state_ref[...] = lax.fori_loop(0, ends_ref.shape[0] - 1, earlier, jnp.zeros((poles, share), F32))
     owner = iota((poles, TILE), 1) // (TILE // in_tile)
 
     def tile(index):
-        chans = tile_of(index)
-        entering = state_ref[:, chans]
+        at = half * (share // TILE) + index
+        chans = tile_of(at)
+        entering = state_ref[:, tile_of(index)]
         apart = jnp.concatenate([jnp.where(owner == g, entering, 0.0) for g in range(in_tile)], axis=0)
         high, low = halves(apart)
-        states = tile_of(index, in_tile * poles)
-        lift = lift_ref[:, states]
+        lift = lift_ref[:, tile_of(at, in_tile * poles)]
         carried = dot(lift, high) + dot(lift, low)
         query = jnp.concatenate([first_ref[:, chans], query_ref[:, chans].astype(F32)[ROWS:]], axis=0)
-        mixed_ref[:, chans] = (query * (base_ref[:, chans] + carried)).astype(BF16)
-
-    unrolled(channels // TILE, tile)
-    share = channels // CORES
-    mine_ref[...] = mixed_ref[:, tile_of(core, share)]
-    other_ref[...] = mixed_ref[:, tile_of(1 - core, share)]
-
-
-def project_kernel(at_ref, own_ref, beside_ref, beyond_ref, across_ref, *rest):
-    *weight_hbms, mine_ref, other_ref, layers_ref, weight_ref, sems = rest
+        mixed_ref[:, tile_of(index)] = (query * (base_ref[:, chans] + carried)).astype(BF16)
+
+    unrolled(share // TILE, tile)
+
+
+def early_kernel(at_ref, own_ref, beside_ref, across_ref, *rest):
+    *weight_hbms, total_ref, rows_ref, layers_ref, weight_ref, sems = rest
     copies = [
         pltpu.make_async_copy(hbm, weight_ref.at[at], sems.at[at]) for at, hbm in enumerate(weight_hbms)
     ]
     for copy in copies:
         copy.start()
     layer = at_ref[0]
-    for bits, ref in enumerate((own_ref, beside_ref, beyond_ref, across_ref)):
+    for bits, ref in ((0, own_ref), (1, beside_ref), (3, across_ref)):
         layers_ref[layer ^ bits] = ref[...]
+    layers_ref[layer ^ 2] = jnp.zeros_like(own_ref)
     for copy in copies:
         copy.wait()
-    length, features = mine_ref.shape
-    for column in range(0, features, COLUMNS):
+    for column in range(0, total_ref.shape[1], COLUMNS):
         columns = slice(column, column + COLUMNS)
         total = None
         for at in range(len(copies)):
             term = dot(layers_ref[at_ref[1 + at]], weight_ref[at, :, columns])
             total = term if total is None else total + term
-        mine_ref[:, columns] = total[:length]
-        other_ref[:, columns] = total[length:].astype(BF16)
+        total_ref[:, columns] = total
+    for at in range(len(copies)):
+
+        @pl.when(at_ref[1 + at] == layer ^ 2)
+        def _():
+            rows_ref[...] = weight_ref[at]
+
+
+def late_kernel(first, beyond_ref, total_ref, rows_ref, out_ref):
+    tokens = pl.ds(first, out_ref.shape[0])
+    out_ref[...] = (total_ref[tokens, :] + dot(beyond_ref[tokens, :], rows_ref[...])).astype(out_ref.dtype)
 
 
 def swap(value, *bits):
@@ -330,16 +351,21 @@
     me = lax.axis_index("ctx").astype(jnp.int32)
     core = me % CORES
     smem = [pl.BlockSpec(memory_space=pltpu.SMEM)]
-    outs = [((length, share), BF16), ((length, share), BF16), ((length, channels), BF16)]
-    mine, other, mixed = call(
-        finish_kernel,
-        outs,
-        "finish",
-        jnp.stack([me, core]), all_ends, step, lift, query, first, base,
-        specs=smem + whole(6),
-        scratch=[pltpu.VMEM((poles, channels), F32)],
-    )
-    if rows != share:
+
+    def finished(half):
+        return call(
+            finish_kernel,
+            [((length, share), BF16)],
+            "finish",
+            jnp.stack([me, half]), all_ends, step, lift, query, first, base,
+            specs=smem + whole(6),
+            scratch=[pltpu.VMEM((poles, share), F32)],
+        )[0]
+
+    if rows == share:
+        other, mine = finished(1 - core), finished(core)
+    else:
+        mixed = jnp.concatenate([finished(jnp.full_like(me, half)) for half in range(CORES)], axis=1)
         by_core = mixed.reshape(length, share // rows, CORES, rows).transpose(2, 0, 1, 3)
         by_core = by_core.reshape(CORES, length, share)
         mine = lax.dynamic_index_in_dim(by_core, core, 0, keepdims=False)
@@ -358,19 +384,26 @@
     first_row = jnp.where(core == 0, 1, 2)
     chip = me // CORES
     place = [chip, chip ^ first_row, chip ^ (3 - first_row), chip ^ 3] if square else [jnp.full_like(me, at) for at in range(4)]
-    mine, other = call(
-        project_kernel,
-        [((length, features), F32), ((length, features), BF16)],
-        "project",
-        jnp.stack([layer] + place), block, beside, beyond, across, *(pltpu.with_memory_space_constraint(part, pltpu.HBM) for part in weight),
-        specs=smem + whole(4) + [pl.BlockSpec(memory_space=pltpu.HBM)] * len(weight),
+    total, last_rows = call(
+        early_kernel,
+        [((CORES * length, features), F32), ((share, features), BF16)],
+        "early",
+        jnp.stack([layer] + place), block, beside, across,
+        *(pltpu.with_memory_space_constraint(part, pltpu.HBM) for part in weight),
+        specs=smem + whole(3) + [pl.BlockSpec(memory_space=pltpu.HBM)] * len(weight),
         scratch=[
             pltpu.VMEM((layers,) + block.shape, BF16),
             pltpu.VMEM((layers, share, features), BF16),
             pltpu.SemaphoreType.DMA((layers,)),
         ],
-        flops=10**9,
+        flops=0,
     )
+    sides = []
+    for side, kind in ((1, BF16), (0, F32)):
+        sides += call(
+            functools.partial(late_kernel, side * length), [((length, features), kind)], "late", beyond, total, last_rows, flops=0
+        )
+    other, mine = sides
     other = swap(other, 1)
     return (mine + other.astype(F32)).astype(BF16)
 

time: 55.8 us -> 51.4 us (0.921)
  waiting for transfers between devices: 16.5 us -> 10.9 us
  Pallas kernels: 15.4 us -> 16.1 us
    ppermute x3, waiting for transfers between devices: 13.4 us -> 7.69 us  [trade(): lax.ppermute(value, 'tp', [(source, source ^ bits) for source in range(co...]
    pallas_call x6 -> x9, Pallas kernels: 15.4 us -> 16.1 us  [call(): pl.pallas_call(kernel, out_shape=tuple((jax.ShapeDtypeStruct(*out) for ou...]
    unnamed x13 -> x12, local copies, waits for them, and re-layouts: 1.16 us -> 1.15 us
  transfers between devices with their start and end apart: 10 -> 10, of which waited for: 6 -> 5; matrix products, arithmetic and copies ran while one was open for 0% -> 0% of each run, Pallas kernels for 21% -> 31%
where the time goes in v13:
time: 51.4 us; the launch traced here: 51.1 us
  starting transfers between devices  21.8 us (42%)
  Pallas kernels  16.1 us (31%)
  waiting for transfers between devices  10.9 us (21%)
  local copies, waits for them, and re-layouts  1.24 us (2%)
  other arithmetic  0.93 us (2%)
    pallas_call x9, Pallas kernels, call(): pl.pallas_call(kernel, out_shape=tuple((jax.ShapeDtypeStruct(*out) for ou...  16.1 us
    ppermute x3, starting transfers between devices, trade(): lax.ppermute(value, 'tp', [(source, source ^ bits) for source in range(co...  8.37 us
    ppermute x3, waiting for transfers between devices, trade(): lax.ppermute(value, 'tp', [(source, source ^ bits) for source in range(co...  7.69 us
    ppermute x5, starting transfers between devices, swap(): return lax.ppermute(value, 'ctx', pairs)  6.27 us
    all_to_all x1, starting transfers between devices, local(): lax.all_to_all(ends, 'ctx', split_axis=0, concat_axis=0, tiled=True)  5.51 us
    ppermute x5, waiting for transfers between devices, swap(): return lax.ppermute(value, 'ctx', pairs)  3.15 us
    ppermute x1, starting transfers between devices, from_behind(): lax.ppermute(value, axis, [(source, source + steps) for source in range(l...  1.63 us
    unnamed x12, local copies, waits for them, and re-layouts  1.15 us
  transfers between devices with their start and end apart: 10, of which 5 were waited for; matrix products, arithmetic and copies ran while one was open for 0% of the time, Pallas kernels for 31%

profile of v13, /device:TPU:0, one launch (start us, length us, event | category | flops | bytes accessed | tf_op | source)
XLA Modules:
  0.0 51.1 jit_solution(8389978727880782016)
XLA Ops:
  0.0 2.9 %collective-permute-start.6 = (bf16[512,1024]{1,0:T(8,128)(2,1)}, bf16[512,1024]{1,0:T(8,128)(2,1)}, u32[]{:S(2)}, u32[]{:S(2)}) collective-permute-start(bf16[512,1024]{1,0:T(8,128)(2,1)} %rest_0_.1), channel_id=1, source_target_pairs={{0,8},{4,20},{8,0},{12,28},{16,24},{20,4},{24,16},{28,12},{1,9},{5... | collective-permute-start | bytes 3145736 | tf_op jit(solution)/shard_map/ppermute | solution.py:292
  2.9 1.1 %copy-done = bf16[3,1024,128]{2,1,0:T(8,128)(2,1)S(1)} copy-done((bf16[3,1024,128]{2,1,0:T(8,128)(2,1)S(1)}, bf16[3,1024,128]{2,1,0:T(8,128)(2,1)}, u32[]{:S(2)}) %copy-start) | copy-done | bytes 786456
  4.1 0.3 tails.1
  4.4 1.6 %collective-permute-start = (bf16[3,8,1024]{2,1,0:T(8,128)(2,1)S(1)}, bf16[3,8,1024]{2,1,0:T(8,128)(2,1)S(1)}, u32[]{:S(2)}, u32[]{:S(2)}) collective-permute-start(bf16[3,8,1024]{2,1,0:T(8,128)(2,1)S(1)} %tails.1), channel_id=1, source_target_pairs={{0,4},{4,8},{8,12},{12,16},{16,20},{20,24},{24,28},{1,5},{5,9},{9,... | collective-permute-start | bytes 147464 | tf_op jit(solution)/shard_map/ppermute | solution.py:26
  6.1 2.6 %prepare.1 = (f32[3,8,1024]{2,1,0:T(8,128)S(1)}, bf16[128,1024]{1,0:T(8,128)(2,1)S(1)}, f32[128,1024]{1,0:T(8,128)S(1)}, bf16[2,2048,128]{2,1,0:T(8,128)(2,1)S(1...) custom-call(bf16[3,1024,128]{2,1,0:T(8,128)(2,1)S(1)} %copy-done, ...), custom_call_target="tpu_custom_call" | custom-call | flops 1000000000 | bytes 10000000 | tf_op jit(solution)/shard_map/prepare/pallas_call | solution.py:55
  8.7 0.0 copy-start.5
  8.7 1.5 %states.1 = (bf16[8,16,1024]{2,1,0:T(8,128)(2,1)}, bf16[128,1024]{1,0:T(8,128)(2,1)S(1)}, f32[8,1024]{1,0:T(8,128)S(1)}) custom-call(bf16[3,8,1024]{2,1,0:T(8,128)(2,1)S(1)} %collective-permute-done.before_ref, f32[3,8,1024]{2,1,0:T(8,128)S(1)} %get-tuple-element.22.heads_ref, f32[3,7,1024]{2,1,0:T(8,128)S(1)} %copy-done.1, ...), custom_call_target="tpu_custom_call" | custom-call | flops 100000000 | bytes 1000000 | tf_op jit(solution)/shard_map/states/pallas_call | solution.py:55
  10.2 5.5 %all-to-all-start = ((bf16[8,16,1024]{2,1,0:T(8,128)(2,1)}), bf16[8,16,1024]{2,1,0:T(8,128)(2,1)S(1)}, u32[]{:S(2)}, u32[]{:S(2)}) async-start(bf16[8,16,1024]{2,1,0:T(8,128)(2,1)} %get-tuple-element.25), calls=%async_computation | async-start | bytes 524288 | tf_op jit(solution)/shard_map/all_to_all | solution.py:341
  15.7 0.1 pad_add_fusion.1.at_ref
  15.8 2.1 %collective-permute-start.3 = (bf16[512,1024]{1,0:T(8,128)(2,1)S(1)}, bf16[512,1024]{1,0:T(8,128)(2,1)}, u32[]{:S(2)}, u32[]{:S(2)}) collective-permute-start(bf16[512,1024]{1,0:T(8,128)(2,1)S(1)} %copy-done.5), channel_id=1, source_target_pairs={{0,16},{4,12},{8,24},{12,4},{16,0},{20,28},{24,8},{28,20},{1,17},{... | collective-permute-start | bytes 3145736 | tf_op jit(solution)/shard_map/ppermute | solution.py:292
  17.9 5.2 %inside.1 = (bf16[128,2048]{1,0:T(8,128)(2,1)S(1)}, f32[128,1024]{1,0:T(8,128)S(1)}) custom-call(bf16[128,1024]{1,0:T(8,128)(2,1)S(1)} %get-tuple-element.27.gated_ref, f32[1,1024]{1,0:T(1,128)S(1)} %get-tuple-element.28.skip_ref, f32[16,128]{1,0:T(8,128)S(1)} %bitcast.13, f32[16,128]{1,0:T(8,128)S(1)} %get-tuple-element.29.coef_ref), custom_call_target="tpu_custom_call" | custom-call | flops 1000000000 | bytes 10000000 | tf_op jit(solution)/shard_map/inside/pallas_call | solution.py:55
  23.1 0.0 all-to-all-done.ends_ref
  23.1 0.9 %finish.3 = bf16[128,512]{1,0:T(8,128)(2,1)S(1)} custom-call(s32[2]{0:T(128)S(1)} %pad_add_fusion.1.at_ref, bf16[8,16,1024]{2,1,0:T(8,128)(2,1)S(1)} %all-to-all-done.ends_ref, f32[16,1024]{1,0:T(8,128)S(1)} %get-tuple-element.26.step_ref, bf16[128,2048]{1,0:T(8,128)(2,1)S(1)} %get-tuple-element.30.lift_ref, ...), custom_call_target="tpu_custom_call" | custom-call | flops 100000000 | bytes 1000000 | tf_op jit(solution)/shard_map/finish/pallas_call | solution.py:55
  24.1 0.1 collective-permute-start.1
  24.1 0.1 pad_add_fusion.at_ref
  24.2 0.9 %finish.2 = bf16[128,512]{1,0:T(8,128)(2,1)S(1)} custom-call(s32[2]{0:T(128)S(1)} %pad_add_fusion.at_ref, bf16[8,16,1024]{2,1,0:T(8,128)(2,1)S(1)} %all-to-all-done.ends_ref, f32[16,1024]{1,0:T(8,128)S(1)} %get-tuple-element.26.step_ref, bf16[128,2048]{1,0:T(8,128)(2,1)S(1)} %get-tuple-element.30.lift_ref, ...), custom_call_target="tpu_custom_call" | custom-call | flops 100000000 | bytes 1000000 | tf_op jit(solution)/shard_map/finish/pallas_call | solution.py:55
  25.1 0.3 collective-permute-done.1
  25.5 1.0 %collective-permute-start.7 = (bf16[512,1024]{1,0:T(8,128)(2,1)}, bf16[512,1024]{1,0:T(8,128)(2,1)}, u32[]{:S(2)}, u32[]{:S(2)}) collective-permute-start(bf16[512,1024]{1,0:T(8,128)(2,1)} %collective-permute-done.6.rest_1_), channel_id=1, source_target_pairs={{0,16},{4,12},{8,24},{12,4},{16,0},{20,28},{24,8},{28,20},{1,17},{... | collective-permute-start | bytes 3145736 | tf_op jit(solution)/shard_map/ppermute | solution.py:292
  26.5 3.6 %collective-permute-start.2 = (bf16[256,512]{1,0:T(8,128)(2,1)S(1)}, bf16[256,512]{1,0:T(8,128)(2,1)S(1)}, u32[]{:S(2)}, u32[]{:S(2)}) collective-permute-start(bf16[256,512]{1,0:T(8,128)(2,1)S(1)} %pad_maximum_fusion.own_ref), channel_id=1, source_target_pairs={{0,3},{1,2},{2,1},{3,0},{4,7},{5,6},{6,5},{7,4},{8,11},{9,10},{10,... | collective-permute-start | bytes 786440 | tf_op jit(solution)/shard_map/ppermute | solution.py:301
  30.1 0.0 collective-permute-start.5
  30.1 7.4 %collective-permute-done.2.across_ref = bf16[256,512]{1,0:T(8,128)(2,1)S(1)} collective-permute-done((bf16[256,512]{1,0:T(8,128)(2,1)S(1)}, bf16[256,512]{1,0:T(8,128)(2,1)S(1)}, u32[]{:S(2)}, u32[]{:S(2)}) %collective-permute-start.2) | collective-permute-done | bytes 262176 | tf_op jit(solution)/shard_map/ppermute | solution.py:301
  37.5 4.8 %collective-permute-start.4 = (bf16[256,512]{1,0:T(8,128)(2,1)S(1)}, bf16[256,512]{1,0:T(8,128)(2,1)S(1)}, u32[]{:S(2)}, u32[]{:S(2)}) collective-permute-start(bf16[256,512]{1,0:T(8,128)(2,1)S(1)} %collective-permute-done.2.across_ref), channel_id=1, source_target_pairs={{0,1},{1,0},{2,3},{3,2},{4,5},{5,4},{6,7},{7,6},{8,9},{9,8},{10,11... | collective-permute-start | bytes 786440 | tf_op jit(solution)/shard_map/ppermute | solution.py:301
  42.2 0.1 stack.44.at_ref
  42.3 0.3 collective-permute-done.5.beside_ref
  42.6 1.7 %collective-permute-done.7.rest_3_ = bf16[512,1024]{1,0:T(8,128)(2,1)} collective-permute-done((bf16[512,1024]{1,0:T(8,128)(2,1)}, bf16[512,1024]{1,0:T(8,128)(2,1)}, u32[]{:S(2)}, u32[]{:S(2)}) %collective-permute-start.7) | collective-permute-done | bytes 1048608 | tf_op jit(solution)/shard_map/ppermute | solution.py:292
  44.3 4.1 %early.1 = (f32[256,1024]{1,0:T(8,128)S(1)}, bf16[512,1024]{1,0:T(8,128)(2,1)S(1)}) custom-call(s32[5]{0:T(128)S(1)} %stack.44.at_ref, bf16[256,512]{1,0:T(8,128)(2,1)S(1)} %pad_maximum_fusion.own_ref, bf16[256,512]{1,0:T(8,128)(2,1)S(1)} %collective-permute-done.5.beside_ref, bf16[256,512]{1,0:T(8,128)(2,1)S(1)} %collective-permute-done.2.across_ref, ...), custom_call_target="tpu_custom_call" | custom-call | tf_op jit(solution)/shard_map/early/pallas_call | solution.py:55
  48.4 0.0 collective-permute-done.4.beyond_ref
  48.4 0.3 late.3
  48.8 0.2 collective-permute-start.8
  48.9 0.3 late.2
  49.3 1.1 %collective-permute-done.8 = bf16[128,1024]{1,0:T(8,128)(2,1)S(1)} collective-permute-done((bf16[128,1024]{1,0:T(8,128)(2,1)S(1)}, bf16[128,1024]{1,0:T(8,128)(2,1)S(1)}, u32[]{:S(2)}, u32[]{:S(2)}) %collective-permute-start.8) | collective-permute-done | bytes 262176 | tf_op jit(solution)/shard_map/ppermute | solution.py:292
  50.4 0.8 %add_convert_fusion = bf16[128,1024]{1,0:T(8,128)(2,1)} fusion(f32[128,1024]{1,0:T(8,128)S(1)} %late.2, bf16[128,1024]{1,0:T(8,128)(2,1)S(1)} %collective-permute-done.8), kind=kLoop, calls=%fused_computation | loop fusion | flops 393216 | bytes 1048576 | tf_op jit(solution)/shard_map/convert_element_type | solution.py:408
  (14 shorter events, 0.0 us)
Async XLA Ops:
  0.0 25.5 %collective-permute-start.6 = (bf16[512,1024]{1,0:T(8,128)(2,1)}, bf16[512,1024]{1,0:T(8,128)(2,1)}, u32[]{:S(2)}, u32[]{:S(2)}) collective-permute-start(bf16[512,1024]{1,0:T(8,128)(2,1)} %rest_0_.1), channel_id=1, source_target_pairs={{0,8},{4,20},{8,0},{12,28},{16,24},{20,4},{24,16},{28,12},{1,9},{5... | collective-permute-start | bytes 3145736 | tf_op jit(solution)/shard_map/ppermute | solution.py:292
  2.9 1.1 %copy-start = (bf16[3,1024,128]{2,1,0:T(8,128)(2,1)S(1)}, bf16[3,1024,128]{2,1,0:T(8,128)(2,1)}, u32[]{:S(2)}) copy-start(bf16[3,1024,128]{2,1,0:T(8,128)(2,1)} %streams_ref.3) | copy-start | bytes 2359300
  4.1 1.9 %copy-start.1 = (f32[3,7,1024]{2,1,0:T(8,128)S(1)}, f32[3,7,1024]{2,1,0:T(8,128)}, u32[]{:S(2)}) copy-start(f32[3,7,1024]{2,1,0:T(8,128)} %taps_ref.3) | copy-start | bytes 258052
  4.1 2.0 %copy-start.2 = (f32[128,16]{0,1:T(8,128)S(1)}, f32[128,16]{0,1:T(8,128)}, u32[]{:S(2)}) copy-start(f32[128,16]{0,1:T(8,128)} %param.9) | copy-start | bytes 24580
  4.1 2.0 %copy-start.3 = (f32[128,16]{0,1:T(8,128)S(1)}, f32[128,16]{0,1:T(8,128)}, u32[]{:S(2)}) copy-start(f32[128,16]{0,1:T(8,128)} %param.8) | copy-start | bytes 24580
  4.4 1.7 %copy-start.4 = (f32[1024]{0:T(1024)S(1)}, f32[1024]{0:T(1024)}, u32[]{:S(2)}) copy-start(f32[1024]{0:T(1024)} %param.10) | copy-start | bytes 12292
  4.4 4.3 %collective-permute-start = (bf16[3,8,1024]{2,1,0:T(8,128)(2,1)S(1)}, bf16[3,8,1024]{2,1,0:T(8,128)(2,1)S(1)}, u32[]{:S(2)}, u32[]{:S(2)}) collective-permute-start(bf16[3,8,1024]{2,1,0:T(8,128)(2,1)S(1)} %tails.1), channel_id=1, source_target_pairs={{0,4},{4,8},{8,12},{12,16},{16,20},{20,24},{24,28},{1,5},{5,9},{9,... | collective-permute-start | bytes 147464 | tf_op jit(solution)/shard_map/ppermute | solution.py:26
  8.7 7.1 %copy-start.5 = (bf16[512,1024]{1,0:T(8,128)(2,1)S(1)}, bf16[512,1024]{1,0:T(8,128)(2,1)}, u32[]{:S(2)}) copy-start(bf16[512,1024]{1,0:T(8,128)(2,1)} %rest_0_.1) | copy-start | bytes 3145732
  10.2 12.9 %all-to-all-start = ((bf16[8,16,1024]{2,1,0:T(8,128)(2,1)}), bf16[8,16,1024]{2,1,0:T(8,128)(2,1)S(1)}, u32[]{:S(2)}, u32[]{:S(2)}) async-start(bf16[8,16,1024]{2,1,0:T(8,128)(2,1)} %get-tuple-element.25), calls=%async_computation | async-start | bytes 524288 | tf_op jit(solution)/shard_map/all_to_all | solution.py:341
  15.8 21.7 %collective-permute-start.3 = (bf16[512,1024]{1,0:T(8,128)(2,1)S(1)}, bf16[512,1024]{1,0:T(8,128)(2,1)}, u32[]{:S(2)}, u32[]{:S(2)}) collective-permute-start(bf16[512,1024]{1,0:T(8,128)(2,1)S(1)} %copy-done.5), channel_id=1, source_target_pairs={{0,16},{4,12},{8,24},{12,4},{16,0},{20,28},{24,8},{28,20},{1,17},{... | collective-permute-start | bytes 3145736 | tf_op jit(solution)/shard_map/ppermute | solution.py:292
  24.1 1.4 %collective-permute-start.1 = (bf16[128,512]{1,0:T(8,128)(2,1)S(1)}, bf16[128,512]{1,0:T(8,128)(2,1)S(1)}, u32[]{:S(2)}, u32[]{:S(2)}) collective-permute-start(bf16[128,512]{1,0:T(8,128)(2,1)S(1)} %finish.3), channel_id=1, source_target_pairs={{0,4},{4,0},{8,12},{12,8},{16,20},{20,16},{24,28},{28,24},{1,5},{5... | collective-permute-start | bytes 393224 | tf_op jit(solution)/shard_map/ppermute | solution.py:292
  25.5 18.8 %collective-permute-start.7 = (bf16[512,1024]{1,0:T(8,128)(2,1)}, bf16[512,1024]{1,0:T(8,128)(2,1)}, u32[]{:S(2)}, u32[]{:S(2)}) collective-permute-start(bf16[512,1024]{1,0:T(8,128)(2,1)} %collective-permute-done.6.rest_1_), channel_id=1, source_target_pairs={{0,16},{4,12},{8,24},{12,4},{16,0},{20,28},{24,8},{28,20},{1,17},{... | collective-permute-start | bytes 3145736 | tf_op jit(solution)/shard_map/ppermute | solution.py:292
  26.5 11.0 %collective-permute-start.2 = (bf16[256,512]{1,0:T(8,128)(2,1)S(1)}, bf16[256,512]{1,0:T(8,128)(2,1)S(1)}, u32[]{:S(2)}, u32[]{:S(2)}) collective-permute-start(bf16[256,512]{1,0:T(8,128)(2,1)S(1)} %pad_maximum_fusion.own_ref), channel_id=1, source_target_pairs={{0,3},{1,2},{2,1},{3,0},{4,7},{5,6},{6,5},{7,4},{8,11},{9,10},{10,... | collective-permute-start | bytes 786440 | tf_op jit(solution)/shard_map/ppermute | solution.py:301
  30.1 12.5 %collective-permute-start.5 = (bf16[256,512]{1,0:T(8,128)(2,1)S(1)}, bf16[256,512]{1,0:T(8,128)(2,1)S(1)}, u32[]{:S(2)}, u32[]{:S(2)}) collective-permute-start(bf16[256,512]{1,0:T(8,128)(2,1)S(1)} %pad_maximum_fusion.own_ref), channel_id=1, source_target_pairs={{0,1},{1,0},{2,3},{3,2},{4,5},{5,4},{6,7},{7,6},{8,9},{9,8},{10,11... | collective-permute-start | bytes 786440 | tf_op jit(solution)/shard_map/ppermute | solution.py:301
  37.5 10.9 %collective-permute-start.4 = (bf16[256,512]{1,0:T(8,128)(2,1)S(1)}, bf16[256,512]{1,0:T(8,128)(2,1)S(1)}, u32[]{:S(2)}, u32[]{:S(2)}) collective-permute-start(bf16[256,512]{1,0:T(8,128)(2,1)S(1)} %collective-permute-done.2.across_ref), channel_id=1, source_target_pairs={{0,1},{1,0},{2,3},{3,2},{4,5},{5,4},{6,7},{7,6},{8,9},{9,8},{10,11... | collective-permute-start | bytes 786440 | tf_op jit(solution)/shard_map/ppermute | solution.py:301
  48.8 1.6 %collective-permute-start.8 = (bf16[128,1024]{1,0:T(8,128)(2,1)S(1)}, bf16[128,1024]{1,0:T(8,128)(2,1)S(1)}, u32[]{:S(2)}, u32[]{:S(2)}) collective-permute-start(bf16[128,1024]{1,0:T(8,128)(2,1)S(1)} %late.3), channel_id=1, source_target_pairs={{0,4},{4,0},{8,12},{12,8},{16,20},{20,16},{24,28},{28,24},{1,5},{5... | collective-permute-start | bytes 786440 | tf_op jit(solution)/shard_map/ppermute | solution.py:292

commit v14 on v13

--- a/solution.py
+++ b/solution.py
@@ -172,44 +172,53 @@
     unrolled(channels // TILE, leave)
 
 
-def inside_kernel(gated_ref, skip_ref, rates_ref, coef_ref, lift_ref, base_ref):
+def inside_kernel(
+    gated_ref, skip_ref, rates_ref, coef_ref, lift_ref, base_ref, response_ref, signal_ref, sum_ref
+):
     length, channels = gated_ref.shape
     poles, groups = rates_ref.shape
     width = channels // groups
     in_tile = TILE // width
+    tiles = channels // TILE
+    strip = STRIP
     unit = identity(length)
     time = iota((poles, length), 1).astype(F32)
     member = (iota((in_tile, in_tile * poles), 1) // poles == iota((in_tile, in_tile * poles), 0)).astype(BF16)
-    strip = STRIP
     lane = iota((width, length), 1)
     causal = iota((strip, length), 1) >= iota((strip, length), 0)
 
-    def tile(index):
-        chans = tile_of(index)
+    def factors(index):
         shift = groups - index * in_tile
         rates = pltpu.roll(rates_ref[...], shift, 1)
         coef = pltpu.roll(coef_ref[...], shift, 1)
+        once = jnp.exp(-rates)
         impulse, lift = [], []
         for g in range(in_tile):
-            rate = jnp.broadcast_to(rates[:, g : g + 1], (poles, length))
-            scale = jnp.broadcast_to(coef[:, g : g + 1], (poles, length))
-            impulse.append(scale * jnp.exp(-rate * time))
-            lift.append(scale * jnp.exp(-rate * (time + 1.0)))
-        states = tile_of(index, in_tile * poles)
-        lift_ref[:, states] = turned(jnp.concatenate(lift, axis=0).astype(BF16), unit).astype(BF16)
+            term = jnp.broadcast_to(coef[:, g : g + 1], (poles, length)) * jnp.exp(-rates[:, g : g + 1] * time)
+            impulse.append(term)
+            lift.append(term * once[:, g : g + 1])
         high, low = halves(jnp.concatenate(impulse, axis=0))
-        response = dot(member, high) + dot(member, low)
-        gated = gated_ref[:, chans]
-        pieces = [turned(gated[at : at + strip], unit).astype(BF16) for at in range(0, length, strip)]
-        parts = []
+        response_ref[pl.ds(pl.multiple_of(index * in_tile, in_tile), in_tile), :] = dot(member, high) + dot(member, low)
+        lift = jnp.concatenate(lift, axis=0).astype(BF16)
+        lift_ref[:, tile_of(index, in_tile * poles)] = turned(lift, unit).astype(BF16)
+
+    def signals(index):
+        gated = gated_ref[:, tile_of(index)]
+        for at in range(length // strip):
+            piece = turned(gated[at * strip : (at + 1) * strip], unit).astype(BF16)
+            signal_ref[at, tile_of(index), :] = piece
+
+    def products(index):
         for pair in range(in_tile // 2):
+            group = index * in_tile + 2 * pair
+            responses = response_ref[pl.ds(group, 2), :]
             blocks = []
-            for g in (2 * pair, 2 * pair + 1):
-                spread = jnp.broadcast_to(response[g : g + 1], (strip, length))
+            for g in range(2):
+                spread = jnp.broadcast_to(responses[g : g + 1], (strip, length))
                 shifted = pltpu.roll(spread, 0, 1, stride=1, stride_axis=0)
                 blocks.append(jnp.where(causal, shifted, 0.0).astype(BF16))
-            rows = slice(pair * 2 * width, (pair + 1) * 2 * width)
-            signal = jnp.concatenate([piece[rows] for piece in pieces], axis=0)
+            rows = pl.ds(pl.multiple_of(group * width, 2 * width), 2 * width)
+            signal = jnp.concatenate([signal_ref[at, rows, :] for at in range(length // strip)], axis=0)
             both = dot(signal, jnp.concatenate(blocks, axis=1))
             for g in range(2):
                 total = None
@@ -219,11 +228,18 @@
                     if at:
                         term = jnp.where(lane >= at * strip, pltpu.roll(term, at * strip, 1), 0.0)
                     total = term if total is None else total + term
-                parts.append(total)
-        high, low = halves(jnp.concatenate(parts, axis=0))
-        base_ref[:, chans] = turned(high, unit) + turned(low, unit) + skip_ref[:, chans] * gated.astype(F32)
-
-    unrolled(channels // TILE, tile)
+                sum_ref[pl.ds(pl.multiple_of((group + g) * width, width), width), :] = total
+
+    def back(index):
+        chans = tile_of(index)
+        high, low = halves(sum_ref[chans, :])
+        direct = skip_ref[:, chans] * gated_ref[:, chans].astype(F32)
+        base_ref[:, chans] = turned(high, unit) + turned(low, unit) + direct
+
+    unrolled(tiles, signals)
+    unrolled(tiles, factors)
+    unrolled(tiles, products)
+    unrolled(tiles, back)
 
 
 def finish_kernel(at_ref, ends_ref, step_ref, lift_ref, query_ref, first_ref, base_ref, mixed_ref, state_ref):
@@ -255,16 +271,18 @@
 
 
 def early_kernel(at_ref, own_ref, beside_ref, across_ref, *rest):
-    *weight_hbms, total_ref, rows_ref, layers_ref, weight_ref, sems = rest
+    *weight_hbms, total_ref, rows_ref, block_ref, layers_ref, weight_ref, sems = rest
     copies = [
         pltpu.make_async_copy(hbm, weight_ref.at[at], sems.at[at]) for at, hbm in enumerate(weight_hbms)
     ]
     for copy in copies:
         copy.start()
     layer = at_ref[0]
+    last = layer ^ 2
     for bits, ref in ((0, own_ref), (1, beside_ref), (3, across_ref)):
         layers_ref[layer ^ bits] = ref[...]
-    layers_ref[layer ^ 2] = jnp.zeros_like(own_ref)
+    layers_ref[last] = jnp.zeros_like(own_ref)
+    block_ref[...] = layers_ref[at_ref[1 + len(copies)]]
     for copy in copies:
         copy.wait()
     for column in range(0, total_ref.shape[1], COLUMNS):
@@ -274,16 +292,20 @@
             term = dot(layers_ref[at_ref[1 + at]], weight_ref[at, :, columns])
             total = term if total is None else total + term
         total_ref[:, columns] = total
+    rows_ref[...] = jnp.zeros_like(rows_ref)
     for at in range(len(copies)):
 
-        @pl.when(at_ref[1 + at] == layer ^ 2)
+        @pl.when(at_ref[1 + at] == last)
         def _():
             rows_ref[...] = weight_ref[at]
 
 
-def late_kernel(first, beyond_ref, total_ref, rows_ref, out_ref):
+def late_kernel(first, at_ref, beyond_ref, total_ref, rows_ref, block_ref, weight_ref, out_ref):
     tokens = pl.ds(first, out_ref.shape[0])
-    out_ref[...] = (total_ref[tokens, :] + dot(beyond_ref[tokens, :], rows_ref[...])).astype(out_ref.dtype)
+    beyond = beyond_ref[tokens, :]
+    block = jnp.where(at_ref[4] == at_ref[0] ^ 2, beyond, block_ref[tokens, :])
+    total = total_ref[tokens, :] + dot(block, weight_ref[...]) + dot(beyond, rows_ref[...])
+    out_ref[...] = total.astype(out_ref.dtype)
 
 
 def swap(value, *bits):
@@ -344,6 +366,11 @@
         [((length, groups * poles), BF16), ((length, channels), F32)],
         "inside",
         gated, skip, rates, coef,
+        scratch=[
+            pltpu.VMEM((groups, length), F32),
+            pltpu.VMEM((length // STRIP, channels, STRIP), BF16),
+            pltpu.VMEM((channels, length), F32),
+        ],
         flops=10**9,
     )
     if square:
@@ -359,6 +386,7 @@
             "finish",
             jnp.stack([me, half]), all_ends, step, lift, query, first, base,
             specs=smem + whole(6),
+            flops=3 * 10**9,
             scratch=[pltpu.VMEM((poles, share), F32)],
         )[0]
 
@@ -384,24 +412,31 @@
     first_row = jnp.where(core == 0, 1, 2)
     chip = me // CORES
     place = [chip, chip ^ first_row, chip ^ (3 - first_row), chip ^ 3] if square else [jnp.full_like(me, at) for at in range(4)]
-    total, last_rows = call(
+    at = jnp.stack([layer] + place)
+    *sooner, latest = weight
+    total, last_rows, last_block = call(
         early_kernel,
-        [((CORES * length, features), F32), ((share, features), BF16)],
+        [((CORES * length, features), F32), ((share, features), BF16), (block.shape, BF16)],
         "early",
-        jnp.stack([layer] + place), block, beside, across,
-        *(pltpu.with_memory_space_constraint(part, pltpu.HBM) for part in weight),
-        specs=smem + whole(3) + [pl.BlockSpec(memory_space=pltpu.HBM)] * len(weight),
+        at, block, beside, across,
+        *(pltpu.with_memory_space_constraint(part, pltpu.HBM) for part in sooner),
+        specs=smem + whole(3) + [pl.BlockSpec(memory_space=pltpu.HBM)] * len(sooner),
         scratch=[
             pltpu.VMEM((layers,) + block.shape, BF16),
-            pltpu.VMEM((layers, share, features), BF16),
-            pltpu.SemaphoreType.DMA((layers,)),
+            pltpu.VMEM((len(sooner), share, features), BF16),
+            pltpu.SemaphoreType.DMA((len(sooner),)),
         ],
-        flops=0,
+        flops=10**10,
     )
     sides = []
     for side, kind in ((1, BF16), (0, F32)):
         sides += call(
-            functools.partial(late_kernel, side * length), [((length, features), kind)], "late", beyond, total, last_rows, flops=0
+            functools.partial(late_kernel, side * length),
+            [((length, features), kind)],
+            "late",
+            at, beyond, total, last_rows, last_block, latest,
+            specs=smem + whole(5),
+            flops=0,
         )
     other, mine = sides
     other = swap(other, 1)

time: 51.4 us -> 52.6 us (1.023)
  local copies, waits for them, and re-layouts: 1.24 us -> 2.84 us
  waiting for transfers between devices: 10.9 us -> 9.81 us
    ppermute x5, waiting for transfers between devices: 3.15 us -> 0.59 us  [swap(): return lax.ppermute(value, 'ctx', pairs)]
    all_to_all x1, waiting for transfers between devices: 0.03 us -> 1.98 us  [local(): lax.all_to_all(ends, 'ctx', split_axis=0, concat_axis=0, tiled=True)]
    all_to_all x1, starting transfers between devices: 5.51 us -> 3.66 us  [local(): lax.all_to_all(ends, 'ctx', split_axis=0, concat_axis=0, tiled=True)]
    unnamed x12 -> x14, local copies, waits for them, and re-layouts: 1.15 us -> 2.76 us
    ppermute x5, starting transfers between devices: 6.27 us -> 7.68 us  [swap(): return lax.ppermute(value, 'ctx', pairs)]
    ppermute x1, starting transfers between devices: 1.63 us -> 2.37 us  [from_behind(): lax.ppermute(value, axis, [(source, source + steps) for source in range(l...]
  transfers between devices with their start and end apart: 10 -> 10, of which waited for: 5 -> 6; matrix products, arithmetic and copies ran while one was open for 0% -> 0% of each run, Pallas kernels for 31% -> 29%
where the time goes in v14:
time: 52.6 us; the launch traced here: 52.2 us
  starting transfers between devices  22.3 us (42%)
  Pallas kernels  16.3 us (31%)
  waiting for transfers between devices  9.81 us (19%)
  local copies, waits for them, and re-layouts  2.84 us (5%)
  other arithmetic  0.93 us (2%)
    pallas_call x9, Pallas kernels, call(): pl.pallas_call(kernel, out_shape=tuple((jax.ShapeDtypeStruct(*out) for ou...  16.3 us
    ppermute x3, starting transfers between devices, trade(): lax.ppermute(value, 'tp', [(source, source ^ bits) for source in range(co...  8.57 us
    ppermute x5, starting transfers between devices, swap(): return lax.ppermute(value, 'ctx', pairs)  7.68 us
    ppermute x3, waiting for transfers between devices, trade(): lax.ppermute(value, 'tp', [(source, source ^ bits) for source in range(co...  7.23 us
    all_to_all x1, starting transfers between devices, local(): lax.all_to_all(ends, 'ctx', split_axis=0, concat_axis=0, tiled=True)  3.66 us
    unnamed x14, local copies, waits for them, and re-layouts  2.76 us
    ppermute x1, starting transfers between devices, from_behind(): lax.ppermute(value, axis, [(source, source + steps) for source in range(l...  2.37 us
    all_to_all x1, waiting for transfers between devices, local(): lax.all_to_all(ends, 'ctx', split_axis=0, concat_axis=0, tiled=True)  1.98 us
  transfers between devices with their start and end apart: 10, of which 6 were waited for; matrix products, arithmetic and copies ran while one was open for 0% of the time, Pallas kernels for 29%

profile of v14, /device:TPU:0, one launch (start us, length us, event | category | flops | bytes accessed | tf_op | source)
XLA Modules:
  0.0 52.2 jit_solution(16396383971601181577)
XLA Ops:
  0.0 1.1 %copy-done = bf16[3,1024,128]{2,1,0:T(8,128)(2,1)S(1)} copy-done((bf16[3,1024,128]{2,1,0:T(8,128)(2,1)S(1)}, bf16[3,1024,128]{2,1,0:T(8,128)(2,1)}, u32[]{:S(2)}) %copy-start) | copy-done | bytes 786456
  1.1 0.3 tails.1
  1.4 2.4 %collective-permute-start = (bf16[3,8,1024]{2,1,0:T(8,128)(2,1)S(1)}, bf16[3,8,1024]{2,1,0:T(8,128)(2,1)S(1)}, u32[]{:S(2)}, u32[]{:S(2)}) collective-permute-start(bf16[3,8,1024]{2,1,0:T(8,128)(2,1)S(1)} %tails.1), channel_id=1, source_target_pairs={{0,4},{4,8},{8,12},{12,16},{16,20},{20,24},{24,28},{1,5},{5,9},{9,... | collective-permute-start | bytes 147464 | tf_op jit(solution)/shard_map/ppermute | solution.py:26
  3.8 2.6 %collective-permute-start.6 = (bf16[512,1024]{1,0:T(8,128)(2,1)}, bf16[512,1024]{1,0:T(8,128)(2,1)}, u32[]{:S(2)}, u32[]{:S(2)}) collective-permute-start(bf16[512,1024]{1,0:T(8,128)(2,1)} %rest_0_.1), channel_id=1, source_target_pairs={{0,8},{4,20},{8,0},{12,28},{16,24},{20,4},{24,16},{28,12},{1,9},{5... | collective-permute-start | bytes 3145736 | tf_op jit(solution)/shard_map/ppermute | solution.py:314
  6.4 0.7 %copy-done.5 = f32[1024]{0:T(1024)S(1)} copy-done((f32[1024]{0:T(1024)S(1)}, f32[1024]{0:T(1024)}, u32[]{:S(2)}) %copy-start.5) | copy-done | bytes 4120
  7.1 0.0 copy-done.4
  7.1 0.9 %copy-done.2 = f32[3,7,1024]{2,1,0:T(8,128)S(1)} copy-done((f32[3,7,1024]{2,1,0:T(8,128)S(1)}, f32[3,7,1024]{2,1,0:T(8,128)}, u32[]{:S(2)}) %copy-start.2) | copy-done | bytes 86040
  8.0 2.6 %prepare.1 = (f32[3,8,1024]{2,1,0:T(8,128)S(1)}, bf16[128,1024]{1,0:T(8,128)(2,1)S(1)}, f32[128,1024]{1,0:T(8,128)S(1)}, bf16[2,2048,128]{2,1,0:T(8,128)(2,1)S(1...) custom-call(bf16[3,1024,128]{2,1,0:T(8,128)(2,1)S(1)} %copy-done.1, ...), custom_call_target="tpu_custom_call" | custom-call | flops 1000000000 | bytes 10000000 | tf_op jit(solution)/shard_map/prepare/pallas_call | solution.py:55
  10.6 1.5 %states.1 = (bf16[8,16,1024]{2,1,0:T(8,128)(2,1)}, bf16[128,1024]{1,0:T(8,128)(2,1)S(1)}, f32[8,1024]{1,0:T(8,128)S(1)}) custom-call(bf16[3,8,1024]{2,1,0:T(8,128)(2,1)S(1)} %collective-permute-done.before_ref, f32[3,8,1024]{2,1,0:T(8,128)S(1)} %get-tuple-element.23.heads_ref, f32[3,7,1024]{2,1,0:T(8,128)S(1)} %copy-done.2, ...), custom_call_target="tpu_custom_call" | custom-call | flops 100000000 | bytes 1000000 | tf_op jit(solution)/shard_map/states/pallas_call | solution.py:55
  12.2 3.7 %all-to-all-start = ((bf16[8,16,1024]{2,1,0:T(8,128)(2,1)}), bf16[8,16,1024]{2,1,0:T(8,128)(2,1)S(1)}, u32[]{:S(2)}, u32[]{:S(2)}) async-start(bf16[8,16,1024]{2,1,0:T(8,128)(2,1)} %get-tuple-element.26), calls=%async_computation | async-start | bytes 524288 | tf_op jit(solution)/shard_map/all_to_all | solution.py:363
  15.8 0.1 pad_add_fusion.1.at_ref
  15.9 2.0 %collective-permute-start.3 = (bf16[512,1024]{1,0:T(8,128)(2,1)S(1)}, bf16[512,1024]{1,0:T(8,128)(2,1)}, u32[]{:S(2)}, u32[]{:S(2)}) collective-permute-start(bf16[512,1024]{1,0:T(8,128)(2,1)S(1)} %copy-done.6), channel_id=1, source_target_pairs={{0,16},{4,12},{8,24},{12,4},{16,0},{20,28},{24,8},{28,20},{1,17},{... | collective-permute-start | bytes 3145736 | tf_op jit(solution)/shard_map/ppermute | solution.py:314
  17.9 0.1 pad_add_fusion.at_ref
  18.0 4.5 %inside.1 = (bf16[128,2048]{1,0:T(8,128)(2,1)S(1)}, f32[128,1024]{1,0:T(8,128)S(1)}) custom-call(bf16[128,1024]{1,0:T(8,128)(2,1)S(1)} %get-tuple-element.28.gated_ref, f32[1,1024]{1,0:T(1,128)S(1)} %get-tuple-element.29.skip_ref, f32[16,128]{1,0:T(8,128)S(1)} %bitcast.13, f32[16,128]{1,0:T(8,128)S(1)} %get-tuple-element.30.coef_ref), custom_call_target="tpu_custom_call" | custom-call | flops 1000000000 | bytes 10000000 | tf_op jit(solution)/shard_map/inside/pallas_call | solution.py:55
  22.5 2.0 %all-to-all-done.ends_ref = bf16[8,16,1024]{2,1,0:T(8,128)(2,1)S(1)} async-done(((bf16[8,16,1024]{2,1,0:T(8,128)(2,1)}), bf16[8,16,1024]{2,1,0:T(8,128)(2,1)S(1)}, u32[]{:S(2)}, u32[]{:S(2)}) %all-to-all-start) | async-done | bytes 262176 | tf_op jit(solution)/shard_map/all_to_all | solution.py:363
  24.5 0.9 %finish.3 = bf16[128,512]{1,0:T(8,128)(2,1)S(1)} custom-call(s32[2]{0:T(128)S(1)} %pad_add_fusion.1.at_ref, bf16[8,16,1024]{2,1,0:T(8,128)(2,1)S(1)} %all-to-all-done.ends_ref, f32[16,1024]{1,0:T(8,128)S(1)} %get-tuple-element.27.step_ref, bf16[128,2048]{1,0:T(8,128)(2,1)S(1)} %get-tuple-element.31.lift_ref, ...), custom_call_target="tpu_custom_call" | custom-call | flops 3000000000 | bytes 30000000 | tf_op jit(solution)/shard_map/finish/pallas_call | solution.py:55
  25.4 0.5 %collective-permute-start.1 = (bf16[128,512]{1,0:T(8,128)(2,1)S(1)}, bf16[128,512]{1,0:T(8,128)(2,1)S(1)}, u32[]{:S(2)}, u32[]{:S(2)}) collective-permute-start(bf16[128,512]{1,0:T(8,128)(2,1)S(1)} %finish.3), channel_id=1, source_target_pairs={{0,4},{4,0},{8,12},{12,8},{16,20},{20,16},{24,28},{28,24},{1,5},{5... | collective-permute-start | bytes 393224 | tf_op jit(solution)/shard_map/ppermute | solution.py:314
  26.0 0.9 %finish.2 = bf16[128,512]{1,0:T(8,128)(2,1)S(1)} custom-call(s32[2]{0:T(128)S(1)} %pad_add_fusion.at_ref, bf16[8,16,1024]{2,1,0:T(8,128)(2,1)S(1)} %all-to-all-done.ends_ref, f32[16,1024]{1,0:T(8,128)S(1)} %get-tuple-element.27.step_ref, bf16[128,2048]{1,0:T(8,128)(2,1)S(1)} %get-tuple-element.31.lift_ref, ...), custom_call_target="tpu_custom_call" | custom-call | flops 3000000000 | bytes 30000000 | tf_op jit(solution)/shard_map/finish/pallas_call | solution.py:55
  26.9 0.1 collective-permute-done.1
  27.0 3.7 %collective-permute-start.2 = (bf16[256,512]{1,0:T(8,128)(2,1)S(1)}, bf16[256,512]{1,0:T(8,128)(2,1)S(1)}, u32[]{:S(2)}, u32[]{:S(2)}) collective-permute-start(bf16[256,512]{1,0:T(8,128)(2,1)S(1)} %pad_maximum_fusion.own_ref), channel_id=1, source_target_pairs={{0,3},{1,2},{2,1},{3,0},{4,7},{5,6},{6,5},{7,4},{8,11},{9,10},{10,... | collective-permute-start | bytes 786440 | tf_op jit(solution)/shard_map/ppermute | solution.py:323
  30.7 2.5 %collective-permute-start.7 = (bf16[512,1024]{1,0:T(8,128)(2,1)}, bf16[512,1024]{1,0:T(8,128)(2,1)S(1)}, u32[]{:S(2)}, u32[]{:S(2)}) collective-permute-start(bf16[512,1024]{1,0:T(8,128)(2,1)} %collective-permute-done.6.rest_1_), channel_id=1, source_target_pairs={{0,16},{4,12},{8,24},{12,4},{16,0},{20,28},{24,8},{28,20},{1,17},{... | collective-permute-start | bytes 3145736 | tf_op jit(solution)/shard_map/ppermute | solution.py:314
  33.2 0.1 stack.39.at_ref
  33.3 4.8 %collective-permute-done.2.across_ref = bf16[256,512]{1,0:T(8,128)(2,1)S(1)} collective-permute-done((bf16[256,512]{1,0:T(8,128)(2,1)S(1)}, bf16[256,512]{1,0:T(8,128)(2,1)S(1)}, u32[]{:S(2)}, u32[]{:S(2)}) %collective-permute-start.2) | collective-permute-done | bytes 262176 | tf_op jit(solution)/shard_map/ppermute | solution.py:323
  38.0 4.8 %collective-permute-start.4 = (bf16[256,512]{1,0:T(8,128)(2,1)S(1)}, bf16[256,512]{1,0:T(8,128)(2,1)S(1)}, u32[]{:S(2)}, u32[]{:S(2)}) collective-permute-start(bf16[256,512]{1,0:T(8,128)(2,1)S(1)} %collective-permute-done.2.across_ref), channel_id=1, source_target_pairs={{0,1},{1,0},{2,3},{3,2},{4,5},{5,4},{6,7},{7,6},{8,9},{9,8},{10,11... | collective-permute-start | bytes 786440 | tf_op jit(solution)/shard_map/ppermute | solution.py:323
  42.9 0.4 collective-permute-done.5.beside_ref
  43.2 3.5 %early.1 = (f32[256,1024]{1,0:T(8,128)S(1)}, bf16[512,1024]{1,0:T(8,128)(2,1)S(1)}, bf16[256,512]{1,0:T(8,128)(2,1)S(1)}) custom-call(s32[5]{0:T(128)S(1)} %stack.39.at_ref, bf16[256,512]{1,0:T(8,128)(2,1)S(1)} %pad_maximum_fusion.own_ref, bf16[256,512]{1,0:T(8,128)(2,1)S(1)} %collective-permute-done.5.beside_ref, ...), custom_call_target="tpu_custom_call" | custom-call | flops 10000000000 | bytes 100000000 | tf_op jit(solution)/shard_map/early/pallas_call | solution.py:55
  46.8 2.1 %collective-permute-done.4.beyond_ref = bf16[256,512]{1,0:T(8,128)(2,1)S(1)} collective-permute-done((bf16[256,512]{1,0:T(8,128)(2,1)S(1)}, bf16[256,512]{1,0:T(8,128)(2,1)S(1)}, u32[]{:S(2)}, u32[]{:S(2)}) %collective-permute-start.4) | collective-permute-done | bytes 262176 | tf_op jit(solution)/shard_map/ppermute | solution.py:323
  48.9 1.0 %late.3 = bf16[128,1024]{1,0:T(8,128)(2,1)S(1)} custom-call(s32[5]{0:T(128)S(1)} %stack.39.at_ref, bf16[256,512]{1,0:T(8,128)(2,1)S(1)} %collective-permute-done.4.beyond_ref, f32[256,1024]{1,0:T(8,128)S(1)} %get-tuple-element.37.total_ref, bf16[512,1024]{1,0:T(8,128)(2,1)S(1)} %get-tuple-element.38.rows_ref, ...), custom_call_target="tpu_custom_call" | custom-call | tf_op jit(solution)/shard_map/late/pallas_call | solution.py:55
  49.9 0.1 collective-permute-start.8
  50.0 1.0 %late.2 = f32[128,1024]{1,0:T(8,128)S(1)} custom-call(s32[5]{0:T(128)S(1)} %stack.39.at_ref, bf16[256,512]{1,0:T(8,128)(2,1)S(1)} %collective-permute-done.4.beyond_ref, f32[256,1024]{1,0:T(8,128)S(1)} %get-tuple-element.37.total_ref, bf16[512,1024]{1,0:T(8,128)(2,1)S(1)} %get-tuple-element.38.rows_ref, bf16[256,512]{1,0:T(8,128)(2,1)S(1)} %get-tuple-element.39.block_ref, ...), custom_call_target="tpu_custom_call" | custom-call | tf_op jit(solution)/shard_map/late/pallas_call | solution.py:55
  51.0 0.5 collective-permute-done.8
  51.5 0.8 %add_convert_fusion = bf16[128,1024]{1,0:T(8,128)(2,1)} fusion(f32[128,1024]{1,0:T(8,128)S(1)} %late.2, bf16[128,1024]{1,0:T(8,128)(2,1)S(1)} %collective-permute-done.8), kind=kLoop, calls=%fused_computation | loop fusion | flops 393216 | bytes 1048576 | tf_op jit(solution)/shard_map/convert_element_type | solution.py:443
  (16 shorter events, 0.1 us)
Async XLA Ops:
  0.0 1.1 %copy-start = (bf16[3,1024,128]{2,1,0:T(8,128)(2,1)S(1)}, bf16[3,1024,128]{2,1,0:T(8,128)(2,1)}, u32[]{:S(2)}) copy-start(bf16[3,1024,128]{2,1,0:T(8,128)(2,1)} %streams_ref.3) | copy-start | bytes 2359300
  1.1 5.3 %copy-start.1 = (bf16[3,1024,128]{2,1,0:T(8,128)(2,1)S(1)}, bf16[3,1024,128]{2,1,0:T(8,128)(2,1)}, u32[]{:S(2)}) copy-start(bf16[3,1024,128]{2,1,0:T(8,128)(2,1)} %streams_ref.3) | copy-start | bytes 2359300
  1.4 9.2 %collective-permute-start = (bf16[3,8,1024]{2,1,0:T(8,128)(2,1)S(1)}, bf16[3,8,1024]{2,1,0:T(8,128)(2,1)S(1)}, u32[]{:S(2)}, u32[]{:S(2)}) collective-permute-start(bf16[3,8,1024]{2,1,0:T(8,128)(2,1)S(1)} %tails.1), channel_id=1, source_target_pairs={{0,4},{4,8},{8,12},{12,16},{16,20},{20,24},{24,28},{1,5},{5,9},{9,... | collective-permute-start | bytes 147464 | tf_op jit(solution)/shard_map/ppermute | solution.py:26
  3.8 26.9 %collective-permute-start.6 = (bf16[512,1024]{1,0:T(8,128)(2,1)}, bf16[512,1024]{1,0:T(8,128)(2,1)}, u32[]{:S(2)}, u32[]{:S(2)}) collective-permute-start(bf16[512,1024]{1,0:T(8,128)(2,1)} %rest_0_.1), channel_id=1, source_target_pairs={{0,8},{4,20},{8,0},{12,28},{16,24},{20,4},{24,16},{28,12},{1,9},{5... | collective-permute-start | bytes 3145736 | tf_op jit(solution)/shard_map/ppermute | solution.py:314
  6.4 0.7 %copy-start.5 = (f32[1024]{0:T(1024)S(1)}, f32[1024]{0:T(1024)}, u32[]{:S(2)}) copy-start(f32[1024]{0:T(1024)} %param.10) | copy-start | bytes 12292
  6.4 0.7 %copy-start.4 = (f32[128,16]{0,1:T(8,128)S(1)}, f32[128,16]{0,1:T(8,128)}, u32[]{:S(2)}) copy-start(f32[128,16]{0,1:T(8,128)} %param.8) | copy-start | bytes 24580
  6.4 0.7 %copy-start.3 = (f32[128,16]{0,1:T(8,128)S(1)}, f32[128,16]{0,1:T(8,128)}, u32[]{:S(2)}) copy-start(f32[128,16]{0,1:T(8,128)} %param.9) | copy-start | bytes 24580
  7.1 0.9 %copy-start.2 = (f32[3,7,1024]{2,1,0:T(8,128)S(1)}, f32[3,7,1024]{2,1,0:T(8,128)}, u32[]{:S(2)}) copy-start(f32[3,7,1024]{2,1,0:T(8,128)} %taps_ref.3) | copy-start | bytes 258052
  10.6 5.3 %copy-start.6 = (bf16[512,1024]{1,0:T(8,128)(2,1)S(1)}, bf16[512,1024]{1,0:T(8,128)(2,1)}, u32[]{:S(2)}) copy-start(bf16[512,1024]{1,0:T(8,128)(2,1)} %rest_0_.1) | copy-start | bytes 3145732
  12.2 12.3 %all-to-all-start = ((bf16[8,16,1024]{2,1,0:T(8,128)(2,1)}), bf16[8,16,1024]{2,1,0:T(8,128)(2,1)S(1)}, u32[]{:S(2)}, u32[]{:S(2)}) async-start(bf16[8,16,1024]{2,1,0:T(8,128)(2,1)} %get-tuple-element.26), calls=%async_computation | async-start | bytes 524288 | tf_op jit(solution)/shard_map/all_to_all | solution.py:363
  15.9 22.1 %collective-permute-start.3 = (bf16[512,1024]{1,0:T(8,128)(2,1)S(1)}, bf16[512,1024]{1,0:T(8,128)(2,1)}, u32[]{:S(2)}, u32[]{:S(2)}) collective-permute-start(bf16[512,1024]{1,0:T(8,128)(2,1)S(1)} %copy-done.6), channel_id=1, source_target_pairs={{0,16},{4,12},{8,24},{12,4},{16,0},{20,28},{24,8},{28,20},{1,17},{... | collective-permute-start | bytes 3145736 | tf_op jit(solution)/shard_map/ppermute | solution.py:314
  25.4 1.5 %collective-permute-start.1 = (bf16[128,512]{1,0:T(8,128)(2,1)S(1)}, bf16[128,512]{1,0:T(8,128)(2,1)S(1)}, u32[]{:S(2)}, u32[]{:S(2)}) collective-permute-start(bf16[128,512]{1,0:T(8,128)(2,1)S(1)} %finish.3), channel_id=1, source_target_pairs={{0,4},{4,0},{8,12},{12,8},{16,20},{20,16},{24,28},{28,24},{1,5},{5... | collective-permute-start | bytes 393224 | tf_op jit(solution)/shard_map/ppermute | solution.py:314
  27.0 11.1 %collective-permute-start.2 = (bf16[256,512]{1,0:T(8,128)(2,1)S(1)}, bf16[256,512]{1,0:T(8,128)(2,1)S(1)}, u32[]{:S(2)}, u32[]{:S(2)}) collective-permute-start(bf16[256,512]{1,0:T(8,128)(2,1)S(1)} %pad_maximum_fusion.own_ref), channel_id=1, source_target_pairs={{0,3},{1,2},{2,1},{3,0},{4,7},{5,6},{6,5},{7,4},{8,11},{9,10},{10,... | collective-permute-start | bytes 786440 | tf_op jit(solution)/shard_map/ppermute | solution.py:323
  30.7 12.5 %collective-permute-start.5 = (bf16[256,512]{1,0:T(8,128)(2,1)S(1)}, bf16[256,512]{1,0:T(8,128)(2,1)S(1)}, u32[]{:S(2)}, u32[]{:S(2)}) collective-permute-start(bf16[256,512]{1,0:T(8,128)(2,1)S(1)} %pad_maximum_fusion.own_ref), channel_id=1, source_target_pairs={{0,1},{1,0},{2,3},{3,2},{4,5},{5,4},{6,7},{7,6},{8,9},{9,8},{10,11... | collective-permute-start | bytes 786440 | tf_op jit(solution)/shard_map/ppermute | solution.py:323
  30.7 18.2 %collective-permute-start.7 = (bf16[512,1024]{1,0:T(8,128)(2,1)}, bf16[512,1024]{1,0:T(8,128)(2,1)S(1)}, u32[]{:S(2)}, u32[]{:S(2)}) collective-permute-start(bf16[512,1024]{1,0:T(8,128)(2,1)} %collective-permute-done.6.rest_1_), channel_id=1, source_target_pairs={{0,16},{4,12},{8,24},{12,4},{16,0},{20,28},{24,8},{28,20},{1,17},{... | collective-permute-start | bytes 3145736 | tf_op jit(solution)/shard_map/ppermute | solution.py:314
  38.0 10.8 %collective-permute-start.4 = (bf16[256,512]{1,0:T(8,128)(2,1)S(1)}, bf16[256,512]{1,0:T(8,128)(2,1)S(1)}, u32[]{:S(2)}, u32[]{:S(2)}) collective-permute-start(bf16[256,512]{1,0:T(8,128)(2,1)S(1)} %collective-permute-done.2.across_ref), channel_id=1, source_target_pairs={{0,1},{1,0},{2,3},{3,2},{4,5},{5,4},{6,7},{7,6},{8,9},{9,8},{10,11... | collective-permute-start | bytes 786440 | tf_op jit(solution)/shard_map/ppermute | solution.py:323
  49.9 1.6 %collective-permute-start.8 = (bf16[128,1024]{1,0:T(8,128)(2,1)S(1)}, bf16[128,1024]{1,0:T(8,128)(2,1)S(1)}, u32[]{:S(2)}, u32[]{:S(2)}) collective-permute-start(bf16[128,1024]{1,0:T(8,128)(2,1)S(1)} %late.3), channel_id=1, source_target_pairs={{0,4},{4,0},{8,12},{12,8},{16,20},{20,16},{24,28},{28,24},{1,5},{5... | collective-permute-start | bytes 786440 | tf_op jit(solution)/shard_map/ppermute | solution.py:314

commit v15 on v14

--- a/solution.py
+++ b/solution.py
@@ -94,7 +94,7 @@
 
 def prepare_kernel(
     streams_ref, taps_ref, rates_ref, residues_ref, skip_ref,
-    heads_ref, query_ref, gated_ref, decay_ref, step_ref, coef_ref, direct_ref, padded_ref,
+    heads_ref, query_ref, gated_ref, decay_ref, step_ref, response_ref, lift_ref, direct_ref, padded_ref,
 ):
     channels, length = streams_ref.shape[1:]
     poles, groups = rates_ref.shape
@@ -103,7 +103,9 @@
     unit = identity(length)
     lag = (length - 1) - iota((poles, length), 1).astype(F32)
     owner = iota((poles, TILE), 1) // width
-    coef_ref[...] = residues_ref[...] * jnp.sqrt(2.0 * rates_ref[...]) / math.sqrt(poles)
+    time = iota((poles, length), 1).astype(F32)
+    member = (iota((in_tile, in_tile * poles), 1) // poles == iota((in_tile, in_tile * poles), 0)).astype(BF16)
+    scale = residues_ref[...] * jnp.sqrt(2.0 * rates_ref[...]) / math.sqrt(poles)
     direct_ref[...] = skip_ref[...]
 
     def turn(index):
@@ -114,17 +116,26 @@
             padded_ref[index * 3 + stream, ROWS:, :] = tokens
             heads_ref[stream, :, chans] = tokens[:ROWS]
 
-    def decays(index):
-        rates = pltpu.roll(rates_ref[...], groups - index * in_tile, 1)
-        decay = []
+    def factors(index):
+        shift = groups - index * in_tile
+        rates = pltpu.roll(rates_ref[...], shift, 1)
+        coef = pltpu.roll(scale, shift, 1)
+        once = jnp.exp(-rates)
+        decay, impulse, lift = [], [], []
         wide = jnp.zeros((poles, TILE), F32)
         for g in range(in_tile):
             rate = jnp.broadcast_to(rates[:, g : g + 1], (poles, length))
             decay.append(jnp.exp(-rate * lag))
+            impulse.append(jnp.broadcast_to(coef[:, g : g + 1], (poles, length)) * jnp.exp(-rate * time))
+            lift.append(impulse[-1] * once[:, g : g + 1])
             wide = jnp.where(owner == g, rate[:, :TILE], wide)
         step_ref[:, tile_of(index)] = jnp.exp(-wide * length)
+        states = tile_of(index, in_tile * poles)
         for part, value in enumerate(halves(jnp.concatenate(decay, axis=0))):
-            decay_ref[part, tile_of(index, in_tile * poles), :] = value
+            decay_ref[part, states, :] = value
+        high, low = halves(jnp.concatenate(impulse, axis=0))
+        response_ref[pl.ds(pl.multiple_of(index * in_tile, in_tile), in_tile), :] = dot(member, high) + dot(member, low)
+        lift_ref[:, states] = turned(jnp.concatenate(lift, axis=0).astype(BF16), unit).astype(BF16)
 
     def filters(index):
         chans = tile_of(index)
@@ -135,7 +146,7 @@
         gated_ref[:, chans] = left * right
 
     unrolled(channels // TILE, turn)
-    unrolled(channels // TILE, decays)
+    unrolled(channels // TILE, factors)
     unrolled(channels // TILE, filters)
 
 
@@ -172,35 +183,16 @@
     unrolled(channels // TILE, leave)
 
 
-def inside_kernel(
-    gated_ref, skip_ref, rates_ref, coef_ref, lift_ref, base_ref, response_ref, signal_ref, sum_ref
-):
+def inside_kernel(gated_ref, skip_ref, response_ref, base_ref, signal_ref, sum_ref):
     length, channels = gated_ref.shape
-    poles, groups = rates_ref.shape
+    groups = response_ref.shape[0]
     width = channels // groups
     in_tile = TILE // width
     tiles = channels // TILE
     strip = STRIP
     unit = identity(length)
-    time = iota((poles, length), 1).astype(F32)
-    member = (iota((in_tile, in_tile * poles), 1) // poles == iota((in_tile, in_tile * poles), 0)).astype(BF16)
     lane = iota((width, length), 1)
     causal = iota((strip, length), 1) >= iota((strip, length), 0)
-
-    def factors(index):
-        shift = groups - index * in_tile
-        rates = pltpu.roll(rates_ref[...], shift, 1)
-        coef = pltpu.roll(coef_ref[...], shift, 1)
-        once = jnp.exp(-rates)
-        impulse, lift = [], []
-        for g in range(in_tile):
-            term = jnp.broadcast_to(coef[:, g : g + 1], (poles, length)) * jnp.exp(-rates[:, g : g + 1] * time)
-            impulse.append(term)
-            lift.append(term * once[:, g : g + 1])
-        high, low = halves(jnp.concatenate(impulse, axis=0))
-        response_ref[pl.ds(pl.multiple_of(index * in_tile, in_tile), in_tile), :] = dot(member, high) + dot(member, low)
-        lift = jnp.concatenate(lift, axis=0).astype(BF16)
-        lift_ref[:, tile_of(index, in_tile * poles)] = turned(lift, unit).astype(BF16)
 
     def signals(index):
         gated = gated_ref[:, tile_of(index)]
@@ -237,7 +229,6 @@
         base_ref[:, chans] = turned(high, unit) + turned(low, unit) + direct
 
     unrolled(tiles, signals)
-    unrolled(tiles, factors)
     unrolled(tiles, products)
     unrolled(tiles, back)
 
@@ -300,12 +291,18 @@
             rows_ref[...] = weight_ref[at]
 
 
-def late_kernel(first, at_ref, beyond_ref, total_ref, rows_ref, block_ref, weight_ref, out_ref):
+def joined_kernel(at_ref, total_ref, rows_ref, block_ref, weight_ref, out_ref, last_ref):
+    out_ref[...] = total_ref[...] + dot(block_ref[...], weight_ref[...])
+    last_ref[...] = rows_ref[...]
+
+    @pl.when(at_ref[4] == at_ref[0] ^ 2)
+    def _():
+        last_ref[...] = weight_ref[...]
+
+
+def late_kernel(first, beyond_ref, total_ref, rows_ref, out_ref):
     tokens = pl.ds(first, out_ref.shape[0])
-    beyond = beyond_ref[tokens, :]
-    block = jnp.where(at_ref[4] == at_ref[0] ^ 2, beyond, block_ref[tokens, :])
-    total = total_ref[tokens, :] + dot(block, weight_ref[...]) + dot(beyond, rows_ref[...])
-    out_ref[...] = total.astype(out_ref.dtype)
+    out_ref[...] = (total_ref[tokens, :] + dot(beyond_ref[tokens, :], rows_ref[...])).astype(out_ref.dtype)
 
 
 def swap(value, *bits):
@@ -337,7 +334,7 @@
     if square:
         near = swap(out_weight, 2, 4)
     tiles = channels // TILE
-    heads, query, gated, decay, step, coef, skip = call(
+    heads, query, gated, decay, step, response, lift, skip = call(
         prepare_kernel,
         [
             ((3, ROWS, channels), F32),
@@ -345,7 +342,8 @@
             ((length, channels), F32),
             ((2, groups * poles, length), BF16),
             ((poles, channels), F32),
-            ((poles, groups), F32),
+            ((groups, length), F32),
+            ((length, groups * poles), BF16),
             ((1, channels), F32),
         ],
         "prepare",
@@ -361,20 +359,19 @@
         scratch=[pltpu.VMEM((3 * tiles, 2 * ROWS, TILE), F32)],
     )
     all_ends = lax.all_to_all(ends, "ctx", split_axis=0, concat_axis=0, tiled=True)
-    lift, base = call(
+    (base,) = call(
         inside_kernel,
-        [((length, groups * poles), BF16), ((length, channels), F32)],
+        [((length, channels), F32)],
         "inside",
-        gated, skip, rates, coef,
+        gated, skip, response,
         scratch=[
-            pltpu.VMEM((groups, length), F32),
             pltpu.VMEM((length // STRIP, channels, STRIP), BF16),
             pltpu.VMEM((channels, length), F32),
         ],
         flops=10**9,
     )
     if square:
-        other_near = swap(after(out_weight, gated), 4, 2)
+        other_near = swap(after(out_weight, (gated, near)), 4, 2)
     me = lax.axis_index("ctx").astype(jnp.int32)
     core = me % CORES
     smem = [pl.BlockSpec(memory_space=pltpu.SMEM)]
@@ -401,7 +398,7 @@
     block = jnp.concatenate([mine, swap(other, 1)], axis=0)
     layer = lax.axis_index("tp").astype(jnp.int32)
     beside, across = trade(block, 1), trade(block, 3)
-    beyond = trade(after(across, other_near) if square else across, 1)
+    beyond = trade(after(across, (beside, other_near)) if square else across, 1)
     if square:
         diagonal = swap(after(near, block), 4, 2)
         weight = (out_weight, near, other_near, diagonal)
@@ -428,14 +425,21 @@
         ],
         flops=10**10,
     )
+    total, last_rows = call(
+        joined_kernel,
+        [((CORES * length, features), F32), ((share, features), BF16)],
+        "joined",
+        at, total, last_rows, last_block, latest,
+        specs=smem + whole(4),
+        flops=0,
+    )
     sides = []
     for side, kind in ((1, BF16), (0, F32)):
         sides += call(
             functools.partial(late_kernel, side * length),
             [((length, features), kind)],
             "late",
-            at, beyond, total, last_rows, last_block, latest,
-            specs=smem + whole(5),
+            beyond, total, last_rows,
             flops=0,
         )
     other, mine = sides

time: 52.6 us -> 54.2 us (1.030)
  waiting for transfers between devices: 9.81 us -> 18.1 us
  starting transfers between devices: 22.3 us -> 17 us
  Pallas kernels: 16.3 us -> 14.8 us
    ppermute x3, waiting for transfers between devices: 7.23 us -> 13.6 us  [trade(): lax.ppermute(value, 'tp', [(source, source ^ bits) for source in range(co...]
    ppermute x3, starting transfers between devices: 8.57 us -> 5.35 us  [trade(): lax.ppermute(value, 'tp', [(source, source ^ bits) for source in range(co...]
    ppermute x5, starting transfers between devices: 7.68 us -> 5.74 us  [swap(): return lax.ppermute(value, 'ctx', pairs)]
    pallas_call x9 -> x10, Pallas kernels: 16.3 us -> 14.8 us  [call(): pl.pallas_call(kernel, out_shape=tuple((jax.ShapeDtypeStruct(*out) for ou...]
    ppermute x5, waiting for transfers between devices: 0.59 us -> 1.62 us  [swap(): return lax.ppermute(value, 'ctx', pairs)]
    all_to_all x1, waiting for transfers between devices: 1.98 us -> 2.9 us  [local(): lax.all_to_all(ends, 'ctx', split_axis=0, concat_axis=0, tiled=True)]
    ppermute x1, starting transfers between devices: 2.37 us -> 1.5 us  [from_behind(): lax.ppermute(value, axis, [(source, source + steps) for source in range(l...]
    all_to_all x1, starting transfers between devices: 3.66 us -> 4.41 us  [local(): lax.all_to_all(ends, 'ctx', split_axis=0, concat_axis=0, tiled=True)]
  transfers between devices with their start and end apart: 10 -> 10, of which waited for: 6 -> 6; matrix products, arithmetic and copies ran while one was open for 0% -> 0% of each run, Pallas kernels for 29% -> 27%
where the time goes in v15:
time: 54.2 us; the launch traced here: 53.9 us
  waiting for transfers between devices  18.1 us (33%)
  starting transfers between devices  17 us (31%)
  Pallas kernels  14.8 us (27%)
  local copies, waits for them, and re-layouts  2.81 us (5%)
  other arithmetic  0.93 us (2%)
    pallas_call x10, Pallas kernels, call(): pl.pallas_call(kernel, out_shape=tuple((jax.ShapeDtypeStruct(*out) for ou...  14.8 us
    ppermute x3, waiting for transfers between devices, trade(): lax.ppermute(value, 'tp', [(source, source ^ bits) for source in range(co...  13.6 us
    ppermute x5, starting transfers between devices, swap(): return lax.ppermute(value, 'ctx', pairs)  5.74 us
    ppermute x3, starting transfers between devices, trade(): lax.ppermute(value, 'tp', [(source, source ^ bits) for source in range(co...  5.35 us
    all_to_all x1, starting transfers between devices, local(): lax.all_to_all(ends, 'ctx', split_axis=0, concat_axis=0, tiled=True)  4.41 us
    all_to_all x1, waiting for transfers between devices, local(): lax.all_to_all(ends, 'ctx', split_axis=0, concat_axis=0, tiled=True)  2.9 us
    unnamed x14, local copies, waits for them, and re-layouts  2.72 us
    ppermute x5, waiting for transfers between devices, swap(): return lax.ppermute(value, 'ctx', pairs)  1.62 us
  transfers between devices with their start and end apart: 10, of which 6 were waited for; matrix products, arithmetic and copies ran while one was open for 0% of the time, Pallas kernels for 27%

profile of v15, /device:TPU:0, one launch (start us, length us, event | category | flops | bytes accessed | tf_op | source)
XLA Modules:
  0.0 53.9 jit_solution(13550209455242244877)
XLA Ops:
  0.0 2.9 %collective-permute-start.4 = (bf16[512,1024]{1,0:T(8,128)(2,1)}, bf16[512,1024]{1,0:T(8,128)(2,1)}, u32[]{:S(2)}, u32[]{:S(2)}) collective-permute-start(bf16[512,1024]{1,0:T(8,128)(2,1)} %rest_0_.1), channel_id=1, source_target_pairs={{0,8},{4,20},{8,0},{12,28},{16,24},{20,4},{24,16},{28,12},{1,9},{5... | collective-permute-start | bytes 3145736 | tf_op jit(solution)/shard_map/ppermute | solution.py:311
  2.9 1.1 %copy-done = bf16[3,1024,128]{2,1,0:T(8,128)(2,1)S(1)} copy-done((bf16[3,1024,128]{2,1,0:T(8,128)(2,1)S(1)}, bf16[3,1024,128]{2,1,0:T(8,128)(2,1)}, u32[]{:S(2)}) %copy-start) | copy-done | bytes 786456
  4.1 0.3 tails.1
  4.4 1.5 %collective-permute-start = (bf16[3,8,1024]{2,1,0:T(8,128)(2,1)S(1)}, bf16[3,8,1024]{2,1,0:T(8,128)(2,1)S(1)}, u32[]{:S(2)}, u32[]{:S(2)}) collective-permute-start(bf16[3,8,1024]{2,1,0:T(8,128)(2,1)S(1)} %tails.1), channel_id=1, source_target_pairs={{0,4},{4,8},{8,12},{12,16},{16,20},{20,24},{24,28},{1,5},{5,9},{9,... | collective-permute-start | bytes 147464 | tf_op jit(solution)/shard_map/ppermute | solution.py:26
  5.9 0.6 %copy-done.5 = f32[1024]{0:T(1024)S(1)} copy-done((f32[1024]{0:T(1024)S(1)}, f32[1024]{0:T(1024)}, u32[]{:S(2)}) %copy-start.5) | copy-done | bytes 4120
  6.6 0.9 %copy-done.2 = f32[3,7,1024]{2,1,0:T(8,128)S(1)} copy-done((f32[3,7,1024]{2,1,0:T(8,128)S(1)}, f32[3,7,1024]{2,1,0:T(8,128)}, u32[]{:S(2)}) %copy-start.2) | copy-done | bytes 86040
  7.5 3.7 %prepare.1 = (f32[3,8,1024]{2,1,0:T(8,128)S(1)}, bf16[128,1024]{1,0:T(8,128)(2,1)S(1)}, f32[128,1024]{1,0:T(8,128)S(1)}, bf16[2,2048,128]{2,1,0:T(8,128)(2,1)S(1...) custom-call(bf16[3,1024,128]{2,1,0:T(8,128)(2,1)S(1)} %copy-done.1, ...), custom_call_target="tpu_custom_call" | custom-call | flops 1000000000 | bytes 10000000 | tf_op jit(solution)/shard_map/prepare/pallas_call | solution.py:55
  11.3 1.5 %states.1 = (bf16[8,16,1024]{2,1,0:T(8,128)(2,1)}, bf16[128,1024]{1,0:T(8,128)(2,1)S(1)}, f32[8,1024]{1,0:T(8,128)S(1)}) custom-call(bf16[3,8,1024]{2,1,0:T(8,128)(2,1)S(1)} %collective-permute-done.before_ref, f32[3,8,1024]{2,1,0:T(8,128)S(1)} %get-tuple-element.24.heads_ref, f32[3,7,1024]{2,1,0:T(8,128)S(1)} %copy-done.2, ...), custom_call_target="tpu_custom_call" | custom-call | flops 100000000 | bytes 1000000 | tf_op jit(solution)/shard_map/states/pallas_call | solution.py:55
  12.8 4.4 %all-to-all-start = ((bf16[8,16,1024]{2,1,0:T(8,128)(2,1)}), bf16[8,16,1024]{2,1,0:T(8,128)(2,1)S(1)}, u32[]{:S(2)}, u32[]{:S(2)}) async-start(bf16[8,16,1024]{2,1,0:T(8,128)(2,1)} %get-tuple-element.27), calls=%async_computation | async-start | bytes 524288 | tf_op jit(solution)/shard_map/all_to_all | solution.py:361
  17.2 0.1 pad_add_fusion.1.at_ref
  17.3 2.0 %collective-permute-start.5 = (bf16[512,1024]{1,0:T(8,128)(2,1)S(1)}, bf16[512,1024]{1,0:T(8,128)(2,1)}, u32[]{:S(2)}, u32[]{:S(2)}) collective-permute-start(bf16[512,1024]{1,0:T(8,128)(2,1)S(1)} %copy-done.6), channel_id=1, source_target_pairs={{0,16},{4,12},{8,24},{12,4},{16,0},{20,28},{24,8},{28,20},{1,17},{... | collective-permute-start | bytes 3145736 | tf_op jit(solution)/shard_map/ppermute | solution.py:311
  19.3 0.1 pad_add_fusion.at_ref
  19.4 2.3 %inside.1.base_ref = f32[128,1024]{1,0:T(8,128)S(1)} custom-call(bf16[128,1024]{1,0:T(8,128)(2,1)S(1)} %get-tuple-element.32.gated_ref, f32[1,1024]{1,0:T(1,128)S(1)} %get-tuple-element.33.skip_ref, f32[128,128]{1,0:T(8,128)S(1)} %get-tuple-element.34.response_ref), custom_call_target="tpu_custom_call" | custom-call | flops 1000000000 | bytes 10000000 | tf_op jit(solution)/shard_map/inside/pallas_call | solution.py:55
  21.7 2.9 %all-to-all-done.ends_ref = bf16[8,16,1024]{2,1,0:T(8,128)(2,1)S(1)} async-done(((bf16[8,16,1024]{2,1,0:T(8,128)(2,1)}), bf16[8,16,1024]{2,1,0:T(8,128)(2,1)S(1)}, u32[]{:S(2)}, u32[]{:S(2)}) %all-to-all-start) | async-done | bytes 262176 | tf_op jit(solution)/shard_map/all_to_all | solution.py:361
  24.6 0.9 %finish.3 = bf16[128,512]{1,0:T(8,128)(2,1)S(1)} custom-call(s32[2]{0:T(128)S(1)} %pad_add_fusion.1.at_ref, bf16[8,16,1024]{2,1,0:T(8,128)(2,1)S(1)} %all-to-all-done.ends_ref, f32[16,1024]{1,0:T(8,128)S(1)} %get-tuple-element.28.step_ref, bf16[128,2048]{1,0:T(8,128)(2,1)S(1)} %get-tuple-element.29.lift_ref, ...), custom_call_target="tpu_custom_call" | custom-call | flops 3000000000 | bytes 30000000 | tf_op jit(solution)/shard_map/finish/pallas_call | solution.py:55
  25.5 0.1 collective-permute-start.1
  25.6 0.9 %finish.2 = bf16[128,512]{1,0:T(8,128)(2,1)S(1)} custom-call(s32[2]{0:T(128)S(1)} %pad_add_fusion.at_ref, bf16[8,16,1024]{2,1,0:T(8,128)(2,1)S(1)} %all-to-all-done.ends_ref, f32[16,1024]{1,0:T(8,128)S(1)} %get-tuple-element.28.step_ref, bf16[128,2048]{1,0:T(8,128)(2,1)S(1)} %get-tuple-element.29.lift_ref, ...), custom_call_target="tpu_custom_call" | custom-call | flops 3000000000 | bytes 30000000 | tf_op jit(solution)/shard_map/finish/pallas_call | solution.py:55
  26.5 0.4 collective-permute-done.1
  27.0 3.7 %collective-permute-start.2 = (bf16[256,512]{1,0:T(8,128)(2,1)S(1)}, bf16[256,512]{1,0:T(8,128)(2,1)S(1)}, u32[]{:S(2)}, u32[]{:S(2)}) collective-permute-start(bf16[256,512]{1,0:T(8,128)(2,1)S(1)} %pad_maximum_fusion.own_ref), channel_id=1, source_target_pairs={{0,3},{1,2},{2,1},{3,0},{4,7},{5,6},{6,5},{7,4},{8,11},{9,10},{10,... | collective-permute-start | bytes 786440 | tf_op jit(solution)/shard_map/ppermute | solution.py:320
  30.6 0.6 %collective-permute-start.7 = (bf16[512,1024]{1,0:T(8,128)(2,1)}, bf16[512,1024]{1,0:T(8,128)(2,1)S(1)}, u32[]{:S(2)}, u32[]{:S(2)}) collective-permute-start(bf16[512,1024]{1,0:T(8,128)(2,1)} %collective-permute-done.4.rest_1_), channel_id=1, source_target_pairs={{0,16},{4,12},{8,24},{12,4},{16,0},{20,28},{24,8},{28,20},{1,17},{... | collective-permute-start | bytes 3145736 | tf_op jit(solution)/shard_map/ppermute | solution.py:311
  31.2 0.1 stack.44.at_ref
  31.3 6.7 %collective-permute-done.2.across_ref = bf16[256,512]{1,0:T(8,128)(2,1)S(1)} collective-permute-done((bf16[256,512]{1,0:T(8,128)(2,1)S(1)}, bf16[256,512]{1,0:T(8,128)(2,1)S(1)}, u32[]{:S(2)}, u32[]{:S(2)}) %collective-permute-start.2) | collective-permute-done | bytes 262176 | tf_op jit(solution)/shard_map/ppermute | solution.py:320
  38.1 4.9 %collective-permute-done.3.beside_ref = bf16[256,512]{1,0:T(8,128)(2,1)S(1)} collective-permute-done((bf16[256,512]{1,0:T(8,128)(2,1)S(1)}, bf16[256,512]{1,0:T(8,128)(2,1)S(1)}, u32[]{:S(2)}, u32[]{:S(2)}) %collective-permute-start.3) | collective-permute-done | bytes 262176 | tf_op jit(solution)/shard_map/ppermute | solution.py:320
  43.0 1.7 %collective-permute-start.6 = (bf16[256,512]{1,0:T(8,128)(2,1)S(1)}, bf16[256,512]{1,0:T(8,128)(2,1)S(1)}, u32[]{:S(2)}, u32[]{:S(2)}) collective-permute-start(bf16[256,512]{1,0:T(8,128)(2,1)S(1)} %collective-permute-done.2.across_ref), channel_id=1, source_target_pairs={{0,1},{1,0},{2,3},{3,2},{4,5},{5,4},{6,7},{7,6},{8,9},{9,8},{10,11... | collective-permute-start | bytes 786440 | tf_op jit(solution)/shard_map/ppermute | solution.py:320
  44.7 3.5 %early.1 = (f32[256,1024]{1,0:T(8,128)S(1)}, bf16[512,1024]{1,0:T(8,128)(2,1)S(1)}, bf16[256,512]{1,0:T(8,128)(2,1)S(1)}) custom-call(s32[5]{0:T(128)S(1)} %stack.44.at_ref, bf16[256,512]{1,0:T(8,128)(2,1)S(1)} %pad_maximum_fusion.own_ref, bf16[256,512]{1,0:T(8,128)(2,1)S(1)} %collective-permute-done.3.beside_ref, ...), custom_call_target="tpu_custom_call" | custom-call | flops 10000000000 | bytes 100000000 | tf_op jit(solution)/shard_map/early/pallas_call | solution.py:55
  48.2 1.0 %joined.1 = (f32[256,1024]{1,0:T(8,128)S(1)}, bf16[512,1024]{1,0:T(8,128)(2,1)S(1)}) custom-call(s32[5]{0:T(128)S(1)} %stack.44.at_ref, f32[256,1024]{1,0:T(8,128)S(1)} %get-tuple-element.37.total_ref, bf16[512,1024]{1,0:T(8,128)(2,1)S(1)} %get-tuple-element.38.rows_ref, bf16[256,512]{1,0:T(8,128)(2,1)S(1)} %get-tuple-element.39.block_ref, ...), custom_call_target="tpu_custom_call" | custom-call | tf_op jit(solution)/shard_map/joined/pallas_call | solution.py:55
  49.2 2.0 %collective-permute-done.6.beyond_ref = bf16[256,512]{1,0:T(8,128)(2,1)S(1)} collective-permute-done((bf16[256,512]{1,0:T(8,128)(2,1)S(1)}, bf16[256,512]{1,0:T(8,128)(2,1)S(1)}, u32[]{:S(2)}, u32[]{:S(2)}) %collective-permute-start.6) | collective-permute-done | bytes 262176 | tf_op jit(solution)/shard_map/ppermute | solution.py:320
  51.2 0.3 late.3
  51.5 0.1 collective-permute-start.8
  51.6 0.3 late.2
  51.9 1.2 %collective-permute-done.8 = bf16[128,1024]{1,0:T(8,128)(2,1)S(1)} collective-permute-done((bf16[128,1024]{1,0:T(8,128)(2,1)S(1)}, bf16[128,1024]{1,0:T(8,128)(2,1)S(1)}, u32[]{:S(2)}, u32[]{:S(2)}) %collective-permute-start.8) | collective-permute-done | bytes 262176 | tf_op jit(solution)/shard_map/ppermute | solution.py:311
  53.1 0.8 %add_convert_fusion = bf16[128,1024]{1,0:T(8,128)(2,1)} fusion(f32[128,1024]{1,0:T(8,128)S(1)} %late.2, bf16[128,1024]{1,0:T(8,128)(2,1)S(1)} %collective-permute-done.8), kind=kLoop, calls=%fused_computation | loop fusion | flops 393216 | bytes 1048576 | tf_op jit(solution)/shard_map/convert_element_type | solution.py:447
  (17 shorter events, 0.1 us)
Async XLA Ops:
  0.0 17.3 %collective-permute-start.4 = (bf16[512,1024]{1,0:T(8,128)(2,1)}, bf16[512,1024]{1,0:T(8,128)(2,1)}, u32[]{:S(2)}, u32[]{:S(2)}) collective-permute-start(bf16[512,1024]{1,0:T(8,128)(2,1)} %rest_0_.1), channel_id=1, source_target_pairs={{0,8},{4,20},{8,0},{12,28},{16,24},{20,4},{24,16},{28,12},{1,9},{5... | collective-permute-start | bytes 3145736 | tf_op jit(solution)/shard_map/ppermute | solution.py:311
  2.9 1.1 %copy-start = (bf16[3,1024,128]{2,1,0:T(8,128)(2,1)S(1)}, bf16[3,1024,128]{2,1,0:T(8,128)(2,1)}, u32[]{:S(2)}) copy-start(bf16[3,1024,128]{2,1,0:T(8,128)(2,1)} %streams_ref.3) | copy-start | bytes 2359300
  4.1 1.9 %copy-start.1 = (bf16[3,1024,128]{2,1,0:T(8,128)(2,1)S(1)}, bf16[3,1024,128]{2,1,0:T(8,128)(2,1)}, u32[]{:S(2)}) copy-start(bf16[3,1024,128]{2,1,0:T(8,128)(2,1)} %streams_ref.3) | copy-start | bytes 2359300
  4.4 6.9 %collective-permute-start = (bf16[3,8,1024]{2,1,0:T(8,128)(2,1)S(1)}, bf16[3,8,1024]{2,1,0:T(8,128)(2,1)S(1)}, u32[]{:S(2)}, u32[]{:S(2)}) collective-permute-start(bf16[3,8,1024]{2,1,0:T(8,128)(2,1)S(1)} %tails.1), channel_id=1, source_target_pairs={{0,4},{4,8},{8,12},{12,16},{16,20},{20,24},{24,28},{1,5},{5,9},{9,... | collective-permute-start | bytes 147464 | tf_op jit(solution)/shard_map/ppermute | solution.py:26
  5.9 0.7 %copy-start.5 = (f32[1024]{0:T(1024)S(1)}, f32[1024]{0:T(1024)}, u32[]{:S(2)}) copy-start(f32[1024]{0:T(1024)} %param.10) | copy-start | bytes 12292
  5.9 0.7 %copy-start.4 = (f32[128,16]{0,1:T(8,128)S(1)}, f32[128,16]{0,1:T(8,128)}, u32[]{:S(2)}) copy-start(f32[128,16]{0,1:T(8,128)} %param.9) | copy-start | bytes 24580
  5.9 0.7 %copy-start.3 = (f32[128,16]{0,1:T(8,128)S(1)}, f32[128,16]{0,1:T(8,128)}, u32[]{:S(2)}) copy-start(f32[128,16]{0,1:T(8,128)} %param.8) | copy-start | bytes 24580
  6.6 0.9 %copy-start.2 = (f32[3,7,1024]{2,1,0:T(8,128)S(1)}, f32[3,7,1024]{2,1,0:T(8,128)}, u32[]{:S(2)}) copy-start(f32[3,7,1024]{2,1,0:T(8,128)} %taps_ref.3) | copy-start | bytes 258052
  11.3 6.0 %copy-start.6 = (bf16[512,1024]{1,0:T(8,128)(2,1)S(1)}, bf16[512,1024]{1,0:T(8,128)(2,1)}, u32[]{:S(2)}) copy-start(bf16[512,1024]{1,0:T(8,128)(2,1)} %rest_0_.1) | copy-start | bytes 3145732
  12.8 11.8 %all-to-all-start = ((bf16[8,16,1024]{2,1,0:T(8,128)(2,1)}), bf16[8,16,1024]{2,1,0:T(8,128)(2,1)S(1)}, u32[]{:S(2)}, u32[]{:S(2)}) async-start(bf16[8,16,1024]{2,1,0:T(8,128)(2,1)} %get-tuple-element.27), calls=%async_computation | async-start | bytes 524288 | tf_op jit(solution)/shard_map/all_to_all | solution.py:361
  17.3 25.7 %collective-permute-start.5 = (bf16[512,1024]{1,0:T(8,128)(2,1)S(1)}, bf16[512,1024]{1,0:T(8,128)(2,1)}, u32[]{:S(2)}, u32[]{:S(2)}) collective-permute-start(bf16[512,1024]{1,0:T(8,128)(2,1)S(1)} %copy-done.6), channel_id=1, source_target_pairs={{0,16},{4,12},{8,24},{12,4},{16,0},{20,28},{24,8},{28,20},{1,17},{... | collective-permute-start | bytes 3145736 | tf_op jit(solution)/shard_map/ppermute | solution.py:311
  25.5 1.4 %collective-permute-start.1 = (bf16[128,512]{1,0:T(8,128)(2,1)S(1)}, bf16[128,512]{1,0:T(8,128)(2,1)S(1)}, u32[]{:S(2)}, u32[]{:S(2)}) collective-permute-start(bf16[128,512]{1,0:T(8,128)(2,1)S(1)} %finish.3), channel_id=1, source_target_pairs={{0,4},{4,0},{8,12},{12,8},{16,20},{20,16},{24,28},{28,24},{1,5},{5... | collective-permute-start | bytes 393224 | tf_op jit(solution)/shard_map/ppermute | solution.py:311
  27.0 11.1 %collective-permute-start.2 = (bf16[256,512]{1,0:T(8,128)(2,1)S(1)}, bf16[256,512]{1,0:T(8,128)(2,1)S(1)}, u32[]{:S(2)}, u32[]{:S(2)}) collective-permute-start(bf16[256,512]{1,0:T(8,128)(2,1)S(1)} %pad_maximum_fusion.own_ref), channel_id=1, source_target_pairs={{0,3},{1,2},{2,1},{3,0},{4,7},{5,6},{6,5},{7,4},{8,11},{9,10},{10,... | collective-permute-start | bytes 786440 | tf_op jit(solution)/shard_map/ppermute | solution.py:320
  30.6 12.3 %collective-permute-start.3 = (bf16[256,512]{1,0:T(8,128)(2,1)S(1)}, bf16[256,512]{1,0:T(8,128)(2,1)S(1)}, u32[]{:S(2)}, u32[]{:S(2)}) collective-permute-start(bf16[256,512]{1,0:T(8,128)(2,1)S(1)} %pad_maximum_fusion.own_ref), channel_id=1, source_target_pairs={{0,1},{1,0},{2,3},{3,2},{4,5},{5,4},{6,7},{7,6},{8,9},{9,8},{10,11... | collective-permute-start | bytes 786440 | tf_op jit(solution)/shard_map/ppermute | solution.py:320
  30.6 17.6 %collective-permute-start.7 = (bf16[512,1024]{1,0:T(8,128)(2,1)}, bf16[512,1024]{1,0:T(8,128)(2,1)S(1)}, u32[]{:S(2)}, u32[]{:S(2)}) collective-permute-start(bf16[512,1024]{1,0:T(8,128)(2,1)} %collective-permute-done.4.rest_1_), channel_id=1, source_target_pairs={{0,16},{4,12},{8,24},{12,4},{16,0},{20,28},{24,8},{28,20},{1,17},{... | collective-permute-start | bytes 3145736 | tf_op jit(solution)/shard_map/ppermute | solution.py:311
  43.0 8.2 %collective-permute-start.6 = (bf16[256,512]{1,0:T(8,128)(2,1)S(1)}, bf16[256,512]{1,0:T(8,128)(2,1)S(1)}, u32[]{:S(2)}, u32[]{:S(2)}) collective-permute-start(bf16[256,512]{1,0:T(8,128)(2,1)S(1)} %collective-permute-done.2.across_ref), channel_id=1, source_target_pairs={{0,1},{1,0},{2,3},{3,2},{4,5},{5,4},{6,7},{7,6},{8,9},{9,8},{10,11... | collective-permute-start | bytes 786440 | tf_op jit(solution)/shard_map/ppermute | solution.py:320
  51.5 1.6 %collective-permute-start.8 = (bf16[128,1024]{1,0:T(8,128)(2,1)S(1)}, bf16[128,1024]{1,0:T(8,128)(2,1)S(1)}, u32[]{:S(2)}, u32[]{:S(2)}) collective-permute-start(bf16[128,1024]{1,0:T(8,128)(2,1)S(1)} %late.3), channel_id=1, source_target_pairs={{0,4},{4,0},{8,12},{12,8},{16,20},{20,16},{24,28},{28,24},{1,5},{5... | collective-permute-start | bytes 786440 | tf_op jit(solution)/shard_map/ppermute | solution.py:311

commit v16 on v15

--- a/solution.py
+++ b/solution.py
@@ -76,12 +76,23 @@
     lax.fori_loop(0, count, step, 0, unroll=math.gcd(count, 4))
 
 
-def tails_kernel(streams_ref, tails_ref):
+def tails_kernel(*refs):
+    count = len(refs) // 2 - 1
+    sources, tails_ref, fetched, sems = refs[:count], refs[count], refs[count + 1 : -1], refs[-1]
+    copies = [
+        pltpu.make_async_copy(source, target, sems.at[at]) for at, (source, target) in enumerate(zip(sources, fetched))
+    ]
+    for copy in copies:
+        copy.start()
+    streams_ref = fetched[0]
     length = streams_ref.shape[2]
     pick = (iota((2 * ROWS, length), 1) == iota((2 * ROWS, length), 0) + (length - ROWS)).astype(BF16)
+    copies[0].wait()
     for stream in range(streams_ref.shape[0]):
         rows = dot(pick, streams_ref[stream], CONTRACT_LANES)
         tails_ref[stream] = rows[:ROWS].astype(BF16)
+    for copy in copies[1:]:
+        copy.wait()
 
 
 def short_conv(stream, chans, rows, padded, taps_ref):
@@ -93,8 +104,8 @@
 
 
 def prepare_kernel(
-    streams_ref, taps_ref, rates_ref, residues_ref, skip_ref,
-    heads_ref, query_ref, gated_ref, decay_ref, step_ref, response_ref, lift_ref, direct_ref, padded_ref,
+    streams_ref, taps_ref, rates_ref, residues_ref,
+    heads_ref, query_ref, gated_ref, decay_ref, step_ref, response_ref, lift_ref, padded_ref,
 ):
     channels, length = streams_ref.shape[1:]
     poles, groups = rates_ref.shape
@@ -106,7 +117,6 @@
     time = iota((poles, length), 1).astype(F32)
     member = (iota((in_tile, in_tile * poles), 1) // poles == iota((in_tile, in_tile * poles), 0)).astype(BF16)
     scale = residues_ref[...] * jnp.sqrt(2.0 * rates_ref[...]) / math.sqrt(poles)
-    direct_ref[...] = skip_ref[...]
 
     def turn(index):
         chans = tile_of(index)
@@ -328,13 +338,20 @@
     share = channels // CORES
     square = blocks == 8 and rows == share
 
-    rates, residues, skip = rates.T, residues.T, skip[None, :]
-    (tails,) = call(tails_kernel, [((3, ROWS, channels), BF16)], "tails", streams)
+    inputs = (streams, conv_weight, rates.T, residues.T, skip[None, :])
+    tails, streams, conv_weight, rates, residues, skip = call(
+        tails_kernel,
+        [((3, ROWS, channels), BF16)] + [(part.shape, part.dtype) for part in inputs],
+        "tails",
+        *(pltpu.with_memory_space_constraint(part, pltpu.HBM) for part in inputs),
+        specs=[pl.BlockSpec(memory_space=pltpu.HBM)] * len(inputs),
+        scratch=[pltpu.SemaphoreType.DMA((len(inputs),))],
+    )
     before = from_behind(tails, "ctx", 1)
     if square:
         near = swap(out_weight, 2, 4)
     tiles = channels // TILE
-    heads, query, gated, decay, step, response, lift, skip = call(
+    heads, query, gated, decay, step, response, lift = call(
         prepare_kernel,
         [
             ((3, ROWS, channels), F32),
@@ -344,10 +361,9 @@
             ((poles, channels), F32),
             ((groups, length), F32),
             ((length, groups * poles), BF16),
-            ((1, channels), F32),
         ],
         "prepare",
-        streams, conv_weight, rates, residues, skip,
+        streams, conv_weight, rates, residues,
         scratch=[pltpu.VMEM((3 * tiles, ROWS + length, TILE), F32)],
         flops=10**9,
     )
@@ -371,7 +387,7 @@
         flops=10**9,
     )
     if square:
-        other_near = swap(after(out_weight, (gated, near)), 4, 2)
+        other_near = swap(after(out_weight, (base, near)), 4, 2)
     me = lax.axis_index("ctx").astype(jnp.int32)
     core = me % CORES
     smem = [pl.BlockSpec(memory_space=pltpu.SMEM)]
@@ -398,7 +414,7 @@
     block = jnp.concatenate([mine, swap(other, 1)], axis=0)
     layer = lax.axis_index("tp").astype(jnp.int32)
     beside, across = trade(block, 1), trade(block, 3)
-    beyond = trade(after(across, (beside, other_near)) if square else across, 1)
+    beyond = trade(after(across, other_near) if square else across, 1)
     if square:
         diagonal = swap(after(near, block), 4, 2)
         weight = (out_weight, near, other_near, diagonal)

time: 54.2 us -> 49.7 us (0.917)
  waiting for transfers between devices: 18.1 us -> 12 us
  starting transfers between devices: 17 us -> 20.2 us
  local copies, waits for them, and re-layouts: 2.81 us -> 0.09 us
  Pallas kernels: 14.8 us -> 16.1 us
    ppermute x3, waiting for transfers between devices: 13.6 us -> 7.88 us  [trade(): lax.ppermute(value, 'tp', [(source, source ^ bits) for source in range(co...]
    ppermute x3, starting transfers between devices: 5.35 us -> 8.18 us  [trade(): lax.ppermute(value, 'tp', [(source, source ^ bits) for source in range(co...]
    unnamed x14 -> x2, local copies, waits for them, and re-layouts: 2.72 us -> 0.01 us
    pallas_call x10, Pallas kernels: 14.8 us -> 16.1 us  [call(): pl.pallas_call(kernel, out_shape=tuple((jax.ShapeDtypeStruct(*out) for ou...]
  transfers between devices with their start and end apart: 10 -> 10, of which waited for: 6 -> 6; matrix products, arithmetic and copies ran while one was open for 0% -> 1% of each run, Pallas kernels for 27% -> 32%
where the time goes in v16:
time: 49.7 us; the launch traced here: 49.4 us
  starting transfers between devices  20.2 us (41%)
  Pallas kernels  16.1 us (32%)
  waiting for transfers between devices  12 us (24%)
  other arithmetic  0.93 us (2%)
    pallas_call x10, Pallas kernels, call(): pl.pallas_call(kernel, out_shape=tuple((jax.ShapeDtypeStruct(*out) for ou...  16.1 us
    ppermute x3, starting transfers between devices, trade(): lax.ppermute(value, 'tp', [(source, source ^ bits) for source in range(co...  8.18 us
    ppermute x3, waiting for transfers between devices, trade(): lax.ppermute(value, 'tp', [(source, source ^ bits) for source in range(co...  7.88 us
    ppermute x5, starting transfers between devices, swap(): return lax.ppermute(value, 'ctx', pairs)  6.16 us
    all_to_all x1, starting transfers between devices, local(): lax.all_to_all(ends, 'ctx', split_axis=0, concat_axis=0, tiled=True)  4.41 us
    all_to_all x1, waiting for transfers between devices, local(): lax.all_to_all(ends, 'ctx', split_axis=0, concat_axis=0, tiled=True)  2.46 us
    ppermute x5, waiting for transfers between devices, swap(): return lax.ppermute(value, 'ctx', pairs)  1.63 us
    ppermute x1, starting transfers between devices, from_behind(): lax.ppermute(value, axis, [(source, source + steps) for source in range(l...  1.49 us
  transfers between devices with their start and end apart: 10, of which 6 were waited for; matrix products, arithmetic and copies ran while one was open for 1% of the time, Pallas kernels for 32%

profile of v16, /device:TPU:0, one launch (start us, length us, event | category | flops | bytes accessed | tf_op | source)
XLA Modules:
  0.0 49.4 jit_solution(2361739311044461733)
XLA Ops:
  0.0 2.9 %collective-permute-start.3 = (bf16[512,1024]{1,0:T(8,128)(2,1)}, bf16[512,1024]{1,0:T(8,128)(2,1)}, u32[]{:S(2)}, u32[]{:S(2)}) collective-permute-start(bf16[512,1024]{1,0:T(8,128)(2,1)} %rest_0_.1), channel_id=1, source_target_pairs={{0,8},{4,20},{8,0},{12,28},{16,24},{20,4},{24,16},{28,12},{1,9},{5... | collective-permute-start | bytes 3145736 | tf_op jit(solution)/shard_map/ppermute | solution.py:321
  2.9 1.5 %tails.1 = (bf16[3,8,1024]{2,1,0:T(8,128)(2,1)S(1)}, bf16[3,1024,128]{2,1,0:T(8,128)(2,1)S(1)}, f32[3,7,1024]{2,1,0:T(8,128)S(1)}, f32[16,128]{1,0:T(8,128)S(1)}...) custom-call(bf16[3,1024,128]{2,1,0:T(8,128)(2,1)} %refs_0_.1, f32[3,7,1024]{2,1,0:T(8,128)} %refs_1_.1, ...), custom_call_target="tpu_custom_call" | custom-call | flops 100000000 | bytes 1000000 | tf_op jit(solution)/shard_map/tails/pallas_call | solution.py:55
  4.5 1.5 %collective-permute-start = (bf16[3,8,1024]{2,1,0:T(8,128)(2,1)S(1)}, bf16[3,8,1024]{2,1,0:T(8,128)(2,1)S(1)}, u32[]{:S(2)}, u32[]{:S(2)}) collective-permute-start(bf16[3,8,1024]{2,1,0:T(8,128)(2,1)S(1)} %get-tuple-element.29), channel_id=1, source_target_pairs={{0,4},{4,8},{8,12},{12,16},{16,20},{20,24},{24,28},{1,5},{5,9},{9,... | collective-permute-start | bytes 147464 | tf_op jit(solution)/shard_map/ppermute | solution.py:26
  6.0 3.7 %prepare.1 = (f32[3,8,1024]{2,1,0:T(8,128)S(1)}, bf16[128,1024]{1,0:T(8,128)(2,1)S(1)}, f32[128,1024]{1,0:T(8,128)S(1)}, bf16[2,2048,128]{2,1,0:T(8,128)(2,1)S(1...) custom-call(bf16[3,1024,128]{2,1,0:T(8,128)(2,1)S(1)} %get-tuple-element.30.streams_ref, ...), custom_call_target="tpu_custom_call" | custom-call | flops 1000000000 | bytes 10000000 | tf_op jit(solution)/shard_map/prepare/pallas_call | solution.py:55
  9.7 0.0 collective-permute-done.before_ref
  9.7 1.5 %states.1 = (bf16[8,16,1024]{2,1,0:T(8,128)(2,1)}, bf16[128,1024]{1,0:T(8,128)(2,1)S(1)}, f32[8,1024]{1,0:T(8,128)S(1)}) custom-call(bf16[3,8,1024]{2,1,0:T(8,128)(2,1)S(1)} %collective-permute-done.before_ref, f32[3,8,1024]{2,1,0:T(8,128)S(1)} %get-tuple-element.34.heads_ref, f32[3,7,1024]{2,1,0:T(8,128)S(1)} %get-tuple-element.31.taps_ref, ...), custom_call_target="tpu_custom_call" | custom-call | flops 100000000 | bytes 1000000 | tf_op jit(solution)/shard_map/states/pallas_call | solution.py:55
  11.2 4.4 %all-to-all-start = ((bf16[8,16,1024]{2,1,0:T(8,128)(2,1)}), bf16[8,16,1024]{2,1,0:T(8,128)(2,1)S(1)}, u32[]{:S(2)}, u32[]{:S(2)}) async-start(bf16[8,16,1024]{2,1,0:T(8,128)(2,1)} %get-tuple-element.37), calls=%async_computation | async-start | bytes 524288 | tf_op jit(solution)/shard_map/all_to_all | solution.py:377
  15.7 0.1 pad_add_fusion.1.at_ref
  15.7 2.3 %inside.1.base_ref = f32[128,1024]{1,0:T(8,128)S(1)} custom-call(bf16[128,1024]{1,0:T(8,128)(2,1)S(1)} %get-tuple-element.42.gated_ref, f32[1,1024]{1,0:T(1,128)S(1)} %get-tuple-element.43.skip_ref, f32[128,128]{1,0:T(8,128)S(1)} %get-tuple-element.44.response_ref), custom_call_target="tpu_custom_call" | custom-call | flops 1000000000 | bytes 10000000 | tf_op jit(solution)/shard_map/inside/pallas_call | solution.py:55
  18.1 0.0 collective-permute-done.3.rest_1_
  18.1 2.2 %collective-permute-start.4 = (bf16[512,1024]{1,0:T(8,128)(2,1)S(1)}, bf16[512,1024]{1,0:T(8,128)(2,1)}, u32[]{:S(2)}, u32[]{:S(2)}) collective-permute-start(bf16[512,1024]{1,0:T(8,128)(2,1)S(1)} %copy-done), channel_id=1, source_target_pairs={{0,16},{4,12},{8,24},{12,4},{16,0},{20,28},{24,8},{28,20},{1,17},{... | collective-permute-start | bytes 3145736 | tf_op jit(solution)/shard_map/ppermute | solution.py:321
  20.2 0.1 pad_add_fusion.at_ref
  20.3 2.5 %all-to-all-done.ends_ref = bf16[8,16,1024]{2,1,0:T(8,128)(2,1)S(1)} async-done(((bf16[8,16,1024]{2,1,0:T(8,128)(2,1)}), bf16[8,16,1024]{2,1,0:T(8,128)(2,1)S(1)}, u32[]{:S(2)}, u32[]{:S(2)}) %all-to-all-start) | async-done | bytes 262176 | tf_op jit(solution)/shard_map/all_to_all | solution.py:377
  22.8 0.9 %finish.3 = bf16[128,512]{1,0:T(8,128)(2,1)S(1)} custom-call(s32[2]{0:T(128)S(1)} %pad_add_fusion.1.at_ref, bf16[8,16,1024]{2,1,0:T(8,128)(2,1)S(1)} %all-to-all-done.ends_ref, f32[16,1024]{1,0:T(8,128)S(1)} %get-tuple-element.38.step_ref, bf16[128,2048]{1,0:T(8,128)(2,1)S(1)} %get-tuple-element.39.lift_ref, ...), custom_call_target="tpu_custom_call" | custom-call | flops 3000000000 | bytes 30000000 | tf_op jit(solution)/shard_map/finish/pallas_call | solution.py:55
  23.7 0.1 collective-permute-start.1
  23.8 0.9 %finish.2 = bf16[128,512]{1,0:T(8,128)(2,1)S(1)} custom-call(s32[2]{0:T(128)S(1)} %pad_add_fusion.at_ref, bf16[8,16,1024]{2,1,0:T(8,128)(2,1)S(1)} %all-to-all-done.ends_ref, f32[16,1024]{1,0:T(8,128)S(1)} %get-tuple-element.38.step_ref, bf16[128,2048]{1,0:T(8,128)(2,1)S(1)} %get-tuple-element.39.lift_ref, ...), custom_call_target="tpu_custom_call" | custom-call | flops 3000000000 | bytes 30000000 | tf_op jit(solution)/shard_map/finish/pallas_call | solution.py:55
  24.7 0.4 collective-permute-done.1
  25.1 3.7 %collective-permute-start.2 = (bf16[256,512]{1,0:T(8,128)(2,1)S(1)}, bf16[256,512]{1,0:T(8,128)(2,1)S(1)}, u32[]{:S(2)}, u32[]{:S(2)}) collective-permute-start(bf16[256,512]{1,0:T(8,128)(2,1)S(1)} %pad_maximum_fusion.own_ref), channel_id=1, source_target_pairs={{0,3},{1,2},{2,1},{3,0},{4,7},{5,6},{6,5},{7,4},{8,11},{9,10},{10,... | collective-permute-start | bytes 786440 | tf_op jit(solution)/shard_map/ppermute | solution.py:330
  28.8 0.9 %collective-permute-start.7 = (bf16[512,1024]{1,0:T(8,128)(2,1)}, bf16[512,1024]{1,0:T(8,128)(2,1)S(1)}, u32[]{:S(2)}, u32[]{:S(2)}) collective-permute-start(bf16[512,1024]{1,0:T(8,128)(2,1)} %collective-permute-done.3.rest_1_), channel_id=1, source_target_pairs={{0,16},{4,12},{8,24},{12,4},{16,0},{20,28},{24,8},{28,20},{1,17},{... | collective-permute-start | bytes 3145736 | tf_op jit(solution)/shard_map/ppermute | solution.py:321
  29.7 0.1 stack.44.at_ref
  29.8 6.4 %collective-permute-done.2.across_ref = bf16[256,512]{1,0:T(8,128)(2,1)S(1)} collective-permute-done((bf16[256,512]{1,0:T(8,128)(2,1)S(1)}, bf16[256,512]{1,0:T(8,128)(2,1)S(1)}, u32[]{:S(2)}, u32[]{:S(2)}) %collective-permute-start.2) | collective-permute-done | bytes 262176 | tf_op jit(solution)/shard_map/ppermute | solution.py:330
  36.2 4.5 %collective-permute-start.5 = (bf16[256,512]{1,0:T(8,128)(2,1)S(1)}, bf16[256,512]{1,0:T(8,128)(2,1)S(1)}, u32[]{:S(2)}, u32[]{:S(2)}) collective-permute-start(bf16[256,512]{1,0:T(8,128)(2,1)S(1)} %collective-permute-done.2.across_ref), channel_id=1, source_target_pairs={{0,1},{1,0},{2,3},{3,2},{4,5},{5,4},{6,7},{7,6},{8,9},{9,8},{10,11... | collective-permute-start | bytes 786440 | tf_op jit(solution)/shard_map/ppermute | solution.py:330
  40.7 0.5 collective-permute-done.6.beside_ref
  41.2 3.5 %early.1 = (f32[256,1024]{1,0:T(8,128)S(1)}, bf16[512,1024]{1,0:T(8,128)(2,1)S(1)}, bf16[256,512]{1,0:T(8,128)(2,1)S(1)}) custom-call(s32[5]{0:T(128)S(1)} %stack.44.at_ref, bf16[256,512]{1,0:T(8,128)(2,1)S(1)} %pad_maximum_fusion.own_ref, bf16[256,512]{1,0:T(8,128)(2,1)S(1)} %collective-permute-done.6.beside_ref, ...), custom_call_target="tpu_custom_call" | custom-call | flops 10000000000 | bytes 100000000 | tf_op jit(solution)/shard_map/early/pallas_call | solution.py:55
  44.8 0.0 collective-permute-done.7.weight_ref
  44.8 1.0 %joined.1 = (f32[256,1024]{1,0:T(8,128)S(1)}, bf16[512,1024]{1,0:T(8,128)(2,1)S(1)}) custom-call(s32[5]{0:T(128)S(1)} %stack.44.at_ref, f32[256,1024]{1,0:T(8,128)S(1)} %get-tuple-element.47.total_ref, bf16[512,1024]{1,0:T(8,128)(2,1)S(1)} %get-tuple-element.48.rows_ref, bf16[256,512]{1,0:T(8,128)(2,1)S(1)} %get-tuple-element.49.block_ref, ...), custom_call_target="tpu_custom_call" | custom-call | tf_op jit(solution)/shard_map/joined/pallas_call | solution.py:55
  45.8 1.0 %collective-permute-done.5.beyond_ref = bf16[256,512]{1,0:T(8,128)(2,1)S(1)} collective-permute-done((bf16[256,512]{1,0:T(8,128)(2,1)S(1)}, bf16[256,512]{1,0:T(8,128)(2,1)S(1)}, u32[]{:S(2)}, u32[]{:S(2)}) %collective-permute-start.5) | collective-permute-done | bytes 262176 | tf_op jit(solution)/shard_map/ppermute | solution.py:330
  46.7 0.3 late.3
  47.1 0.1 collective-permute-start.8
  47.1 0.3 late.2
  47.5 1.2 %collective-permute-done.8 = bf16[128,1024]{1,0:T(8,128)(2,1)S(1)} collective-permute-done((bf16[128,1024]{1,0:T(8,128)(2,1)S(1)}, bf16[128,1024]{1,0:T(8,128)(2,1)S(1)}, u32[]{:S(2)}, u32[]{:S(2)}) %collective-permute-start.8) | collective-permute-done | bytes 262176 | tf_op jit(solution)/shard_map/ppermute | solution.py:321
  48.7 0.8 %add_convert_fusion = bf16[128,1024]{1,0:T(8,128)(2,1)} fusion(f32[128,1024]{1,0:T(8,128)S(1)} %late.2, bf16[128,1024]{1,0:T(8,128)(2,1)S(1)} %collective-permute-done.8), kind=kLoop, calls=%fused_computation | loop fusion | flops 393216 | bytes 1048576 | tf_op jit(solution)/shard_map/convert_element_type | solution.py:463
  (5 shorter events, 0.0 us)
Async XLA Ops:
  0.0 18.1 %collective-permute-start.3 = (bf16[512,1024]{1,0:T(8,128)(2,1)}, bf16[512,1024]{1,0:T(8,128)(2,1)}, u32[]{:S(2)}, u32[]{:S(2)}) collective-permute-start(bf16[512,1024]{1,0:T(8,128)(2,1)} %rest_0_.1), channel_id=1, source_target_pairs={{0,8},{4,20},{8,0},{12,28},{16,24},{20,4},{24,16},{28,12},{1,9},{5... | collective-permute-start | bytes 3145736 | tf_op jit(solution)/shard_map/ppermute | solution.py:321
  4.5 5.3 %collective-permute-start = (bf16[3,8,1024]{2,1,0:T(8,128)(2,1)S(1)}, bf16[3,8,1024]{2,1,0:T(8,128)(2,1)S(1)}, u32[]{:S(2)}, u32[]{:S(2)}) collective-permute-start(bf16[3,8,1024]{2,1,0:T(8,128)(2,1)S(1)} %get-tuple-element.29), channel_id=1, source_target_pairs={{0,4},{4,8},{8,12},{12,16},{16,20},{20,24},{24,28},{1,5},{5,9},{9,... | collective-permute-start | bytes 147464 | tf_op jit(solution)/shard_map/ppermute | solution.py:26
  11.2 11.5 %all-to-all-start = ((bf16[8,16,1024]{2,1,0:T(8,128)(2,1)}), bf16[8,16,1024]{2,1,0:T(8,128)(2,1)S(1)}, u32[]{:S(2)}, u32[]{:S(2)}) async-start(bf16[8,16,1024]{2,1,0:T(8,128)(2,1)} %get-tuple-element.37), calls=%async_computation | async-start | bytes 524288 | tf_op jit(solution)/shard_map/all_to_all | solution.py:377
  15.7 2.3 %copy-start = (bf16[512,1024]{1,0:T(8,128)(2,1)S(1)}, bf16[512,1024]{1,0:T(8,128)(2,1)}, u32[]{:S(2)}) copy-start(bf16[512,1024]{1,0:T(8,128)(2,1)} %rest_0_.1) | copy-start | bytes 3145732
  18.1 18.2 %collective-permute-start.4 = (bf16[512,1024]{1,0:T(8,128)(2,1)S(1)}, bf16[512,1024]{1,0:T(8,128)(2,1)}, u32[]{:S(2)}, u32[]{:S(2)}) collective-permute-start(bf16[512,1024]{1,0:T(8,128)(2,1)S(1)} %copy-done), channel_id=1, source_target_pairs={{0,16},{4,12},{8,24},{12,4},{16,0},{20,28},{24,8},{28,20},{1,17},{... | collective-permute-start | bytes 3145736 | tf_op jit(solution)/shard_map/ppermute | solution.py:321
  23.7 1.4 %collective-permute-start.1 = (bf16[128,512]{1,0:T(8,128)(2,1)S(1)}, bf16[128,512]{1,0:T(8,128)(2,1)S(1)}, u32[]{:S(2)}, u32[]{:S(2)}) collective-permute-start(bf16[128,512]{1,0:T(8,128)(2,1)S(1)} %finish.3), channel_id=1, source_target_pairs={{0,4},{4,0},{8,12},{12,8},{16,20},{20,16},{24,28},{28,24},{1,5},{5... | collective-permute-start | bytes 393224 | tf_op jit(solution)/shard_map/ppermute | solution.py:321
  25.1 11.1 %collective-permute-start.2 = (bf16[256,512]{1,0:T(8,128)(2,1)S(1)}, bf16[256,512]{1,0:T(8,128)(2,1)S(1)}, u32[]{:S(2)}, u32[]{:S(2)}) collective-permute-start(bf16[256,512]{1,0:T(8,128)(2,1)S(1)} %pad_maximum_fusion.own_ref), channel_id=1, source_target_pairs={{0,3},{1,2},{2,1},{3,0},{4,7},{5,6},{6,5},{7,4},{8,11},{9,10},{10,... | collective-permute-start | bytes 786440 | tf_op jit(solution)/shard_map/ppermute | solution.py:330
  28.8 12.4 %collective-permute-start.6 = (bf16[256,512]{1,0:T(8,128)(2,1)S(1)}, bf16[256,512]{1,0:T(8,128)(2,1)S(1)}, u32[]{:S(2)}, u32[]{:S(2)}) collective-permute-start(bf16[256,512]{1,0:T(8,128)(2,1)S(1)} %pad_maximum_fusion.own_ref), channel_id=1, source_target_pairs={{0,1},{1,0},{2,3},{3,2},{4,5},{5,4},{6,7},{7,6},{8,9},{9,8},{10,11... | collective-permute-start | bytes 786440 | tf_op jit(solution)/shard_map/ppermute | solution.py:330
  28.8 16.0 %collective-permute-start.7 = (bf16[512,1024]{1,0:T(8,128)(2,1)}, bf16[512,1024]{1,0:T(8,128)(2,1)S(1)}, u32[]{:S(2)}, u32[]{:S(2)}) collective-permute-start(bf16[512,1024]{1,0:T(8,128)(2,1)} %collective-permute-done.3.rest_1_), channel_id=1, source_target_pairs={{0,16},{4,12},{8,24},{12,4},{16,0},{20,28},{24,8},{28,20},{1,17},{... | collective-permute-start | bytes 3145736 | tf_op jit(solution)/shard_map/ppermute | solution.py:321
  36.2 10.5 %collective-permute-start.5 = (bf16[256,512]{1,0:T(8,128)(2,1)S(1)}, bf16[256,512]{1,0:T(8,128)(2,1)S(1)}, u32[]{:S(2)}, u32[]{:S(2)}) collective-permute-start(bf16[256,512]{1,0:T(8,128)(2,1)S(1)} %collective-permute-done.2.across_ref), channel_id=1, source_target_pairs={{0,1},{1,0},{2,3},{3,2},{4,5},{5,4},{6,7},{7,6},{8,9},{9,8},{10,11... | collective-permute-start | bytes 786440 | tf_op jit(solution)/shard_map/ppermute | solution.py:330
  47.1 1.6 %collective-permute-start.8 = (bf16[128,1024]{1,0:T(8,128)(2,1)S(1)}, bf16[128,1024]{1,0:T(8,128)(2,1)S(1)}, u32[]{:S(2)}, u32[]{:S(2)}) collective-permute-start(bf16[128,1024]{1,0:T(8,128)(2,1)S(1)} %late.3), channel_id=1, source_target_pairs={{0,4},{4,0},{8,12},{12,8},{16,20},{20,16},{24,28},{28,24},{1,5},{5... | collective-permute-start | bytes 786440 | tf_op jit(solution)/shard_map/ppermute | solution.py:321

commit v17 on v16

--- a/solution.py
+++ b/solution.py
@@ -271,7 +271,11 @@
     unrolled(share // TILE, tile)
 
 
-def early_kernel(at_ref, own_ref, beside_ref, across_ref, *rest):
+def corner_kernel(block_ref, corner_ref):
+    corner_ref[...] = block_ref[: corner_ref.shape[0], : corner_ref.shape[1]]
+
+
+def early_kernel(at_ref, own_ref, beside_ref, across_ref, corner_ref, *rest):
     *weight_hbms, total_ref, rows_ref, block_ref, layers_ref, weight_ref, sems = rest
     copies = [
         pltpu.make_async_copy(hbm, weight_ref.at[at], sems.at[at]) for at, hbm in enumerate(weight_hbms)
@@ -282,6 +286,7 @@
     last = layer ^ 2
     for bits, ref in ((0, own_ref), (1, beside_ref), (3, across_ref)):
         layers_ref[layer ^ bits] = ref[...]
+    layers_ref[layer ^ 1, : corner_ref.shape[0], : corner_ref.shape[1]] = corner_ref[...]
     layers_ref[last] = jnp.zeros_like(own_ref)
     block_ref[...] = layers_ref[at_ref[1 + len(copies)]]
     for copy in copies:
@@ -414,7 +419,8 @@
     block = jnp.concatenate([mine, swap(other, 1)], axis=0)
     layer = lax.axis_index("tp").astype(jnp.int32)
     beside, across = trade(block, 1), trade(block, 3)
-    beyond = trade(after(across, other_near) if square else across, 1)
+    (corner,) = call(corner_kernel, [((2 * ROWS, TILE), BF16)], "corner", beside, flops=0)
+    beyond = trade(after(across, (corner, other_near)) if square else across, 1)
     if square:
         diagonal = swap(after(near, block), 4, 2)
         weight = (out_weight, near, other_near, diagonal)
@@ -431,9 +437,9 @@
         early_kernel,
         [((CORES * length, features), F32), ((share, features), BF16), (block.shape, BF16)],
         "early",
-        at, block, beside, across,
+        at, block, beside, across, corner,
         *(pltpu.with_memory_space_constraint(part, pltpu.HBM) for part in sooner),
-        specs=smem + whole(3) + [pl.BlockSpec(memory_space=pltpu.HBM)] * len(sooner),
+        specs=smem + whole(4) + [pl.BlockSpec(memory_space=pltpu.HBM)] * len(sooner),
         scratch=[
             pltpu.VMEM((layers,) + block.shape, BF16),
             pltpu.VMEM((len(sooner), share, features), BF16),

time: 49.7 us -> 51.7 us (1.040)
  waiting for transfers between devices: 12 us -> 17.5 us
  starting transfers between devices: 20.2 us -> 16.8 us
    ppermute x3, waiting for transfers between devices: 7.88 us -> 13.4 us  [trade(): lax.ppermute(value, 'tp', [(source, source ^ bits) for source in range(co...]
    ppermute x3, starting transfers between devices: 8.18 us -> 4.69 us  [trade(): lax.ppermute(value, 'tp', [(source, source ^ bits) for source in range(co...]
    pallas_call x10 -> x11, Pallas kernels: 16.1 us -> 16.1 us  [call(): pl.pallas_call(kernel, out_shape=tuple((jax.ShapeDtypeStruct(*out) for ou...]
  transfers between devices with their start and end apart: 10 -> 10, of which waited for: 6 -> 6; matrix products, arithmetic and copies ran while one was open for 1% -> 0% of each run, Pallas kernels for 32% -> 31%
where the time goes in v17:
time: 51.7 us; the launch traced here: 51.5 us
  waiting for transfers between devices  17.5 us (34%)
  starting transfers between devices  16.8 us (32%)
  Pallas kernels  16.1 us (31%)
  other arithmetic  0.93 us (2%)
    pallas_call x11, Pallas kernels, call(): pl.pallas_call(kernel, out_shape=tuple((jax.ShapeDtypeStruct(*out) for ou...  16.1 us
    ppermute x3, waiting for transfers between devices, trade(): lax.ppermute(value, 'tp', [(source, source ^ bits) for source in range(co...  13.4 us
    ppermute x5, starting transfers between devices, swap(): return lax.ppermute(value, 'ctx', pairs)  6.17 us
    ppermute x3, starting transfers between devices, trade(): lax.ppermute(value, 'tp', [(source, source ^ bits) for source in range(co...  4.69 us
    all_to_all x1, starting transfers between devices, local(): lax.all_to_all(ends, 'ctx', split_axis=0, concat_axis=0, tiled=True)  4.41 us
    all_to_all x1, waiting for transfers between devices, local(): lax.all_to_all(ends, 'ctx', split_axis=0, concat_axis=0, tiled=True)  2.46 us
    ppermute x5, waiting for transfers between devices, swap(): return lax.ppermute(value, 'ctx', pairs)  1.62 us
    ppermute x1, starting transfers between devices, from_behind(): lax.ppermute(value, axis, [(source, source + steps) for source in range(l...  1.49 us
  transfers between devices with their start and end apart: 10, of which 6 were waited for; matrix products, arithmetic and copies ran while one was open for 0% of the time, Pallas kernels for 31%

profile of v17, /device:TPU:0, one launch (start us, length us, event | category | flops | bytes accessed | tf_op | source)
XLA Modules:
  0.0 51.5 jit_solution(5893980608613129175)
XLA Ops:
  0.0 2.9 %collective-permute-start.4 = (bf16[512,1024]{1,0:T(8,128)(2,1)}, bf16[512,1024]{1,0:T(8,128)(2,1)}, u32[]{:S(2)}, u32[]{:S(2)}) collective-permute-start(bf16[512,1024]{1,0:T(8,128)(2,1)} %rest_0_.1), channel_id=1, source_target_pairs={{0,8},{4,20},{8,0},{12,28},{16,24},{20,4},{24,16},{28,12},{1,9},{5... | collective-permute-start | bytes 3145736 | tf_op jit(solution)/shard_map/ppermute | solution.py:326
  2.9 1.5 %tails.1 = (bf16[3,8,1024]{2,1,0:T(8,128)(2,1)S(1)}, bf16[3,1024,128]{2,1,0:T(8,128)(2,1)S(1)}, f32[3,7,1024]{2,1,0:T(8,128)S(1)}, f32[16,128]{1,0:T(8,128)S(1)}...) custom-call(bf16[3,1024,128]{2,1,0:T(8,128)(2,1)} %refs_0_.1, f32[3,7,1024]{2,1,0:T(8,128)} %refs_1_.1, ...), custom_call_target="tpu_custom_call" | custom-call | flops 100000000 | bytes 1000000 | tf_op jit(solution)/shard_map/tails/pallas_call | solution.py:55
  4.5 1.5 %collective-permute-start = (bf16[3,8,1024]{2,1,0:T(8,128)(2,1)S(1)}, bf16[3,8,1024]{2,1,0:T(8,128)(2,1)S(1)}, u32[]{:S(2)}, u32[]{:S(2)}) collective-permute-start(bf16[3,8,1024]{2,1,0:T(8,128)(2,1)S(1)} %get-tuple-element.29), channel_id=1, source_target_pairs={{0,4},{4,8},{8,12},{12,16},{16,20},{20,24},{24,28},{1,5},{5,9},{9,... | collective-permute-start | bytes 147464 | tf_op jit(solution)/shard_map/ppermute | solution.py:26
  6.0 3.7 %prepare.1 = (f32[3,8,1024]{2,1,0:T(8,128)S(1)}, bf16[128,1024]{1,0:T(8,128)(2,1)S(1)}, f32[128,1024]{1,0:T(8,128)S(1)}, bf16[2,2048,128]{2,1,0:T(8,128)(2,1)S(1...) custom-call(bf16[3,1024,128]{2,1,0:T(8,128)(2,1)S(1)} %get-tuple-element.30.streams_ref, ...), custom_call_target="tpu_custom_call" | custom-call | flops 1000000000 | bytes 10000000 | tf_op jit(solution)/shard_map/prepare/pallas_call | solution.py:55
  9.7 0.0 collective-permute-done.before_ref
  9.7 1.5 %states.1 = (bf16[8,16,1024]{2,1,0:T(8,128)(2,1)}, bf16[128,1024]{1,0:T(8,128)(2,1)S(1)}, f32[8,1024]{1,0:T(8,128)S(1)}) custom-call(bf16[3,8,1024]{2,1,0:T(8,128)(2,1)S(1)} %collective-permute-done.before_ref, f32[3,8,1024]{2,1,0:T(8,128)S(1)} %get-tuple-element.34.heads_ref, f32[3,7,1024]{2,1,0:T(8,128)S(1)} %get-tuple-element.31.taps_ref, ...), custom_call_target="tpu_custom_call" | custom-call | flops 100000000 | bytes 1000000 | tf_op jit(solution)/shard_map/states/pallas_call | solution.py:55
  11.2 4.4 %all-to-all-start = ((bf16[8,16,1024]{2,1,0:T(8,128)(2,1)}), bf16[8,16,1024]{2,1,0:T(8,128)(2,1)S(1)}, u32[]{:S(2)}, u32[]{:S(2)}) async-start(bf16[8,16,1024]{2,1,0:T(8,128)(2,1)} %get-tuple-element.37), calls=%async_computation | async-start | bytes 524288 | tf_op jit(solution)/shard_map/all_to_all | solution.py:382
  15.7 0.1 pad_add_fusion.1.at_ref
  15.7 2.3 %inside.1.base_ref = f32[128,1024]{1,0:T(8,128)S(1)} custom-call(bf16[128,1024]{1,0:T(8,128)(2,1)S(1)} %get-tuple-element.42.gated_ref, f32[1,1024]{1,0:T(1,128)S(1)} %get-tuple-element.43.skip_ref, f32[128,128]{1,0:T(8,128)S(1)} %get-tuple-element.44.response_ref), custom_call_target="tpu_custom_call" | custom-call | flops 1000000000 | bytes 10000000 | tf_op jit(solution)/shard_map/inside/pallas_call | solution.py:55
  18.1 0.0 collective-permute-done.4.rest_1_
  18.1 2.2 %collective-permute-start.5 = (bf16[512,1024]{1,0:T(8,128)(2,1)S(1)}, bf16[512,1024]{1,0:T(8,128)(2,1)}, u32[]{:S(2)}, u32[]{:S(2)}) collective-permute-start(bf16[512,1024]{1,0:T(8,128)(2,1)S(1)} %copy-done), channel_id=1, source_target_pairs={{0,16},{4,12},{8,24},{12,4},{16,0},{20,28},{24,8},{28,20},{1,17},{... | collective-permute-start | bytes 3145736 | tf_op jit(solution)/shard_map/ppermute | solution.py:326
  20.2 0.1 pad_add_fusion.at_ref
  20.3 2.5 %all-to-all-done.ends_ref = bf16[8,16,1024]{2,1,0:T(8,128)(2,1)S(1)} async-done(((bf16[8,16,1024]{2,1,0:T(8,128)(2,1)}), bf16[8,16,1024]{2,1,0:T(8,128)(2,1)S(1)}, u32[]{:S(2)}, u32[]{:S(2)}) %all-to-all-start) | async-done | bytes 262176 | tf_op jit(solution)/shard_map/all_to_all | solution.py:382
  22.8 0.9 %finish.3 = bf16[128,512]{1,0:T(8,128)(2,1)S(1)} custom-call(s32[2]{0:T(128)S(1)} %pad_add_fusion.1.at_ref, bf16[8,16,1024]{2,1,0:T(8,128)(2,1)S(1)} %all-to-all-done.ends_ref, f32[16,1024]{1,0:T(8,128)S(1)} %get-tuple-element.38.step_ref, bf16[128,2048]{1,0:T(8,128)(2,1)S(1)} %get-tuple-element.39.lift_ref, ...), custom_call_target="tpu_custom_call" | custom-call | flops 3000000000 | bytes 30000000 | tf_op jit(solution)/shard_map/finish/pallas_call | solution.py:55
  23.7 0.1 collective-permute-start.1
  23.8 0.9 %finish.2 = bf16[128,512]{1,0:T(8,128)(2,1)S(1)} custom-call(s32[2]{0:T(128)S(1)} %pad_add_fusion.at_ref, bf16[8,16,1024]{2,1,0:T(8,128)(2,1)S(1)} %all-to-all-done.ends_ref, f32[16,1024]{1,0:T(8,128)S(1)} %get-tuple-element.38.step_ref, bf16[128,2048]{1,0:T(8,128)(2,1)S(1)} %get-tuple-element.39.lift_ref, ...), custom_call_target="tpu_custom_call" | custom-call | flops 3000000000 | bytes 30000000 | tf_op jit(solution)/shard_map/finish/pallas_call | solution.py:55
  24.7 0.4 collective-permute-done.1
  25.1 1.6 %collective-permute-start.3 = (bf16[256,512]{1,0:T(8,128)(2,1)S(1)}, bf16[256,512]{1,0:T(8,128)(2,1)S(1)}, u32[]{:S(2)}, u32[]{:S(2)}) collective-permute-start(bf16[256,512]{1,0:T(8,128)(2,1)S(1)} %pad_maximum_fusion.own_ref), channel_id=1, source_target_pairs={{0,1},{1,0},{2,3},{3,2},{4,5},{5,4},{6,7},{7,6},{8,9},{9,8},{10,11... | collective-permute-start | bytes 786440 | tf_op jit(solution)/shard_map/ppermute | solution.py:335
  26.8 2.5 %collective-permute-start.2 = (bf16[256,512]{1,0:T(8,128)(2,1)S(1)}, bf16[256,512]{1,0:T(8,128)(2,1)S(1)}, u32[]{:S(2)}, u32[]{:S(2)}) collective-permute-start(bf16[256,512]{1,0:T(8,128)(2,1)S(1)} %pad_maximum_fusion.own_ref), channel_id=1, source_target_pairs={{0,3},{1,2},{2,1},{3,0},{4,7},{5,6},{6,5},{7,4},{8,11},{9,10},{10,... | collective-permute-start | bytes 786440 | tf_op jit(solution)/shard_map/ppermute | solution.py:335
  29.2 0.9 %collective-permute-start.7 = (bf16[512,1024]{1,0:T(8,128)(2,1)}, bf16[512,1024]{1,0:T(8,128)(2,1)S(1)}, u32[]{:S(2)}, u32[]{:S(2)}) collective-permute-start(bf16[512,1024]{1,0:T(8,128)(2,1)} %collective-permute-done.4.rest_1_), channel_id=1, source_target_pairs={{0,16},{4,12},{8,24},{12,4},{16,0},{20,28},{24,8},{28,20},{1,17},{... | collective-permute-start | bytes 3145736 | tf_op jit(solution)/shard_map/ppermute | solution.py:326
  30.2 0.1 stack.44.at_ref
  30.3 3.3 %collective-permute-done.3.block_ref.beside_ref = bf16[256,512]{1,0:T(8,128)(2,1)S(1)} collective-permute-done((bf16[256,512]{1,0:T(8,128)(2,1)S(1)}, bf16[256,512]{1,0:T(8,128)(2,1)S(1)}, u32[]{:S(2)}, u32[]{:S(2)}) %collective-permute-start.3) | collective-permute-done | bytes 262176 | tf_op jit(solution)/shard_map/ppermute | solution.py:335
  33.6 7.7 %collective-permute-done.2.across_ref = bf16[256,512]{1,0:T(8,128)(2,1)S(1)} collective-permute-done((bf16[256,512]{1,0:T(8,128)(2,1)S(1)}, bf16[256,512]{1,0:T(8,128)(2,1)S(1)}, u32[]{:S(2)}, u32[]{:S(2)}) %collective-permute-start.2) | collective-permute-done | bytes 262176 | tf_op jit(solution)/shard_map/ppermute | solution.py:335
  41.3 0.6 %collective-permute-start.6 = (bf16[256,512]{1,0:T(8,128)(2,1)S(1)}, bf16[256,512]{1,0:T(8,128)(2,1)S(1)}, u32[]{:S(2)}, u32[]{:S(2)}) collective-permute-start(bf16[256,512]{1,0:T(8,128)(2,1)S(1)} %collective-permute-done.2.across_ref), channel_id=1, source_target_pairs={{0,1},{1,0},{2,3},{3,2},{4,5},{5,4},{6,7},{7,6},{8,9},{9,8},{10,11... | collective-permute-start | bytes 786440 | tf_op jit(solution)/shard_map/ppermute | solution.py:335
  41.9 3.5 %early.1 = (f32[256,1024]{1,0:T(8,128)S(1)}, bf16[512,1024]{1,0:T(8,128)(2,1)S(1)}, bf16[256,512]{1,0:T(8,128)(2,1)S(1)}) custom-call(s32[5]{0:T(128)S(1)} %stack.44.at_ref, bf16[256,512]{1,0:T(8,128)(2,1)S(1)} %pad_maximum_fusion.own_ref, bf16[256,512]{1,0:T(8,128)(2,1)S(1)} %collective-permute-done.3.block_ref.beside_ref, ...), custom_call_target="tpu_custom_call" | custom-call | flops 10000000000 | bytes 100000000 | tf_op jit(solution)/shard_map/early/pallas_call | solution.py:55
  45.4 1.0 %joined.1 = (f32[256,1024]{1,0:T(8,128)S(1)}, bf16[512,1024]{1,0:T(8,128)(2,1)S(1)}) custom-call(s32[5]{0:T(128)S(1)} %stack.44.at_ref, f32[256,1024]{1,0:T(8,128)S(1)} %get-tuple-element.47.total_ref, bf16[512,1024]{1,0:T(8,128)(2,1)S(1)} %get-tuple-element.48.rows_ref, bf16[256,512]{1,0:T(8,128)(2,1)S(1)} %get-tuple-element.49.block_ref, ...), custom_call_target="tpu_custom_call" | custom-call | tf_op jit(solution)/shard_map/joined/pallas_call | solution.py:55
  46.4 2.3 %collective-permute-done.6.beyond_ref = bf16[256,512]{1,0:T(8,128)(2,1)S(1)} collective-permute-done((bf16[256,512]{1,0:T(8,128)(2,1)S(1)}, bf16[256,512]{1,0:T(8,128)(2,1)S(1)}, u32[]{:S(2)}, u32[]{:S(2)}) %collective-permute-start.6) | collective-permute-done | bytes 262176 | tf_op jit(solution)/shard_map/ppermute | solution.py:335
  48.8 0.3 late.3
  49.1 0.1 collective-permute-start.8
  49.2 0.3 late.2
  49.5 1.2 %collective-permute-done.8 = bf16[128,1024]{1,0:T(8,128)(2,1)S(1)} collective-permute-done((bf16[128,1024]{1,0:T(8,128)(2,1)S(1)}, bf16[128,1024]{1,0:T(8,128)(2,1)S(1)}, u32[]{:S(2)}, u32[]{:S(2)}) %collective-permute-start.8) | collective-permute-done | bytes 262176 | tf_op jit(solution)/shard_map/ppermute | solution.py:326
  50.7 0.8 %add_convert_fusion = bf16[128,1024]{1,0:T(8,128)(2,1)} fusion(f32[128,1024]{1,0:T(8,128)S(1)} %late.2, bf16[128,1024]{1,0:T(8,128)(2,1)S(1)} %collective-permute-done.8), kind=kLoop, calls=%fused_computation | loop fusion | flops 393216 | bytes 1048576 | tf_op jit(solution)/shard_map/convert_element_type | solution.py:469
  (6 shorter events, 0.0 us)
Async XLA Ops:
  0.0 18.1 %collective-permute-start.4 = (bf16[512,1024]{1,0:T(8,128)(2,1)}, bf16[512,1024]{1,0:T(8,128)(2,1)}, u32[]{:S(2)}, u32[]{:S(2)}) collective-permute-start(bf16[512,1024]{1,0:T(8,128)(2,1)} %rest_0_.1), channel_id=1, source_target_pairs={{0,8},{4,20},{8,0},{12,28},{16,24},{20,4},{24,16},{28,12},{1,9},{5... | collective-permute-start | bytes 3145736 | tf_op jit(solution)/shard_map/ppermute | solution.py:326
  4.5 5.3 %collective-permute-start = (bf16[3,8,1024]{2,1,0:T(8,128)(2,1)S(1)}, bf16[3,8,1024]{2,1,0:T(8,128)(2,1)S(1)}, u32[]{:S(2)}, u32[]{:S(2)}) collective-permute-start(bf16[3,8,1024]{2,1,0:T(8,128)(2,1)S(1)} %get-tuple-element.29), channel_id=1, source_target_pairs={{0,4},{4,8},{8,12},{12,16},{16,20},{20,24},{24,28},{1,5},{5,9},{9,... | collective-permute-start | bytes 147464 | tf_op jit(solution)/shard_map/ppermute | solution.py:26
  11.2 11.5 %all-to-all-start = ((bf16[8,16,1024]{2,1,0:T(8,128)(2,1)}), bf16[8,16,1024]{2,1,0:T(8,128)(2,1)S(1)}, u32[]{:S(2)}, u32[]{:S(2)}) async-start(bf16[8,16,1024]{2,1,0:T(8,128)(2,1)} %get-tuple-element.37), calls=%async_computation | async-start | bytes 524288 | tf_op jit(solution)/shard_map/all_to_all | solution.py:382
  15.7 2.3 %copy-start = (bf16[512,1024]{1,0:T(8,128)(2,1)S(1)}, bf16[512,1024]{1,0:T(8,128)(2,1)}, u32[]{:S(2)}) copy-start(bf16[512,1024]{1,0:T(8,128)(2,1)} %rest_0_.1) | copy-start | bytes 3145732
  18.1 23.2 %collective-permute-start.5 = (bf16[512,1024]{1,0:T(8,128)(2,1)S(1)}, bf16[512,1024]{1,0:T(8,128)(2,1)}, u32[]{:S(2)}, u32[]{:S(2)}) collective-permute-start(bf16[512,1024]{1,0:T(8,128)(2,1)S(1)} %copy-done), channel_id=1, source_target_pairs={{0,16},{4,12},{8,24},{12,4},{16,0},{20,28},{24,8},{28,20},{1,17},{... | collective-permute-start | bytes 3145736 | tf_op jit(solution)/shard_map/ppermute | solution.py:326
  23.7 1.4 %collective-permute-start.1 = (bf16[128,512]{1,0:T(8,128)(2,1)S(1)}, bf16[128,512]{1,0:T(8,128)(2,1)S(1)}, u32[]{:S(2)}, u32[]{:S(2)}) collective-permute-start(bf16[128,512]{1,0:T(8,128)(2,1)S(1)} %finish.3), channel_id=1, source_target_pairs={{0,4},{4,0},{8,12},{12,8},{16,20},{20,16},{24,28},{28,24},{1,5},{5... | collective-permute-start | bytes 393224 | tf_op jit(solution)/shard_map/ppermute | solution.py:326
  25.1 8.4 %collective-permute-start.3 = (bf16[256,512]{1,0:T(8,128)(2,1)S(1)}, bf16[256,512]{1,0:T(8,128)(2,1)S(1)}, u32[]{:S(2)}, u32[]{:S(2)}) collective-permute-start(bf16[256,512]{1,0:T(8,128)(2,1)S(1)} %pad_maximum_fusion.own_ref), channel_id=1, source_target_pairs={{0,1},{1,0},{2,3},{3,2},{4,5},{5,4},{6,7},{7,6},{8,9},{9,8},{10,11... | collective-permute-start | bytes 786440 | tf_op jit(solution)/shard_map/ppermute | solution.py:335
  26.8 14.5 %collective-permute-start.2 = (bf16[256,512]{1,0:T(8,128)(2,1)S(1)}, bf16[256,512]{1,0:T(8,128)(2,1)S(1)}, u32[]{:S(2)}, u32[]{:S(2)}) collective-permute-start(bf16[256,512]{1,0:T(8,128)(2,1)S(1)} %pad_maximum_fusion.own_ref), channel_id=1, source_target_pairs={{0,3},{1,2},{2,1},{3,0},{4,7},{5,6},{6,5},{7,4},{8,11},{9,10},{10,... | collective-permute-start | bytes 786440 | tf_op jit(solution)/shard_map/ppermute | solution.py:335
  29.2 16.2 %collective-permute-start.7 = (bf16[512,1024]{1,0:T(8,128)(2,1)}, bf16[512,1024]{1,0:T(8,128)(2,1)S(1)}, u32[]{:S(2)}, u32[]{:S(2)}) collective-permute-start(bf16[512,1024]{1,0:T(8,128)(2,1)} %collective-permute-done.4.rest_1_), channel_id=1, source_target_pairs={{0,16},{4,12},{8,24},{12,4},{16,0},{20,28},{24,8},{28,20},{1,17},{... | collective-permute-start | bytes 3145736 | tf_op jit(solution)/shard_map/ppermute | solution.py:326
  41.3 7.5 %collective-permute-start.6 = (bf16[256,512]{1,0:T(8,128)(2,1)S(1)}, bf16[256,512]{1,0:T(8,128)(2,1)S(1)}, u32[]{:S(2)}, u32[]{:S(2)}) collective-permute-start(bf16[256,512]{1,0:T(8,128)(2,1)S(1)} %collective-permute-done.2.across_ref), channel_id=1, source_target_pairs={{0,1},{1,0},{2,3},{3,2},{4,5},{5,4},{6,7},{7,6},{8,9},{9,8},{10,11... | collective-permute-start | bytes 786440 | tf_op jit(solution)/shard_map/ppermute | solution.py:335
  49.1 1.6 %collective-permute-start.8 = (bf16[128,1024]{1,0:T(8,128)(2,1)S(1)}, bf16[128,1024]{1,0:T(8,128)(2,1)S(1)}, u32[]{:S(2)}, u32[]{:S(2)}) collective-permute-start(bf16[128,1024]{1,0:T(8,128)(2,1)S(1)} %late.3), channel_id=1, source_target_pairs={{0,4},{4,0},{8,12},{12,8},{16,20},{20,16},{24,28},{28,24},{1,5},{5... | collective-permute-start | bytes 786440 | tf_op jit(solution)/shard_map/ppermute | solution.py:326

commit v18 on v16

--- a/solution.py
+++ b/solution.py
@@ -271,48 +271,48 @@
     unrolled(share // TILE, tile)
 
 
-def early_kernel(at_ref, own_ref, beside_ref, across_ref, *rest):
+def early_kernel(at_ref, own_ref, beside_ref, middle_ref, ends_ref, *rest):
     *weight_hbms, total_ref, rows_ref, block_ref, layers_ref, weight_ref, sems = rest
-    copies = [
-        pltpu.make_async_copy(hbm, weight_ref.at[at], sems.at[at]) for at, hbm in enumerate(weight_hbms)
-    ]
+    count = len(weight_hbms)
+    layer = at_ref[0]
+    last = layer ^ 2
+    copies = [pltpu.make_async_copy(hbm, weight_ref.at[at], sems.at[at]) for at, hbm in enumerate(weight_hbms)]
+    fetches = [pltpu.make_async_copy(hbm, rows_ref, sems.at[count]) for hbm in weight_hbms]
     for copy in copies:
         copy.start()
-    layer = at_ref[0]
-    last = layer ^ 2
-    for bits, ref in ((0, own_ref), (1, beside_ref), (3, across_ref)):
-        layers_ref[layer ^ bits] = ref[...]
+    for at, fetch in enumerate(fetches):
+        pl.when(at_ref[1 + at] == last)(fetch.start)
+    layers_ref[layer] = own_ref[...]
+    layers_ref[layer ^ 1] = beside_ref[...]
+    layers_ref[layer ^ 3] = jnp.where((layer == 0) | (layer == 3), ends_ref[...], middle_ref[...])
     layers_ref[last] = jnp.zeros_like(own_ref)
-    block_ref[...] = layers_ref[at_ref[1 + len(copies)]]
-    for copy in copies:
+    block_ref[...] = layers_ref[at_ref[1 + count]]
+    for at, copy in enumerate(copies):
         copy.wait()
-    for column in range(0, total_ref.shape[1], COLUMNS):
-        columns = slice(column, column + COLUMNS)
-        total = None
-        for at in range(len(copies)):
-            term = dot(layers_ref[at_ref[1 + at]], weight_ref[at, :, columns])
-            total = term if total is None else total + term
-        total_ref[:, columns] = total
-    rows_ref[...] = jnp.zeros_like(rows_ref)
-    for at in range(len(copies)):
-
-        @pl.when(at_ref[1 + at] == last)
-        def _():
-            rows_ref[...] = weight_ref[at]
-
-
-def joined_kernel(at_ref, total_ref, rows_ref, block_ref, weight_ref, out_ref, last_ref):
+        block = layers_ref[at_ref[1 + at]]
+        for column in range(0, total_ref.shape[1], COLUMNS):
+            columns = slice(column, column + COLUMNS)
+            term = dot(block, weight_ref[at, :, columns])
+            total_ref[:, columns] = total_ref[:, columns] + term if at else term
+    for at, fetch in enumerate(fetches):
+        pl.when(at_ref[1 + at] == last)(fetch.wait)
+
+
+def joined_kernel(total_ref, block_ref, weight_ref, out_ref):
     out_ref[...] = total_ref[...] + dot(block_ref[...], weight_ref[...])
-    last_ref[...] = rows_ref[...]
-
-    @pl.when(at_ref[4] == at_ref[0] ^ 2)
-    def _():
-        last_ref[...] = weight_ref[...]
-
-
-def late_kernel(first, beyond_ref, total_ref, rows_ref, out_ref):
+
+
+def late_kernel(first, at_ref, inwards_ref, outwards_ref, total_ref, rows_ref, weight_ref, out_ref):
     tokens = pl.ds(first, out_ref.shape[0])
-    out_ref[...] = (total_ref[tokens, :] + dot(beyond_ref[tokens, :], rows_ref[...])).astype(out_ref.dtype)
+    edge = (at_ref[0] == 0) | (at_ref[0] == 3)
+    beyond = jnp.where(edge, outwards_ref[tokens, :], inwards_ref[tokens, :])
+
+    def add(rows):
+        out_ref[...] = (total_ref[tokens, :] + dot(beyond, rows[...])).astype(out_ref.dtype)
+
+    latest = at_ref[4] == at_ref[0] ^ 2
+    pl.when(latest)(lambda: add(weight_ref))
+    pl.when(jnp.logical_not(latest))(lambda: add(rows_ref))
 
 
 def swap(value, *bits):
@@ -325,9 +325,8 @@
     return lax.optimization_barrier((value, earlier))[0]
 
 
-def trade(value, bits):
-    count = lax.axis_size("tp")
-    return lax.ppermute(value, "tp", [(source, source ^ bits) for source in range(count)])
+def along(value, *pairs):
+    return lax.ppermute(value, "tp", pairs)
 
 
 def local(streams, conv_weight, rates, residues, skip, out_weight):
@@ -387,7 +386,7 @@
         flops=10**9,
     )
     if square:
-        other_near = swap(after(out_weight, (base, near)), 4, 2)
+        other_near = swap(after(out_weight, (gated, near)), 4, 2)
     me = lax.axis_index("ctx").astype(jnp.int32)
     core = me % CORES
     smem = [pl.BlockSpec(memory_space=pltpu.SMEM)]
@@ -413,8 +412,11 @@
         other = lax.dynamic_index_in_dim(by_core, 1 - core, 0, keepdims=False)
     block = jnp.concatenate([mine, swap(other, 1)], axis=0)
     layer = lax.axis_index("tp").astype(jnp.int32)
-    beside, across = trade(block, 1), trade(block, 3)
-    beyond = trade(after(across, other_near) if square else across, 1)
+    beside = along(block, (0, 1), (1, 0), (2, 3), (3, 2))
+    middle = along(block, (1, 2), (2, 1))
+    ends = along(block, (0, 3), (3, 0))
+    inwards = along(beside, (1, 2), (2, 1))
+    outwards = along(after(middle, other_near) if square else middle, (1, 0), (2, 3))
     if square:
         diagonal = swap(after(near, block), 4, 2)
         weight = (out_weight, near, other_near, diagonal)
@@ -431,23 +433,18 @@
         early_kernel,
         [((CORES * length, features), F32), ((share, features), BF16), (block.shape, BF16)],
         "early",
-        at, block, beside, across,
+        at, block, beside, middle, ends,
         *(pltpu.with_memory_space_constraint(part, pltpu.HBM) for part in sooner),
-        specs=smem + whole(3) + [pl.BlockSpec(memory_space=pltpu.HBM)] * len(sooner),
+        specs=smem + whole(4) + [pl.BlockSpec(memory_space=pltpu.HBM)] * len(sooner),
         scratch=[
             pltpu.VMEM((layers,) + block.shape, BF16),
             pltpu.VMEM((len(sooner), share, features), BF16),
-            pltpu.SemaphoreType.DMA((len(sooner),)),
+            pltpu.SemaphoreType.DMA((len(sooner) + 1,)),
         ],
         flops=10**10,
     )
-    total, last_rows = call(
-        joined_kernel,
-        [((CORES * length, features), F32), ((share, features), BF16)],
-        "joined",
-        at, total, last_rows, last_block, latest,
-        specs=smem + whole(4),
-        flops=0,
+    (total,) = call(
+        joined_kernel, [((CORES * length, features), F32)], "joined", total, last_block, latest, flops=0
     )
     sides = []
     for side, kind in ((1, BF16), (0, F32)):
@@ -455,7 +452,8 @@
             functools.partial(late_kernel, side * length),
             [((length, features), kind)],
             "late",
-            beyond, total, last_rows,
+            at, inwards, outwards, total, last_rows, latest,
+            specs=smem + whole(5),
             flops=0,
         )
     other, mine = sides

time: 49.7 us -> 54.7 us (1.10)
  waiting for transfers between devices: 12 us -> 17.3 us
    ppermute x5, waiting for transfers between devices: 1.63 us -> 4.61 us  [swap(): return lax.ppermute(value, 'ctx', pairs)]
    ppermute x3 -> x5, waiting for transfers between devices: 7.88 us -> 10.2 us  [along(): return lax.ppermute(value, 'tp', pairs)]
    ppermute x5, starting transfers between devices: 6.16 us -> 5.3 us  [swap(): return lax.ppermute(value, 'ctx', pairs)]
    ppermute x3 -> x5, starting transfers between devices: 8.18 us -> 8.64 us  [along(): return lax.ppermute(value, 'tp', pairs)]
  transfers between devices with their start and end apart: 10 -> 12, of which waited for: 6 -> 8; matrix products, arithmetic and copies ran while one was open for 1% -> 0% of each run, Pallas kernels for 32% -> 28%
where the time goes in v18:
time: 54.7 us; the launch traced here: 54.3 us
  starting transfers between devices  19.8 us (36%)
  waiting for transfers between devices  17.3 us (32%)
  Pallas kernels  16 us (29%)
  other arithmetic  0.92 us (2%)
    pallas_call x10, Pallas kernels, call(): pl.pallas_call(kernel, out_shape=tuple((jax.ShapeDtypeStruct(*out) for ou...  16 us
    ppermute x5, waiting for transfers between devices, along(): return lax.ppermute(value, 'tp', pairs)  10.2 us
    ppermute x5, starting transfers between devices, along(): return lax.ppermute(value, 'tp', pairs)  8.64 us
    ppermute x5, starting transfers between devices, swap(): return lax.ppermute(value, 'ctx', pairs)  5.3 us
    ppermute x5, waiting for transfers between devices, swap(): return lax.ppermute(value, 'ctx', pairs)  4.61 us
    all_to_all x1, starting transfers between devices, local(): lax.all_to_all(ends, 'ctx', split_axis=0, concat_axis=0, tiled=True)  4.4 us
    all_to_all x1, waiting for transfers between devices, local(): lax.all_to_all(ends, 'ctx', split_axis=0, concat_axis=0, tiled=True)  2.58 us
    ppermute x1, starting transfers between devices, from_behind(): lax.ppermute(value, axis, [(source, source + steps) for source in range(l...  1.49 us
  transfers between devices with their start and end apart: 12, of which 8 were waited for; matrix products, arithmetic and copies ran while one was open for 0% of the time, Pallas kernels for 28%

profile of v18, /device:TPU:0, one launch (start us, length us, event | category | flops | bytes accessed | tf_op | source)
XLA Modules:
  0.0 54.3 jit_solution(3585225501122480724)
XLA Ops:
  0.0 2.9 %collective-permute-start.5 = (bf16[512,1024]{1,0:T(8,128)(2,1)}, bf16[512,1024]{1,0:T(8,128)(2,1)}, u32[]{:S(2)}, u32[]{:S(2)}) collective-permute-start(bf16[512,1024]{1,0:T(8,128)(2,1)} %rest_0_.1), channel_id=1, source_target_pairs={{0,8},{4,20},{8,0},{12,28},{16,24},{20,4},{24,16},{28,12},{1,9},{5... | collective-permute-start | bytes 3145736 | tf_op jit(solution)/shard_map/ppermute | solution.py:321
  2.9 1.5 %tails.1 = (bf16[3,8,1024]{2,1,0:T(8,128)(2,1)S(1)}, bf16[3,1024,128]{2,1,0:T(8,128)(2,1)S(1)}, f32[3,7,1024]{2,1,0:T(8,128)S(1)}, f32[16,128]{1,0:T(8,128)S(1)}...) custom-call(bf16[3,1024,128]{2,1,0:T(8,128)(2,1)} %refs_0_.1, f32[3,7,1024]{2,1,0:T(8,128)} %refs_1_.1, ...), custom_call_target="tpu_custom_call" | custom-call | flops 100000000 | bytes 1000000 | tf_op jit(solution)/shard_map/tails/pallas_call | solution.py:55
  4.5 1.5 %collective-permute-start = (bf16[3,8,1024]{2,1,0:T(8,128)(2,1)S(1)}, bf16[3,8,1024]{2,1,0:T(8,128)(2,1)S(1)}, u32[]{:S(2)}, u32[]{:S(2)}) collective-permute-start(bf16[3,8,1024]{2,1,0:T(8,128)(2,1)S(1)} %get-tuple-element.27), channel_id=1, source_target_pairs={{0,4},{4,8},{8,12},{12,16},{16,20},{20,24},{24,28},{1,5},{5,9},{9,... | collective-permute-start | bytes 147464 | tf_op jit(solution)/shard_map/ppermute | solution.py:26
  6.0 3.7 %prepare.1 = (f32[3,8,1024]{2,1,0:T(8,128)S(1)}, bf16[128,1024]{1,0:T(8,128)(2,1)S(1)}, f32[128,1024]{1,0:T(8,128)S(1)}, bf16[2,2048,128]{2,1,0:T(8,128)(2,1)S(1...) custom-call(bf16[3,1024,128]{2,1,0:T(8,128)(2,1)S(1)} %get-tuple-element.28.streams_ref, ...), custom_call_target="tpu_custom_call" | custom-call | flops 1000000000 | bytes 10000000 | tf_op jit(solution)/shard_map/prepare/pallas_call | solution.py:55
  9.7 1.5 %states.1 = (bf16[8,16,1024]{2,1,0:T(8,128)(2,1)}, bf16[128,1024]{1,0:T(8,128)(2,1)S(1)}, f32[8,1024]{1,0:T(8,128)S(1)}) custom-call(bf16[3,8,1024]{2,1,0:T(8,128)(2,1)S(1)} %collective-permute-done.before_ref, f32[3,8,1024]{2,1,0:T(8,128)S(1)} %get-tuple-element.32.heads_ref, f32[3,7,1024]{2,1,0:T(8,128)S(1)} %get-tuple-element.29.taps_ref, ...), custom_call_target="tpu_custom_call" | custom-call | flops 100000000 | bytes 1000000 | tf_op jit(solution)/shard_map/states/pallas_call | solution.py:55
  11.2 4.4 %all-to-all-start = ((bf16[8,16,1024]{2,1,0:T(8,128)(2,1)}), bf16[8,16,1024]{2,1,0:T(8,128)(2,1)S(1)}, u32[]{:S(2)}, u32[]{:S(2)}) async-start(bf16[8,16,1024]{2,1,0:T(8,128)(2,1)} %get-tuple-element.35), calls=%async_computation | async-start | bytes 524288 | tf_op jit(solution)/shard_map/all_to_all | solution.py:376
  15.7 0.1 pad_add_fusion.1.at_ref
  15.7 0.8 %collective-permute-done.5.rest_1_ = bf16[512,1024]{1,0:T(8,128)(2,1)} collective-permute-done((bf16[512,1024]{1,0:T(8,128)(2,1)}, bf16[512,1024]{1,0:T(8,128)(2,1)}, u32[]{:S(2)}, u32[]{:S(2)}) %collective-permute-start.5) | collective-permute-done | bytes 1048608 | tf_op jit(solution)/shard_map/ppermute | solution.py:321
  16.6 1.5 %collective-permute-start.6 = (bf16[512,1024]{1,0:T(8,128)(2,1)S(1)}, bf16[512,1024]{1,0:T(8,128)(2,1)}, u32[]{:S(2)}, u32[]{:S(2)}) collective-permute-start(bf16[512,1024]{1,0:T(8,128)(2,1)S(1)} %copy-done), channel_id=1, source_target_pairs={{0,16},{4,12},{8,24},{12,4},{16,0},{20,28},{24,8},{28,20},{1,17},{... | collective-permute-start | bytes 3145736 | tf_op jit(solution)/shard_map/ppermute | solution.py:321
  18.1 0.1 pad_add_fusion.at_ref
  18.2 2.3 %inside.1.base_ref = f32[128,1024]{1,0:T(8,128)S(1)} custom-call(bf16[128,1024]{1,0:T(8,128)(2,1)S(1)} %get-tuple-element.40.gated_ref, f32[1,1024]{1,0:T(1,128)S(1)} %get-tuple-element.41.skip_ref, f32[128,128]{1,0:T(8,128)S(1)} %get-tuple-element.42.response_ref), custom_call_target="tpu_custom_call" | custom-call | flops 1000000000 | bytes 10000000 | tf_op jit(solution)/shard_map/inside/pallas_call | solution.py:55
  20.5 2.6 %all-to-all-done.ends_ref = bf16[8,16,1024]{2,1,0:T(8,128)(2,1)S(1)} async-done(((bf16[8,16,1024]{2,1,0:T(8,128)(2,1)}), bf16[8,16,1024]{2,1,0:T(8,128)(2,1)S(1)}, u32[]{:S(2)}, u32[]{:S(2)}) %all-to-all-start) | async-done | bytes 262176 | tf_op jit(solution)/shard_map/all_to_all | solution.py:376
  23.1 0.9 %finish.3 = bf16[128,512]{1,0:T(8,128)(2,1)S(1)} custom-call(s32[2]{0:T(128)S(1)} %pad_add_fusion.1.at_ref, bf16[8,16,1024]{2,1,0:T(8,128)(2,1)S(1)} %all-to-all-done.ends_ref, f32[16,1024]{1,0:T(8,128)S(1)} %get-tuple-element.36.step_ref, bf16[128,2048]{1,0:T(8,128)(2,1)S(1)} %get-tuple-element.37.lift_ref, ...), custom_call_target="tpu_custom_call" | custom-call | flops 3000000000 | bytes 30000000 | tf_op jit(solution)/shard_map/finish/pallas_call | solution.py:55
  24.1 0.9 %finish.2 = bf16[128,512]{1,0:T(8,128)(2,1)S(1)} custom-call(s32[2]{0:T(128)S(1)} %pad_add_fusion.at_ref, bf16[8,16,1024]{2,1,0:T(8,128)(2,1)S(1)} %all-to-all-done.ends_ref, f32[16,1024]{1,0:T(8,128)S(1)} %get-tuple-element.36.step_ref, bf16[128,2048]{1,0:T(8,128)(2,1)S(1)} %get-tuple-element.37.lift_ref, ...), custom_call_target="tpu_custom_call" | custom-call | flops 3000000000 | bytes 30000000 | tf_op jit(solution)/shard_map/finish/pallas_call | solution.py:55
  25.0 0.4 collective-permute-done.1
  25.4 1.6 %collective-permute-start.2 = (bf16[256,512]{1,0:T(8,128)(2,1)S(1)}, bf16[256,512]{1,0:T(8,128)(2,1)S(1)}, u32[]{:S(2)}, u32[]{:S(2)}) collective-permute-start(bf16[256,512]{1,0:T(8,128)(2,1)S(1)} %pad_maximum_fusion.own_ref), channel_id=1, source_target_pairs={{0,1},{1,0},{2,3},{3,2},{4,5},{5,4},{6,7},{7,6},{8,9},{9,8},{10,11... | collective-permute-start | bytes 786440 | tf_op jit(solution)/shard_map/ppermute | solution.py:329
  27.1 0.7 %collective-permute-start.4 = (bf16[256,512]{1,0:T(8,128)(2,1)S(1)}, bf16[256,512]{1,0:T(8,128)(2,1)S(1)}, u32[]{:S(2)}, u32[]{:S(2)}) collective-permute-start(bf16[256,512]{1,0:T(8,128)(2,1)S(1)} %pad_maximum_fusion.own_ref), channel_id=1, source_target_pairs={{1,2},{2,1},{5,6},{6,5},{9,10},{10,9},{13,14},{14,13},{17,18},{18,... | collective-permute-start | bytes 786440 | tf_op jit(solution)/shard_map/ppermute | solution.py:329
  27.7 4.4 %collective-permute-start.8 = (bf16[256,512]{1,0:T(8,128)(2,1)S(1)}, bf16[256,512]{1,0:T(8,128)(2,1)S(1)}, u32[]{:S(2)}, u32[]{:S(2)}) collective-permute-start(bf16[256,512]{1,0:T(8,128)(2,1)S(1)} %pad_maximum_fusion.own_ref), channel_id=1, source_target_pairs={{0,3},{3,0},{4,7},{7,4},{8,11},{11,8},{12,15},{15,12},{16,19},{19,... | collective-permute-start | bytes 786440 | tf_op jit(solution)/shard_map/ppermute | solution.py:329
  32.1 0.7 %collective-permute-start.9 = (bf16[512,1024]{1,0:T(8,128)(2,1)}, bf16[512,1024]{1,0:T(8,128)(2,1)S(1)}, u32[]{:S(2)}, u32[]{:S(2)}) collective-permute-start(bf16[512,1024]{1,0:T(8,128)(2,1)} %collective-permute-done.5.rest_1_), channel_id=1, source_target_pairs={{0,16},{4,12},{8,24},{12,4},{16,0},{20,28},{24,8},{28,20},{1,17},{... | collective-permute-start | bytes 3145736 | tf_op jit(solution)/shard_map/ppermute | solution.py:321
  32.8 0.1 stack.39.at_ref
  32.9 0.9 %collective-permute-done.2.beside_ref = bf16[256,512]{1,0:T(8,128)(2,1)S(1)} collective-permute-done((bf16[256,512]{1,0:T(8,128)(2,1)S(1)}, bf16[256,512]{1,0:T(8,128)(2,1)S(1)}, u32[]{:S(2)}, u32[]{:S(2)}) %collective-permute-start.2) | collective-permute-done | bytes 262176 | tf_op jit(solution)/shard_map/ppermute | solution.py:329
  33.8 0.7 %collective-permute-start.3 = (bf16[256,512]{1,0:T(8,128)(2,1)S(1)}, bf16[256,512]{1,0:T(8,128)(2,1)S(1)}, u32[]{:S(2)}, u32[]{:S(2)}) collective-permute-start(bf16[256,512]{1,0:T(8,128)(2,1)S(1)} %collective-permute-done.2.beside_ref), channel_id=1, source_target_pairs={{1,2},{2,1},{5,6},{6,5},{9,10},{10,9},{13,14},{14,13},{17,18},{18,... | collective-permute-start | bytes 786440 | tf_op jit(solution)/shard_map/ppermute | solution.py:329
  34.5 1.3 %collective-permute-start.7 = (bf16[256,512]{1,0:T(8,128)(2,1)S(1)}, bf16[256,512]{1,0:T(8,128)(2,1)S(1)}, u32[]{:S(2)}, u32[]{:S(2)}) collective-permute-start(bf16[256,512]{1,0:T(8,128)(2,1)S(1)} %collective-permute-done.4.middle_ref), channel_id=1, source_target_pairs={{1,0},{2,3},{5,4},{6,7},{9,8},{10,11},{13,12},{14,15},{17,16},{18,... | collective-permute-start | bytes 786440 | tf_op jit(solution)/shard_map/ppermute | solution.py:329
  35.8 5.7 %collective-permute-done.8.ends_ref = bf16[256,512]{1,0:T(8,128)(2,1)S(1)} collective-permute-done((bf16[256,512]{1,0:T(8,128)(2,1)S(1)}, bf16[256,512]{1,0:T(8,128)(2,1)S(1)}, u32[]{:S(2)}, u32[]{:S(2)}) %collective-permute-start.8) | collective-permute-done | bytes 262176 | tf_op jit(solution)/shard_map/ppermute | solution.py:329
  41.6 2.9 %early.1 = (f32[256,1024]{1,0:T(8,128)S(1)}, bf16[512,1024]{1,0:T(8,128)(2,1)S(1)}, bf16[256,512]{1,0:T(8,128)(2,1)S(1)}) custom-call(s32[5]{0:T(128)S(1)} %stack.39.at_ref, bf16[256,512]{1,0:T(8,128)(2,1)S(1)} %pad_maximum_fusion.own_ref, bf16[256,512]{1,0:T(8,128)(2,1)S(1)} %collective-permute-done.2.beside_ref, ...), custom_call_target="tpu_custom_call" | custom-call | flops 10000000000 | bytes 100000000 | tf_op jit(solution)/shard_map/early/pallas_call | solution.py:55
  44.5 2.7 %collective-permute-done.9.weight_ref = bf16[512,1024]{1,0:T(8,128)(2,1)S(1)} collective-permute-done((bf16[512,1024]{1,0:T(8,128)(2,1)}, bf16[512,1024]{1,0:T(8,128)(2,1)S(1)}, u32[]{:S(2)}, u32[]{:S(2)}) %collective-permute-start.9) | collective-permute-done | bytes 1048608 | tf_op jit(solution)/shard_map/ppermute | solution.py:321
  47.2 0.4 joined.1.total_ref
  47.7 3.5 %collective-permute-done.7.outwards_ref = bf16[256,512]{1,0:T(8,128)(2,1)S(1)} collective-permute-done((bf16[256,512]{1,0:T(8,128)(2,1)S(1)}, bf16[256,512]{1,0:T(8,128)(2,1)S(1)}, u32[]{:S(2)}, u32[]{:S(2)}) %collective-permute-start.7) | collective-permute-done | bytes 262176 | tf_op jit(solution)/shard_map/ppermute | solution.py:329
  51.1 0.9 %late.3 = bf16[128,1024]{1,0:T(8,128)(2,1)S(1)} custom-call(s32[5]{0:T(128)S(1)} %stack.39.at_ref, bf16[256,512]{1,0:T(8,128)(2,1)S(1)} %collective-permute-done.3.inwards_ref, bf16[256,512]{1,0:T(8,128)(2,1)S(1)} %collective-permute-done.7.outwards_ref, f32[256,1024]{1,0:T(8,128)S(1)} %joined.1.total_ref, bf16[512,1024]{1,0:T(8,128)(2,1)S(1)} %get-tuple-element.48.rows_ref, ...), custom_call_target="tpu_custom_call" | custom-call | tf_op jit(solution)/shard_map/late/pallas_call | solution.py:55
  52.1 0.9 %late.2 = f32[128,1024]{1,0:T(8,128)S(1)} custom-call(s32[5]{0:T(128)S(1)} %stack.39.at_ref, bf16[256,512]{1,0:T(8,128)(2,1)S(1)} %collective-permute-done.3.inwards_ref, bf16[256,512]{1,0:T(8,128)(2,1)S(1)} %collective-permute-done.7.outwards_ref, f32[256,1024]{1,0:T(8,128)S(1)} %joined.1.total_ref, bf16[512,1024]{1,0:T(8,128)(2,1)S(1)} %get-tuple-element.48.rows_ref, ...), custom_call_target="tpu_custom_call" | custom-call | tf_op jit(solution)/shard_map/late/pallas_call | solution.py:55
  52.9 0.7 %collective-permute-done.10 = bf16[128,1024]{1,0:T(8,128)(2,1)S(1)} collective-permute-done((bf16[128,1024]{1,0:T(8,128)(2,1)S(1)}, bf16[128,1024]{1,0:T(8,128)(2,1)S(1)}, u32[]{:S(2)}, u32[]{:S(2)}) %collective-permute-start.10) | collective-permute-done | bytes 262176 | tf_op jit(solution)/shard_map/ppermute | solution.py:321
  53.6 0.8 %add_convert_fusion = bf16[128,1024]{1,0:T(8,128)(2,1)} fusion(f32[128,1024]{1,0:T(8,128)S(1)} %late.2, bf16[128,1024]{1,0:T(8,128)(2,1)S(1)} %collective-permute-done.10), kind=kLoop, calls=%fused_computation | loop fusion | flops 393216 | bytes 1048576 | tf_op jit(solution)/shard_map/convert_element_type | solution.py:461
  (9 shorter events, 0.2 us)
Async XLA Ops:
  0.0 16.6 %collective-permute-start.5 = (bf16[512,1024]{1,0:T(8,128)(2,1)}, bf16[512,1024]{1,0:T(8,128)(2,1)}, u32[]{:S(2)}, u32[]{:S(2)}) collective-permute-start(bf16[512,1024]{1,0:T(8,128)(2,1)} %rest_0_.1), channel_id=1, source_target_pairs={{0,8},{4,20},{8,0},{12,28},{16,24},{20,4},{24,16},{28,12},{1,9},{5... | collective-permute-start | bytes 3145736 | tf_op jit(solution)/shard_map/ppermute | solution.py:321
  4.5 5.3 %collective-permute-start = (bf16[3,8,1024]{2,1,0:T(8,128)(2,1)S(1)}, bf16[3,8,1024]{2,1,0:T(8,128)(2,1)S(1)}, u32[]{:S(2)}, u32[]{:S(2)}) collective-permute-start(bf16[3,8,1024]{2,1,0:T(8,128)(2,1)S(1)} %get-tuple-element.27), channel_id=1, source_target_pairs={{0,4},{4,8},{8,12},{12,16},{16,20},{20,24},{24,28},{1,5},{5,9},{9,... | collective-permute-start | bytes 147464 | tf_op jit(solution)/shard_map/ppermute | solution.py:26
  9.7 6.8 %copy-start = (bf16[512,1024]{1,0:T(8,128)(2,1)S(1)}, bf16[512,1024]{1,0:T(8,128)(2,1)}, u32[]{:S(2)}) copy-start(bf16[512,1024]{1,0:T(8,128)(2,1)} %rest_0_.1) | copy-start | bytes 3145732
  11.2 11.8 %all-to-all-start = ((bf16[8,16,1024]{2,1,0:T(8,128)(2,1)}), bf16[8,16,1024]{2,1,0:T(8,128)(2,1)S(1)}, u32[]{:S(2)}, u32[]{:S(2)}) async-start(bf16[8,16,1024]{2,1,0:T(8,128)(2,1)} %get-tuple-element.35), calls=%async_computation | async-start | bytes 524288 | tf_op jit(solution)/shard_map/all_to_all | solution.py:376
  16.6 18.0 %collective-permute-start.6 = (bf16[512,1024]{1,0:T(8,128)(2,1)S(1)}, bf16[512,1024]{1,0:T(8,128)(2,1)}, u32[]{:S(2)}, u32[]{:S(2)}) collective-permute-start(bf16[512,1024]{1,0:T(8,128)(2,1)S(1)} %copy-done), channel_id=1, source_target_pairs={{0,16},{4,12},{8,24},{12,4},{16,0},{20,28},{24,8},{28,20},{1,17},{... | collective-permute-start | bytes 3145736 | tf_op jit(solution)/shard_map/ppermute | solution.py:321
  24.0 1.4 %collective-permute-start.1 = (bf16[128,512]{1,0:T(8,128)(2,1)S(1)}, bf16[128,512]{1,0:T(8,128)(2,1)S(1)}, u32[]{:S(2)}, u32[]{:S(2)}) collective-permute-start(bf16[128,512]{1,0:T(8,128)(2,1)S(1)} %finish.3), channel_id=1, source_target_pairs={{0,4},{4,0},{8,12},{12,8},{16,20},{20,16},{24,28},{28,24},{1,5},{5... | collective-permute-start | bytes 393224 | tf_op jit(solution)/shard_map/ppermute | solution.py:321
  25.4 8.4 %collective-permute-start.2 = (bf16[256,512]{1,0:T(8,128)(2,1)S(1)}, bf16[256,512]{1,0:T(8,128)(2,1)S(1)}, u32[]{:S(2)}, u32[]{:S(2)}) collective-permute-start(bf16[256,512]{1,0:T(8,128)(2,1)S(1)} %pad_maximum_fusion.own_ref), channel_id=1, source_target_pairs={{0,1},{1,0},{2,3},{3,2},{4,5},{5,4},{6,7},{7,6},{8,9},{9,8},{10,11... | collective-permute-start | bytes 786440 | tf_op jit(solution)/shard_map/ppermute | solution.py:329
  27.1 7.5 %collective-permute-start.4 = (bf16[256,512]{1,0:T(8,128)(2,1)S(1)}, bf16[256,512]{1,0:T(8,128)(2,1)S(1)}, u32[]{:S(2)}, u32[]{:S(2)}) collective-permute-start(bf16[256,512]{1,0:T(8,128)(2,1)S(1)} %pad_maximum_fusion.own_ref), channel_id=1, source_target_pairs={{1,2},{2,1},{5,6},{6,5},{9,10},{10,9},{13,14},{14,13},{17,18},{18,... | collective-permute-start | bytes 786440 | tf_op jit(solution)/shard_map/ppermute | solution.py:329
  27.7 13.9 %collective-permute-start.8 = (bf16[256,512]{1,0:T(8,128)(2,1)S(1)}, bf16[256,512]{1,0:T(8,128)(2,1)S(1)}, u32[]{:S(2)}, u32[]{:S(2)}) collective-permute-start(bf16[256,512]{1,0:T(8,128)(2,1)S(1)} %pad_maximum_fusion.own_ref), channel_id=1, source_target_pairs={{0,3},{3,0},{4,7},{7,4},{8,11},{11,8},{12,15},{15,12},{16,19},{19,... | collective-permute-start | bytes 786440 | tf_op jit(solution)/shard_map/ppermute | solution.py:329
  32.1 15.1 %collective-permute-start.9 = (bf16[512,1024]{1,0:T(8,128)(2,1)}, bf16[512,1024]{1,0:T(8,128)(2,1)S(1)}, u32[]{:S(2)}, u32[]{:S(2)}) collective-permute-start(bf16[512,1024]{1,0:T(8,128)(2,1)} %collective-permute-done.5.rest_1_), channel_id=1, source_target_pairs={{0,16},{4,12},{8,24},{12,4},{16,0},{20,28},{24,8},{28,20},{1,17},{... | collective-permute-start | bytes 3145736 | tf_op jit(solution)/shard_map/ppermute | solution.py:321
  33.8 13.8 %collective-permute-start.3 = (bf16[256,512]{1,0:T(8,128)(2,1)S(1)}, bf16[256,512]{1,0:T(8,128)(2,1)S(1)}, u32[]{:S(2)}, u32[]{:S(2)}) collective-permute-start(bf16[256,512]{1,0:T(8,128)(2,1)S(1)} %collective-permute-done.2.beside_ref), channel_id=1, source_target_pairs={{1,2},{2,1},{5,6},{6,5},{9,10},{10,9},{13,14},{14,13},{17,18},{18,... | collective-permute-start | bytes 786440 | tf_op jit(solution)/shard_map/ppermute | solution.py:329
  34.5 16.6 %collective-permute-start.7 = (bf16[256,512]{1,0:T(8,128)(2,1)S(1)}, bf16[256,512]{1,0:T(8,128)(2,1)S(1)}, u32[]{:S(2)}, u32[]{:S(2)}) collective-permute-start(bf16[256,512]{1,0:T(8,128)(2,1)S(1)} %collective-permute-done.4.middle_ref), channel_id=1, source_target_pairs={{1,0},{2,3},{5,4},{6,7},{9,8},{10,11},{13,12},{14,15},{17,16},{18,... | collective-permute-start | bytes 786440 | tf_op jit(solution)/shard_map/ppermute | solution.py:329
  52.0 1.6 %collective-permute-start.10 = (bf16[128,1024]{1,0:T(8,128)(2,1)S(1)}, bf16[128,1024]{1,0:T(8,128)(2,1)S(1)}, u32[]{:S(2)}, u32[]{:S(2)}) collective-permute-start(bf16[128,1024]{1,0:T(8,128)(2,1)S(1)} %late.3), channel_id=1, source_target_pairs={{0,4},{4,0},{8,12},{12,8},{16,20},{20,16},{24,28},{28,24},{1,5},{5... | collective-permute-start | bytes 786440 | tf_op jit(solution)/shard_map/ppermute | solution.py:321

commit v19 on v16

--- a/solution.py
+++ b/solution.py
@@ -130,19 +130,18 @@
         shift = groups - index * in_tile
         rates = pltpu.roll(rates_ref[...], shift, 1)
         coef = pltpu.roll(scale, shift, 1)
-        once = jnp.exp(-rates)
         decay, impulse, lift = [], [], []
         wide = jnp.zeros((poles, TILE), F32)
         for g in range(in_tile):
             rate = jnp.broadcast_to(rates[:, g : g + 1], (poles, length))
             decay.append(jnp.exp(-rate * lag))
-            impulse.append(jnp.broadcast_to(coef[:, g : g + 1], (poles, length)) * jnp.exp(-rate * time))
-            lift.append(impulse[-1] * once[:, g : g + 1])
+            amplitude = jnp.broadcast_to(coef[:, g : g + 1], (poles, length))
+            impulse.append(amplitude * jnp.exp(-rate * time))
+            lift.append(amplitude * jnp.exp(-rate * (time + 1.0)))
             wide = jnp.where(owner == g, rate[:, :TILE], wide)
         step_ref[:, tile_of(index)] = jnp.exp(-wide * length)
         states = tile_of(index, in_tile * poles)
-        for part, value in enumerate(halves(jnp.concatenate(decay, axis=0))):
-            decay_ref[part, states, :] = value
+        decay_ref[states, :] = jnp.concatenate(decay, axis=0).astype(BF16)
         high, low = halves(jnp.concatenate(impulse, axis=0))
         response_ref[pl.ds(pl.multiple_of(index * in_tile, in_tile), in_tile), :] = dot(member, high) + dot(member, low)
         lift_ref[:, states] = turned(jnp.concatenate(lift, axis=0).astype(BF16), unit).astype(BF16)
@@ -163,7 +162,7 @@
 def states_kernel(before_ref, heads_ref, taps_ref, gated_ref, decay_ref, ends_ref, final_ref, first_ref, padded_ref):
     length, channels = gated_ref.shape
     poles = ends_ref.shape[1]
-    in_tile = decay_ref.shape[1] // poles * TILE // channels
+    in_tile = decay_ref.shape[0] // poles * TILE // channels
     owner = iota((poles, TILE), 1) // (TILE // in_tile)
 
     def begin(index):
@@ -181,7 +180,7 @@
         chans = tile_of(index)
         gated = final_ref[:, chans]
         states = tile_of(index, in_tile * poles)
-        every = dot(decay_ref[0, states, :], gated) + dot(decay_ref[1, states, :], gated)
+        every = dot(decay_ref[states, :], gated)
         ends = jnp.zeros((poles, TILE), F32)
         for g in range(in_tile):
             ends = jnp.where(owner == g, every[g * poles : (g + 1) * poles], ends)
@@ -262,9 +261,7 @@
         chans = tile_of(at)
         entering = state_ref[:, tile_of(index)]
         apart = jnp.concatenate([jnp.where(owner == g, entering, 0.0) for g in range(in_tile)], axis=0)
-        high, low = halves(apart)
-        lift = lift_ref[:, tile_of(at, in_tile * poles)]
-        carried = dot(lift, high) + dot(lift, low)
+        carried = dot(lift_ref[:, tile_of(at, in_tile * poles)], apart.astype(BF16))
         query = jnp.concatenate([first_ref[:, chans], query_ref[:, chans].astype(F32)[ROWS:]], axis=0)
         mixed_ref[:, tile_of(index)] = (query * (base_ref[:, chans] + carried)).astype(BF16)
 
@@ -273,41 +270,39 @@
 
 def early_kernel(at_ref, own_ref, beside_ref, across_ref, *rest):
     *weight_hbms, total_ref, rows_ref, block_ref, layers_ref, weight_ref, sems = rest
-    copies = [
-        pltpu.make_async_copy(hbm, weight_ref.at[at], sems.at[at]) for at, hbm in enumerate(weight_hbms)
-    ]
+    count = len(weight_hbms)
+    layer = at_ref[0]
+    last = layer ^ 2
+    copies = [pltpu.make_async_copy(hbm, weight_ref.at[at], sems.at[at]) for at, hbm in enumerate(weight_hbms)]
+    fetches = [pltpu.make_async_copy(hbm, rows_ref, sems.at[count]) for hbm in weight_hbms]
     for copy in copies:
         copy.start()
-    layer = at_ref[0]
-    last = layer ^ 2
+    for at, fetch in enumerate(fetches):
+        pl.when(at_ref[1 + at] == last)(fetch.start)
     for bits, ref in ((0, own_ref), (1, beside_ref), (3, across_ref)):
         layers_ref[layer ^ bits] = ref[...]
     layers_ref[last] = jnp.zeros_like(own_ref)
-    block_ref[...] = layers_ref[at_ref[1 + len(copies)]]
-    for copy in copies:
+    block_ref[...] = layers_ref[at_ref[1 + count]]
+    for at, copy in enumerate(copies):
         copy.wait()
-    for column in range(0, total_ref.shape[1], COLUMNS):
-        columns = slice(column, column + COLUMNS)
-        total = None
-        for at in range(len(copies)):
-            term = dot(layers_ref[at_ref[1 + at]], weight_ref[at, :, columns])
-            total = term if total is None else total + term
-        total_ref[:, columns] = total
-    rows_ref[...] = jnp.zeros_like(rows_ref)
-    for at in range(len(copies)):
-
-        @pl.when(at_ref[1 + at] == last)
-        def _():
-            rows_ref[...] = weight_ref[at]
+        block = layers_ref[at_ref[1 + at]]
+        for column in range(0, total_ref.shape[1], COLUMNS):
+            columns = slice(column, column + COLUMNS)
+            term = dot(block, weight_ref[at, :, columns])
+            total_ref[:, columns] = total_ref[:, columns] + term if at else term
+    for at, fetch in enumerate(fetches):
+        pl.when(at_ref[1 + at] == last)(fetch.wait)
 
 
 def joined_kernel(at_ref, total_ref, rows_ref, block_ref, weight_ref, out_ref, last_ref):
     out_ref[...] = total_ref[...] + dot(block_ref[...], weight_ref[...])
-    last_ref[...] = rows_ref[...]
-
-    @pl.when(at_ref[4] == at_ref[0] ^ 2)
-    def _():
-        last_ref[...] = weight_ref[...]
+
+    def keep(rows):
+        last_ref[...] = rows[...]
+
+    latest = at_ref[4] == at_ref[0] ^ 2
+    pl.when(latest)(lambda: keep(weight_ref))
+    pl.when(jnp.logical_not(latest))(lambda: keep(rows_ref))
 
 
 def late_kernel(first, beyond_ref, total_ref, rows_ref, out_ref):
@@ -357,7 +352,7 @@
             ((3, ROWS, channels), F32),
             ((length, channels), BF16),
             ((length, channels), F32),
-            ((2, groups * poles, length), BF16),
+            ((groups * poles, length), BF16),
             ((poles, channels), F32),
             ((groups, length), F32),
             ((length, groups * poles), BF16),
@@ -437,7 +432,7 @@
         scratch=[
             pltpu.VMEM((layers,) + block.shape, BF16),
             pltpu.VMEM((len(sooner), share, features), BF16),
-            pltpu.SemaphoreType.DMA((len(sooner),)),
+            pltpu.SemaphoreType.DMA((len(sooner) + 1,)),
         ],
         flops=10**10,
     )

time: 49.7 us -> 49.5 us (level)
  Pallas kernels: 16.1 us -> 14.8 us
  waiting for transfers between devices: 12 us -> 12.8 us
    pallas_call x10, Pallas kernels: 16.1 us -> 14.8 us  [call(): pl.pallas_call(kernel, out_shape=tuple((jax.ShapeDtypeStruct(*out) for ou...]
    ppermute x5, waiting for transfers between devices: 1.63 us -> 2.44 us  [swap(): return lax.ppermute(value, 'ctx', pairs)]
  transfers between devices with their start and end apart: 10 -> 10, of which waited for: 6 -> 7; matrix products, arithmetic and copies ran while one was open for 1% -> 1% of each run, Pallas kernels for 32% -> 29%
where the time goes in v19:
time: 49.5 us; the launch traced here: 49.2 us
  starting transfers between devices  20.5 us (41%)
  Pallas kernels  14.8 us (30%)
  waiting for transfers between devices  12.8 us (26%)
  other arithmetic  0.93 us (2%)
    pallas_call x10, Pallas kernels, call(): pl.pallas_call(kernel, out_shape=tuple((jax.ShapeDtypeStruct(*out) for ou...  14.8 us
    ppermute x3, starting transfers between devices, trade(): lax.ppermute(value, 'tp', [(source, source ^ bits) for source in range(co...  8.16 us
    ppermute x3, waiting for transfers between devices, trade(): lax.ppermute(value, 'tp', [(source, source ^ bits) for source in range(co...  7.89 us
    ppermute x5, starting transfers between devices, swap(): return lax.ppermute(value, 'ctx', pairs)  6.02 us
    all_to_all x1, starting transfers between devices, local(): lax.all_to_all(ends, 'ctx', split_axis=0, concat_axis=0, tiled=True)  4.82 us
    all_to_all x1, waiting for transfers between devices, local(): lax.all_to_all(ends, 'ctx', split_axis=0, concat_axis=0, tiled=True)  2.46 us
    ppermute x5, waiting for transfers between devices, swap(): return lax.ppermute(value, 'ctx', pairs)  2.44 us
    ppermute x1, starting transfers between devices, from_behind(): lax.ppermute(value, axis, [(source, source + steps) for source in range(l...  1.49 us
  transfers between devices with their start and end apart: 10, of which 7 were waited for; matrix products, arithmetic and copies ran while one was open for 1% of the time, Pallas kernels for 29%

profile of v19, /device:TPU:0, one launch (start us, length us, event | category | flops | bytes accessed | tf_op | source)
XLA Modules:
  0.0 49.2 jit_solution(16329813898520262716)
XLA Ops:
  0.0 2.9 %collective-permute-start.3 = (bf16[512,1024]{1,0:T(8,128)(2,1)}, bf16[512,1024]{1,0:T(8,128)(2,1)}, u32[]{:S(2)}, u32[]{:S(2)}) collective-permute-start(bf16[512,1024]{1,0:T(8,128)(2,1)} %rest_0_.1), channel_id=1, source_target_pairs={{0,8},{4,20},{8,0},{12,28},{16,24},{20,4},{24,16},{28,12},{1,9},{5... | collective-permute-start | bytes 3145736 | tf_op jit(solution)/shard_map/ppermute | solution.py:316
  2.9 1.5 %tails.1 = (bf16[3,8,1024]{2,1,0:T(8,128)(2,1)S(1)}, bf16[3,1024,128]{2,1,0:T(8,128)(2,1)S(1)}, f32[3,7,1024]{2,1,0:T(8,128)S(1)}, f32[16,128]{1,0:T(8,128)S(1)}...) custom-call(bf16[3,1024,128]{2,1,0:T(8,128)(2,1)} %refs_0_.1, f32[3,7,1024]{2,1,0:T(8,128)} %refs_1_.1, ...), custom_call_target="tpu_custom_call" | custom-call | flops 100000000 | bytes 1000000 | tf_op jit(solution)/shard_map/tails/pallas_call | solution.py:55
  4.5 1.5 %collective-permute-start = (bf16[3,8,1024]{2,1,0:T(8,128)(2,1)S(1)}, bf16[3,8,1024]{2,1,0:T(8,128)(2,1)S(1)}, u32[]{:S(2)}, u32[]{:S(2)}) collective-permute-start(bf16[3,8,1024]{2,1,0:T(8,128)(2,1)S(1)} %get-tuple-element.29), channel_id=1, source_target_pairs={{0,4},{4,8},{8,12},{12,16},{16,20},{20,24},{24,28},{1,5},{5,9},{9,... | collective-permute-start | bytes 147464 | tf_op jit(solution)/shard_map/ppermute | solution.py:26
  6.0 3.3 %prepare.1 = (f32[3,8,1024]{2,1,0:T(8,128)S(1)}, bf16[128,1024]{1,0:T(8,128)(2,1)S(1)}, f32[128,1024]{1,0:T(8,128)S(1)}, bf16[2048,128]{1,0:T(8,128)(2,1)S(1)}, ...) custom-call(bf16[3,1024,128]{2,1,0:T(8,128)(2,1)S(1)} %get-tuple-element.30.streams_ref, ...), custom_call_target="tpu_custom_call" | custom-call | flops 1000000000 | bytes 10000000 | tf_op jit(solution)/shard_map/prepare/pallas_call | solution.py:55
  9.3 0.0 collective-permute-done.before_ref
  9.3 1.4 %states.1 = (bf16[8,16,1024]{2,1,0:T(8,128)(2,1)}, bf16[128,1024]{1,0:T(8,128)(2,1)S(1)}, f32[8,1024]{1,0:T(8,128)S(1)}) custom-call(bf16[3,8,1024]{2,1,0:T(8,128)(2,1)S(1)} %collective-permute-done.before_ref, f32[3,8,1024]{2,1,0:T(8,128)S(1)} %get-tuple-element.34.heads_ref, f32[3,7,1024]{2,1,0:T(8,128)S(1)} %get-tuple-element.31.taps_ref, ...), custom_call_target="tpu_custom_call" | custom-call | flops 100000000 | bytes 1000000 | tf_op jit(solution)/shard_map/states/pallas_call | solution.py:55
  10.7 4.8 %all-to-all-start = ((bf16[8,16,1024]{2,1,0:T(8,128)(2,1)}), bf16[8,16,1024]{2,1,0:T(8,128)(2,1)S(1)}, u32[]{:S(2)}, u32[]{:S(2)}) async-start(bf16[8,16,1024]{2,1,0:T(8,128)(2,1)} %get-tuple-element.37), calls=%async_computation | async-start | bytes 524288 | tf_op jit(solution)/shard_map/all_to_all | solution.py:372
  15.5 0.1 pad_add_fusion.1.at_ref
  15.6 2.3 %inside.1.base_ref = f32[128,1024]{1,0:T(8,128)S(1)} custom-call(bf16[128,1024]{1,0:T(8,128)(2,1)S(1)} %get-tuple-element.42.gated_ref, f32[1,1024]{1,0:T(1,128)S(1)} %get-tuple-element.43.skip_ref, f32[128,128]{1,0:T(8,128)S(1)} %get-tuple-element.44.response_ref), custom_call_target="tpu_custom_call" | custom-call | flops 1000000000 | bytes 10000000 | tf_op jit(solution)/shard_map/inside/pallas_call | solution.py:55
  17.9 2.2 %collective-permute-start.4 = (bf16[512,1024]{1,0:T(8,128)(2,1)S(1)}, bf16[512,1024]{1,0:T(8,128)(2,1)}, u32[]{:S(2)}, u32[]{:S(2)}) collective-permute-start(bf16[512,1024]{1,0:T(8,128)(2,1)S(1)} %copy-done), channel_id=1, source_target_pairs={{0,16},{4,12},{8,24},{12,4},{16,0},{20,28},{24,8},{28,20},{1,17},{... | collective-permute-start | bytes 3145736 | tf_op jit(solution)/shard_map/ppermute | solution.py:316
  20.1 0.1 pad_add_fusion.at_ref
  20.2 2.5 %all-to-all-done.ends_ref = bf16[8,16,1024]{2,1,0:T(8,128)(2,1)S(1)} async-done(((bf16[8,16,1024]{2,1,0:T(8,128)(2,1)}), bf16[8,16,1024]{2,1,0:T(8,128)(2,1)S(1)}, u32[]{:S(2)}, u32[]{:S(2)}) %all-to-all-start) | async-done | bytes 262176 | tf_op jit(solution)/shard_map/all_to_all | solution.py:372
  22.6 0.8 %finish.3 = bf16[128,512]{1,0:T(8,128)(2,1)S(1)} custom-call(s32[2]{0:T(128)S(1)} %pad_add_fusion.1.at_ref, bf16[8,16,1024]{2,1,0:T(8,128)(2,1)S(1)} %all-to-all-done.ends_ref, f32[16,1024]{1,0:T(8,128)S(1)} %get-tuple-element.38.step_ref, bf16[128,2048]{1,0:T(8,128)(2,1)S(1)} %get-tuple-element.39.lift_ref, ...), custom_call_target="tpu_custom_call" | custom-call | flops 3000000000 | bytes 30000000 | tf_op jit(solution)/shard_map/finish/pallas_call | solution.py:55
  23.5 0.1 collective-permute-start.1
  23.6 0.8 %finish.2 = bf16[128,512]{1,0:T(8,128)(2,1)S(1)} custom-call(s32[2]{0:T(128)S(1)} %pad_add_fusion.at_ref, bf16[8,16,1024]{2,1,0:T(8,128)(2,1)S(1)} %all-to-all-done.ends_ref, f32[16,1024]{1,0:T(8,128)S(1)} %get-tuple-element.38.step_ref, bf16[128,2048]{1,0:T(8,128)(2,1)S(1)} %get-tuple-element.39.lift_ref, ...), custom_call_target="tpu_custom_call" | custom-call | flops 3000000000 | bytes 30000000 | tf_op jit(solution)/shard_map/finish/pallas_call | solution.py:55
  24.4 0.5 %collective-permute-done.1 = bf16[128,512]{1,0:T(8,128)(2,1)S(1)} collective-permute-done((bf16[128,512]{1,0:T(8,128)(2,1)S(1)}, bf16[128,512]{1,0:T(8,128)(2,1)S(1)}, u32[]{:S(2)}, u32[]{:S(2)}) %collective-permute-start.1) | collective-permute-done | bytes 131104 | tf_op jit(solution)/shard_map/ppermute | solution.py:316
  24.9 3.7 %collective-permute-start.2 = (bf16[256,512]{1,0:T(8,128)(2,1)S(1)}, bf16[256,512]{1,0:T(8,128)(2,1)S(1)}, u32[]{:S(2)}, u32[]{:S(2)}) collective-permute-start(bf16[256,512]{1,0:T(8,128)(2,1)S(1)} %pad_maximum_fusion.own_ref), channel_id=1, source_target_pairs={{0,3},{1,2},{2,1},{3,0},{4,7},{5,6},{6,5},{7,4},{8,11},{9,10},{10,... | collective-permute-start | bytes 786440 | tf_op jit(solution)/shard_map/ppermute | solution.py:325
  28.6 0.8 %collective-permute-start.7 = (bf16[512,1024]{1,0:T(8,128)(2,1)}, bf16[512,1024]{1,0:T(8,128)(2,1)S(1)}, u32[]{:S(2)}, u32[]{:S(2)}) collective-permute-start(bf16[512,1024]{1,0:T(8,128)(2,1)} %collective-permute-done.3.rest_1_), channel_id=1, source_target_pairs={{0,16},{4,12},{8,24},{12,4},{16,0},{20,28},{24,8},{28,20},{1,17},{... | collective-permute-start | bytes 3145736 | tf_op jit(solution)/shard_map/ppermute | solution.py:316
  29.3 0.1 stack.44.at_ref
  29.4 6.6 %collective-permute-done.2.across_ref = bf16[256,512]{1,0:T(8,128)(2,1)S(1)} collective-permute-done((bf16[256,512]{1,0:T(8,128)(2,1)S(1)}, bf16[256,512]{1,0:T(8,128)(2,1)S(1)}, u32[]{:S(2)}, u32[]{:S(2)}) %collective-permute-start.2) | collective-permute-done | bytes 262176 | tf_op jit(solution)/shard_map/ppermute | solution.py:325
  36.0 0.0 collective-permute-done.4.rest_2_
  36.0 4.5 %collective-permute-start.5 = (bf16[256,512]{1,0:T(8,128)(2,1)S(1)}, bf16[256,512]{1,0:T(8,128)(2,1)S(1)}, u32[]{:S(2)}, u32[]{:S(2)}) collective-permute-start(bf16[256,512]{1,0:T(8,128)(2,1)S(1)} %collective-permute-done.2.across_ref), channel_id=1, source_target_pairs={{0,1},{1,0},{2,3},{3,2},{4,5},{5,4},{6,7},{7,6},{8,9},{9,8},{10,11... | collective-permute-start | bytes 786440 | tf_op jit(solution)/shard_map/ppermute | solution.py:325
  40.5 0.5 collective-permute-done.6.beside_ref
  41.0 2.9 %early.1 = (f32[256,1024]{1,0:T(8,128)S(1)}, bf16[512,1024]{1,0:T(8,128)(2,1)S(1)}, bf16[256,512]{1,0:T(8,128)(2,1)S(1)}) custom-call(s32[5]{0:T(128)S(1)} %stack.44.at_ref, bf16[256,512]{1,0:T(8,128)(2,1)S(1)} %pad_maximum_fusion.own_ref, bf16[256,512]{1,0:T(8,128)(2,1)S(1)} %collective-permute-done.6.beside_ref, ...), custom_call_target="tpu_custom_call" | custom-call | flops 10000000000 | bytes 100000000 | tf_op jit(solution)/shard_map/early/pallas_call | solution.py:55
  43.9 0.7 %collective-permute-done.7.weight_ref = bf16[512,1024]{1,0:T(8,128)(2,1)S(1)} collective-permute-done((bf16[512,1024]{1,0:T(8,128)(2,1)}, bf16[512,1024]{1,0:T(8,128)(2,1)S(1)}, u32[]{:S(2)}, u32[]{:S(2)}) %collective-permute-start.7) | collective-permute-done | bytes 1048608 | tf_op jit(solution)/shard_map/ppermute | solution.py:316
  44.6 1.1 %joined.1 = (f32[256,1024]{1,0:T(8,128)S(1)}, bf16[512,1024]{1,0:T(8,128)(2,1)S(1)}) custom-call(s32[5]{0:T(128)S(1)} %stack.44.at_ref, f32[256,1024]{1,0:T(8,128)S(1)} %get-tuple-element.47.total_ref, bf16[512,1024]{1,0:T(8,128)(2,1)S(1)} %get-tuple-element.48.rows_ref, bf16[256,512]{1,0:T(8,128)(2,1)S(1)} %get-tuple-element.49.block_ref, ...), custom_call_target="tpu_custom_call" | custom-call | tf_op jit(solution)/shard_map/joined/pallas_call | solution.py:55
  45.7 0.8 %collective-permute-done.5.beyond_ref = bf16[256,512]{1,0:T(8,128)(2,1)S(1)} collective-permute-done((bf16[256,512]{1,0:T(8,128)(2,1)S(1)}, bf16[256,512]{1,0:T(8,128)(2,1)S(1)}, u32[]{:S(2)}, u32[]{:S(2)}) %collective-permute-start.5) | collective-permute-done | bytes 262176 | tf_op jit(solution)/shard_map/ppermute | solution.py:325
  46.5 0.3 late.3
  46.8 0.1 collective-permute-start.8
  46.9 0.3 late.2
  47.2 1.2 %collective-permute-done.8 = bf16[128,1024]{1,0:T(8,128)(2,1)S(1)} collective-permute-done((bf16[128,1024]{1,0:T(8,128)(2,1)S(1)}, bf16[128,1024]{1,0:T(8,128)(2,1)S(1)}, u32[]{:S(2)}, u32[]{:S(2)}) %collective-permute-start.8) | collective-permute-done | bytes 262176 | tf_op jit(solution)/shard_map/ppermute | solution.py:316
  48.4 0.8 %add_convert_fusion = bf16[128,1024]{1,0:T(8,128)(2,1)} fusion(f32[128,1024]{1,0:T(8,128)S(1)} %late.2, bf16[128,1024]{1,0:T(8,128)(2,1)S(1)} %collective-permute-done.8), kind=kLoop, calls=%fused_computation | loop fusion | flops 393216 | bytes 1048576 | tf_op jit(solution)/shard_map/convert_element_type | solution.py:458
  (5 shorter events, 0.0 us)
Async XLA Ops:
  0.0 17.9 %collective-permute-start.3 = (bf16[512,1024]{1,0:T(8,128)(2,1)}, bf16[512,1024]{1,0:T(8,128)(2,1)}, u32[]{:S(2)}, u32[]{:S(2)}) collective-permute-start(bf16[512,1024]{1,0:T(8,128)(2,1)} %rest_0_.1), channel_id=1, source_target_pairs={{0,8},{4,20},{8,0},{12,28},{16,24},{20,4},{24,16},{28,12},{1,9},{5... | collective-permute-start | bytes 3145736 | tf_op jit(solution)/shard_map/ppermute | solution.py:316
  4.5 4.9 %collective-permute-start = (bf16[3,8,1024]{2,1,0:T(8,128)(2,1)S(1)}, bf16[3,8,1024]{2,1,0:T(8,128)(2,1)S(1)}, u32[]{:S(2)}, u32[]{:S(2)}) collective-permute-start(bf16[3,8,1024]{2,1,0:T(8,128)(2,1)S(1)} %get-tuple-element.29), channel_id=1, source_target_pairs={{0,4},{4,8},{8,12},{12,16},{16,20},{20,24},{24,28},{1,5},{5,9},{9,... | collective-permute-start | bytes 147464 | tf_op jit(solution)/shard_map/ppermute | solution.py:26
  10.7 11.9 %all-to-all-start = ((bf16[8,16,1024]{2,1,0:T(8,128)(2,1)}), bf16[8,16,1024]{2,1,0:T(8,128)(2,1)S(1)}, u32[]{:S(2)}, u32[]{:S(2)}) async-start(bf16[8,16,1024]{2,1,0:T(8,128)(2,1)} %get-tuple-element.37), calls=%async_computation | async-start | bytes 524288 | tf_op jit(solution)/shard_map/all_to_all | solution.py:372
  15.6 2.3 %copy-start = (bf16[512,1024]{1,0:T(8,128)(2,1)S(1)}, bf16[512,1024]{1,0:T(8,128)(2,1)}, u32[]{:S(2)}) copy-start(bf16[512,1024]{1,0:T(8,128)(2,1)} %rest_0_.1) | copy-start | bytes 3145732
  17.9 18.1 %collective-permute-start.4 = (bf16[512,1024]{1,0:T(8,128)(2,1)S(1)}, bf16[512,1024]{1,0:T(8,128)(2,1)}, u32[]{:S(2)}, u32[]{:S(2)}) collective-permute-start(bf16[512,1024]{1,0:T(8,128)(2,1)S(1)} %copy-done), channel_id=1, source_target_pairs={{0,16},{4,12},{8,24},{12,4},{16,0},{20,28},{24,8},{28,20},{1,17},{... | collective-permute-start | bytes 3145736 | tf_op jit(solution)/shard_map/ppermute | solution.py:316
  23.5 1.4 %collective-permute-start.1 = (bf16[128,512]{1,0:T(8,128)(2,1)S(1)}, bf16[128,512]{1,0:T(8,128)(2,1)S(1)}, u32[]{:S(2)}, u32[]{:S(2)}) collective-permute-start(bf16[128,512]{1,0:T(8,128)(2,1)S(1)} %finish.3), channel_id=1, source_target_pairs={{0,4},{4,0},{8,12},{12,8},{16,20},{20,16},{24,28},{28,24},{1,5},{5... | collective-permute-start | bytes 393224 | tf_op jit(solution)/shard_map/ppermute | solution.py:316
  24.9 11.1 %collective-permute-start.2 = (bf16[256,512]{1,0:T(8,128)(2,1)S(1)}, bf16[256,512]{1,0:T(8,128)(2,1)S(1)}, u32[]{:S(2)}, u32[]{:S(2)}) collective-permute-start(bf16[256,512]{1,0:T(8,128)(2,1)S(1)} %pad_maximum_fusion.own_ref), channel_id=1, source_target_pairs={{0,3},{1,2},{2,1},{3,0},{4,7},{5,6},{6,5},{7,4},{8,11},{9,10},{10,... | collective-permute-start | bytes 786440 | tf_op jit(solution)/shard_map/ppermute | solution.py:325
  28.6 12.4 %collective-permute-start.6 = (bf16[256,512]{1,0:T(8,128)(2,1)S(1)}, bf16[256,512]{1,0:T(8,128)(2,1)S(1)}, u32[]{:S(2)}, u32[]{:S(2)}) collective-permute-start(bf16[256,512]{1,0:T(8,128)(2,1)S(1)} %pad_maximum_fusion.own_ref), channel_id=1, source_target_pairs={{0,1},{1,0},{2,3},{3,2},{4,5},{5,4},{6,7},{7,6},{8,9},{9,8},{10,11... | collective-permute-start | bytes 786440 | tf_op jit(solution)/shard_map/ppermute | solution.py:325
  28.6 16.1 %collective-permute-start.7 = (bf16[512,1024]{1,0:T(8,128)(2,1)}, bf16[512,1024]{1,0:T(8,128)(2,1)S(1)}, u32[]{:S(2)}, u32[]{:S(2)}) collective-permute-start(bf16[512,1024]{1,0:T(8,128)(2,1)} %collective-permute-done.3.rest_1_), channel_id=1, source_target_pairs={{0,16},{4,12},{8,24},{12,4},{16,0},{20,28},{24,8},{28,20},{1,17},{... | collective-permute-start | bytes 3145736 | tf_op jit(solution)/shard_map/ppermute | solution.py:316
  36.0 10.5 %collective-permute-start.5 = (bf16[256,512]{1,0:T(8,128)(2,1)S(1)}, bf16[256,512]{1,0:T(8,128)(2,1)S(1)}, u32[]{:S(2)}, u32[]{:S(2)}) collective-permute-start(bf16[256,512]{1,0:T(8,128)(2,1)S(1)} %collective-permute-done.2.across_ref), channel_id=1, source_target_pairs={{0,1},{1,0},{2,3},{3,2},{4,5},{5,4},{6,7},{7,6},{8,9},{9,8},{10,11... | collective-permute-start | bytes 786440 | tf_op jit(solution)/shard_map/ppermute | solution.py:325
  46.8 1.6 %collective-permute-start.8 = (bf16[128,1024]{1,0:T(8,128)(2,1)S(1)}, bf16[128,1024]{1,0:T(8,128)(2,1)S(1)}, u32[]{:S(2)}, u32[]{:S(2)}) collective-permute-start(bf16[128,1024]{1,0:T(8,128)(2,1)S(1)} %late.3), channel_id=1, source_target_pairs={{0,4},{4,0},{8,12},{12,8},{16,20},{20,16},{24,28},{28,24},{1,5},{5... | collective-permute-start | bytes 786440 | tf_op jit(solution)/shard_map/ppermute | solution.py:316

commit v20 on v19

--- a/solution.py
+++ b/solution.py
@@ -268,7 +268,11 @@
     unrolled(share // TILE, tile)
 
 
-def early_kernel(at_ref, own_ref, beside_ref, across_ref, *rest):
+def corner_kernel(block_ref, corner_ref):
+    corner_ref[...] = block_ref[: corner_ref.shape[0], : corner_ref.shape[1]]
+
+
+def early_kernel(at_ref, own_ref, beside_ref, theirs_ref, across_ref, corner_ref, *rest):
     *weight_hbms, total_ref, rows_ref, block_ref, layers_ref, weight_ref, sems = rest
     count = len(weight_hbms)
     layer = at_ref[0]
@@ -279,8 +283,12 @@
         copy.start()
     for at, fetch in enumerate(fetches):
         pl.when(at_ref[1 + at] == last)(fetch.start)
-    for bits, ref in ((0, own_ref), (1, beside_ref), (3, across_ref)):
-        layers_ref[layer ^ bits] = ref[...]
+    length = beside_ref.shape[0]
+    layers_ref[layer] = own_ref[...]
+    layers_ref[layer ^ 1, :length] = beside_ref[...]
+    layers_ref[layer ^ 1, length:] = theirs_ref[...]
+    layers_ref[layer ^ 1, : corner_ref.shape[0], : corner_ref.shape[1]] = corner_ref[...]
+    layers_ref[layer ^ 3] = across_ref[...]
     layers_ref[last] = jnp.zeros_like(own_ref)
     block_ref[...] = layers_ref[at_ref[1 + count]]
     for at, copy in enumerate(copies):
@@ -406,10 +414,12 @@
         by_core = by_core.reshape(CORES, length, share)
         mine = lax.dynamic_index_in_dim(by_core, core, 0, keepdims=False)
         other = lax.dynamic_index_in_dim(by_core, 1 - core, 0, keepdims=False)
-    block = jnp.concatenate([mine, swap(other, 1)], axis=0)
+    theirs = swap(other, 1)
+    block = jnp.concatenate([mine, theirs], axis=0)
     layer = lax.axis_index("tp").astype(jnp.int32)
-    beside, across = trade(block, 1), trade(block, 3)
-    beyond = trade(after(across, other_near) if square else across, 1)
+    beside, beside_theirs, across = trade(mine, 1), trade(theirs, 1), trade(block, 3)
+    (corner,) = call(corner_kernel, [((2 * ROWS, TILE), BF16)], "corner", beside, flops=3 * 10**9)
+    beyond = trade(after(across, (corner, other_near)) if square else across, 1)
     if square:
         diagonal = swap(after(near, block), 4, 2)
         weight = (out_weight, near, other_near, diagonal)
@@ -426,9 +436,9 @@
         early_kernel,
         [((CORES * length, features), F32), ((share, features), BF16), (block.shape, BF16)],
         "early",
-        at, block, beside, across,
+        at, block, beside, beside_theirs, across, corner,
         *(pltpu.with_memory_space_constraint(part, pltpu.HBM) for part in sooner),
-        specs=smem + whole(3) + [pl.BlockSpec(memory_space=pltpu.HBM)] * len(sooner),
+        specs=smem + whole(5) + [pl.BlockSpec(memory_space=pltpu.HBM)] * len(sooner),
         scratch=[
             pltpu.VMEM((layers,) + block.shape, BF16),
             pltpu.VMEM((len(sooner), share, features), BF16),

time: 49.5 us -> 50.8 us (1.026)
  waiting for transfers between devices: 12.8 us -> 14.2 us
    ppermute x3 -> x4, waiting for transfers between devices: 7.89 us -> 10.4 us  [trade(): lax.ppermute(value, 'tp', [(source, source ^ bits) for source in range(co...]
    ppermute x5, waiting for transfers between devices: 2.44 us -> 1.29 us  [swap(): return lax.ppermute(value, 'ctx', pairs)]
    ppermute x3 -> x4, starting transfers between devices: 8.16 us -> 8.07 us  [trade(): lax.ppermute(value, 'tp', [(source, source ^ bits) for source in range(co...]
    pallas_call x10 -> x11, Pallas kernels: 14.8 us -> 14.8 us  [call(): pl.pallas_call(kernel, out_shape=tuple((jax.ShapeDtypeStruct(*out) for ou...]
  transfers between devices with their start and end apart: 10 -> 11, of which waited for: 7 -> 6; matrix products, arithmetic and copies ran while one was open for 1% -> 0% of each run, Pallas kernels for 29% -> 29%
where the time goes in v20:
time: 50.8 us; the launch traced here: 50.5 us
  starting transfers between devices  20.4 us (40%)
  Pallas kernels  14.8 us (29%)
  waiting for transfers between devices  14.2 us (28%)
  other arithmetic  0.93 us (2%)
    pallas_call x11, Pallas kernels, call(): pl.pallas_call(kernel, out_shape=tuple((jax.ShapeDtypeStruct(*out) for ou...  14.8 us
    ppermute x4, waiting for transfers between devices, trade(): lax.ppermute(value, 'tp', [(source, source ^ bits) for source in range(co...  10.4 us
    ppermute x4, starting transfers between devices, trade(): lax.ppermute(value, 'tp', [(source, source ^ bits) for source in range(co...  8.07 us
    ppermute x5, starting transfers between devices, swap(): return lax.ppermute(value, 'ctx', pairs)  6.03 us
    all_to_all x1, starting transfers between devices, local(): lax.all_to_all(ends, 'ctx', split_axis=0, concat_axis=0, tiled=True)  4.82 us
    all_to_all x1, waiting for transfers between devices, local(): lax.all_to_all(ends, 'ctx', split_axis=0, concat_axis=0, tiled=True)  2.46 us
    ppermute x1, starting transfers between devices, from_behind(): lax.ppermute(value, axis, [(source, source + steps) for source in range(l...  1.49 us
    ppermute x5, waiting for transfers between devices, swap(): return lax.ppermute(value, 'ctx', pairs)  1.29 us
  transfers between devices with their start and end apart: 11, of which 6 were waited for; matrix products, arithmetic and copies ran while one was open for 0% of the time, Pallas kernels for 29%

profile of v20, /device:TPU:0, one launch (start us, length us, event | category | flops | bytes accessed | tf_op | source)
XLA Modules:
  0.0 50.5 jit_solution(7330621511743999771)
XLA Ops:
  0.0 2.9 %collective-permute-start.4 = (bf16[512,1024]{1,0:T(8,128)(2,1)}, bf16[512,1024]{1,0:T(8,128)(2,1)}, u32[]{:S(2)}, u32[]{:S(2)}) collective-permute-start(bf16[512,1024]{1,0:T(8,128)(2,1)} %rest_0_.1), channel_id=1, source_target_pairs={{0,8},{4,20},{8,0},{12,28},{16,24},{20,4},{24,16},{28,12},{1,9},{5... | collective-permute-start | bytes 3145736 | tf_op jit(solution)/shard_map/ppermute | solution.py:324
  2.9 1.5 %tails.1 = (bf16[3,8,1024]{2,1,0:T(8,128)(2,1)S(1)}, bf16[3,1024,128]{2,1,0:T(8,128)(2,1)S(1)}, f32[3,7,1024]{2,1,0:T(8,128)S(1)}, f32[16,128]{1,0:T(8,128)S(1)}...) custom-call(bf16[3,1024,128]{2,1,0:T(8,128)(2,1)} %refs_0_.1, f32[3,7,1024]{2,1,0:T(8,128)} %refs_1_.1, ...), custom_call_target="tpu_custom_call" | custom-call | flops 100000000 | bytes 1000000 | tf_op jit(solution)/shard_map/tails/pallas_call | solution.py:55
  4.5 1.5 %collective-permute-start = (bf16[3,8,1024]{2,1,0:T(8,128)(2,1)S(1)}, bf16[3,8,1024]{2,1,0:T(8,128)(2,1)S(1)}, u32[]{:S(2)}, u32[]{:S(2)}) collective-permute-start(bf16[3,8,1024]{2,1,0:T(8,128)(2,1)S(1)} %get-tuple-element.29), channel_id=1, source_target_pairs={{0,4},{4,8},{8,12},{12,16},{16,20},{20,24},{24,28},{1,5},{5,9},{9,... | collective-permute-start | bytes 147464 | tf_op jit(solution)/shard_map/ppermute | solution.py:26
  6.0 3.3 %prepare.1 = (f32[3,8,1024]{2,1,0:T(8,128)S(1)}, bf16[128,1024]{1,0:T(8,128)(2,1)S(1)}, f32[128,1024]{1,0:T(8,128)S(1)}, bf16[2048,128]{1,0:T(8,128)(2,1)S(1)}, ...) custom-call(bf16[3,1024,128]{2,1,0:T(8,128)(2,1)S(1)} %get-tuple-element.30.streams_ref, ...), custom_call_target="tpu_custom_call" | custom-call | flops 1000000000 | bytes 10000000 | tf_op jit(solution)/shard_map/prepare/pallas_call | solution.py:55
  9.3 0.0 collective-permute-done.before_ref
  9.3 1.4 %states.1 = (bf16[8,16,1024]{2,1,0:T(8,128)(2,1)}, bf16[128,1024]{1,0:T(8,128)(2,1)S(1)}, f32[8,1024]{1,0:T(8,128)S(1)}) custom-call(bf16[3,8,1024]{2,1,0:T(8,128)(2,1)S(1)} %collective-permute-done.before_ref, f32[3,8,1024]{2,1,0:T(8,128)S(1)} %get-tuple-element.34.heads_ref, f32[3,7,1024]{2,1,0:T(8,128)S(1)} %get-tuple-element.31.taps_ref, ...), custom_call_target="tpu_custom_call" | custom-call | flops 100000000 | bytes 1000000 | tf_op jit(solution)/shard_map/states/pallas_call | solution.py:55
  10.7 4.8 %all-to-all-start = ((bf16[8,16,1024]{2,1,0:T(8,128)(2,1)}), bf16[8,16,1024]{2,1,0:T(8,128)(2,1)S(1)}, u32[]{:S(2)}, u32[]{:S(2)}) async-start(bf16[8,16,1024]{2,1,0:T(8,128)(2,1)} %get-tuple-element.37), calls=%async_computation | async-start | bytes 524288 | tf_op jit(solution)/shard_map/all_to_all | solution.py:380
  15.5 0.1 pad_add_fusion.1.at_ref
  15.6 2.3 %inside.1.base_ref = f32[128,1024]{1,0:T(8,128)S(1)} custom-call(bf16[128,1024]{1,0:T(8,128)(2,1)S(1)} %get-tuple-element.42.gated_ref, f32[1,1024]{1,0:T(1,128)S(1)} %get-tuple-element.43.skip_ref, f32[128,128]{1,0:T(8,128)S(1)} %get-tuple-element.44.response_ref), custom_call_target="tpu_custom_call" | custom-call | flops 1000000000 | bytes 10000000 | tf_op jit(solution)/shard_map/inside/pallas_call | solution.py:55
  17.9 2.2 %collective-permute-start.5 = (bf16[512,1024]{1,0:T(8,128)(2,1)S(1)}, bf16[512,1024]{1,0:T(8,128)(2,1)}, u32[]{:S(2)}, u32[]{:S(2)}) collective-permute-start(bf16[512,1024]{1,0:T(8,128)(2,1)S(1)} %copy-done), channel_id=1, source_target_pairs={{0,16},{4,12},{8,24},{12,4},{16,0},{20,28},{24,8},{28,20},{1,17},{... | collective-permute-start | bytes 3145736 | tf_op jit(solution)/shard_map/ppermute | solution.py:324
  20.1 0.1 pad_add_fusion.at_ref
  20.2 2.5 %all-to-all-done.ends_ref = bf16[8,16,1024]{2,1,0:T(8,128)(2,1)S(1)} async-done(((bf16[8,16,1024]{2,1,0:T(8,128)(2,1)}), bf16[8,16,1024]{2,1,0:T(8,128)(2,1)S(1)}, u32[]{:S(2)}, u32[]{:S(2)}) %all-to-all-start) | async-done | bytes 262176 | tf_op jit(solution)/shard_map/all_to_all | solution.py:380
  22.6 0.8 %finish.3 = bf16[128,512]{1,0:T(8,128)(2,1)S(1)} custom-call(s32[2]{0:T(128)S(1)} %pad_add_fusion.1.at_ref, bf16[8,16,1024]{2,1,0:T(8,128)(2,1)S(1)} %all-to-all-done.ends_ref, f32[16,1024]{1,0:T(8,128)S(1)} %get-tuple-element.38.step_ref, bf16[128,2048]{1,0:T(8,128)(2,1)S(1)} %get-tuple-element.39.lift_ref, ...), custom_call_target="tpu_custom_call" | custom-call | flops 3000000000 | bytes 30000000 | tf_op jit(solution)/shard_map/finish/pallas_call | solution.py:55
  23.5 0.1 collective-permute-start.1
  23.6 0.8 %finish.2 = bf16[128,512]{1,0:T(8,128)(2,1)S(1)} custom-call(s32[2]{0:T(128)S(1)} %pad_add_fusion.at_ref, bf16[8,16,1024]{2,1,0:T(8,128)(2,1)S(1)} %all-to-all-done.ends_ref, f32[16,1024]{1,0:T(8,128)S(1)} %get-tuple-element.38.step_ref, bf16[128,2048]{1,0:T(8,128)(2,1)S(1)} %get-tuple-element.39.lift_ref, ...), custom_call_target="tpu_custom_call" | custom-call | flops 3000000000 | bytes 30000000 | tf_op jit(solution)/shard_map/finish/pallas_call | solution.py:55
  24.4 1.6 %collective-permute-start.3 = (bf16[128,512]{1,0:T(8,128)(2,1)S(1)}, bf16[128,512]{1,0:T(8,128)(2,1)S(1)}, u32[]{:S(2)}, u32[]{:S(2)}) collective-permute-start(bf16[128,512]{1,0:T(8,128)(2,1)S(1)} %finish.2), channel_id=1, source_target_pairs={{0,1},{1,0},{2,3},{3,2},{4,5},{5,4},{6,7},{7,6},{8,9},{9,8},{10,11... | collective-permute-start | bytes 393224 | tf_op jit(solution)/shard_map/ppermute | solution.py:333
  26.0 0.1 stack.44.at_ref
  26.1 2.5 %collective-permute-start.2 = (bf16[256,512]{1,0:T(8,128)(2,1)S(1)}, bf16[256,512]{1,0:T(8,128)(2,1)S(1)}, u32[]{:S(2)}, u32[]{:S(2)}) collective-permute-start(bf16[256,512]{1,0:T(8,128)(2,1)S(1)} %pad_maximum_fusion.own_ref), channel_id=1, source_target_pairs={{0,3},{1,2},{2,1},{3,0},{4,7},{5,6},{6,5},{7,4},{8,11},{9,10},{10,... | collective-permute-start | bytes 786440 | tf_op jit(solution)/shard_map/ppermute | solution.py:333
  28.7 0.7 %collective-permute-start.7 = (bf16[128,512]{1,0:T(8,128)(2,1)S(1)}, bf16[128,512]{1,0:T(8,128)(2,1)S(1)}, u32[]{:S(2)}, u32[]{:S(2)}) collective-permute-start(bf16[128,512]{1,0:T(8,128)(2,1)S(1)} %collective-permute-done.1), channel_id=1, source_target_pairs={{0,1},{1,0},{2,3},{3,2},{4,5},{5,4},{6,7},{7,6},{8,9},{9,8},{10,11... | collective-permute-start | bytes 393224 | tf_op jit(solution)/shard_map/ppermute | solution.py:333
  29.3 0.8 %collective-permute-start.8 = (bf16[512,1024]{1,0:T(8,128)(2,1)}, bf16[512,1024]{1,0:T(8,128)(2,1)S(1)}, u32[]{:S(2)}, u32[]{:S(2)}) collective-permute-start(bf16[512,1024]{1,0:T(8,128)(2,1)} %collective-permute-done.4.rest_1_), channel_id=1, source_target_pairs={{0,16},{4,12},{8,24},{12,4},{16,0},{20,28},{24,8},{28,20},{1,17},{... | collective-permute-start | bytes 3145736 | tf_op jit(solution)/shard_map/ppermute | solution.py:324
  30.1 0.2 collective-permute-done.3.block_ref.beside_ref
  30.4 8.1 %collective-permute-done.2.across_ref = bf16[256,512]{1,0:T(8,128)(2,1)S(1)} collective-permute-done((bf16[256,512]{1,0:T(8,128)(2,1)S(1)}, bf16[256,512]{1,0:T(8,128)(2,1)S(1)}, u32[]{:S(2)}, u32[]{:S(2)}) %collective-permute-start.2) | collective-permute-done | bytes 262176 | tf_op jit(solution)/shard_map/ppermute | solution.py:333
  38.4 3.2 %collective-permute-start.6 = (bf16[256,512]{1,0:T(8,128)(2,1)S(1)}, bf16[256,512]{1,0:T(8,128)(2,1)S(1)}, u32[]{:S(2)}, u32[]{:S(2)}) collective-permute-start(bf16[256,512]{1,0:T(8,128)(2,1)S(1)} %collective-permute-done.2.across_ref), channel_id=1, source_target_pairs={{0,1},{1,0},{2,3},{3,2},{4,5},{5,4},{6,7},{7,6},{8,9},{9,8},{10,11... | collective-permute-start | bytes 786440 | tf_op jit(solution)/shard_map/ppermute | solution.py:333
  41.6 2.9 %early.1 = (f32[256,1024]{1,0:T(8,128)S(1)}, bf16[512,1024]{1,0:T(8,128)(2,1)S(1)}, bf16[256,512]{1,0:T(8,128)(2,1)S(1)}) custom-call(s32[5]{0:T(128)S(1)} %stack.44.at_ref, bf16[256,512]{1,0:T(8,128)(2,1)S(1)} %pad_maximum_fusion.own_ref, bf16[128,512]{1,0:T(8,128)(2,1)S(1)} %collective-permute-done.3.block_ref.beside_ref, ...), custom_call_target="tpu_custom_call" | custom-call | flops 10000000000 | bytes 100000000 | tf_op jit(solution)/shard_map/early/pallas_call | solution.py:55
  44.5 0.1 collective-permute-done.8.weight_ref
  44.6 1.1 %joined.1 = (f32[256,1024]{1,0:T(8,128)S(1)}, bf16[512,1024]{1,0:T(8,128)(2,1)S(1)}) custom-call(s32[5]{0:T(128)S(1)} %stack.44.at_ref, f32[256,1024]{1,0:T(8,128)S(1)} %get-tuple-element.47.total_ref, bf16[512,1024]{1,0:T(8,128)(2,1)S(1)} %get-tuple-element.48.rows_ref, bf16[256,512]{1,0:T(8,128)(2,1)S(1)} %get-tuple-element.49.block_ref, ...), custom_call_target="tpu_custom_call" | custom-call | tf_op jit(solution)/shard_map/joined/pallas_call | solution.py:55
  45.7 2.1 %collective-permute-done.6.beyond_ref = bf16[256,512]{1,0:T(8,128)(2,1)S(1)} collective-permute-done((bf16[256,512]{1,0:T(8,128)(2,1)S(1)}, bf16[256,512]{1,0:T(8,128)(2,1)S(1)}, u32[]{:S(2)}, u32[]{:S(2)}) %collective-permute-start.6) | collective-permute-done | bytes 262176 | tf_op jit(solution)/shard_map/ppermute | solution.py:333
  47.8 0.3 late.3
  48.2 0.1 collective-permute-start.9
  48.2 0.3 late.2
  48.6 1.2 %collective-permute-done.9 = bf16[128,1024]{1,0:T(8,128)(2,1)S(1)} collective-permute-done((bf16[128,1024]{1,0:T(8,128)(2,1)S(1)}, bf16[128,1024]{1,0:T(8,128)(2,1)S(1)}, u32[]{:S(2)}, u32[]{:S(2)}) %collective-permute-start.9) | collective-permute-done | bytes 262176 | tf_op jit(solution)/shard_map/ppermute | solution.py:324
  49.8 0.8 %add_convert_fusion = bf16[128,1024]{1,0:T(8,128)(2,1)} fusion(f32[128,1024]{1,0:T(8,128)S(1)} %late.2, bf16[128,1024]{1,0:T(8,128)(2,1)S(1)} %collective-permute-done.9), kind=kLoop, calls=%fused_computation | loop fusion | flops 393216 | bytes 1048576 | tf_op jit(solution)/shard_map/convert_element_type | solution.py:468
  (8 shorter events, 0.0 us)
Async XLA Ops:
  0.0 17.9 %collective-permute-start.4 = (bf16[512,1024]{1,0:T(8,128)(2,1)}, bf16[512,1024]{1,0:T(8,128)(2,1)}, u32[]{:S(2)}, u32[]{:S(2)}) collective-permute-start(bf16[512,1024]{1,0:T(8,128)(2,1)} %rest_0_.1), channel_id=1, source_target_pairs={{0,8},{4,20},{8,0},{12,28},{16,24},{20,4},{24,16},{28,12},{1,9},{5... | collective-permute-start | bytes 3145736 | tf_op jit(solution)/shard_map/ppermute | solution.py:324
  4.5 4.9 %collective-permute-start = (bf16[3,8,1024]{2,1,0:T(8,128)(2,1)S(1)}, bf16[3,8,1024]{2,1,0:T(8,128)(2,1)S(1)}, u32[]{:S(2)}, u32[]{:S(2)}) collective-permute-start(bf16[3,8,1024]{2,1,0:T(8,128)(2,1)S(1)} %get-tuple-element.29), channel_id=1, source_target_pairs={{0,4},{4,8},{8,12},{12,16},{16,20},{20,24},{24,28},{1,5},{5,9},{9,... | collective-permute-start | bytes 147464 | tf_op jit(solution)/shard_map/ppermute | solution.py:26
  10.7 11.9 %all-to-all-start = ((bf16[8,16,1024]{2,1,0:T(8,128)(2,1)}), bf16[8,16,1024]{2,1,0:T(8,128)(2,1)S(1)}, u32[]{:S(2)}, u32[]{:S(2)}) async-start(bf16[8,16,1024]{2,1,0:T(8,128)(2,1)} %get-tuple-element.37), calls=%async_computation | async-start | bytes 524288 | tf_op jit(solution)/shard_map/all_to_all | solution.py:380
  15.6 2.3 %copy-start = (bf16[512,1024]{1,0:T(8,128)(2,1)S(1)}, bf16[512,1024]{1,0:T(8,128)(2,1)}, u32[]{:S(2)}) copy-start(bf16[512,1024]{1,0:T(8,128)(2,1)} %rest_0_.1) | copy-start | bytes 3145732
  17.9 20.5 %collective-permute-start.5 = (bf16[512,1024]{1,0:T(8,128)(2,1)S(1)}, bf16[512,1024]{1,0:T(8,128)(2,1)}, u32[]{:S(2)}, u32[]{:S(2)}) collective-permute-start(bf16[512,1024]{1,0:T(8,128)(2,1)S(1)} %copy-done), channel_id=1, source_target_pairs={{0,16},{4,12},{8,24},{12,4},{16,0},{20,28},{24,8},{28,20},{1,17},{... | collective-permute-start | bytes 3145736 | tf_op jit(solution)/shard_map/ppermute | solution.py:324
  23.5 2.6 %collective-permute-start.1 = (bf16[128,512]{1,0:T(8,128)(2,1)S(1)}, bf16[128,512]{1,0:T(8,128)(2,1)S(1)}, u32[]{:S(2)}, u32[]{:S(2)}) collective-permute-start(bf16[128,512]{1,0:T(8,128)(2,1)S(1)} %finish.3), channel_id=1, source_target_pairs={{0,4},{4,0},{8,12},{12,8},{16,20},{20,16},{24,28},{28,24},{1,5},{5... | collective-permute-start | bytes 393224 | tf_op jit(solution)/shard_map/ppermute | solution.py:324
  24.4 6.0 %collective-permute-start.3 = (bf16[128,512]{1,0:T(8,128)(2,1)S(1)}, bf16[128,512]{1,0:T(8,128)(2,1)S(1)}, u32[]{:S(2)}, u32[]{:S(2)}) collective-permute-start(bf16[128,512]{1,0:T(8,128)(2,1)S(1)} %finish.2), channel_id=1, source_target_pairs={{0,1},{1,0},{2,3},{3,2},{4,5},{5,4},{6,7},{7,6},{8,9},{9,8},{10,11... | collective-permute-start | bytes 393224 | tf_op jit(solution)/shard_map/ppermute | solution.py:333
  26.1 12.3 %collective-permute-start.2 = (bf16[256,512]{1,0:T(8,128)(2,1)S(1)}, bf16[256,512]{1,0:T(8,128)(2,1)S(1)}, u32[]{:S(2)}, u32[]{:S(2)}) collective-permute-start(bf16[256,512]{1,0:T(8,128)(2,1)S(1)} %pad_maximum_fusion.own_ref), channel_id=1, source_target_pairs={{0,3},{1,2},{2,1},{3,0},{4,7},{5,6},{6,5},{7,4},{8,11},{9,10},{10,... | collective-permute-start | bytes 786440 | tf_op jit(solution)/shard_map/ppermute | solution.py:333
  28.7 13.0 %collective-permute-start.7 = (bf16[128,512]{1,0:T(8,128)(2,1)S(1)}, bf16[128,512]{1,0:T(8,128)(2,1)S(1)}, u32[]{:S(2)}, u32[]{:S(2)}) collective-permute-start(bf16[128,512]{1,0:T(8,128)(2,1)S(1)} %collective-permute-done.1), channel_id=1, source_target_pairs={{0,1},{1,0},{2,3},{3,2},{4,5},{5,4},{6,7},{7,6},{8,9},{9,8},{10,11... | collective-permute-start | bytes 393224 | tf_op jit(solution)/shard_map/ppermute | solution.py:333
  29.3 15.3 %collective-permute-start.8 = (bf16[512,1024]{1,0:T(8,128)(2,1)}, bf16[512,1024]{1,0:T(8,128)(2,1)S(1)}, u32[]{:S(2)}, u32[]{:S(2)}) collective-permute-start(bf16[512,1024]{1,0:T(8,128)(2,1)} %collective-permute-done.4.rest_1_), channel_id=1, source_target_pairs={{0,16},{4,12},{8,24},{12,4},{16,0},{20,28},{24,8},{28,20},{1,17},{... | collective-permute-start | bytes 3145736 | tf_op jit(solution)/shard_map/ppermute | solution.py:324
  38.4 9.4 %collective-permute-start.6 = (bf16[256,512]{1,0:T(8,128)(2,1)S(1)}, bf16[256,512]{1,0:T(8,128)(2,1)S(1)}, u32[]{:S(2)}, u32[]{:S(2)}) collective-permute-start(bf16[256,512]{1,0:T(8,128)(2,1)S(1)} %collective-permute-done.2.across_ref), channel_id=1, source_target_pairs={{0,1},{1,0},{2,3},{3,2},{4,5},{5,4},{6,7},{7,6},{8,9},{9,8},{10,11... | collective-permute-start | bytes 786440 | tf_op jit(solution)/shard_map/ppermute | solution.py:333
  48.2 1.6 %collective-permute-start.9 = (bf16[128,1024]{1,0:T(8,128)(2,1)S(1)}, bf16[128,1024]{1,0:T(8,128)(2,1)S(1)}, u32[]{:S(2)}, u32[]{:S(2)}) collective-permute-start(bf16[128,1024]{1,0:T(8,128)(2,1)S(1)} %late.3), channel_id=1, source_target_pairs={{0,4},{4,0},{8,12},{12,8},{16,20},{20,16},{24,28},{28,24},{1,5},{5... | collective-permute-start | bytes 786440 | tf_op jit(solution)/shard_map/ppermute | solution.py:324

commit v21 on v19

--- a/solution.py
+++ b/solution.py
@@ -268,7 +268,11 @@
     unrolled(share // TILE, tile)
 
 
-def early_kernel(at_ref, own_ref, beside_ref, across_ref, *rest):
+def corner_kernel(block_ref, corner_ref):
+    corner_ref[...] = block_ref[: corner_ref.shape[0], : corner_ref.shape[1]]
+
+
+def early_kernel(at_ref, own_ref, beside_ref, middle_ref, across_ref, corner_ref, *rest):
     *weight_hbms, total_ref, rows_ref, block_ref, layers_ref, weight_ref, sems = rest
     count = len(weight_hbms)
     layer = at_ref[0]
@@ -279,8 +283,12 @@
         copy.start()
     for at, fetch in enumerate(fetches):
         pl.when(at_ref[1 + at] == last)(fetch.start)
-    for bits, ref in ((0, own_ref), (1, beside_ref), (3, across_ref)):
-        layers_ref[layer ^ bits] = ref[...]
+    edge = (layer == 0) | (layer == 3)
+    corner = tuple(slice(0, size) for size in corner_ref.shape)
+    layers_ref[layer] = own_ref[...]
+    layers_ref[layer ^ 1] = beside_ref[...]
+    layers_ref[layer ^ 3] = jnp.where(edge, across_ref[...], middle_ref[...])
+    layers_ref[(layer ^ 3, *corner)] = jnp.where(edge, across_ref[corner], corner_ref[...])
     layers_ref[last] = jnp.zeros_like(own_ref)
     block_ref[...] = layers_ref[at_ref[1 + count]]
     for at, copy in enumerate(copies):
@@ -305,9 +313,11 @@
     pl.when(jnp.logical_not(latest))(lambda: keep(rows_ref))
 
 
-def late_kernel(first, beyond_ref, total_ref, rows_ref, out_ref):
+def late_kernel(first, at_ref, inwards_ref, outwards_ref, total_ref, rows_ref, out_ref):
     tokens = pl.ds(first, out_ref.shape[0])
-    out_ref[...] = (total_ref[tokens, :] + dot(beyond_ref[tokens, :], rows_ref[...])).astype(out_ref.dtype)
+    edge = (at_ref[0] == 0) | (at_ref[0] == 3)
+    beyond = jnp.where(edge, outwards_ref[tokens, :], inwards_ref[tokens, :])
+    out_ref[...] = (total_ref[tokens, :] + dot(beyond, rows_ref[...])).astype(out_ref.dtype)
 
 
 def swap(value, *bits):
@@ -320,9 +330,8 @@
     return lax.optimization_barrier((value, earlier))[0]
 
 
-def trade(value, bits):
-    count = lax.axis_size("tp")
-    return lax.ppermute(value, "tp", [(source, source ^ bits) for source in range(count)])
+def along(value, *pairs):
+    return lax.ppermute(value, "tp", pairs)
 
 
 def local(streams, conv_weight, rates, residues, skip, out_weight):
@@ -382,7 +391,7 @@
         flops=10**9,
     )
     if square:
-        other_near = swap(after(out_weight, (base, near)), 4, 2)
+        other_near = swap(after(out_weight, (gated, near)), 4, 2)
     me = lax.axis_index("ctx").astype(jnp.int32)
     core = me % CORES
     smem = [pl.BlockSpec(memory_space=pltpu.SMEM)]
@@ -408,8 +417,12 @@
         other = lax.dynamic_index_in_dim(by_core, 1 - core, 0, keepdims=False)
     block = jnp.concatenate([mine, swap(other, 1)], axis=0)
     layer = lax.axis_index("tp").astype(jnp.int32)
-    beside, across = trade(block, 1), trade(block, 3)
-    beyond = trade(after(across, other_near) if square else across, 1)
+    middle = along(block, (1, 2), (2, 1))
+    beside = along(block, (0, 1), (1, 0), (2, 3), (3, 2))
+    across = along(block, (0, 3), (3, 0))
+    (corner,) = call(corner_kernel, [((2 * ROWS, TILE), BF16)], "corner", middle, flops=3 * 10**9)
+    outwards = along(after(middle, corner), (1, 0), (2, 3))
+    inwards = along(after(beside, (corner, other_near)) if square else beside, (1, 2), (2, 1))
     if square:
         diagonal = swap(after(near, block), 4, 2)
         weight = (out_weight, near, other_near, diagonal)
@@ -426,9 +439,9 @@
         early_kernel,
         [((CORES * length, features), F32), ((share, features), BF16), (block.shape, BF16)],
         "early",
-        at, block, beside, across,
+        at, block, beside, middle, across, corner,
         *(pltpu.with_memory_space_constraint(part, pltpu.HBM) for part in sooner),
-        specs=smem + whole(3) + [pl.BlockSpec(memory_space=pltpu.HBM)] * len(sooner),
+        specs=smem + whole(5) + [pl.BlockSpec(memory_space=pltpu.HBM)] * len(sooner),
         scratch=[
             pltpu.VMEM((layers,) + block.shape, BF16),
             pltpu.VMEM((len(sooner), share, features), BF16),
@@ -450,7 +463,8 @@
             functools.partial(late_kernel, side * length),
             [((length, features), kind)],
             "late",
-            beyond, total, last_rows,
+            at, inwards, outwards, total, last_rows,
+            specs=smem + whole(4),
             flops=0,
         )
     other, mine = sides

time: 49.5 us -> 52.9 us (1.069)
  starting transfers between devices: 20.5 us -> 22.6 us
  Pallas kernels: 14.8 us -> 15.8 us
    ppermute x3 -> x5, starting transfers between devices: 8.16 us -> 10.2 us  [along(): return lax.ppermute(value, 'tp', pairs)]
    pallas_call x10 -> x11, Pallas kernels: 14.8 us -> 15.8 us  [call(): pl.pallas_call(kernel, out_shape=tuple((jax.ShapeDtypeStruct(*out) for ou...]
    ppermute x5, waiting for transfers between devices: 2.44 us -> 3.39 us  [swap(): return lax.ppermute(value, 'ctx', pairs)]
    ppermute x3 -> x5, waiting for transfers between devices: 7.89 us -> 7.16 us  [along(): return lax.ppermute(value, 'tp', pairs)]
  transfers between devices with their start and end apart: 10 -> 12, of which waited for: 7 -> 6; matrix products, arithmetic and copies ran while one was open for 1% -> 0% of each run, Pallas kernels for 29% -> 28%
where the time goes in v21:
time: 52.9 us; the launch traced here: 52.6 us
  starting transfers between devices  22.6 us (43%)
  Pallas kernels  15.8 us (30%)
  waiting for transfers between devices  12.9 us (24%)
  other arithmetic  0.94 us (2%)
    pallas_call x11, Pallas kernels, call(): pl.pallas_call(kernel, out_shape=tuple((jax.ShapeDtypeStruct(*out) for ou...  15.8 us
    ppermute x5, starting transfers between devices, along(): return lax.ppermute(value, 'tp', pairs)  10.2 us
    ppermute x5, waiting for transfers between devices, along(): return lax.ppermute(value, 'tp', pairs)  7.16 us
    ppermute x5, starting transfers between devices, swap(): return lax.ppermute(value, 'ctx', pairs)  6.08 us
    all_to_all x1, starting transfers between devices, local(): lax.all_to_all(ends, 'ctx', split_axis=0, concat_axis=0, tiled=True)  4.82 us
    ppermute x5, waiting for transfers between devices, swap(): return lax.ppermute(value, 'ctx', pairs)  3.39 us
    all_to_all x1, waiting for transfers between devices, local(): lax.all_to_all(ends, 'ctx', split_axis=0, concat_axis=0, tiled=True)  2.38 us
    ppermute x1, starting transfers between devices, from_behind(): lax.ppermute(value, axis, [(source, source + steps) for source in range(l...  1.49 us
  transfers between devices with their start and end apart: 12, of which 6 were waited for; matrix products, arithmetic and copies ran while one was open for 0% of the time, Pallas kernels for 28%

profile of v21, /device:TPU:0, one launch (start us, length us, event | category | flops | bytes accessed | tf_op | source)
XLA Modules:
  0.0 52.6 jit_solution(484942276724100262)
XLA Ops:
  0.0 2.9 %collective-permute-start.4 = (bf16[512,1024]{1,0:T(8,128)(2,1)}, bf16[512,1024]{1,0:T(8,128)(2,1)}, u32[]{:S(2)}, u32[]{:S(2)}) collective-permute-start(bf16[512,1024]{1,0:T(8,128)(2,1)} %rest_0_.1), channel_id=1, source_target_pairs={{0,8},{4,20},{8,0},{12,28},{16,24},{20,4},{24,16},{28,12},{1,9},{5... | collective-permute-start | bytes 3145736 | tf_op jit(solution)/shard_map/ppermute | solution.py:326
  2.9 1.5 %tails.1 = (bf16[3,8,1024]{2,1,0:T(8,128)(2,1)S(1)}, bf16[3,1024,128]{2,1,0:T(8,128)(2,1)S(1)}, f32[3,7,1024]{2,1,0:T(8,128)S(1)}, f32[16,128]{1,0:T(8,128)S(1)}...) custom-call(bf16[3,1024,128]{2,1,0:T(8,128)(2,1)} %refs_0_.1, f32[3,7,1024]{2,1,0:T(8,128)} %refs_1_.1, ...), custom_call_target="tpu_custom_call" | custom-call | flops 100000000 | bytes 1000000 | tf_op jit(solution)/shard_map/tails/pallas_call | solution.py:55
  4.5 1.5 %collective-permute-start = (bf16[3,8,1024]{2,1,0:T(8,128)(2,1)S(1)}, bf16[3,8,1024]{2,1,0:T(8,128)(2,1)S(1)}, u32[]{:S(2)}, u32[]{:S(2)}) collective-permute-start(bf16[3,8,1024]{2,1,0:T(8,128)(2,1)S(1)} %get-tuple-element.30), channel_id=1, source_target_pairs={{0,4},{4,8},{8,12},{12,16},{16,20},{20,24},{24,28},{1,5},{5,9},{9,... | collective-permute-start | bytes 147464 | tf_op jit(solution)/shard_map/ppermute | solution.py:26
  6.0 3.3 %prepare.1 = (f32[3,8,1024]{2,1,0:T(8,128)S(1)}, bf16[128,1024]{1,0:T(8,128)(2,1)S(1)}, f32[128,1024]{1,0:T(8,128)S(1)}, bf16[2048,128]{1,0:T(8,128)(2,1)S(1)}, ...) custom-call(bf16[3,1024,128]{2,1,0:T(8,128)(2,1)S(1)} %get-tuple-element.31.streams_ref, ...), custom_call_target="tpu_custom_call" | custom-call | flops 1000000000 | bytes 10000000 | tf_op jit(solution)/shard_map/prepare/pallas_call | solution.py:55
  9.3 1.4 %states.1 = (bf16[8,16,1024]{2,1,0:T(8,128)(2,1)}, bf16[128,1024]{1,0:T(8,128)(2,1)S(1)}, f32[8,1024]{1,0:T(8,128)S(1)}) custom-call(bf16[3,8,1024]{2,1,0:T(8,128)(2,1)S(1)} %collective-permute-done.before_ref, f32[3,8,1024]{2,1,0:T(8,128)S(1)} %get-tuple-element.35.heads_ref, f32[3,7,1024]{2,1,0:T(8,128)S(1)} %get-tuple-element.32.taps_ref, ...), custom_call_target="tpu_custom_call" | custom-call | flops 100000000 | bytes 1000000 | tf_op jit(solution)/shard_map/states/pallas_call | solution.py:55
  10.7 4.8 %all-to-all-start = ((bf16[8,16,1024]{2,1,0:T(8,128)(2,1)}), bf16[8,16,1024]{2,1,0:T(8,128)(2,1)S(1)}, u32[]{:S(2)}, u32[]{:S(2)}) async-start(bf16[8,16,1024]{2,1,0:T(8,128)(2,1)} %get-tuple-element.38), calls=%async_computation | async-start | bytes 524288 | tf_op jit(solution)/shard_map/all_to_all | solution.py:381
  15.5 0.1 pad_add_fusion.1.at_ref
  15.6 0.1 pad_add_fusion.at_ref
  15.7 2.3 %inside.1.base_ref = f32[128,1024]{1,0:T(8,128)S(1)} custom-call(bf16[128,1024]{1,0:T(8,128)(2,1)S(1)} %get-tuple-element.43.gated_ref, f32[1,1024]{1,0:T(1,128)S(1)} %get-tuple-element.44.skip_ref, f32[128,128]{1,0:T(8,128)S(1)} %get-tuple-element.45.response_ref), custom_call_target="tpu_custom_call" | custom-call | flops 1000000000 | bytes 10000000 | tf_op jit(solution)/shard_map/inside/pallas_call | solution.py:55
  18.0 2.2 %collective-permute-start.5 = (bf16[512,1024]{1,0:T(8,128)(2,1)S(1)}, bf16[512,1024]{1,0:T(8,128)(2,1)}, u32[]{:S(2)}, u32[]{:S(2)}) collective-permute-start(bf16[512,1024]{1,0:T(8,128)(2,1)S(1)} %copy-done), channel_id=1, source_target_pairs={{0,16},{4,12},{8,24},{12,4},{16,0},{20,28},{24,8},{28,20},{1,17},{... | collective-permute-start | bytes 3145736 | tf_op jit(solution)/shard_map/ppermute | solution.py:326
  20.2 2.4 %all-to-all-done.ends_ref = bf16[8,16,1024]{2,1,0:T(8,128)(2,1)S(1)} async-done(((bf16[8,16,1024]{2,1,0:T(8,128)(2,1)}), bf16[8,16,1024]{2,1,0:T(8,128)(2,1)S(1)}, u32[]{:S(2)}, u32[]{:S(2)}) %all-to-all-start) | async-done | bytes 262176 | tf_op jit(solution)/shard_map/all_to_all | solution.py:381
  22.6 0.8 %finish.3 = bf16[128,512]{1,0:T(8,128)(2,1)S(1)} custom-call(s32[2]{0:T(128)S(1)} %pad_add_fusion.1.at_ref, bf16[8,16,1024]{2,1,0:T(8,128)(2,1)S(1)} %all-to-all-done.ends_ref, f32[16,1024]{1,0:T(8,128)S(1)} %get-tuple-element.39.step_ref, bf16[128,2048]{1,0:T(8,128)(2,1)S(1)} %get-tuple-element.40.lift_ref, ...), custom_call_target="tpu_custom_call" | custom-call | flops 3000000000 | bytes 30000000 | tf_op jit(solution)/shard_map/finish/pallas_call | solution.py:55
  23.4 0.1 collective-permute-start.1
  23.5 0.8 %finish.2 = bf16[128,512]{1,0:T(8,128)(2,1)S(1)} custom-call(s32[2]{0:T(128)S(1)} %pad_add_fusion.at_ref, bf16[8,16,1024]{2,1,0:T(8,128)(2,1)S(1)} %all-to-all-done.ends_ref, f32[16,1024]{1,0:T(8,128)S(1)} %get-tuple-element.39.step_ref, bf16[128,2048]{1,0:T(8,128)(2,1)S(1)} %get-tuple-element.40.lift_ref, ...), custom_call_target="tpu_custom_call" | custom-call | flops 3000000000 | bytes 30000000 | tf_op jit(solution)/shard_map/finish/pallas_call | solution.py:55
  24.3 0.5 collective-permute-done.1
  24.8 0.7 %collective-permute-start.3 = (bf16[256,512]{1,0:T(8,128)(2,1)S(1)}, bf16[256,512]{1,0:T(8,128)(2,1)S(1)}, u32[]{:S(2)}, u32[]{:S(2)}) collective-permute-start(bf16[256,512]{1,0:T(8,128)(2,1)S(1)} %pad_maximum_fusion.own_ref), channel_id=1, source_target_pairs={{1,2},{2,1},{5,6},{6,5},{9,10},{10,9},{13,14},{14,13},{17,18},{18,... | collective-permute-start | bytes 786440 | tf_op jit(solution)/shard_map/ppermute | solution.py:334
  25.5 0.1 stack.39.at_ref
  25.6 4.4 %collective-permute-start.2 = (bf16[256,512]{1,0:T(8,128)(2,1)S(1)}, bf16[256,512]{1,0:T(8,128)(2,1)S(1)}, u32[]{:S(2)}, u32[]{:S(2)}) collective-permute-start(bf16[256,512]{1,0:T(8,128)(2,1)S(1)} %pad_maximum_fusion.own_ref), channel_id=1, source_target_pairs={{0,1},{1,0},{2,3},{3,2},{4,5},{5,4},{6,7},{7,6},{8,9},{9,8},{10,11... | collective-permute-start | bytes 786440 | tf_op jit(solution)/shard_map/ppermute | solution.py:334
  30.0 3.2 %collective-permute-start.8 = (bf16[256,512]{1,0:T(8,128)(2,1)S(1)}, bf16[256,512]{1,0:T(8,128)(2,1)S(1)}, u32[]{:S(2)}, u32[]{:S(2)}) collective-permute-start(bf16[256,512]{1,0:T(8,128)(2,1)S(1)} %pad_maximum_fusion.own_ref), channel_id=1, source_target_pairs={{0,3},{3,0},{4,7},{7,4},{8,11},{11,8},{12,15},{15,12},{16,19},{19,... | collective-permute-start | bytes 786440 | tf_op jit(solution)/shard_map/ppermute | solution.py:334
  33.3 0.8 %collective-permute-start.9 = (bf16[512,1024]{1,0:T(8,128)(2,1)}, bf16[512,1024]{1,0:T(8,128)(2,1)S(1)}, u32[]{:S(2)}, u32[]{:S(2)}) collective-permute-start(bf16[512,1024]{1,0:T(8,128)(2,1)} %collective-permute-done.4.rest_1_), channel_id=1, source_target_pairs={{0,16},{4,12},{8,24},{12,4},{16,0},{20,28},{24,8},{28,20},{1,17},{... | collective-permute-start | bytes 3145736 | tf_op jit(solution)/shard_map/ppermute | solution.py:326
  34.1 1.3 %collective-permute-start.7 = (bf16[256,512]{1,0:T(8,128)(2,1)S(1)}, bf16[256,512]{1,0:T(8,128)(2,1)S(1)}, u32[]{:S(2)}, u32[]{:S(2)}) collective-permute-start(bf16[256,512]{1,0:T(8,128)(2,1)S(1)} %collective-permute-done.3.block_ref.middle_ref), channel_id=1, source_target_pairs={{1,0},{2,3},{5,4},{6,7},{9,8},{10,11},{13,12},{14,15},{17,16},{18,... | collective-permute-start | bytes 786440 | tf_op jit(solution)/shard_map/ppermute | solution.py:334
  35.4 1.3 %collective-permute-done.2.beside_ref = bf16[256,512]{1,0:T(8,128)(2,1)S(1)} collective-permute-done((bf16[256,512]{1,0:T(8,128)(2,1)S(1)}, bf16[256,512]{1,0:T(8,128)(2,1)S(1)}, u32[]{:S(2)}, u32[]{:S(2)}) %collective-permute-start.2) | collective-permute-done | bytes 262176 | tf_op jit(solution)/shard_map/ppermute | solution.py:334
  36.7 0.7 %collective-permute-start.6 = (bf16[256,512]{1,0:T(8,128)(2,1)S(1)}, bf16[256,512]{1,0:T(8,128)(2,1)S(1)}, u32[]{:S(2)}, u32[]{:S(2)}) collective-permute-start(bf16[256,512]{1,0:T(8,128)(2,1)S(1)} %collective-permute-done.2.beside_ref), channel_id=1, source_target_pairs={{1,2},{2,1},{5,6},{6,5},{9,10},{10,9},{13,14},{14,13},{17,18},{18,... | collective-permute-start | bytes 786440 | tf_op jit(solution)/shard_map/ppermute | solution.py:334
  37.4 5.8 %collective-permute-done.8.across_ref = bf16[256,512]{1,0:T(8,128)(2,1)S(1)} collective-permute-done((bf16[256,512]{1,0:T(8,128)(2,1)S(1)}, bf16[256,512]{1,0:T(8,128)(2,1)S(1)}, u32[]{:S(2)}, u32[]{:S(2)}) %collective-permute-start.8) | collective-permute-done | bytes 262176 | tf_op jit(solution)/shard_map/ppermute | solution.py:334
  43.2 2.9 %early.1 = (f32[256,1024]{1,0:T(8,128)S(1)}, bf16[512,1024]{1,0:T(8,128)(2,1)S(1)}, bf16[256,512]{1,0:T(8,128)(2,1)S(1)}) custom-call(s32[5]{0:T(128)S(1)} %stack.39.at_ref, bf16[256,512]{1,0:T(8,128)(2,1)S(1)} %pad_maximum_fusion.own_ref, bf16[256,512]{1,0:T(8,128)(2,1)S(1)} %collective-permute-done.2.beside_ref, ...), custom_call_target="tpu_custom_call" | custom-call | flops 10000000000 | bytes 100000000 | tf_op jit(solution)/shard_map/early/pallas_call | solution.py:55
  46.1 2.2 %collective-permute-done.9.weight_ref = bf16[512,1024]{1,0:T(8,128)(2,1)S(1)} collective-permute-done((bf16[512,1024]{1,0:T(8,128)(2,1)}, bf16[512,1024]{1,0:T(8,128)(2,1)S(1)}, u32[]{:S(2)}, u32[]{:S(2)}) %collective-permute-start.9) | collective-permute-done | bytes 1048608 | tf_op jit(solution)/shard_map/ppermute | solution.py:326
  48.3 1.0 %joined.1 = (f32[256,1024]{1,0:T(8,128)S(1)}, bf16[512,1024]{1,0:T(8,128)(2,1)S(1)}) custom-call(s32[5]{0:T(128)S(1)} %stack.39.at_ref, f32[256,1024]{1,0:T(8,128)S(1)} %get-tuple-element.49.total_ref, bf16[512,1024]{1,0:T(8,128)(2,1)S(1)} %get-tuple-element.50.rows_ref, bf16[256,512]{1,0:T(8,128)(2,1)S(1)} %get-tuple-element.51.block_ref, ...), custom_call_target="tpu_custom_call" | custom-call | tf_op jit(solution)/shard_map/joined/pallas_call | solution.py:55
  49.4 0.8 %late.3 = bf16[128,1024]{1,0:T(8,128)(2,1)S(1)} custom-call(s32[5]{0:T(128)S(1)} %stack.39.at_ref, bf16[256,512]{1,0:T(8,128)(2,1)S(1)} %collective-permute-done.6.inwards_ref, bf16[256,512]{1,0:T(8,128)(2,1)S(1)} %collective-permute-done.7.outwards_ref, f32[256,1024]{1,0:T(8,128)S(1)} %get-tuple-element.53.total_ref, ...), custom_call_target="tpu_custom_call" | custom-call | tf_op jit(solution)/shard_map/late/pallas_call | solution.py:55
  50.3 0.1 collective-permute-start.10
  50.3 0.8 %late.2 = f32[128,1024]{1,0:T(8,128)S(1)} custom-call(s32[5]{0:T(128)S(1)} %stack.39.at_ref, bf16[256,512]{1,0:T(8,128)(2,1)S(1)} %collective-permute-done.6.inwards_ref, bf16[256,512]{1,0:T(8,128)(2,1)S(1)} %collective-permute-done.7.outwards_ref, f32[256,1024]{1,0:T(8,128)S(1)} %get-tuple-element.53.total_ref, bf16[512,1024]{1,0:T(8,128)(2,1)S(1)} %get-tuple-element.54.rows_ref), custom_call_target="tpu_custom_call" | custom-call | tf_op jit(solution)/shard_map/late/pallas_call | solution.py:55
  51.2 0.7 %collective-permute-done.10 = bf16[128,1024]{1,0:T(8,128)(2,1)S(1)} collective-permute-done((bf16[128,1024]{1,0:T(8,128)(2,1)S(1)}, bf16[128,1024]{1,0:T(8,128)(2,1)S(1)}, u32[]{:S(2)}, u32[]{:S(2)}) %collective-permute-start.10) | collective-permute-done | bytes 262176 | tf_op jit(solution)/shard_map/ppermute | solution.py:326
  51.9 0.8 %add_convert_fusion = bf16[128,1024]{1,0:T(8,128)(2,1)} fusion(f32[128,1024]{1,0:T(8,128)S(1)} %late.2, bf16[128,1024]{1,0:T(8,128)(2,1)S(1)} %collective-permute-done.10), kind=kLoop, calls=%fused_computation | loop fusion | flops 393216 | bytes 1048576 | tf_op jit(solution)/shard_map/convert_element_type | solution.py:472
  (10 shorter events, 0.0 us)
Async XLA Ops:
  0.0 18.0 %collective-permute-start.4 = (bf16[512,1024]{1,0:T(8,128)(2,1)}, bf16[512,1024]{1,0:T(8,128)(2,1)}, u32[]{:S(2)}, u32[]{:S(2)}) collective-permute-start(bf16[512,1024]{1,0:T(8,128)(2,1)} %rest_0_.1), channel_id=1, source_target_pairs={{0,8},{4,20},{8,0},{12,28},{16,24},{20,4},{24,16},{28,12},{1,9},{5... | collective-permute-start | bytes 3145736 | tf_op jit(solution)/shard_map/ppermute | solution.py:326
  4.5 4.9 %collective-permute-start = (bf16[3,8,1024]{2,1,0:T(8,128)(2,1)S(1)}, bf16[3,8,1024]{2,1,0:T(8,128)(2,1)S(1)}, u32[]{:S(2)}, u32[]{:S(2)}) collective-permute-start(bf16[3,8,1024]{2,1,0:T(8,128)(2,1)S(1)} %get-tuple-element.30), channel_id=1, source_target_pairs={{0,4},{4,8},{8,12},{12,16},{16,20},{20,24},{24,28},{1,5},{5,9},{9,... | collective-permute-start | bytes 147464 | tf_op jit(solution)/shard_map/ppermute | solution.py:26
  10.7 11.9 %all-to-all-start = ((bf16[8,16,1024]{2,1,0:T(8,128)(2,1)}), bf16[8,16,1024]{2,1,0:T(8,128)(2,1)S(1)}, u32[]{:S(2)}, u32[]{:S(2)}) async-start(bf16[8,16,1024]{2,1,0:T(8,128)(2,1)} %get-tuple-element.38), calls=%async_computation | async-start | bytes 524288 | tf_op jit(solution)/shard_map/all_to_all | solution.py:381
  15.7 2.3 %copy-start = (bf16[512,1024]{1,0:T(8,128)(2,1)S(1)}, bf16[512,1024]{1,0:T(8,128)(2,1)}, u32[]{:S(2)}) copy-start(bf16[512,1024]{1,0:T(8,128)(2,1)} %rest_0_.1) | copy-start | bytes 3145732
  18.0 18.7 %collective-permute-start.5 = (bf16[512,1024]{1,0:T(8,128)(2,1)S(1)}, bf16[512,1024]{1,0:T(8,128)(2,1)}, u32[]{:S(2)}, u32[]{:S(2)}) collective-permute-start(bf16[512,1024]{1,0:T(8,128)(2,1)S(1)} %copy-done), channel_id=1, source_target_pairs={{0,16},{4,12},{8,24},{12,4},{16,0},{20,28},{24,8},{28,20},{1,17},{... | collective-permute-start | bytes 3145736 | tf_op jit(solution)/shard_map/ppermute | solution.py:326
  23.4 1.4 %collective-permute-start.1 = (bf16[128,512]{1,0:T(8,128)(2,1)S(1)}, bf16[128,512]{1,0:T(8,128)(2,1)S(1)}, u32[]{:S(2)}, u32[]{:S(2)}) collective-permute-start(bf16[128,512]{1,0:T(8,128)(2,1)S(1)} %finish.3), channel_id=1, source_target_pairs={{0,4},{4,0},{8,12},{12,8},{16,20},{20,16},{24,28},{28,24},{1,5},{5... | collective-permute-start | bytes 393224 | tf_op jit(solution)/shard_map/ppermute | solution.py:326
  24.8 9.3 %collective-permute-start.3 = (bf16[256,512]{1,0:T(8,128)(2,1)S(1)}, bf16[256,512]{1,0:T(8,128)(2,1)S(1)}, u32[]{:S(2)}, u32[]{:S(2)}) collective-permute-start(bf16[256,512]{1,0:T(8,128)(2,1)S(1)} %pad_maximum_fusion.own_ref), channel_id=1, source_target_pairs={{1,2},{2,1},{5,6},{6,5},{9,10},{10,9},{13,14},{14,13},{17,18},{18,... | collective-permute-start | bytes 786440 | tf_op jit(solution)/shard_map/ppermute | solution.py:334
  25.6 11.1 %collective-permute-start.2 = (bf16[256,512]{1,0:T(8,128)(2,1)S(1)}, bf16[256,512]{1,0:T(8,128)(2,1)S(1)}, u32[]{:S(2)}, u32[]{:S(2)}) collective-permute-start(bf16[256,512]{1,0:T(8,128)(2,1)S(1)} %pad_maximum_fusion.own_ref), channel_id=1, source_target_pairs={{0,1},{1,0},{2,3},{3,2},{4,5},{5,4},{6,7},{7,6},{8,9},{9,8},{10,11... | collective-permute-start | bytes 786440 | tf_op jit(solution)/shard_map/ppermute | solution.py:334
  30.0 13.2 %collective-permute-start.8 = (bf16[256,512]{1,0:T(8,128)(2,1)S(1)}, bf16[256,512]{1,0:T(8,128)(2,1)S(1)}, u32[]{:S(2)}, u32[]{:S(2)}) collective-permute-start(bf16[256,512]{1,0:T(8,128)(2,1)S(1)} %pad_maximum_fusion.own_ref), channel_id=1, source_target_pairs={{0,3},{3,0},{4,7},{7,4},{8,11},{11,8},{12,15},{15,12},{16,19},{19,... | collective-permute-start | bytes 786440 | tf_op jit(solution)/shard_map/ppermute | solution.py:334
  33.3 15.1 %collective-permute-start.9 = (bf16[512,1024]{1,0:T(8,128)(2,1)}, bf16[512,1024]{1,0:T(8,128)(2,1)S(1)}, u32[]{:S(2)}, u32[]{:S(2)}) collective-permute-start(bf16[512,1024]{1,0:T(8,128)(2,1)} %collective-permute-done.4.rest_1_), channel_id=1, source_target_pairs={{0,16},{4,12},{8,24},{12,4},{16,0},{20,28},{24,8},{28,20},{1,17},{... | collective-permute-start | bytes 3145736 | tf_op jit(solution)/shard_map/ppermute | solution.py:326
  34.1 15.3 %collective-permute-start.7 = (bf16[256,512]{1,0:T(8,128)(2,1)S(1)}, bf16[256,512]{1,0:T(8,128)(2,1)S(1)}, u32[]{:S(2)}, u32[]{:S(2)}) collective-permute-start(bf16[256,512]{1,0:T(8,128)(2,1)S(1)} %collective-permute-done.3.block_ref.middle_ref), channel_id=1, source_target_pairs={{1,0},{2,3},{5,4},{6,7},{9,8},{10,11},{13,12},{14,15},{17,16},{18,... | collective-permute-start | bytes 786440 | tf_op jit(solution)/shard_map/ppermute | solution.py:334
  36.7 12.7 %collective-permute-start.6 = (bf16[256,512]{1,0:T(8,128)(2,1)S(1)}, bf16[256,512]{1,0:T(8,128)(2,1)S(1)}, u32[]{:S(2)}, u32[]{:S(2)}) collective-permute-start(bf16[256,512]{1,0:T(8,128)(2,1)S(1)} %collective-permute-done.2.beside_ref), channel_id=1, source_target_pairs={{1,2},{2,1},{5,6},{6,5},{9,10},{10,9},{13,14},{14,13},{17,18},{18,... | collective-permute-start | bytes 786440 | tf_op jit(solution)/shard_map/ppermute | solution.py:334
  50.3 1.6 %collective-permute-start.10 = (bf16[128,1024]{1,0:T(8,128)(2,1)S(1)}, bf16[128,1024]{1,0:T(8,128)(2,1)S(1)}, u32[]{:S(2)}, u32[]{:S(2)}) collective-permute-start(bf16[128,1024]{1,0:T(8,128)(2,1)S(1)} %late.3), channel_id=1, source_target_pairs={{0,4},{4,0},{8,12},{12,8},{16,20},{20,16},{24,28},{28,24},{1,5},{5... | collective-permute-start | bytes 786440 | tf_op jit(solution)/shard_map/ppermute | solution.py:326

commit v22 on v19

--- a/solution.py
+++ b/solution.py
@@ -139,7 +139,7 @@
             impulse.append(amplitude * jnp.exp(-rate * time))
             lift.append(amplitude * jnp.exp(-rate * (time + 1.0)))
             wide = jnp.where(owner == g, rate[:, :TILE], wide)
-        step_ref[:, tile_of(index)] = jnp.exp(-wide * length)
+        step_ref[:, tile_of(index)] = -wide * length
         states = tile_of(index, in_tile * poles)
         decay_ref[states, :] = jnp.concatenate(decay, axis=0).astype(BF16)
         high, low = halves(jnp.concatenate(impulse, axis=0))
@@ -159,9 +159,11 @@
     unrolled(channels // TILE, filters)
 
 
-def states_kernel(before_ref, heads_ref, taps_ref, gated_ref, decay_ref, ends_ref, final_ref, first_ref, padded_ref):
+def states_kernel(
+    before_ref, heads_ref, taps_ref, gated_ref, decay_ref, ends_ref, sent_ref, final_ref, first_ref, padded_ref
+):
     length, channels = gated_ref.shape
-    poles = ends_ref.shape[1]
+    poles = ends_ref.shape[0]
     in_tile = decay_ref.shape[0] // poles * TILE // channels
     owner = iota((poles, TILE), 1) // (TILE // in_tile)
 
@@ -184,27 +186,25 @@
         ends = jnp.zeros((poles, TILE), F32)
         for g in range(in_tile):
             ends = jnp.where(owner == g, every[g * poles : (g + 1) * poles], ends)
-        ends = ends.astype(BF16)
-        for block in range(ends_ref.shape[0]):
-            ends_ref[block, :, chans] = ends
+        ends_ref[:, chans] = ends
+        sent_ref[:, chans] = ends.astype(BF16)
 
     unrolled(channels // TILE, begin)
     unrolled(channels // TILE, leave)
 
 
-def inside_kernel(gated_ref, skip_ref, response_ref, base_ref, signal_ref, sum_ref):
-    length, channels = gated_ref.shape
-    groups = response_ref.shape[0]
-    width = channels // groups
+def inside_kernel(begin, gated_ref, skip_ref, response_ref, base_ref, signal_ref, sum_ref):
+    length = gated_ref.shape[0]
+    width = gated_ref.shape[1] // response_ref.shape[0]
     in_tile = TILE // width
-    tiles = channels // TILE
+    tiles = base_ref.shape[1] // TILE
     strip = STRIP
     unit = identity(length)
     lane = iota((width, length), 1)
     causal = iota((strip, length), 1) >= iota((strip, length), 0)
 
     def signals(index):
-        gated = gated_ref[:, tile_of(index)]
+        gated = gated_ref[:, tile_of(begin + index)]
         for at in range(length // strip):
             piece = turned(gated[at * strip : (at + 1) * strip], unit).astype(BF16)
             signal_ref[at, tile_of(index), :] = piece
@@ -212,7 +212,7 @@
     def products(index):
         for pair in range(in_tile // 2):
             group = index * in_tile + 2 * pair
-            responses = response_ref[pl.ds(group, 2), :]
+            responses = response_ref[pl.ds(begin * in_tile + group, 2), :]
             blocks = []
             for g in range(2):
                 spread = jnp.broadcast_to(responses[g : g + 1], (strip, length))
@@ -233,8 +233,9 @@
 
     def back(index):
         chans = tile_of(index)
+        here = tile_of(begin + index)
         high, low = halves(sum_ref[chans, :])
-        direct = skip_ref[:, chans] * gated_ref[:, chans].astype(F32)
+        direct = skip_ref[:, here] * gated_ref[:, here].astype(F32)
         base_ref[:, chans] = turned(high, unit) + turned(low, unit) + direct
 
     unrolled(tiles, signals)
@@ -242,18 +243,31 @@
     unrolled(tiles, back)
 
 
-def finish_kernel(at_ref, ends_ref, step_ref, lift_ref, query_ref, first_ref, base_ref, mixed_ref, state_ref):
+def join_kernel(bit, me_ref, arrived_ref, ends_ref, entering_ref, wide_ref, joined_ref, sent_ref, later_ref):
+    me = me_ref[0]
+    high = (me >> bit) % 2 == 1
+    arrived = arrived_ref[...].astype(F32)
+    wide = wide_ref[...]
+    over = jnp.exp(wide * (1 << bit))
+    joined = jnp.where(high, over * arrived + ends_ref[...], over * ends_ref[...] + arrived)
+    joined_ref[...] = joined
+    sent_ref[...] = joined.astype(BF16)
+    before = (me % (1 << bit)).astype(F32)
+    later_ref[...] = entering_ref[...] + jnp.where(high, jnp.exp(wide * before) * arrived, 0.0)
+
+
+def finish_kernel(
+    bit, at_ref, arrived_ref, entering_ref, wide_ref, lift_ref, query_ref, first_ref, left_ref, right_ref, mixed_ref, state_ref
+):
     length, share = mixed_ref.shape
-    poles, channels = step_ref.shape
+    poles, channels = wide_ref.shape
     in_tile = lift_ref.shape[1] // poles * TILE // channels
     me, half = at_ref[0], at_ref[1]
     here = tile_of(half, share)
-    step = step_ref[:, here]
-
-    def earlier(block, state):
-        return jnp.where(block < me, step * state + ends_ref[block, :, here].astype(F32), state)
-
-    state_ref[...] = lax.fori_loop(0, ends_ref.shape[0] - 1, earlier, jnp.zeros((poles, share), F32))
+    high = (me >> bit) % 2 == 1
+    before = (me % (1 << bit)).astype(F32)
+    reached = jnp.exp(wide_ref[:, here] * before) * arrived_ref[:, here].astype(F32)
+    state_ref[...] = entering_ref[:, here] + jnp.where(high, reached, 0.0)
     owner = iota((poles, TILE), 1) // (TILE // in_tile)
 
     def tile(index):
@@ -263,7 +277,8 @@
         apart = jnp.concatenate([jnp.where(owner == g, entering, 0.0) for g in range(in_tile)], axis=0)
         carried = dot(lift_ref[:, tile_of(at, in_tile * poles)], apart.astype(BF16))
         query = jnp.concatenate([first_ref[:, chans], query_ref[:, chans].astype(F32)[ROWS:]], axis=0)
-        mixed_ref[:, tile_of(index)] = (query * (base_ref[:, chans] + carried)).astype(BF16)
+        base = jnp.where(half == 0, left_ref[:, tile_of(index)], right_ref[:, tile_of(index)])
+        mixed_ref[:, tile_of(index)] = (query * (base + carried)).astype(BF16)
 
     unrolled(share // TILE, tile)
 
@@ -346,7 +361,7 @@
     if square:
         near = swap(out_weight, 2, 4)
     tiles = channels // TILE
-    heads, query, gated, decay, step, response, lift = call(
+    heads, query, gated, decay, wide, response, lift = call(
         prepare_kernel,
         [
             ((3, ROWS, channels), F32),
@@ -362,38 +377,56 @@
         scratch=[pltpu.VMEM((3 * tiles, ROWS + length, TILE), F32)],
         flops=10**9,
     )
-    ends, gated, first = call(
+    ends, sent, gated, first = call(
         states_kernel,
-        [((blocks, poles, channels), BF16), ((length, channels), BF16), ((ROWS, channels), F32)],
+        [((poles, channels), F32), ((poles, channels), BF16), ((length, channels), BF16), ((ROWS, channels), F32)],
         "states",
         before, heads, conv_weight, gated, decay,
         scratch=[pltpu.VMEM((3 * tiles, 2 * ROWS, TILE), F32)],
     )
-    all_ends = lax.all_to_all(ends, "ctx", split_axis=0, concat_axis=0, tiled=True)
-    (base,) = call(
-        inside_kernel,
-        [((length, channels), F32)],
-        "inside",
-        gated, skip, response,
-        scratch=[
-            pltpu.VMEM((length // STRIP, channels, STRIP), BF16),
-            pltpu.VMEM((channels, length), F32),
-        ],
-        flops=10**9,
-    )
+    me = lax.axis_index("ctx").astype(jnp.int32)
+
+    def within(half):
+        return call(
+            functools.partial(inside_kernel, half * tiles // 2),
+            [((length, channels // 2), F32)],
+            "inside",
+            gated, skip, response,
+            scratch=[
+                pltpu.VMEM((length // STRIP, channels // 2, STRIP), BF16),
+                pltpu.VMEM((channels // 2, length), F32),
+            ],
+            flops=10**9,
+        )[0]
+
+    bases, entering = [], jnp.zeros((poles, channels), F32)
+    steps = (blocks - 1).bit_length()
+    for bit in range(steps):
+        arrived = swap(sent, 1 << bit)
+        if bit < steps - 1:
+            ends, sent, entering = call(
+                functools.partial(join_kernel, bit),
+                [((poles, channels), F32), ((poles, channels), BF16), ((poles, channels), F32)],
+                "join",
+                me[None], arrived, ends, entering, wide,
+                specs=[pl.BlockSpec(memory_space=pltpu.SMEM)] + whole(4),
+            )
+        if bit == steps - 2:
+            bases.append(within(0))
+            sent = after(sent, bases[0])
+    bases.append(within(1))
     if square:
-        other_near = swap(after(out_weight, (base, near)), 4, 2)
-    me = lax.axis_index("ctx").astype(jnp.int32)
+        other_near = swap(after(out_weight, (bases[-1], near)), 4, 2)
     core = me % CORES
     smem = [pl.BlockSpec(memory_space=pltpu.SMEM)]
 
     def finished(half):
         return call(
-            finish_kernel,
+            functools.partial(finish_kernel, steps - 1),
             [((length, share), BF16)],
             "finish",
-            jnp.stack([me, half]), all_ends, step, lift, query, first, base,
-            specs=smem + whole(6),
+            jnp.stack([me, half]), arrived, entering, wide, lift, query, first, *bases,
+            specs=smem + whole(8),
             flops=3 * 10**9,
             scratch=[pltpu.VMEM((poles, share), F32)],
         )[0]

time: 49.5 us -> 49.4 us (level)
  waiting for transfers between devices: 12.8 us -> 13.8 us
  Pallas kernels: 14.8 us -> 14 us
    ppermute x5 -> x8, waiting for transfers between devices: 2.44 us -> 7.33 us  [swap(): return lax.ppermute(value, 'ctx', pairs)]
    all_to_all x1 -> x0, starting transfers between devices: 4.82 us -> none  [local(): lax.all_to_all(ends, 'ctx', split_axis=0, concat_axis=0, tiled=True)]
    ppermute x5 -> x8, starting transfers between devices: 6.02 us -> 9.9 us  [swap(): return lax.ppermute(value, 'ctx', pairs)]
    all_to_all x1 -> x0, waiting for transfers between devices: 2.46 us -> none  [local(): lax.all_to_all(ends, 'ctx', split_axis=0, concat_axis=0, tiled=True)]
    ppermute x3, waiting for transfers between devices: 7.89 us -> 6.42 us  [trade(): lax.ppermute(value, 'tp', [(source, source ^ bits) for source in range(co...]
    ppermute x3, starting transfers between devices: 8.16 us -> 8.97 us  [trade(): lax.ppermute(value, 'tp', [(source, source ^ bits) for source in range(co...]
    pallas_call x10 -> x13, Pallas kernels: 14.8 us -> 14 us  [call(): pl.pallas_call(kernel, out_shape=tuple((jax.ShapeDtypeStruct(*out) for ou...]
  transfers between devices with their start and end apart: 10 -> 12, of which waited for: 7 -> 7; matrix products, arithmetic and copies ran while one was open for 1% -> 1% of each run, Pallas kernels for 29% -> 28%
where the time goes in v22:
time: 49.4 us; the launch traced here: 49.3 us
  starting transfers between devices  20.4 us (41%)
  Pallas kernels  14 us (28%)
  waiting for transfers between devices  13.8 us (28%)
  other arithmetic  0.93 us (2%)
    pallas_call x13, Pallas kernels, call(): pl.pallas_call(kernel, out_shape=tuple((jax.ShapeDtypeStruct(*out) for ou...  14 us
    ppermute x8, starting transfers between devices, swap(): return lax.ppermute(value, 'ctx', pairs)  9.9 us
    ppermute x3, starting transfers between devices, trade(): lax.ppermute(value, 'tp', [(source, source ^ bits) for source in range(co...  8.97 us
    ppermute x8, waiting for transfers between devices, swap(): return lax.ppermute(value, 'ctx', pairs)  7.33 us
    ppermute x3, waiting for transfers between devices, trade(): lax.ppermute(value, 'tp', [(source, source ^ bits) for source in range(co...  6.42 us
    ppermute x1, starting transfers between devices, from_behind(): lax.ppermute(value, axis, [(source, source + steps) for source in range(l...  1.49 us
  transfers between devices with their start and end apart: 12, of which 7 were waited for; matrix products, arithmetic and copies ran while one was open for 1% of the time, Pallas kernels for 28%

profile of v22, /device:TPU:0, one launch (start us, length us, event | category | flops | bytes accessed | tf_op | source)
XLA Modules:
  0.0 49.3 jit_solution(17570950008715487967)
XLA Ops:
  0.0 2.9 %collective-permute-start.6 = (bf16[512,1024]{1,0:T(8,128)(2,1)}, bf16[512,1024]{1,0:T(8,128)(2,1)}, u32[]{:S(2)}, u32[]{:S(2)}) collective-permute-start(bf16[512,1024]{1,0:T(8,128)(2,1)} %rest_0_.1), channel_id=1, source_target_pairs={{0,8},{4,20},{8,0},{12,28},{16,24},{20,4},{24,16},{28,12},{1,9},{5... | collective-permute-start | bytes 3145736 | tf_op jit(solution)/shard_map/ppermute | solution.py:331
  2.9 1.5 %tails.1 = (bf16[3,8,1024]{2,1,0:T(8,128)(2,1)S(1)}, bf16[3,1024,128]{2,1,0:T(8,128)(2,1)S(1)}, f32[3,7,1024]{2,1,0:T(8,128)S(1)}, f32[16,128]{1,0:T(8,128)S(1)}...) custom-call(bf16[3,1024,128]{2,1,0:T(8,128)(2,1)} %refs_0_.1, f32[3,7,1024]{2,1,0:T(8,128)} %refs_1_.1, ...), custom_call_target="tpu_custom_call" | custom-call | flops 100000000 | bytes 1000000 | tf_op jit(solution)/shard_map/tails/pallas_call | solution.py:55
  4.5 1.5 %collective-permute-start = (bf16[3,8,1024]{2,1,0:T(8,128)(2,1)S(1)}, bf16[3,8,1024]{2,1,0:T(8,128)(2,1)S(1)}, u32[]{:S(2)}, u32[]{:S(2)}) collective-permute-start(bf16[3,8,1024]{2,1,0:T(8,128)(2,1)S(1)} %get-tuple-element.36), channel_id=1, source_target_pairs={{0,4},{4,8},{8,12},{12,16},{16,20},{20,24},{24,28},{1,5},{5,9},{9,... | collective-permute-start | bytes 147464 | tf_op jit(solution)/shard_map/ppermute | solution.py:26
  6.0 0.1 pad_add_fusion.1.at_ref
  6.0 3.3 %prepare.1 = (f32[3,8,1024]{2,1,0:T(8,128)S(1)}, bf16[128,1024]{1,0:T(8,128)(2,1)S(1)}, f32[128,1024]{1,0:T(8,128)S(1)}, bf16[2048,128]{1,0:T(8,128)(2,1)S(1)}, ...) custom-call(bf16[3,1024,128]{2,1,0:T(8,128)(2,1)S(1)} %get-tuple-element.37.streams_ref, ...), custom_call_target="tpu_custom_call" | custom-call | flops 1000000000 | bytes 10000000 | tf_op jit(solution)/shard_map/prepare/pallas_call | solution.py:55
  9.4 0.6 %states.1 = (f32[16,1024]{1,0:T(8,128)S(1)}, bf16[16,1024]{1,0:T(8,128)(2,1)S(1)}, bf16[128,1024]{1,0:T(8,128)(2,1)S(1)}, f32[8,1024]{1,0:T(8,128)S(1)}) custom-call(bf16[3,8,1024]{2,1,0:T(8,128)(2,1)S(1)} %collective-permute-done.before_ref, f32[3,8,1024]{2,1,0:T(8,128)S(1)} %get-tuple-element.41.heads_ref, f32[3,7,1024]{2,1,0:T(8,128)S(1)} %get-tuple-element.38.taps_ref, ...), custom_call_target="tpu_custom_call" | custom-call | flops 100000000 | bytes 1000000 | tf_op jit(solution)/shard_map/states/pallas_call | solution.py:55
  10.0 0.6 %collective-permute-start.1 = (bf16[16,1024]{1,0:T(8,128)(2,1)S(1)}, bf16[16,1024]{1,0:T(8,128)(2,1)S(1)}, u32[]{:S(2)}, u32[]{:S(2)}) collective-permute-start(bf16[16,1024]{1,0:T(8,128)(2,1)S(1)} %get-tuple-element.44), channel_id=1, source_target_pairs={{0,4},{4,0},{8,12},{12,8},{16,20},{20,16},{24,28},{28,24},{1,5},{5... | collective-permute-start | bytes 98312 | tf_op jit(solution)/shard_map/ppermute | solution.py:331
  10.6 0.8 %inside.2.left_ref = f32[128,512]{1,0:T(8,128)S(1)} custom-call(bf16[128,1024]{1,0:T(8,128)(2,1)S(1)} %get-tuple-element.51.gated_ref, f32[1,1024]{1,0:T(1,128)S(1)} %get-tuple-element.52.skip_ref, f32[128,128]{1,0:T(8,128)S(1)} %get-tuple-element.53.response_ref), custom_call_target="tpu_custom_call" | custom-call | flops 1000000000 | bytes 10000000 | tf_op jit(solution)/shard_map/inside/pallas_call | solution.py:55
  11.6 3.0 %collective-permute-start.2 = (bf16[16,1024]{1,0:T(8,128)(2,1)S(1)}, bf16[16,1024]{1,0:T(8,128)(2,1)S(1)}, u32[]{:S(2)}, u32[]{:S(2)}) collective-permute-start(bf16[16,1024]{1,0:T(8,128)(2,1)S(1)} %get-tuple-element.47), channel_id=1, source_target_pairs={{0,8},{4,12},{8,0},{12,4},{16,24},{20,28},{24,16},{28,20},{1,9},{5... | collective-permute-start | bytes 98312 | tf_op jit(solution)/shard_map/ppermute | solution.py:331
  14.6 0.8 %inside.3.right_ref = f32[128,512]{1,0:T(8,128)S(1)} custom-call(bf16[128,1024]{1,0:T(8,128)(2,1)S(1)} %get-tuple-element.51.gated_ref, f32[1,1024]{1,0:T(1,128)S(1)} %get-tuple-element.52.skip_ref, f32[128,128]{1,0:T(8,128)S(1)} %get-tuple-element.53.response_ref), custom_call_target="tpu_custom_call" | custom-call | flops 1000000000 | bytes 10000000 | tf_op jit(solution)/shard_map/inside/pallas_call | solution.py:55
  15.5 1.7 %collective-permute-done.2.arrived_ref = bf16[16,1024]{1,0:T(8,128)(2,1)S(1)} collective-permute-done((bf16[16,1024]{1,0:T(8,128)(2,1)S(1)}, bf16[16,1024]{1,0:T(8,128)(2,1)S(1)}, u32[]{:S(2)}, u32[]{:S(2)}) %collective-permute-start.2) | collective-permute-done | bytes 32800 | tf_op jit(solution)/shard_map/ppermute | solution.py:331
  17.2 0.7 %join.3 = (f32[16,1024]{1,0:T(8,128)}, bf16[16,1024]{1,0:T(8,128)(2,1)S(1)}, f32[16,1024]{1,0:T(8,128)S(1)}) custom-call(s32[1]{0:T(128)} %bitcast.me_ref, bf16[16,1024]{1,0:T(8,128)(2,1)S(1)} %collective-permute-done.2.arrived_ref, f32[16,1024]{1,0:T(8,128)S(1)} %get-tuple-element.48.ends_ref, f32[16,1024]{1,0:T(8,128)S(1)} %get-tuple-element.49.entering_ref, ...), custom_call_target="tpu_custom_call" | custom-call | flops 100000000 | bytes 1000000 | tf_op jit(solution)/shard_map/join/pallas_call | solution.py:55
  17.8 1.7 %collective-permute-start.3 = (bf16[16,1024]{1,0:T(8,128)(2,1)S(1)}, bf16[16,1024]{1,0:T(8,128)(2,1)S(1)}, u32[]{:S(2)}, u32[]{:S(2)}) collective-permute-start(bf16[16,1024]{1,0:T(8,128)(2,1)S(1)} %get-tuple-element.54), channel_id=1, source_target_pairs={{0,16},{4,20},{8,24},{12,28},{16,0},{20,4},{24,8},{28,12},{1,17},{... | collective-permute-start | bytes 98312 | tf_op jit(solution)/shard_map/ppermute | solution.py:331
  19.5 0.4 collective-permute-start.7
  19.8 0.1 pad_add_fusion.at_ref
  19.9 1.8 %collective-permute-done.3.arrived_ref = bf16[16,1024]{1,0:T(8,128)(2,1)S(1)} collective-permute-done((bf16[16,1024]{1,0:T(8,128)(2,1)S(1)}, bf16[16,1024]{1,0:T(8,128)(2,1)S(1)}, u32[]{:S(2)}, u32[]{:S(2)}) %collective-permute-start.3) | collective-permute-done | bytes 32800 | tf_op jit(solution)/shard_map/ppermute | solution.py:331
  21.7 0.8 %finish.3 = bf16[128,512]{1,0:T(8,128)(2,1)S(1)} custom-call(s32[2]{0:T(128)S(1)} %pad_add_fusion.1.at_ref, bf16[16,1024]{1,0:T(8,128)(2,1)S(1)} %collective-permute-done.3.arrived_ref, f32[16,1024]{1,0:T(8,128)S(1)} %get-tuple-element.55.entering_ref, f32[16,1024]{1,0:T(8,128)S(1)} %get-tuple-element.46.wide_ref, ...), custom_call_target="tpu_custom_call" | custom-call | flops 3000000000 | bytes 30000000 | tf_op jit(solution)/shard_map/finish/pallas_call | solution.py:55
  22.6 0.8 %finish.2 = bf16[128,512]{1,0:T(8,128)(2,1)S(1)} custom-call(s32[2]{0:T(128)S(1)} %pad_add_fusion.at_ref, bf16[16,1024]{1,0:T(8,128)(2,1)S(1)} %collective-permute-done.3.arrived_ref, f32[16,1024]{1,0:T(8,128)S(1)} %get-tuple-element.55.entering_ref, f32[16,1024]{1,0:T(8,128)S(1)} %get-tuple-element.46.wide_ref, ...), custom_call_target="tpu_custom_call" | custom-call | flops 3000000000 | bytes 30000000 | tf_op jit(solution)/shard_map/finish/pallas_call | solution.py:55
  23.4 0.5 %collective-permute-done.4 = bf16[128,512]{1,0:T(8,128)(2,1)S(1)} collective-permute-done((bf16[128,512]{1,0:T(8,128)(2,1)S(1)}, bf16[128,512]{1,0:T(8,128)(2,1)S(1)}, u32[]{:S(2)}, u32[]{:S(2)}) %collective-permute-start.4) | collective-permute-done | bytes 131104 | tf_op jit(solution)/shard_map/ppermute | solution.py:331
  24.0 4.2 %collective-permute-start.5 = (bf16[256,512]{1,0:T(8,128)(2,1)S(1)}, bf16[256,512]{1,0:T(8,128)(2,1)S(1)}, u32[]{:S(2)}, u32[]{:S(2)}) collective-permute-start(bf16[256,512]{1,0:T(8,128)(2,1)S(1)} %pad_maximum_fusion.own_ref), channel_id=1, source_target_pairs={{0,3},{1,2},{2,1},{3,0},{4,7},{5,6},{6,5},{7,4},{8,11},{9,10},{10,... | collective-permute-start | bytes 786440 | tf_op jit(solution)/shard_map/ppermute | solution.py:340
  28.2 1.1 %collective-permute-start.10 = (bf16[512,1024]{1,0:T(8,128)(2,1)}, bf16[512,1024]{1,0:T(8,128)(2,1)S(1)}, u32[]{:S(2)}, u32[]{:S(2)}) collective-permute-start(bf16[512,1024]{1,0:T(8,128)(2,1)} %collective-permute-done.6.rest_1_), channel_id=1, source_target_pairs={{0,16},{4,12},{8,24},{12,4},{16,0},{20,28},{24,8},{28,20},{1,17},{... | collective-permute-start | bytes 3145736 | tf_op jit(solution)/shard_map/ppermute | solution.py:331
  29.3 0.1 stack.44.at_ref
  29.4 5.9 %collective-permute-done.5.across_ref = bf16[256,512]{1,0:T(8,128)(2,1)S(1)} collective-permute-done((bf16[256,512]{1,0:T(8,128)(2,1)S(1)}, bf16[256,512]{1,0:T(8,128)(2,1)S(1)}, u32[]{:S(2)}, u32[]{:S(2)}) %collective-permute-start.5) | collective-permute-done | bytes 262176 | tf_op jit(solution)/shard_map/ppermute | solution.py:340
  35.3 4.8 %collective-permute-start.8 = (bf16[256,512]{1,0:T(8,128)(2,1)S(1)}, bf16[256,512]{1,0:T(8,128)(2,1)S(1)}, u32[]{:S(2)}, u32[]{:S(2)}) collective-permute-start(bf16[256,512]{1,0:T(8,128)(2,1)S(1)} %collective-permute-done.5.across_ref), channel_id=1, source_target_pairs={{0,1},{1,0},{2,3},{3,2},{4,5},{5,4},{6,7},{7,6},{8,9},{9,8},{10,11... | collective-permute-start | bytes 786440 | tf_op jit(solution)/shard_map/ppermute | solution.py:340
  40.1 0.5 collective-permute-done.9.beside_ref
  40.6 2.9 %early.1 = (f32[256,1024]{1,0:T(8,128)S(1)}, bf16[512,1024]{1,0:T(8,128)(2,1)S(1)}, bf16[256,512]{1,0:T(8,128)(2,1)S(1)}) custom-call(s32[5]{0:T(128)S(1)} %stack.44.at_ref, bf16[256,512]{1,0:T(8,128)(2,1)S(1)} %pad_maximum_fusion.own_ref, bf16[256,512]{1,0:T(8,128)(2,1)S(1)} %collective-permute-done.9.beside_ref, ...), custom_call_target="tpu_custom_call" | custom-call | flops 10000000000 | bytes 100000000 | tf_op jit(solution)/shard_map/early/pallas_call | solution.py:55
  43.5 2.0 %collective-permute-done.10.weight_ref = bf16[512,1024]{1,0:T(8,128)(2,1)S(1)} collective-permute-done((bf16[512,1024]{1,0:T(8,128)(2,1)}, bf16[512,1024]{1,0:T(8,128)(2,1)S(1)}, u32[]{:S(2)}, u32[]{:S(2)}) %collective-permute-start.10) | collective-permute-done | bytes 1048608 | tf_op jit(solution)/shard_map/ppermute | solution.py:331
  45.5 1.1 %joined.1 = (f32[256,1024]{1,0:T(8,128)S(1)}, bf16[512,1024]{1,0:T(8,128)(2,1)S(1)}) custom-call(s32[5]{0:T(128)S(1)} %stack.44.at_ref, f32[256,1024]{1,0:T(8,128)S(1)} %get-tuple-element.61.total_ref, bf16[512,1024]{1,0:T(8,128)(2,1)S(1)} %get-tuple-element.62.rows_ref, bf16[256,512]{1,0:T(8,128)(2,1)S(1)} %get-tuple-element.63.block_ref, ...), custom_call_target="tpu_custom_call" | custom-call | tf_op jit(solution)/shard_map/joined/pallas_call | solution.py:55
  46.6 0.3 late.3
  47.0 0.3 late.2
  47.3 1.2 %collective-permute-done.11 = bf16[128,1024]{1,0:T(8,128)(2,1)S(1)} collective-permute-done((bf16[128,1024]{1,0:T(8,128)(2,1)S(1)}, bf16[128,1024]{1,0:T(8,128)(2,1)S(1)}, u32[]{:S(2)}, u32[]{:S(2)}) %collective-permute-start.11) | collective-permute-done | bytes 262176 | tf_op jit(solution)/shard_map/ppermute | solution.py:331
  48.5 0.8 %add_convert_fusion = bf16[128,1024]{1,0:T(8,128)(2,1)} fusion(f32[128,1024]{1,0:T(8,128)S(1)} %late.2, bf16[128,1024]{1,0:T(8,128)(2,1)S(1)} %collective-permute-done.11), kind=kLoop, calls=%fused_computation | loop fusion | flops 393216 | bytes 1048576 | tf_op jit(solution)/shard_map/convert_element_type | solution.py:491
  (13 shorter events, 0.2 us)
Async XLA Ops:
  0.0 19.5 %collective-permute-start.6 = (bf16[512,1024]{1,0:T(8,128)(2,1)}, bf16[512,1024]{1,0:T(8,128)(2,1)}, u32[]{:S(2)}, u32[]{:S(2)}) collective-permute-start(bf16[512,1024]{1,0:T(8,128)(2,1)} %rest_0_.1), channel_id=1, source_target_pairs={{0,8},{4,20},{8,0},{12,28},{16,24},{20,4},{24,16},{28,12},{1,9},{5... | collective-permute-start | bytes 3145736 | tf_op jit(solution)/shard_map/ppermute | solution.py:331
  4.5 4.9 %collective-permute-start = (bf16[3,8,1024]{2,1,0:T(8,128)(2,1)S(1)}, bf16[3,8,1024]{2,1,0:T(8,128)(2,1)S(1)}, u32[]{:S(2)}, u32[]{:S(2)}) collective-permute-start(bf16[3,8,1024]{2,1,0:T(8,128)(2,1)S(1)} %get-tuple-element.36), channel_id=1, source_target_pairs={{0,4},{4,8},{8,12},{12,16},{16,20},{20,24},{24,28},{1,5},{5,9},{9,... | collective-permute-start | bytes 147464 | tf_op jit(solution)/shard_map/ppermute | solution.py:26
  10.0 1.5 %collective-permute-start.1 = (bf16[16,1024]{1,0:T(8,128)(2,1)S(1)}, bf16[16,1024]{1,0:T(8,128)(2,1)S(1)}, u32[]{:S(2)}, u32[]{:S(2)}) collective-permute-start(bf16[16,1024]{1,0:T(8,128)(2,1)S(1)} %get-tuple-element.44), channel_id=1, source_target_pairs={{0,4},{4,0},{8,12},{12,8},{16,20},{20,16},{24,28},{28,24},{1,5},{5... | collective-permute-start | bytes 98312 | tf_op jit(solution)/shard_map/ppermute | solution.py:331
  11.6 7.9 %copy-start = (bf16[512,1024]{1,0:T(8,128)(2,1)S(1)}, bf16[512,1024]{1,0:T(8,128)(2,1)}, u32[]{:S(2)}) copy-start(bf16[512,1024]{1,0:T(8,128)(2,1)} %rest_0_.1) | copy-start | bytes 3145732
  11.6 5.6 %collective-permute-start.2 = (bf16[16,1024]{1,0:T(8,128)(2,1)S(1)}, bf16[16,1024]{1,0:T(8,128)(2,1)S(1)}, u32[]{:S(2)}, u32[]{:S(2)}) collective-permute-start(bf16[16,1024]{1,0:T(8,128)(2,1)S(1)} %get-tuple-element.47), channel_id=1, source_target_pairs={{0,8},{4,12},{8,0},{12,4},{16,24},{20,28},{24,16},{28,20},{1,9},{5... | collective-permute-start | bytes 98312 | tf_op jit(solution)/shard_map/ppermute | solution.py:331
  17.8 3.9 %collective-permute-start.3 = (bf16[16,1024]{1,0:T(8,128)(2,1)S(1)}, bf16[16,1024]{1,0:T(8,128)(2,1)S(1)}, u32[]{:S(2)}, u32[]{:S(2)}) collective-permute-start(bf16[16,1024]{1,0:T(8,128)(2,1)S(1)} %get-tuple-element.54), channel_id=1, source_target_pairs={{0,16},{4,20},{8,24},{12,28},{16,0},{20,4},{24,8},{28,12},{1,17},{... | collective-permute-start | bytes 98312 | tf_op jit(solution)/shard_map/ppermute | solution.py:331
  19.5 15.8 %collective-permute-start.7 = (bf16[512,1024]{1,0:T(8,128)(2,1)S(1)}, bf16[512,1024]{1,0:T(8,128)(2,1)}, u32[]{:S(2)}, u32[]{:S(2)}) collective-permute-start(bf16[512,1024]{1,0:T(8,128)(2,1)S(1)} %copy-done), channel_id=1, source_target_pairs={{0,16},{4,12},{8,24},{12,4},{16,0},{20,28},{24,8},{28,20},{1,17},{... | collective-permute-start | bytes 3145736 | tf_op jit(solution)/shard_map/ppermute | solution.py:331
  22.5 1.4 %collective-permute-start.4 = (bf16[128,512]{1,0:T(8,128)(2,1)S(1)}, bf16[128,512]{1,0:T(8,128)(2,1)S(1)}, u32[]{:S(2)}, u32[]{:S(2)}) collective-permute-start(bf16[128,512]{1,0:T(8,128)(2,1)S(1)} %finish.3), channel_id=1, source_target_pairs={{0,4},{4,0},{8,12},{12,8},{16,20},{20,16},{24,28},{28,24},{1,5},{5... | collective-permute-start | bytes 393224 | tf_op jit(solution)/shard_map/ppermute | solution.py:331
  24.0 11.4 %collective-permute-start.5 = (bf16[256,512]{1,0:T(8,128)(2,1)S(1)}, bf16[256,512]{1,0:T(8,128)(2,1)S(1)}, u32[]{:S(2)}, u32[]{:S(2)}) collective-permute-start(bf16[256,512]{1,0:T(8,128)(2,1)S(1)} %pad_maximum_fusion.own_ref), channel_id=1, source_target_pairs={{0,3},{1,2},{2,1},{3,0},{4,7},{5,6},{6,5},{7,4},{8,11},{9,10},{10,... | collective-permute-start | bytes 786440 | tf_op jit(solution)/shard_map/ppermute | solution.py:340
  28.2 12.4 %collective-permute-start.9 = (bf16[256,512]{1,0:T(8,128)(2,1)S(1)}, bf16[256,512]{1,0:T(8,128)(2,1)S(1)}, u32[]{:S(2)}, u32[]{:S(2)}) collective-permute-start(bf16[256,512]{1,0:T(8,128)(2,1)S(1)} %pad_maximum_fusion.own_ref), channel_id=1, source_target_pairs={{0,1},{1,0},{2,3},{3,2},{4,5},{5,4},{6,7},{7,6},{8,9},{9,8},{10,11... | collective-permute-start | bytes 786440 | tf_op jit(solution)/shard_map/ppermute | solution.py:340
  28.2 17.4 %collective-permute-start.10 = (bf16[512,1024]{1,0:T(8,128)(2,1)}, bf16[512,1024]{1,0:T(8,128)(2,1)S(1)}, u32[]{:S(2)}, u32[]{:S(2)}) collective-permute-start(bf16[512,1024]{1,0:T(8,128)(2,1)} %collective-permute-done.6.rest_1_), channel_id=1, source_target_pairs={{0,16},{4,12},{8,24},{12,4},{16,0},{20,28},{24,8},{28,20},{1,17},{... | collective-permute-start | bytes 3145736 | tf_op jit(solution)/shard_map/ppermute | solution.py:331
  35.3 11.3 %collective-permute-start.8 = (bf16[256,512]{1,0:T(8,128)(2,1)S(1)}, bf16[256,512]{1,0:T(8,128)(2,1)S(1)}, u32[]{:S(2)}, u32[]{:S(2)}) collective-permute-start(bf16[256,512]{1,0:T(8,128)(2,1)S(1)} %collective-permute-done.5.across_ref), channel_id=1, source_target_pairs={{0,1},{1,0},{2,3},{3,2},{4,5},{5,4},{6,7},{7,6},{8,9},{9,8},{10,11... | collective-permute-start | bytes 786440 | tf_op jit(solution)/shard_map/ppermute | solution.py:340
  46.9 1.6 %collective-permute-start.11 = (bf16[128,1024]{1,0:T(8,128)(2,1)S(1)}, bf16[128,1024]{1,0:T(8,128)(2,1)S(1)}, u32[]{:S(2)}, u32[]{:S(2)}) collective-permute-start(bf16[128,1024]{1,0:T(8,128)(2,1)S(1)} %late.3), channel_id=1, source_target_pairs={{0,4},{4,0},{8,12},{12,8},{16,20},{20,16},{24,28},{28,24},{1,5},{5... | collective-permute-start | bytes 786440 | tf_op jit(solution)/shard_map/ppermute | solution.py:331

commit v23 on v22

--- a/solution.py
+++ b/solution.py
@@ -51,13 +51,14 @@
     return [pl.BlockSpec(memory_space=pltpu.VMEM)] * count
 
 
-def call(kernel, outs, name, *operands, specs=None, scratch=(), flops=10**8):
+def call(kernel, outs, name, *operands, specs=None, scratch=(), flops=10**8, aliases=None, out_specs=None):
     return pl.pallas_call(
         kernel,
         out_shape=tuple(jax.ShapeDtypeStruct(*out) for out in outs),
         in_specs=whole(len(operands)) if specs is None else specs,
-        out_specs=tuple(whole(len(outs))),
+        out_specs=tuple(out_specs or whole(len(outs))),
         scratch_shapes=scratch,
+        input_output_aliases=aliases or {},
         compiler_params=pltpu.CompilerParams(vmem_limit_bytes=VMEM_LIMIT),
         cost_estimate=pl.CostEstimate(flops=flops, bytes_accessed=flops // 100, transcendentals=0),
         name=name,
@@ -243,15 +244,16 @@
     unrolled(tiles, back)
 
 
-def join_kernel(bit, me_ref, arrived_ref, ends_ref, entering_ref, wide_ref, joined_ref, sent_ref, later_ref):
+def join_kernel(bit, me_ref, arrived_ref, ends_ref, entering_ref, wide_ref, sent_ref, later_ref, *joined_ref):
     me = me_ref[0]
     high = (me >> bit) % 2 == 1
     arrived = arrived_ref[...].astype(F32)
     wide = wide_ref[...]
     over = jnp.exp(wide * (1 << bit))
     joined = jnp.where(high, over * arrived + ends_ref[...], over * ends_ref[...] + arrived)
-    joined_ref[...] = joined
     sent_ref[...] = joined.astype(BF16)
+    for ref in joined_ref:
+        ref[...] = joined
     before = (me % (1 << bit)).astype(F32)
     later_ref[...] = entering_ref[...] + jnp.where(high, jnp.exp(wide * before) * arrived, 0.0)
 
@@ -309,15 +311,13 @@
         pl.when(at_ref[1 + at] == last)(fetch.wait)
 
 
-def joined_kernel(at_ref, total_ref, rows_ref, block_ref, weight_ref, out_ref, last_ref):
+def joined_kernel(at_ref, total_ref, rows_ref, block_ref, weight_ref, out_ref, last_ref, sem):
+    del rows_ref
+    latest = at_ref[4] == at_ref[0] ^ 2
+    keep = pltpu.make_async_copy(weight_ref, last_ref, sem)
+    pl.when(latest)(keep.start)
     out_ref[...] = total_ref[...] + dot(block_ref[...], weight_ref[...])
-
-    def keep(rows):
-        last_ref[...] = rows[...]
-
-    latest = at_ref[4] == at_ref[0] ^ 2
-    pl.when(latest)(lambda: keep(weight_ref))
-    pl.when(jnp.logical_not(latest))(lambda: keep(rows_ref))
+    pl.when(latest)(keep.wait)
 
 
 def late_kernel(first, beyond_ref, total_ref, rows_ref, out_ref):
@@ -399,16 +399,17 @@
             flops=10**9,
         )[0]
 
-    bases, entering = [], jnp.zeros((poles, channels), F32)
+    bases, ends, entering = [], [ends], jnp.zeros((poles, channels), F32)
     steps = (blocks - 1).bit_length()
     for bit in range(steps):
         arrived = swap(sent, 1 << bit)
         if bit < steps - 1:
-            ends, sent, entering = call(
+            outs = [((poles, channels), BF16), ((poles, channels), F32), ((poles, channels), F32)]
+            sent, entering, *ends = call(
                 functools.partial(join_kernel, bit),
-                [((poles, channels), F32), ((poles, channels), BF16), ((poles, channels), F32)],
+                outs[: 2 if bit == steps - 2 else 3],
                 "join",
-                me[None], arrived, ends, entering, wide,
+                me[None], arrived, ends[0], entering, wide,
                 specs=[pl.BlockSpec(memory_space=pltpu.SMEM)] + whole(4),
             )
         if bit == steps - 2:
@@ -469,13 +470,17 @@
         ],
         flops=10**10,
     )
+    anywhere = [pl.BlockSpec(memory_space=pl.ANY)]
     total, last_rows = call(
         joined_kernel,
         [((CORES * length, features), F32), ((share, features), BF16)],
         "joined",
         at, total, last_rows, last_block, latest,
-        specs=smem + whole(4),
+        specs=smem + whole(1) + anywhere + whole(2),
+        out_specs=whole(1) + anywhere,
+        scratch=[pltpu.SemaphoreType.DMA],
         flops=0,
+        aliases={2: 1},
     )
     sides = []
     for side, kind in ((1, BF16), (0, F32)):

time: 49.4 us -> 48.9 us (0.990)
  Pallas kernels: 14 us -> 13.3 us
    pallas_call x13, Pallas kernels: 14 us -> 13.3 us  [call(): pl.pallas_call(kernel, out_shape=tuple((jax.ShapeDtypeStruct(*out) for ou...]
  transfers between devices with their start and end apart: 12 -> 12, of which waited for: 7 -> 7; matrix products, arithmetic and copies ran while one was open for 1% -> 1% of each run, Pallas kernels for 28% -> 27%
where the time goes in v23:
time: 48.9 us; the launch traced here: 48.7 us
  starting transfers between devices  20.4 us (42%)
  waiting for transfers between devices  13.7 us (28%)
  Pallas kernels  13.3 us (27%)
  other arithmetic  0.93 us (2%)
    pallas_call x13, Pallas kernels, call(): pl.pallas_call(kernel, out_shape=tuple((jax.ShapeDtypeStruct(*out) for ou...  13.3 us
    ppermute x8, starting transfers between devices, swap(): return lax.ppermute(value, 'ctx', pairs)  9.97 us
    ppermute x3, starting transfers between devices, trade(): lax.ppermute(value, 'tp', [(source, source ^ bits) for source in range(co...  8.97 us
    ppermute x8, waiting for transfers between devices, swap(): return lax.ppermute(value, 'ctx', pairs)  7.33 us
    ppermute x3, waiting for transfers between devices, trade(): lax.ppermute(value, 'tp', [(source, source ^ bits) for source in range(co...  6.42 us
    ppermute x1, starting transfers between devices, from_behind(): lax.ppermute(value, axis, [(source, source + steps) for source in range(l...  1.49 us
  transfers between devices with their start and end apart: 12, of which 7 were waited for; matrix products, arithmetic and copies ran while one was open for 1% of the time, Pallas kernels for 27%

profile of v23, /device:TPU:0, one launch (start us, length us, event | category | flops | bytes accessed | tf_op | source)
XLA Modules:
  0.0 48.7 jit_solution(17530093161216477573)
XLA Ops:
  0.0 2.9 %collective-permute-start.6 = (bf16[512,1024]{1,0:T(8,128)(2,1)}, bf16[512,1024]{1,0:T(8,128)(2,1)}, u32[]{:S(2)}, u32[]{:S(2)}) collective-permute-start(bf16[512,1024]{1,0:T(8,128)(2,1)} %rest_0_.1), channel_id=1, source_target_pairs={{0,8},{4,20},{8,0},{12,28},{16,24},{20,4},{24,16},{28,12},{1,9},{5... | collective-permute-start | bytes 3145736 | tf_op jit(solution)/shard_map/ppermute | solution.py:331
  2.9 1.5 %tails.1 = (bf16[3,8,1024]{2,1,0:T(8,128)(2,1)S(1)}, bf16[3,1024,128]{2,1,0:T(8,128)(2,1)S(1)}, f32[3,7,1024]{2,1,0:T(8,128)S(1)}, f32[16,128]{1,0:T(8,128)S(1)}...) custom-call(bf16[3,1024,128]{2,1,0:T(8,128)(2,1)} %refs_0_.1, f32[3,7,1024]{2,1,0:T(8,128)} %refs_1_.1, ...), custom_call_target="tpu_custom_call" | custom-call | flops 100000000 | bytes 1000000 | tf_op jit(solution)/shard_map/tails/pallas_call | solution.py:55
  4.5 1.5 %collective-permute-start = (bf16[3,8,1024]{2,1,0:T(8,128)(2,1)S(1)}, bf16[3,8,1024]{2,1,0:T(8,128)(2,1)S(1)}, u32[]{:S(2)}, u32[]{:S(2)}) collective-permute-start(bf16[3,8,1024]{2,1,0:T(8,128)(2,1)S(1)} %get-tuple-element.36), channel_id=1, source_target_pairs={{0,4},{4,8},{8,12},{12,16},{16,20},{20,24},{24,28},{1,5},{5,9},{9,... | collective-permute-start | bytes 147464 | tf_op jit(solution)/shard_map/ppermute | solution.py:26
  6.0 0.1 pad_add_fusion.1.at_ref
  6.0 3.3 %prepare.1 = (f32[3,8,1024]{2,1,0:T(8,128)S(1)}, bf16[128,1024]{1,0:T(8,128)(2,1)S(1)}, f32[128,1024]{1,0:T(8,128)S(1)}, bf16[2048,128]{1,0:T(8,128)(2,1)S(1)}, ...) custom-call(bf16[3,1024,128]{2,1,0:T(8,128)(2,1)S(1)} %get-tuple-element.37.streams_ref, ...), custom_call_target="tpu_custom_call" | custom-call | flops 1000000000 | bytes 10000000 | tf_op jit(solution)/shard_map/prepare/pallas_call | solution.py:55
  9.4 0.6 %states.1 = (f32[16,1024]{1,0:T(8,128)S(1)}, bf16[16,1024]{1,0:T(8,128)(2,1)S(1)}, bf16[128,1024]{1,0:T(8,128)(2,1)S(1)}, f32[8,1024]{1,0:T(8,128)S(1)}) custom-call(bf16[3,8,1024]{2,1,0:T(8,128)(2,1)S(1)} %collective-permute-done.before_ref, f32[3,8,1024]{2,1,0:T(8,128)S(1)} %get-tuple-element.41.heads_ref, f32[3,7,1024]{2,1,0:T(8,128)S(1)} %get-tuple-element.38.taps_ref, ...), custom_call_target="tpu_custom_call" | custom-call | flops 100000000 | bytes 1000000 | tf_op jit(solution)/shard_map/states/pallas_call | solution.py:55
  10.0 0.6 %collective-permute-start.1 = (bf16[16,1024]{1,0:T(8,128)(2,1)S(1)}, bf16[16,1024]{1,0:T(8,128)(2,1)S(1)}, u32[]{:S(2)}, u32[]{:S(2)}) collective-permute-start(bf16[16,1024]{1,0:T(8,128)(2,1)S(1)} %get-tuple-element.44), channel_id=1, source_target_pairs={{0,4},{4,0},{8,12},{12,8},{16,20},{20,16},{24,28},{28,24},{1,5},{5... | collective-permute-start | bytes 98312 | tf_op jit(solution)/shard_map/ppermute | solution.py:331
  10.6 0.8 %inside.2.left_ref = f32[128,512]{1,0:T(8,128)S(1)} custom-call(bf16[128,1024]{1,0:T(8,128)(2,1)S(1)} %get-tuple-element.51.gated_ref, f32[1,1024]{1,0:T(1,128)S(1)} %get-tuple-element.52.skip_ref, f32[128,128]{1,0:T(8,128)S(1)} %get-tuple-element.53.response_ref), custom_call_target="tpu_custom_call" | custom-call | flops 1000000000 | bytes 10000000 | tf_op jit(solution)/shard_map/inside/pallas_call | solution.py:55
  11.6 3.0 %collective-permute-start.2 = (bf16[16,1024]{1,0:T(8,128)(2,1)S(1)}, bf16[16,1024]{1,0:T(8,128)(2,1)S(1)}, u32[]{:S(2)}, u32[]{:S(2)}) collective-permute-start(bf16[16,1024]{1,0:T(8,128)(2,1)S(1)} %get-tuple-element.47), channel_id=1, source_target_pairs={{0,8},{4,12},{8,0},{12,4},{16,24},{20,28},{24,16},{28,20},{1,9},{5... | collective-permute-start | bytes 98312 | tf_op jit(solution)/shard_map/ppermute | solution.py:331
  14.6 0.8 %inside.3.right_ref = f32[128,512]{1,0:T(8,128)S(1)} custom-call(bf16[128,1024]{1,0:T(8,128)(2,1)S(1)} %get-tuple-element.51.gated_ref, f32[1,1024]{1,0:T(1,128)S(1)} %get-tuple-element.52.skip_ref, f32[128,128]{1,0:T(8,128)S(1)} %get-tuple-element.53.response_ref), custom_call_target="tpu_custom_call" | custom-call | flops 1000000000 | bytes 10000000 | tf_op jit(solution)/shard_map/inside/pallas_call | solution.py:55
  15.5 1.7 %collective-permute-done.2.arrived_ref = bf16[16,1024]{1,0:T(8,128)(2,1)S(1)} collective-permute-done((bf16[16,1024]{1,0:T(8,128)(2,1)S(1)}, bf16[16,1024]{1,0:T(8,128)(2,1)S(1)}, u32[]{:S(2)}, u32[]{:S(2)}) %collective-permute-start.2) | collective-permute-done | bytes 32800 | tf_op jit(solution)/shard_map/ppermute | solution.py:331
  17.2 1.7 %collective-permute-start.3 = (bf16[16,1024]{1,0:T(8,128)(2,1)S(1)}, bf16[16,1024]{1,0:T(8,128)(2,1)S(1)}, u32[]{:S(2)}, u32[]{:S(2)}) collective-permute-start(bf16[16,1024]{1,0:T(8,128)(2,1)S(1)} %get-tuple-element.54), channel_id=1, source_target_pairs={{0,16},{4,20},{8,24},{12,28},{16,0},{20,4},{24,8},{28,12},{1,17},{... | collective-permute-start | bytes 98312 | tf_op jit(solution)/shard_map/ppermute | solution.py:331
  18.9 0.4 collective-permute-start.7
  19.3 0.1 pad_add_fusion.at_ref
  19.4 1.8 %collective-permute-done.3.arrived_ref = bf16[16,1024]{1,0:T(8,128)(2,1)S(1)} collective-permute-done((bf16[16,1024]{1,0:T(8,128)(2,1)S(1)}, bf16[16,1024]{1,0:T(8,128)(2,1)S(1)}, u32[]{:S(2)}, u32[]{:S(2)}) %collective-permute-start.3) | collective-permute-done | bytes 32800 | tf_op jit(solution)/shard_map/ppermute | solution.py:331
  21.2 0.8 %finish.3 = bf16[128,512]{1,0:T(8,128)(2,1)S(1)} custom-call(s32[2]{0:T(128)S(1)} %pad_add_fusion.1.at_ref, bf16[16,1024]{1,0:T(8,128)(2,1)S(1)} %collective-permute-done.3.arrived_ref, f32[16,1024]{1,0:T(8,128)S(1)} %get-tuple-element.55.entering_ref, f32[16,1024]{1,0:T(8,128)S(1)} %get-tuple-element.46.wide_ref, ...), custom_call_target="tpu_custom_call" | custom-call | flops 3000000000 | bytes 30000000 | tf_op jit(solution)/shard_map/finish/pallas_call | solution.py:55
  22.0 0.1 collective-permute-start.4
  22.1 0.8 %finish.2 = bf16[128,512]{1,0:T(8,128)(2,1)S(1)} custom-call(s32[2]{0:T(128)S(1)} %pad_add_fusion.at_ref, bf16[16,1024]{1,0:T(8,128)(2,1)S(1)} %collective-permute-done.3.arrived_ref, f32[16,1024]{1,0:T(8,128)S(1)} %get-tuple-element.55.entering_ref, f32[16,1024]{1,0:T(8,128)S(1)} %get-tuple-element.46.wide_ref, ...), custom_call_target="tpu_custom_call" | custom-call | flops 3000000000 | bytes 30000000 | tf_op jit(solution)/shard_map/finish/pallas_call | solution.py:55
  22.8 0.5 %collective-permute-done.4 = bf16[128,512]{1,0:T(8,128)(2,1)S(1)} collective-permute-done((bf16[128,512]{1,0:T(8,128)(2,1)S(1)}, bf16[128,512]{1,0:T(8,128)(2,1)S(1)}, u32[]{:S(2)}, u32[]{:S(2)}) %collective-permute-start.4) | collective-permute-done | bytes 131104 | tf_op jit(solution)/shard_map/ppermute | solution.py:331
  23.4 4.2 %collective-permute-start.5 = (bf16[256,512]{1,0:T(8,128)(2,1)S(1)}, bf16[256,512]{1,0:T(8,128)(2,1)S(1)}, u32[]{:S(2)}, u32[]{:S(2)}) collective-permute-start(bf16[256,512]{1,0:T(8,128)(2,1)S(1)} %pad_maximum_fusion.own_ref), channel_id=1, source_target_pairs={{0,3},{1,2},{2,1},{3,0},{4,7},{5,6},{6,5},{7,4},{8,11},{9,10},{10,... | collective-permute-start | bytes 786440 | tf_op jit(solution)/shard_map/ppermute | solution.py:340
  27.6 1.1 %collective-permute-start.10 = (bf16[512,1024]{1,0:T(8,128)(2,1)}, bf16[512,1024]{1,0:T(8,128)(2,1)S(1)}, u32[]{:S(2)}, u32[]{:S(2)}) collective-permute-start(bf16[512,1024]{1,0:T(8,128)(2,1)} %collective-permute-done.6.rest_1_), channel_id=1, source_target_pairs={{0,16},{4,12},{8,24},{12,4},{16,0},{20,28},{24,8},{28,20},{1,17},{... | collective-permute-start | bytes 3145736 | tf_op jit(solution)/shard_map/ppermute | solution.py:331
  28.8 0.1 stack.44.at_ref
  28.8 5.9 %collective-permute-done.5.across_ref = bf16[256,512]{1,0:T(8,128)(2,1)S(1)} collective-permute-done((bf16[256,512]{1,0:T(8,128)(2,1)S(1)}, bf16[256,512]{1,0:T(8,128)(2,1)S(1)}, u32[]{:S(2)}, u32[]{:S(2)}) %collective-permute-start.5) | collective-permute-done | bytes 262176 | tf_op jit(solution)/shard_map/ppermute | solution.py:340
  34.8 4.8 %collective-permute-start.8 = (bf16[256,512]{1,0:T(8,128)(2,1)S(1)}, bf16[256,512]{1,0:T(8,128)(2,1)S(1)}, u32[]{:S(2)}, u32[]{:S(2)}) collective-permute-start(bf16[256,512]{1,0:T(8,128)(2,1)S(1)} %collective-permute-done.5.across_ref), channel_id=1, source_target_pairs={{0,1},{1,0},{2,3},{3,2},{4,5},{5,4},{6,7},{7,6},{8,9},{9,8},{10,11... | collective-permute-start | bytes 786440 | tf_op jit(solution)/shard_map/ppermute | solution.py:340
  39.6 0.5 collective-permute-done.9.beside_ref
  40.0 2.9 %early.1 = (f32[256,1024]{1,0:T(8,128)S(1)}, bf16[512,1024]{1,0:T(8,128)(2,1)S(1)}, bf16[256,512]{1,0:T(8,128)(2,1)S(1)}) custom-call(s32[5]{0:T(128)S(1)} %stack.44.at_ref, bf16[256,512]{1,0:T(8,128)(2,1)S(1)} %pad_maximum_fusion.own_ref, bf16[256,512]{1,0:T(8,128)(2,1)S(1)} %collective-permute-done.9.beside_ref, ...), custom_call_target="tpu_custom_call" | custom-call | flops 10000000000 | bytes 100000000 | tf_op jit(solution)/shard_map/early/pallas_call | solution.py:55
  42.9 2.0 %collective-permute-done.10.weight_ref = bf16[512,1024]{1,0:T(8,128)(2,1)S(1)} collective-permute-done((bf16[512,1024]{1,0:T(8,128)(2,1)}, bf16[512,1024]{1,0:T(8,128)(2,1)S(1)}, u32[]{:S(2)}, u32[]{:S(2)}) %collective-permute-start.10) | collective-permute-done | bytes 1048608 | tf_op jit(solution)/shard_map/ppermute | solution.py:331
  45.0 1.0 %joined.1 = (f32[256,1024]{1,0:T(8,128)S(1)}, bf16[512,1024]{1,0:T(8,128)(2,1)S(1)}) custom-call(s32[5]{0:T(128)S(1)} %stack.44.at_ref, f32[256,1024]{1,0:T(8,128)S(1)} %get-tuple-element.61.total_ref, bf16[512,1024]{1,0:T(8,128)(2,1)S(1)} %get-tuple-element.62.rows_ref, ...), custom_call_target="tpu_custom_call", output_to_operand_aliasing={{1}: (2, {})} | custom-call | tf_op jit(solution)/shard_map/joined/pallas_call | solution.py:55
  46.0 0.3 late.3
  46.4 0.3 late.2
  46.7 1.2 %collective-permute-done.11 = bf16[128,1024]{1,0:T(8,128)(2,1)S(1)} collective-permute-done((bf16[128,1024]{1,0:T(8,128)(2,1)S(1)}, bf16[128,1024]{1,0:T(8,128)(2,1)S(1)}, u32[]{:S(2)}, u32[]{:S(2)}) %collective-permute-start.11) | collective-permute-done | bytes 262176 | tf_op jit(solution)/shard_map/ppermute | solution.py:331
  47.9 0.8 %add_convert_fusion = bf16[128,1024]{1,0:T(8,128)(2,1)} fusion(f32[128,1024]{1,0:T(8,128)S(1)} %late.2, bf16[128,1024]{1,0:T(8,128)(2,1)S(1)} %collective-permute-done.11), kind=kLoop, calls=%fused_computation | loop fusion | flops 393216 | bytes 1048576 | tf_op jit(solution)/shard_map/convert_element_type | solution.py:496
  (13 shorter events, 0.2 us)
Async XLA Ops:
  0.0 18.9 %collective-permute-start.6 = (bf16[512,1024]{1,0:T(8,128)(2,1)}, bf16[512,1024]{1,0:T(8,128)(2,1)}, u32[]{:S(2)}, u32[]{:S(2)}) collective-permute-start(bf16[512,1024]{1,0:T(8,128)(2,1)} %rest_0_.1), channel_id=1, source_target_pairs={{0,8},{4,20},{8,0},{12,28},{16,24},{20,4},{24,16},{28,12},{1,9},{5... | collective-permute-start | bytes 3145736 | tf_op jit(solution)/shard_map/ppermute | solution.py:331
  4.5 4.9 %collective-permute-start = (bf16[3,8,1024]{2,1,0:T(8,128)(2,1)S(1)}, bf16[3,8,1024]{2,1,0:T(8,128)(2,1)S(1)}, u32[]{:S(2)}, u32[]{:S(2)}) collective-permute-start(bf16[3,8,1024]{2,1,0:T(8,128)(2,1)S(1)} %get-tuple-element.36), channel_id=1, source_target_pairs={{0,4},{4,8},{8,12},{12,16},{16,20},{20,24},{24,28},{1,5},{5,9},{9,... | collective-permute-start | bytes 147464 | tf_op jit(solution)/shard_map/ppermute | solution.py:26
  10.0 1.5 %collective-permute-start.1 = (bf16[16,1024]{1,0:T(8,128)(2,1)S(1)}, bf16[16,1024]{1,0:T(8,128)(2,1)S(1)}, u32[]{:S(2)}, u32[]{:S(2)}) collective-permute-start(bf16[16,1024]{1,0:T(8,128)(2,1)S(1)} %get-tuple-element.44), channel_id=1, source_target_pairs={{0,4},{4,0},{8,12},{12,8},{16,20},{20,16},{24,28},{28,24},{1,5},{5... | collective-permute-start | bytes 98312 | tf_op jit(solution)/shard_map/ppermute | solution.py:331
  11.6 7.4 %copy-start = (bf16[512,1024]{1,0:T(8,128)(2,1)S(1)}, bf16[512,1024]{1,0:T(8,128)(2,1)}, u32[]{:S(2)}) copy-start(bf16[512,1024]{1,0:T(8,128)(2,1)} %rest_0_.1) | copy-start | bytes 3145732
  11.6 5.6 %collective-permute-start.2 = (bf16[16,1024]{1,0:T(8,128)(2,1)S(1)}, bf16[16,1024]{1,0:T(8,128)(2,1)S(1)}, u32[]{:S(2)}, u32[]{:S(2)}) collective-permute-start(bf16[16,1024]{1,0:T(8,128)(2,1)S(1)} %get-tuple-element.47), channel_id=1, source_target_pairs={{0,8},{4,12},{8,0},{12,4},{16,24},{20,28},{24,16},{28,20},{1,9},{5... | collective-permute-start | bytes 98312 | tf_op jit(solution)/shard_map/ppermute | solution.py:331
  17.2 4.0 %collective-permute-start.3 = (bf16[16,1024]{1,0:T(8,128)(2,1)S(1)}, bf16[16,1024]{1,0:T(8,128)(2,1)S(1)}, u32[]{:S(2)}, u32[]{:S(2)}) collective-permute-start(bf16[16,1024]{1,0:T(8,128)(2,1)S(1)} %get-tuple-element.54), channel_id=1, source_target_pairs={{0,16},{4,20},{8,24},{12,28},{16,0},{20,4},{24,8},{28,12},{1,17},{... | collective-permute-start | bytes 98312 | tf_op jit(solution)/shard_map/ppermute | solution.py:331
  18.9 15.8 %collective-permute-start.7 = (bf16[512,1024]{1,0:T(8,128)(2,1)S(1)}, bf16[512,1024]{1,0:T(8,128)(2,1)}, u32[]{:S(2)}, u32[]{:S(2)}) collective-permute-start(bf16[512,1024]{1,0:T(8,128)(2,1)S(1)} %copy-done), channel_id=1, source_target_pairs={{0,16},{4,12},{8,24},{12,4},{16,0},{20,28},{24,8},{28,20},{1,17},{... | collective-permute-start | bytes 3145736 | tf_op jit(solution)/shard_map/ppermute | solution.py:331
  22.0 1.4 %collective-permute-start.4 = (bf16[128,512]{1,0:T(8,128)(2,1)S(1)}, bf16[128,512]{1,0:T(8,128)(2,1)S(1)}, u32[]{:S(2)}, u32[]{:S(2)}) collective-permute-start(bf16[128,512]{1,0:T(8,128)(2,1)S(1)} %finish.3), channel_id=1, source_target_pairs={{0,4},{4,0},{8,12},{12,8},{16,20},{20,16},{24,28},{28,24},{1,5},{5... | collective-permute-start | bytes 393224 | tf_op jit(solution)/shard_map/ppermute | solution.py:331
  23.4 11.4 %collective-permute-start.5 = (bf16[256,512]{1,0:T(8,128)(2,1)S(1)}, bf16[256,512]{1,0:T(8,128)(2,1)S(1)}, u32[]{:S(2)}, u32[]{:S(2)}) collective-permute-start(bf16[256,512]{1,0:T(8,128)(2,1)S(1)} %pad_maximum_fusion.own_ref), channel_id=1, source_target_pairs={{0,3},{1,2},{2,1},{3,0},{4,7},{5,6},{6,5},{7,4},{8,11},{9,10},{10,... | collective-permute-start | bytes 786440 | tf_op jit(solution)/shard_map/ppermute | solution.py:340
  27.6 12.4 %collective-permute-start.9 = (bf16[256,512]{1,0:T(8,128)(2,1)S(1)}, bf16[256,512]{1,0:T(8,128)(2,1)S(1)}, u32[]{:S(2)}, u32[]{:S(2)}) collective-permute-start(bf16[256,512]{1,0:T(8,128)(2,1)S(1)} %pad_maximum_fusion.own_ref), channel_id=1, source_target_pairs={{0,1},{1,0},{2,3},{3,2},{4,5},{5,4},{6,7},{7,6},{8,9},{9,8},{10,11... | collective-permute-start | bytes 786440 | tf_op jit(solution)/shard_map/ppermute | solution.py:340
  27.6 17.4 %collective-permute-start.10 = (bf16[512,1024]{1,0:T(8,128)(2,1)}, bf16[512,1024]{1,0:T(8,128)(2,1)S(1)}, u32[]{:S(2)}, u32[]{:S(2)}) collective-permute-start(bf16[512,1024]{1,0:T(8,128)(2,1)} %collective-permute-done.6.rest_1_), channel_id=1, source_target_pairs={{0,16},{4,12},{8,24},{12,4},{16,0},{20,28},{24,8},{28,20},{1,17},{... | collective-permute-start | bytes 3145736 | tf_op jit(solution)/shard_map/ppermute | solution.py:331
  34.8 11.2 %collective-permute-start.8 = (bf16[256,512]{1,0:T(8,128)(2,1)S(1)}, bf16[256,512]{1,0:T(8,128)(2,1)S(1)}, u32[]{:S(2)}, u32[]{:S(2)}) collective-permute-start(bf16[256,512]{1,0:T(8,128)(2,1)S(1)} %collective-permute-done.5.across_ref), channel_id=1, source_target_pairs={{0,1},{1,0},{2,3},{3,2},{4,5},{5,4},{6,7},{7,6},{8,9},{9,8},{10,11... | collective-permute-start | bytes 786440 | tf_op jit(solution)/shard_map/ppermute | solution.py:340
  46.3 1.6 %collective-permute-start.11 = (bf16[128,1024]{1,0:T(8,128)(2,1)S(1)}, bf16[128,1024]{1,0:T(8,128)(2,1)S(1)}, u32[]{:S(2)}, u32[]{:S(2)}) collective-permute-start(bf16[128,1024]{1,0:T(8,128)(2,1)S(1)} %late.3), channel_id=1, source_target_pairs={{0,4},{4,0},{8,12},{12,8},{16,20},{20,16},{24,28},{28,24},{1,5},{5... | collective-permute-start | bytes 786440 | tf_op jit(solution)/shard_map/ppermute | solution.py:331

commit v24 on v23

--- a/solution.py
+++ b/solution.py
@@ -311,13 +311,16 @@
         pl.when(at_ref[1 + at] == last)(fetch.wait)
 
 
-def joined_kernel(at_ref, total_ref, rows_ref, block_ref, weight_ref, out_ref, last_ref, sem):
+def joined_kernel(total_ref, block_ref, weight_ref, out_ref):
+    out_ref[...] = total_ref[...] + dot(block_ref[...], weight_ref[...])
+
+
+def keep_kernel(at_ref, rows_ref, weight_ref, last_ref, sem):
     del rows_ref
     latest = at_ref[4] == at_ref[0] ^ 2
-    keep = pltpu.make_async_copy(weight_ref, last_ref, sem)
-    pl.when(latest)(keep.start)
-    out_ref[...] = total_ref[...] + dot(block_ref[...], weight_ref[...])
-    pl.when(latest)(keep.wait)
+    copy = pltpu.make_async_copy(weight_ref, last_ref, sem)
+    pl.when(latest)(copy.start)
+    pl.when(latest)(copy.wait)
 
 
 def late_kernel(first, beyond_ref, total_ref, rows_ref, out_ref):
@@ -470,17 +473,20 @@
         ],
         flops=10**10,
     )
+    (total,) = call(
+        joined_kernel, [((CORES * length, features), F32)], "joined", total, last_block, latest, flops=0
+    )
     anywhere = [pl.BlockSpec(memory_space=pl.ANY)]
-    total, last_rows = call(
-        joined_kernel,
-        [((CORES * length, features), F32), ((share, features), BF16)],
-        "joined",
-        at, total, last_rows, last_block, latest,
-        specs=smem + whole(1) + anywhere + whole(2),
-        out_specs=whole(1) + anywhere,
+    (last_rows,) = call(
+        keep_kernel,
+        [((share, features), BF16)],
+        "keep",
+        at, last_rows, latest,
+        specs=smem + anywhere * 2,
+        out_specs=anywhere,
         scratch=[pltpu.SemaphoreType.DMA],
         flops=0,
-        aliases={2: 1},
+        aliases={1: 0},
     )
     sides = []
     for side, kind in ((1, BF16), (0, F32)):

time: 48.9 us -> 48.9 us (level)
    pallas_call x13 -> x14, Pallas kernels: 13.3 us -> 13.3 us  [call(): pl.pallas_call(kernel, out_shape=tuple((jax.ShapeDtypeStruct(*out) for ou...]
where the time goes in v24:
time: 48.9 us; the launch traced here: 48.7 us
  starting transfers between devices  20.4 us (42%)
  waiting for transfers between devices  13.8 us (28%)
  Pallas kernels  13.3 us (27%)
  other arithmetic  0.93 us (2%)
    pallas_call x14, Pallas kernels, call(): pl.pallas_call(kernel, out_shape=tuple((jax.ShapeDtypeStruct(*out) for ou...  13.3 us
    ppermute x8, starting transfers between devices, swap(): return lax.ppermute(value, 'ctx', pairs)  9.97 us
    ppermute x3, starting transfers between devices, trade(): lax.ppermute(value, 'tp', [(source, source ^ bits) for source in range(co...  8.97 us
    ppermute x8, waiting for transfers between devices, swap(): return lax.ppermute(value, 'ctx', pairs)  7.33 us
    ppermute x3, waiting for transfers between devices, trade(): lax.ppermute(value, 'tp', [(source, source ^ bits) for source in range(co...  6.42 us
    ppermute x1, starting transfers between devices, from_behind(): lax.ppermute(value, axis, [(source, source + steps) for source in range(l...  1.49 us
  transfers between devices with their start and end apart: 12, of which 7 were waited for; matrix products, arithmetic and copies ran while one was open for 1% of the time, Pallas kernels for 27%

profile of v24, /device:TPU:0, one launch (start us, length us, event | category | flops | bytes accessed | tf_op | source)
XLA Modules:
  0.0 48.7 jit_solution(5801915713376402797)
XLA Ops:
  0.0 2.9 %collective-permute-start.6 = (bf16[512,1024]{1,0:T(8,128)(2,1)}, bf16[512,1024]{1,0:T(8,128)(2,1)}, u32[]{:S(2)}, u32[]{:S(2)}) collective-permute-start(bf16[512,1024]{1,0:T(8,128)(2,1)} %rest_0_.1), channel_id=1, source_target_pairs={{0,8},{4,20},{8,0},{12,28},{16,24},{20,4},{24,16},{28,12},{1,9},{5... | collective-permute-start | bytes 3145736 | tf_op jit(solution)/shard_map/ppermute | solution.py:334
  2.9 1.5 %tails.1 = (bf16[3,8,1024]{2,1,0:T(8,128)(2,1)S(1)}, bf16[3,1024,128]{2,1,0:T(8,128)(2,1)S(1)}, f32[3,7,1024]{2,1,0:T(8,128)S(1)}, f32[16,128]{1,0:T(8,128)S(1)}...) custom-call(bf16[3,1024,128]{2,1,0:T(8,128)(2,1)} %refs_0_.1, f32[3,7,1024]{2,1,0:T(8,128)} %refs_1_.1, ...), custom_call_target="tpu_custom_call" | custom-call | flops 100000000 | bytes 1000000 | tf_op jit(solution)/shard_map/tails/pallas_call | solution.py:55
  4.5 1.5 %collective-permute-start = (bf16[3,8,1024]{2,1,0:T(8,128)(2,1)S(1)}, bf16[3,8,1024]{2,1,0:T(8,128)(2,1)S(1)}, u32[]{:S(2)}, u32[]{:S(2)}) collective-permute-start(bf16[3,8,1024]{2,1,0:T(8,128)(2,1)S(1)} %get-tuple-element.34), channel_id=1, source_target_pairs={{0,4},{4,8},{8,12},{12,16},{16,20},{20,24},{24,28},{1,5},{5,9},{9,... | collective-permute-start | bytes 147464 | tf_op jit(solution)/shard_map/ppermute | solution.py:26
  6.0 0.1 pad_add_fusion.1.at_ref
  6.0 3.3 %prepare.1 = (f32[3,8,1024]{2,1,0:T(8,128)S(1)}, bf16[128,1024]{1,0:T(8,128)(2,1)S(1)}, f32[128,1024]{1,0:T(8,128)S(1)}, bf16[2048,128]{1,0:T(8,128)(2,1)S(1)}, ...) custom-call(bf16[3,1024,128]{2,1,0:T(8,128)(2,1)S(1)} %get-tuple-element.35.streams_ref, ...), custom_call_target="tpu_custom_call" | custom-call | flops 1000000000 | bytes 10000000 | tf_op jit(solution)/shard_map/prepare/pallas_call | solution.py:55
  9.4 0.6 %states.1 = (f32[16,1024]{1,0:T(8,128)S(1)}, bf16[16,1024]{1,0:T(8,128)(2,1)S(1)}, bf16[128,1024]{1,0:T(8,128)(2,1)S(1)}, f32[8,1024]{1,0:T(8,128)S(1)}) custom-call(bf16[3,8,1024]{2,1,0:T(8,128)(2,1)S(1)} %collective-permute-done.before_ref, f32[3,8,1024]{2,1,0:T(8,128)S(1)} %get-tuple-element.39.heads_ref, f32[3,7,1024]{2,1,0:T(8,128)S(1)} %get-tuple-element.36.taps_ref, ...), custom_call_target="tpu_custom_call" | custom-call | flops 100000000 | bytes 1000000 | tf_op jit(solution)/shard_map/states/pallas_call | solution.py:55
  10.0 0.6 %collective-permute-start.1 = (bf16[16,1024]{1,0:T(8,128)(2,1)S(1)}, bf16[16,1024]{1,0:T(8,128)(2,1)S(1)}, u32[]{:S(2)}, u32[]{:S(2)}) collective-permute-start(bf16[16,1024]{1,0:T(8,128)(2,1)S(1)} %get-tuple-element.42), channel_id=1, source_target_pairs={{0,4},{4,0},{8,12},{12,8},{16,20},{20,16},{24,28},{28,24},{1,5},{5... | collective-permute-start | bytes 98312 | tf_op jit(solution)/shard_map/ppermute | solution.py:334
  10.6 0.8 %inside.2.left_ref = f32[128,512]{1,0:T(8,128)S(1)} custom-call(bf16[128,1024]{1,0:T(8,128)(2,1)S(1)} %get-tuple-element.49.gated_ref, f32[1,1024]{1,0:T(1,128)S(1)} %get-tuple-element.50.skip_ref, f32[128,128]{1,0:T(8,128)S(1)} %get-tuple-element.51.response_ref), custom_call_target="tpu_custom_call" | custom-call | flops 1000000000 | bytes 10000000 | tf_op jit(solution)/shard_map/inside/pallas_call | solution.py:55
  11.6 3.0 %collective-permute-start.2 = (bf16[16,1024]{1,0:T(8,128)(2,1)S(1)}, bf16[16,1024]{1,0:T(8,128)(2,1)S(1)}, u32[]{:S(2)}, u32[]{:S(2)}) collective-permute-start(bf16[16,1024]{1,0:T(8,128)(2,1)S(1)} %get-tuple-element.45), channel_id=1, source_target_pairs={{0,8},{4,12},{8,0},{12,4},{16,24},{20,28},{24,16},{28,20},{1,9},{5... | collective-permute-start | bytes 98312 | tf_op jit(solution)/shard_map/ppermute | solution.py:334
  14.6 0.8 %inside.3.right_ref = f32[128,512]{1,0:T(8,128)S(1)} custom-call(bf16[128,1024]{1,0:T(8,128)(2,1)S(1)} %get-tuple-element.49.gated_ref, f32[1,1024]{1,0:T(1,128)S(1)} %get-tuple-element.50.skip_ref, f32[128,128]{1,0:T(8,128)S(1)} %get-tuple-element.51.response_ref), custom_call_target="tpu_custom_call" | custom-call | flops 1000000000 | bytes 10000000 | tf_op jit(solution)/shard_map/inside/pallas_call | solution.py:55
  15.5 1.7 %collective-permute-done.2.arrived_ref = bf16[16,1024]{1,0:T(8,128)(2,1)S(1)} collective-permute-done((bf16[16,1024]{1,0:T(8,128)(2,1)S(1)}, bf16[16,1024]{1,0:T(8,128)(2,1)S(1)}, u32[]{:S(2)}, u32[]{:S(2)}) %collective-permute-start.2) | collective-permute-done | bytes 32800 | tf_op jit(solution)/shard_map/ppermute | solution.py:334
  17.2 1.7 %collective-permute-start.3 = (bf16[16,1024]{1,0:T(8,128)(2,1)S(1)}, bf16[16,1024]{1,0:T(8,128)(2,1)S(1)}, u32[]{:S(2)}, u32[]{:S(2)}) collective-permute-start(bf16[16,1024]{1,0:T(8,128)(2,1)S(1)} %get-tuple-element.52), channel_id=1, source_target_pairs={{0,16},{4,20},{8,24},{12,28},{16,0},{20,4},{24,8},{28,12},{1,17},{... | collective-permute-start | bytes 98312 | tf_op jit(solution)/shard_map/ppermute | solution.py:334
  18.9 0.4 collective-permute-start.7
  19.3 0.1 pad_add_fusion.at_ref
  19.4 1.8 %collective-permute-done.3.arrived_ref = bf16[16,1024]{1,0:T(8,128)(2,1)S(1)} collective-permute-done((bf16[16,1024]{1,0:T(8,128)(2,1)S(1)}, bf16[16,1024]{1,0:T(8,128)(2,1)S(1)}, u32[]{:S(2)}, u32[]{:S(2)}) %collective-permute-start.3) | collective-permute-done | bytes 32800 | tf_op jit(solution)/shard_map/ppermute | solution.py:334
  21.2 0.8 %finish.3 = bf16[128,512]{1,0:T(8,128)(2,1)S(1)} custom-call(s32[2]{0:T(128)S(1)} %pad_add_fusion.1.at_ref, bf16[16,1024]{1,0:T(8,128)(2,1)S(1)} %collective-permute-done.3.arrived_ref, f32[16,1024]{1,0:T(8,128)S(1)} %get-tuple-element.53.entering_ref, f32[16,1024]{1,0:T(8,128)S(1)} %get-tuple-element.44.wide_ref, ...), custom_call_target="tpu_custom_call" | custom-call | flops 3000000000 | bytes 30000000 | tf_op jit(solution)/shard_map/finish/pallas_call | solution.py:55
  22.1 0.8 %finish.2 = bf16[128,512]{1,0:T(8,128)(2,1)S(1)} custom-call(s32[2]{0:T(128)S(1)} %pad_add_fusion.at_ref, bf16[16,1024]{1,0:T(8,128)(2,1)S(1)} %collective-permute-done.3.arrived_ref, f32[16,1024]{1,0:T(8,128)S(1)} %get-tuple-element.53.entering_ref, f32[16,1024]{1,0:T(8,128)S(1)} %get-tuple-element.44.wide_ref, ...), custom_call_target="tpu_custom_call" | custom-call | flops 3000000000 | bytes 30000000 | tf_op jit(solution)/shard_map/finish/pallas_call | solution.py:55
  22.8 0.5 %collective-permute-done.4 = bf16[128,512]{1,0:T(8,128)(2,1)S(1)} collective-permute-done((bf16[128,512]{1,0:T(8,128)(2,1)S(1)}, bf16[128,512]{1,0:T(8,128)(2,1)S(1)}, u32[]{:S(2)}, u32[]{:S(2)}) %collective-permute-start.4) | collective-permute-done | bytes 131104 | tf_op jit(solution)/shard_map/ppermute | solution.py:334
  23.4 4.2 %collective-permute-start.5 = (bf16[256,512]{1,0:T(8,128)(2,1)S(1)}, bf16[256,512]{1,0:T(8,128)(2,1)S(1)}, u32[]{:S(2)}, u32[]{:S(2)}) collective-permute-start(bf16[256,512]{1,0:T(8,128)(2,1)S(1)} %pad_maximum_fusion.own_ref), channel_id=1, source_target_pairs={{0,3},{1,2},{2,1},{3,0},{4,7},{5,6},{6,5},{7,4},{8,11},{9,10},{10,... | collective-permute-start | bytes 786440 | tf_op jit(solution)/shard_map/ppermute | solution.py:343
  27.6 1.1 %collective-permute-start.10 = (bf16[512,1024]{1,0:T(8,128)(2,1)}, bf16[512,1024]{1,0:T(8,128)(2,1)S(1)}, u32[]{:S(2)}, u32[]{:S(2)}) collective-permute-start(bf16[512,1024]{1,0:T(8,128)(2,1)} %collective-permute-done.6.rest_1_), channel_id=1, source_target_pairs={{0,16},{4,12},{8,24},{12,4},{16,0},{20,28},{24,8},{28,20},{1,17},{... | collective-permute-start | bytes 3145736 | tf_op jit(solution)/shard_map/ppermute | solution.py:334
  28.8 0.1 stack.44.at_ref
  28.8 5.9 %collective-permute-done.5.across_ref = bf16[256,512]{1,0:T(8,128)(2,1)S(1)} collective-permute-done((bf16[256,512]{1,0:T(8,128)(2,1)S(1)}, bf16[256,512]{1,0:T(8,128)(2,1)S(1)}, u32[]{:S(2)}, u32[]{:S(2)}) %collective-permute-start.5) | collective-permute-done | bytes 262176 | tf_op jit(solution)/shard_map/ppermute | solution.py:343
  34.8 4.8 %collective-permute-start.8 = (bf16[256,512]{1,0:T(8,128)(2,1)S(1)}, bf16[256,512]{1,0:T(8,128)(2,1)S(1)}, u32[]{:S(2)}, u32[]{:S(2)}) collective-permute-start(bf16[256,512]{1,0:T(8,128)(2,1)S(1)} %collective-permute-done.5.across_ref), channel_id=1, source_target_pairs={{0,1},{1,0},{2,3},{3,2},{4,5},{5,4},{6,7},{7,6},{8,9},{9,8},{10,11... | collective-permute-start | bytes 786440 | tf_op jit(solution)/shard_map/ppermute | solution.py:343
  39.6 0.5 collective-permute-done.9.beside_ref
  40.0 2.9 %early.1 = (f32[256,1024]{1,0:T(8,128)S(1)}, bf16[512,1024]{1,0:T(8,128)(2,1)S(1)}, bf16[256,512]{1,0:T(8,128)(2,1)S(1)}) custom-call(s32[5]{0:T(128)S(1)} %stack.44.at_ref, bf16[256,512]{1,0:T(8,128)(2,1)S(1)} %pad_maximum_fusion.own_ref, bf16[256,512]{1,0:T(8,128)(2,1)S(1)} %collective-permute-done.9.beside_ref, ...), custom_call_target="tpu_custom_call" | custom-call | flops 10000000000 | bytes 100000000 | tf_op jit(solution)/shard_map/early/pallas_call | solution.py:55
  42.9 2.0 %collective-permute-done.10.weight_ref = bf16[512,1024]{1,0:T(8,128)(2,1)S(1)} collective-permute-done((bf16[512,1024]{1,0:T(8,128)(2,1)}, bf16[512,1024]{1,0:T(8,128)(2,1)S(1)}, u32[]{:S(2)}, u32[]{:S(2)}) %collective-permute-start.10) | collective-permute-done | bytes 1048608 | tf_op jit(solution)/shard_map/ppermute | solution.py:334
  45.0 0.6 %keep.1.rows_ref = bf16[512,1024]{1,0:T(8,128)(2,1)S(1)} custom-call(s32[5]{0:T(128)S(1)} %stack.44.at_ref, bf16[512,1024]{1,0:T(8,128)(2,1)S(1)} %get-tuple-element.62.rows_ref, bf16[512,1024]{1,0:T(8,128)(2,1)S(1)} %collective-permute-done.10.weight_ref), custom_call_target="tpu_custom_call", output_to_operand_aliasing={{}: (1, {})} | custom-call | tf_op jit(solution)/shard_map/keep/pallas_call | solution.py:55
  45.6 0.5 joined.1.total_ref
  46.0 0.3 late.3
  46.4 0.3 late.2
  46.7 1.2 %collective-permute-done.11 = bf16[128,1024]{1,0:T(8,128)(2,1)S(1)} collective-permute-done((bf16[128,1024]{1,0:T(8,128)(2,1)S(1)}, bf16[128,1024]{1,0:T(8,128)(2,1)S(1)}, u32[]{:S(2)}, u32[]{:S(2)}) %collective-permute-start.11) | collective-permute-done | bytes 262176 | tf_op jit(solution)/shard_map/ppermute | solution.py:334
  47.9 0.8 %add_convert_fusion = bf16[128,1024]{1,0:T(8,128)(2,1)} fusion(f32[128,1024]{1,0:T(8,128)S(1)} %late.2, bf16[128,1024]{1,0:T(8,128)(2,1)S(1)} %collective-permute-done.11), kind=kLoop, calls=%fused_computation | loop fusion | flops 393216 | bytes 1048576 | tf_op jit(solution)/shard_map/convert_element_type | solution.py:502
  (14 shorter events, 0.3 us)
Async XLA Ops:
  0.0 18.9 %collective-permute-start.6 = (bf16[512,1024]{1,0:T(8,128)(2,1)}, bf16[512,1024]{1,0:T(8,128)(2,1)}, u32[]{:S(2)}, u32[]{:S(2)}) collective-permute-start(bf16[512,1024]{1,0:T(8,128)(2,1)} %rest_0_.1), channel_id=1, source_target_pairs={{0,8},{4,20},{8,0},{12,28},{16,24},{20,4},{24,16},{28,12},{1,9},{5... | collective-permute-start | bytes 3145736 | tf_op jit(solution)/shard_map/ppermute | solution.py:334
  4.5 4.9 %collective-permute-start = (bf16[3,8,1024]{2,1,0:T(8,128)(2,1)S(1)}, bf16[3,8,1024]{2,1,0:T(8,128)(2,1)S(1)}, u32[]{:S(2)}, u32[]{:S(2)}) collective-permute-start(bf16[3,8,1024]{2,1,0:T(8,128)(2,1)S(1)} %get-tuple-element.34), channel_id=1, source_target_pairs={{0,4},{4,8},{8,12},{12,16},{16,20},{20,24},{24,28},{1,5},{5,9},{9,... | collective-permute-start | bytes 147464 | tf_op jit(solution)/shard_map/ppermute | solution.py:26
  10.0 1.5 %collective-permute-start.1 = (bf16[16,1024]{1,0:T(8,128)(2,1)S(1)}, bf16[16,1024]{1,0:T(8,128)(2,1)S(1)}, u32[]{:S(2)}, u32[]{:S(2)}) collective-permute-start(bf16[16,1024]{1,0:T(8,128)(2,1)S(1)} %get-tuple-element.42), channel_id=1, source_target_pairs={{0,4},{4,0},{8,12},{12,8},{16,20},{20,16},{24,28},{28,24},{1,5},{5... | collective-permute-start | bytes 98312 | tf_op jit(solution)/shard_map/ppermute | solution.py:334
  11.6 7.4 %copy-start = (bf16[512,1024]{1,0:T(8,128)(2,1)S(1)}, bf16[512,1024]{1,0:T(8,128)(2,1)}, u32[]{:S(2)}) copy-start(bf16[512,1024]{1,0:T(8,128)(2,1)} %rest_0_.1) | copy-start | bytes 3145732
  11.6 5.6 %collective-permute-start.2 = (bf16[16,1024]{1,0:T(8,128)(2,1)S(1)}, bf16[16,1024]{1,0:T(8,128)(2,1)S(1)}, u32[]{:S(2)}, u32[]{:S(2)}) collective-permute-start(bf16[16,1024]{1,0:T(8,128)(2,1)S(1)} %get-tuple-element.45), channel_id=1, source_target_pairs={{0,8},{4,12},{8,0},{12,4},{16,24},{20,28},{24,16},{28,20},{1,9},{5... | collective-permute-start | bytes 98312 | tf_op jit(solution)/shard_map/ppermute | solution.py:334
  17.2 4.0 %collective-permute-start.3 = (bf16[16,1024]{1,0:T(8,128)(2,1)S(1)}, bf16[16,1024]{1,0:T(8,128)(2,1)S(1)}, u32[]{:S(2)}, u32[]{:S(2)}) collective-permute-start(bf16[16,1024]{1,0:T(8,128)(2,1)S(1)} %get-tuple-element.52), channel_id=1, source_target_pairs={{0,16},{4,20},{8,24},{12,28},{16,0},{20,4},{24,8},{28,12},{1,17},{... | collective-permute-start | bytes 98312 | tf_op jit(solution)/shard_map/ppermute | solution.py:334
  18.9 15.8 %collective-permute-start.7 = (bf16[512,1024]{1,0:T(8,128)(2,1)S(1)}, bf16[512,1024]{1,0:T(8,128)(2,1)}, u32[]{:S(2)}, u32[]{:S(2)}) collective-permute-start(bf16[512,1024]{1,0:T(8,128)(2,1)S(1)} %copy-done), channel_id=1, source_target_pairs={{0,16},{4,12},{8,24},{12,4},{16,0},{20,28},{24,8},{28,20},{1,17},{... | collective-permute-start | bytes 3145736 | tf_op jit(solution)/shard_map/ppermute | solution.py:334
  22.0 1.4 %collective-permute-start.4 = (bf16[128,512]{1,0:T(8,128)(2,1)S(1)}, bf16[128,512]{1,0:T(8,128)(2,1)S(1)}, u32[]{:S(2)}, u32[]{:S(2)}) collective-permute-start(bf16[128,512]{1,0:T(8,128)(2,1)S(1)} %finish.3), channel_id=1, source_target_pairs={{0,4},{4,0},{8,12},{12,8},{16,20},{20,16},{24,28},{28,24},{1,5},{5... | collective-permute-start | bytes 393224 | tf_op jit(solution)/shard_map/ppermute | solution.py:334
  23.4 11.4 %collective-permute-start.5 = (bf16[256,512]{1,0:T(8,128)(2,1)S(1)}, bf16[256,512]{1,0:T(8,128)(2,1)S(1)}, u32[]{:S(2)}, u32[]{:S(2)}) collective-permute-start(bf16[256,512]{1,0:T(8,128)(2,1)S(1)} %pad_maximum_fusion.own_ref), channel_id=1, source_target_pairs={{0,3},{1,2},{2,1},{3,0},{4,7},{5,6},{6,5},{7,4},{8,11},{9,10},{10,... | collective-permute-start | bytes 786440 | tf_op jit(solution)/shard_map/ppermute | solution.py:343
  27.6 12.4 %collective-permute-start.9 = (bf16[256,512]{1,0:T(8,128)(2,1)S(1)}, bf16[256,512]{1,0:T(8,128)(2,1)S(1)}, u32[]{:S(2)}, u32[]{:S(2)}) collective-permute-start(bf16[256,512]{1,0:T(8,128)(2,1)S(1)} %pad_maximum_fusion.own_ref), channel_id=1, source_target_pairs={{0,1},{1,0},{2,3},{3,2},{4,5},{5,4},{6,7},{7,6},{8,9},{9,8},{10,11... | collective-permute-start | bytes 786440 | tf_op jit(solution)/shard_map/ppermute | solution.py:343
  27.6 17.4 %collective-permute-start.10 = (bf16[512,1024]{1,0:T(8,128)(2,1)}, bf16[512,1024]{1,0:T(8,128)(2,1)S(1)}, u32[]{:S(2)}, u32[]{:S(2)}) collective-permute-start(bf16[512,1024]{1,0:T(8,128)(2,1)} %collective-permute-done.6.rest_1_), channel_id=1, source_target_pairs={{0,16},{4,12},{8,24},{12,4},{16,0},{20,28},{24,8},{28,20},{1,17},{... | collective-permute-start | bytes 3145736 | tf_op jit(solution)/shard_map/ppermute | solution.py:334
  34.8 11.2 %collective-permute-start.8 = (bf16[256,512]{1,0:T(8,128)(2,1)S(1)}, bf16[256,512]{1,0:T(8,128)(2,1)S(1)}, u32[]{:S(2)}, u32[]{:S(2)}) collective-permute-start(bf16[256,512]{1,0:T(8,128)(2,1)S(1)} %collective-permute-done.5.across_ref), channel_id=1, source_target_pairs={{0,1},{1,0},{2,3},{3,2},{4,5},{5,4},{6,7},{7,6},{8,9},{9,8},{10,11... | collective-permute-start | bytes 786440 | tf_op jit(solution)/shard_map/ppermute | solution.py:343
  46.3 1.6 %collective-permute-start.11 = (bf16[128,1024]{1,0:T(8,128)(2,1)S(1)}, bf16[128,1024]{1,0:T(8,128)(2,1)S(1)}, u32[]{:S(2)}, u32[]{:S(2)}) collective-permute-start(bf16[128,1024]{1,0:T(8,128)(2,1)S(1)} %late.3), channel_id=1, source_target_pairs={{0,4},{4,0},{8,12},{12,8},{16,20},{20,16},{24,28},{28,24},{1,5},{5... | collective-permute-start | bytes 786440 | tf_op jit(solution)/shard_map/ppermute | solution.py:334

commit v25 on v24

--- a/solution.py
+++ b/solution.py
@@ -244,8 +244,8 @@
     unrolled(tiles, back)
 
 
-def join_kernel(bit, me_ref, arrived_ref, ends_ref, entering_ref, wide_ref, sent_ref, later_ref, *joined_ref):
-    me = me_ref[0]
+def join_kernel(bit, arrived_ref, ends_ref, entering_ref, wide_ref, sent_ref, later_ref, *joined_ref):
+    me = lax.axis_index("ctx")
     high = (me >> bit) % 2 == 1
     arrived = arrived_ref[...].astype(F32)
     wide = wide_ref[...]
@@ -259,12 +259,13 @@
 
 
 def finish_kernel(
-    bit, at_ref, arrived_ref, entering_ref, wide_ref, lift_ref, query_ref, first_ref, left_ref, right_ref, mixed_ref, state_ref
+    bit, half, arrived_ref, entering_ref, wide_ref, lift_ref, query_ref, first_ref, left_ref, right_ref, mixed_ref, state_ref
 ):
     length, share = mixed_ref.shape
     poles, channels = wide_ref.shape
     in_tile = lift_ref.shape[1] // poles * TILE // channels
-    me, half = at_ref[0], at_ref[1]
+    me = lax.axis_index("ctx")
+    half = half(me % CORES)
     here = tile_of(half, share)
     high = (me >> bit) % 2 == 1
     before = (me % (1 << bit)).astype(F32)
@@ -315,9 +316,10 @@
     out_ref[...] = total_ref[...] + dot(block_ref[...], weight_ref[...])
 
 
-def keep_kernel(at_ref, rows_ref, weight_ref, last_ref, sem):
+def keep_kernel(square, rows_ref, weight_ref, last_ref, sem):
     del rows_ref
-    latest = at_ref[4] == at_ref[0] ^ 2
+    chip = lax.axis_index("ctx") // CORES if square else 0
+    latest = chip ^ 3 == lax.axis_index("tp") ^ 2
     copy = pltpu.make_async_copy(weight_ref, last_ref, sem)
     pl.when(latest)(copy.start)
     pl.when(latest)(copy.wait)
@@ -412,33 +414,31 @@
                 functools.partial(join_kernel, bit),
                 outs[: 2 if bit == steps - 2 else 3],
                 "join",
-                me[None], arrived, ends[0], entering, wide,
-                specs=[pl.BlockSpec(memory_space=pltpu.SMEM)] + whole(4),
+                arrived, ends[0], entering, wide,
             )
         if bit == steps - 2:
             bases.append(within(0))
             sent = after(sent, bases[0])
     bases.append(within(1))
     if square:
-        other_near = swap(after(out_weight, (bases[-1], near)), 4, 2)
+        other_near = swap(after(out_weight, (entering, sent, near)), 4, 2)
     core = me % CORES
     smem = [pl.BlockSpec(memory_space=pltpu.SMEM)]
 
     def finished(half):
         return call(
-            functools.partial(finish_kernel, steps - 1),
+            functools.partial(finish_kernel, steps - 1, half),
             [((length, share), BF16)],
             "finish",
-            jnp.stack([me, half]), arrived, entering, wide, lift, query, first, *bases,
-            specs=smem + whole(8),
-            flops=3 * 10**9,
+            arrived, entering, wide, lift, query, first, *bases,
+            flops=5 * 10**9,
             scratch=[pltpu.VMEM((poles, share), F32)],
         )[0]
 
     if rows == share:
-        other, mine = finished(1 - core), finished(core)
+        other, mine = finished(lambda core: 1 - core), finished(lambda core: core)
     else:
-        mixed = jnp.concatenate([finished(jnp.full_like(me, half)) for half in range(CORES)], axis=1)
+        mixed = jnp.concatenate([finished(lambda core, half=half: half) for half in range(CORES)], axis=1)
         by_core = mixed.reshape(length, share // rows, CORES, rows).transpose(2, 0, 1, 3)
         by_core = by_core.reshape(CORES, length, share)
         mine = lax.dynamic_index_in_dim(by_core, core, 0, keepdims=False)
@@ -478,15 +478,15 @@
     )
     anywhere = [pl.BlockSpec(memory_space=pl.ANY)]
     (last_rows,) = call(
-        keep_kernel,
+        functools.partial(keep_kernel, square),
         [((share, features), BF16)],
         "keep",
-        at, last_rows, latest,
-        specs=smem + anywhere * 2,
+        last_rows, latest,
+        specs=anywhere * 2,
         out_specs=anywhere,
         scratch=[pltpu.SemaphoreType.DMA],
         flops=0,
-        aliases={1: 0},
+        aliases={0: 0},
     )
     sides = []
     for side, kind in ((1, BF16), (0, F32)):

time: 48.9 us -> 49.2 us (level)
  waiting for transfers between devices: 13.8 us -> 16.4 us
  Pallas kernels: 13.3 us -> 11.7 us
    ppermute x8, waiting for transfers between devices: 7.33 us -> 9.93 us  [swap(): return lax.ppermute(value, 'ctx', pairs)]
    pallas_call x14, Pallas kernels: 13.3 us -> 11.7 us  [call(): pl.pallas_call(kernel, out_shape=tuple((jax.ShapeDtypeStruct(*out) for ou...]
    ppermute x3, starting transfers between devices: 8.97 us -> 8.47 us  [trade(): lax.ppermute(value, 'tp', [(source, source ^ bits) for source in range(co...]
  transfers between devices with their start and end apart: 12 -> 12, of which waited for: 7 -> 9; matrix products, arithmetic and copies ran while one was open for 1% -> 0% of each run, Pallas kernels for 27% -> 23%
where the time goes in v25:
time: 49.2 us; the launch traced here: 49.1 us
  starting transfers between devices  20 us (41%)
  waiting for transfers between devices  16.4 us (33%)
  Pallas kernels  11.7 us (24%)
  other arithmetic  0.78 us (2%)
    pallas_call x14, Pallas kernels, call(): pl.pallas_call(kernel, out_shape=tuple((jax.ShapeDtypeStruct(*out) for ou...  11.7 us
    ppermute x8, starting transfers between devices, swap(): return lax.ppermute(value, 'ctx', pairs)  10 us
    ppermute x8, waiting for transfers between devices, swap(): return lax.ppermute(value, 'ctx', pairs)  9.93 us
    ppermute x3, starting transfers between devices, trade(): lax.ppermute(value, 'tp', [(source, source ^ bits) for source in range(co...  8.47 us
    ppermute x3, waiting for transfers between devices, trade(): lax.ppermute(value, 'tp', [(source, source ^ bits) for source in range(co...  6.43 us
    ppermute x1, starting transfers between devices, from_behind(): lax.ppermute(value, axis, [(source, source + steps) for source in range(l...  1.49 us
  transfers between devices with their start and end apart: 12, of which 9 were waited for; matrix products, arithmetic and copies ran while one was open for 0% of the time, Pallas kernels for 23%

profile of v25, /device:TPU:0, one launch (start us, length us, event | category | flops | bytes accessed | tf_op | source)
XLA Modules:
  0.0 49.1 jit_solution(4242842020370951712)
XLA Ops:
  0.0 2.9 %collective-permute-start.6 = (bf16[512,1024]{1,0:T(8,128)(2,1)}, bf16[512,1024]{1,0:T(8,128)(2,1)}, u32[]{:S(2)}, u32[]{:S(2)}) collective-permute-start(bf16[512,1024]{1,0:T(8,128)(2,1)} %rest_0_.1), channel_id=1, source_target_pairs={{0,8},{4,20},{8,0},{12,28},{16,24},{20,4},{24,16},{28,12},{1,9},{5... | collective-permute-start | bytes 3145736 | tf_op jit(solution)/shard_map/ppermute | solution.py:336
  2.9 1.5 %tails.1 = (bf16[3,8,1024]{2,1,0:T(8,128)(2,1)S(1)}, bf16[3,1024,128]{2,1,0:T(8,128)(2,1)S(1)}, f32[3,7,1024]{2,1,0:T(8,128)S(1)}, f32[16,128]{1,0:T(8,128)S(1)}...) custom-call(bf16[3,1024,128]{2,1,0:T(8,128)(2,1)} %refs_0_.1, f32[3,7,1024]{2,1,0:T(8,128)} %refs_1_.1, f32[16,128]{1,0:T(8,128)} %bitcast.8, ...), custom_call_target="tpu_custom_call" | custom-call | flops 100000000 | bytes 1000000 | tf_op jit(solution)/shard_map/tails/pallas_call | solution.py:55
  4.5 1.5 %collective-permute-start = (bf16[3,8,1024]{2,1,0:T(8,128)(2,1)S(1)}, bf16[3,8,1024]{2,1,0:T(8,128)(2,1)S(1)}, u32[]{:S(2)}, u32[]{:S(2)}) collective-permute-start(bf16[3,8,1024]{2,1,0:T(8,128)(2,1)S(1)} %get-tuple-element.34), channel_id=1, source_target_pairs={{0,4},{4,8},{8,12},{12,16},{16,20},{20,24},{24,28},{1,5},{5,9},{9,... | collective-permute-start | bytes 147464 | tf_op jit(solution)/shard_map/ppermute | solution.py:26
  5.9 3.3 %prepare.1 = (f32[3,8,1024]{2,1,0:T(8,128)S(1)}, bf16[128,1024]{1,0:T(8,128)(2,1)S(1)}, f32[128,1024]{1,0:T(8,128)S(1)}, bf16[2048,128]{1,0:T(8,128)(2,1)S(1)}, ...) custom-call(bf16[3,1024,128]{2,1,0:T(8,128)(2,1)S(1)} %get-tuple-element.35.streams_ref, ...), custom_call_target="tpu_custom_call" | custom-call | flops 1000000000 | bytes 10000000 | tf_op jit(solution)/shard_map/prepare/pallas_call | solution.py:55
  9.3 0.6 %states.1 = (f32[16,1024]{1,0:T(8,128)S(1)}, bf16[16,1024]{1,0:T(8,128)(2,1)S(1)}, bf16[128,1024]{1,0:T(8,128)(2,1)S(1)}, f32[8,1024]{1,0:T(8,128)S(1)}) custom-call(bf16[3,8,1024]{2,1,0:T(8,128)(2,1)S(1)} %collective-permute-done.before_ref, f32[3,8,1024]{2,1,0:T(8,128)S(1)} %get-tuple-element.39.heads_ref, f32[3,7,1024]{2,1,0:T(8,128)S(1)} %get-tuple-element.36.taps_ref, ...), custom_call_target="tpu_custom_call" | custom-call | flops 100000000 | bytes 1000000 | tf_op jit(solution)/shard_map/states/pallas_call | solution.py:55
  9.9 0.6 %collective-permute-start.1 = (bf16[16,1024]{1,0:T(8,128)(2,1)S(1)}, bf16[16,1024]{1,0:T(8,128)(2,1)S(1)}, u32[]{:S(2)}, u32[]{:S(2)}) collective-permute-start(bf16[16,1024]{1,0:T(8,128)(2,1)S(1)} %get-tuple-element.42), channel_id=1, source_target_pairs={{0,4},{4,0},{8,12},{12,8},{16,20},{20,16},{24,28},{28,24},{1,5},{5... | collective-permute-start | bytes 98312 | tf_op jit(solution)/shard_map/ppermute | solution.py:336
  10.5 0.9 %collective-permute-done.1.arrived_ref = bf16[16,1024]{1,0:T(8,128)(2,1)S(1)} collective-permute-done((bf16[16,1024]{1,0:T(8,128)(2,1)S(1)}, bf16[16,1024]{1,0:T(8,128)(2,1)S(1)}, u32[]{:S(2)}, u32[]{:S(2)}) %collective-permute-start.1) | collective-permute-done | bytes 32800 | tf_op jit(solution)/shard_map/ppermute | solution.py:336
  11.5 3.0 %collective-permute-start.2 = (bf16[16,1024]{1,0:T(8,128)(2,1)S(1)}, bf16[16,1024]{1,0:T(8,128)(2,1)S(1)}, u32[]{:S(2)}, u32[]{:S(2)}) collective-permute-start(bf16[16,1024]{1,0:T(8,128)(2,1)S(1)} %get-tuple-element.45), channel_id=1, source_target_pairs={{0,8},{4,12},{8,0},{12,4},{16,24},{20,28},{24,16},{28,20},{1,9},{5... | collective-permute-start | bytes 98312 | tf_op jit(solution)/shard_map/ppermute | solution.py:336
  14.5 0.8 %inside.2.left_ref = f32[128,512]{1,0:T(8,128)S(1)} custom-call(bf16[128,1024]{1,0:T(8,128)(2,1)S(1)} %get-tuple-element.49.gated_ref, f32[1,1024]{1,0:T(1,128)S(1)} %get-tuple-element.50.skip_ref, f32[128,128]{1,0:T(8,128)S(1)} %get-tuple-element.51.response_ref), custom_call_target="tpu_custom_call" | custom-call | flops 1000000000 | bytes 10000000 | tf_op jit(solution)/shard_map/inside/pallas_call | solution.py:55
  15.3 1.8 %collective-permute-done.2.arrived_ref = bf16[16,1024]{1,0:T(8,128)(2,1)S(1)} collective-permute-done((bf16[16,1024]{1,0:T(8,128)(2,1)S(1)}, bf16[16,1024]{1,0:T(8,128)(2,1)S(1)}, u32[]{:S(2)}, u32[]{:S(2)}) %collective-permute-start.2) | collective-permute-done | bytes 32800 | tf_op jit(solution)/shard_map/ppermute | solution.py:336
  17.2 1.7 %collective-permute-start.3 = (bf16[16,1024]{1,0:T(8,128)(2,1)S(1)}, bf16[16,1024]{1,0:T(8,128)(2,1)S(1)}, u32[]{:S(2)}, u32[]{:S(2)}) collective-permute-start(bf16[16,1024]{1,0:T(8,128)(2,1)S(1)} %get-tuple-element.52), channel_id=1, source_target_pairs={{0,16},{4,20},{8,24},{12,28},{16,0},{20,4},{24,8},{28,12},{1,17},{... | collective-permute-start | bytes 98312 | tf_op jit(solution)/shard_map/ppermute | solution.py:336
  18.9 0.8 %inside.3.right_ref = f32[128,512]{1,0:T(8,128)S(1)} custom-call(bf16[128,1024]{1,0:T(8,128)(2,1)S(1)} %get-tuple-element.49.gated_ref, f32[1,1024]{1,0:T(1,128)S(1)} %get-tuple-element.50.skip_ref, f32[128,128]{1,0:T(8,128)S(1)} %get-tuple-element.51.response_ref), custom_call_target="tpu_custom_call" | custom-call | flops 1000000000 | bytes 10000000 | tf_op jit(solution)/shard_map/inside/pallas_call | solution.py:55
  19.8 0.4 collective-permute-start.7
  20.2 1.0 %collective-permute-done.3.arrived_ref = bf16[16,1024]{1,0:T(8,128)(2,1)S(1)} collective-permute-done((bf16[16,1024]{1,0:T(8,128)(2,1)S(1)}, bf16[16,1024]{1,0:T(8,128)(2,1)S(1)}, u32[]{:S(2)}, u32[]{:S(2)}) %collective-permute-start.3) | collective-permute-done | bytes 32800 | tf_op jit(solution)/shard_map/ppermute | solution.py:336
  21.2 0.2 finish.3
  21.4 0.1 collective-permute-start.4
  21.5 0.2 finish.2
  21.8 1.1 %collective-permute-done.4 = bf16[128,512]{1,0:T(8,128)(2,1)S(1)} collective-permute-done((bf16[128,512]{1,0:T(8,128)(2,1)S(1)}, bf16[128,512]{1,0:T(8,128)(2,1)S(1)}, u32[]{:S(2)}, u32[]{:S(2)}) %collective-permute-start.4) | collective-permute-done | bytes 131104 | tf_op jit(solution)/shard_map/ppermute | solution.py:336
  22.9 4.2 %collective-permute-start.5 = (bf16[256,512]{1,0:T(8,128)(2,1)S(1)}, bf16[256,512]{1,0:T(8,128)(2,1)S(1)}, u32[]{:S(2)}, u32[]{:S(2)}) collective-permute-start(bf16[256,512]{1,0:T(8,128)(2,1)S(1)} %pad_maximum_fusion.own_ref), channel_id=1, source_target_pairs={{0,3},{1,2},{2,1},{3,0},{4,7},{5,6},{6,5},{7,4},{8,11},{9,10},{10,... | collective-permute-start | bytes 786440 | tf_op jit(solution)/shard_map/ppermute | solution.py:345
  27.1 1.1 %collective-permute-start.10 = (bf16[512,1024]{1,0:T(8,128)(2,1)}, bf16[512,1024]{1,0:T(8,128)(2,1)S(1)}, u32[]{:S(2)}, u32[]{:S(2)}) collective-permute-start(bf16[512,1024]{1,0:T(8,128)(2,1)} %collective-permute-done.6.rest_1_), channel_id=1, source_target_pairs={{0,16},{4,12},{8,24},{12,4},{16,0},{20,28},{24,8},{28,20},{1,17},{... | collective-permute-start | bytes 3145736 | tf_op jit(solution)/shard_map/ppermute | solution.py:336
  28.2 0.1 stack.23.at_ref
  28.3 6.0 %collective-permute-done.5.across_ref = bf16[256,512]{1,0:T(8,128)(2,1)S(1)} collective-permute-done((bf16[256,512]{1,0:T(8,128)(2,1)S(1)}, bf16[256,512]{1,0:T(8,128)(2,1)S(1)}, u32[]{:S(2)}, u32[]{:S(2)}) %collective-permute-start.5) | collective-permute-done | bytes 262176 | tf_op jit(solution)/shard_map/ppermute | solution.py:345
  34.3 0.5 %collective-permute-done.7.rest_2_ = bf16[512,1024]{1,0:T(8,128)(2,1)} collective-permute-done((bf16[512,1024]{1,0:T(8,128)(2,1)S(1)}, bf16[512,1024]{1,0:T(8,128)(2,1)}, u32[]{:S(2)}, u32[]{:S(2)}) %collective-permute-start.7) | collective-permute-done | bytes 1048608 | tf_op jit(solution)/shard_map/ppermute | solution.py:336
  34.8 4.3 %collective-permute-start.8 = (bf16[256,512]{1,0:T(8,128)(2,1)S(1)}, bf16[256,512]{1,0:T(8,128)(2,1)S(1)}, u32[]{:S(2)}, u32[]{:S(2)}) collective-permute-start(bf16[256,512]{1,0:T(8,128)(2,1)S(1)} %collective-permute-done.5.across_ref), channel_id=1, source_target_pairs={{0,1},{1,0},{2,3},{3,2},{4,5},{5,4},{6,7},{7,6},{8,9},{9,8},{10,11... | collective-permute-start | bytes 786440 | tf_op jit(solution)/shard_map/ppermute | solution.py:345
  39.0 0.5 collective-permute-done.9.beside_ref
  39.5 2.9 %early.1 = (f32[256,1024]{1,0:T(8,128)S(1)}, bf16[512,1024]{1,0:T(8,128)(2,1)S(1)}, bf16[256,512]{1,0:T(8,128)(2,1)S(1)}) custom-call(s32[5]{0:T(128)S(1)} %stack.23.at_ref, bf16[256,512]{1,0:T(8,128)(2,1)S(1)} %pad_maximum_fusion.own_ref, bf16[256,512]{1,0:T(8,128)(2,1)S(1)} %collective-permute-done.9.beside_ref, ...), custom_call_target="tpu_custom_call" | custom-call | flops 10000000000 | bytes 100000000 | tf_op jit(solution)/shard_map/early/pallas_call | solution.py:55
  42.4 3.5 %collective-permute-done.10.weight_ref = bf16[512,1024]{1,0:T(8,128)(2,1)S(1)} collective-permute-done((bf16[512,1024]{1,0:T(8,128)(2,1)}, bf16[512,1024]{1,0:T(8,128)(2,1)S(1)}, u32[]{:S(2)}, u32[]{:S(2)}) %collective-permute-start.10) | collective-permute-done | bytes 1048608 | tf_op jit(solution)/shard_map/ppermute | solution.py:336
  45.9 0.5 joined.1.total_ref
  46.4 0.3 late.3
  46.8 0.3 late.2
  47.1 1.2 %collective-permute-done.11 = bf16[128,1024]{1,0:T(8,128)(2,1)S(1)} collective-permute-done((bf16[128,1024]{1,0:T(8,128)(2,1)S(1)}, bf16[128,1024]{1,0:T(8,128)(2,1)S(1)}, u32[]{:S(2)}, u32[]{:S(2)}) %collective-permute-start.11) | collective-permute-done | bytes 262176 | tf_op jit(solution)/shard_map/ppermute | solution.py:336
  48.3 0.8 %add_convert_fusion = bf16[128,1024]{1,0:T(8,128)(2,1)} fusion(f32[128,1024]{1,0:T(8,128)S(1)} %late.2, bf16[128,1024]{1,0:T(8,128)(2,1)S(1)} %collective-permute-done.11), kind=kLoop, calls=%fused_computation | loop fusion | flops 393216 | bytes 1048576 | tf_op jit(solution)/shard_map/convert_element_type | solution.py:502
  (12 shorter events, 0.2 us)
Async XLA Ops:
  0.0 19.8 %collective-permute-start.6 = (bf16[512,1024]{1,0:T(8,128)(2,1)}, bf16[512,1024]{1,0:T(8,128)(2,1)}, u32[]{:S(2)}, u32[]{:S(2)}) collective-permute-start(bf16[512,1024]{1,0:T(8,128)(2,1)} %rest_0_.1), channel_id=1, source_target_pairs={{0,8},{4,20},{8,0},{12,28},{16,24},{20,4},{24,16},{28,12},{1,9},{5... | collective-permute-start | bytes 3145736 | tf_op jit(solution)/shard_map/ppermute | solution.py:336
  4.5 4.8 %collective-permute-start = (bf16[3,8,1024]{2,1,0:T(8,128)(2,1)S(1)}, bf16[3,8,1024]{2,1,0:T(8,128)(2,1)S(1)}, u32[]{:S(2)}, u32[]{:S(2)}) collective-permute-start(bf16[3,8,1024]{2,1,0:T(8,128)(2,1)S(1)} %get-tuple-element.34), channel_id=1, source_target_pairs={{0,4},{4,8},{8,12},{12,16},{16,20},{20,24},{24,28},{1,5},{5,9},{9,... | collective-permute-start | bytes 147464 | tf_op jit(solution)/shard_map/ppermute | solution.py:26
  9.9 1.5 %collective-permute-start.1 = (bf16[16,1024]{1,0:T(8,128)(2,1)S(1)}, bf16[16,1024]{1,0:T(8,128)(2,1)S(1)}, u32[]{:S(2)}, u32[]{:S(2)}) collective-permute-start(bf16[16,1024]{1,0:T(8,128)(2,1)S(1)} %get-tuple-element.42), channel_id=1, source_target_pairs={{0,4},{4,0},{8,12},{12,8},{16,20},{20,16},{24,28},{28,24},{1,5},{5... | collective-permute-start | bytes 98312 | tf_op jit(solution)/shard_map/ppermute | solution.py:336
  11.5 5.7 %collective-permute-start.2 = (bf16[16,1024]{1,0:T(8,128)(2,1)S(1)}, bf16[16,1024]{1,0:T(8,128)(2,1)S(1)}, u32[]{:S(2)}, u32[]{:S(2)}) collective-permute-start(bf16[16,1024]{1,0:T(8,128)(2,1)S(1)} %get-tuple-element.45), channel_id=1, source_target_pairs={{0,8},{4,12},{8,0},{12,4},{16,24},{20,28},{24,16},{28,20},{1,9},{5... | collective-permute-start | bytes 98312 | tf_op jit(solution)/shard_map/ppermute | solution.py:336
  17.2 2.6 %copy-start = (bf16[512,1024]{1,0:T(8,128)(2,1)S(1)}, bf16[512,1024]{1,0:T(8,128)(2,1)}, u32[]{:S(2)}) copy-start(bf16[512,1024]{1,0:T(8,128)(2,1)} %rest_0_.1) | copy-start | bytes 3145732
  17.2 4.0 %collective-permute-start.3 = (bf16[16,1024]{1,0:T(8,128)(2,1)S(1)}, bf16[16,1024]{1,0:T(8,128)(2,1)S(1)}, u32[]{:S(2)}, u32[]{:S(2)}) collective-permute-start(bf16[16,1024]{1,0:T(8,128)(2,1)S(1)} %get-tuple-element.52), channel_id=1, source_target_pairs={{0,16},{4,20},{8,24},{12,28},{16,0},{20,4},{24,8},{28,12},{1,17},{... | collective-permute-start | bytes 98312 | tf_op jit(solution)/shard_map/ppermute | solution.py:336
  19.8 15.0 %collective-permute-start.7 = (bf16[512,1024]{1,0:T(8,128)(2,1)S(1)}, bf16[512,1024]{1,0:T(8,128)(2,1)}, u32[]{:S(2)}, u32[]{:S(2)}) collective-permute-start(bf16[512,1024]{1,0:T(8,128)(2,1)S(1)} %copy-done), channel_id=1, source_target_pairs={{0,16},{4,12},{8,24},{12,4},{16,0},{20,28},{24,8},{28,20},{1,17},{... | collective-permute-start | bytes 3145736 | tf_op jit(solution)/shard_map/ppermute | solution.py:336
  21.4 1.4 %collective-permute-start.4 = (bf16[128,512]{1,0:T(8,128)(2,1)S(1)}, bf16[128,512]{1,0:T(8,128)(2,1)S(1)}, u32[]{:S(2)}, u32[]{:S(2)}) collective-permute-start(bf16[128,512]{1,0:T(8,128)(2,1)S(1)} %finish.3), channel_id=1, source_target_pairs={{0,4},{4,0},{8,12},{12,8},{16,20},{20,16},{24,28},{28,24},{1,5},{5... | collective-permute-start | bytes 393224 | tf_op jit(solution)/shard_map/ppermute | solution.py:336
  22.9 11.4 %collective-permute-start.5 = (bf16[256,512]{1,0:T(8,128)(2,1)S(1)}, bf16[256,512]{1,0:T(8,128)(2,1)S(1)}, u32[]{:S(2)}, u32[]{:S(2)}) collective-permute-start(bf16[256,512]{1,0:T(8,128)(2,1)S(1)} %pad_maximum_fusion.own_ref), channel_id=1, source_target_pairs={{0,3},{1,2},{2,1},{3,0},{4,7},{5,6},{6,5},{7,4},{8,11},{9,10},{10,... | collective-permute-start | bytes 786440 | tf_op jit(solution)/shard_map/ppermute | solution.py:345
  27.1 12.4 %collective-permute-start.9 = (bf16[256,512]{1,0:T(8,128)(2,1)S(1)}, bf16[256,512]{1,0:T(8,128)(2,1)S(1)}, u32[]{:S(2)}, u32[]{:S(2)}) collective-permute-start(bf16[256,512]{1,0:T(8,128)(2,1)S(1)} %pad_maximum_fusion.own_ref), channel_id=1, source_target_pairs={{0,1},{1,0},{2,3},{3,2},{4,5},{5,4},{6,7},{7,6},{8,9},{9,8},{10,11... | collective-permute-start | bytes 786440 | tf_op jit(solution)/shard_map/ppermute | solution.py:345
  27.1 18.8 %collective-permute-start.10 = (bf16[512,1024]{1,0:T(8,128)(2,1)}, bf16[512,1024]{1,0:T(8,128)(2,1)S(1)}, u32[]{:S(2)}, u32[]{:S(2)}) collective-permute-start(bf16[512,1024]{1,0:T(8,128)(2,1)} %collective-permute-done.6.rest_1_), channel_id=1, source_target_pairs={{0,16},{4,12},{8,24},{12,4},{16,0},{20,28},{24,8},{28,20},{1,17},{... | collective-permute-start | bytes 3145736 | tf_op jit(solution)/shard_map/ppermute | solution.py:336
  34.8 11.6 %collective-permute-start.8 = (bf16[256,512]{1,0:T(8,128)(2,1)S(1)}, bf16[256,512]{1,0:T(8,128)(2,1)S(1)}, u32[]{:S(2)}, u32[]{:S(2)}) collective-permute-start(bf16[256,512]{1,0:T(8,128)(2,1)S(1)} %collective-permute-done.5.across_ref), channel_id=1, source_target_pairs={{0,1},{1,0},{2,3},{3,2},{4,5},{5,4},{6,7},{7,6},{8,9},{9,8},{10,11... | collective-permute-start | bytes 786440 | tf_op jit(solution)/shard_map/ppermute | solution.py:345
  46.7 1.6 %collective-permute-start.11 = (bf16[128,1024]{1,0:T(8,128)(2,1)S(1)}, bf16[128,1024]{1,0:T(8,128)(2,1)S(1)}, u32[]{:S(2)}, u32[]{:S(2)}) collective-permute-start(bf16[128,1024]{1,0:T(8,128)(2,1)S(1)} %late.3), channel_id=1, source_target_pairs={{0,4},{4,0},{8,12},{12,8},{16,20},{20,16},{24,28},{28,24},{1,5},{5... | collective-permute-start | bytes 786440 | tf_op jit(solution)/shard_map/ppermute | solution.py:336

commit v26 on v25

--- a/solution.py
+++ b/solution.py
@@ -417,9 +417,8 @@
                 arrived, ends[0], entering, wide,
             )
         if bit == steps - 2:
-            bases.append(within(0))
-            sent = after(sent, bases[0])
-    bases.append(within(1))
+            bases = [within(0), within(1)]
+            sent = after(sent, tuple(bases))
     if square:
         other_near = swap(after(out_weight, (entering, sent, near)), 4, 2)
     core = me % CORES

time: 49.2 us -> 48.3 us (0.982)
  waiting for transfers between devices: 16.4 us -> 15 us
    ppermute x8, waiting for transfers between devices: 9.93 us -> 8.59 us  [swap(): return lax.ppermute(value, 'ctx', pairs)]
    ppermute x3, starting transfers between devices: 8.47 us -> 8.97 us  [trade(): lax.ppermute(value, 'tp', [(source, source ^ bits) for source in range(co...]
  transfers between devices with their start and end apart: 12 -> 12, of which waited for: 9 -> 7; matrix products, arithmetic and copies ran while one was open for 0% -> 0% of each run, Pallas kernels for 23% -> 24%
where the time goes in v26:
time: 48.3 us; the launch traced here: 48.2 us
  starting transfers between devices  20.4 us (42%)
  waiting for transfers between devices  15 us (31%)
  Pallas kernels  11.7 us (24%)
  other arithmetic  0.78 us (2%)
    pallas_call x14, Pallas kernels, call(): pl.pallas_call(kernel, out_shape=tuple((jax.ShapeDtypeStruct(*out) for ou...  11.7 us
    ppermute x8, starting transfers between devices, swap(): return lax.ppermute(value, 'ctx', pairs)  9.97 us
    ppermute x3, starting transfers between devices, trade(): lax.ppermute(value, 'tp', [(source, source ^ bits) for source in range(co...  8.97 us
    ppermute x8, waiting for transfers between devices, swap(): return lax.ppermute(value, 'ctx', pairs)  8.59 us
    ppermute x3, waiting for transfers between devices, trade(): lax.ppermute(value, 'tp', [(source, source ^ bits) for source in range(co...  6.42 us
    ppermute x1, starting transfers between devices, from_behind(): lax.ppermute(value, axis, [(source, source + steps) for source in range(l...  1.49 us
  transfers between devices with their start and end apart: 12, of which 7 were waited for; matrix products, arithmetic and copies ran while one was open for 0% of the time, Pallas kernels for 24%

profile of v26, /device:TPU:0, one launch (start us, length us, event | category | flops | bytes accessed | tf_op | source)
XLA Modules:
  0.0 48.2 jit_solution(420817590879223899)
XLA Ops:
  0.0 2.9 %collective-permute-start.6 = (bf16[512,1024]{1,0:T(8,128)(2,1)}, bf16[512,1024]{1,0:T(8,128)(2,1)}, u32[]{:S(2)}, u32[]{:S(2)}) collective-permute-start(bf16[512,1024]{1,0:T(8,128)(2,1)} %rest_0_.1), channel_id=1, source_target_pairs={{0,8},{4,20},{8,0},{12,28},{16,24},{20,4},{24,16},{28,12},{1,9},{5... | collective-permute-start | bytes 3145736 | tf_op jit(solution)/shard_map/ppermute | solution.py:336
  2.9 1.5 %tails.1 = (bf16[3,8,1024]{2,1,0:T(8,128)(2,1)S(1)}, bf16[3,1024,128]{2,1,0:T(8,128)(2,1)S(1)}, f32[3,7,1024]{2,1,0:T(8,128)S(1)}, f32[16,128]{1,0:T(8,128)S(1)}...) custom-call(bf16[3,1024,128]{2,1,0:T(8,128)(2,1)} %refs_0_.1, f32[3,7,1024]{2,1,0:T(8,128)} %refs_1_.1, f32[16,128]{1,0:T(8,128)} %bitcast.8, ...), custom_call_target="tpu_custom_call" | custom-call | flops 100000000 | bytes 1000000 | tf_op jit(solution)/shard_map/tails/pallas_call | solution.py:55
  4.5 1.5 %collective-permute-start = (bf16[3,8,1024]{2,1,0:T(8,128)(2,1)S(1)}, bf16[3,8,1024]{2,1,0:T(8,128)(2,1)S(1)}, u32[]{:S(2)}, u32[]{:S(2)}) collective-permute-start(bf16[3,8,1024]{2,1,0:T(8,128)(2,1)S(1)} %get-tuple-element.34), channel_id=1, source_target_pairs={{0,4},{4,8},{8,12},{12,16},{16,20},{20,24},{24,28},{1,5},{5,9},{9,... | collective-permute-start | bytes 147464 | tf_op jit(solution)/shard_map/ppermute | solution.py:26
  5.9 3.3 %prepare.1 = (f32[3,8,1024]{2,1,0:T(8,128)S(1)}, bf16[128,1024]{1,0:T(8,128)(2,1)S(1)}, f32[128,1024]{1,0:T(8,128)S(1)}, bf16[2048,128]{1,0:T(8,128)(2,1)S(1)}, ...) custom-call(bf16[3,1024,128]{2,1,0:T(8,128)(2,1)S(1)} %get-tuple-element.35.streams_ref, ...), custom_call_target="tpu_custom_call" | custom-call | flops 1000000000 | bytes 10000000 | tf_op jit(solution)/shard_map/prepare/pallas_call | solution.py:55
  9.3 0.6 %states.1 = (f32[16,1024]{1,0:T(8,128)S(1)}, bf16[16,1024]{1,0:T(8,128)(2,1)S(1)}, bf16[128,1024]{1,0:T(8,128)(2,1)S(1)}, f32[8,1024]{1,0:T(8,128)S(1)}) custom-call(bf16[3,8,1024]{2,1,0:T(8,128)(2,1)S(1)} %collective-permute-done.before_ref, f32[3,8,1024]{2,1,0:T(8,128)S(1)} %get-tuple-element.39.heads_ref, f32[3,7,1024]{2,1,0:T(8,128)S(1)} %get-tuple-element.36.taps_ref, ...), custom_call_target="tpu_custom_call" | custom-call | flops 100000000 | bytes 1000000 | tf_op jit(solution)/shard_map/states/pallas_call | solution.py:55
  9.9 0.6 %collective-permute-start.1 = (bf16[16,1024]{1,0:T(8,128)(2,1)S(1)}, bf16[16,1024]{1,0:T(8,128)(2,1)S(1)}, u32[]{:S(2)}, u32[]{:S(2)}) collective-permute-start(bf16[16,1024]{1,0:T(8,128)(2,1)S(1)} %get-tuple-element.42), channel_id=1, source_target_pairs={{0,4},{4,0},{8,12},{12,8},{16,20},{20,16},{24,28},{28,24},{1,5},{5... | collective-permute-start | bytes 98312 | tf_op jit(solution)/shard_map/ppermute | solution.py:336
  10.5 0.8 %inside.2.left_ref = f32[128,512]{1,0:T(8,128)S(1)} custom-call(bf16[128,1024]{1,0:T(8,128)(2,1)S(1)} %get-tuple-element.49.gated_ref, f32[1,1024]{1,0:T(1,128)S(1)} %get-tuple-element.50.skip_ref, f32[128,128]{1,0:T(8,128)S(1)} %get-tuple-element.51.response_ref), custom_call_target="tpu_custom_call" | custom-call | flops 1000000000 | bytes 10000000 | tf_op jit(solution)/shard_map/inside/pallas_call | solution.py:55
  11.4 0.0 collective-permute-done.1.arrived_ref
  11.5 3.0 %collective-permute-start.2 = (bf16[16,1024]{1,0:T(8,128)(2,1)S(1)}, bf16[16,1024]{1,0:T(8,128)(2,1)S(1)}, u32[]{:S(2)}, u32[]{:S(2)}) collective-permute-start(bf16[16,1024]{1,0:T(8,128)(2,1)S(1)} %get-tuple-element.45), channel_id=1, source_target_pairs={{0,8},{4,12},{8,0},{12,4},{16,24},{20,28},{24,16},{28,20},{1,9},{5... | collective-permute-start | bytes 98312 | tf_op jit(solution)/shard_map/ppermute | solution.py:336
  14.5 0.8 %inside.3.right_ref = f32[128,512]{1,0:T(8,128)S(1)} custom-call(bf16[128,1024]{1,0:T(8,128)(2,1)S(1)} %get-tuple-element.49.gated_ref, f32[1,1024]{1,0:T(1,128)S(1)} %get-tuple-element.50.skip_ref, f32[128,128]{1,0:T(8,128)S(1)} %get-tuple-element.51.response_ref), custom_call_target="tpu_custom_call" | custom-call | flops 1000000000 | bytes 10000000 | tf_op jit(solution)/shard_map/inside/pallas_call | solution.py:55
  15.3 1.8 %collective-permute-done.2.arrived_ref = bf16[16,1024]{1,0:T(8,128)(2,1)S(1)} collective-permute-done((bf16[16,1024]{1,0:T(8,128)(2,1)S(1)}, bf16[16,1024]{1,0:T(8,128)(2,1)S(1)}, u32[]{:S(2)}, u32[]{:S(2)}) %collective-permute-start.2) | collective-permute-done | bytes 32800 | tf_op jit(solution)/shard_map/ppermute | solution.py:336
  17.2 1.7 %collective-permute-start.3 = (bf16[16,1024]{1,0:T(8,128)(2,1)S(1)}, bf16[16,1024]{1,0:T(8,128)(2,1)S(1)}, u32[]{:S(2)}, u32[]{:S(2)}) collective-permute-start(bf16[16,1024]{1,0:T(8,128)(2,1)S(1)} %get-tuple-element.52), channel_id=1, source_target_pairs={{0,16},{4,20},{8,24},{12,28},{16,0},{20,4},{24,8},{28,12},{1,17},{... | collective-permute-start | bytes 98312 | tf_op jit(solution)/shard_map/ppermute | solution.py:336
  18.9 0.3 collective-permute-start.7
  19.3 1.9 %collective-permute-done.3.arrived_ref = bf16[16,1024]{1,0:T(8,128)(2,1)S(1)} collective-permute-done((bf16[16,1024]{1,0:T(8,128)(2,1)S(1)}, bf16[16,1024]{1,0:T(8,128)(2,1)S(1)}, u32[]{:S(2)}, u32[]{:S(2)}) %collective-permute-start.3) | collective-permute-done | bytes 32800 | tf_op jit(solution)/shard_map/ppermute | solution.py:336
  21.2 0.2 finish.3
  21.4 0.1 collective-permute-start.4
  21.5 0.2 finish.2
  21.8 1.1 %collective-permute-done.4 = bf16[128,512]{1,0:T(8,128)(2,1)S(1)} collective-permute-done((bf16[128,512]{1,0:T(8,128)(2,1)S(1)}, bf16[128,512]{1,0:T(8,128)(2,1)S(1)}, u32[]{:S(2)}, u32[]{:S(2)}) %collective-permute-start.4) | collective-permute-done | bytes 131104 | tf_op jit(solution)/shard_map/ppermute | solution.py:336
  22.9 4.2 %collective-permute-start.5 = (bf16[256,512]{1,0:T(8,128)(2,1)S(1)}, bf16[256,512]{1,0:T(8,128)(2,1)S(1)}, u32[]{:S(2)}, u32[]{:S(2)}) collective-permute-start(bf16[256,512]{1,0:T(8,128)(2,1)S(1)} %pad_maximum_fusion.own_ref), channel_id=1, source_target_pairs={{0,3},{1,2},{2,1},{3,0},{4,7},{5,6},{6,5},{7,4},{8,11},{9,10},{10,... | collective-permute-start | bytes 786440 | tf_op jit(solution)/shard_map/ppermute | solution.py:345
  27.1 1.1 %collective-permute-start.10 = (bf16[512,1024]{1,0:T(8,128)(2,1)}, bf16[512,1024]{1,0:T(8,128)(2,1)S(1)}, u32[]{:S(2)}, u32[]{:S(2)}) collective-permute-start(bf16[512,1024]{1,0:T(8,128)(2,1)} %collective-permute-done.6.rest_1_), channel_id=1, source_target_pairs={{0,16},{4,12},{8,24},{12,4},{16,0},{20,28},{24,8},{28,20},{1,17},{... | collective-permute-start | bytes 3145736 | tf_op jit(solution)/shard_map/ppermute | solution.py:336
  28.2 0.1 stack.23.at_ref
  28.3 5.9 %collective-permute-done.5.across_ref = bf16[256,512]{1,0:T(8,128)(2,1)S(1)} collective-permute-done((bf16[256,512]{1,0:T(8,128)(2,1)S(1)}, bf16[256,512]{1,0:T(8,128)(2,1)S(1)}, u32[]{:S(2)}, u32[]{:S(2)}) %collective-permute-start.5) | collective-permute-done | bytes 262176 | tf_op jit(solution)/shard_map/ppermute | solution.py:345
  34.3 4.8 %collective-permute-start.8 = (bf16[256,512]{1,0:T(8,128)(2,1)S(1)}, bf16[256,512]{1,0:T(8,128)(2,1)S(1)}, u32[]{:S(2)}, u32[]{:S(2)}) collective-permute-start(bf16[256,512]{1,0:T(8,128)(2,1)S(1)} %collective-permute-done.5.across_ref), channel_id=1, source_target_pairs={{0,1},{1,0},{2,3},{3,2},{4,5},{5,4},{6,7},{7,6},{8,9},{9,8},{10,11... | collective-permute-start | bytes 786440 | tf_op jit(solution)/shard_map/ppermute | solution.py:345
  39.0 0.5 collective-permute-done.9.beside_ref
  39.5 2.9 %early.1 = (f32[256,1024]{1,0:T(8,128)S(1)}, bf16[512,1024]{1,0:T(8,128)(2,1)S(1)}, bf16[256,512]{1,0:T(8,128)(2,1)S(1)}) custom-call(s32[5]{0:T(128)S(1)} %stack.23.at_ref, bf16[256,512]{1,0:T(8,128)(2,1)S(1)} %pad_maximum_fusion.own_ref, bf16[256,512]{1,0:T(8,128)(2,1)S(1)} %collective-permute-done.9.beside_ref, ...), custom_call_target="tpu_custom_call" | custom-call | flops 10000000000 | bytes 100000000 | tf_op jit(solution)/shard_map/early/pallas_call | solution.py:55
  42.4 2.6 %collective-permute-done.10.weight_ref = bf16[512,1024]{1,0:T(8,128)(2,1)S(1)} collective-permute-done((bf16[512,1024]{1,0:T(8,128)(2,1)}, bf16[512,1024]{1,0:T(8,128)(2,1)S(1)}, u32[]{:S(2)}, u32[]{:S(2)}) %collective-permute-start.10) | collective-permute-done | bytes 1048608 | tf_op jit(solution)/shard_map/ppermute | solution.py:336
  45.0 0.5 joined.1.total_ref
  45.5 0.3 late.3
  45.8 0.1 collective-permute-start.11
  45.9 0.3 late.2
  46.2 1.2 %collective-permute-done.11 = bf16[128,1024]{1,0:T(8,128)(2,1)S(1)} collective-permute-done((bf16[128,1024]{1,0:T(8,128)(2,1)S(1)}, bf16[128,1024]{1,0:T(8,128)(2,1)S(1)}, u32[]{:S(2)}, u32[]{:S(2)}) %collective-permute-start.11) | collective-permute-done | bytes 262176 | tf_op jit(solution)/shard_map/ppermute | solution.py:336
  47.4 0.8 %add_convert_fusion = bf16[128,1024]{1,0:T(8,128)(2,1)} fusion(f32[128,1024]{1,0:T(8,128)S(1)} %late.2, bf16[128,1024]{1,0:T(8,128)(2,1)S(1)} %collective-permute-done.11), kind=kLoop, calls=%fused_computation | loop fusion | flops 393216 | bytes 1048576 | tf_op jit(solution)/shard_map/convert_element_type | solution.py:501
  (12 shorter events, 0.1 us)
Async XLA Ops:
  0.0 18.9 %collective-permute-start.6 = (bf16[512,1024]{1,0:T(8,128)(2,1)}, bf16[512,1024]{1,0:T(8,128)(2,1)}, u32[]{:S(2)}, u32[]{:S(2)}) collective-permute-start(bf16[512,1024]{1,0:T(8,128)(2,1)} %rest_0_.1), channel_id=1, source_target_pairs={{0,8},{4,20},{8,0},{12,28},{16,24},{20,4},{24,16},{28,12},{1,9},{5... | collective-permute-start | bytes 3145736 | tf_op jit(solution)/shard_map/ppermute | solution.py:336
  4.5 4.8 %collective-permute-start = (bf16[3,8,1024]{2,1,0:T(8,128)(2,1)S(1)}, bf16[3,8,1024]{2,1,0:T(8,128)(2,1)S(1)}, u32[]{:S(2)}, u32[]{:S(2)}) collective-permute-start(bf16[3,8,1024]{2,1,0:T(8,128)(2,1)S(1)} %get-tuple-element.34), channel_id=1, source_target_pairs={{0,4},{4,8},{8,12},{12,16},{16,20},{20,24},{24,28},{1,5},{5,9},{9,... | collective-permute-start | bytes 147464 | tf_op jit(solution)/shard_map/ppermute | solution.py:26
  9.9 1.5 %collective-permute-start.1 = (bf16[16,1024]{1,0:T(8,128)(2,1)S(1)}, bf16[16,1024]{1,0:T(8,128)(2,1)S(1)}, u32[]{:S(2)}, u32[]{:S(2)}) collective-permute-start(bf16[16,1024]{1,0:T(8,128)(2,1)S(1)} %get-tuple-element.42), channel_id=1, source_target_pairs={{0,4},{4,0},{8,12},{12,8},{16,20},{20,16},{24,28},{28,24},{1,5},{5... | collective-permute-start | bytes 98312 | tf_op jit(solution)/shard_map/ppermute | solution.py:336
  11.5 7.5 %copy-start = (bf16[512,1024]{1,0:T(8,128)(2,1)S(1)}, bf16[512,1024]{1,0:T(8,128)(2,1)}, u32[]{:S(2)}) copy-start(bf16[512,1024]{1,0:T(8,128)(2,1)} %rest_0_.1) | copy-start | bytes 3145732
  11.5 5.7 %collective-permute-start.2 = (bf16[16,1024]{1,0:T(8,128)(2,1)S(1)}, bf16[16,1024]{1,0:T(8,128)(2,1)S(1)}, u32[]{:S(2)}, u32[]{:S(2)}) collective-permute-start(bf16[16,1024]{1,0:T(8,128)(2,1)S(1)} %get-tuple-element.45), channel_id=1, source_target_pairs={{0,8},{4,12},{8,0},{12,4},{16,24},{20,28},{24,16},{28,20},{1,9},{5... | collective-permute-start | bytes 98312 | tf_op jit(solution)/shard_map/ppermute | solution.py:336
  17.2 4.0 %collective-permute-start.3 = (bf16[16,1024]{1,0:T(8,128)(2,1)S(1)}, bf16[16,1024]{1,0:T(8,128)(2,1)S(1)}, u32[]{:S(2)}, u32[]{:S(2)}) collective-permute-start(bf16[16,1024]{1,0:T(8,128)(2,1)S(1)} %get-tuple-element.52), channel_id=1, source_target_pairs={{0,16},{4,20},{8,24},{12,28},{16,0},{20,4},{24,8},{28,12},{1,17},{... | collective-permute-start | bytes 98312 | tf_op jit(solution)/shard_map/ppermute | solution.py:336
  18.9 15.3 %collective-permute-start.7 = (bf16[512,1024]{1,0:T(8,128)(2,1)S(1)}, bf16[512,1024]{1,0:T(8,128)(2,1)}, u32[]{:S(2)}, u32[]{:S(2)}) collective-permute-start(bf16[512,1024]{1,0:T(8,128)(2,1)S(1)} %copy-done), channel_id=1, source_target_pairs={{0,16},{4,12},{8,24},{12,4},{16,0},{20,28},{24,8},{28,20},{1,17},{... | collective-permute-start | bytes 3145736 | tf_op jit(solution)/shard_map/ppermute | solution.py:336
  21.4 1.4 %collective-permute-start.4 = (bf16[128,512]{1,0:T(8,128)(2,1)S(1)}, bf16[128,512]{1,0:T(8,128)(2,1)S(1)}, u32[]{:S(2)}, u32[]{:S(2)}) collective-permute-start(bf16[128,512]{1,0:T(8,128)(2,1)S(1)} %finish.3), channel_id=1, source_target_pairs={{0,4},{4,0},{8,12},{12,8},{16,20},{20,16},{24,28},{28,24},{1,5},{5... | collective-permute-start | bytes 393224 | tf_op jit(solution)/shard_map/ppermute | solution.py:336
  22.9 11.4 %collective-permute-start.5 = (bf16[256,512]{1,0:T(8,128)(2,1)S(1)}, bf16[256,512]{1,0:T(8,128)(2,1)S(1)}, u32[]{:S(2)}, u32[]{:S(2)}) collective-permute-start(bf16[256,512]{1,0:T(8,128)(2,1)S(1)} %pad_maximum_fusion.own_ref), channel_id=1, source_target_pairs={{0,3},{1,2},{2,1},{3,0},{4,7},{5,6},{6,5},{7,4},{8,11},{9,10},{10,... | collective-permute-start | bytes 786440 | tf_op jit(solution)/shard_map/ppermute | solution.py:345
  27.1 12.4 %collective-permute-start.9 = (bf16[256,512]{1,0:T(8,128)(2,1)S(1)}, bf16[256,512]{1,0:T(8,128)(2,1)S(1)}, u32[]{:S(2)}, u32[]{:S(2)}) collective-permute-start(bf16[256,512]{1,0:T(8,128)(2,1)S(1)} %pad_maximum_fusion.own_ref), channel_id=1, source_target_pairs={{0,1},{1,0},{2,3},{3,2},{4,5},{5,4},{6,7},{7,6},{8,9},{9,8},{10,11... | collective-permute-start | bytes 786440 | tf_op jit(solution)/shard_map/ppermute | solution.py:345
  27.1 17.9 %collective-permute-start.10 = (bf16[512,1024]{1,0:T(8,128)(2,1)}, bf16[512,1024]{1,0:T(8,128)(2,1)S(1)}, u32[]{:S(2)}, u32[]{:S(2)}) collective-permute-start(bf16[512,1024]{1,0:T(8,128)(2,1)} %collective-permute-done.6.rest_1_), channel_id=1, source_target_pairs={{0,16},{4,12},{8,24},{12,4},{16,0},{20,28},{24,8},{28,20},{1,17},{... | collective-permute-start | bytes 3145736 | tf_op jit(solution)/shard_map/ppermute | solution.py:336
  34.3 11.2 %collective-permute-start.8 = (bf16[256,512]{1,0:T(8,128)(2,1)S(1)}, bf16[256,512]{1,0:T(8,128)(2,1)S(1)}, u32[]{:S(2)}, u32[]{:S(2)}) collective-permute-start(bf16[256,512]{1,0:T(8,128)(2,1)S(1)} %collective-permute-done.5.across_ref), channel_id=1, source_target_pairs={{0,1},{1,0},{2,3},{3,2},{4,5},{5,4},{6,7},{7,6},{8,9},{9,8},{10,11... | collective-permute-start | bytes 786440 | tf_op jit(solution)/shard_map/ppermute | solution.py:345
  45.8 1.6 %collective-permute-start.11 = (bf16[128,1024]{1,0:T(8,128)(2,1)S(1)}, bf16[128,1024]{1,0:T(8,128)(2,1)S(1)}, u32[]{:S(2)}, u32[]{:S(2)}) collective-permute-start(bf16[128,1024]{1,0:T(8,128)(2,1)S(1)} %late.3), channel_id=1, source_target_pairs={{0,4},{4,0},{8,12},{12,8},{16,20},{20,16},{24,28},{28,24},{1,5},{5... | collective-permute-start | bytes 786440 | tf_op jit(solution)/shard_map/ppermute | solution.py:336

commit v27 on v26

--- a/solution.py
+++ b/solution.py
@@ -312,10 +312,6 @@
         pl.when(at_ref[1 + at] == last)(fetch.wait)
 
 
-def joined_kernel(total_ref, block_ref, weight_ref, out_ref):
-    out_ref[...] = total_ref[...] + dot(block_ref[...], weight_ref[...])
-
-
 def keep_kernel(square, rows_ref, weight_ref, last_ref, sem):
     del rows_ref
     chip = lax.axis_index("ctx") // CORES if square else 0
@@ -325,9 +321,10 @@
     pl.when(latest)(copy.wait)
 
 
-def late_kernel(first, beyond_ref, total_ref, rows_ref, out_ref):
+def late_kernel(first, beyond_ref, total_ref, rows_ref, block_ref, weight_ref, out_ref):
     tokens = pl.ds(first, out_ref.shape[0])
-    out_ref[...] = (total_ref[tokens, :] + dot(beyond_ref[tokens, :], rows_ref[...])).astype(out_ref.dtype)
+    total = total_ref[tokens, :] + dot(block_ref[tokens, :], weight_ref[...])
+    out_ref[...] = (total + dot(beyond_ref[tokens, :], rows_ref[...])).astype(out_ref.dtype)
 
 
 def swap(value, *bits):
@@ -472,9 +469,6 @@
         ],
         flops=10**10,
     )
-    (total,) = call(
-        joined_kernel, [((CORES * length, features), F32)], "joined", total, last_block, latest, flops=0
-    )
     anywhere = [pl.BlockSpec(memory_space=pl.ANY)]
     (last_rows,) = call(
         functools.partial(keep_kernel, square),
@@ -493,7 +487,7 @@
             functools.partial(late_kernel, side * length),
             [((length, features), kind)],
             "late",
-            beyond, total, last_rows,
+            beyond, total, last_rows, last_block, latest,
             flops=0,
         )
     other, mine = sides

time: 48.3 us -> 48 us (level)
    pallas_call x14 -> x13, Pallas kernels: 11.7 us -> 11.5 us  [call(): pl.pallas_call(kernel, out_shape=tuple((jax.ShapeDtypeStruct(*out) for ou...]
  transfers between devices with their start and end apart: 12 -> 12, of which waited for: 7 -> 7; matrix products, arithmetic and copies ran while one was open for 0% -> 0% of each run, Pallas kernels for 24% -> 23%
where the time goes in v27:
time: 48 us; the launch traced here: 47.8 us
  starting transfers between devices  20.4 us (42%)
  waiting for transfers between devices  14.9 us (31%)
  Pallas kernels  11.5 us (24%)
  other arithmetic  0.78 us (2%)
    pallas_call x13, Pallas kernels, call(): pl.pallas_call(kernel, out_shape=tuple((jax.ShapeDtypeStruct(*out) for ou...  11.5 us
    ppermute x8, starting transfers between devices, swap(): return lax.ppermute(value, 'ctx', pairs)  9.97 us
    ppermute x3, starting transfers between devices, trade(): lax.ppermute(value, 'tp', [(source, source ^ bits) for source in range(co...  8.97 us
    ppermute x8, waiting for transfers between devices, swap(): return lax.ppermute(value, 'ctx', pairs)  8.46 us
    ppermute x3, waiting for transfers between devices, trade(): lax.ppermute(value, 'tp', [(source, source ^ bits) for source in range(co...  6.44 us
    ppermute x1, starting transfers between devices, from_behind(): lax.ppermute(value, axis, [(source, source + steps) for source in range(l...  1.49 us
  transfers between devices with their start and end apart: 12, of which 7 were waited for; matrix products, arithmetic and copies ran while one was open for 0% of the time, Pallas kernels for 23%

profile of v27, /device:TPU:0, one launch (start us, length us, event | category | flops | bytes accessed | tf_op | source)
XLA Modules:
  0.0 47.8 jit_solution(8335774040740093374)
XLA Ops:
  0.0 2.9 %collective-permute-start.6 = (bf16[512,1024]{1,0:T(8,128)(2,1)}, bf16[512,1024]{1,0:T(8,128)(2,1)}, u32[]{:S(2)}, u32[]{:S(2)}) collective-permute-start(bf16[512,1024]{1,0:T(8,128)(2,1)} %rest_0_.1), channel_id=1, source_target_pairs={{0,8},{4,20},{8,0},{12,28},{16,24},{20,4},{24,16},{28,12},{1,9},{5... | collective-permute-start | bytes 3145736 | tf_op jit(solution)/shard_map/ppermute | solution.py:333
  2.9 1.5 %tails.1 = (bf16[3,8,1024]{2,1,0:T(8,128)(2,1)S(1)}, bf16[3,1024,128]{2,1,0:T(8,128)(2,1)S(1)}, f32[3,7,1024]{2,1,0:T(8,128)S(1)}, f32[16,128]{1,0:T(8,128)S(1)}...) custom-call(bf16[3,1024,128]{2,1,0:T(8,128)(2,1)} %refs_0_.1, f32[3,7,1024]{2,1,0:T(8,128)} %refs_1_.1, f32[16,128]{1,0:T(8,128)} %bitcast.8, ...), custom_call_target="tpu_custom_call" | custom-call | flops 100000000 | bytes 1000000 | tf_op jit(solution)/shard_map/tails/pallas_call | solution.py:55
  4.5 1.5 %collective-permute-start = (bf16[3,8,1024]{2,1,0:T(8,128)(2,1)S(1)}, bf16[3,8,1024]{2,1,0:T(8,128)(2,1)S(1)}, u32[]{:S(2)}, u32[]{:S(2)}) collective-permute-start(bf16[3,8,1024]{2,1,0:T(8,128)(2,1)S(1)} %get-tuple-element.34), channel_id=1, source_target_pairs={{0,4},{4,8},{8,12},{12,16},{16,20},{20,24},{24,28},{1,5},{5,9},{9,... | collective-permute-start | bytes 147464 | tf_op jit(solution)/shard_map/ppermute | solution.py:26
  5.9 3.3 %prepare.1 = (f32[3,8,1024]{2,1,0:T(8,128)S(1)}, bf16[128,1024]{1,0:T(8,128)(2,1)S(1)}, f32[128,1024]{1,0:T(8,128)S(1)}, bf16[2048,128]{1,0:T(8,128)(2,1)S(1)}, ...) custom-call(bf16[3,1024,128]{2,1,0:T(8,128)(2,1)S(1)} %get-tuple-element.35.streams_ref, ...), custom_call_target="tpu_custom_call" | custom-call | flops 1000000000 | bytes 10000000 | tf_op jit(solution)/shard_map/prepare/pallas_call | solution.py:55
  9.3 0.6 %states.1 = (f32[16,1024]{1,0:T(8,128)S(1)}, bf16[16,1024]{1,0:T(8,128)(2,1)S(1)}, bf16[128,1024]{1,0:T(8,128)(2,1)S(1)}, f32[8,1024]{1,0:T(8,128)S(1)}) custom-call(bf16[3,8,1024]{2,1,0:T(8,128)(2,1)S(1)} %collective-permute-done.before_ref, f32[3,8,1024]{2,1,0:T(8,128)S(1)} %get-tuple-element.39.heads_ref, f32[3,7,1024]{2,1,0:T(8,128)S(1)} %get-tuple-element.36.taps_ref, ...), custom_call_target="tpu_custom_call" | custom-call | flops 100000000 | bytes 1000000 | tf_op jit(solution)/shard_map/states/pallas_call | solution.py:55
  9.9 0.6 %collective-permute-start.1 = (bf16[16,1024]{1,0:T(8,128)(2,1)S(1)}, bf16[16,1024]{1,0:T(8,128)(2,1)S(1)}, u32[]{:S(2)}, u32[]{:S(2)}) collective-permute-start(bf16[16,1024]{1,0:T(8,128)(2,1)S(1)} %get-tuple-element.42), channel_id=1, source_target_pairs={{0,4},{4,0},{8,12},{12,8},{16,20},{20,16},{24,28},{28,24},{1,5},{5... | collective-permute-start | bytes 98312 | tf_op jit(solution)/shard_map/ppermute | solution.py:333
  10.5 0.8 %inside.2.left_ref = f32[128,512]{1,0:T(8,128)S(1)} custom-call(bf16[128,1024]{1,0:T(8,128)(2,1)S(1)} %get-tuple-element.49.gated_ref, f32[1,1024]{1,0:T(1,128)S(1)} %get-tuple-element.50.skip_ref, f32[128,128]{1,0:T(8,128)S(1)} %get-tuple-element.51.response_ref), custom_call_target="tpu_custom_call" | custom-call | flops 1000000000 | bytes 10000000 | tf_op jit(solution)/shard_map/inside/pallas_call | solution.py:55
  11.4 0.0 collective-permute-done.1.arrived_ref
  11.5 3.0 %collective-permute-start.2 = (bf16[16,1024]{1,0:T(8,128)(2,1)S(1)}, bf16[16,1024]{1,0:T(8,128)(2,1)S(1)}, u32[]{:S(2)}, u32[]{:S(2)}) collective-permute-start(bf16[16,1024]{1,0:T(8,128)(2,1)S(1)} %get-tuple-element.45), channel_id=1, source_target_pairs={{0,8},{4,12},{8,0},{12,4},{16,24},{20,28},{24,16},{28,20},{1,9},{5... | collective-permute-start | bytes 98312 | tf_op jit(solution)/shard_map/ppermute | solution.py:333
  14.5 0.8 %inside.3.right_ref = f32[128,512]{1,0:T(8,128)S(1)} custom-call(bf16[128,1024]{1,0:T(8,128)(2,1)S(1)} %get-tuple-element.49.gated_ref, f32[1,1024]{1,0:T(1,128)S(1)} %get-tuple-element.50.skip_ref, f32[128,128]{1,0:T(8,128)S(1)} %get-tuple-element.51.response_ref), custom_call_target="tpu_custom_call" | custom-call | flops 1000000000 | bytes 10000000 | tf_op jit(solution)/shard_map/inside/pallas_call | solution.py:55
  15.3 1.8 %collective-permute-done.2.arrived_ref = bf16[16,1024]{1,0:T(8,128)(2,1)S(1)} collective-permute-done((bf16[16,1024]{1,0:T(8,128)(2,1)S(1)}, bf16[16,1024]{1,0:T(8,128)(2,1)S(1)}, u32[]{:S(2)}, u32[]{:S(2)}) %collective-permute-start.2) | collective-permute-done | bytes 32800 | tf_op jit(solution)/shard_map/ppermute | solution.py:333
  17.2 1.7 %collective-permute-start.3 = (bf16[16,1024]{1,0:T(8,128)(2,1)S(1)}, bf16[16,1024]{1,0:T(8,128)(2,1)S(1)}, u32[]{:S(2)}, u32[]{:S(2)}) collective-permute-start(bf16[16,1024]{1,0:T(8,128)(2,1)S(1)} %get-tuple-element.52), channel_id=1, source_target_pairs={{0,16},{4,20},{8,24},{12,28},{16,0},{20,4},{24,8},{28,12},{1,17},{... | collective-permute-start | bytes 98312 | tf_op jit(solution)/shard_map/ppermute | solution.py:333
  18.9 0.3 collective-permute-start.7
  19.3 1.9 %collective-permute-done.3.arrived_ref = bf16[16,1024]{1,0:T(8,128)(2,1)S(1)} collective-permute-done((bf16[16,1024]{1,0:T(8,128)(2,1)S(1)}, bf16[16,1024]{1,0:T(8,128)(2,1)S(1)}, u32[]{:S(2)}, u32[]{:S(2)}) %collective-permute-start.3) | collective-permute-done | bytes 32800 | tf_op jit(solution)/shard_map/ppermute | solution.py:333
  21.2 0.2 finish.3
  21.4 0.1 collective-permute-start.4
  21.5 0.2 finish.2
  21.8 1.1 %collective-permute-done.4 = bf16[128,512]{1,0:T(8,128)(2,1)S(1)} collective-permute-done((bf16[128,512]{1,0:T(8,128)(2,1)S(1)}, bf16[128,512]{1,0:T(8,128)(2,1)S(1)}, u32[]{:S(2)}, u32[]{:S(2)}) %collective-permute-start.4) | collective-permute-done | bytes 131104 | tf_op jit(solution)/shard_map/ppermute | solution.py:333
  22.9 4.2 %collective-permute-start.5 = (bf16[256,512]{1,0:T(8,128)(2,1)S(1)}, bf16[256,512]{1,0:T(8,128)(2,1)S(1)}, u32[]{:S(2)}, u32[]{:S(2)}) collective-permute-start(bf16[256,512]{1,0:T(8,128)(2,1)S(1)} %pad_maximum_fusion.own_ref), channel_id=1, source_target_pairs={{0,3},{1,2},{2,1},{3,0},{4,7},{5,6},{6,5},{7,4},{8,11},{9,10},{10,... | collective-permute-start | bytes 786440 | tf_op jit(solution)/shard_map/ppermute | solution.py:342
  27.1 1.1 %collective-permute-start.10 = (bf16[512,1024]{1,0:T(8,128)(2,1)}, bf16[512,1024]{1,0:T(8,128)(2,1)S(1)}, u32[]{:S(2)}, u32[]{:S(2)}) collective-permute-start(bf16[512,1024]{1,0:T(8,128)(2,1)} %collective-permute-done.6.rest_1_), channel_id=1, source_target_pairs={{0,16},{4,12},{8,24},{12,4},{16,0},{20,28},{24,8},{28,20},{1,17},{... | collective-permute-start | bytes 3145736 | tf_op jit(solution)/shard_map/ppermute | solution.py:333
  28.2 0.1 stack.23.at_ref
  28.3 5.9 %collective-permute-done.5.across_ref = bf16[256,512]{1,0:T(8,128)(2,1)S(1)} collective-permute-done((bf16[256,512]{1,0:T(8,128)(2,1)S(1)}, bf16[256,512]{1,0:T(8,128)(2,1)S(1)}, u32[]{:S(2)}, u32[]{:S(2)}) %collective-permute-start.5) | collective-permute-done | bytes 262176 | tf_op jit(solution)/shard_map/ppermute | solution.py:342
  34.3 4.8 %collective-permute-start.8 = (bf16[256,512]{1,0:T(8,128)(2,1)S(1)}, bf16[256,512]{1,0:T(8,128)(2,1)S(1)}, u32[]{:S(2)}, u32[]{:S(2)}) collective-permute-start(bf16[256,512]{1,0:T(8,128)(2,1)S(1)} %collective-permute-done.5.across_ref), channel_id=1, source_target_pairs={{0,1},{1,0},{2,3},{3,2},{4,5},{5,4},{6,7},{7,6},{8,9},{9,8},{10,11... | collective-permute-start | bytes 786440 | tf_op jit(solution)/shard_map/ppermute | solution.py:342
  39.0 0.5 collective-permute-done.9.beside_ref
  39.5 2.9 %early.1 = (f32[256,1024]{1,0:T(8,128)S(1)}, bf16[512,1024]{1,0:T(8,128)(2,1)S(1)}, bf16[256,512]{1,0:T(8,128)(2,1)S(1)}) custom-call(s32[5]{0:T(128)S(1)} %stack.23.at_ref, bf16[256,512]{1,0:T(8,128)(2,1)S(1)} %pad_maximum_fusion.own_ref, bf16[256,512]{1,0:T(8,128)(2,1)S(1)} %collective-permute-done.9.beside_ref, ...), custom_call_target="tpu_custom_call" | custom-call | flops 10000000000 | bytes 100000000 | tf_op jit(solution)/shard_map/early/pallas_call | solution.py:55
  42.4 2.6 %collective-permute-done.10.weight_ref = bf16[512,1024]{1,0:T(8,128)(2,1)S(1)} collective-permute-done((bf16[512,1024]{1,0:T(8,128)(2,1)}, bf16[512,1024]{1,0:T(8,128)(2,1)S(1)}, u32[]{:S(2)}, u32[]{:S(2)}) %collective-permute-start.10) | collective-permute-done | bytes 1048608 | tf_op jit(solution)/shard_map/ppermute | solution.py:333
  45.0 0.0 collective-permute-done.8.beyond_ref
  45.0 0.4 late.3
  45.5 0.1 collective-permute-start.11
  45.5 0.4 late.2
  46.0 1.1 %collective-permute-done.11 = bf16[128,1024]{1,0:T(8,128)(2,1)S(1)} collective-permute-done((bf16[128,1024]{1,0:T(8,128)(2,1)S(1)}, bf16[128,1024]{1,0:T(8,128)(2,1)S(1)}, u32[]{:S(2)}, u32[]{:S(2)}) %collective-permute-start.11) | collective-permute-done | bytes 262176 | tf_op jit(solution)/shard_map/ppermute | solution.py:333
  47.1 0.8 %add_convert_fusion = bf16[128,1024]{1,0:T(8,128)(2,1)} fusion(f32[128,1024]{1,0:T(8,128)S(1)} %late.2, bf16[128,1024]{1,0:T(8,128)(2,1)S(1)} %collective-permute-done.11), kind=kLoop, calls=%fused_computation | loop fusion | flops 393216 | bytes 1048576 | tf_op jit(solution)/shard_map/convert_element_type | solution.py:495
  (11 shorter events, 0.1 us)
Async XLA Ops:
  0.0 18.9 %collective-permute-start.6 = (bf16[512,1024]{1,0:T(8,128)(2,1)}, bf16[512,1024]{1,0:T(8,128)(2,1)}, u32[]{:S(2)}, u32[]{:S(2)}) collective-permute-start(bf16[512,1024]{1,0:T(8,128)(2,1)} %rest_0_.1), channel_id=1, source_target_pairs={{0,8},{4,20},{8,0},{12,28},{16,24},{20,4},{24,16},{28,12},{1,9},{5... | collective-permute-start | bytes 3145736 | tf_op jit(solution)/shard_map/ppermute | solution.py:333
  4.5 4.8 %collective-permute-start = (bf16[3,8,1024]{2,1,0:T(8,128)(2,1)S(1)}, bf16[3,8,1024]{2,1,0:T(8,128)(2,1)S(1)}, u32[]{:S(2)}, u32[]{:S(2)}) collective-permute-start(bf16[3,8,1024]{2,1,0:T(8,128)(2,1)S(1)} %get-tuple-element.34), channel_id=1, source_target_pairs={{0,4},{4,8},{8,12},{12,16},{16,20},{20,24},{24,28},{1,5},{5,9},{9,... | collective-permute-start | bytes 147464 | tf_op jit(solution)/shard_map/ppermute | solution.py:26
  9.9 1.5 %collective-permute-start.1 = (bf16[16,1024]{1,0:T(8,128)(2,1)S(1)}, bf16[16,1024]{1,0:T(8,128)(2,1)S(1)}, u32[]{:S(2)}, u32[]{:S(2)}) collective-permute-start(bf16[16,1024]{1,0:T(8,128)(2,1)S(1)} %get-tuple-element.42), channel_id=1, source_target_pairs={{0,4},{4,0},{8,12},{12,8},{16,20},{20,16},{24,28},{28,24},{1,5},{5... | collective-permute-start | bytes 98312 | tf_op jit(solution)/shard_map/ppermute | solution.py:333
  11.5 7.5 %copy-start = (bf16[512,1024]{1,0:T(8,128)(2,1)S(1)}, bf16[512,1024]{1,0:T(8,128)(2,1)}, u32[]{:S(2)}) copy-start(bf16[512,1024]{1,0:T(8,128)(2,1)} %rest_0_.1) | copy-start | bytes 3145732
  11.5 5.7 %collective-permute-start.2 = (bf16[16,1024]{1,0:T(8,128)(2,1)S(1)}, bf16[16,1024]{1,0:T(8,128)(2,1)S(1)}, u32[]{:S(2)}, u32[]{:S(2)}) collective-permute-start(bf16[16,1024]{1,0:T(8,128)(2,1)S(1)} %get-tuple-element.45), channel_id=1, source_target_pairs={{0,8},{4,12},{8,0},{12,4},{16,24},{20,28},{24,16},{28,20},{1,9},{5... | collective-permute-start | bytes 98312 | tf_op jit(solution)/shard_map/ppermute | solution.py:333
  17.2 4.0 %collective-permute-start.3 = (bf16[16,1024]{1,0:T(8,128)(2,1)S(1)}, bf16[16,1024]{1,0:T(8,128)(2,1)S(1)}, u32[]{:S(2)}, u32[]{:S(2)}) collective-permute-start(bf16[16,1024]{1,0:T(8,128)(2,1)S(1)} %get-tuple-element.52), channel_id=1, source_target_pairs={{0,16},{4,20},{8,24},{12,28},{16,0},{20,4},{24,8},{28,12},{1,17},{... | collective-permute-start | bytes 98312 | tf_op jit(solution)/shard_map/ppermute | solution.py:333
  18.9 15.3 %collective-permute-start.7 = (bf16[512,1024]{1,0:T(8,128)(2,1)S(1)}, bf16[512,1024]{1,0:T(8,128)(2,1)}, u32[]{:S(2)}, u32[]{:S(2)}) collective-permute-start(bf16[512,1024]{1,0:T(8,128)(2,1)S(1)} %copy-done), channel_id=1, source_target_pairs={{0,16},{4,12},{8,24},{12,4},{16,0},{20,28},{24,8},{28,20},{1,17},{... | collective-permute-start | bytes 3145736 | tf_op jit(solution)/shard_map/ppermute | solution.py:333
  21.4 1.4 %collective-permute-start.4 = (bf16[128,512]{1,0:T(8,128)(2,1)S(1)}, bf16[128,512]{1,0:T(8,128)(2,1)S(1)}, u32[]{:S(2)}, u32[]{:S(2)}) collective-permute-start(bf16[128,512]{1,0:T(8,128)(2,1)S(1)} %finish.3), channel_id=1, source_target_pairs={{0,4},{4,0},{8,12},{12,8},{16,20},{20,16},{24,28},{28,24},{1,5},{5... | collective-permute-start | bytes 393224 | tf_op jit(solution)/shard_map/ppermute | solution.py:333
  22.9 11.4 %collective-permute-start.5 = (bf16[256,512]{1,0:T(8,128)(2,1)S(1)}, bf16[256,512]{1,0:T(8,128)(2,1)S(1)}, u32[]{:S(2)}, u32[]{:S(2)}) collective-permute-start(bf16[256,512]{1,0:T(8,128)(2,1)S(1)} %pad_maximum_fusion.own_ref), channel_id=1, source_target_pairs={{0,3},{1,2},{2,1},{3,0},{4,7},{5,6},{6,5},{7,4},{8,11},{9,10},{10,... | collective-permute-start | bytes 786440 | tf_op jit(solution)/shard_map/ppermute | solution.py:342
  27.1 12.4 %collective-permute-start.9 = (bf16[256,512]{1,0:T(8,128)(2,1)S(1)}, bf16[256,512]{1,0:T(8,128)(2,1)S(1)}, u32[]{:S(2)}, u32[]{:S(2)}) collective-permute-start(bf16[256,512]{1,0:T(8,128)(2,1)S(1)} %pad_maximum_fusion.own_ref), channel_id=1, source_target_pairs={{0,1},{1,0},{2,3},{3,2},{4,5},{5,4},{6,7},{7,6},{8,9},{9,8},{10,11... | collective-permute-start | bytes 786440 | tf_op jit(solution)/shard_map/ppermute | solution.py:342
  27.1 17.9 %collective-permute-start.10 = (bf16[512,1024]{1,0:T(8,128)(2,1)}, bf16[512,1024]{1,0:T(8,128)(2,1)S(1)}, u32[]{:S(2)}, u32[]{:S(2)}) collective-permute-start(bf16[512,1024]{1,0:T(8,128)(2,1)} %collective-permute-done.6.rest_1_), channel_id=1, source_target_pairs={{0,16},{4,12},{8,24},{12,4},{16,0},{20,28},{24,8},{28,20},{1,17},{... | collective-permute-start | bytes 3145736 | tf_op jit(solution)/shard_map/ppermute | solution.py:333
  34.3 10.8 %collective-permute-start.8 = (bf16[256,512]{1,0:T(8,128)(2,1)S(1)}, bf16[256,512]{1,0:T(8,128)(2,1)S(1)}, u32[]{:S(2)}, u32[]{:S(2)}) collective-permute-start(bf16[256,512]{1,0:T(8,128)(2,1)S(1)} %collective-permute-done.5.across_ref), channel_id=1, source_target_pairs={{0,1},{1,0},{2,3},{3,2},{4,5},{5,4},{6,7},{7,6},{8,9},{9,8},{10,11... | collective-permute-start | bytes 786440 | tf_op jit(solution)/shard_map/ppermute | solution.py:342
  45.5 1.6 %collective-permute-start.11 = (bf16[128,1024]{1,0:T(8,128)(2,1)S(1)}, bf16[128,1024]{1,0:T(8,128)(2,1)S(1)}, u32[]{:S(2)}, u32[]{:S(2)}) collective-permute-start(bf16[128,1024]{1,0:T(8,128)(2,1)S(1)} %late.3), channel_id=1, source_target_pairs={{0,4},{4,0},{8,12},{12,8},{16,20},{20,16},{24,28},{28,24},{1,5},{5... | collective-permute-start | bytes 786440 | tf_op jit(solution)/shard_map/ppermute | solution.py:333
